TPU v7x, 32 devices: a whole 2x2x4 slice. The times are simulated.
32 devices in a mesh: store: 8 (over y, x, core), layer: 4 (over z).
Axes of the slice: x: 2, y: 2, z: 4, core: 2. Of those that a mesh axis runs over, the one named last changes fastest.
Arguments:
- query_grads: bfloat16 [64, 32768], P('store', 'layer'), may hold values from -6 to 6
- factor_out: float32 [8, 64, 64], P('layer'), may hold values from -0.75 to 0.75
- factor_in: float32 [8, 64, 64], P('layer'), may hold values from -0.75 to 0.75
- page_store: bfloat16 [2048, 32768], P('store', 'layer'), may hold values from -0.03125 to 0.03125
- page_home: int32 [2048], replicated, may hold values from 0 to 2047, as said below
- cand_lists: int32 [8, 256], P('store'), may hold values from 0 to 2047, as said below
- counts: int32 [8], P('store'), may hold values from 32 to 256, as said below
Outputs:
- influence: float32 [8, 256, 64], P('store', 'layer')
Inputs may be any that keep to these rules, and one draw needn't show every extreme that they name: `page_home`: A permutation: every location holds one page id. The holder of location p is p // 256. `cand_lists`: among the first counts[b] slots of list b the ids are distinct, and at most 32 of them lie at one holder; in every list some holder has exactly 32. Slots from counts[b] on hold arbitrary ids. `counts`: some list uses all 256 slots.
All inputs are finite; a program needn't handle non-finite values.
Results may differ from a plain program's by a relative error of at most 0.0029.
Values may be sent and summed in bfloat16 or wider, within the bound.
No kernel may reach another device: no remote copies, remote signals or barrier semaphores. Data moves between devices by JAX's collectives and lax.ppermute only.
A program may use at most 128 MiB of HBM per device.

v0:
```python
import jax
import jax.numpy as jnp
from jax import lax
from jax.sharding import PartitionSpec as P


def on_device(query_grads, factor_out, factor_in, page_store, page_home, cand_lists, counts):
    rank_size = factor_out.shape[-1]
    layers_here = factor_out.shape[0]
    local_rows = query_grads.shape[0]
    matrices = query_grads.astype(jnp.float32).reshape(
        local_rows, layers_here, rank_size, rank_size
    )
    conditioned = jnp.einsum(
        "lab,nlbc,lcd->nlad", factor_out, matrices, factor_in, precision=lax.Precision.HIGHEST
    )
    conditioned = conditioned.reshape(local_rows, layers_here * rank_size * rank_size).astype(
        jnp.bfloat16
    )
    all_queries = lax.all_gather(conditioned, "store", axis=0, tiled=True)
    holders = lax.axis_size("store")
    per_holder = page_store.shape[0]
    wanted = cand_lists[0]
    total_slots = wanted.shape[0]
    capacity = total_slots // holders
    usable = jnp.arange(total_slots) < counts[0]
    location = page_home[wanted]
    holder = location // per_holder
    within = location % per_holder
    onehot = ((holder[:, None] == jnp.arange(holders)[None, :]) & usable[:, None]).astype(jnp.int32)
    before = jnp.cumsum(onehot, axis=0) - onehot
    position = holder * capacity + jnp.sum(before * onehot, axis=1)
    target = jnp.where(usable, position, holders * capacity)
    request = jnp.full((holders * capacity,), -1, jnp.int32).at[target].set(within, mode="drop")
    asked = lax.all_to_all(
        request.reshape(holders, capacity), "store", split_axis=0, concat_axis=0, tiled=True
    )
    present = asked >= 0
    fetched = page_store[jnp.maximum(asked, 0)]
    width = fetched.shape[-1]
    dimension_spec = (((1,), (1,)), ((), ()))
    outgoing = jnp.where(present[:, :, None], fetched, jnp.zeros((), jnp.bfloat16))
    arrived = lax.all_to_all(outgoing, "store", split_axis=0, concat_axis=0, tiled=True)
    partial_value = lax.dot_general(
        arrived.reshape(holders * capacity, width),
        all_queries,
        dimension_spec,
        preferred_element_type=jnp.float32,
    )
    picked = partial_value[jnp.where(usable, position, 0)]
    terms = jnp.where(usable[:, None], picked, jnp.zeros((), jnp.float32))
    summed = lax.psum_scatter(terms, "layer", scatter_dimension=0, tiled=True)
    return summed[None]


def solution(mesh):
    placed = (
        P("store", "layer"),
        P("layer", None, None),
        P("layer", None, None),
        P("store", "layer"),
        P(),
        P("store", None),
        P("store"),
    )
    return jax.shard_map(
        on_device, mesh=mesh, in_specs=placed, out_specs=P("store", "layer", None), check_vma=False
    )
```

profile of v0, /device:TPU:0, one launch (start us, length us, event | category | flops | bytes accessed | tf_op | source)
XLA Modules:
  0.0 127.0 jit_solution(6871824505146924201)
XLA Ops:
  6.5 0.0 copy-start
  6.5 0.7 compare_select_fusion.2
  7.3 1.9 %gather_fusion = s32[256]{0:T(256)S(1)} fusion(s32[2048]{0:T(1024)} %param.11, s32[1024]{0:T(1024)S(1)} %pad_clamp_fusion.2), kind=kCustom, calls=%fused_computation | custom fusion | bytes 3072 | tf_op jit(solution)/shard_map/gather | solution.py:27
  9.9 0.6 reduce-window.6
  10.5 0.2 slice_reduce_fusion
  10.7 0.1 fusion.5
  10.9 1.4 %scatter_custom_fusion = s32[256]{0:T(256)S(1)} fusion(s32[256]{0:T(256)S(1)} %bitcast.63, s32[256]{0:T(256)S(1)} %get-tuple-element.7, s32[]{:T(128)} %constant.38.clone.1), kind=kCustom, calls=%fused_computation.50 | custom fusion | bytes 1028 | tf_op jit(solution)/shard_map/scatter | solution.py:34
  12.3 0.1 all_to_all.9
  12.4 9.6 %all_to_all.14 = s32[8,1,32]{2,1,0:T(1,128)S(1)} all-to-all(s32[8,1,32]{2,1,0:T(1,128)S(1)} %all_to_all.9), channel_id=1, replica_groups=mesh['store'=8,'layer'=4] {'store'}, dimensions={0} | all-to-all | bytes 2048 | tf_op jit(solution)/shard_map/all_to_all | solution.py:35
  22.0 0.1 reshape.198
  22.1 11.7 %gather_fusion.1 = bf16[256,8192]{1,0:T(8,128)(2,1)} fusion(bf16[256,8192]{1,0:T(8,128)(2,1)} %param.10, s32[1024]{0:T(1024)S(1)} %pad_clamp_fusion.1), kind=kCustom, calls=%fused_computation.1 | custom fusion | bytes 8389632 | tf_op jit(solution)/shard_map/gather | solution.py:39
  33.8 4.5 %broadcast_select_fusion = bf16[8,32,8192]{2,1,0:T(8,128)(2,1)} fusion(bf16[8,32,8192]{2,1,0:T(8,128)(2,1)} %bitcast.56, pred[8,32]{1,0:T(8,128)(4,1)S(1)} %compare_bitcast_fusion), kind=kLoop, calls=%fused_computation.4 | loop fusion | flops 2097152 | bytes 8388864 | tf_op jit(solution)/shard_map/jit(_where)/select_n | solution.py:42
  38.2 0.0 copy-start.1
  38.2 0.0 copy-start.2
  38.2 4.7 %all-to-all-start.1 = ((bf16[8,32,8192]{2,1,0:T(8,128)(2,1)}), bf16[8,32,8192]{2,1,0:T(8,128)(2,1)}, u32[]{:S(2)}, u32[]{:S(2)}) async-start(bf16[8,32,8192]{2,1,0:T(8,128)(2,1)} %broadcast_select_fusion), calls=%async_computation.1 | async-start | bytes 8388608 | tf_op jit(solution)/shard_map/all_to_all | solution.py:43
  42.9 0.2 all-gather.2.cloned.1.call-start
  43.1 0.0 copy-done.1
  43.2 0.2 reshape.187
  43.4 0.0 copy-done
  43.4 0.4 convolution_bitcast_fusion
  43.9 0.0 copy-done.2
  43.9 1.0 fusion
  44.9 0.9 convert_element_type.21
  45.8 0.0 all-gather.2.cloned.1.call-update
  45.8 0.0 reduce-scatter.2.cloned.1.call-start
  45.9 39.7 %all-gather.2.cloned.1.call-done = bf16[64,8192]{1,0:T(8,128)(2,1)} async-done(((bf16[8,8192]{1,0:T(8,128)(2,1)}), bf16[64,8192]{1,0:T(8,128)(2,1)}) %all-gather.2.cloned.1.call-update) | async-done | bytes 1048592 | tf_op jit(solution)/shard_map/all_gather | solution.py:20
  85.6 10.6 %all-to-all-done.1 = bf16[8,32,8192]{2,1,0:T(8,128)(2,1)} async-done(((bf16[8,32,8192]{2,1,0:T(8,128)(2,1)}), bf16[8,32,8192]{2,1,0:T(8,128)(2,1)}, u32[]{:S(2)}, u32[]{:S(2)}) %all-to-all-start.1) | async-done | bytes 4194336 | tf_op jit(solution)/shard_map/all_to_all | solution.py:43
  96.2 3.7 %fusion.11 = f32[256,64]{1,0:T(8,128)S(1)} fusion(bf16[256,8192]{1,0:T(8,128)(2,1)} %bitcast.13, bf16[64,8192]{1,0:T(8,128)(2,1)} %all-gather.2.cloned.1.call-done), kind=kOutput, calls=%fused_computation.52 | convolution fusion | flops 268435456 | bytes 5308416 | tf_op jit(solution)/shard_map/dot_general | solution.py:44
  99.9 0.7 gather_fusion.2
  100.7 0.7 broadcast_select_fusion.1
  101.4 0.0 reduce-scatter.2.cloned.1.call-update
  101.4 18.8 %reduce-scatter.2.cloned.1.call-done = f32[64,64]{1,0:T(8,128)} async-done(((f32[256,64]{1,0:T(8,128)}), f32[64,64]{1,0:T(8,128)}) %reduce-scatter.2.cloned.1.call-update) | async-done | bytes 16400 | tf_op jit(solution)/shard_map/reduce_scatter | solution.py:52
  (15 shorter events, 0.2 us)
Async XLA Ops:
  6.5 36.9 %copy-start = (f32[2,64,64]{2,1,0:T(8,128)S(1)}, f32[2,64,64]{2,1,0:T(8,128)}, u32[]{:S(2)}) copy-start(f32[2,64,64]{2,1,0:T(8,128)} %param.8) | copy-start | bytes 98308
  38.2 4.9 %copy-start.1 = (bf16[8,8192]{1,0:T(8,128)(2,1)S(1)}, bf16[8,8192]{1,0:T(8,128)(2,1)}, u32[]{:S(2)}) copy-start(bf16[8,8192]{1,0:T(8,128)(2,1)} %param.7) | copy-start | bytes 393220
  38.2 5.6 %copy-start.2 = (f32[2,64,64]{2,1,0:T(8,128)S(1)}, f32[2,64,64]{2,1,0:T(8,128)}, u32[]{:S(2)}) copy-start(f32[2,64,64]{2,1,0:T(8,128)} %param.9) | copy-start | bytes 98308
  38.2 58.0 %all-to-all-start.1 = ((bf16[8,32,8192]{2,1,0:T(8,128)(2,1)}), bf16[8,32,8192]{2,1,0:T(8,128)(2,1)}, u32[]{:S(2)}, u32[]{:S(2)}) async-start(bf16[8,32,8192]{2,1,0:T(8,128)(2,1)} %broadcast_select_fusion), calls=%async_computation.1 | async-start | bytes 8388608 | tf_op jit(solution)/shard_map/all_to_all | solution.py:43
  42.9 42.7 %all-gather.2.cloned.1.call-start = ((), (), s32[]{:S(2)}) async-start(), calls=%async_computation.3 | async-start | bytes 1179648 | tf_op jit(solution)/shard_map/all_gather | solution.py:20
  45.8 74.4 %reduce-scatter.2.cloned.1.call-start = ((), (), s32[]{:S(2)}) async-start(), calls=%async_computation.4 | async-start | bytes 163840 | tf_op jit(solution)/shard_map/reduce_scatter | solution.py:52
Sparse Core Ops, SparseCore 0:
  46.0 39.6 all-gather.1
  101.5 18.6 reduce-scatter.1
where the time goes:
time: 127 us
  waiting for transfers between devices  69.1 us (54%)
  local copies, waits for them, and re-layouts  17.3 us (14%)
  between operations  14.2 us (11%)
  blocking collectives  9.62 us (8%)
  other arithmetic  6.72 us (5%)
  matrix products  5.13 us (4%)
  starting transfers between devices  4.94 us (4%)
    all_gather x1, waiting for transfers between devices, on_device(): all_queries = lax.all_gather(conditioned, 'store', axis=0, tiled=True)  39.7 us
    reduce_scatter x1, waiting for transfers between devices, on_device(): summed = lax.psum_scatter(terms, 'layer', scatter_dimension=0, tiled=True)  18.8 us
    gather x1, local copies, waits for them, and re-layouts, on_device(): fetched = page_store[jnp.maximum(asked, 0)]  11.7 us
    all_to_all x1, waiting for transfers between devices, on_device(): lax.all_to_all(outgoing, 'store', split_axis=0, concat_axis=0, tiled=True)  10.6 us
    all_to_all x1, blocking collectives, on_device(): lax.all_to_all(request.reshape(holders, capacity), 'store', split_axis=0,...  9.62 us
    all_to_all x1, starting transfers between devices, on_device(): lax.all_to_all(outgoing, 'store', split_axis=0, concat_axis=0, tiled=True)  4.68 us
    select_n x1, other arithmetic, on_device(): jnp.where(present[:, :, None], fetched, jnp.zeros((), jnp.bfloat16))  4.45 us
    dot_general x1, matrix products, on_device(): lax.dot_general(arrived.reshape(holders * capacity, width), all_queries,...  3.71 us
  transfers between devices with their start and end apart: 3, of which 3 were waited for; matrix products, arithmetic and copies ran while one was open for 2% of the time, Pallas kernels for 0%

commit v1 on v0

v1 whole, which is shorter than its diff:
```python
import functools

import jax
import jax.numpy as jnp
from jax import lax
from jax.experimental import pallas as pl
from jax.experimental.pallas import tpu as pltpu
from jax.sharding import PartitionSpec as P

HIGHEST = lax.Precision.HIGHEST
VMEM = pl.BlockSpec(memory_space=pltpu.VMEM)
SMEM = pl.BlockSpec(memory_space=pltpu.SMEM)
ANY = pl.BlockSpec(memory_space=pl.ANY)
LANES = 128
CHUNKS = 4


def iota(shape, dimension):
    return lax.broadcasted_iota(jnp.int32, shape, dimension)


def condition_kernel(holders, per_holder, count_ref, query_ref, out_factor_ref, in_factor_ref, home_ref, cand_ref, packed_ref):
    rows, width = query_ref.shape
    layers, rank, _ = in_factor_ref.shape
    half = rank // 2
    query = query_ref[...].astype(jnp.float32)
    low = iota((half, LANES), 1) < rank
    zero = jnp.zeros((rank, rank), jnp.float32)
    for layer in range(layers):
        first = layer * half
        packed = jnp.concatenate(
            [query[:, (first + t) * LANES:(first + t + 1) * LANES] for t in range(half)], axis=0
        )
        factor = in_factor_ref[layer]
        doubled = jnp.concatenate(
            [jnp.concatenate([factor, zero], axis=1), jnp.concatenate([zero, factor], axis=1)], axis=0
        )
        right = jnp.dot(packed, doubled, precision=HIGHEST, preferred_element_type=jnp.float32)
        right = jnp.swapaxes(right.reshape(half, rows, LANES), 0, 1)
        wide = jnp.concatenate([right[q] for q in range(rows)], axis=1)
        left = jnp.dot(out_factor_ref[layer], wide, precision=HIGHEST, preferred_element_type=jnp.float32)
        done = []
        for q in range(rows):
            part = left[:, q * LANES:(q + 1) * LANES]
            ee, eo, oe, oo = (part[i * half:(i + 1) * half] for i in range(4))
            done.append(jnp.where(low, ee, oo) + pltpu.roll(jnp.where(low, oe, eo), rank, 1))
        done = jnp.swapaxes(jnp.stack(done), 0, 1)
        for t in range(half):
            packed_ref[:, (first + t) * LANES:(first + t + 1) * LANES] = done[t].astype(jnp.bfloat16)

    slots = cand_ref.shape[1]
    groups = home_ref.shape[0]
    wanted = cand_ref[...]
    onehot = (iota((LANES, slots), 0) == wanted % LANES).astype(jnp.float32).astype(jnp.bfloat16)
    home = home_ref[...]
    table = jnp.concatenate([home // per_holder, home % per_holder], axis=0).astype(jnp.float32).astype(jnp.bfloat16)
    found = jnp.dot(table, onehot, preferred_element_type=jnp.float32)
    mine = iota((groups, slots), 0) == wanted // LANES
    holder = jnp.sum(jnp.where(mine, found[:groups], 0.0), axis=0, keepdims=True)
    within = jnp.sum(jnp.where(mine, found[groups:], 0.0), axis=0, keepdims=True)
    holder = jnp.where(iota((1, slots), 1) < count_ref[0], holder, float(holders))
    rest = jnp.zeros((rows - 2, slots), jnp.float32)
    packed_ref[:, width:] = jnp.concatenate([holder, within, rest], axis=0).astype(jnp.bfloat16)


def score_kernel(holders, me_ref, *refs):
    packed_refs, pages_ref, out_refs = refs[:holders], refs[holders], refs[holders + 1:2 * holders + 1]
    held, total, arrived = refs[2 * holders + 1:]
    me = me_ref[0]
    count, width = pages_ref.shape
    rows = packed_refs[0].shape[0]
    slots = packed_refs[0].shape[1] - width
    step = width // CHUNKS
    copies = [
        pltpu.make_async_copy(
            pages_ref.at[:, pl.ds(i * step, step)], held.at[:, pl.ds(i * step, step)], arrived.at[i]
        )
        for i in range(CHUNKS)
    ]
    for copy in copies:
        copy.start()
    scores = jnp.zeros((holders * rows, count), jnp.float32)
    for i in range(CHUNKS):
        columns = slice(i * step, (i + 1) * step)
        queries = jnp.concatenate([ref[:, columns].astype(jnp.float32) for ref in packed_refs], axis=0)
        copies[i].wait()
        scores = scores + lax.dot_general(
            queries.astype(jnp.bfloat16), held[:, columns], (((1,), (1,)), ((), ())),
            preferred_element_type=jnp.float32,
        )
    for k in range(holders):
        start = pl.multiple_of((me ^ k) * rows, rows)
        total[pl.ds(start, rows), :] = scores[k * rows:(k + 1) * rows]
    ordered = total[...].astype(jnp.bfloat16)
    page = iota((count, slots), 0).astype(jnp.float32)
    here = me.astype(jnp.float32)
    for k in range(holders):
        notes = packed_refs[k][:, width:].astype(jnp.float32)
        chosen = jnp.where(notes[0:1] == here, notes[1:2], -1.0)
        onehot = (page == chosen).astype(jnp.float32).astype(jnp.bfloat16)
        out_refs[k][...] = jnp.dot(ordered, onehot, preferred_element_type=jnp.float32).astype(jnp.bfloat16)


def split_kernel(holders, groups, me_ref, *refs):
    me = me_ref[0]
    total = refs[0][...].astype(jnp.float32)
    for ref in refs[1:holders]:
        total = total + ref[...].astype(jnp.float32)
    share = total.shape[1] // groups
    parts = [total[:, g * share:(g + 1) * share] for g in range(groups)]
    for j in range(groups):
        part = parts[0]
        for g in range(1, groups):
            part = jnp.where((me ^ j) == g, parts[g], part)
        refs[holders + j][...] = part.astype(jnp.bfloat16)


def add_kernel(*refs):
    total = refs[0][...].astype(jnp.float32)
    for ref in refs[1:-1]:
        total = total + ref[...].astype(jnp.float32)
    refs[-1][0] = total.T


def swap(value, axis, distance):
    size = lax.axis_size(axis)
    return lax.ppermute(value, axis, [(i, i ^ distance) for i in range(size)])


def on_device(query_grads, factor_out, factor_in, page_store, page_home, cand_lists, counts):
    holders = lax.axis_size("store")
    groups = lax.axis_size("layer")
    rows, width = query_grads.shape
    layers, rank, _ = factor_out.shape
    per_holder = page_store.shape[0]
    slots = cand_lists.shape[1]
    bf16 = jnp.bfloat16
    store_at = lax.axis_index("store").astype(jnp.int32).reshape(1)
    layer_at = lax.axis_index("layer").astype(jnp.int32).reshape(1)

    out_factor = factor_out.reshape(layers, rank // 2, 2, rank // 2, 2)
    out_factor = out_factor.transpose(0, 2, 4, 1, 3).reshape(layers, 2 * rank, rank // 2)
    packed = pl.pallas_call(
        functools.partial(condition_kernel, holders, per_holder),
        out_shape=jax.ShapeDtypeStruct((rows, width + slots), bf16),
        in_specs=[SMEM] + [VMEM] * 5,
        out_specs=VMEM,
    )(counts, query_grads, out_factor, factor_in, page_home.reshape(-1, LANES), cand_lists)

    blocks = [None] * holders
    blocks[0] = packed
    blocks[1] = swap(packed, "store", 1)
    for k in range(2, holders, 2):
        blocks[k] = swap(packed, "store", k)
    for k in range(2, holders, 2):
        blocks[k + 1] = swap(blocks[k], "store", 1)

    total = holders * rows
    picked = pl.pallas_call(
        functools.partial(score_kernel, holders),
        out_shape=[jax.ShapeDtypeStruct((total, slots), bf16)] * holders,
        in_specs=[SMEM] + [VMEM] * holders + [ANY],
        out_specs=[VMEM] * holders,
        scratch_shapes=[
            pltpu.VMEM((per_holder, width), bf16),
            pltpu.VMEM((total, per_holder), jnp.float32),
            pltpu.SemaphoreType.DMA((CHUNKS,)),
        ],
        compiler_params=pltpu.CompilerParams(vmem_limit_bytes=56 * 2**20),
    )(store_at, *blocks, page_store)

    landed = [picked[0]] + [swap(picked[k], "store", k) for k in range(1, holders)]
    share = slots // groups
    parts = pl.pallas_call(
        functools.partial(split_kernel, holders, groups),
        out_shape=[jax.ShapeDtypeStruct((total, share), bf16)] * groups,
        in_specs=[SMEM] + [VMEM] * holders,
        out_specs=[VMEM] * groups,
        compiler_params=pltpu.CompilerParams(vmem_limit_bytes=56 * 2**20),
    )(layer_at, *landed)

    terms = [parts[0]] + [swap(parts[j], "layer", j) for j in range(1, groups)]
    return pl.pallas_call(
        add_kernel,
        out_shape=jax.ShapeDtypeStruct((1, share, total), jnp.float32),
        in_specs=[VMEM] * groups,
        out_specs=VMEM,
    )(*terms)


def solution(mesh):
    placed = (
        P("store", "layer"),
        P("layer", None, None),
        P("layer", None, None),
        P("store", "layer"),
        P(),
        P("store", None),
        P("store"),
    )
    return jax.shard_map(
        on_device, mesh=mesh, in_specs=placed, out_specs=P("store", "layer", None), check_vma=False
    )
```

time: 127 us -> 52.1 us (0.41)
  waiting for transfers between devices: 69.1 us -> 16.2 us
  between operations: 14.2 us -> 0.76 us
  Pallas kernels: 0 us -> 12.8 us
  local copies, waits for them, and re-layouts: 17.3 us -> 6.36 us
  starting transfers between devices: 4.94 us -> 15.7 us
  blocking collectives: 9.62 us -> 0 us
  other arithmetic: 6.72 us -> 0 us
  matrix products: 5.13 us -> 0 us
    all_gather x1 -> x0, waiting for transfers between devices: 39.7 us -> none  [on_device(): all_queries = lax.all_gather(conditioned, 'store', axis=0, tiled=True)]
    reduce_scatter x1 -> x0, waiting for transfers between devices: 18.8 us -> none  [on_device(): summed = lax.psum_scatter(terms, 'layer', scatter_dimension=0, tiled=True)]
    ppermute x0 -> x17, waiting for transfers between devices: none -> 16.2 us  [swap(): return lax.ppermute(value, axis, [(i, i ^ distance) for i in range(size)])]
    ppermute x0 -> x17, starting transfers between devices: none -> 15.7 us  [swap(): return lax.ppermute(value, axis, [(i, i ^ distance) for i in range(size)])]
    gather x3 -> x0, local copies, waits for them, and re-layouts: 14.4 us -> none  [the longest x1 11.7 us: on_device(): fetched = page_store[jnp.maximum(asked, 0)]]
    pallas_call x0 -> x4, Pallas kernels: none -> 12.8 us  [the longest x1 6.23 us: on_device(): pl.pallas_call(functools.partial(score_kernel, holders), out_shape=[jax.S...]
    all_to_all x1 -> x0, waiting for transfers between devices: 10.6 us -> none  [on_device(): lax.all_to_all(outgoing, 'store', split_axis=0, concat_axis=0, tiled=True)]
    all_to_all x1 -> x0, blocking collectives: 9.62 us -> none  [on_device(): lax.all_to_all(request.reshape(holders, capacity), 'store', split_axis=0,...]
  transfers between devices with their start and end apart: 3 -> 17, of which waited for: 3 -> 10; matrix products, arithmetic and copies ran while one was open for 2% -> 0% of each run, Pallas kernels for 0% -> 0%
where the time goes in v1:
time: 52.1 us; the launch traced here: 51.8 us
  waiting for transfers between devices  16.2 us (31%)
  starting transfers between devices  15.7 us (30%)
  Pallas kernels  12.8 us (25%)
  local copies, waits for them, and re-layouts  6.36 us (12%)
  between operations  0.76 us (1%)
    ppermute x17, waiting for transfers between devices, swap(): return lax.ppermute(value, axis, [(i, i ^ distance) for i in range(size)])  16.2 us
    ppermute x17, starting transfers between devices, swap(): return lax.ppermute(value, axis, [(i, i ^ distance) for i in range(size)])  15.7 us
    pallas_call x1, Pallas kernels, on_device(): pl.pallas_call(functools.partial(score_kernel, holders), out_shape=[jax.S...  6.23 us
    pallas_call x1, Pallas kernels, on_device(): pl.pallas_call(functools.partial(condition_kernel, holders, per_holder),...  3.28 us
    reshape x1, local copies, waits for them, and re-layouts, on_device(): out_factor = factor_out.reshape(layers, rank // 2, 2, rank // 2, 2)  2.99 us
    unnamed x34, local copies, waits for them, and re-layouts  1.83 us
    pallas_call x1, Pallas kernels, on_device(): pl.pallas_call(functools.partial(split_kernel, holders, groups), out_shap...  1.81 us
    transpose x1, local copies, waits for them, and re-layouts, on_device(): out_factor.transpose(0, 2, 4, 1, 3).reshape(layers, 2 * rank, rank // 2)  1.54 us
  transfers between devices with their start and end apart: 17, of which 10 were waited for; matrix products, arithmetic and copies ran while one was open for 0% of the time, Pallas kernels for 0%

profile of v1, /device:TPU:0, one launch (start us, length us, event | category | flops | bytes accessed | tf_op | source)
XLA Modules:
  0.0 51.8 jit_solution(16383129218753030283)
XLA Ops:
  0.0 3.0 %reshape.17 = f32[2,32,2,32,2]{4,3,2,1,0:T(8,128)S(1)} reshape(f32[2,64,64]{2,1,0:T(8,128)} %param.8) | data formatting | bytes 65536 | tf_op jit(solution)/shard_map/reshape | solution.py:141
  3.0 1.5 %copy.9 = f32[2,2,2,32,32]{4,3,2,1,0:T(8,128)} copy(f32[2,2,2,32,32]{2,4,1,3,0:T(8,128)S(1)} %bitcast.5) | data formatting | bytes 65536 | tf_op jit(solution)/shard_map/transpose | solution.py:142
  5.2 3.3 %shard_map.73.refs_0_ = bf16[8,8448]{1,0:T(8,128)(2,1)} custom-call(s32[1]{0:T(128)S(6)} %copy.10.count_ref, bf16[8,8192]{1,0:T(8,128)(2,1)} %query_ref.1, f32[2,128,32]{2,1,0:T(8,128)} %bitcast.6, f32[2,64,64]{2,1,0:T(8,128)} %in_factor_ref.1, s32[16,128]{1,0:T(8,128)} %bitcast.7, s32[1,256]{1,0:T(1,128)} %cand_ref.1), custom_call_target="tpu_custom_call" | custom-call | tf_op jit(solution)/shard_map/pallas_call | solution.py:143
  8.5 2.9 %collective-permute-start.1 = (bf16[8,8448]{1,0:T(8,128)(2,1)}, bf16[8,8448]{1,0:T(8,128)(2,1)S(1)}, u32[]{:S(2)}, u32[]{:S(2)}) collective-permute-start(bf16[8,8448]{1,0:T(8,128)(2,1)} %shard_map.73.refs_0_), channel_id=1, source_target_pairs={{0,8},{4,12},{8,0},{12,4},{16,24},{20,28},{24,16},{28,20},{1,9},{5... | collective-permute-start | bytes 405512 | tf_op jit(solution)/shard_map/ppermute | solution.py:127
  11.4 1.5 %collective-permute-start.3 = (bf16[8,8448]{1,0:T(8,128)(2,1)}, bf16[8,8448]{1,0:T(8,128)(2,1)S(1)}, u32[]{:S(2)}, u32[]{:S(2)}) collective-permute-start(bf16[8,8448]{1,0:T(8,128)(2,1)} %shard_map.73.refs_0_), channel_id=1, source_target_pairs={{0,16},{4,20},{8,24},{12,28},{16,0},{20,4},{24,8},{28,12},{1,17},{... | collective-permute-start | bytes 405512 | tf_op jit(solution)/shard_map/ppermute | solution.py:127
  12.9 0.0 collective-permute-start.5
  12.9 0.0 collective-permute-start
  12.9 2.8 %collective-permute-done.1.refs_2_ = bf16[8,8448]{1,0:T(8,128)(2,1)S(1)} collective-permute-done((bf16[8,8448]{1,0:T(8,128)(2,1)}, bf16[8,8448]{1,0:T(8,128)(2,1)S(1)}, u32[]{:S(2)}, u32[]{:S(2)}) %collective-permute-start.1) | collective-permute-done | bytes 135200 | tf_op jit(solution)/shard_map/ppermute | solution.py:127
  15.7 0.0 collective-permute-start.2
  15.7 3.8 %collective-permute-done.3.refs_4_ = bf16[8,8448]{1,0:T(8,128)(2,1)S(1)} collective-permute-done((bf16[8,8448]{1,0:T(8,128)(2,1)}, bf16[8,8448]{1,0:T(8,128)(2,1)S(1)}, u32[]{:S(2)}, u32[]{:S(2)}) %collective-permute-start.3) | collective-permute-done | bytes 135200 | tf_op jit(solution)/shard_map/ppermute | solution.py:127
  19.6 0.0 collective-permute-start.4
  19.6 0.0 collective-permute-done.5.refs_6_
  19.6 0.0 copy-start.2
  19.6 0.5 collective-permute-start.6
  20.1 0.0 collective-permute-done.refs_1_
  20.1 0.0 collective-permute-done.2.refs_3_
  20.1 0.0 copy-start.4
  20.1 0.8 %collective-permute-done.4.refs_5_ = bf16[8,8448]{1,0:T(8,128)(2,1)S(1)} collective-permute-done((bf16[8,8448]{1,0:T(8,128)(2,1)S(1)}, bf16[8,8448]{1,0:T(8,128)(2,1)S(1)}, u32[]{:S(2)}, u32[]{:S(2)}) %collective-permute-start.4) | collective-permute-done | bytes 135200 | tf_op jit(solution)/shard_map/ppermute | solution.py:127
  20.9 0.2 collective-permute-done.6.refs_7_
  21.1 0.4 copy-done.5
  21.6 0.2 copy-done.6
  21.8 6.2 %shard_map.74 = (bf16[64,256]{1,0:T(8,128)(2,1)}, bf16[64,256]{1,0:T(8,128)(2,1)}, bf16[64,256]{1,0:T(8,128)(2,1)}, bf16[64,256]{1,0:T(8,128)(2,1)}, bf16[64,256...) custom-call(s32[1]{0:T(128)} %bitcast.1.me_ref, ...), custom_call_target="tpu_custom_call" | custom-call | tf_op jit(solution)/shard_map/pallas_call | solution.py:159
  28.0 1.6 %collective-permute-start.10 = (bf16[64,256]{1,0:T(8,128)(2,1)}, bf16[64,256]{1,0:T(8,128)(2,1)S(1)}, u32[]{:S(2)}, u32[]{:S(2)}) collective-permute-start(bf16[64,256]{1,0:T(8,128)(2,1)} %get-tuple-element.21), channel_id=1, source_target_pairs={{0,16},{4,20},{8,24},{12,28},{16,0},{20,4},{24,8},{28,12},{1,17},{... | collective-permute-start | bytes 98312 | tf_op jit(solution)/shard_map/ppermute | solution.py:127
  29.6 0.2 collective-permute-start.11
  29.7 1.5 %collective-permute-start.12 = (bf16[64,256]{1,0:T(8,128)(2,1)}, bf16[64,256]{1,0:T(8,128)(2,1)S(1)}, u32[]{:S(2)}, u32[]{:S(2)}) collective-permute-start(bf16[64,256]{1,0:T(8,128)(2,1)} %get-tuple-element.23), channel_id=1, source_target_pairs={{0,24},{4,28},{8,16},{12,20},{16,8},{20,12},{24,0},{28,4},{1,25},{... | collective-permute-start | bytes 98312 | tf_op jit(solution)/shard_map/ppermute | solution.py:127
  31.2 1.2 %collective-permute-start.13 = (bf16[64,256]{1,0:T(8,128)(2,1)}, bf16[64,256]{1,0:T(8,128)(2,1)S(1)}, u32[]{:S(2)}, u32[]{:S(2)}) collective-permute-start(bf16[64,256]{1,0:T(8,128)(2,1)} %get-tuple-element.24), channel_id=1, source_target_pairs={{0,28},{4,24},{8,20},{12,16},{16,12},{20,8},{24,4},{28,0},{1,29},{... | collective-permute-start | bytes 98312 | tf_op jit(solution)/shard_map/ppermute | solution.py:127
  32.5 0.3 collective-permute-start.7
  32.8 0.0 collective-permute-done.10.refs_4_
  32.8 0.9 %collective-permute-start.8 = (bf16[64,256]{1,0:T(8,128)(2,1)}, bf16[64,256]{1,0:T(8,128)(2,1)S(1)}, u32[]{:S(2)}, u32[]{:S(2)}) collective-permute-start(bf16[64,256]{1,0:T(8,128)(2,1)} %get-tuple-element.19), channel_id=1, source_target_pairs={{0,8},{4,12},{8,0},{12,4},{16,24},{20,28},{24,16},{28,20},{1,9},{5... | collective-permute-start | bytes 98312 | tf_op jit(solution)/shard_map/ppermute | solution.py:127
  33.7 0.0 collective-permute-done.11.refs_5_
  33.7 0.7 %collective-permute-start.9 = (bf16[64,256]{1,0:T(8,128)(2,1)}, bf16[64,256]{1,0:T(8,128)(2,1)S(1)}, u32[]{:S(2)}, u32[]{:S(2)}) collective-permute-start(bf16[64,256]{1,0:T(8,128)(2,1)} %get-tuple-element.20), channel_id=1, source_target_pairs={{0,12},{4,8},{8,4},{12,0},{16,28},{20,24},{24,20},{28,16},{1,13},{... | collective-permute-start | bytes 98312 | tf_op jit(solution)/shard_map/ppermute | solution.py:127
  34.3 0.4 collective-permute-done.12.refs_6_
  34.8 0.9 %collective-permute-done.13.refs_7_ = bf16[64,256]{1,0:T(8,128)(2,1)S(1)} collective-permute-done((bf16[64,256]{1,0:T(8,128)(2,1)}, bf16[64,256]{1,0:T(8,128)(2,1)S(1)}, u32[]{:S(2)}, u32[]{:S(2)}) %collective-permute-start.13) | collective-permute-done | bytes 32800 | tf_op jit(solution)/shard_map/ppermute | solution.py:127
  35.7 0.0 collective-permute-done.7.refs_1_
  35.7 1.3 %collective-permute-done.8.refs_2_ = bf16[64,256]{1,0:T(8,128)(2,1)S(1)} collective-permute-done((bf16[64,256]{1,0:T(8,128)(2,1)}, bf16[64,256]{1,0:T(8,128)(2,1)S(1)}, u32[]{:S(2)}, u32[]{:S(2)}) %collective-permute-start.8) | collective-permute-done | bytes 32800 | tf_op jit(solution)/shard_map/ppermute | solution.py:127
  36.9 0.5 collective-permute-done.9.refs_3_
  37.4 0.0 copy-done.7
  37.4 0.1 copy-done.12
  37.5 0.5 copy-done.13
  38.0 1.8 %shard_map.75 = (bf16[64,64]{1,0:T(8,128)(2,1)}, bf16[64,64]{1,0:T(8,128)(2,1)}, bf16[64,64]{1,0:T(8,128)(2,1)}, bf16[64,64]{1,0:T(8,128)(2,1)}) custom-call(s32[1]{0:T(128)} %bitcast.me_ref, bf16[64,256]{1,0:T(8,128)(2,1)} %get-tuple-element.17.refs_0_, bf16[64,256]{1,0:T(8,128)(2,1)} %copy-done.11, bf16[64,256]{1,0:T(8,128)(2,1)} %copy-done.12, ...), custom_call_target="tpu_custom_call" | custom-call | tf_op jit(solution)/shard_map/pallas_call | solution.py:174
  39.8 1.6 %collective-permute-start.14 = (bf16[64,64]{1,0:T(8,128)(2,1)}, bf16[64,64]{1,0:T(8,128)(2,1)S(1)}, u32[]{:S(2)}, u32[]{:S(2)}) collective-permute-start(bf16[64,64]{1,0:T(8,128)(2,1)} %get-tuple-element.26), channel_id=1, source_target_pairs={{0,1},{1,0},{2,3},{3,2},{4,5},{5,4},{6,7},{7,6},{8,9},{9,8},{10,11... | collective-permute-start | bytes 24584 | tf_op jit(solution)/shard_map/ppermute | solution.py:127
  41.4 2.6 %collective-permute-start.15 = (bf16[64,64]{1,0:T(8,128)(2,1)}, bf16[64,64]{1,0:T(8,128)(2,1)S(1)}, u32[]{:S(2)}, u32[]{:S(2)}) collective-permute-start(bf16[64,64]{1,0:T(8,128)(2,1)} %get-tuple-element.27), channel_id=1, source_target_pairs={{0,2},{1,3},{2,0},{3,1},{4,6},{5,7},{6,4},{7,5},{8,10},{9,11},{10,... | collective-permute-start | bytes 24584 | tf_op jit(solution)/shard_map/ppermute | solution.py:127
  44.0 0.2 collective-permute-start.16
  44.2 0.0 collective-permute-done.14.refs_1_
  44.2 2.2 %collective-permute-done.15.refs_2_ = bf16[64,64]{1,0:T(8,128)(2,1)S(1)} collective-permute-done((bf16[64,64]{1,0:T(8,128)(2,1)}, bf16[64,64]{1,0:T(8,128)(2,1)S(1)}, u32[]{:S(2)}, u32[]{:S(2)}) %collective-permute-start.15) | collective-permute-done | bytes 8224 | tf_op jit(solution)/shard_map/ppermute | solution.py:127
  46.4 3.3 %collective-permute-done.16.refs_3_ = bf16[64,64]{1,0:T(8,128)(2,1)S(1)} collective-permute-done((bf16[64,64]{1,0:T(8,128)(2,1)}, bf16[64,64]{1,0:T(8,128)(2,1)S(1)}, u32[]{:S(2)}, u32[]{:S(2)}) %collective-permute-start.16) | collective-permute-done | bytes 8224 | tf_op jit(solution)/shard_map/ppermute | solution.py:127
  49.7 0.6 %copy-done.16 = bf16[64,64]{1,0:T(8,128)(2,1)} copy-done((bf16[64,64]{1,0:T(8,128)(2,1)}, bf16[64,64]{1,0:T(8,128)(2,1)S(1)}, u32[]{:S(2)}) %copy-start.16) | copy-done | bytes 8216
  50.3 1.5 %shard_map.76 = f32[1,64,64]{2,1,0:T(8,128)} custom-call(bf16[64,64]{1,0:T(8,128)(2,1)} %get-tuple-element.25.refs_0_, bf16[64,64]{1,0:T(8,128)(2,1)} %copy-done.14, bf16[64,64]{1,0:T(8,128)(2,1)} %copy-done.15, bf16[64,64]{1,0:T(8,128)(2,1)} %copy-done.16), custom_call_target="tpu_custom_call" | custom-call | tf_op jit(solution)/shard_map/pallas_call | solution.py:183
  (26 shorter events, 0.0 us)
Async XLA Ops:
  8.5 7.2 %collective-permute-start.1 = (bf16[8,8448]{1,0:T(8,128)(2,1)}, bf16[8,8448]{1,0:T(8,128)(2,1)S(1)}, u32[]{:S(2)}, u32[]{:S(2)}) collective-permute-start(bf16[8,8448]{1,0:T(8,128)(2,1)} %shard_map.73.refs_0_), channel_id=1, source_target_pairs={{0,8},{4,12},{8,0},{12,4},{16,24},{20,28},{24,16},{28,20},{1,9},{5... | collective-permute-start | bytes 405512 | tf_op jit(solution)/shard_map/ppermute | solution.py:127
  11.4 8.2 %collective-permute-start.3 = (bf16[8,8448]{1,0:T(8,128)(2,1)}, bf16[8,8448]{1,0:T(8,128)(2,1)S(1)}, u32[]{:S(2)}, u32[]{:S(2)}) collective-permute-start(bf16[8,8448]{1,0:T(8,128)(2,1)} %shard_map.73.refs_0_), channel_id=1, source_target_pairs={{0,16},{4,20},{8,24},{12,28},{16,0},{20,4},{24,8},{28,12},{1,17},{... | collective-permute-start | bytes 405512 | tf_op jit(solution)/shard_map/ppermute | solution.py:127
  12.9 6.6 %collective-permute-start.5 = (bf16[8,8448]{1,0:T(8,128)(2,1)}, bf16[8,8448]{1,0:T(8,128)(2,1)S(1)}, u32[]{:S(2)}, u32[]{:S(2)}) collective-permute-start(bf16[8,8448]{1,0:T(8,128)(2,1)} %shard_map.73.refs_0_), channel_id=1, source_target_pairs={{0,24},{4,28},{8,16},{12,20},{16,8},{20,12},{24,0},{28,4},{1,25},{... | collective-permute-start | bytes 405512 | tf_op jit(solution)/shard_map/ppermute | solution.py:127
  12.9 7.2 %collective-permute-start = (bf16[8,8448]{1,0:T(8,128)(2,1)}, bf16[8,8448]{1,0:T(8,128)(2,1)S(1)}, u32[]{:S(2)}, u32[]{:S(2)}) collective-permute-start(bf16[8,8448]{1,0:T(8,128)(2,1)} %shard_map.73.refs_0_), channel_id=1, source_target_pairs={{0,4},{4,0},{8,12},{12,8},{16,20},{20,16},{24,28},{28,24},{1,5},{5... | collective-permute-start | bytes 405512 | tf_op jit(solution)/shard_map/ppermute | solution.py:127
  15.7 5.4 %copy-start = (bf16[8,8448]{1,0:T(8,128)(2,1)}, bf16[8,8448]{1,0:T(8,128)(2,1)S(1)}, u32[]{:S(2)}) copy-start(bf16[8,8448]{1,0:T(8,128)(2,1)S(1)} %collective-permute-done.1.refs_2_) | copy-start | bytes 405508
  15.7 4.4 %collective-permute-start.2 = (bf16[8,8448]{1,0:T(8,128)(2,1)S(1)}, bf16[8,8448]{1,0:T(8,128)(2,1)S(1)}, u32[]{:S(2)}, u32[]{:S(2)}) collective-permute-start(bf16[8,8448]{1,0:T(8,128)(2,1)S(1)} %collective-permute-done.1.refs_2_), channel_id=1, source_target_pairs={{0,4},{4,0},{8,12},{12,8},{16,20},{20,16},{24,28},{28,24},{1,5},{5... | collective-permute-start | bytes 405512 | tf_op jit(solution)/shard_map/ppermute | solution.py:127
  19.6 1.6 %copy-start.1 = (bf16[8,8448]{1,0:T(8,128)(2,1)}, bf16[8,8448]{1,0:T(8,128)(2,1)S(1)}, u32[]{:S(2)}) copy-start(bf16[8,8448]{1,0:T(8,128)(2,1)S(1)} %collective-permute-done.3.refs_4_) | copy-start | bytes 405508
  19.6 1.4 %collective-permute-start.4 = (bf16[8,8448]{1,0:T(8,128)(2,1)S(1)}, bf16[8,8448]{1,0:T(8,128)(2,1)S(1)}, u32[]{:S(2)}, u32[]{:S(2)}) collective-permute-start(bf16[8,8448]{1,0:T(8,128)(2,1)S(1)} %collective-permute-done.3.refs_4_), channel_id=1, source_target_pairs={{0,4},{4,0},{8,12},{12,8},{16,20},{20,16},{24,28},{28,24},{1,5},{5... | collective-permute-start | bytes 405512 | tf_op jit(solution)/shard_map/ppermute | solution.py:127
  19.6 1.5 %copy-start.2 = (bf16[8,8448]{1,0:T(8,128)(2,1)}, bf16[8,8448]{1,0:T(8,128)(2,1)S(1)}, u32[]{:S(2)}) copy-start(bf16[8,8448]{1,0:T(8,128)(2,1)S(1)} %collective-permute-done.5.refs_6_) | copy-start | bytes 405508
  19.6 1.5 %collective-permute-start.6 = (bf16[8,8448]{1,0:T(8,128)(2,1)S(1)}, bf16[8,8448]{1,0:T(8,128)(2,1)S(1)}, u32[]{:S(2)}, u32[]{:S(2)}) collective-permute-start(bf16[8,8448]{1,0:T(8,128)(2,1)S(1)} %collective-permute-done.5.refs_6_), channel_id=1, source_target_pairs={{0,4},{4,0},{8,12},{12,8},{16,20},{20,16},{24,28},{28,24},{1,5},{5... | collective-permute-start | bytes 405512 | tf_op jit(solution)/shard_map/ppermute | solution.py:127
  20.1 1.0 %copy-start.3 = (bf16[8,8448]{1,0:T(8,128)(2,1)}, bf16[8,8448]{1,0:T(8,128)(2,1)S(1)}, u32[]{:S(2)}) copy-start(bf16[8,8448]{1,0:T(8,128)(2,1)S(1)} %collective-permute-done.refs_1_) | copy-start | bytes 405508
  20.1 1.0 %copy-start.4 = (bf16[8,8448]{1,0:T(8,128)(2,1)}, bf16[8,8448]{1,0:T(8,128)(2,1)S(1)}, u32[]{:S(2)}) copy-start(bf16[8,8448]{1,0:T(8,128)(2,1)S(1)} %collective-permute-done.2.refs_3_) | copy-start | bytes 405508
  20.9 0.7 %copy-start.5 = (bf16[8,8448]{1,0:T(8,128)(2,1)}, bf16[8,8448]{1,0:T(8,128)(2,1)S(1)}, u32[]{:S(2)}) copy-start(bf16[8,8448]{1,0:T(8,128)(2,1)S(1)} %collective-permute-done.4.refs_5_) | copy-start | bytes 405508
  21.1 0.7 %copy-start.6 = (bf16[8,8448]{1,0:T(8,128)(2,1)}, bf16[8,8448]{1,0:T(8,128)(2,1)S(1)}, u32[]{:S(2)}) copy-start(bf16[8,8448]{1,0:T(8,128)(2,1)S(1)} %collective-permute-done.6.refs_7_) | copy-start | bytes 405508
  28.0 4.8 %collective-permute-start.10 = (bf16[64,256]{1,0:T(8,128)(2,1)}, bf16[64,256]{1,0:T(8,128)(2,1)S(1)}, u32[]{:S(2)}, u32[]{:S(2)}) collective-permute-start(bf16[64,256]{1,0:T(8,128)(2,1)} %get-tuple-element.21), channel_id=1, source_target_pairs={{0,16},{4,20},{8,24},{12,28},{16,0},{20,4},{24,8},{28,12},{1,17},{... | collective-permute-start | bytes 98312 | tf_op jit(solution)/shard_map/ppermute | solution.py:127
  29.6 4.1 %collective-permute-start.11 = (bf16[64,256]{1,0:T(8,128)(2,1)}, bf16[64,256]{1,0:T(8,128)(2,1)S(1)}, u32[]{:S(2)}, u32[]{:S(2)}) collective-permute-start(bf16[64,256]{1,0:T(8,128)(2,1)} %get-tuple-element.22), channel_id=1, source_target_pairs={{0,20},{4,16},{8,28},{12,24},{16,4},{20,0},{24,12},{28,8},{1,21},{... | collective-permute-start | bytes 98312 | tf_op jit(solution)/shard_map/ppermute | solution.py:127
  29.7 5.0 %collective-permute-start.12 = (bf16[64,256]{1,0:T(8,128)(2,1)}, bf16[64,256]{1,0:T(8,128)(2,1)S(1)}, u32[]{:S(2)}, u32[]{:S(2)}) collective-permute-start(bf16[64,256]{1,0:T(8,128)(2,1)} %get-tuple-element.23), channel_id=1, source_target_pairs={{0,24},{4,28},{8,16},{12,20},{16,8},{20,12},{24,0},{28,4},{1,25},{... | collective-permute-start | bytes 98312 | tf_op jit(solution)/shard_map/ppermute | solution.py:127
  31.2 4.4 %collective-permute-start.13 = (bf16[64,256]{1,0:T(8,128)(2,1)}, bf16[64,256]{1,0:T(8,128)(2,1)S(1)}, u32[]{:S(2)}, u32[]{:S(2)}) collective-permute-start(bf16[64,256]{1,0:T(8,128)(2,1)} %get-tuple-element.24), channel_id=1, source_target_pairs={{0,28},{4,24},{8,20},{12,16},{16,12},{20,8},{24,4},{28,0},{1,29},{... | collective-permute-start | bytes 98312 | tf_op jit(solution)/shard_map/ppermute | solution.py:127
  32.5 3.2 %collective-permute-start.7 = (bf16[64,256]{1,0:T(8,128)(2,1)}, bf16[64,256]{1,0:T(8,128)(2,1)S(1)}, u32[]{:S(2)}, u32[]{:S(2)}) collective-permute-start(bf16[64,256]{1,0:T(8,128)(2,1)} %get-tuple-element.18), channel_id=1, source_target_pairs={{0,4},{4,0},{8,12},{12,8},{16,20},{20,16},{24,28},{28,24},{1,5},{5... | collective-permute-start | bytes 98312 | tf_op jit(solution)/shard_map/ppermute | solution.py:127
  32.8 4.6 %copy-start.7 = (bf16[64,256]{1,0:T(8,128)(2,1)}, bf16[64,256]{1,0:T(8,128)(2,1)S(1)}, u32[]{:S(2)}) copy-start(bf16[64,256]{1,0:T(8,128)(2,1)S(1)} %collective-permute-done.10.refs_4_) | copy-start | bytes 98308
  32.8 4.2 %collective-permute-start.8 = (bf16[64,256]{1,0:T(8,128)(2,1)}, bf16[64,256]{1,0:T(8,128)(2,1)S(1)}, u32[]{:S(2)}, u32[]{:S(2)}) collective-permute-start(bf16[64,256]{1,0:T(8,128)(2,1)} %get-tuple-element.19), channel_id=1, source_target_pairs={{0,8},{4,12},{8,0},{12,4},{16,24},{20,28},{24,16},{28,20},{1,9},{5... | collective-permute-start | bytes 98312 | tf_op jit(solution)/shard_map/ppermute | solution.py:127
  33.7 3.7 %copy-start.8 = (bf16[64,256]{1,0:T(8,128)(2,1)}, bf16[64,256]{1,0:T(8,128)(2,1)S(1)}, u32[]{:S(2)}) copy-start(bf16[64,256]{1,0:T(8,128)(2,1)S(1)} %collective-permute-done.11.refs_5_) | copy-start | bytes 98308
  33.7 3.7 %collective-permute-start.9 = (bf16[64,256]{1,0:T(8,128)(2,1)}, bf16[64,256]{1,0:T(8,128)(2,1)S(1)}, u32[]{:S(2)}, u32[]{:S(2)}) collective-permute-start(bf16[64,256]{1,0:T(8,128)(2,1)} %get-tuple-element.20), channel_id=1, source_target_pairs={{0,12},{4,8},{8,4},{12,0},{16,28},{20,24},{24,20},{28,16},{1,13},{... | collective-permute-start | bytes 98312 | tf_op jit(solution)/shard_map/ppermute | solution.py:127
  34.8 2.7 %copy-start.9 = (bf16[64,256]{1,0:T(8,128)(2,1)}, bf16[64,256]{1,0:T(8,128)(2,1)S(1)}, u32[]{:S(2)}) copy-start(bf16[64,256]{1,0:T(8,128)(2,1)S(1)} %collective-permute-done.12.refs_6_) | copy-start | bytes 98308
  35.7 1.7 %copy-start.10 = (bf16[64,256]{1,0:T(8,128)(2,1)}, bf16[64,256]{1,0:T(8,128)(2,1)S(1)}, u32[]{:S(2)}) copy-start(bf16[64,256]{1,0:T(8,128)(2,1)S(1)} %collective-permute-done.13.refs_7_) | copy-start | bytes 98308
  35.7 1.8 %copy-start.11 = (bf16[64,256]{1,0:T(8,128)(2,1)}, bf16[64,256]{1,0:T(8,128)(2,1)S(1)}, u32[]{:S(2)}) copy-start(bf16[64,256]{1,0:T(8,128)(2,1)S(1)} %collective-permute-done.7.refs_1_) | copy-start | bytes 98308
  36.9 0.6 %copy-start.12 = (bf16[64,256]{1,0:T(8,128)(2,1)}, bf16[64,256]{1,0:T(8,128)(2,1)S(1)}, u32[]{:S(2)}) copy-start(bf16[64,256]{1,0:T(8,128)(2,1)S(1)} %collective-permute-done.8.refs_2_) | copy-start | bytes 98308
  37.4 0.6 %copy-start.13 = (bf16[64,256]{1,0:T(8,128)(2,1)}, bf16[64,256]{1,0:T(8,128)(2,1)S(1)}, u32[]{:S(2)}) copy-start(bf16[64,256]{1,0:T(8,128)(2,1)S(1)} %collective-permute-done.9.refs_3_) | copy-start | bytes 98308
  39.8 4.4 %collective-permute-start.14 = (bf16[64,64]{1,0:T(8,128)(2,1)}, bf16[64,64]{1,0:T(8,128)(2,1)S(1)}, u32[]{:S(2)}, u32[]{:S(2)}) collective-permute-start(bf16[64,64]{1,0:T(8,128)(2,1)} %get-tuple-element.26), channel_id=1, source_target_pairs={{0,1},{1,0},{2,3},{3,2},{4,5},{5,4},{6,7},{7,6},{8,9},{9,8},{10,11... | collective-permute-start | bytes 24584 | tf_op jit(solution)/shard_map/ppermute | solution.py:127
  41.4 5.0 %collective-permute-start.15 = (bf16[64,64]{1,0:T(8,128)(2,1)}, bf16[64,64]{1,0:T(8,128)(2,1)S(1)}, u32[]{:S(2)}, u32[]{:S(2)}) collective-permute-start(bf16[64,64]{1,0:T(8,128)(2,1)} %get-tuple-element.27), channel_id=1, source_target_pairs={{0,2},{1,3},{2,0},{3,1},{4,6},{5,7},{6,4},{7,5},{8,10},{9,11},{10,... | collective-permute-start | bytes 24584 | tf_op jit(solution)/shard_map/ppermute | solution.py:127
  44.0 5.7 %collective-permute-start.16 = (bf16[64,64]{1,0:T(8,128)(2,1)}, bf16[64,64]{1,0:T(8,128)(2,1)S(1)}, u32[]{:S(2)}, u32[]{:S(2)}) collective-permute-start(bf16[64,64]{1,0:T(8,128)(2,1)} %get-tuple-element.28), channel_id=1, source_target_pairs={{0,3},{1,2},{2,1},{3,0},{4,7},{5,6},{6,5},{7,4},{8,11},{9,10},{10,... | collective-permute-start | bytes 24584 | tf_op jit(solution)/shard_map/ppermute | solution.py:127
  44.2 5.5 %copy-start.14 = (bf16[64,64]{1,0:T(8,128)(2,1)}, bf16[64,64]{1,0:T(8,128)(2,1)S(1)}, u32[]{:S(2)}) copy-start(bf16[64,64]{1,0:T(8,128)(2,1)S(1)} %collective-permute-done.14.refs_1_) | copy-start | bytes 24580
  46.4 3.4 %copy-start.15 = (bf16[64,64]{1,0:T(8,128)(2,1)}, bf16[64,64]{1,0:T(8,128)(2,1)S(1)}, u32[]{:S(2)}) copy-start(bf16[64,64]{1,0:T(8,128)(2,1)S(1)} %collective-permute-done.15.refs_2_) | copy-start | bytes 24580
  49.7 0.6 %copy-start.16 = (bf16[64,64]{1,0:T(8,128)(2,1)}, bf16[64,64]{1,0:T(8,128)(2,1)S(1)}, u32[]{:S(2)}) copy-start(bf16[64,64]{1,0:T(8,128)(2,1)S(1)} %collective-permute-done.16.refs_3_) | copy-start | bytes 24580

commit v2 on v1

v2 whole, which is shorter than its diff:
```python
import functools

import jax
import jax.numpy as jnp
from jax import lax
from jax.experimental import pallas as pl
from jax.experimental.pallas import tpu as pltpu
from jax.sharding import PartitionSpec as P

HIGHEST = lax.Precision.HIGHEST
VMEM = pl.BlockSpec(memory_space=pltpu.VMEM)
SMEM = pl.BlockSpec(memory_space=pltpu.SMEM)
LANES = 128
CHUNKS = 4


def iota(shape, dimension):
    return lax.broadcasted_iota(jnp.int32, shape, dimension)


def bit_reversed(size):
    bits = size.bit_length() - 1
    return [sum(((p >> b) & 1) << (bits - 1 - b) for b in range(bits)) for p in range(size)]


def parts_of(value):
    parts = []
    for _ in range(3):
        part = value.astype(jnp.bfloat16)
        value = value - part.astype(jnp.float32)
        parts.append(part)
    return parts


def condition_kernel(
    holders, groups, per_holder, count_ref, at_ref, query_ref, out_factor_ref, in_factor_ref, home_ref, cand_ref, packed_ref
):
    rows, width = query_ref.shape
    layers, rank, _ = in_factor_ref.shape
    half = rank // 2
    query = query_ref[...].astype(jnp.float32)
    low = iota((half, LANES), 1) < rank
    zero = jnp.zeros((rank, rank), jnp.float32)
    source = iota((rank, rank), 0)
    place = iota((rank, rank), 1)
    split = (source == 2 * (place % half) + place // half).astype(jnp.float32)
    for layer in range(layers):
        first = layer * half
        packed = jnp.concatenate(
            [query[:, (first + t) * LANES:(first + t + 1) * LANES] for t in range(half)], axis=0
        ).astype(jnp.bfloat16)
        factor = in_factor_ref[layer]
        doubled = jnp.concatenate(
            [jnp.concatenate([factor, zero], axis=1), jnp.concatenate([zero, factor], axis=1)], axis=0
        )
        right = sum(jnp.dot(packed, part, preferred_element_type=jnp.float32) for part in parts_of(doubled)[::-1])
        right = jnp.swapaxes(right.reshape(half, rows, LANES), 0, 1)
        wide = jnp.concatenate([right[q] for q in range(rows)], axis=1)
        sorted_columns = jnp.dot(out_factor_ref[layer], split, precision=HIGHEST, preferred_element_type=jnp.float32)
        sorted_both = lax.dot_general(
            split, sorted_columns, (((0,), (0,)), ((), ())), precision=HIGHEST, preferred_element_type=jnp.float32
        )
        quarters = jnp.concatenate(
            [sorted_both[r * half:(r + 1) * half, c * half:(c + 1) * half] for r in range(2) for c in range(2)], axis=0
        )
        left = jnp.dot(quarters, wide, precision=HIGHEST, preferred_element_type=jnp.float32)
        done = []
        for q in range(rows):
            part = left[:, q * LANES:(q + 1) * LANES]
            ee, eo, oe, oo = (part[i * half:(i + 1) * half] for i in range(4))
            done.append(jnp.where(low, ee, oo) + pltpu.roll(jnp.where(low, oe, eo), rank, 1))
        done = jnp.swapaxes(jnp.stack(done), 0, 1)
        for t in range(half):
            packed_ref[:, (first + t) * LANES:(first + t + 1) * LANES] = done[t].astype(jnp.bfloat16)

    slots = cand_ref.shape[1]
    share = slots // groups
    home_rows = home_ref.shape[0]
    wanted = jnp.where(iota((1, slots), 1) < count_ref[0], cand_ref[...], -1)
    ranges = [wanted[:, g * share:(g + 1) * share] for g in range(groups)]
    ordered = []
    for j in bit_reversed(groups):
        chosen = ranges[0]
        for g in range(1, groups):
            chosen = jnp.where((at_ref[0] ^ j) == g, ranges[g], chosen)
        ordered.append(chosen)
    wanted = jnp.concatenate(ordered, axis=1)
    known = jnp.maximum(wanted, 0)
    onehot = (iota((LANES, slots), 0) == known % LANES).astype(jnp.float32).astype(jnp.bfloat16)
    home = home_ref[...]
    table = jnp.concatenate([home // per_holder, home % per_holder], axis=0).astype(jnp.float32).astype(jnp.bfloat16)
    found = jnp.dot(table, onehot, preferred_element_type=jnp.float32)
    mine = iota((home_rows, slots), 0) == known // LANES
    holder = jnp.sum(jnp.where(mine, found[:home_rows], 0.0), axis=0, keepdims=True)
    within = jnp.sum(jnp.where(mine, found[home_rows:], 0.0), axis=0, keepdims=True)
    holder = jnp.where(wanted >= 0, holder, float(holders))
    rest = jnp.zeros((rows - 2, slots), jnp.float32)
    packed_ref[:, width:] = jnp.concatenate([holder, within, rest], axis=0).astype(jnp.bfloat16)


def score_kernel(holders, me_ref, *refs):
    packed_refs, pages_ref = refs[:holders], refs[holders]
    keep_ref, send_ref, total = refs[holders + 1:]
    me = me_ref[0]
    count, width = pages_ref.shape
    rows = packed_refs[0].shape[0]
    slots = packed_refs[0].shape[1] - width
    step = width // CHUNKS
    scores = jnp.zeros((holders * rows, count), jnp.float32)
    for i in range(CHUNKS):
        columns = slice(i * step, (i + 1) * step)
        queries = jnp.concatenate([ref[:, columns].astype(jnp.float32) for ref in packed_refs], axis=0)
        scores = scores + lax.dot_general(
            queries.astype(jnp.bfloat16), pages_ref[:, columns], (((1,), (1,)), ((), ())),
            preferred_element_type=jnp.float32,
        )
    for k in range(holders):
        start = pl.multiple_of((me ^ k) * rows, rows)
        total[pl.ds(start, rows), :] = scores[k * rows:(k + 1) * rows]
    ordered = total[...].astype(jnp.bfloat16)
    page = iota((count, slots), 0).astype(jnp.float32)
    here = me.astype(jnp.float32)
    for place, k in enumerate(bit_reversed(holders)):
        notes = packed_refs[k][:, width:].astype(jnp.float32)
        chosen = jnp.where(notes[0:1] == here, notes[1:2], -1.0)
        onehot = (page == chosen).astype(jnp.float32).astype(jnp.bfloat16)
        picked = jnp.dot(ordered, onehot, preferred_element_type=jnp.float32).astype(jnp.bfloat16)
        target = (keep_ref, send_ref)[place // (holders // 2)]
        target[place % (holders // 2)] = picked


def add_kernel(one_ref, other_ref, out_ref):
    out_ref[0] = (one_ref[...] + other_ref[...]).T


def swap(value, axis, distance):
    size = lax.axis_size(axis)
    return lax.ppermute(value, axis, [(i, i ^ distance) for i in range(size)])


def on_device(query_grads, factor_out, factor_in, page_store, page_home, cand_lists, counts):
    holders = lax.axis_size("store")
    groups = lax.axis_size("layer")
    rows, width = query_grads.shape
    layers, rank, _ = factor_out.shape
    per_holder = page_store.shape[0]
    slots = cand_lists.shape[1]
    bf16 = jnp.bfloat16
    store_at = lax.axis_index("store").astype(jnp.int32).reshape(1)
    layer_at = lax.axis_index("layer").astype(jnp.int32).reshape(1)

    packed = pl.pallas_call(
        functools.partial(condition_kernel, holders, groups, per_holder),
        out_shape=jax.ShapeDtypeStruct((rows, width + slots), bf16),
        in_specs=[SMEM] * 2 + [VMEM] * 5,
        out_specs=VMEM,
        compiler_params=pltpu.CompilerParams(vmem_limit_bytes=8 * 2**20),
    )(counts, layer_at, query_grads, factor_out, factor_in, page_home.reshape(-1, LANES), cand_lists)

    blocks = [None] * holders
    blocks[0] = packed
    blocks[1] = swap(packed, "store", 1)
    for k in range(2, holders, 2):
        blocks[k] = swap(packed, "store", k)
    for k in range(2, holders, 2):
        blocks[k + 1] = swap(blocks[k], "store", 1)

    total = holders * rows
    bytes_out = 2 * holders * total * slots
    bytes_in = 2 * holders * rows * (width + slots) + 2 * per_holder * width
    keep, send = pl.pallas_call(
        functools.partial(score_kernel, holders),
        out_shape=[jax.ShapeDtypeStruct((holders // 2, total, slots), bf16)] * 2,
        in_specs=[SMEM] + [VMEM] * (holders + 1),
        out_specs=[VMEM] * 2,
        scratch_shapes=[pltpu.VMEM((total, per_holder), jnp.float32)],
        compiler_params=pltpu.CompilerParams(vmem_limit_bytes=8 * 2**20 + bytes_in + bytes_out),
    )(store_at, *blocks, page_store)

    distance = 1
    while True:
        landed = swap(send, "store", distance)
        distance *= 2
        if distance == holders:
            break
        cut = keep.shape[0] // 2
        keep, send = keep[:cut] + landed[:cut], keep[cut:] + landed[cut:]
    scores = (keep + landed)[0]

    distance = 1
    while distance < groups:
        cut = scores.shape[1] // 2
        landed = swap(scores[:, cut:], "layer", distance).astype(jnp.float32)
        keep = scores[:, :cut].astype(jnp.float32)
        distance *= 2
        if distance < groups:
            scores = keep + landed
    return pl.pallas_call(
        add_kernel,
        out_shape=jax.ShapeDtypeStruct((1, slots // groups, total), jnp.float32),
        in_specs=[VMEM] * 2,
        out_specs=VMEM,
        compiler_params=pltpu.CompilerParams(vmem_limit_bytes=2 * 2**20),
    )(keep, landed)


def solution(mesh):
    placed = (
        P("store", "layer"),
        P("layer", None, None),
        P("layer", None, None),
        P("store", "layer"),
        P(),
        P("store", None),
        P("store"),
    )
    return jax.shard_map(
        on_device, mesh=mesh, in_specs=placed, out_specs=P("store", "layer", None), check_vma=False
    )
```

time: 52.1 us -> 42.1 us (0.81)
  Pallas kernels: 12.8 us -> 4.44 us
  starting transfers between devices: 15.7 us -> 13.4 us
  waiting for transfers between devices: 16.2 us -> 17 us
    pallas_call x1, Pallas kernels: 6.23 us -> 1.91 us  [on_device(): pl.pallas_call(functools.partial(score_kernel, holders), out_shape=[jax.S...]
    unnamed x34 -> x12, local copies, waits for them, and re-layouts: 1.83 us -> 6.14 us
    pallas_call x3 -> x2, Pallas kernels: 6.56 us -> 2.53 us  [the longest x1 1.83 us: on_device(): pl.pallas_call(functools.partial(condition_kernel, holders, groups, per_h...]
    reshape x1 -> x0, local copies, waits for them, and re-layouts: 2.99 us -> none  [on_device(): out_factor = factor_out.reshape(layers, rank // 2, 2, rank // 2, 2)]
    ppermute x17 -> x12, starting transfers between devices: 15.7 us -> 13.4 us  [swap(): return lax.ppermute(value, axis, [(i, i ^ distance) for i in range(size)])]
    transpose x1 -> x0, local copies, waits for them, and re-layouts: 1.54 us -> none  [on_device(): out_factor.transpose(0, 2, 4, 1, 3).reshape(layers, 2 * rank, rank // 2)]
    ppermute x17 -> x12, waiting for transfers between devices: 16.2 us -> 17 us  [swap(): return lax.ppermute(value, axis, [(i, i ^ distance) for i in range(size)])]
  transfers between devices with their start and end apart: 17 -> 12, of which waited for: 10 -> 10; matrix products, arithmetic and copies ran while one was open for 0% -> 0% of each run, Pallas kernels for 0% -> 0%
where the time goes in v2:
time: 42.1 us; the launch traced here: 41.7 us
  waiting for transfers between devices  17 us (40%)
  starting transfers between devices  13.4 us (32%)
  local copies, waits for them, and re-layouts  6.22 us (15%)
  Pallas kernels  4.44 us (11%)
  between operations  0.7 us (2%)
    ppermute x12, waiting for transfers between devices, swap(): return lax.ppermute(value, axis, [(i, i ^ distance) for i in range(size)])  17 us
    ppermute x12, starting transfers between devices, swap(): return lax.ppermute(value, axis, [(i, i ^ distance) for i in range(size)])  13.4 us
    unnamed x12, local copies, waits for them, and re-layouts  6.14 us
    pallas_call x1, Pallas kernels, on_device(): pl.pallas_call(functools.partial(score_kernel, holders), out_shape=[jax.S...  1.91 us
    pallas_call x1, Pallas kernels, on_device(): pl.pallas_call(functools.partial(condition_kernel, holders, groups, per_h...  1.83 us
  transfers between devices with their start and end apart: 12, of which 10 were waited for; matrix products, arithmetic and copies ran while one was open for 0% of the time, Pallas kernels for 0%

profile of v2, /device:TPU:0, one launch (start us, length us, event | category | flops | bytes accessed | tf_op | source)
XLA Modules:
  0.0 41.7 jit_solution(5568259981244218381)
XLA Ops:
  0.7 0.0 copy-start.1
  0.7 0.9 %copy-done.1 = bf16[8,8192]{1,0:T(8,128)(2,1)S(1)} copy-done((bf16[8,8192]{1,0:T(8,128)(2,1)S(1)}, bf16[8,8192]{1,0:T(8,128)(2,1)}, u32[]{:S(2)}) %copy-start.1) | copy-done | bytes 131096
  1.6 0.0 copy-start.2
  1.6 0.8 %copy-done.2 = f32[2,64,64]{2,1,0:T(8,128)S(1)} copy-done((f32[2,64,64]{2,1,0:T(8,128)S(1)}, f32[2,64,64]{2,1,0:T(8,128)}, u32[]{:S(2)}) %copy-start.2) | copy-done | bytes 32792
  2.4 0.0 copy-start.3
  2.4 0.8 %copy-done.3 = f32[2,64,64]{2,1,0:T(8,128)S(1)} copy-done((f32[2,64,64]{2,1,0:T(8,128)S(1)}, f32[2,64,64]{2,1,0:T(8,128)}, u32[]{:S(2)}) %copy-start.3) | copy-done | bytes 32792
  3.2 0.0 copy-start.4
  3.2 0.7 %copy-done.4 = s32[2048]{0:T(1024)S(1)} copy-done((s32[2048]{0:T(1024)S(1)}, s32[2048]{0:T(1024)}, u32[]{:S(2)}) %copy-start.4) | copy-done | bytes 8216
  3.9 0.0 copy-start.5
  3.9 0.7 %copy-done.5 = s32[1,256]{1,0:T(1,128)S(1)} copy-done((s32[1,256]{1,0:T(1,128)S(1)}, s32[1,256]{1,0:T(1,128)}, u32[]{:S(2)}) %copy-start.5) | copy-done | bytes 1048
  4.6 1.8 %shard_map.73.refs_0_ = bf16[8,8448]{1,0:T(8,128)(2,1)S(1)} custom-call(s32[1]{0:T(128)S(6)} %copy.8.count_ref, s32[1]{0:T(128)} %bitcast.1.at_ref, bf16[8,8192]{1,0:T(8,128)(2,1)S(1)} %copy-done.1, f32[2,64,64]{2,1,0:T(8,128)S(1)} %copy-done.2, f32[2,64,64]{2,1,0:T(8,128)S(1)} %copy-done.3, s32[16,128]{1,0:T(8,128)S(1)} %bitcast.5, s32[1,256]{1,0:T(1,128)S(1)} %copy-done.5), custom_call_target="tpu_custom_call" | custom-call | tf_op jit(solution)/shard_map/pallas_call | solution.py:152
  6.5 4.0 %collective-permute-start.5 = (bf16[8,8448]{1,0:T(8,128)(2,1)S(1)}, bf16[8,8448]{1,0:T(8,128)(2,1)S(1)}, u32[]{:S(2)}, u32[]{:S(2)}) collective-permute-start(bf16[8,8448]{1,0:T(8,128)(2,1)S(1)} %shard_map.73.refs_0_), channel_id=1, source_target_pairs={{0,24},{4,28},{8,16},{12,20},{16,8},{20,12},{24,0},{28,4},{1,25},{... | collective-permute-start | bytes 405512 | tf_op jit(solution)/shard_map/ppermute | solution.py:138
  10.4 0.5 %collective-permute-start.3 = (bf16[8,8448]{1,0:T(8,128)(2,1)S(1)}, bf16[8,8448]{1,0:T(8,128)(2,1)S(1)}, u32[]{:S(2)}, u32[]{:S(2)}) collective-permute-start(bf16[8,8448]{1,0:T(8,128)(2,1)S(1)} %shard_map.73.refs_0_), channel_id=1, source_target_pairs={{0,16},{4,20},{8,24},{12,28},{16,0},{20,4},{24,8},{28,12},{1,17},{... | collective-permute-start | bytes 405512 | tf_op jit(solution)/shard_map/ppermute | solution.py:138
  10.9 0.1 collective-permute-start.1
  11.1 0.0 collective-permute-start
  11.1 3.3 %collective-permute-done.5.refs_6_ = bf16[8,8448]{1,0:T(8,128)(2,1)S(1)} collective-permute-done((bf16[8,8448]{1,0:T(8,128)(2,1)S(1)}, bf16[8,8448]{1,0:T(8,128)(2,1)S(1)}, u32[]{:S(2)}, u32[]{:S(2)}) %collective-permute-start.5) | collective-permute-done | bytes 135200 | tf_op jit(solution)/shard_map/ppermute | solution.py:138
  14.4 0.0 collective-permute-start.6
  14.4 2.5 %collective-permute-done.3.refs_4_ = bf16[8,8448]{1,0:T(8,128)(2,1)S(1)} collective-permute-done((bf16[8,8448]{1,0:T(8,128)(2,1)S(1)}, bf16[8,8448]{1,0:T(8,128)(2,1)S(1)}, u32[]{:S(2)}, u32[]{:S(2)}) %collective-permute-start.3) | collective-permute-done | bytes 135200 | tf_op jit(solution)/shard_map/ppermute | solution.py:138
  16.9 0.0 collective-permute-start.4
  16.9 0.2 collective-permute-done.1.refs_2_
  17.1 0.3 collective-permute-start.2
  17.4 0.0 collective-permute-done.refs_1_
  17.4 0.0 collective-permute-done.6.refs_7_
  17.4 0.8 %collective-permute-done.4.refs_5_ = bf16[8,8448]{1,0:T(8,128)(2,1)S(1)} collective-permute-done((bf16[8,8448]{1,0:T(8,128)(2,1)S(1)}, bf16[8,8448]{1,0:T(8,128)(2,1)S(1)}, u32[]{:S(2)}, u32[]{:S(2)}) %collective-permute-start.4) | collective-permute-done | bytes 135200 | tf_op jit(solution)/shard_map/ppermute | solution.py:138
  18.2 0.3 collective-permute-done.2.refs_3_
  18.5 0.0 copy-start
  18.5 2.2 %copy-done = bf16[256,8192]{1,0:T(8,128)(2,1)S(1)} copy-done((bf16[256,8192]{1,0:T(8,128)(2,1)S(1)}, bf16[256,8192]{1,0:T(8,128)(2,1)}, u32[]{:S(2)}) %copy-start) | copy-done | bytes 4194328
  20.7 1.9 %shard_map.74 = (bf16[4,64,256]{2,1,0:T(8,128)(2,1)S(1)}, bf16[4,64,256]{2,1,0:T(8,128)(2,1)S(1)}) custom-call(s32[1]{0:T(128)} %bitcast.me_ref, bf16[8,8448]{1,0:T(8,128)(2,1)S(1)} %shard_map.73.refs_0_, bf16[8,8448]{1,0:T(8,128)(2,1)S(1)} %collective-permute-done.refs_1_, bf16[8,8448]{1,0:T(8,128)(2,1)S(1)} %collective-permute-done.1.refs_2_, ...), custom_call_target="tpu_custom_call" | custom-call | tf_op jit(solution)/shard_map/pallas_call | solution.py:171
  22.6 0.3 collective-permute-start.7
  22.9 1.1 %collective-permute-done.7 = bf16[4,64,256]{2,1,0:T(8,128)(2,1)S(1)} collective-permute-done((bf16[4,64,256]{2,1,0:T(8,128)(2,1)S(1)}, bf16[4,64,256]{2,1,0:T(8,128)(2,1)S(1)}, u32[]{:S(2)}, u32[]{:S(2)}) %collective-permute-start.7) | collective-permute-done | bytes 131104 | tf_op jit(solution)/shard_map/ppermute | solution.py:138
  24.0 1.7 %collective-permute-start.8 = (bf16[2,64,256]{2,1,0:T(8,128)(2,1)S(1)}, bf16[2,64,256]{2,1,0:T(8,128)(2,1)S(1)}, u32[]{:S(2)}, u32[]{:S(2)}) collective-permute-start(bf16[2,64,256]{2,1,0:T(8,128)(2,1)S(1)} %get-tuple-element.10), channel_id=1, source_target_pairs={{0,8},{4,12},{8,0},{12,4},{16,24},{20,28},{24,16},{28,20},{1,9},{5... | collective-permute-start | bytes 196616 | tf_op jit(solution)/shard_map/ppermute | solution.py:138
  25.7 2.6 %collective-permute-done.8 = bf16[2,64,256]{2,1,0:T(8,128)(2,1)S(1)} collective-permute-done((bf16[2,64,256]{2,1,0:T(8,128)(2,1)S(1)}, bf16[2,64,256]{2,1,0:T(8,128)(2,1)S(1)}, u32[]{:S(2)}, u32[]{:S(2)}) %collective-permute-start.8) | collective-permute-done | bytes 65568 | tf_op jit(solution)/shard_map/ppermute | solution.py:138
  28.4 1.7 %collective-permute-start.9 = (bf16[1,64,256]{2,1,0:T(8,128)(2,1)S(1)}, bf16[1,64,256]{2,1,0:T(8,128)(2,1)S(1)}, u32[]{:S(2)}, u32[]{:S(2)}) collective-permute-start(bf16[1,64,256]{2,1,0:T(8,128)(2,1)S(1)} %slice_add_fusion.2), channel_id=1, source_target_pairs={{0,16},{4,20},{8,24},{12,28},{16,0},{20,4},{24,8},{28,12},{1,17},{... | collective-permute-start | bytes 98312 | tf_op jit(solution)/shard_map/ppermute | solution.py:138
  30.1 2.2 %collective-permute-done.9 = bf16[1,64,256]{2,1,0:T(8,128)(2,1)S(1)} collective-permute-done((bf16[1,64,256]{2,1,0:T(8,128)(2,1)S(1)}, bf16[1,64,256]{2,1,0:T(8,128)(2,1)S(1)}, u32[]{:S(2)}, u32[]{:S(2)}) %collective-permute-start.9) | collective-permute-done | bytes 32800 | tf_op jit(solution)/shard_map/ppermute | solution.py:138
  32.3 1.8 %collective-permute-start.10 = (bf16[64,128]{1,0:T(8,128)(2,1)S(1)}, bf16[64,128]{1,0:T(8,128)(2,1)S(1)}, u32[]{:S(2)}, u32[]{:S(2)}) collective-permute-start(bf16[64,128]{1,0:T(8,128)(2,1)S(1)} %slice.55), channel_id=1, source_target_pairs={{0,1},{1,0},{2,3},{3,2},{4,5},{5,4},{6,7},{7,6},{8,9},{9,8},{10,11... | collective-permute-start | bytes 49160 | tf_op jit(solution)/shard_map/ppermute | solution.py:138
  34.1 2.0 %collective-permute-done.10 = bf16[64,128]{1,0:T(8,128)(2,1)S(1)} collective-permute-done((bf16[64,128]{1,0:T(8,128)(2,1)S(1)}, bf16[64,128]{1,0:T(8,128)(2,1)S(1)}, u32[]{:S(2)}, u32[]{:S(2)}) %collective-permute-start.10) | collective-permute-done | bytes 16416 | tf_op jit(solution)/shard_map/ppermute | solution.py:138
  36.1 0.1 fusion.2
  36.2 3.0 %collective-permute-start.11 = (f32[64,64]{1,0:T(8,128)S(1)}, f32[64,64]{1,0:T(8,128)S(1)}, u32[]{:S(2)}, u32[]{:S(2)}) collective-permute-start(f32[64,64]{1,0:T(8,128)S(1)} %get-tuple-element.11), channel_id=1, source_target_pairs={{0,2},{1,3},{2,0},{3,1},{4,6},{5,7},{6,4},{7,5},{8,10},{9,11},{10,... | collective-permute-start | bytes 49160 | tf_op jit(solution)/shard_map/ppermute | solution.py:138
  39.2 1.9 %collective-permute-done.11.other_ref = f32[64,64]{1,0:T(8,128)S(1)} collective-permute-done((f32[64,64]{1,0:T(8,128)S(1)}, f32[64,64]{1,0:T(8,128)S(1)}, u32[]{:S(2)}, u32[]{:S(2)}) %collective-permute-start.11) | collective-permute-done | bytes 16416 | tf_op jit(solution)/shard_map/ppermute | solution.py:138
  41.0 0.7 %shard_map.75 = f32[1,64,64]{2,1,0:T(8,128)} custom-call(f32[64,64]{1,0:T(8,128)S(1)} %get-tuple-element.12.one_ref, f32[64,64]{1,0:T(8,128)S(1)} %collective-permute-done.11.other_ref), custom_call_target="tpu_custom_call" | custom-call | tf_op jit(solution)/shard_map/pallas_call | solution.py:198
  (5 shorter events, 0.0 us)
Async XLA Ops:
  0.7 0.9 %copy-start.1 = (bf16[8,8192]{1,0:T(8,128)(2,1)S(1)}, bf16[8,8192]{1,0:T(8,128)(2,1)}, u32[]{:S(2)}) copy-start(bf16[8,8192]{1,0:T(8,128)(2,1)} %query_ref.1) | copy-start | bytes 393220
  1.6 0.8 %copy-start.2 = (f32[2,64,64]{2,1,0:T(8,128)S(1)}, f32[2,64,64]{2,1,0:T(8,128)}, u32[]{:S(2)}) copy-start(f32[2,64,64]{2,1,0:T(8,128)} %out_factor_ref.1) | copy-start | bytes 98308
  2.4 0.8 %copy-start.3 = (f32[2,64,64]{2,1,0:T(8,128)S(1)}, f32[2,64,64]{2,1,0:T(8,128)}, u32[]{:S(2)}) copy-start(f32[2,64,64]{2,1,0:T(8,128)} %in_factor_ref.1) | copy-start | bytes 98308
  3.2 0.7 %copy-start.4 = (s32[2048]{0:T(1024)S(1)}, s32[2048]{0:T(1024)}, u32[]{:S(2)}) copy-start(s32[2048]{0:T(1024)} %param.11) | copy-start | bytes 24580
  3.9 0.7 %copy-start.5 = (s32[1,256]{1,0:T(1,128)S(1)}, s32[1,256]{1,0:T(1,128)}, u32[]{:S(2)}) copy-start(s32[1,256]{1,0:T(1,128)} %cand_ref.1) | copy-start | bytes 3076
  6.5 8.0 %collective-permute-start.5 = (bf16[8,8448]{1,0:T(8,128)(2,1)S(1)}, bf16[8,8448]{1,0:T(8,128)(2,1)S(1)}, u32[]{:S(2)}, u32[]{:S(2)}) collective-permute-start(bf16[8,8448]{1,0:T(8,128)(2,1)S(1)} %shard_map.73.refs_0_), channel_id=1, source_target_pairs={{0,24},{4,28},{8,16},{12,20},{16,8},{20,12},{24,0},{28,4},{1,25},{... | collective-permute-start | bytes 405512 | tf_op jit(solution)/shard_map/ppermute | solution.py:138
  10.4 6.5 %collective-permute-start.3 = (bf16[8,8448]{1,0:T(8,128)(2,1)S(1)}, bf16[8,8448]{1,0:T(8,128)(2,1)S(1)}, u32[]{:S(2)}, u32[]{:S(2)}) collective-permute-start(bf16[8,8448]{1,0:T(8,128)(2,1)S(1)} %shard_map.73.refs_0_), channel_id=1, source_target_pairs={{0,16},{4,20},{8,24},{12,28},{16,0},{20,4},{24,8},{28,12},{1,17},{... | collective-permute-start | bytes 405512 | tf_op jit(solution)/shard_map/ppermute | solution.py:138
  10.9 6.2 %collective-permute-start.1 = (bf16[8,8448]{1,0:T(8,128)(2,1)S(1)}, bf16[8,8448]{1,0:T(8,128)(2,1)S(1)}, u32[]{:S(2)}, u32[]{:S(2)}) collective-permute-start(bf16[8,8448]{1,0:T(8,128)(2,1)S(1)} %shard_map.73.refs_0_), channel_id=1, source_target_pairs={{0,8},{4,12},{8,0},{12,4},{16,24},{20,28},{24,16},{28,20},{1,9},{5... | collective-permute-start | bytes 405512 | tf_op jit(solution)/shard_map/ppermute | solution.py:138
  11.1 6.4 %collective-permute-start = (bf16[8,8448]{1,0:T(8,128)(2,1)S(1)}, bf16[8,8448]{1,0:T(8,128)(2,1)S(1)}, u32[]{:S(2)}, u32[]{:S(2)}) collective-permute-start(bf16[8,8448]{1,0:T(8,128)(2,1)S(1)} %shard_map.73.refs_0_), channel_id=1, source_target_pairs={{0,4},{4,0},{8,12},{12,8},{16,20},{20,16},{24,28},{28,24},{1,5},{5... | collective-permute-start | bytes 405512 | tf_op jit(solution)/shard_map/ppermute | solution.py:138
  14.4 3.0 %collective-permute-start.6 = (bf16[8,8448]{1,0:T(8,128)(2,1)S(1)}, bf16[8,8448]{1,0:T(8,128)(2,1)S(1)}, u32[]{:S(2)}, u32[]{:S(2)}) collective-permute-start(bf16[8,8448]{1,0:T(8,128)(2,1)S(1)} %collective-permute-done.5.refs_6_), channel_id=1, source_target_pairs={{0,4},{4,0},{8,12},{12,8},{16,20},{20,16},{24,28},{28,24},{1,5},{5... | collective-permute-start | bytes 405512 | tf_op jit(solution)/shard_map/ppermute | solution.py:138
  16.9 1.4 %collective-permute-start.4 = (bf16[8,8448]{1,0:T(8,128)(2,1)S(1)}, bf16[8,8448]{1,0:T(8,128)(2,1)S(1)}, u32[]{:S(2)}, u32[]{:S(2)}) collective-permute-start(bf16[8,8448]{1,0:T(8,128)(2,1)S(1)} %collective-permute-done.3.refs_4_), channel_id=1, source_target_pairs={{0,4},{4,0},{8,12},{12,8},{16,20},{20,16},{24,28},{28,24},{1,5},{5... | collective-permute-start | bytes 405512 | tf_op jit(solution)/shard_map/ppermute | solution.py:138
  17.1 1.4 %collective-permute-start.2 = (bf16[8,8448]{1,0:T(8,128)(2,1)S(1)}, bf16[8,8448]{1,0:T(8,128)(2,1)S(1)}, u32[]{:S(2)}, u32[]{:S(2)}) collective-permute-start(bf16[8,8448]{1,0:T(8,128)(2,1)S(1)} %collective-permute-done.1.refs_2_), channel_id=1, source_target_pairs={{0,4},{4,0},{8,12},{12,8},{16,20},{20,16},{24,28},{28,24},{1,5},{5... | collective-permute-start | bytes 405512 | tf_op jit(solution)/shard_map/ppermute | solution.py:138
  18.5 2.2 %copy-start = (bf16[256,8192]{1,0:T(8,128)(2,1)S(1)}, bf16[256,8192]{1,0:T(8,128)(2,1)}, u32[]{:S(2)}) copy-start(bf16[256,8192]{1,0:T(8,128)(2,1)} %refs_8_.1) | copy-start | bytes 12582916
  22.6 1.4 %collective-permute-start.7 = (bf16[4,64,256]{2,1,0:T(8,128)(2,1)S(1)}, bf16[4,64,256]{2,1,0:T(8,128)(2,1)S(1)}, u32[]{:S(2)}, u32[]{:S(2)}) collective-permute-start(bf16[4,64,256]{2,1,0:T(8,128)(2,1)S(1)} %get-tuple-element.8), channel_id=1, source_target_pairs={{0,4},{4,0},{8,12},{12,8},{16,20},{20,16},{24,28},{28,24},{1,5},{5... | collective-permute-start | bytes 393224 | tf_op jit(solution)/shard_map/ppermute | solution.py:138
  24.0 4.3 %collective-permute-start.8 = (bf16[2,64,256]{2,1,0:T(8,128)(2,1)S(1)}, bf16[2,64,256]{2,1,0:T(8,128)(2,1)S(1)}, u32[]{:S(2)}, u32[]{:S(2)}) collective-permute-start(bf16[2,64,256]{2,1,0:T(8,128)(2,1)S(1)} %get-tuple-element.10), channel_id=1, source_target_pairs={{0,8},{4,12},{8,0},{12,4},{16,24},{20,28},{24,16},{28,20},{1,9},{5... | collective-permute-start | bytes 196616 | tf_op jit(solution)/shard_map/ppermute | solution.py:138
  28.4 3.9 %collective-permute-start.9 = (bf16[1,64,256]{2,1,0:T(8,128)(2,1)S(1)}, bf16[1,64,256]{2,1,0:T(8,128)(2,1)S(1)}, u32[]{:S(2)}, u32[]{:S(2)}) collective-permute-start(bf16[1,64,256]{2,1,0:T(8,128)(2,1)S(1)} %slice_add_fusion.2), channel_id=1, source_target_pairs={{0,16},{4,20},{8,24},{12,28},{16,0},{20,4},{24,8},{28,12},{1,17},{... | collective-permute-start | bytes 98312 | tf_op jit(solution)/shard_map/ppermute | solution.py:138
  32.3 3.8 %collective-permute-start.10 = (bf16[64,128]{1,0:T(8,128)(2,1)S(1)}, bf16[64,128]{1,0:T(8,128)(2,1)S(1)}, u32[]{:S(2)}, u32[]{:S(2)}) collective-permute-start(bf16[64,128]{1,0:T(8,128)(2,1)S(1)} %slice.55), channel_id=1, source_target_pairs={{0,1},{1,0},{2,3},{3,2},{4,5},{5,4},{6,7},{7,6},{8,9},{9,8},{10,11... | collective-permute-start | bytes 49160 | tf_op jit(solution)/shard_map/ppermute | solution.py:138
  36.2 4.8 %collective-permute-start.11 = (f32[64,64]{1,0:T(8,128)S(1)}, f32[64,64]{1,0:T(8,128)S(1)}, u32[]{:S(2)}, u32[]{:S(2)}) collective-permute-start(f32[64,64]{1,0:T(8,128)S(1)} %get-tuple-element.11), channel_id=1, source_target_pairs={{0,2},{1,3},{2,0},{3,1},{4,6},{5,7},{6,4},{7,5},{8,10},{9,11},{10,... | collective-permute-start | bytes 49160 | tf_op jit(solution)/shard_map/ppermute | solution.py:138

commit v3 on v2

--- a/solution.py
+++ b/solution.py
@@ -10,6 +10,7 @@
 HIGHEST = lax.Precision.HIGHEST
 VMEM = pl.BlockSpec(memory_space=pltpu.VMEM)
 SMEM = pl.BlockSpec(memory_space=pltpu.SMEM)
+HBM = pl.BlockSpec(memory_space=pltpu.HBM)
 LANES = 128
 CHUNKS = 4
 
@@ -32,9 +33,18 @@
     return parts
 
 
-def condition_kernel(
-    holders, groups, per_holder, count_ref, at_ref, query_ref, out_factor_ref, in_factor_ref, home_ref, cand_ref, packed_ref
-):
+def condition_kernel(holders, groups, count_ref, at_ref, *refs):
+    sources, packed_ref, pages_ref, landing, arrived = refs[:6], refs[6], refs[7], refs[8:13], refs[13]
+    copies = [
+        pltpu.make_async_copy(source, target, arrived.at[i])
+        for i, (source, target) in enumerate(zip(sources, landing + (pages_ref,)))
+    ]
+    for copy in copies:
+        copy.start()
+    for copy in copies[:-1]:
+        copy.wait()
+    query_ref, in_factor_ref, out_factor_ref, home_ref, cand_ref = landing
+    per_holder = pages_ref.shape[0]
     rows, width = query_ref.shape
     layers, rank, _ = in_factor_ref.shape
     half = rank // 2
@@ -96,6 +106,7 @@
     holder = jnp.where(wanted >= 0, holder, float(holders))
     rest = jnp.zeros((rows - 2, slots), jnp.float32)
     packed_ref[:, width:] = jnp.concatenate([holder, within, rest], axis=0).astype(jnp.bfloat16)
+    copies[-1].wait()
 
 
 def score_kernel(holders, me_ref, *refs):
@@ -129,13 +140,16 @@
         target[place % (holders // 2)] = picked
 
 
-def add_kernel(one_ref, other_ref, out_ref):
-    out_ref[0] = (one_ref[...] + other_ref[...]).T
+def finish_kernel(me_ref, one_ref, other_ref, handed_ref, out_ref):
+    out_ref[0] = jnp.where(me_ref[0] % 2 == 1, one_ref[...] + other_ref[...], handed_ref[...]).T
 
 
 def swap(value, axis, distance):
-    size = lax.axis_size(axis)
-    return lax.ppermute(value, axis, [(i, i ^ distance) for i in range(size)])
+    return lax.ppermute(value, axis, [(i, i ^ distance) for i in range(lax.axis_size(axis))])
+
+
+def swap_seconds(value, distance):
+    return lax.ppermute(value, "store", [(i, i ^ distance) for i in range(1, lax.axis_size("store"), 2)])
 
 
 def on_device(query_grads, factor_out, factor_in, page_store, page_home, cand_lists, counts):
@@ -149,13 +163,22 @@
     store_at = lax.axis_index("store").astype(jnp.int32).reshape(1)
     layer_at = lax.axis_index("layer").astype(jnp.int32).reshape(1)
 
-    packed = pl.pallas_call(
-        functools.partial(condition_kernel, holders, groups, per_holder),
-        out_shape=jax.ShapeDtypeStruct((rows, width + slots), bf16),
-        in_specs=[SMEM] * 2 + [VMEM] * 5,
-        out_specs=VMEM,
-        compiler_params=pltpu.CompilerParams(vmem_limit_bytes=8 * 2**20),
-    )(counts, layer_at, query_grads, factor_out, factor_in, page_home.reshape(-1, LANES), cand_lists)
+    home = page_home.reshape(-1, LANES)
+    sources = [
+        pltpu.with_memory_space_constraint(source, pltpu.HBM)
+        for source in (query_grads, factor_in, factor_out, home, cand_lists, page_store)
+    ]
+    packed, pages = pl.pallas_call(
+        functools.partial(condition_kernel, holders, groups),
+        out_shape=[
+            jax.ShapeDtypeStruct((rows, width + slots), bf16), jax.ShapeDtypeStruct(page_store.shape, bf16)
+        ],
+        in_specs=[SMEM] * 2 + [HBM] * len(sources),
+        out_specs=[VMEM] * 2,
+        scratch_shapes=[pltpu.VMEM(source.shape, source.dtype) for source in sources[:-1]]
+        + [pltpu.SemaphoreType.DMA((len(sources),))],
+        compiler_params=pltpu.CompilerParams(vmem_limit_bytes=14 * 2**20),
+    )(counts, layer_at, *sources)
 
     blocks = [None] * holders
     blocks[0] = packed
@@ -175,33 +198,41 @@
         out_specs=[VMEM] * 2,
         scratch_shapes=[pltpu.VMEM((total, per_holder), jnp.float32)],
         compiler_params=pltpu.CompilerParams(vmem_limit_bytes=8 * 2**20 + bytes_in + bytes_out),
-    )(store_at, *blocks, page_store)
-
-    distance = 1
-    while True:
-        landed = swap(send, "store", distance)
+    )(store_at, *blocks, pages)
+
+    even, odd = keep, send
+    first_to_second = [(i, i + 1) for i in range(0, holders, 2)]
+    odd, even = (
+        odd + lax.ppermute(even, "store", first_to_second), even + lax.ppermute(odd, "store", first_to_second)
+    )
+    both = jnp.stack([even, odd])
+    distance = 2
+    while distance < holders:
+        cut = both.shape[1] // 2
+        both = both[:, :cut] + swap_seconds(both[:, cut:], distance)
         distance *= 2
-        if distance == holders:
-            break
-        cut = keep.shape[0] // 2
-        keep, send = keep[:cut] + landed[:cut], keep[cut:] + landed[cut:]
-    scores = (keep + landed)[0]
+    both = both[:, 0]
 
     distance = 1
     while distance < groups:
-        cut = scores.shape[1] // 2
-        landed = swap(scores[:, cut:], "layer", distance).astype(jnp.float32)
-        keep = scores[:, :cut].astype(jnp.float32)
+        cut = both.shape[2] // 2
+        moving = both[:, :, cut:]
+        landed = lax.ppermute(
+            moving, ("store", "layer"),
+            [(s * groups + g, s * groups + (g ^ distance)) for s in range(1, holders, 2) for g in range(groups)],
+        ).astype(jnp.float32)
+        keep = both[:, :, :cut].astype(jnp.float32)
         distance *= 2
         if distance < groups:
-            scores = keep + landed
+            both = keep + landed
+    handed = lax.ppermute(keep[1] + landed[1], "store", [(i + 1, i) for i in range(0, holders, 2)])
     return pl.pallas_call(
-        add_kernel,
+        finish_kernel,
         out_shape=jax.ShapeDtypeStruct((1, slots // groups, total), jnp.float32),
-        in_specs=[VMEM] * 2,
+        in_specs=[SMEM] + [VMEM] * 3,
         out_specs=VMEM,
         compiler_params=pltpu.CompilerParams(vmem_limit_bytes=2 * 2**20),
-    )(keep, landed)
+    )(store_at, keep[0], landed[0], handed)
 
 
 def solution(mesh):

time: 42.1 us -> 50.9 us (1.21)
  waiting for transfers between devices: 17 us -> 27.9 us
  local copies, waits for them, and re-layouts: 6.22 us -> 4.23 us
  starting transfers between devices: 13.4 us -> 12.2 us
  Pallas kernels: 4.44 us -> 5.43 us
    ppermute x12 -> x14, waiting for transfers between devices: 17 us -> 27.9 us  [the longest x1 19.7 us: on_device(): lax.ppermute(keep[1] + landed[1], 'store', [(i + 1, i) for i in range(0,...]
    unnamed x12 -> x4, local copies, waits for them, and re-layouts: 6.14 us -> 4.14 us
    ppermute x12 -> x14, starting transfers between devices: 13.4 us -> 12.2 us  [the longest x7 4.74 us: swap(): lax.ppermute(value, axis, [(i, i ^ distance) for i in range(lax.axis_size...]
    pallas_call x2, Pallas kernels: 2.53 us -> 3.52 us  [the longest x1 2.82 us: on_device(): pl.pallas_call(functools.partial(condition_kernel, holders, groups), out_...]
  transfers between devices with their start and end apart: 12 -> 14, of which waited for: 10 -> 7; matrix products, arithmetic and copies ran while one was open for 0% -> 0% of each run, Pallas kernels for 0% -> 0%
where the time goes in v3:
time: 50.9 us; the launch traced here: 50.7 us
  waiting for transfers between devices  27.9 us (55%)
  starting transfers between devices  12.2 us (24%)
  Pallas kernels  5.43 us (11%)
  local copies, waits for them, and re-layouts  4.23 us (8%)
  between operations  0.84 us (2%)
    ppermute x1, waiting for transfers between devices, on_device(): lax.ppermute(keep[1] + landed[1], 'store', [(i + 1, i) for i in range(0,...  19.7 us
    ppermute x7, waiting for transfers between devices, swap(): lax.ppermute(value, axis, [(i, i ^ distance) for i in range(lax.axis_size...  7.23 us
    ppermute x7, starting transfers between devices, swap(): lax.ppermute(value, axis, [(i, i ^ distance) for i in range(lax.axis_size...  4.74 us
    unnamed x4, local copies, waits for them, and re-layouts  4.14 us
    pallas_call x1, Pallas kernels, on_device(): pl.pallas_call(functools.partial(condition_kernel, holders, groups), out_...  2.82 us
    ppermute x1, starting transfers between devices, on_device(): lax.ppermute(even, 'store', first_to_second)  2.18 us
    pallas_call x1, Pallas kernels, on_device(): pl.pallas_call(functools.partial(score_kernel, holders), out_shape=[jax.S...  1.91 us
    ppermute x2, starting transfers between devices, swap_seconds(): lax.ppermute(value, 'store', [(i, i ^ distance) for i in range(1, lax.axi...  1.33 us
  transfers between devices with their start and end apart: 14, of which 7 were waited for; matrix products, arithmetic and copies ran while one was open for 0% of the time, Pallas kernels for 0%

profile of v3, /device:TPU:0, one launch (start us, length us, event | category | flops | bytes accessed | tf_op | source)
XLA Modules:
  0.0 50.7 jit_solution(17191053211904005649)
XLA Ops:
  0.7 2.8 %shard_map.73 = (bf16[8,8448]{1,0:T(8,128)(2,1)S(1)}, bf16[256,8192]{1,0:T(8,128)(2,1)S(1)}) custom-call(s32[1]{0:T(128)S(6)} %copy.8.count_ref, s32[1]{0:T(128)} %bitcast.1.at_ref, bf16[8,8192]{1,0:T(8,128)(2,1)} %refs_0_.1, f32[2,64,64]{2,1,0:T(8,128)} %refs_1_.1, f32[2,64,64]{2,1,0:T(8,128)} %refs_2_.1, s32[16,128]{1,0:T(8,128)} %bitcast.15, ...), custom_call_target="tpu_custom_call" | custom-call | tf_op jit(solution)/shard_map/pallas_call | solution.py:171
  3.5 0.0 copy-start
  3.5 1.9 %copy-done = bf16[256,8192]{1,0:T(8,128)(2,1)} copy-done((bf16[256,8192]{1,0:T(8,128)(2,1)}, bf16[256,8192]{1,0:T(8,128)(2,1)S(1)}, u32[]{:S(2)}) %copy-start) | copy-done | bytes 4194328
  5.4 3.9 %collective-permute-start.5 = (bf16[8,8448]{1,0:T(8,128)(2,1)S(1)}, bf16[8,8448]{1,0:T(8,128)(2,1)S(1)}, u32[]{:S(2)}, u32[]{:S(2)}) collective-permute-start(bf16[8,8448]{1,0:T(8,128)(2,1)S(1)} %get-tuple-element.9.refs_0_), channel_id=1, source_target_pairs={{0,24},{4,28},{8,16},{12,20},{16,8},{20,12},{24,0},{28,4},{1,25},{... | collective-permute-start | bytes 405512 | tf_op jit(solution)/shard_map/ppermute | solution.py:148
  9.3 0.5 collective-permute-start.3
  9.8 0.1 collective-permute-start.1
  9.9 0.0 collective-permute-start
  9.9 3.4 %collective-permute-done.5.refs_6_ = bf16[8,8448]{1,0:T(8,128)(2,1)S(1)} collective-permute-done((bf16[8,8448]{1,0:T(8,128)(2,1)S(1)}, bf16[8,8448]{1,0:T(8,128)(2,1)S(1)}, u32[]{:S(2)}, u32[]{:S(2)}) %collective-permute-start.5) | collective-permute-done | bytes 135200 | tf_op jit(solution)/shard_map/ppermute | solution.py:148
  13.3 0.0 collective-permute-start.6
  13.3 2.5 %collective-permute-done.3.refs_4_ = bf16[8,8448]{1,0:T(8,128)(2,1)S(1)} collective-permute-done((bf16[8,8448]{1,0:T(8,128)(2,1)S(1)}, bf16[8,8448]{1,0:T(8,128)(2,1)S(1)}, u32[]{:S(2)}, u32[]{:S(2)}) %collective-permute-start.3) | collective-permute-done | bytes 135200 | tf_op jit(solution)/shard_map/ppermute | solution.py:148
  15.8 0.0 collective-permute-start.4
  15.8 0.2 collective-permute-done.1.refs_2_
  16.1 0.3 collective-permute-start.2
  16.3 0.0 collective-permute-done.refs_1_
  16.3 0.0 collective-permute-done.6.refs_7_
  16.3 0.8 %collective-permute-done.4.refs_5_ = bf16[8,8448]{1,0:T(8,128)(2,1)S(1)} collective-permute-done((bf16[8,8448]{1,0:T(8,128)(2,1)S(1)}, bf16[8,8448]{1,0:T(8,128)(2,1)S(1)}, u32[]{:S(2)}, u32[]{:S(2)}) %collective-permute-start.4) | collective-permute-done | bytes 135200 | tf_op jit(solution)/shard_map/ppermute | solution.py:148
  17.2 0.3 collective-permute-done.2.refs_3_
  17.4 0.0 copy-start.1
  17.4 2.2 %copy-done.1 = bf16[256,8192]{1,0:T(8,128)(2,1)S(1)} copy-done((bf16[256,8192]{1,0:T(8,128)(2,1)S(1)}, bf16[256,8192]{1,0:T(8,128)(2,1)}, u32[]{:S(2)}) %copy-start.1) | copy-done | bytes 4194328
  19.6 1.9 %shard_map.74 = (bf16[4,64,256]{2,1,0:T(8,128)(2,1)S(1)}, bf16[4,64,256]{2,1,0:T(8,128)(2,1)S(1)}) custom-call(s32[1]{0:T(128)} %bitcast.me_ref, bf16[8,8448]{1,0:T(8,128)(2,1)S(1)} %get-tuple-element.9.refs_0_, bf16[8,8448]{1,0:T(8,128)(2,1)S(1)} %collective-permute-done.refs_1_, bf16[8,8448]{1,0:T(8,128)(2,1)S(1)} %collective-permute-done.1.refs_2_, ...), custom_call_target="tpu_custom_call" | custom-call | tf_op jit(solution)/shard_map/pallas_call | solution.py:194
  21.5 2.2 %collective-permute-start.8 = (bf16[4,64,256]{2,1,0:T(8,128)(2,1)S(1)}, bf16[4,64,256]{2,1,0:T(8,128)(2,1)S(1)}, u32[]{:S(2)}, u32[]{:S(2)}) collective-permute-start(bf16[4,64,256]{2,1,0:T(8,128)(2,1)S(1)} %get-tuple-element.11), channel_id=1, source_target_pairs={{0,4},{8,12},{16,20},{24,28},{1,5},{9,13},{17,21},{25,29},{2,6},{1... | collective-permute-start | bytes 393224 | tf_op jit(solution)/shard_map/ppermute | solution.py:206
  23.7 1.3 %collective-permute-start.7 = (bf16[4,64,256]{2,1,0:T(8,128)(2,1)S(1)}, bf16[4,64,256]{2,1,0:T(8,128)(2,1)S(1)}, u32[]{:S(2)}, u32[]{:S(2)}) collective-permute-start(bf16[4,64,256]{2,1,0:T(8,128)(2,1)S(1)} %get-tuple-element.12), channel_id=1, source_target_pairs={{0,4},{8,12},{16,20},{24,28},{1,5},{9,13},{17,21},{25,29},{2,6},{1... | collective-permute-start | bytes 393224 | tf_op jit(solution)/shard_map/ppermute | solution.py:206
  25.0 0.0 collective-permute-done.8
  25.1 0.9 %collective-permute-done.7 = bf16[4,64,256]{2,1,0:T(8,128)(2,1)S(1)} collective-permute-done((bf16[4,64,256]{2,1,0:T(8,128)(2,1)S(1)}, bf16[4,64,256]{2,1,0:T(8,128)(2,1)S(1)}, u32[]{:S(2)}, u32[]{:S(2)}) %collective-permute-start.7) | collective-permute-done | bytes 131104 | tf_op jit(solution)/shard_map/ppermute | solution.py:206
  26.0 0.7 %collective-permute-start.9 = (bf16[2,2,64,256]{3,2,0,1:T(8,128)(2,1)S(1)}, bf16[2,2,64,256]{3,2,0,1:T(8,128)(2,1)S(1)}, u32[]{:S(2)}, u32[]{:S(2)}) collective-permute-start(bf16[2,2,64,256]{3,2,0,1:T(8,128)(2,1)S(1)} %pad_maximum_fusion), channel_id=1, source_target_pairs={{4,12},{12,4},{20,28},{28,20},{5,13},{13,5},{21,29},{29,21},{6,14}... | collective-permute-start | bytes 393224 | tf_op jit(solution)/shard_map/ppermute | solution.py:152
  26.7 0.0 collective-permute-done.9
  26.7 0.7 %collective-permute-start.10 = (bf16[2,1,64,256]{3,2,0,1:T(8,128)(2,1)S(1)}, bf16[2,1,64,256]{3,2,0,1:T(8,128)(2,1)S(1)}, u32[]{:S(2)}, u32[]{:S(2)}) collective-permute-start(bf16[2,1,64,256]{3,2,0,1:T(8,128)(2,1)S(1)} %slice.50), channel_id=1, source_target_pairs={{4,20},{12,28},{20,4},{28,12},{5,21},{13,29},{21,5},{29,13},{6,22}... | collective-permute-start | bytes 196616 | tf_op jit(solution)/shard_map/ppermute | solution.py:152
  27.4 0.0 collective-permute-done.10
  27.5 0.7 %collective-permute-start.11 = (bf16[2,64,128]{2,1,0:T(8,128)(2,1)S(1)}, bf16[2,64,128]{2,1,0:T(8,128)(2,1)S(1)}, u32[]{:S(2)}, u32[]{:S(2)}) collective-permute-start(bf16[2,64,128]{2,1,0:T(8,128)(2,1)S(1)} %slice.52), channel_id=1, source_target_pairs={{4,5},{5,4},{6,7},{7,6},{12,13},{13,12},{14,15},{15,14},{20,21},{2... | collective-permute-start | bytes 98312 | tf_op jit(solution)/shard_map/ppermute | solution.py:220
  28.1 0.0 collective-permute-done.11
  28.2 0.1 slice.54
  28.2 0.7 %collective-permute-start.12 = (f32[2,64,64]{2,1,0:T(8,128)S(1)}, f32[2,64,64]{2,1,0:T(8,128)S(1)}, u32[]{:S(2)}, u32[]{:S(2)}) collective-permute-start(f32[2,64,64]{2,1,0:T(8,128)S(1)} %slice.54), channel_id=1, source_target_pairs={{4,6},{5,7},{6,4},{7,5},{12,14},{13,15},{14,12},{15,13},{20,22},{2... | collective-permute-start | bytes 98312 | tf_op jit(solution)/shard_map/ppermute | solution.py:220
  28.9 0.0 collective-permute-done.12
  28.9 1.3 %collective-permute-start.13 = (f32[64,64]{1,0:T(8,128)S(1)}, f32[64,64]{1,0:T(8,128)S(1)}, u32[]{:S(2)}, u32[]{:S(2)}) collective-permute-start(f32[64,64]{1,0:T(8,128)S(1)} %get-tuple-element.13), channel_id=1, source_target_pairs={{4,0},{12,8},{20,16},{28,24},{5,1},{13,9},{21,17},{29,25},{6,2},{1... | collective-permute-start | bytes 49160 | tf_op jit(solution)/shard_map/ppermute | solution.py:228
  30.2 19.7 %collective-permute-done.13.handed_ref = f32[64,64]{1,0:T(8,128)S(1)} collective-permute-done((f32[64,64]{1,0:T(8,128)S(1)}, f32[64,64]{1,0:T(8,128)S(1)}, u32[]{:S(2)}, u32[]{:S(2)}) %collective-permute-start.13) | collective-permute-done | bytes 16416 | tf_op jit(solution)/shard_map/ppermute | solution.py:228
  50.0 0.7 %shard_map.75 = f32[1,64,64]{2,1,0:T(8,128)} custom-call(s32[1]{0:T(128)} %bitcast.me_ref, f32[64,64]{1,0:T(8,128)S(1)} %get-tuple-element.14.one_ref, f32[64,64]{1,0:T(8,128)S(1)} %get-tuple-element.15.other_ref, f32[64,64]{1,0:T(8,128)S(1)} %collective-permute-done.13.handed_ref), custom_call_target="tpu_custom_call" | custom-call | tf_op jit(solution)/shard_map/pallas_call | solution.py:229
  (9 shorter events, 0.1 us)
Async XLA Ops:
  3.5 2.0 %copy-start = (bf16[256,8192]{1,0:T(8,128)(2,1)}, bf16[256,8192]{1,0:T(8,128)(2,1)S(1)}, u32[]{:S(2)}) copy-start(bf16[256,8192]{1,0:T(8,128)(2,1)S(1)} %get-tuple-element.10.refs_8_) | copy-start | bytes 12582916
  5.4 7.9 %collective-permute-start.5 = (bf16[8,8448]{1,0:T(8,128)(2,1)S(1)}, bf16[8,8448]{1,0:T(8,128)(2,1)S(1)}, u32[]{:S(2)}, u32[]{:S(2)}) collective-permute-start(bf16[8,8448]{1,0:T(8,128)(2,1)S(1)} %get-tuple-element.9.refs_0_), channel_id=1, source_target_pairs={{0,24},{4,28},{8,16},{12,20},{16,8},{20,12},{24,0},{28,4},{1,25},{... | collective-permute-start | bytes 405512 | tf_op jit(solution)/shard_map/ppermute | solution.py:148
  9.3 6.5 %collective-permute-start.3 = (bf16[8,8448]{1,0:T(8,128)(2,1)S(1)}, bf16[8,8448]{1,0:T(8,128)(2,1)S(1)}, u32[]{:S(2)}, u32[]{:S(2)}) collective-permute-start(bf16[8,8448]{1,0:T(8,128)(2,1)S(1)} %get-tuple-element.9.refs_0_), channel_id=1, source_target_pairs={{0,16},{4,20},{8,24},{12,28},{16,0},{20,4},{24,8},{28,12},{1,17},{... | collective-permute-start | bytes 405512 | tf_op jit(solution)/shard_map/ppermute | solution.py:148
  9.8 6.2 %collective-permute-start.1 = (bf16[8,8448]{1,0:T(8,128)(2,1)S(1)}, bf16[8,8448]{1,0:T(8,128)(2,1)S(1)}, u32[]{:S(2)}, u32[]{:S(2)}) collective-permute-start(bf16[8,8448]{1,0:T(8,128)(2,1)S(1)} %get-tuple-element.9.refs_0_), channel_id=1, source_target_pairs={{0,8},{4,12},{8,0},{12,4},{16,24},{20,28},{24,16},{28,20},{1,9},{5... | collective-permute-start | bytes 405512 | tf_op jit(solution)/shard_map/ppermute | solution.py:148
  9.9 6.4 %collective-permute-start = (bf16[8,8448]{1,0:T(8,128)(2,1)S(1)}, bf16[8,8448]{1,0:T(8,128)(2,1)S(1)}, u32[]{:S(2)}, u32[]{:S(2)}) collective-permute-start(bf16[8,8448]{1,0:T(8,128)(2,1)S(1)} %get-tuple-element.9.refs_0_), channel_id=1, source_target_pairs={{0,4},{4,0},{8,12},{12,8},{16,20},{20,16},{24,28},{28,24},{1,5},{5... | collective-permute-start | bytes 405512 | tf_op jit(solution)/shard_map/ppermute | solution.py:148
  13.3 3.0 %collective-permute-start.6 = (bf16[8,8448]{1,0:T(8,128)(2,1)S(1)}, bf16[8,8448]{1,0:T(8,128)(2,1)S(1)}, u32[]{:S(2)}, u32[]{:S(2)}) collective-permute-start(bf16[8,8448]{1,0:T(8,128)(2,1)S(1)} %collective-permute-done.5.refs_6_), channel_id=1, source_target_pairs={{0,4},{4,0},{8,12},{12,8},{16,20},{20,16},{24,28},{28,24},{1,5},{5... | collective-permute-start | bytes 405512 | tf_op jit(solution)/shard_map/ppermute | solution.py:148
  15.8 1.4 %collective-permute-start.4 = (bf16[8,8448]{1,0:T(8,128)(2,1)S(1)}, bf16[8,8448]{1,0:T(8,128)(2,1)S(1)}, u32[]{:S(2)}, u32[]{:S(2)}) collective-permute-start(bf16[8,8448]{1,0:T(8,128)(2,1)S(1)} %collective-permute-done.3.refs_4_), channel_id=1, source_target_pairs={{0,4},{4,0},{8,12},{12,8},{16,20},{20,16},{24,28},{28,24},{1,5},{5... | collective-permute-start | bytes 405512 | tf_op jit(solution)/shard_map/ppermute | solution.py:148
  16.1 1.4 %collective-permute-start.2 = (bf16[8,8448]{1,0:T(8,128)(2,1)S(1)}, bf16[8,8448]{1,0:T(8,128)(2,1)S(1)}, u32[]{:S(2)}, u32[]{:S(2)}) collective-permute-start(bf16[8,8448]{1,0:T(8,128)(2,1)S(1)} %collective-permute-done.1.refs_2_), channel_id=1, source_target_pairs={{0,4},{4,0},{8,12},{12,8},{16,20},{20,16},{24,28},{28,24},{1,5},{5... | collective-permute-start | bytes 405512 | tf_op jit(solution)/shard_map/ppermute | solution.py:148
  17.4 2.2 %copy-start.1 = (bf16[256,8192]{1,0:T(8,128)(2,1)S(1)}, bf16[256,8192]{1,0:T(8,128)(2,1)}, u32[]{:S(2)}) copy-start(bf16[256,8192]{1,0:T(8,128)(2,1)} %copy-done) | copy-start | bytes 12582916
  21.5 3.5 %collective-permute-start.8 = (bf16[4,64,256]{2,1,0:T(8,128)(2,1)S(1)}, bf16[4,64,256]{2,1,0:T(8,128)(2,1)S(1)}, u32[]{:S(2)}, u32[]{:S(2)}) collective-permute-start(bf16[4,64,256]{2,1,0:T(8,128)(2,1)S(1)} %get-tuple-element.11), channel_id=1, source_target_pairs={{0,4},{8,12},{16,20},{24,28},{1,5},{9,13},{17,21},{25,29},{2,6},{1... | collective-permute-start | bytes 393224 | tf_op jit(solution)/shard_map/ppermute | solution.py:206
  23.7 2.3 %collective-permute-start.7 = (bf16[4,64,256]{2,1,0:T(8,128)(2,1)S(1)}, bf16[4,64,256]{2,1,0:T(8,128)(2,1)S(1)}, u32[]{:S(2)}, u32[]{:S(2)}) collective-permute-start(bf16[4,64,256]{2,1,0:T(8,128)(2,1)S(1)} %get-tuple-element.12), channel_id=1, source_target_pairs={{0,4},{8,12},{16,20},{24,28},{1,5},{9,13},{17,21},{25,29},{2,6},{1... | collective-permute-start | bytes 393224 | tf_op jit(solution)/shard_map/ppermute | solution.py:206
  26.0 0.7 %collective-permute-start.9 = (bf16[2,2,64,256]{3,2,0,1:T(8,128)(2,1)S(1)}, bf16[2,2,64,256]{3,2,0,1:T(8,128)(2,1)S(1)}, u32[]{:S(2)}, u32[]{:S(2)}) collective-permute-start(bf16[2,2,64,256]{3,2,0,1:T(8,128)(2,1)S(1)} %pad_maximum_fusion), channel_id=1, source_target_pairs={{4,12},{12,4},{20,28},{28,20},{5,13},{13,5},{21,29},{29,21},{6,14}... | collective-permute-start | bytes 393224 | tf_op jit(solution)/shard_map/ppermute | solution.py:152
  26.7 0.7 %collective-permute-start.10 = (bf16[2,1,64,256]{3,2,0,1:T(8,128)(2,1)S(1)}, bf16[2,1,64,256]{3,2,0,1:T(8,128)(2,1)S(1)}, u32[]{:S(2)}, u32[]{:S(2)}) collective-permute-start(bf16[2,1,64,256]{3,2,0,1:T(8,128)(2,1)S(1)} %slice.50), channel_id=1, source_target_pairs={{4,20},{12,28},{20,4},{28,12},{5,21},{13,29},{21,5},{29,13},{6,22}... | collective-permute-start | bytes 196616 | tf_op jit(solution)/shard_map/ppermute | solution.py:152
  27.5 0.7 %collective-permute-start.11 = (bf16[2,64,128]{2,1,0:T(8,128)(2,1)S(1)}, bf16[2,64,128]{2,1,0:T(8,128)(2,1)S(1)}, u32[]{:S(2)}, u32[]{:S(2)}) collective-permute-start(bf16[2,64,128]{2,1,0:T(8,128)(2,1)S(1)} %slice.52), channel_id=1, source_target_pairs={{4,5},{5,4},{6,7},{7,6},{12,13},{13,12},{14,15},{15,14},{20,21},{2... | collective-permute-start | bytes 98312 | tf_op jit(solution)/shard_map/ppermute | solution.py:220
  28.2 0.7 %collective-permute-start.12 = (f32[2,64,64]{2,1,0:T(8,128)S(1)}, f32[2,64,64]{2,1,0:T(8,128)S(1)}, u32[]{:S(2)}, u32[]{:S(2)}) collective-permute-start(f32[2,64,64]{2,1,0:T(8,128)S(1)} %slice.54), channel_id=1, source_target_pairs={{4,6},{5,7},{6,4},{7,5},{12,14},{13,15},{14,12},{15,13},{20,22},{2... | collective-permute-start | bytes 98312 | tf_op jit(solution)/shard_map/ppermute | solution.py:220
  28.9 21.0 %collective-permute-start.13 = (f32[64,64]{1,0:T(8,128)S(1)}, f32[64,64]{1,0:T(8,128)S(1)}, u32[]{:S(2)}, u32[]{:S(2)}) collective-permute-start(f32[64,64]{1,0:T(8,128)S(1)} %get-tuple-element.13), channel_id=1, source_target_pairs={{4,0},{12,8},{20,16},{28,24},{5,1},{13,9},{21,17},{29,25},{6,2},{1... | collective-permute-start | bytes 49160 | tf_op jit(solution)/shard_map/ppermute | solution.py:228

commit v4 on v3

--- a/solution.py
+++ b/solution.py
@@ -19,9 +19,19 @@
     return lax.broadcasted_iota(jnp.int32, shape, dimension)
 
 
-def bit_reversed(size):
-    bits = size.bit_length() - 1
-    return [sum(((p >> b) & 1) << (bits - 1 - b) for b in range(bits)) for p in range(size)]
+def store_steps(holders):
+    return [1] + [(1 << b) | 1 for b in range(1, holders.bit_length() - 1)]
+
+
+def layer_steps(groups):
+    return [1 << b for b in range(groups.bit_length() - 1)]
+
+
+def halving_order(steps):
+    order = [0]
+    for step in reversed(steps):
+        order = order + [k ^ step for k in order]
+    return order
 
 
 def parts_of(value):
@@ -89,7 +99,7 @@
     wanted = jnp.where(iota((1, slots), 1) < count_ref[0], cand_ref[...], -1)
     ranges = [wanted[:, g * share:(g + 1) * share] for g in range(groups)]
     ordered = []
-    for j in bit_reversed(groups):
+    for j in halving_order(layer_steps(groups)):
         chosen = ranges[0]
         for g in range(1, groups):
             chosen = jnp.where((at_ref[0] ^ j) == g, ranges[g], chosen)
@@ -131,7 +141,7 @@
     ordered = total[...].astype(jnp.bfloat16)
     page = iota((count, slots), 0).astype(jnp.float32)
     here = me.astype(jnp.float32)
-    for place, k in enumerate(bit_reversed(holders)):
+    for place, k in enumerate(halving_order(store_steps(holders))):
         notes = packed_refs[k][:, width:].astype(jnp.float32)
         chosen = jnp.where(notes[0:1] == here, notes[1:2], -1.0)
         onehot = (page == chosen).astype(jnp.float32).astype(jnp.bfloat16)
@@ -140,16 +150,12 @@
         target[place % (holders // 2)] = picked
 
 
-def finish_kernel(me_ref, one_ref, other_ref, handed_ref, out_ref):
-    out_ref[0] = jnp.where(me_ref[0] % 2 == 1, one_ref[...] + other_ref[...], handed_ref[...]).T
+def add_kernel(one_ref, other_ref, out_ref):
+    out_ref[0] = (one_ref[...] + other_ref[...]).T
 
 
 def swap(value, axis, distance):
     return lax.ppermute(value, axis, [(i, i ^ distance) for i in range(lax.axis_size(axis))])
-
-
-def swap_seconds(value, distance):
-    return lax.ppermute(value, "store", [(i, i ^ distance) for i in range(1, lax.axis_size("store"), 2)])
 
 
 def on_device(query_grads, factor_out, factor_in, page_store, page_home, cand_lists, counts):
@@ -171,7 +177,7 @@
     packed, pages = pl.pallas_call(
         functools.partial(condition_kernel, holders, groups),
         out_shape=[
-            jax.ShapeDtypeStruct((rows, width + slots), bf16), jax.ShapeDtypeStruct(page_store.shape, bf16)
+            jax.ShapeDtypeStruct((rows, width + slots), bf16), pltpu.VMEM(page_store.shape, bf16)
         ],
         in_specs=[SMEM] * 2 + [HBM] * len(sources),
         out_specs=[VMEM] * 2,
@@ -198,41 +204,28 @@
         out_specs=[VMEM] * 2,
         scratch_shapes=[pltpu.VMEM((total, per_holder), jnp.float32)],
         compiler_params=pltpu.CompilerParams(vmem_limit_bytes=8 * 2**20 + bytes_in + bytes_out),
-    )(store_at, *blocks, pages)
-
-    even, odd = keep, send
-    first_to_second = [(i, i + 1) for i in range(0, holders, 2)]
-    odd, even = (
-        odd + lax.ppermute(even, "store", first_to_second), even + lax.ppermute(odd, "store", first_to_second)
-    )
-    both = jnp.stack([even, odd])
-    distance = 2
-    while distance < holders:
-        cut = both.shape[1] // 2
-        both = both[:, :cut] + swap_seconds(both[:, cut:], distance)
-        distance *= 2
-    both = both[:, 0]
-
-    distance = 1
-    while distance < groups:
-        cut = both.shape[2] // 2
-        moving = both[:, :, cut:]
-        landed = lax.ppermute(
-            moving, ("store", "layer"),
-            [(s * groups + g, s * groups + (g ^ distance)) for s in range(1, holders, 2) for g in range(groups)],
-        ).astype(jnp.float32)
-        keep = both[:, :, :cut].astype(jnp.float32)
-        distance *= 2
-        if distance < groups:
-            both = keep + landed
-    handed = lax.ppermute(keep[1] + landed[1], "store", [(i + 1, i) for i in range(0, holders, 2)])
+    )(store_at, *blocks, pltpu.with_memory_space_constraint(pages, pltpu.VMEM))
+
+    for step in store_steps(holders):
+        landed = swap(send, "store", step)
+        cut = keep.shape[0] // 2
+        if cut:
+            keep, send = keep[:cut] + landed[:cut], keep[cut:] + landed[cut:]
+    scores = (keep + landed)[0]
+
+    for step in layer_steps(groups):
+        cut = scores.shape[1] // 2
+        landed = swap(scores[:, cut:], "layer", step).astype(jnp.float32)
+        keep = scores[:, :cut].astype(jnp.float32)
+        if step < groups // 2:
+            scores = keep + landed
     return pl.pallas_call(
-        finish_kernel,
+        add_kernel,
         out_shape=jax.ShapeDtypeStruct((1, slots // groups, total), jnp.float32),
-        in_specs=[SMEM] + [VMEM] * 3,
+        in_specs=[VMEM] * 2,
         out_specs=VMEM,
         compiler_params=pltpu.CompilerParams(vmem_limit_bytes=2 * 2**20),
-    )(store_at, keep[0], landed[0], handed)
+    )(keep, landed)
 
 
 def solution(mesh):

time: 50.9 us -> 40 us (0.79)
  waiting for transfers between devices: 27.9 us -> 17 us
    ppermute x7 -> x0, waiting for transfers between devices: 20.7 us -> none  [the longest x1 19.7 us: on_device(): lax.ppermute(keep[1] + landed[1], 'store', [(i + 1, i) for i in range(0,...]
    ppermute x7 -> x12, waiting for transfers between devices: 7.23 us -> 17 us  [swap(): lax.ppermute(value, axis, [(i, i ^ distance) for i in range(lax.axis_size...]
    ppermute x7 -> x12, starting transfers between devices: 4.74 us -> 12.5 us  [swap(): lax.ppermute(value, axis, [(i, i ^ distance) for i in range(lax.axis_size...]
    ppermute x7 -> x0, starting transfers between devices: 7.43 us -> none  [the longest x1 2.18 us: on_device(): lax.ppermute(even, 'store', first_to_second)]
  transfers between devices with their start and end apart: 14 -> 12, of which waited for: 7 -> 10; matrix products, arithmetic and copies ran while one was open for 0% -> 0% of each run, Pallas kernels for 0% -> 0%
where the time goes in v4:
time: 40 us; the launch traced here: 39.8 us
  waiting for transfers between devices  17 us (42%)
  starting transfers between devices  12.5 us (31%)
  Pallas kernels  5.43 us (14%)
  local copies, waits for them, and re-layouts  4.22 us (11%)
  between operations  0.69 us (2%)
    ppermute x12, waiting for transfers between devices, swap(): lax.ppermute(value, axis, [(i, i ^ distance) for i in range(lax.axis_size...  17 us
    ppermute x12, starting transfers between devices, swap(): lax.ppermute(value, axis, [(i, i ^ distance) for i in range(lax.axis_size...  12.5 us
    unnamed x4, local copies, waits for them, and re-layouts  4.14 us
    pallas_call x1, Pallas kernels, on_device(): pl.pallas_call(functools.partial(condition_kernel, holders, groups), out_...  2.82 us
    pallas_call x1, Pallas kernels, on_device(): pl.pallas_call(functools.partial(score_kernel, holders), out_shape=[jax.S...  1.91 us
  transfers between devices with their start and end apart: 12, of which 10 were waited for; matrix products, arithmetic and copies ran while one was open for 0% of the time, Pallas kernels for 0%

profile of v4, /device:TPU:0, one launch (start us, length us, event | category | flops | bytes accessed | tf_op | source)
XLA Modules:
  0.0 39.8 jit_solution(9635619388091284478)
XLA Ops:
  0.7 2.8 %shard_map.73 = (bf16[8,8448]{1,0:T(8,128)(2,1)S(1)}, bf16[256,8192]{1,0:T(8,128)(2,1)S(1)}) custom-call(s32[1]{0:T(128)S(6)} %copy.8.count_ref, s32[1]{0:T(128)} %bitcast.1.at_ref, bf16[8,8192]{1,0:T(8,128)(2,1)} %refs_0_.1, f32[2,64,64]{2,1,0:T(8,128)} %refs_1_.1, f32[2,64,64]{2,1,0:T(8,128)} %refs_2_.1, s32[16,128]{1,0:T(8,128)} %bitcast.5, ...), custom_call_target="tpu_custom_call" | custom-call | tf_op jit(solution)/shard_map/pallas_call | solution.py:177
  3.5 0.0 copy-start
  3.5 2.0 %copy-done = bf16[256,8192]{1,0:T(8,128)(2,1)} copy-done((bf16[256,8192]{1,0:T(8,128)(2,1)}, bf16[256,8192]{1,0:T(8,128)(2,1)S(1)}, u32[]{:S(2)}) %copy-start) | copy-done | bytes 4194328
  5.4 3.9 %collective-permute-start.5 = (bf16[8,8448]{1,0:T(8,128)(2,1)S(1)}, bf16[8,8448]{1,0:T(8,128)(2,1)S(1)}, u32[]{:S(2)}, u32[]{:S(2)}) collective-permute-start(bf16[8,8448]{1,0:T(8,128)(2,1)S(1)} %get-tuple-element.9.refs_0_), channel_id=1, source_target_pairs={{0,24},{4,28},{8,16},{12,20},{16,8},{20,12},{24,0},{28,4},{1,25},{... | collective-permute-start | bytes 405512 | tf_op jit(solution)/shard_map/ppermute | solution.py:158
  9.3 0.5 %collective-permute-start.3 = (bf16[8,8448]{1,0:T(8,128)(2,1)S(1)}, bf16[8,8448]{1,0:T(8,128)(2,1)S(1)}, u32[]{:S(2)}, u32[]{:S(2)}) collective-permute-start(bf16[8,8448]{1,0:T(8,128)(2,1)S(1)} %get-tuple-element.9.refs_0_), channel_id=1, source_target_pairs={{0,16},{4,20},{8,24},{12,28},{16,0},{20,4},{24,8},{28,12},{1,17},{... | collective-permute-start | bytes 405512 | tf_op jit(solution)/shard_map/ppermute | solution.py:158
  9.9 0.1 collective-permute-start.1
  9.9 0.0 collective-permute-start
  9.9 3.4 %collective-permute-done.5.refs_6_ = bf16[8,8448]{1,0:T(8,128)(2,1)S(1)} collective-permute-done((bf16[8,8448]{1,0:T(8,128)(2,1)S(1)}, bf16[8,8448]{1,0:T(8,128)(2,1)S(1)}, u32[]{:S(2)}, u32[]{:S(2)}) %collective-permute-start.5) | collective-permute-done | bytes 135200 | tf_op jit(solution)/shard_map/ppermute | solution.py:158
  13.3 0.0 collective-permute-start.6
  13.3 2.5 %collective-permute-done.3.refs_4_ = bf16[8,8448]{1,0:T(8,128)(2,1)S(1)} collective-permute-done((bf16[8,8448]{1,0:T(8,128)(2,1)S(1)}, bf16[8,8448]{1,0:T(8,128)(2,1)S(1)}, u32[]{:S(2)}, u32[]{:S(2)}) %collective-permute-start.3) | collective-permute-done | bytes 135200 | tf_op jit(solution)/shard_map/ppermute | solution.py:158
  15.8 0.0 collective-permute-start.4
  15.8 0.2 collective-permute-done.1.refs_2_
  16.1 0.3 collective-permute-start.2
  16.3 0.0 collective-permute-done.refs_1_
  16.3 0.0 collective-permute-done.6.refs_7_
  16.3 0.8 %collective-permute-done.4.refs_5_ = bf16[8,8448]{1,0:T(8,128)(2,1)S(1)} collective-permute-done((bf16[8,8448]{1,0:T(8,128)(2,1)S(1)}, bf16[8,8448]{1,0:T(8,128)(2,1)S(1)}, u32[]{:S(2)}, u32[]{:S(2)}) %collective-permute-start.4) | collective-permute-done | bytes 135200 | tf_op jit(solution)/shard_map/ppermute | solution.py:158
  17.2 0.3 collective-permute-done.2.refs_3_
  17.4 0.0 copy-start.1
  17.4 2.2 %copy-done.1 = bf16[256,8192]{1,0:T(8,128)(2,1)S(1)} copy-done((bf16[256,8192]{1,0:T(8,128)(2,1)S(1)}, bf16[256,8192]{1,0:T(8,128)(2,1)}, u32[]{:S(2)}) %copy-start.1) | copy-done | bytes 4194328
  19.6 1.9 %shard_map.74 = (bf16[4,64,256]{2,1,0:T(8,128)(2,1)S(1)}, bf16[4,64,256]{2,1,0:T(8,128)(2,1)S(1)}) custom-call(s32[1]{0:T(128)} %bitcast.me_ref, bf16[8,8448]{1,0:T(8,128)(2,1)S(1)} %get-tuple-element.9.refs_0_, bf16[8,8448]{1,0:T(8,128)(2,1)S(1)} %collective-permute-done.refs_1_, bf16[8,8448]{1,0:T(8,128)(2,1)S(1)} %collective-permute-done.1.refs_2_, ...), custom_call_target="tpu_custom_call" | custom-call | tf_op jit(solution)/shard_map/pallas_call | solution.py:200
  21.5 0.3 collective-permute-start.7
  21.9 1.1 %collective-permute-done.7 = bf16[4,64,256]{2,1,0:T(8,128)(2,1)S(1)} collective-permute-done((bf16[4,64,256]{2,1,0:T(8,128)(2,1)S(1)}, bf16[4,64,256]{2,1,0:T(8,128)(2,1)S(1)}, u32[]{:S(2)}, u32[]{:S(2)}) %collective-permute-start.7) | collective-permute-done | bytes 131104 | tf_op jit(solution)/shard_map/ppermute | solution.py:158
  23.0 1.6 %collective-permute-start.8 = (bf16[2,64,256]{2,1,0:T(8,128)(2,1)S(1)}, bf16[2,64,256]{2,1,0:T(8,128)(2,1)S(1)}, u32[]{:S(2)}, u32[]{:S(2)}) collective-permute-start(bf16[2,64,256]{2,1,0:T(8,128)(2,1)S(1)} %get-tuple-element.14), channel_id=1, source_target_pairs={{0,12},{4,8},{8,4},{12,0},{16,28},{20,24},{24,20},{28,16},{1,13},{... | collective-permute-start | bytes 196616 | tf_op jit(solution)/shard_map/ppermute | solution.py:158
  24.6 2.5 %collective-permute-done.8 = bf16[2,64,256]{2,1,0:T(8,128)(2,1)S(1)} collective-permute-done((bf16[2,64,256]{2,1,0:T(8,128)(2,1)S(1)}, bf16[2,64,256]{2,1,0:T(8,128)(2,1)S(1)}, u32[]{:S(2)}, u32[]{:S(2)}) %collective-permute-start.8) | collective-permute-done | bytes 65568 | tf_op jit(solution)/shard_map/ppermute | solution.py:158
  27.1 1.4 %collective-permute-start.9 = (bf16[1,64,256]{2,1,0:T(8,128)(2,1)S(1)}, bf16[1,64,256]{2,1,0:T(8,128)(2,1)S(1)}, u32[]{:S(2)}, u32[]{:S(2)}) collective-permute-start(bf16[1,64,256]{2,1,0:T(8,128)(2,1)S(1)} %slice_add_fusion.2), channel_id=1, source_target_pairs={{0,20},{4,16},{8,28},{12,24},{16,4},{20,0},{24,12},{28,8},{1,21},{... | collective-permute-start | bytes 98312 | tf_op jit(solution)/shard_map/ppermute | solution.py:158
  28.5 1.9 %collective-permute-done.9 = bf16[1,64,256]{2,1,0:T(8,128)(2,1)S(1)} collective-permute-done((bf16[1,64,256]{2,1,0:T(8,128)(2,1)S(1)}, bf16[1,64,256]{2,1,0:T(8,128)(2,1)S(1)}, u32[]{:S(2)}, u32[]{:S(2)}) %collective-permute-start.9) | collective-permute-done | bytes 32800 | tf_op jit(solution)/shard_map/ppermute | solution.py:158
  30.4 1.7 %collective-permute-start.10 = (bf16[64,128]{1,0:T(8,128)(2,1)S(1)}, bf16[64,128]{1,0:T(8,128)(2,1)S(1)}, u32[]{:S(2)}, u32[]{:S(2)}) collective-permute-start(bf16[64,128]{1,0:T(8,128)(2,1)S(1)} %slice.55), channel_id=1, source_target_pairs={{0,1},{1,0},{2,3},{3,2},{4,5},{5,4},{6,7},{7,6},{8,9},{9,8},{10,11... | collective-permute-start | bytes 49160 | tf_op jit(solution)/shard_map/ppermute | solution.py:158
  32.1 2.1 %collective-permute-done.10 = bf16[64,128]{1,0:T(8,128)(2,1)S(1)} collective-permute-done((bf16[64,128]{1,0:T(8,128)(2,1)S(1)}, bf16[64,128]{1,0:T(8,128)(2,1)S(1)}, u32[]{:S(2)}, u32[]{:S(2)}) %collective-permute-start.10) | collective-permute-done | bytes 16416 | tf_op jit(solution)/shard_map/ppermute | solution.py:158
  34.2 0.1 fusion.2
  34.3 2.7 %collective-permute-start.11 = (f32[64,64]{1,0:T(8,128)S(1)}, f32[64,64]{1,0:T(8,128)S(1)}, u32[]{:S(2)}, u32[]{:S(2)}) collective-permute-start(f32[64,64]{1,0:T(8,128)S(1)} %get-tuple-element.15), channel_id=1, source_target_pairs={{0,2},{1,3},{2,0},{3,1},{4,6},{5,7},{6,4},{7,5},{8,10},{9,11},{10,... | collective-permute-start | bytes 49160 | tf_op jit(solution)/shard_map/ppermute | solution.py:158
  37.0 2.2 %collective-permute-done.11.other_ref = f32[64,64]{1,0:T(8,128)S(1)} collective-permute-done((f32[64,64]{1,0:T(8,128)S(1)}, f32[64,64]{1,0:T(8,128)S(1)}, u32[]{:S(2)}, u32[]{:S(2)}) %collective-permute-start.11) | collective-permute-done | bytes 16416 | tf_op jit(solution)/shard_map/ppermute | solution.py:158
  39.1 0.7 %shard_map.75 = f32[1,64,64]{2,1,0:T(8,128)} custom-call(f32[64,64]{1,0:T(8,128)S(1)} %get-tuple-element.16.one_ref, f32[64,64]{1,0:T(8,128)S(1)} %collective-permute-done.11.other_ref), custom_call_target="tpu_custom_call" | custom-call | tf_op jit(solution)/shard_map/pallas_call | solution.py:222
  (5 shorter events, 0.0 us)
Async XLA Ops:
  3.5 2.0 %copy-start = (bf16[256,8192]{1,0:T(8,128)(2,1)}, bf16[256,8192]{1,0:T(8,128)(2,1)S(1)}, u32[]{:S(2)}) copy-start(bf16[256,8192]{1,0:T(8,128)(2,1)S(1)} %get-tuple-element.10.refs_8_) | copy-start | bytes 12582916
  5.4 7.9 %collective-permute-start.5 = (bf16[8,8448]{1,0:T(8,128)(2,1)S(1)}, bf16[8,8448]{1,0:T(8,128)(2,1)S(1)}, u32[]{:S(2)}, u32[]{:S(2)}) collective-permute-start(bf16[8,8448]{1,0:T(8,128)(2,1)S(1)} %get-tuple-element.9.refs_0_), channel_id=1, source_target_pairs={{0,24},{4,28},{8,16},{12,20},{16,8},{20,12},{24,0},{28,4},{1,25},{... | collective-permute-start | bytes 405512 | tf_op jit(solution)/shard_map/ppermute | solution.py:158
  9.3 6.5 %collective-permute-start.3 = (bf16[8,8448]{1,0:T(8,128)(2,1)S(1)}, bf16[8,8448]{1,0:T(8,128)(2,1)S(1)}, u32[]{:S(2)}, u32[]{:S(2)}) collective-permute-start(bf16[8,8448]{1,0:T(8,128)(2,1)S(1)} %get-tuple-element.9.refs_0_), channel_id=1, source_target_pairs={{0,16},{4,20},{8,24},{12,28},{16,0},{20,4},{24,8},{28,12},{1,17},{... | collective-permute-start | bytes 405512 | tf_op jit(solution)/shard_map/ppermute | solution.py:158
  9.9 6.2 %collective-permute-start.1 = (bf16[8,8448]{1,0:T(8,128)(2,1)S(1)}, bf16[8,8448]{1,0:T(8,128)(2,1)S(1)}, u32[]{:S(2)}, u32[]{:S(2)}) collective-permute-start(bf16[8,8448]{1,0:T(8,128)(2,1)S(1)} %get-tuple-element.9.refs_0_), channel_id=1, source_target_pairs={{0,8},{4,12},{8,0},{12,4},{16,24},{20,28},{24,16},{28,20},{1,9},{5... | collective-permute-start | bytes 405512 | tf_op jit(solution)/shard_map/ppermute | solution.py:158
  9.9 6.4 %collective-permute-start = (bf16[8,8448]{1,0:T(8,128)(2,1)S(1)}, bf16[8,8448]{1,0:T(8,128)(2,1)S(1)}, u32[]{:S(2)}, u32[]{:S(2)}) collective-permute-start(bf16[8,8448]{1,0:T(8,128)(2,1)S(1)} %get-tuple-element.9.refs_0_), channel_id=1, source_target_pairs={{0,4},{4,0},{8,12},{12,8},{16,20},{20,16},{24,28},{28,24},{1,5},{5... | collective-permute-start | bytes 405512 | tf_op jit(solution)/shard_map/ppermute | solution.py:158
  13.3 3.0 %collective-permute-start.6 = (bf16[8,8448]{1,0:T(8,128)(2,1)S(1)}, bf16[8,8448]{1,0:T(8,128)(2,1)S(1)}, u32[]{:S(2)}, u32[]{:S(2)}) collective-permute-start(bf16[8,8448]{1,0:T(8,128)(2,1)S(1)} %collective-permute-done.5.refs_6_), channel_id=1, source_target_pairs={{0,4},{4,0},{8,12},{12,8},{16,20},{20,16},{24,28},{28,24},{1,5},{5... | collective-permute-start | bytes 405512 | tf_op jit(solution)/shard_map/ppermute | solution.py:158
  15.8 1.4 %collective-permute-start.4 = (bf16[8,8448]{1,0:T(8,128)(2,1)S(1)}, bf16[8,8448]{1,0:T(8,128)(2,1)S(1)}, u32[]{:S(2)}, u32[]{:S(2)}) collective-permute-start(bf16[8,8448]{1,0:T(8,128)(2,1)S(1)} %collective-permute-done.3.refs_4_), channel_id=1, source_target_pairs={{0,4},{4,0},{8,12},{12,8},{16,20},{20,16},{24,28},{28,24},{1,5},{5... | collective-permute-start | bytes 405512 | tf_op jit(solution)/shard_map/ppermute | solution.py:158
  16.1 1.4 %collective-permute-start.2 = (bf16[8,8448]{1,0:T(8,128)(2,1)S(1)}, bf16[8,8448]{1,0:T(8,128)(2,1)S(1)}, u32[]{:S(2)}, u32[]{:S(2)}) collective-permute-start(bf16[8,8448]{1,0:T(8,128)(2,1)S(1)} %collective-permute-done.1.refs_2_), channel_id=1, source_target_pairs={{0,4},{4,0},{8,12},{12,8},{16,20},{20,16},{24,28},{28,24},{1,5},{5... | collective-permute-start | bytes 405512 | tf_op jit(solution)/shard_map/ppermute | solution.py:158
  17.4 2.2 %copy-start.1 = (bf16[256,8192]{1,0:T(8,128)(2,1)S(1)}, bf16[256,8192]{1,0:T(8,128)(2,1)}, u32[]{:S(2)}) copy-start(bf16[256,8192]{1,0:T(8,128)(2,1)} %copy-done) | copy-start | bytes 12582916
  21.5 1.4 %collective-permute-start.7 = (bf16[4,64,256]{2,1,0:T(8,128)(2,1)S(1)}, bf16[4,64,256]{2,1,0:T(8,128)(2,1)S(1)}, u32[]{:S(2)}, u32[]{:S(2)}) collective-permute-start(bf16[4,64,256]{2,1,0:T(8,128)(2,1)S(1)} %get-tuple-element.12), channel_id=1, source_target_pairs={{0,4},{4,0},{8,12},{12,8},{16,20},{20,16},{24,28},{28,24},{1,5},{5... | collective-permute-start | bytes 393224 | tf_op jit(solution)/shard_map/ppermute | solution.py:158
  23.0 4.1 %collective-permute-start.8 = (bf16[2,64,256]{2,1,0:T(8,128)(2,1)S(1)}, bf16[2,64,256]{2,1,0:T(8,128)(2,1)S(1)}, u32[]{:S(2)}, u32[]{:S(2)}) collective-permute-start(bf16[2,64,256]{2,1,0:T(8,128)(2,1)S(1)} %get-tuple-element.14), channel_id=1, source_target_pairs={{0,12},{4,8},{8,4},{12,0},{16,28},{20,24},{24,20},{28,16},{1,13},{... | collective-permute-start | bytes 196616 | tf_op jit(solution)/shard_map/ppermute | solution.py:158
  27.1 3.3 %collective-permute-start.9 = (bf16[1,64,256]{2,1,0:T(8,128)(2,1)S(1)}, bf16[1,64,256]{2,1,0:T(8,128)(2,1)S(1)}, u32[]{:S(2)}, u32[]{:S(2)}) collective-permute-start(bf16[1,64,256]{2,1,0:T(8,128)(2,1)S(1)} %slice_add_fusion.2), channel_id=1, source_target_pairs={{0,20},{4,16},{8,28},{12,24},{16,4},{20,0},{24,12},{28,8},{1,21},{... | collective-permute-start | bytes 98312 | tf_op jit(solution)/shard_map/ppermute | solution.py:158
  30.4 3.8 %collective-permute-start.10 = (bf16[64,128]{1,0:T(8,128)(2,1)S(1)}, bf16[64,128]{1,0:T(8,128)(2,1)S(1)}, u32[]{:S(2)}, u32[]{:S(2)}) collective-permute-start(bf16[64,128]{1,0:T(8,128)(2,1)S(1)} %slice.55), channel_id=1, source_target_pairs={{0,1},{1,0},{2,3},{3,2},{4,5},{5,4},{6,7},{7,6},{8,9},{9,8},{10,11... | collective-permute-start | bytes 49160 | tf_op jit(solution)/shard_map/ppermute | solution.py:158
  34.3 4.8 %collective-permute-start.11 = (f32[64,64]{1,0:T(8,128)S(1)}, f32[64,64]{1,0:T(8,128)S(1)}, u32[]{:S(2)}, u32[]{:S(2)}) collective-permute-start(f32[64,64]{1,0:T(8,128)S(1)} %get-tuple-element.15), channel_id=1, source_target_pairs={{0,2},{1,3},{2,0},{3,1},{4,6},{5,7},{6,4},{7,5},{8,10},{9,11},{10,... | collective-permute-start | bytes 49160 | tf_op jit(solution)/shard_map/ppermute | solution.py:158

commit v5 on v4

--- a/solution.py
+++ b/solution.py
@@ -43,7 +43,7 @@
     return parts
 
 
-def condition_kernel(holders, groups, count_ref, at_ref, *refs):
+def condition_kernel(holders, groups, count_ref, *refs):
     sources, packed_ref, pages_ref, landing, arrived = refs[:6], refs[6], refs[7], refs[8:13], refs[13]
     copies = [
         pltpu.make_async_copy(source, target, arrived.at[i])
@@ -55,6 +55,7 @@
         copy.wait()
     query_ref, in_factor_ref, out_factor_ref, home_ref, cand_ref = landing
     per_holder = pages_ref.shape[0]
+    at = lax.axis_index("layer")
     rows, width = query_ref.shape
     layers, rank, _ = in_factor_ref.shape
     half = rank // 2
@@ -102,7 +103,7 @@
     for j in halving_order(layer_steps(groups)):
         chosen = ranges[0]
         for g in range(1, groups):
-            chosen = jnp.where((at_ref[0] ^ j) == g, ranges[g], chosen)
+            chosen = jnp.where((at ^ j) == g, ranges[g], chosen)
         ordered.append(chosen)
     wanted = jnp.concatenate(ordered, axis=1)
     known = jnp.maximum(wanted, 0)
@@ -119,10 +120,10 @@
     copies[-1].wait()
 
 
-def score_kernel(holders, me_ref, *refs):
+def score_kernel(holders, *refs):
     packed_refs, pages_ref = refs[:holders], refs[holders]
     keep_ref, send_ref, total = refs[holders + 1:]
-    me = me_ref[0]
+    me = lax.axis_index("store")
     count, width = pages_ref.shape
     rows = packed_refs[0].shape[0]
     slots = packed_refs[0].shape[1] - width
@@ -166,8 +167,6 @@
     per_holder = page_store.shape[0]
     slots = cand_lists.shape[1]
     bf16 = jnp.bfloat16
-    store_at = lax.axis_index("store").astype(jnp.int32).reshape(1)
-    layer_at = lax.axis_index("layer").astype(jnp.int32).reshape(1)
 
     home = page_home.reshape(-1, LANES)
     sources = [
@@ -179,12 +178,12 @@
         out_shape=[
             jax.ShapeDtypeStruct((rows, width + slots), bf16), pltpu.VMEM(page_store.shape, bf16)
         ],
-        in_specs=[SMEM] * 2 + [HBM] * len(sources),
+        in_specs=[SMEM] + [HBM] * len(sources),
         out_specs=[VMEM] * 2,
         scratch_shapes=[pltpu.VMEM(source.shape, source.dtype) for source in sources[:-1]]
         + [pltpu.SemaphoreType.DMA((len(sources),))],
         compiler_params=pltpu.CompilerParams(vmem_limit_bytes=14 * 2**20),
-    )(counts, layer_at, *sources)
+    )(counts, *sources)
 
     blocks = [None] * holders
     blocks[0] = packed
@@ -200,11 +199,11 @@
     keep, send = pl.pallas_call(
         functools.partial(score_kernel, holders),
         out_shape=[jax.ShapeDtypeStruct((holders // 2, total, slots), bf16)] * 2,
-        in_specs=[SMEM] + [VMEM] * (holders + 1),
+        in_specs=[VMEM] * (holders + 1),
         out_specs=[VMEM] * 2,
         scratch_shapes=[pltpu.VMEM((total, per_holder), jnp.float32)],
         compiler_params=pltpu.CompilerParams(vmem_limit_bytes=8 * 2**20 + bytes_in + bytes_out),
-    )(store_at, *blocks, pltpu.with_memory_space_constraint(pages, pltpu.VMEM))
+    )(*blocks, pltpu.with_memory_space_constraint(pages, pltpu.VMEM))
 
     for step in store_steps(holders):
         landed = swap(send, "store", step)

time: 40 us -> 35.9 us (0.90)
  local copies, waits for them, and re-layouts: 4.22 us -> 0.08 us
    unnamed x4 -> x0, local copies, waits for them, and re-layouts: 4.14 us -> none
where the time goes in v5:
time: 35.9 us; the launch traced here: 35.8 us
  waiting for transfers between devices  16.9 us (47%)
  starting transfers between devices  12.6 us (35%)
  Pallas kernels  5.44 us (15%)
  between operations  0.68 us (2%)
    ppermute x12, waiting for transfers between devices, swap(): lax.ppermute(value, axis, [(i, i ^ distance) for i in range(lax.axis_size...  16.9 us
    ppermute x12, starting transfers between devices, swap(): lax.ppermute(value, axis, [(i, i ^ distance) for i in range(lax.axis_size...  12.6 us
    pallas_call x1, Pallas kernels, on_device(): pl.pallas_call(functools.partial(condition_kernel, holders, groups), out_...  2.82 us
    pallas_call x1, Pallas kernels, on_device(): pl.pallas_call(functools.partial(score_kernel, holders), out_shape=[jax.S...  1.92 us
  transfers between devices with their start and end apart: 12, of which 10 were waited for; matrix products, arithmetic and copies ran while one was open for 0% of the time, Pallas kernels for 0%

profile of v5, /device:TPU:0, one launch (start us, length us, event | category | flops | bytes accessed | tf_op | source)
XLA Modules:
  0.0 35.8 jit_solution(14678950620390142475)
XLA Ops:
  0.7 2.8 %shard_map.73 = (bf16[8,8448]{1,0:T(8,128)(2,1)S(1)}, bf16[256,8192]{1,0:T(8,128)(2,1)S(1)}) custom-call(s32[1]{0:T(128)S(6)} %copy.8.count_ref, bf16[8,8192]{1,0:T(8,128)(2,1)} %refs_0_.1, f32[2,64,64]{2,1,0:T(8,128)} %refs_1_.1, f32[2,64,64]{2,1,0:T(8,128)} %refs_2_.1, s32[16,128]{1,0:T(8,128)} %bitcast.3, s32[1,256]{1,0:T(1,128)} %refs_4_.1, ...), custom_call_target="tpu_custom_call" | custom-call | tf_op jit(solution)/shard_map/pallas_call | solution.py:176
  3.5 4.0 %collective-permute-start.5 = (bf16[8,8448]{1,0:T(8,128)(2,1)S(1)}, bf16[8,8448]{1,0:T(8,128)(2,1)S(1)}, u32[]{:S(2)}, u32[]{:S(2)}) collective-permute-start(bf16[8,8448]{1,0:T(8,128)(2,1)S(1)} %get-tuple-element.9.refs_0_), channel_id=1, source_target_pairs={{0,24},{4,28},{8,16},{12,20},{16,8},{20,12},{24,0},{28,4},{1,25},{... | collective-permute-start | bytes 405512 | tf_op jit(solution)/shard_map/ppermute | solution.py:159
  7.4 0.5 %collective-permute-start.3 = (bf16[8,8448]{1,0:T(8,128)(2,1)S(1)}, bf16[8,8448]{1,0:T(8,128)(2,1)S(1)}, u32[]{:S(2)}, u32[]{:S(2)}) collective-permute-start(bf16[8,8448]{1,0:T(8,128)(2,1)S(1)} %get-tuple-element.9.refs_0_), channel_id=1, source_target_pairs={{0,16},{4,20},{8,24},{12,28},{16,0},{20,4},{24,8},{28,12},{1,17},{... | collective-permute-start | bytes 405512 | tf_op jit(solution)/shard_map/ppermute | solution.py:159
  8.0 0.1 collective-permute-start.1
  8.1 0.0 collective-permute-start
  8.1 3.3 %collective-permute-done.5.refs_6_ = bf16[8,8448]{1,0:T(8,128)(2,1)S(1)} collective-permute-done((bf16[8,8448]{1,0:T(8,128)(2,1)S(1)}, bf16[8,8448]{1,0:T(8,128)(2,1)S(1)}, u32[]{:S(2)}, u32[]{:S(2)}) %collective-permute-start.5) | collective-permute-done | bytes 135200 | tf_op jit(solution)/shard_map/ppermute | solution.py:159
  11.4 0.0 collective-permute-start.6
  11.4 2.5 %collective-permute-done.3.refs_4_ = bf16[8,8448]{1,0:T(8,128)(2,1)S(1)} collective-permute-done((bf16[8,8448]{1,0:T(8,128)(2,1)S(1)}, bf16[8,8448]{1,0:T(8,128)(2,1)S(1)}, u32[]{:S(2)}, u32[]{:S(2)}) %collective-permute-start.3) | collective-permute-done | bytes 135200 | tf_op jit(solution)/shard_map/ppermute | solution.py:159
  13.9 0.0 collective-permute-start.4
  13.9 0.2 collective-permute-done.1.refs_2_
  14.2 0.3 collective-permute-start.2
  14.4 0.0 collective-permute-done.refs_1_
  14.4 0.0 collective-permute-done.6.refs_7_
  14.4 0.8 %collective-permute-done.4.refs_5_ = bf16[8,8448]{1,0:T(8,128)(2,1)S(1)} collective-permute-done((bf16[8,8448]{1,0:T(8,128)(2,1)S(1)}, bf16[8,8448]{1,0:T(8,128)(2,1)S(1)}, u32[]{:S(2)}, u32[]{:S(2)}) %collective-permute-start.4) | collective-permute-done | bytes 135200 | tf_op jit(solution)/shard_map/ppermute | solution.py:159
  15.3 0.3 collective-permute-done.2.refs_3_
  15.5 1.9 %shard_map.74 = (bf16[4,64,256]{2,1,0:T(8,128)(2,1)S(1)}, bf16[4,64,256]{2,1,0:T(8,128)(2,1)S(1)}) custom-call(bf16[8,8448]{1,0:T(8,128)(2,1)S(1)} %get-tuple-element.9.refs_0_, bf16[8,8448]{1,0:T(8,128)(2,1)S(1)} %collective-permute-done.refs_1_, bf16[8,8448]{1,0:T(8,128)(2,1)S(1)} %collective-permute-done.1.refs_2_, ...), custom_call_target="tpu_custom_call" | custom-call | tf_op jit(solution)/shard_map/pallas_call | solution.py:199
  17.5 0.3 collective-permute-start.7
  17.8 1.1 %collective-permute-done.7 = bf16[4,64,256]{2,1,0:T(8,128)(2,1)S(1)} collective-permute-done((bf16[4,64,256]{2,1,0:T(8,128)(2,1)S(1)}, bf16[4,64,256]{2,1,0:T(8,128)(2,1)S(1)}, u32[]{:S(2)}, u32[]{:S(2)}) %collective-permute-start.7) | collective-permute-done | bytes 131104 | tf_op jit(solution)/shard_map/ppermute | solution.py:159
  18.9 1.6 %collective-permute-start.8 = (bf16[2,64,256]{2,1,0:T(8,128)(2,1)S(1)}, bf16[2,64,256]{2,1,0:T(8,128)(2,1)S(1)}, u32[]{:S(2)}, u32[]{:S(2)}) collective-permute-start(bf16[2,64,256]{2,1,0:T(8,128)(2,1)S(1)} %get-tuple-element.14), channel_id=1, source_target_pairs={{0,12},{4,8},{8,4},{12,0},{16,28},{20,24},{24,20},{28,16},{1,13},{... | collective-permute-start | bytes 196616 | tf_op jit(solution)/shard_map/ppermute | solution.py:159
  20.5 2.5 %collective-permute-done.8 = bf16[2,64,256]{2,1,0:T(8,128)(2,1)S(1)} collective-permute-done((bf16[2,64,256]{2,1,0:T(8,128)(2,1)S(1)}, bf16[2,64,256]{2,1,0:T(8,128)(2,1)S(1)}, u32[]{:S(2)}, u32[]{:S(2)}) %collective-permute-start.8) | collective-permute-done | bytes 65568 | tf_op jit(solution)/shard_map/ppermute | solution.py:159
  23.0 1.4 %collective-permute-start.9 = (bf16[1,64,256]{2,1,0:T(8,128)(2,1)S(1)}, bf16[1,64,256]{2,1,0:T(8,128)(2,1)S(1)}, u32[]{:S(2)}, u32[]{:S(2)}) collective-permute-start(bf16[1,64,256]{2,1,0:T(8,128)(2,1)S(1)} %slice_add_fusion.2), channel_id=1, source_target_pairs={{0,20},{4,16},{8,28},{12,24},{16,4},{20,0},{24,12},{28,8},{1,21},{... | collective-permute-start | bytes 98312 | tf_op jit(solution)/shard_map/ppermute | solution.py:159
  24.4 1.9 %collective-permute-done.9 = bf16[1,64,256]{2,1,0:T(8,128)(2,1)S(1)} collective-permute-done((bf16[1,64,256]{2,1,0:T(8,128)(2,1)S(1)}, bf16[1,64,256]{2,1,0:T(8,128)(2,1)S(1)}, u32[]{:S(2)}, u32[]{:S(2)}) %collective-permute-start.9) | collective-permute-done | bytes 32800 | tf_op jit(solution)/shard_map/ppermute | solution.py:159
  26.4 1.7 %collective-permute-start.10 = (bf16[64,128]{1,0:T(8,128)(2,1)S(1)}, bf16[64,128]{1,0:T(8,128)(2,1)S(1)}, u32[]{:S(2)}, u32[]{:S(2)}) collective-permute-start(bf16[64,128]{1,0:T(8,128)(2,1)S(1)} %slice.55), channel_id=1, source_target_pairs={{0,1},{1,0},{2,3},{3,2},{4,5},{5,4},{6,7},{7,6},{8,9},{9,8},{10,11... | collective-permute-start | bytes 49160 | tf_op jit(solution)/shard_map/ppermute | solution.py:159
  28.1 2.1 %collective-permute-done.10 = bf16[64,128]{1,0:T(8,128)(2,1)S(1)} collective-permute-done((bf16[64,128]{1,0:T(8,128)(2,1)S(1)}, bf16[64,128]{1,0:T(8,128)(2,1)S(1)}, u32[]{:S(2)}, u32[]{:S(2)}) %collective-permute-start.10) | collective-permute-done | bytes 16416 | tf_op jit(solution)/shard_map/ppermute | solution.py:159
  30.2 0.1 fusion.2
  30.2 2.7 %collective-permute-start.11 = (f32[64,64]{1,0:T(8,128)S(1)}, f32[64,64]{1,0:T(8,128)S(1)}, u32[]{:S(2)}, u32[]{:S(2)}) collective-permute-start(f32[64,64]{1,0:T(8,128)S(1)} %get-tuple-element.15), channel_id=1, source_target_pairs={{0,2},{1,3},{2,0},{3,1},{4,6},{5,7},{6,4},{7,5},{8,10},{9,11},{10,... | collective-permute-start | bytes 49160 | tf_op jit(solution)/shard_map/ppermute | solution.py:159
  32.9 2.2 %collective-permute-done.11.other_ref = f32[64,64]{1,0:T(8,128)S(1)} collective-permute-done((f32[64,64]{1,0:T(8,128)S(1)}, f32[64,64]{1,0:T(8,128)S(1)}, u32[]{:S(2)}, u32[]{:S(2)}) %collective-permute-start.11) | collective-permute-done | bytes 16416 | tf_op jit(solution)/shard_map/ppermute | solution.py:159
  35.1 0.7 %shard_map.75 = f32[1,64,64]{2,1,0:T(8,128)} custom-call(f32[64,64]{1,0:T(8,128)S(1)} %get-tuple-element.16.one_ref, f32[64,64]{1,0:T(8,128)S(1)} %collective-permute-done.11.other_ref), custom_call_target="tpu_custom_call" | custom-call | tf_op jit(solution)/shard_map/pallas_call | solution.py:221
  (5 shorter events, 0.0 us)
Async XLA Ops:
  3.5 8.0 %collective-permute-start.5 = (bf16[8,8448]{1,0:T(8,128)(2,1)S(1)}, bf16[8,8448]{1,0:T(8,128)(2,1)S(1)}, u32[]{:S(2)}, u32[]{:S(2)}) collective-permute-start(bf16[8,8448]{1,0:T(8,128)(2,1)S(1)} %get-tuple-element.9.refs_0_), channel_id=1, source_target_pairs={{0,24},{4,28},{8,16},{12,20},{16,8},{20,12},{24,0},{28,4},{1,25},{... | collective-permute-start | bytes 405512 | tf_op jit(solution)/shard_map/ppermute | solution.py:159
  7.4 6.5 %collective-permute-start.3 = (bf16[8,8448]{1,0:T(8,128)(2,1)S(1)}, bf16[8,8448]{1,0:T(8,128)(2,1)S(1)}, u32[]{:S(2)}, u32[]{:S(2)}) collective-permute-start(bf16[8,8448]{1,0:T(8,128)(2,1)S(1)} %get-tuple-element.9.refs_0_), channel_id=1, source_target_pairs={{0,16},{4,20},{8,24},{12,28},{16,0},{20,4},{24,8},{28,12},{1,17},{... | collective-permute-start | bytes 405512 | tf_op jit(solution)/shard_map/ppermute | solution.py:159
  8.0 6.2 %collective-permute-start.1 = (bf16[8,8448]{1,0:T(8,128)(2,1)S(1)}, bf16[8,8448]{1,0:T(8,128)(2,1)S(1)}, u32[]{:S(2)}, u32[]{:S(2)}) collective-permute-start(bf16[8,8448]{1,0:T(8,128)(2,1)S(1)} %get-tuple-element.9.refs_0_), channel_id=1, source_target_pairs={{0,8},{4,12},{8,0},{12,4},{16,24},{20,28},{24,16},{28,20},{1,9},{5... | collective-permute-start | bytes 405512 | tf_op jit(solution)/shard_map/ppermute | solution.py:159
  8.1 6.4 %collective-permute-start = (bf16[8,8448]{1,0:T(8,128)(2,1)S(1)}, bf16[8,8448]{1,0:T(8,128)(2,1)S(1)}, u32[]{:S(2)}, u32[]{:S(2)}) collective-permute-start(bf16[8,8448]{1,0:T(8,128)(2,1)S(1)} %get-tuple-element.9.refs_0_), channel_id=1, source_target_pairs={{0,4},{4,0},{8,12},{12,8},{16,20},{20,16},{24,28},{28,24},{1,5},{5... | collective-permute-start | bytes 405512 | tf_op jit(solution)/shard_map/ppermute | solution.py:159
  11.4 3.0 %collective-permute-start.6 = (bf16[8,8448]{1,0:T(8,128)(2,1)S(1)}, bf16[8,8448]{1,0:T(8,128)(2,1)S(1)}, u32[]{:S(2)}, u32[]{:S(2)}) collective-permute-start(bf16[8,8448]{1,0:T(8,128)(2,1)S(1)} %collective-permute-done.5.refs_6_), channel_id=1, source_target_pairs={{0,4},{4,0},{8,12},{12,8},{16,20},{20,16},{24,28},{28,24},{1,5},{5... | collective-permute-start | bytes 405512 | tf_op jit(solution)/shard_map/ppermute | solution.py:159
  13.9 1.4 %collective-permute-start.4 = (bf16[8,8448]{1,0:T(8,128)(2,1)S(1)}, bf16[8,8448]{1,0:T(8,128)(2,1)S(1)}, u32[]{:S(2)}, u32[]{:S(2)}) collective-permute-start(bf16[8,8448]{1,0:T(8,128)(2,1)S(1)} %collective-permute-done.3.refs_4_), channel_id=1, source_target_pairs={{0,4},{4,0},{8,12},{12,8},{16,20},{20,16},{24,28},{28,24},{1,5},{5... | collective-permute-start | bytes 405512 | tf_op jit(solution)/shard_map/ppermute | solution.py:159
  14.2 1.4 %collective-permute-start.2 = (bf16[8,8448]{1,0:T(8,128)(2,1)S(1)}, bf16[8,8448]{1,0:T(8,128)(2,1)S(1)}, u32[]{:S(2)}, u32[]{:S(2)}) collective-permute-start(bf16[8,8448]{1,0:T(8,128)(2,1)S(1)} %collective-permute-done.1.refs_2_), channel_id=1, source_target_pairs={{0,4},{4,0},{8,12},{12,8},{16,20},{20,16},{24,28},{28,24},{1,5},{5... | collective-permute-start | bytes 405512 | tf_op jit(solution)/shard_map/ppermute | solution.py:159
  17.5 1.4 %collective-permute-start.7 = (bf16[4,64,256]{2,1,0:T(8,128)(2,1)S(1)}, bf16[4,64,256]{2,1,0:T(8,128)(2,1)S(1)}, u32[]{:S(2)}, u32[]{:S(2)}) collective-permute-start(bf16[4,64,256]{2,1,0:T(8,128)(2,1)S(1)} %get-tuple-element.12), channel_id=1, source_target_pairs={{0,4},{4,0},{8,12},{12,8},{16,20},{20,16},{24,28},{28,24},{1,5},{5... | collective-permute-start | bytes 393224 | tf_op jit(solution)/shard_map/ppermute | solution.py:159
  18.9 4.1 %collective-permute-start.8 = (bf16[2,64,256]{2,1,0:T(8,128)(2,1)S(1)}, bf16[2,64,256]{2,1,0:T(8,128)(2,1)S(1)}, u32[]{:S(2)}, u32[]{:S(2)}) collective-permute-start(bf16[2,64,256]{2,1,0:T(8,128)(2,1)S(1)} %get-tuple-element.14), channel_id=1, source_target_pairs={{0,12},{4,8},{8,4},{12,0},{16,28},{20,24},{24,20},{28,16},{1,13},{... | collective-permute-start | bytes 196616 | tf_op jit(solution)/shard_map/ppermute | solution.py:159
  23.0 3.3 %collective-permute-start.9 = (bf16[1,64,256]{2,1,0:T(8,128)(2,1)S(1)}, bf16[1,64,256]{2,1,0:T(8,128)(2,1)S(1)}, u32[]{:S(2)}, u32[]{:S(2)}) collective-permute-start(bf16[1,64,256]{2,1,0:T(8,128)(2,1)S(1)} %slice_add_fusion.2), channel_id=1, source_target_pairs={{0,20},{4,16},{8,28},{12,24},{16,4},{20,0},{24,12},{28,8},{1,21},{... | collective-permute-start | bytes 98312 | tf_op jit(solution)/shard_map/ppermute | solution.py:159
  26.4 3.8 %collective-permute-start.10 = (bf16[64,128]{1,0:T(8,128)(2,1)S(1)}, bf16[64,128]{1,0:T(8,128)(2,1)S(1)}, u32[]{:S(2)}, u32[]{:S(2)}) collective-permute-start(bf16[64,128]{1,0:T(8,128)(2,1)S(1)} %slice.55), channel_id=1, source_target_pairs={{0,1},{1,0},{2,3},{3,2},{4,5},{5,4},{6,7},{7,6},{8,9},{9,8},{10,11... | collective-permute-start | bytes 49160 | tf_op jit(solution)/shard_map/ppermute | solution.py:159
  30.2 4.8 %collective-permute-start.11 = (f32[64,64]{1,0:T(8,128)S(1)}, f32[64,64]{1,0:T(8,128)S(1)}, u32[]{:S(2)}, u32[]{:S(2)}) collective-permute-start(f32[64,64]{1,0:T(8,128)S(1)} %get-tuple-element.15), channel_id=1, source_target_pairs={{0,2},{1,3},{2,0},{3,1},{4,6},{5,7},{6,4},{7,5},{8,10},{9,11},{10,... | collective-permute-start | bytes 49160 | tf_op jit(solution)/shard_map/ppermute | solution.py:159

commit v6 on v5

--- a/solution.py
+++ b/solution.py
@@ -17,10 +17,6 @@
 
 def iota(shape, dimension):
     return lax.broadcasted_iota(jnp.int32, shape, dimension)
-
-
-def store_steps(holders):
-    return [1] + [(1 << b) | 1 for b in range(1, holders.bit_length() - 1)]
 
 
 def layer_steps(groups):
@@ -43,8 +39,12 @@
     return parts
 
 
-def condition_kernel(holders, groups, count_ref, *refs):
-    sources, packed_ref, pages_ref, landing, arrived = refs[:6], refs[6], refs[7], refs[8:13], refs[13]
+def exact_bf16(value):
+    return value.astype(jnp.float32).astype(jnp.bfloat16)
+
+
+def condition_kernel(holders, groups, capacity, count_ref, *refs):
+    sources, packed_ref, pages_ref, found_ref, landing, arrived = refs[:6], refs[6], refs[7], refs[8], refs[9:14], refs[14]
     copies = [
         pltpu.make_async_copy(source, target, arrived.at[i])
         for i, (source, target) in enumerate(zip(sources, landing + (pages_ref,)))
@@ -115,18 +115,30 @@
     holder = jnp.sum(jnp.where(mine, found[:home_rows], 0.0), axis=0, keepdims=True)
     within = jnp.sum(jnp.where(mine, found[home_rows:], 0.0), axis=0, keepdims=True)
     holder = jnp.where(wanted >= 0, holder, float(holders))
-    rest = jnp.zeros((rows - 2, slots), jnp.float32)
-    packed_ref[:, width:] = jnp.concatenate([holder, within, rest], axis=0).astype(jnp.bfloat16)
+    at_holder = iota((holders, slots), 0).astype(jnp.float32) == holder
+    earlier = exact_bf16(iota((slots, slots), 0) < iota((slots, slots), 1))
+    before = jnp.dot(exact_bf16(at_holder), earlier, preferred_element_type=jnp.float32)
+    rank_there = jnp.sum(jnp.where(at_holder, before, 0.0), axis=0, keepdims=True)
+    ranked = exact_bf16(iota((capacity, slots), 0).astype(jnp.float32) == rank_there)
+    asked = lax.dot_general(
+        exact_bf16(jnp.where(at_holder, within + 1.0, 0.0)), ranked, (((1,), (1,)), ((), ())),
+        preferred_element_type=jnp.float32,
+    )
+    blocks = [asked[h:h + rows] for h in range(0, holders, rows)]
+    spare = packed_ref.shape[1] - width - capacity * len(blocks)
+    if spare:
+        blocks.append(jnp.zeros((rows, spare), jnp.float32))
+    packed_ref[:, width:] = jnp.concatenate(blocks, axis=1).astype(jnp.bfloat16)
+    found_ref[...] = jnp.concatenate([holder, rank_there, jnp.zeros((6, slots), jnp.float32)], axis=0)
     copies[-1].wait()
 
 
-def score_kernel(holders, *refs):
-    packed_refs, pages_ref = refs[:holders], refs[holders]
-    keep_ref, send_ref, total = refs[holders + 1:]
+def score_kernel(holders, capacity, *refs):
+    packed_refs, pages_ref, out_ref, total = refs[:holders], refs[holders], refs[holders + 1], refs[holders + 2]
     me = lax.axis_index("store")
     count, width = pages_ref.shape
     rows = packed_refs[0].shape[0]
-    slots = packed_refs[0].shape[1] - width
+    half = capacity // 2
     step = width // CHUNKS
     scores = jnp.zeros((holders * rows, count), jnp.float32)
     for i in range(CHUNKS):
@@ -139,16 +151,47 @@
     for k in range(holders):
         start = pl.multiple_of((me ^ k) * rows, rows)
         total[pl.ds(start, rows), :] = scores[k * rows:(k + 1) * rows]
-    ordered = total[...].astype(jnp.bfloat16)
-    page = iota((count, slots), 0).astype(jnp.float32)
-    here = me.astype(jnp.float32)
-    for place, k in enumerate(halving_order(store_steps(holders))):
+    asked = []
+    for k in range(holders):
         notes = packed_refs[k][:, width:].astype(jnp.float32)
-        chosen = jnp.where(notes[0:1] == here, notes[1:2], -1.0)
-        onehot = (page == chosen).astype(jnp.float32).astype(jnp.bfloat16)
-        picked = jnp.dot(ordered, onehot, preferred_element_type=jnp.float32).astype(jnp.bfloat16)
-        target = (keep_ref, send_ref)[place // (holders // 2)]
-        target[place % (holders // 2)] = picked
+        notes = jnp.sum(jnp.where(iota(notes.shape, 0) == me % rows, notes, 0.0), axis=0, keepdims=True)
+        mine = notes[:, :capacity]
+        for block in range(1, holders // rows):
+            mine = jnp.where(me // rows == block, notes[:, block * capacity:(block + 1) * capacity], mine)
+        asked.append(mine)
+    page = iota((count, holders * half), 0).astype(jnp.float32) + 1.0
+    picked = jnp.zeros((holders * half, 2 * holders * rows), jnp.float32)
+    parts = parts_of(total[...])[::-1]
+    nothing = jnp.zeros_like(parts[0])
+    for side in range(2):
+        chosen = exact_bf16(page == jnp.concatenate([row[:, side * half:(side + 1) * half] for row in asked], axis=1))
+        for part in parts:
+            wide = jnp.concatenate([nothing, part] if side else [part, nothing], axis=0)
+            picked = picked + lax.dot_general(
+                chosen, wide, (((0,), (1,)), ((), ())), preferred_element_type=jnp.float32
+            )
+    for k in range(holders):
+        out_ref[me ^ k] = picked[k * half:(k + 1) * half]
+
+
+def spread_kernel(holders, found_ref, landed_ref, keep_ref, send_ref):
+    half = landed_ref.shape[1]
+    slots = found_ref.shape[1]
+    total = landed_ref.shape[2] // 2
+    cut = slots // 2
+    holder, rank_there = found_ref[0:1], found_ref[1:2]
+    place = iota((holders * half, slots), 0).astype(jnp.float32)
+    parts = parts_of(jnp.concatenate([landed_ref[h] for h in range(holders)], axis=0))[::-1]
+    result = jnp.zeros((total, slots), jnp.float32)
+    for side in range(2):
+        on_side = (rank_there >= half) if side else (rank_there < half)
+        target = jnp.where(on_side, holder * half + rank_there - side * half, -1.0)
+        chosen = exact_bf16(place == target)
+        for part in parts:
+            spread = lax.dot_general(part, chosen, (((0,), (0,)), ((), ())), preferred_element_type=jnp.float32)
+            result = result + spread[side * total:(side + 1) * total]
+    keep_ref[...] = result[:, :cut]
+    send_ref[...] = result[:, cut:]
 
 
 def add_kernel(one_ref, other_ref, out_ref):
@@ -168,21 +211,25 @@
     slots = cand_lists.shape[1]
     bf16 = jnp.bfloat16
 
+    capacity = slots // holders
     home = page_home.reshape(-1, LANES)
     sources = [
         pltpu.with_memory_space_constraint(source, pltpu.HBM)
         for source in (query_grads, factor_in, factor_out, home, cand_lists, page_store)
     ]
-    packed, pages = pl.pallas_call(
-        functools.partial(condition_kernel, holders, groups),
+    notes = max(LANES, holders // rows * capacity)
+    packed, pages, found = pl.pallas_call(
+        functools.partial(condition_kernel, holders, groups, capacity),
         out_shape=[
-            jax.ShapeDtypeStruct((rows, width + slots), bf16), pltpu.VMEM(page_store.shape, bf16)
+            jax.ShapeDtypeStruct((rows, width + notes), bf16),
+            pltpu.VMEM(page_store.shape, bf16),
+            jax.ShapeDtypeStruct((8, slots), jnp.float32),
         ],
         in_specs=[SMEM] + [HBM] * len(sources),
-        out_specs=[VMEM] * 2,
+        out_specs=[VMEM] * 3,
         scratch_shapes=[pltpu.VMEM(source.shape, source.dtype) for source in sources[:-1]]
         + [pltpu.SemaphoreType.DMA((len(sources),))],
-        compiler_params=pltpu.CompilerParams(vmem_limit_bytes=14 * 2**20),
+        compiler_params=pltpu.CompilerParams(vmem_limit_bytes=10 * 2**20 + 24 * slots * slots),
     )(counts, *sources)
 
     blocks = [None] * holders
@@ -194,30 +241,31 @@
         blocks[k + 1] = swap(blocks[k], "store", 1)
 
     total = holders * rows
-    bytes_out = 2 * holders * total * slots
-    bytes_in = 2 * holders * rows * (width + slots) + 2 * per_holder * width
+    bytes_in = 2 * holders * rows * (width + notes) + 2 * per_holder * width
+    asked = pl.pallas_call(
+        functools.partial(score_kernel, holders, capacity),
+        out_shape=jax.ShapeDtypeStruct((holders, capacity // 2, 2 * total), jnp.float32),
+        in_specs=[VMEM] * (holders + 1),
+        out_specs=VMEM,
+        scratch_shapes=[pltpu.VMEM((total, per_holder), jnp.float32)],
+        compiler_params=pltpu.CompilerParams(vmem_limit_bytes=8 * 2**20 + bytes_in + 48 * total * slots),
+    )(*blocks, pltpu.with_memory_space_constraint(pages, pltpu.VMEM))
+
+    landed = lax.all_to_all(asked, "store", split_axis=0, concat_axis=0, tiled=True)
     keep, send = pl.pallas_call(
-        functools.partial(score_kernel, holders),
-        out_shape=[jax.ShapeDtypeStruct((holders // 2, total, slots), bf16)] * 2,
-        in_specs=[VMEM] * (holders + 1),
+        functools.partial(spread_kernel, holders),
+        out_shape=[jax.ShapeDtypeStruct((total, slots // 2), jnp.float32)] * 2,
+        in_specs=[VMEM] * 2,
         out_specs=[VMEM] * 2,
-        scratch_shapes=[pltpu.VMEM((total, per_holder), jnp.float32)],
-        compiler_params=pltpu.CompilerParams(vmem_limit_bytes=8 * 2**20 + bytes_in + bytes_out),
-    )(*blocks, pltpu.with_memory_space_constraint(pages, pltpu.VMEM))
-
-    for step in store_steps(holders):
-        landed = swap(send, "store", step)
-        cut = keep.shape[0] // 2
-        if cut:
-            keep, send = keep[:cut] + landed[:cut], keep[cut:] + landed[cut:]
-    scores = (keep + landed)[0]
+        compiler_params=pltpu.CompilerParams(vmem_limit_bytes=4 * 2**20 + 64 * total * slots),
+    )(found, landed)
 
     for step in layer_steps(groups):
-        cut = scores.shape[1] // 2
-        landed = swap(scores[:, cut:], "layer", step).astype(jnp.float32)
-        keep = scores[:, :cut].astype(jnp.float32)
+        landed = swap(send, "layer", step)
         if step < groups // 2:
             scores = keep + landed
+            cut = scores.shape[1] // 2
+            keep, send = scores[:, :cut], scores[:, cut:]
     return pl.pallas_call(
         add_kernel,
         out_shape=jax.ShapeDtypeStruct((1, slots // groups, total), jnp.float32),

time: 35.9 us -> 35.4 us (0.986)
  blocking collectives: 0 us -> 7.86 us
  waiting for transfers between devices: 16.9 us -> 11.4 us
  starting transfers between devices: 12.6 us -> 9.36 us
  Pallas kernels: 5.44 us -> 5.84 us
    all_to_all x0 -> x1, blocking collectives: none -> 7.86 us  [on_device(): lax.all_to_all(asked, 'store', split_axis=0, concat_axis=0, tiled=True)]
    ppermute x12 -> x9, waiting for transfers between devices: 16.9 us -> 11.4 us  [swap(): lax.ppermute(value, axis, [(i, i ^ distance) for i in range(lax.axis_size...]
    ppermute x12 -> x9, starting transfers between devices: 12.6 us -> 9.36 us  [swap(): lax.ppermute(value, axis, [(i, i ^ distance) for i in range(lax.axis_size...]
    pallas_call x2 -> x3, Pallas kernels: 4.74 us -> 5.14 us  [the longest x1 3 us: on_device(): pl.pallas_call(functools.partial(condition_kernel, holders, groups, capac...]
  transfers between devices with their start and end apart: 12 -> 9, of which waited for: 10 -> 7; matrix products, arithmetic and copies ran while one was open for 0% -> 0% of each run, Pallas kernels for 0% -> 0%
where the time goes in v6:
time: 35.4 us; the launch traced here: 35.2 us
  waiting for transfers between devices  11.4 us (32%)
  starting transfers between devices  9.36 us (26%)
  blocking collectives  7.86 us (22%)
  Pallas kernels  5.84 us (16%)
  between operations  0.69 us (2%)
    ppermute x9, waiting for transfers between devices, swap(): lax.ppermute(value, axis, [(i, i ^ distance) for i in range(lax.axis_size...  11.4 us
    ppermute x9, starting transfers between devices, swap(): lax.ppermute(value, axis, [(i, i ^ distance) for i in range(lax.axis_size...  9.36 us
    all_to_all x1, blocking collectives, on_device(): lax.all_to_all(asked, 'store', split_axis=0, concat_axis=0, tiled=True)  7.86 us
    pallas_call x1, Pallas kernels, on_device(): pl.pallas_call(functools.partial(condition_kernel, holders, groups, capac...  3 us
    pallas_call x1, Pallas kernels, on_device(): pl.pallas_call(functools.partial(score_kernel, holders, capacity), out_sh...  1.85 us
  transfers between devices with their start and end apart: 9, of which 7 were waited for; matrix products, arithmetic and copies ran while one was open for 0% of the time, Pallas kernels for 0%

profile of v6, /device:TPU:0, one launch (start us, length us, event | category | flops | bytes accessed | tf_op | source)
XLA Modules:
  0.0 35.2 jit_solution(7829263813628072751)
XLA Ops:
  0.7 3.0 %shard_map.73 = (bf16[8,8320]{1,0:T(8,128)(2,1)S(1)}, bf16[256,8192]{1,0:T(8,128)(2,1)S(1)}, f32[8,256]{1,0:T(8,128)S(1)}) custom-call(s32[1]{0:T(128)S(6)} %copy.8.count_ref, bf16[8,8192]{1,0:T(8,128)(2,1)} %refs_0_.1, f32[2,64,64]{2,1,0:T(8,128)} %refs_1_.1, f32[2,64,64]{2,1,0:T(8,128)} %refs_2_.1, s32[16,128]{1,0:T(8,128)} %bitcast.1, s32[1,256]{1,0:T(1,128)} %refs_4_.1, ...), custom_call_target="tpu_custom_call" | custom-call | tf_op jit(solution)/shard_map/pallas_call | solution.py:221
  3.7 4.0 %collective-permute-start.5 = (bf16[8,8320]{1,0:T(8,128)(2,1)S(1)}, bf16[8,8320]{1,0:T(8,128)(2,1)S(1)}, u32[]{:S(2)}, u32[]{:S(2)}) collective-permute-start(bf16[8,8320]{1,0:T(8,128)(2,1)S(1)} %get-tuple-element.11.refs_0_), channel_id=1, source_target_pairs={{0,24},{4,28},{8,16},{12,20},{16,8},{20,12},{24,0},{28,4},{1,25},{... | collective-permute-start | bytes 399368 | tf_op jit(solution)/shard_map/ppermute | solution.py:202
  7.6 0.5 %collective-permute-start.3 = (bf16[8,8320]{1,0:T(8,128)(2,1)S(1)}, bf16[8,8320]{1,0:T(8,128)(2,1)S(1)}, u32[]{:S(2)}, u32[]{:S(2)}) collective-permute-start(bf16[8,8320]{1,0:T(8,128)(2,1)S(1)} %get-tuple-element.11.refs_0_), channel_id=1, source_target_pairs={{0,16},{4,20},{8,24},{12,28},{16,0},{20,4},{24,8},{28,12},{1,17},{... | collective-permute-start | bytes 399368 | tf_op jit(solution)/shard_map/ppermute | solution.py:202
  8.1 0.1 collective-permute-start.1
  8.3 0.0 collective-permute-start
  8.3 3.3 %collective-permute-done.5.refs_6_ = bf16[8,8320]{1,0:T(8,128)(2,1)S(1)} collective-permute-done((bf16[8,8320]{1,0:T(8,128)(2,1)S(1)}, bf16[8,8320]{1,0:T(8,128)(2,1)S(1)}, u32[]{:S(2)}, u32[]{:S(2)}) %collective-permute-start.5) | collective-permute-done | bytes 133152 | tf_op jit(solution)/shard_map/ppermute | solution.py:202
  11.6 0.0 collective-permute-start.6
  11.6 2.4 %collective-permute-done.3.refs_4_ = bf16[8,8320]{1,0:T(8,128)(2,1)S(1)} collective-permute-done((bf16[8,8320]{1,0:T(8,128)(2,1)S(1)}, bf16[8,8320]{1,0:T(8,128)(2,1)S(1)}, u32[]{:S(2)}, u32[]{:S(2)}) %collective-permute-start.3) | collective-permute-done | bytes 133152 | tf_op jit(solution)/shard_map/ppermute | solution.py:202
  14.0 0.0 collective-permute-start.4
  14.0 0.2 collective-permute-done.1.refs_2_
  14.3 0.3 collective-permute-start.2
  14.5 0.0 collective-permute-done.refs_1_
  14.5 0.0 collective-permute-done.6.refs_7_
  14.5 0.8 %collective-permute-done.4.refs_5_ = bf16[8,8320]{1,0:T(8,128)(2,1)S(1)} collective-permute-done((bf16[8,8320]{1,0:T(8,128)(2,1)S(1)}, bf16[8,8320]{1,0:T(8,128)(2,1)S(1)}, u32[]{:S(2)}, u32[]{:S(2)}) %collective-permute-start.4) | collective-permute-done | bytes 133152 | tf_op jit(solution)/shard_map/ppermute | solution.py:202
  15.4 0.2 collective-permute-done.2.refs_3_
  15.6 1.9 %shard_map.74 = f32[8,16,128]{2,1,0:T(8,128)S(1)} custom-call(bf16[8,8320]{1,0:T(8,128)(2,1)S(1)} %get-tuple-element.11.refs_0_, bf16[8,8320]{1,0:T(8,128)(2,1)S(1)} %collective-permute-done.refs_1_, bf16[8,8320]{1,0:T(8,128)(2,1)S(1)} %collective-permute-done.1.refs_2_, bf16[8,8320]{1,0:T(8,128)(2,1)S(1)} %collective-permute-done.2.refs_3_, ...), custom_call_target="tpu_custom_call" | custom-call | tf_op jit(solution)/shard_map/pallas_call | solution.py:245
  17.5 7.9 %all_to_all.5.landed_ref = f32[8,16,128]{2,1,0:T(8,128)S(1)} all-to-all(f32[8,16,128]{2,1,0:T(8,128)S(1)} %shard_map.74), channel_id=1, replica_groups=mesh['store'=8,'layer'=4] {'store'}, dimensions={0} | all-to-all | bytes 131072 | tf_op jit(solution)/shard_map/all_to_all | solution.py:254
  25.3 0.3 shard_map.75
  25.6 1.8 %collective-permute-start.7 = (f32[64,128]{1,0:T(8,128)S(1)}, f32[64,128]{1,0:T(8,128)S(1)}, u32[]{:S(2)}, u32[]{:S(2)}) collective-permute-start(f32[64,128]{1,0:T(8,128)S(1)} %get-tuple-element.14), channel_id=1, source_target_pairs={{0,1},{1,0},{2,3},{3,2},{4,5},{5,4},{6,7},{7,6},{8,9},{9,8},{10,11... | collective-permute-start | bytes 98312 | tf_op jit(solution)/shard_map/ppermute | solution.py:202
  27.4 2.2 %collective-permute-done.7 = f32[64,128]{1,0:T(8,128)S(1)} collective-permute-done((f32[64,128]{1,0:T(8,128)S(1)}, f32[64,128]{1,0:T(8,128)S(1)}, u32[]{:S(2)}, u32[]{:S(2)}) %collective-permute-start.7) | collective-permute-done | bytes 32800 | tf_op jit(solution)/shard_map/ppermute | solution.py:202
  29.6 0.1 fusion
  29.7 2.7 %collective-permute-start.8 = (f32[64,64]{1,0:T(8,128)S(1)}, f32[64,64]{1,0:T(8,128)S(1)}, u32[]{:S(2)}, u32[]{:S(2)}) collective-permute-start(f32[64,64]{1,0:T(8,128)S(1)} %get-tuple-element.15), channel_id=1, source_target_pairs={{0,2},{1,3},{2,0},{3,1},{4,6},{5,7},{6,4},{7,5},{8,10},{9,11},{10,... | collective-permute-start | bytes 49160 | tf_op jit(solution)/shard_map/ppermute | solution.py:202
  32.4 2.1 %collective-permute-done.8.other_ref = f32[64,64]{1,0:T(8,128)S(1)} collective-permute-done((f32[64,64]{1,0:T(8,128)S(1)}, f32[64,64]{1,0:T(8,128)S(1)}, u32[]{:S(2)}, u32[]{:S(2)}) %collective-permute-start.8) | collective-permute-done | bytes 16416 | tf_op jit(solution)/shard_map/ppermute | solution.py:202
  34.5 0.7 %shard_map.76 = f32[1,64,64]{2,1,0:T(8,128)} custom-call(f32[64,64]{1,0:T(8,128)S(1)} %get-tuple-element.16.one_ref, f32[64,64]{1,0:T(8,128)S(1)} %collective-permute-done.8.other_ref), custom_call_target="tpu_custom_call" | custom-call | tf_op jit(solution)/shard_map/pallas_call | solution.py:269
  (1 shorter events, 0.0 us)
Async XLA Ops:
  3.7 7.9 %collective-permute-start.5 = (bf16[8,8320]{1,0:T(8,128)(2,1)S(1)}, bf16[8,8320]{1,0:T(8,128)(2,1)S(1)}, u32[]{:S(2)}, u32[]{:S(2)}) collective-permute-start(bf16[8,8320]{1,0:T(8,128)(2,1)S(1)} %get-tuple-element.11.refs_0_), channel_id=1, source_target_pairs={{0,24},{4,28},{8,16},{12,20},{16,8},{20,12},{24,0},{28,4},{1,25},{... | collective-permute-start | bytes 399368 | tf_op jit(solution)/shard_map/ppermute | solution.py:202
  7.6 6.4 %collective-permute-start.3 = (bf16[8,8320]{1,0:T(8,128)(2,1)S(1)}, bf16[8,8320]{1,0:T(8,128)(2,1)S(1)}, u32[]{:S(2)}, u32[]{:S(2)}) collective-permute-start(bf16[8,8320]{1,0:T(8,128)(2,1)S(1)} %get-tuple-element.11.refs_0_), channel_id=1, source_target_pairs={{0,16},{4,20},{8,24},{12,28},{16,0},{20,4},{24,8},{28,12},{1,17},{... | collective-permute-start | bytes 399368 | tf_op jit(solution)/shard_map/ppermute | solution.py:202
  8.1 6.1 %collective-permute-start.1 = (bf16[8,8320]{1,0:T(8,128)(2,1)S(1)}, bf16[8,8320]{1,0:T(8,128)(2,1)S(1)}, u32[]{:S(2)}, u32[]{:S(2)}) collective-permute-start(bf16[8,8320]{1,0:T(8,128)(2,1)S(1)} %get-tuple-element.11.refs_0_), channel_id=1, source_target_pairs={{0,8},{4,12},{8,0},{12,4},{16,24},{20,28},{24,16},{28,20},{1,9},{5... | collective-permute-start | bytes 399368 | tf_op jit(solution)/shard_map/ppermute | solution.py:202
  8.3 6.3 %collective-permute-start = (bf16[8,8320]{1,0:T(8,128)(2,1)S(1)}, bf16[8,8320]{1,0:T(8,128)(2,1)S(1)}, u32[]{:S(2)}, u32[]{:S(2)}) collective-permute-start(bf16[8,8320]{1,0:T(8,128)(2,1)S(1)} %get-tuple-element.11.refs_0_), channel_id=1, source_target_pairs={{0,4},{4,0},{8,12},{12,8},{16,20},{20,16},{24,28},{28,24},{1,5},{5... | collective-permute-start | bytes 399368 | tf_op jit(solution)/shard_map/ppermute | solution.py:202
  11.6 3.0 %collective-permute-start.6 = (bf16[8,8320]{1,0:T(8,128)(2,1)S(1)}, bf16[8,8320]{1,0:T(8,128)(2,1)S(1)}, u32[]{:S(2)}, u32[]{:S(2)}) collective-permute-start(bf16[8,8320]{1,0:T(8,128)(2,1)S(1)} %collective-permute-done.5.refs_6_), channel_id=1, source_target_pairs={{0,4},{4,0},{8,12},{12,8},{16,20},{20,16},{24,28},{28,24},{1,5},{5... | collective-permute-start | bytes 399368 | tf_op jit(solution)/shard_map/ppermute | solution.py:202
  14.0 1.4 %collective-permute-start.4 = (bf16[8,8320]{1,0:T(8,128)(2,1)S(1)}, bf16[8,8320]{1,0:T(8,128)(2,1)S(1)}, u32[]{:S(2)}, u32[]{:S(2)}) collective-permute-start(bf16[8,8320]{1,0:T(8,128)(2,1)S(1)} %collective-permute-done.3.refs_4_), channel_id=1, source_target_pairs={{0,4},{4,0},{8,12},{12,8},{16,20},{20,16},{24,28},{28,24},{1,5},{5... | collective-permute-start | bytes 399368 | tf_op jit(solution)/shard_map/ppermute | solution.py:202
  14.3 1.4 %collective-permute-start.2 = (bf16[8,8320]{1,0:T(8,128)(2,1)S(1)}, bf16[8,8320]{1,0:T(8,128)(2,1)S(1)}, u32[]{:S(2)}, u32[]{:S(2)}) collective-permute-start(bf16[8,8320]{1,0:T(8,128)(2,1)S(1)} %collective-permute-done.1.refs_2_), channel_id=1, source_target_pairs={{0,4},{4,0},{8,12},{12,8},{16,20},{20,16},{24,28},{28,24},{1,5},{5... | collective-permute-start | bytes 399368 | tf_op jit(solution)/shard_map/ppermute | solution.py:202
  25.6 4.0 %collective-permute-start.7 = (f32[64,128]{1,0:T(8,128)S(1)}, f32[64,128]{1,0:T(8,128)S(1)}, u32[]{:S(2)}, u32[]{:S(2)}) collective-permute-start(f32[64,128]{1,0:T(8,128)S(1)} %get-tuple-element.14), channel_id=1, source_target_pairs={{0,1},{1,0},{2,3},{3,2},{4,5},{5,4},{6,7},{7,6},{8,9},{9,8},{10,11... | collective-permute-start | bytes 98312 | tf_op jit(solution)/shard_map/ppermute | solution.py:202
  29.7 4.8 %collective-permute-start.8 = (f32[64,64]{1,0:T(8,128)S(1)}, f32[64,64]{1,0:T(8,128)S(1)}, u32[]{:S(2)}, u32[]{:S(2)}) collective-permute-start(f32[64,64]{1,0:T(8,128)S(1)} %get-tuple-element.15), channel_id=1, source_target_pairs={{0,2},{1,3},{2,0},{3,1},{4,6},{5,7},{6,4},{7,5},{8,10},{9,11},{10,... | collective-permute-start | bytes 49160 | tf_op jit(solution)/shard_map/ppermute | solution.py:202

commit v7 on v6

--- a/solution.py
+++ b/solution.py
@@ -17,17 +17,6 @@
 
 def iota(shape, dimension):
     return lax.broadcasted_iota(jnp.int32, shape, dimension)
-
-
-def layer_steps(groups):
-    return [1 << b for b in range(groups.bit_length() - 1)]
-
-
-def halving_order(steps):
-    order = [0]
-    for step in reversed(steps):
-        order = order + [k ^ step for k in order]
-    return order
 
 
 def parts_of(value):
@@ -43,7 +32,7 @@
     return value.astype(jnp.float32).astype(jnp.bfloat16)
 
 
-def condition_kernel(holders, groups, capacity, count_ref, *refs):
+def condition_kernel(holders, capacity, count_ref, *refs):
     sources, packed_ref, pages_ref, found_ref, landing, arrived = refs[:6], refs[6], refs[7], refs[8], refs[9:14], refs[14]
     copies = [
         pltpu.make_async_copy(source, target, arrived.at[i])
@@ -55,7 +44,6 @@
         copy.wait()
     query_ref, in_factor_ref, out_factor_ref, home_ref, cand_ref = landing
     per_holder = pages_ref.shape[0]
-    at = lax.axis_index("layer")
     rows, width = query_ref.shape
     layers, rank, _ = in_factor_ref.shape
     half = rank // 2
@@ -95,17 +83,8 @@
             packed_ref[:, (first + t) * LANES:(first + t + 1) * LANES] = done[t].astype(jnp.bfloat16)
 
     slots = cand_ref.shape[1]
-    share = slots // groups
     home_rows = home_ref.shape[0]
     wanted = jnp.where(iota((1, slots), 1) < count_ref[0], cand_ref[...], -1)
-    ranges = [wanted[:, g * share:(g + 1) * share] for g in range(groups)]
-    ordered = []
-    for j in halving_order(layer_steps(groups)):
-        chosen = ranges[0]
-        for g in range(1, groups):
-            chosen = jnp.where((at ^ j) == g, ranges[g], chosen)
-        ordered.append(chosen)
-    wanted = jnp.concatenate(ordered, axis=1)
     known = jnp.maximum(wanted, 0)
     onehot = (iota((LANES, slots), 0) == known % LANES).astype(jnp.float32).astype(jnp.bfloat16)
     home = home_ref[...]
@@ -174,11 +153,12 @@
         out_ref[me ^ k] = picked[k * half:(k + 1) * half]
 
 
-def spread_kernel(holders, found_ref, landed_ref, keep_ref, send_ref):
+def spread_kernel(holders, found_ref, landed_ref, out_ref):
     half = landed_ref.shape[1]
     slots = found_ref.shape[1]
     total = landed_ref.shape[2] // 2
-    cut = slots // 2
+    groups = out_ref.shape[0]
+    share = slots // groups
     holder, rank_there = found_ref[0:1], found_ref[1:2]
     place = iota((holders * half, slots), 0).astype(jnp.float32)
     parts = parts_of(jnp.concatenate([landed_ref[h] for h in range(holders)], axis=0))[::-1]
@@ -190,12 +170,17 @@
         for part in parts:
             spread = lax.dot_general(part, chosen, (((0,), (0,)), ((), ())), preferred_element_type=jnp.float32)
             result = result + spread[side * total:(side + 1) * total]
-    keep_ref[...] = result[:, :cut]
-    send_ref[...] = result[:, cut:]
-
-
-def add_kernel(one_ref, other_ref, out_ref):
-    out_ref[0] = (one_ref[...] + other_ref[...]).T
+    for g in range(groups):
+        block = result[:, g * share:(g + 1) * share]
+        out_ref[g] = jnp.concatenate([block[:total // 2], block[total // 2:]], axis=1)
+
+
+def add_kernel(terms_ref, out_ref):
+    total = terms_ref[0]
+    for g in range(1, terms_ref.shape[0]):
+        total = total + terms_ref[g]
+    share = total.shape[1] // 2
+    out_ref[0] = jnp.concatenate([total[:, :share], total[:, share:]], axis=0).T
 
 
 def swap(value, axis, distance):
@@ -219,7 +204,7 @@
     ]
     notes = max(LANES, holders // rows * capacity)
     packed, pages, found = pl.pallas_call(
-        functools.partial(condition_kernel, holders, groups, capacity),
+        functools.partial(condition_kernel, holders, capacity),
         out_shape=[
             jax.ShapeDtypeStruct((rows, width + notes), bf16),
             pltpu.VMEM(page_store.shape, bf16),
@@ -252,27 +237,22 @@
     )(*blocks, pltpu.with_memory_space_constraint(pages, pltpu.VMEM))
 
     landed = lax.all_to_all(asked, "store", split_axis=0, concat_axis=0, tiled=True)
-    keep, send = pl.pallas_call(
+    share = slots // groups
+    terms = pl.pallas_call(
         functools.partial(spread_kernel, holders),
-        out_shape=[jax.ShapeDtypeStruct((total, slots // 2), jnp.float32)] * 2,
+        out_shape=jax.ShapeDtypeStruct((groups, total // 2, 2 * share), jnp.float32),
         in_specs=[VMEM] * 2,
-        out_specs=[VMEM] * 2,
+        out_specs=VMEM,
         compiler_params=pltpu.CompilerParams(vmem_limit_bytes=4 * 2**20 + 64 * total * slots),
     )(found, landed)
-
-    for step in layer_steps(groups):
-        landed = swap(send, "layer", step)
-        if step < groups // 2:
-            scores = keep + landed
-            cut = scores.shape[1] // 2
-            keep, send = scores[:, :cut], scores[:, cut:]
+    terms = lax.all_to_all(terms, "layer", split_axis=0, concat_axis=0, tiled=True)
     return pl.pallas_call(
         add_kernel,
-        out_shape=jax.ShapeDtypeStruct((1, slots // groups, total), jnp.float32),
-        in_specs=[VMEM] * 2,
+        out_shape=jax.ShapeDtypeStruct((1, share, total), jnp.float32),
+        in_specs=[VMEM],
         out_specs=VMEM,
-        compiler_params=pltpu.CompilerParams(vmem_limit_bytes=2 * 2**20),
-    )(keep, landed)
+        compiler_params=pltpu.CompilerParams(vmem_limit_bytes=4 * 2**20),
+    )(terms)
 
 
 def solution(mesh):

time: 35.4 us -> 37.2 us (1.051)
  blocking collectives: 7.86 us -> 18.4 us
  starting transfers between devices: 9.36 us -> 4.88 us
  waiting for transfers between devices: 11.4 us -> 7.07 us
    all_to_all x0 -> x1, blocking collectives: none -> 10.5 us  [on_device(): lax.all_to_all(terms, 'layer', split_axis=0, concat_axis=0, tiled=True)]
    ppermute x9 -> x7, starting transfers between devices: 9.36 us -> 4.88 us  [swap(): lax.ppermute(value, axis, [(i, i ^ distance) for i in range(lax.axis_size...]
    ppermute x9 -> x7, waiting for transfers between devices: 11.4 us -> 7.07 us  [swap(): lax.ppermute(value, axis, [(i, i ^ distance) for i in range(lax.axis_size...]
  transfers between devices with their start and end apart: 9 -> 7, of which waited for: 7 -> 5; matrix products, arithmetic and copies ran while one was open for 0% -> 0% of each run, Pallas kernels for 0% -> 0%
where the time goes in v7:
time: 37.2 us; the launch traced here: 37 us
  blocking collectives  18.4 us (49%)
  waiting for transfers between devices  7.07 us (19%)
  Pallas kernels  5.99 us (16%)
  starting transfers between devices  4.88 us (13%)
  between operations  0.68 us (2%)
    all_to_all x1, blocking collectives, on_device(): lax.all_to_all(terms, 'layer', split_axis=0, concat_axis=0, tiled=True)  10.5 us
    all_to_all x1, blocking collectives, on_device(): lax.all_to_all(asked, 'store', split_axis=0, concat_axis=0, tiled=True)  7.86 us
    ppermute x7, waiting for transfers between devices, swap(): lax.ppermute(value, axis, [(i, i ^ distance) for i in range(lax.axis_size...  7.07 us
    ppermute x7, starting transfers between devices, swap(): lax.ppermute(value, axis, [(i, i ^ distance) for i in range(lax.axis_size...  4.88 us
    pallas_call x1, Pallas kernels, on_device(): pl.pallas_call(functools.partial(condition_kernel, holders, capacity), ou...  3.01 us
    pallas_call x1, Pallas kernels, on_device(): pl.pallas_call(functools.partial(score_kernel, holders, capacity), out_sh...  1.85 us
    pallas_call x1, Pallas kernels, on_device(): pl.pallas_call(add_kernel, out_shape=jax.ShapeDtypeStruct((1, share, tota...  0.76 us
  transfers between devices with their start and end apart: 7, of which 5 were waited for; matrix products, arithmetic and copies ran while one was open for 0% of the time, Pallas kernels for 0%

profile of v7, /device:TPU:0, one launch (start us, length us, event | category | flops | bytes accessed | tf_op | source)
XLA Modules:
  0.0 37.0 jit_solution(5415515357240987386)
XLA Ops:
  0.7 3.0 %shard_map.73 = (bf16[8,8320]{1,0:T(8,128)(2,1)S(1)}, bf16[256,8192]{1,0:T(8,128)(2,1)S(1)}, f32[8,256]{1,0:T(8,128)S(1)}) custom-call(s32[1]{0:T(128)S(6)} %copy.8.count_ref, bf16[8,8192]{1,0:T(8,128)(2,1)} %refs_0_.1, f32[2,64,64]{2,1,0:T(8,128)} %refs_1_.1, f32[2,64,64]{2,1,0:T(8,128)} %refs_2_.1, s32[16,128]{1,0:T(8,128)} %bitcast.1, s32[1,256]{1,0:T(1,128)} %refs_4_.1, ...), custom_call_target="tpu_custom_call" | custom-call | tf_op jit(solution)/shard_map/pallas_call | solution.py:206
  3.7 4.0 %collective-permute-start.5 = (bf16[8,8320]{1,0:T(8,128)(2,1)S(1)}, bf16[8,8320]{1,0:T(8,128)(2,1)S(1)}, u32[]{:S(2)}, u32[]{:S(2)}) collective-permute-start(bf16[8,8320]{1,0:T(8,128)(2,1)S(1)} %get-tuple-element.9.refs_0_), channel_id=1, source_target_pairs={{0,24},{4,28},{8,16},{12,20},{16,8},{20,12},{24,0},{28,4},{1,25},{... | collective-permute-start | bytes 399368 | tf_op jit(solution)/shard_map/ppermute | solution.py:187
  7.6 0.5 %collective-permute-start.3 = (bf16[8,8320]{1,0:T(8,128)(2,1)S(1)}, bf16[8,8320]{1,0:T(8,128)(2,1)S(1)}, u32[]{:S(2)}, u32[]{:S(2)}) collective-permute-start(bf16[8,8320]{1,0:T(8,128)(2,1)S(1)} %get-tuple-element.9.refs_0_), channel_id=1, source_target_pairs={{0,16},{4,20},{8,24},{12,28},{16,0},{20,4},{24,8},{28,12},{1,17},{... | collective-permute-start | bytes 399368 | tf_op jit(solution)/shard_map/ppermute | solution.py:187
  8.1 0.1 collective-permute-start.1
  8.3 0.0 collective-permute-start
  8.3 3.3 %collective-permute-done.5.refs_6_ = bf16[8,8320]{1,0:T(8,128)(2,1)S(1)} collective-permute-done((bf16[8,8320]{1,0:T(8,128)(2,1)S(1)}, bf16[8,8320]{1,0:T(8,128)(2,1)S(1)}, u32[]{:S(2)}, u32[]{:S(2)}) %collective-permute-start.5) | collective-permute-done | bytes 133152 | tf_op jit(solution)/shard_map/ppermute | solution.py:187
  11.6 0.0 collective-permute-start.6
  11.6 2.4 %collective-permute-done.3.refs_4_ = bf16[8,8320]{1,0:T(8,128)(2,1)S(1)} collective-permute-done((bf16[8,8320]{1,0:T(8,128)(2,1)S(1)}, bf16[8,8320]{1,0:T(8,128)(2,1)S(1)}, u32[]{:S(2)}, u32[]{:S(2)}) %collective-permute-start.3) | collective-permute-done | bytes 133152 | tf_op jit(solution)/shard_map/ppermute | solution.py:187
  14.0 0.0 collective-permute-start.4
  14.0 0.2 collective-permute-done.1.refs_2_
  14.3 0.3 collective-permute-start.2
  14.5 0.0 collective-permute-done.refs_1_
  14.5 0.0 collective-permute-done.6.refs_7_
  14.5 0.8 %collective-permute-done.4.refs_5_ = bf16[8,8320]{1,0:T(8,128)(2,1)S(1)} collective-permute-done((bf16[8,8320]{1,0:T(8,128)(2,1)S(1)}, bf16[8,8320]{1,0:T(8,128)(2,1)S(1)}, u32[]{:S(2)}, u32[]{:S(2)}) %collective-permute-start.4) | collective-permute-done | bytes 133152 | tf_op jit(solution)/shard_map/ppermute | solution.py:187
  15.4 0.3 collective-permute-done.2.refs_3_
  15.6 1.9 %shard_map.74 = f32[8,16,128]{2,1,0:T(8,128)S(1)} custom-call(bf16[8,8320]{1,0:T(8,128)(2,1)S(1)} %get-tuple-element.9.refs_0_, bf16[8,8320]{1,0:T(8,128)(2,1)S(1)} %collective-permute-done.refs_1_, bf16[8,8320]{1,0:T(8,128)(2,1)S(1)} %collective-permute-done.1.refs_2_, bf16[8,8320]{1,0:T(8,128)(2,1)S(1)} %collective-permute-done.2.refs_3_, ...), custom_call_target="tpu_custom_call" | custom-call | tf_op jit(solution)/shard_map/pallas_call | solution.py:230
  17.5 7.9 %all_to_all.10.landed_ref = f32[8,16,128]{2,1,0:T(8,128)S(1)} all-to-all(f32[8,16,128]{2,1,0:T(8,128)S(1)} %shard_map.74), channel_id=1, replica_groups=mesh['store'=8,'layer'=4] {'store'}, dimensions={0} | all-to-all | bytes 131072 | tf_op jit(solution)/shard_map/all_to_all | solution.py:239
  25.3 0.4 %shard_map.75 = f32[4,32,128]{2,1,0:T(8,128)S(1)} custom-call(f32[8,256]{1,0:T(8,128)S(1)} %get-tuple-element.8.found_ref, f32[8,16,128]{2,1,0:T(8,128)S(1)} %all_to_all.10.landed_ref), custom_call_target="tpu_custom_call" | custom-call | tf_op jit(solution)/shard_map/pallas_call | solution.py:241
  25.7 10.5 %all_to_all.11.terms_ref = f32[4,32,128]{2,1,0:T(8,128)S(1)} all-to-all(f32[4,32,128]{2,1,0:T(8,128)S(1)} %shard_map.75), channel_id=1, replica_groups=mesh['store'=8,'layer'=4] {'layer'}, dimensions={0} | all-to-all | bytes 131072 | tf_op jit(solution)/shard_map/all_to_all | solution.py:248
  36.3 0.8 %shard_map.76 = f32[1,64,64]{2,1,0:T(8,128)} custom-call(f32[4,32,128]{2,1,0:T(8,128)S(1)} %all_to_all.11.terms_ref), custom_call_target="tpu_custom_call" | custom-call | tf_op jit(solution)/shard_map/pallas_call | solution.py:249
Async XLA Ops:
  3.7 7.9 %collective-permute-start.5 = (bf16[8,8320]{1,0:T(8,128)(2,1)S(1)}, bf16[8,8320]{1,0:T(8,128)(2,1)S(1)}, u32[]{:S(2)}, u32[]{:S(2)}) collective-permute-start(bf16[8,8320]{1,0:T(8,128)(2,1)S(1)} %get-tuple-element.9.refs_0_), channel_id=1, source_target_pairs={{0,24},{4,28},{8,16},{12,20},{16,8},{20,12},{24,0},{28,4},{1,25},{... | collective-permute-start | bytes 399368 | tf_op jit(solution)/shard_map/ppermute | solution.py:187
  7.6 6.4 %collective-permute-start.3 = (bf16[8,8320]{1,0:T(8,128)(2,1)S(1)}, bf16[8,8320]{1,0:T(8,128)(2,1)S(1)}, u32[]{:S(2)}, u32[]{:S(2)}) collective-permute-start(bf16[8,8320]{1,0:T(8,128)(2,1)S(1)} %get-tuple-element.9.refs_0_), channel_id=1, source_target_pairs={{0,16},{4,20},{8,24},{12,28},{16,0},{20,4},{24,8},{28,12},{1,17},{... | collective-permute-start | bytes 399368 | tf_op jit(solution)/shard_map/ppermute | solution.py:187
  8.1 6.1 %collective-permute-start.1 = (bf16[8,8320]{1,0:T(8,128)(2,1)S(1)}, bf16[8,8320]{1,0:T(8,128)(2,1)S(1)}, u32[]{:S(2)}, u32[]{:S(2)}) collective-permute-start(bf16[8,8320]{1,0:T(8,128)(2,1)S(1)} %get-tuple-element.9.refs_0_), channel_id=1, source_target_pairs={{0,8},{4,12},{8,0},{12,4},{16,24},{20,28},{24,16},{28,20},{1,9},{5... | collective-permute-start | bytes 399368 | tf_op jit(solution)/shard_map/ppermute | solution.py:187
  8.3 6.3 %collective-permute-start = (bf16[8,8320]{1,0:T(8,128)(2,1)S(1)}, bf16[8,8320]{1,0:T(8,128)(2,1)S(1)}, u32[]{:S(2)}, u32[]{:S(2)}) collective-permute-start(bf16[8,8320]{1,0:T(8,128)(2,1)S(1)} %get-tuple-element.9.refs_0_), channel_id=1, source_target_pairs={{0,4},{4,0},{8,12},{12,8},{16,20},{20,16},{24,28},{28,24},{1,5},{5... | collective-permute-start | bytes 399368 | tf_op jit(solution)/shard_map/ppermute | solution.py:187
  11.6 3.0 %collective-permute-start.6 = (bf16[8,8320]{1,0:T(8,128)(2,1)S(1)}, bf16[8,8320]{1,0:T(8,128)(2,1)S(1)}, u32[]{:S(2)}, u32[]{:S(2)}) collective-permute-start(bf16[8,8320]{1,0:T(8,128)(2,1)S(1)} %collective-permute-done.5.refs_6_), channel_id=1, source_target_pairs={{0,4},{4,0},{8,12},{12,8},{16,20},{20,16},{24,28},{28,24},{1,5},{5... | collective-permute-start | bytes 399368 | tf_op jit(solution)/shard_map/ppermute | solution.py:187
  14.0 1.4 %collective-permute-start.4 = (bf16[8,8320]{1,0:T(8,128)(2,1)S(1)}, bf16[8,8320]{1,0:T(8,128)(2,1)S(1)}, u32[]{:S(2)}, u32[]{:S(2)}) collective-permute-start(bf16[8,8320]{1,0:T(8,128)(2,1)S(1)} %collective-permute-done.3.refs_4_), channel_id=1, source_target_pairs={{0,4},{4,0},{8,12},{12,8},{16,20},{20,16},{24,28},{28,24},{1,5},{5... | collective-permute-start | bytes 399368 | tf_op jit(solution)/shard_map/ppermute | solution.py:187
  14.3 1.4 %collective-permute-start.2 = (bf16[8,8320]{1,0:T(8,128)(2,1)S(1)}, bf16[8,8320]{1,0:T(8,128)(2,1)S(1)}, u32[]{:S(2)}, u32[]{:S(2)}) collective-permute-start(bf16[8,8320]{1,0:T(8,128)(2,1)S(1)} %collective-permute-done.1.refs_2_), channel_id=1, source_target_pairs={{0,4},{4,0},{8,12},{12,8},{16,20},{20,16},{24,28},{28,24},{1,5},{5... | collective-permute-start | bytes 399368 | tf_op jit(solution)/shard_map/ppermute | solution.py:187

commit v8 on v6

--- a/solution.py
+++ b/solution.py
@@ -17,6 +17,22 @@
 
 def iota(shape, dimension):
     return lax.broadcasted_iota(jnp.int32, shape, dimension)
+
+
+def gather_plan(holders):
+    if holders == 8:
+        across = [((2, 4), None), ((4, 2), None), ((4, 2), 0)]
+    else:
+        across = [((k, k), None) for k in range(2, holders, 2)]
+    plan, owners = [], []
+    for pairs, source in across:
+        before = owners[source] if source is not None else (0, 0)
+        owners.append((before[0] ^ pairs[0], before[1] ^ pairs[1]))
+        plan.append((source, pairs, owners[-1]))
+    plan.append((None, (1, 1), (1, 1)))
+    for place in range(len(across)):
+        plan.append((place, (1, 1), (owners[place][1] ^ 1, owners[place][0] ^ 1)))
+    return plan
 
 
 def layer_steps(groups):
@@ -136,6 +152,7 @@
 def score_kernel(holders, capacity, *refs):
     packed_refs, pages_ref, out_ref, total = refs[:holders], refs[holders], refs[holders + 1], refs[holders + 2]
     me = lax.axis_index("store")
+    owners = [me] + [me ^ jnp.where(me % 2 == 1, second, first) for _, _, (first, second) in gather_plan(holders)]
     count, width = pages_ref.shape
     rows = packed_refs[0].shape[0]
     half = capacity // 2
@@ -149,7 +166,7 @@
             preferred_element_type=jnp.float32,
         )
     for k in range(holders):
-        start = pl.multiple_of((me ^ k) * rows, rows)
+        start = pl.multiple_of(owners[k] * rows, rows)
         total[pl.ds(start, rows), :] = scores[k * rows:(k + 1) * rows]
     asked = []
     for k in range(holders):
@@ -171,7 +188,7 @@
                 chosen, wide, (((0,), (1,)), ((), ())), preferred_element_type=jnp.float32
             )
     for k in range(holders):
-        out_ref[me ^ k] = picked[k * half:(k + 1) * half]
+        out_ref[owners[k]] = picked[k * half:(k + 1) * half]
 
 
 def spread_kernel(holders, found_ref, landed_ref, keep_ref, send_ref):
@@ -232,13 +249,11 @@
         compiler_params=pltpu.CompilerParams(vmem_limit_bytes=10 * 2**20 + 24 * slots * slots),
     )(counts, *sources)
 
-    blocks = [None] * holders
-    blocks[0] = packed
-    blocks[1] = swap(packed, "store", 1)
-    for k in range(2, holders, 2):
-        blocks[k] = swap(packed, "store", k)
-    for k in range(2, holders, 2):
-        blocks[k + 1] = swap(blocks[k], "store", 1)
+    blocks = []
+    for source, pairs, _ in gather_plan(holders):
+        moving = packed if source is None else blocks[source]
+        blocks.append(lax.ppermute(moving, "store", [(i, i ^ pairs[i % 2]) for i in range(holders)]))
+    blocks = [packed] + blocks
 
     total = holders * rows
     bytes_in = 2 * holders * rows * (width + notes) + 2 * per_holder * width

time: 35.4 us -> 37.5 us (1.059)
  starting transfers between devices: 9.36 us -> 10.8 us
  blocking collectives: 7.86 us -> 8.73 us
    ppermute x9 -> x2, waiting for transfers between devices: 11.4 us -> 4.56 us  [swap(): lax.ppermute(value, axis, [(i, i ^ distance) for i in range(lax.axis_size...]
    ppermute x0 -> x7, starting transfers between devices: none -> 6.6 us  [on_device(): lax.ppermute(moving, 'store', [(i, i ^ pairs[i % 2]) for i in range(holde...]
    ppermute x0 -> x7, waiting for transfers between devices: none -> 6.55 us  [on_device(): lax.ppermute(moving, 'store', [(i, i ^ pairs[i % 2]) for i in range(holde...]
    ppermute x9 -> x2, starting transfers between devices: 9.36 us -> 4.24 us  [swap(): lax.ppermute(value, axis, [(i, i ^ distance) for i in range(lax.axis_size...]
    all_to_all x1, blocking collectives: 7.86 us -> 8.73 us  [on_device(): lax.all_to_all(asked, 'store', split_axis=0, concat_axis=0, tiled=True)]
  transfers between devices with their start and end apart: 9 -> 9, of which waited for: 7 -> 5; matrix products, arithmetic and copies ran while one was open for 0% -> 0% of each run, Pallas kernels for 0% -> 0%
where the time goes in v8:
time: 37.5 us; the launch traced here: 37.3 us
  waiting for transfers between devices  11.1 us (30%)
  starting transfers between devices  10.8 us (29%)
  blocking collectives  8.73 us (23%)
  Pallas kernels  5.84 us (16%)
  between operations  0.7 us (2%)
    all_to_all x1, blocking collectives, on_device(): lax.all_to_all(asked, 'store', split_axis=0, concat_axis=0, tiled=True)  8.73 us
    ppermute x7, starting transfers between devices, on_device(): lax.ppermute(moving, 'store', [(i, i ^ pairs[i % 2]) for i in range(holde...  6.6 us
    ppermute x7, waiting for transfers between devices, on_device(): lax.ppermute(moving, 'store', [(i, i ^ pairs[i % 2]) for i in range(holde...  6.55 us
    ppermute x2, waiting for transfers between devices, swap(): lax.ppermute(value, axis, [(i, i ^ distance) for i in range(lax.axis_size...  4.56 us
    ppermute x2, starting transfers between devices, swap(): lax.ppermute(value, axis, [(i, i ^ distance) for i in range(lax.axis_size...  4.24 us
    pallas_call x1, Pallas kernels, on_device(): pl.pallas_call(functools.partial(condition_kernel, holders, groups, capac...  3 us
    pallas_call x1, Pallas kernels, on_device(): pl.pallas_call(functools.partial(score_kernel, holders, capacity), out_sh...  1.84 us
  transfers between devices with their start and end apart: 9, of which 5 were waited for; matrix products, arithmetic and copies ran while one was open for 0% of the time, Pallas kernels for 0%

profile of v8, /device:TPU:0, one launch (start us, length us, event | category | flops | bytes accessed | tf_op | source)
XLA Modules:
  0.0 37.3 jit_solution(2090577941677434102)
XLA Ops:
  0.7 3.0 %shard_map.73 = (bf16[8,8320]{1,0:T(8,128)(2,1)S(1)}, bf16[256,8192]{1,0:T(8,128)(2,1)S(1)}, f32[8,256]{1,0:T(8,128)S(1)}) custom-call(s32[1]{0:T(128)S(6)} %copy.8.count_ref, bf16[8,8192]{1,0:T(8,128)(2,1)} %refs_0_.1, f32[2,64,64]{2,1,0:T(8,128)} %refs_1_.1, f32[2,64,64]{2,1,0:T(8,128)} %refs_2_.1, s32[16,128]{1,0:T(8,128)} %bitcast.1, s32[1,256]{1,0:T(1,128)} %refs_4_.1, ...), custom_call_target="tpu_custom_call" | custom-call | tf_op jit(solution)/shard_map/pallas_call | solution.py:238
  3.7 3.0 %collective-permute-start = (bf16[8,8320]{1,0:T(8,128)(2,1)S(1)}, bf16[8,8320]{1,0:T(8,128)(2,1)S(1)}, u32[]{:S(2)}, u32[]{:S(2)}) collective-permute-start(bf16[8,8320]{1,0:T(8,128)(2,1)S(1)} %get-tuple-element.11.refs_0_), channel_id=1, source_target_pairs={{0,8},{4,20},{8,0},{12,28},{16,24},{20,4},{24,16},{28,12},{1,9},{5... | collective-permute-start | bytes 399368 | tf_op jit(solution)/shard_map/ppermute | solution.py:255
  6.7 1.5 %collective-permute-start.1 = (bf16[8,8320]{1,0:T(8,128)(2,1)S(1)}, bf16[8,8320]{1,0:T(8,128)(2,1)S(1)}, u32[]{:S(2)}, u32[]{:S(2)}) collective-permute-start(bf16[8,8320]{1,0:T(8,128)(2,1)S(1)} %get-tuple-element.11.refs_0_), channel_id=1, source_target_pairs={{0,16},{4,12},{8,24},{12,4},{16,0},{20,28},{24,8},{28,20},{1,17},{... | collective-permute-start | bytes 399368 | tf_op jit(solution)/shard_map/ppermute | solution.py:255
  8.2 2.3 %collective-permute-done.refs_1_ = bf16[8,8320]{1,0:T(8,128)(2,1)S(1)} collective-permute-done((bf16[8,8320]{1,0:T(8,128)(2,1)S(1)}, bf16[8,8320]{1,0:T(8,128)(2,1)S(1)}, u32[]{:S(2)}, u32[]{:S(2)}) %collective-permute-start) | collective-permute-done | bytes 133152 | tf_op jit(solution)/shard_map/ppermute | solution.py:255
  10.5 1.6 %collective-permute-start.2 = (bf16[8,8320]{1,0:T(8,128)(2,1)S(1)}, bf16[8,8320]{1,0:T(8,128)(2,1)S(1)}, u32[]{:S(2)}, u32[]{:S(2)}) collective-permute-start(bf16[8,8320]{1,0:T(8,128)(2,1)S(1)} %collective-permute-done.refs_1_), channel_id=1, source_target_pairs={{0,16},{4,12},{8,24},{12,4},{16,0},{20,28},{24,8},{28,20},{1,17},{... | collective-permute-start | bytes 399368 | tf_op jit(solution)/shard_map/ppermute | solution.py:255
  12.1 0.0 collective-permute-start.3
  12.1 0.5 %collective-permute-start.4 = (bf16[8,8320]{1,0:T(8,128)(2,1)S(1)}, bf16[8,8320]{1,0:T(8,128)(2,1)S(1)}, u32[]{:S(2)}, u32[]{:S(2)}) collective-permute-start(bf16[8,8320]{1,0:T(8,128)(2,1)S(1)} %collective-permute-done.refs_1_), channel_id=1, source_target_pairs={{0,4},{4,0},{8,12},{12,8},{16,20},{20,16},{24,28},{28,24},{1,5},{5... | collective-permute-start | bytes 399368 | tf_op jit(solution)/shard_map/ppermute | solution.py:255
  12.6 0.0 collective-permute-done.1.refs_2_
  12.6 0.0 collective-permute-start.5
  12.6 2.9 %collective-permute-done.2.refs_3_ = bf16[8,8320]{1,0:T(8,128)(2,1)S(1)} collective-permute-done((bf16[8,8320]{1,0:T(8,128)(2,1)S(1)}, bf16[8,8320]{1,0:T(8,128)(2,1)S(1)}, u32[]{:S(2)}, u32[]{:S(2)}) %collective-permute-start.2) | collective-permute-done | bytes 133152 | tf_op jit(solution)/shard_map/ppermute | solution.py:255
  15.5 0.0 collective-permute-start.6
  15.5 0.0 collective-permute-done.3.refs_4_
  15.5 0.0 collective-permute-done.5.refs_6_
  15.5 0.0 collective-permute-done.4.refs_5_
  15.5 1.3 %collective-permute-done.6.refs_7_ = bf16[8,8320]{1,0:T(8,128)(2,1)S(1)} collective-permute-done((bf16[8,8320]{1,0:T(8,128)(2,1)S(1)}, bf16[8,8320]{1,0:T(8,128)(2,1)S(1)}, u32[]{:S(2)}, u32[]{:S(2)}) %collective-permute-start.6) | collective-permute-done | bytes 133152 | tf_op jit(solution)/shard_map/ppermute | solution.py:255
  16.8 1.8 %shard_map.74 = f32[8,16,128]{2,1,0:T(8,128)S(1)} custom-call(bf16[8,8320]{1,0:T(8,128)(2,1)S(1)} %get-tuple-element.11.refs_0_, bf16[8,8320]{1,0:T(8,128)(2,1)S(1)} %collective-permute-done.refs_1_, bf16[8,8320]{1,0:T(8,128)(2,1)S(1)} %collective-permute-done.1.refs_2_, bf16[8,8320]{1,0:T(8,128)(2,1)S(1)} %collective-permute-done.2.refs_3_, ...), custom_call_target="tpu_custom_call" | custom-call | tf_op jit(solution)/shard_map/pallas_call | solution.py:260
  18.7 8.7 %all_to_all.5.landed_ref = f32[8,16,128]{2,1,0:T(8,128)S(1)} all-to-all(f32[8,16,128]{2,1,0:T(8,128)S(1)} %shard_map.74), channel_id=1, replica_groups=mesh['store'=8,'layer'=4] {'store'}, dimensions={0} | all-to-all | bytes 131072 | tf_op jit(solution)/shard_map/all_to_all | solution.py:269
  27.4 0.3 shard_map.75
  27.7 1.6 %collective-permute-start.7 = (f32[64,128]{1,0:T(8,128)S(1)}, f32[64,128]{1,0:T(8,128)S(1)}, u32[]{:S(2)}, u32[]{:S(2)}) collective-permute-start(f32[64,128]{1,0:T(8,128)S(1)} %get-tuple-element.14), channel_id=1, source_target_pairs={{0,1},{1,0},{2,3},{3,2},{4,5},{5,4},{6,7},{7,6},{8,9},{9,8},{10,11... | collective-permute-start | bytes 98312 | tf_op jit(solution)/shard_map/ppermute | solution.py:219
  29.4 2.3 %collective-permute-done.7 = f32[64,128]{1,0:T(8,128)S(1)} collective-permute-done((f32[64,128]{1,0:T(8,128)S(1)}, f32[64,128]{1,0:T(8,128)S(1)}, u32[]{:S(2)}, u32[]{:S(2)}) %collective-permute-start.7) | collective-permute-done | bytes 32800 | tf_op jit(solution)/shard_map/ppermute | solution.py:219
  31.7 0.1 fusion
  31.8 2.6 %collective-permute-start.8 = (f32[64,64]{1,0:T(8,128)S(1)}, f32[64,64]{1,0:T(8,128)S(1)}, u32[]{:S(2)}, u32[]{:S(2)}) collective-permute-start(f32[64,64]{1,0:T(8,128)S(1)} %get-tuple-element.15), channel_id=1, source_target_pairs={{0,2},{1,3},{2,0},{3,1},{4,6},{5,7},{6,4},{7,5},{8,10},{9,11},{10,... | collective-permute-start | bytes 49160 | tf_op jit(solution)/shard_map/ppermute | solution.py:219
  34.4 2.2 %collective-permute-done.8.other_ref = f32[64,64]{1,0:T(8,128)S(1)} collective-permute-done((f32[64,64]{1,0:T(8,128)S(1)}, f32[64,64]{1,0:T(8,128)S(1)}, u32[]{:S(2)}, u32[]{:S(2)}) %collective-permute-start.8) | collective-permute-done | bytes 16416 | tf_op jit(solution)/shard_map/ppermute | solution.py:219
  36.6 0.7 %shard_map.76 = f32[1,64,64]{2,1,0:T(8,128)} custom-call(f32[64,64]{1,0:T(8,128)S(1)} %get-tuple-element.16.one_ref, f32[64,64]{1,0:T(8,128)S(1)} %collective-permute-done.8.other_ref), custom_call_target="tpu_custom_call" | custom-call | tf_op jit(solution)/shard_map/pallas_call | solution.py:284
  (1 shorter events, 0.0 us)
Async XLA Ops:
  3.7 6.8 %collective-permute-start = (bf16[8,8320]{1,0:T(8,128)(2,1)S(1)}, bf16[8,8320]{1,0:T(8,128)(2,1)S(1)}, u32[]{:S(2)}, u32[]{:S(2)}) collective-permute-start(bf16[8,8320]{1,0:T(8,128)(2,1)S(1)} %get-tuple-element.11.refs_0_), channel_id=1, source_target_pairs={{0,8},{4,20},{8,0},{12,28},{16,24},{20,4},{24,16},{28,12},{1,9},{5... | collective-permute-start | bytes 399368 | tf_op jit(solution)/shard_map/ppermute | solution.py:255
  6.7 5.9 %collective-permute-start.1 = (bf16[8,8320]{1,0:T(8,128)(2,1)S(1)}, bf16[8,8320]{1,0:T(8,128)(2,1)S(1)}, u32[]{:S(2)}, u32[]{:S(2)}) collective-permute-start(bf16[8,8320]{1,0:T(8,128)(2,1)S(1)} %get-tuple-element.11.refs_0_), channel_id=1, source_target_pairs={{0,16},{4,12},{8,24},{12,4},{16,0},{20,28},{24,8},{28,20},{1,17},{... | collective-permute-start | bytes 399368 | tf_op jit(solution)/shard_map/ppermute | solution.py:255
  10.5 5.0 %collective-permute-start.2 = (bf16[8,8320]{1,0:T(8,128)(2,1)S(1)}, bf16[8,8320]{1,0:T(8,128)(2,1)S(1)}, u32[]{:S(2)}, u32[]{:S(2)}) collective-permute-start(bf16[8,8320]{1,0:T(8,128)(2,1)S(1)} %collective-permute-done.refs_1_), channel_id=1, source_target_pairs={{0,16},{4,12},{8,24},{12,4},{16,0},{20,28},{24,8},{28,20},{1,17},{... | collective-permute-start | bytes 399368 | tf_op jit(solution)/shard_map/ppermute | solution.py:255
  12.1 3.4 %collective-permute-start.3 = (bf16[8,8320]{1,0:T(8,128)(2,1)S(1)}, bf16[8,8320]{1,0:T(8,128)(2,1)S(1)}, u32[]{:S(2)}, u32[]{:S(2)}) collective-permute-start(bf16[8,8320]{1,0:T(8,128)(2,1)S(1)} %get-tuple-element.11.refs_0_), channel_id=1, source_target_pairs={{0,4},{4,0},{8,12},{12,8},{16,20},{20,16},{24,28},{28,24},{1,5},{5... | collective-permute-start | bytes 399368 | tf_op jit(solution)/shard_map/ppermute | solution.py:255
  12.1 3.4 %collective-permute-start.4 = (bf16[8,8320]{1,0:T(8,128)(2,1)S(1)}, bf16[8,8320]{1,0:T(8,128)(2,1)S(1)}, u32[]{:S(2)}, u32[]{:S(2)}) collective-permute-start(bf16[8,8320]{1,0:T(8,128)(2,1)S(1)} %collective-permute-done.refs_1_), channel_id=1, source_target_pairs={{0,4},{4,0},{8,12},{12,8},{16,20},{20,16},{24,28},{28,24},{1,5},{5... | collective-permute-start | bytes 399368 | tf_op jit(solution)/shard_map/ppermute | solution.py:255
  12.6 2.9 %collective-permute-start.5 = (bf16[8,8320]{1,0:T(8,128)(2,1)S(1)}, bf16[8,8320]{1,0:T(8,128)(2,1)S(1)}, u32[]{:S(2)}, u32[]{:S(2)}) collective-permute-start(bf16[8,8320]{1,0:T(8,128)(2,1)S(1)} %collective-permute-done.1.refs_2_), channel_id=1, source_target_pairs={{0,4},{4,0},{8,12},{12,8},{16,20},{20,16},{24,28},{28,24},{1,5},{5... | collective-permute-start | bytes 399368 | tf_op jit(solution)/shard_map/ppermute | solution.py:255
  15.5 1.4 %collective-permute-start.6 = (bf16[8,8320]{1,0:T(8,128)(2,1)S(1)}, bf16[8,8320]{1,0:T(8,128)(2,1)S(1)}, u32[]{:S(2)}, u32[]{:S(2)}) collective-permute-start(bf16[8,8320]{1,0:T(8,128)(2,1)S(1)} %collective-permute-done.2.refs_3_), channel_id=1, source_target_pairs={{0,4},{4,0},{8,12},{12,8},{16,20},{20,16},{24,28},{28,24},{1,5},{5... | collective-permute-start | bytes 399368 | tf_op jit(solution)/shard_map/ppermute | solution.py:255
  27.7 4.0 %collective-permute-start.7 = (f32[64,128]{1,0:T(8,128)S(1)}, f32[64,128]{1,0:T(8,128)S(1)}, u32[]{:S(2)}, u32[]{:S(2)}) collective-permute-start(f32[64,128]{1,0:T(8,128)S(1)} %get-tuple-element.14), channel_id=1, source_target_pairs={{0,1},{1,0},{2,3},{3,2},{4,5},{5,4},{6,7},{7,6},{8,9},{9,8},{10,11... | collective-permute-start | bytes 98312 | tf_op jit(solution)/shard_map/ppermute | solution.py:219
  31.8 4.8 %collective-permute-start.8 = (f32[64,64]{1,0:T(8,128)S(1)}, f32[64,64]{1,0:T(8,128)S(1)}, u32[]{:S(2)}, u32[]{:S(2)}) collective-permute-start(f32[64,64]{1,0:T(8,128)S(1)} %get-tuple-element.15), channel_id=1, source_target_pairs={{0,2},{1,3},{2,0},{3,1},{4,6},{5,7},{6,4},{7,5},{8,10},{9,11},{10,... | collective-permute-start | bytes 49160 | tf_op jit(solution)/shard_map/ppermute | solution.py:219

commit v9 on v7

--- a/solution.py
+++ b/solution.py
@@ -32,7 +32,7 @@
     return value.astype(jnp.float32).astype(jnp.bfloat16)
 
 
-def condition_kernel(holders, capacity, count_ref, *refs):
+def condition_kernel(holders, groups, capacity, count_ref, *refs):
     sources, packed_ref, pages_ref, found_ref, landing, arrived = refs[:6], refs[6], refs[7], refs[8], refs[9:14], refs[14]
     copies = [
         pltpu.make_async_copy(source, target, arrived.at[i])
@@ -84,7 +84,17 @@
 
     slots = cand_ref.shape[1]
     home_rows = home_ref.shape[0]
+    share = slots // groups
+    at = lax.axis_index("layer")
     wanted = jnp.where(iota((1, slots), 1) < count_ref[0], cand_ref[...], -1)
+    ranges = [wanted[:, g * share:(g + 1) * share] for g in range(groups)]
+    ordered = []
+    for j in range(groups):
+        chosen = ranges[0]
+        for g in range(1, groups):
+            chosen = jnp.where((at ^ j) == g, ranges[g], chosen)
+        ordered.append(chosen)
+    wanted = jnp.concatenate(ordered, axis=1)
     known = jnp.maximum(wanted, 0)
     onehot = (iota((LANES, slots), 0) == known % LANES).astype(jnp.float32).astype(jnp.bfloat16)
     home = home_ref[...]
@@ -153,11 +163,11 @@
         out_ref[me ^ k] = picked[k * half:(k + 1) * half]
 
 
-def spread_kernel(holders, found_ref, landed_ref, out_ref):
+def spread_kernel(holders, found_ref, landed_ref, *out_refs):
     half = landed_ref.shape[1]
     slots = found_ref.shape[1]
     total = landed_ref.shape[2] // 2
-    groups = out_ref.shape[0]
+    groups = len(out_refs)
     share = slots // groups
     holder, rank_there = found_ref[0:1], found_ref[1:2]
     place = iota((holders * half, slots), 0).astype(jnp.float32)
@@ -172,13 +182,14 @@
             result = result + spread[side * total:(side + 1) * total]
     for g in range(groups):
         block = result[:, g * share:(g + 1) * share]
-        out_ref[g] = jnp.concatenate([block[:total // 2], block[total // 2:]], axis=1)
-
-
-def add_kernel(terms_ref, out_ref):
-    total = terms_ref[0]
-    for g in range(1, terms_ref.shape[0]):
-        total = total + terms_ref[g]
+        out_refs[g][...] = jnp.concatenate([block[:total // 2], block[total // 2:]], axis=1)
+
+
+def add_kernel(*refs):
+    out_ref = refs[-1]
+    total = refs[0][...]
+    for ref in refs[1:-1]:
+        total = total + ref[...]
     share = total.shape[1] // 2
     out_ref[0] = jnp.concatenate([total[:, :share], total[:, share:]], axis=0).T
 
@@ -204,7 +215,7 @@
     ]
     notes = max(LANES, holders // rows * capacity)
     packed, pages, found = pl.pallas_call(
-        functools.partial(condition_kernel, holders, capacity),
+        functools.partial(condition_kernel, holders, groups, capacity),
         out_shape=[
             jax.ShapeDtypeStruct((rows, width + notes), bf16),
             pltpu.VMEM(page_store.shape, bf16),
@@ -240,19 +251,19 @@
     share = slots // groups
     terms = pl.pallas_call(
         functools.partial(spread_kernel, holders),
-        out_shape=jax.ShapeDtypeStruct((groups, total // 2, 2 * share), jnp.float32),
+        out_shape=[jax.ShapeDtypeStruct((total // 2, 2 * share), jnp.float32)] * groups,
         in_specs=[VMEM] * 2,
-        out_specs=VMEM,
+        out_specs=[VMEM] * groups,
         compiler_params=pltpu.CompilerParams(vmem_limit_bytes=4 * 2**20 + 64 * total * slots),
     )(found, landed)
-    terms = lax.all_to_all(terms, "layer", split_axis=0, concat_axis=0, tiled=True)
+    terms = [terms[0]] + [swap(terms[j], "layer", j) for j in reversed(range(1, groups))]
     return pl.pallas_call(
         add_kernel,
         out_shape=jax.ShapeDtypeStruct((1, share, total), jnp.float32),
-        in_specs=[VMEM],
+        in_specs=[VMEM] * groups,
         out_specs=VMEM,
         compiler_params=pltpu.CompilerParams(vmem_limit_bytes=4 * 2**20),
-    )(terms)
+    )(*terms)
 
 
 def solution(mesh):

time: 37.2 us -> 35.1 us (0.944)
  blocking collectives: 18.4 us -> 7.86 us
  starting transfers between devices: 4.88 us -> 9.34 us
  waiting for transfers between devices: 7.07 us -> 11 us
    all_to_all x1 -> x0, blocking collectives: 10.5 us -> none  [on_device(): lax.all_to_all(terms, 'layer', split_axis=0, concat_axis=0, tiled=True)]
    ppermute x7 -> x10, starting transfers between devices: 4.88 us -> 9.34 us  [swap(): lax.ppermute(value, axis, [(i, i ^ distance) for i in range(lax.axis_size...]
    ppermute x7 -> x10, waiting for transfers between devices: 7.07 us -> 11 us  [swap(): lax.ppermute(value, axis, [(i, i ^ distance) for i in range(lax.axis_size...]
  transfers between devices with their start and end apart: 7 -> 10, of which waited for: 5 -> 7; matrix products, arithmetic and copies ran while one was open for 0% -> 0% of each run, Pallas kernels for 0% -> 0%
where the time goes in v9:
time: 35.1 us; the launch traced here: 34.9 us
  waiting for transfers between devices  11 us (31%)
  starting transfers between devices  9.34 us (27%)
  blocking collectives  7.86 us (22%)
  Pallas kernels  5.99 us (17%)
  between operations  0.69 us (2%)
    ppermute x10, waiting for transfers between devices, swap(): lax.ppermute(value, axis, [(i, i ^ distance) for i in range(lax.axis_size...  11 us
    ppermute x10, starting transfers between devices, swap(): lax.ppermute(value, axis, [(i, i ^ distance) for i in range(lax.axis_size...  9.34 us
    all_to_all x1, blocking collectives, on_device(): lax.all_to_all(asked, 'store', split_axis=0, concat_axis=0, tiled=True)  7.86 us
    pallas_call x1, Pallas kernels, on_device(): pl.pallas_call(functools.partial(condition_kernel, holders, groups, capac...  3 us
    pallas_call x1, Pallas kernels, on_device(): pl.pallas_call(functools.partial(score_kernel, holders, capacity), out_sh...  1.86 us
    pallas_call x1, Pallas kernels, on_device(): pl.pallas_call(add_kernel, out_shape=jax.ShapeDtypeStruct((1, share, tota...  0.76 us
  transfers between devices with their start and end apart: 10, of which 7 were waited for; matrix products, arithmetic and copies ran while one was open for 0% of the time, Pallas kernels for 0%

profile of v9, /device:TPU:0, one launch (start us, length us, event | category | flops | bytes accessed | tf_op | source)
XLA Modules:
  0.0 34.9 jit_solution(1781820957405884848)
XLA Ops:
  0.7 3.0 %shard_map.73 = (bf16[8,8320]{1,0:T(8,128)(2,1)S(1)}, bf16[256,8192]{1,0:T(8,128)(2,1)S(1)}, f32[8,256]{1,0:T(8,128)S(1)}) custom-call(s32[1]{0:T(128)S(6)} %copy.8.count_ref, bf16[8,8192]{1,0:T(8,128)(2,1)} %refs_0_.1, f32[2,64,64]{2,1,0:T(8,128)} %refs_1_.1, f32[2,64,64]{2,1,0:T(8,128)} %refs_2_.1, s32[16,128]{1,0:T(8,128)} %bitcast.1, s32[1,256]{1,0:T(1,128)} %refs_4_.1, ...), custom_call_target="tpu_custom_call" | custom-call | tf_op jit(solution)/shard_map/pallas_call | solution.py:217
  3.7 4.0 %collective-permute-start.5 = (bf16[8,8320]{1,0:T(8,128)(2,1)S(1)}, bf16[8,8320]{1,0:T(8,128)(2,1)S(1)}, u32[]{:S(2)}, u32[]{:S(2)}) collective-permute-start(bf16[8,8320]{1,0:T(8,128)(2,1)S(1)} %get-tuple-element.13.refs_0_), channel_id=1, source_target_pairs={{0,24},{4,28},{8,16},{12,20},{16,8},{20,12},{24,0},{28,4},{1,25},{... | collective-permute-start | bytes 399368 | tf_op jit(solution)/shard_map/ppermute | solution.py:198
  7.6 0.5 %collective-permute-start.3 = (bf16[8,8320]{1,0:T(8,128)(2,1)S(1)}, bf16[8,8320]{1,0:T(8,128)(2,1)S(1)}, u32[]{:S(2)}, u32[]{:S(2)}) collective-permute-start(bf16[8,8320]{1,0:T(8,128)(2,1)S(1)} %get-tuple-element.13.refs_0_), channel_id=1, source_target_pairs={{0,16},{4,20},{8,24},{12,28},{16,0},{20,4},{24,8},{28,12},{1,17},{... | collective-permute-start | bytes 399368 | tf_op jit(solution)/shard_map/ppermute | solution.py:198
  8.1 0.1 collective-permute-start.1
  8.3 0.0 collective-permute-start
  8.3 3.3 %collective-permute-done.5.refs_6_ = bf16[8,8320]{1,0:T(8,128)(2,1)S(1)} collective-permute-done((bf16[8,8320]{1,0:T(8,128)(2,1)S(1)}, bf16[8,8320]{1,0:T(8,128)(2,1)S(1)}, u32[]{:S(2)}, u32[]{:S(2)}) %collective-permute-start.5) | collective-permute-done | bytes 133152 | tf_op jit(solution)/shard_map/ppermute | solution.py:198
  11.6 0.0 collective-permute-start.6
  11.6 2.4 %collective-permute-done.3.refs_4_ = bf16[8,8320]{1,0:T(8,128)(2,1)S(1)} collective-permute-done((bf16[8,8320]{1,0:T(8,128)(2,1)S(1)}, bf16[8,8320]{1,0:T(8,128)(2,1)S(1)}, u32[]{:S(2)}, u32[]{:S(2)}) %collective-permute-start.3) | collective-permute-done | bytes 133152 | tf_op jit(solution)/shard_map/ppermute | solution.py:198
  14.0 0.0 collective-permute-start.4
  14.0 0.2 collective-permute-done.1.refs_2_
  14.3 0.3 collective-permute-start.2
  14.5 0.0 collective-permute-done.refs_1_
  14.5 0.0 collective-permute-done.6.refs_7_
  14.5 0.8 %collective-permute-done.4.refs_5_ = bf16[8,8320]{1,0:T(8,128)(2,1)S(1)} collective-permute-done((bf16[8,8320]{1,0:T(8,128)(2,1)S(1)}, bf16[8,8320]{1,0:T(8,128)(2,1)S(1)}, u32[]{:S(2)}, u32[]{:S(2)}) %collective-permute-start.4) | collective-permute-done | bytes 133152 | tf_op jit(solution)/shard_map/ppermute | solution.py:198
  15.4 0.2 collective-permute-done.2.refs_3_
  15.6 1.9 %shard_map.74 = f32[8,16,128]{2,1,0:T(8,128)S(1)} custom-call(bf16[8,8320]{1,0:T(8,128)(2,1)S(1)} %get-tuple-element.13.refs_0_, bf16[8,8320]{1,0:T(8,128)(2,1)S(1)} %collective-permute-done.refs_1_, bf16[8,8320]{1,0:T(8,128)(2,1)S(1)} %collective-permute-done.1.refs_2_, bf16[8,8320]{1,0:T(8,128)(2,1)S(1)} %collective-permute-done.2.refs_3_, ...), custom_call_target="tpu_custom_call" | custom-call | tf_op jit(solution)/shard_map/pallas_call | solution.py:241
  17.5 7.9 %all_to_all.5.landed_ref = f32[8,16,128]{2,1,0:T(8,128)S(1)} all-to-all(f32[8,16,128]{2,1,0:T(8,128)S(1)} %shard_map.74), channel_id=1, replica_groups=mesh['store'=8,'layer'=4] {'store'}, dimensions={0} | all-to-all | bytes 131072 | tf_op jit(solution)/shard_map/all_to_all | solution.py:250
  25.3 0.4 %shard_map.75 = (f32[32,128]{1,0:T(8,128)S(1)}, f32[32,128]{1,0:T(8,128)S(1)}, f32[32,128]{1,0:T(8,128)S(1)}, f32[32,128]{1,0:T(8,128)S(1)}) custom-call(f32[8,256]{1,0:T(8,128)S(1)} %get-tuple-element.12.found_ref, f32[8,16,128]{2,1,0:T(8,128)S(1)} %all_to_all.5.landed_ref), custom_call_target="tpu_custom_call" | custom-call | tf_op jit(solution)/shard_map/pallas_call | solution.py:252
  25.7 3.8 %collective-permute-start.7 = (f32[32,128]{1,0:T(8,128)S(1)}, f32[32,128]{1,0:T(8,128)S(1)}, u32[]{:S(2)}, u32[]{:S(2)}) collective-permute-start(f32[32,128]{1,0:T(8,128)S(1)} %get-tuple-element.16), channel_id=1, source_target_pairs={{0,3},{1,2},{2,1},{3,0},{4,7},{5,6},{6,5},{7,4},{8,11},{9,10},{10,... | collective-permute-start | bytes 49160 | tf_op jit(solution)/shard_map/ppermute | solution.py:198
  29.5 0.0 collective-permute-start.8
  29.5 0.7 %collective-permute-start.9 = (f32[32,128]{1,0:T(8,128)S(1)}, f32[32,128]{1,0:T(8,128)S(1)}, u32[]{:S(2)}, u32[]{:S(2)}) collective-permute-start(f32[32,128]{1,0:T(8,128)S(1)} %get-tuple-element.18), channel_id=1, source_target_pairs={{0,1},{1,0},{2,3},{3,2},{4,5},{5,4},{6,7},{7,6},{8,9},{9,8},{10,11... | collective-permute-start | bytes 49160 | tf_op jit(solution)/shard_map/ppermute | solution.py:198
  30.2 1.1 %collective-permute-done.7.refs_1_ = f32[32,128]{1,0:T(8,128)S(1)} collective-permute-done((f32[32,128]{1,0:T(8,128)S(1)}, f32[32,128]{1,0:T(8,128)S(1)}, u32[]{:S(2)}, u32[]{:S(2)}) %collective-permute-start.7) | collective-permute-done | bytes 16416 | tf_op jit(solution)/shard_map/ppermute | solution.py:198
  31.3 2.8 %collective-permute-done.8.refs_2_ = f32[32,128]{1,0:T(8,128)S(1)} collective-permute-done((f32[32,128]{1,0:T(8,128)S(1)}, f32[32,128]{1,0:T(8,128)S(1)}, u32[]{:S(2)}, u32[]{:S(2)}) %collective-permute-start.8) | collective-permute-done | bytes 16416 | tf_op jit(solution)/shard_map/ppermute | solution.py:198
  34.1 0.0 collective-permute-done.9.refs_3_
  34.1 0.8 %shard_map.76 = f32[1,64,64]{2,1,0:T(8,128)} custom-call(f32[32,128]{1,0:T(8,128)S(1)} %get-tuple-element.15.refs_0_, f32[32,128]{1,0:T(8,128)S(1)} %collective-permute-done.7.refs_1_, f32[32,128]{1,0:T(8,128)S(1)} %collective-permute-done.8.refs_2_, f32[32,128]{1,0:T(8,128)S(1)} %collective-permute-done.9.refs_3_), custom_call_target="tpu_custom_call" | custom-call | tf_op jit(solution)/shard_map/pallas_call | solution.py:260
Async XLA Ops:
  3.7 7.9 %collective-permute-start.5 = (bf16[8,8320]{1,0:T(8,128)(2,1)S(1)}, bf16[8,8320]{1,0:T(8,128)(2,1)S(1)}, u32[]{:S(2)}, u32[]{:S(2)}) collective-permute-start(bf16[8,8320]{1,0:T(8,128)(2,1)S(1)} %get-tuple-element.13.refs_0_), channel_id=1, source_target_pairs={{0,24},{4,28},{8,16},{12,20},{16,8},{20,12},{24,0},{28,4},{1,25},{... | collective-permute-start | bytes 399368 | tf_op jit(solution)/shard_map/ppermute | solution.py:198
  7.6 6.4 %collective-permute-start.3 = (bf16[8,8320]{1,0:T(8,128)(2,1)S(1)}, bf16[8,8320]{1,0:T(8,128)(2,1)S(1)}, u32[]{:S(2)}, u32[]{:S(2)}) collective-permute-start(bf16[8,8320]{1,0:T(8,128)(2,1)S(1)} %get-tuple-element.13.refs_0_), channel_id=1, source_target_pairs={{0,16},{4,20},{8,24},{12,28},{16,0},{20,4},{24,8},{28,12},{1,17},{... | collective-permute-start | bytes 399368 | tf_op jit(solution)/shard_map/ppermute | solution.py:198
  8.1 6.1 %collective-permute-start.1 = (bf16[8,8320]{1,0:T(8,128)(2,1)S(1)}, bf16[8,8320]{1,0:T(8,128)(2,1)S(1)}, u32[]{:S(2)}, u32[]{:S(2)}) collective-permute-start(bf16[8,8320]{1,0:T(8,128)(2,1)S(1)} %get-tuple-element.13.refs_0_), channel_id=1, source_target_pairs={{0,8},{4,12},{8,0},{12,4},{16,24},{20,28},{24,16},{28,20},{1,9},{5... | collective-permute-start | bytes 399368 | tf_op jit(solution)/shard_map/ppermute | solution.py:198
  8.3 6.3 %collective-permute-start = (bf16[8,8320]{1,0:T(8,128)(2,1)S(1)}, bf16[8,8320]{1,0:T(8,128)(2,1)S(1)}, u32[]{:S(2)}, u32[]{:S(2)}) collective-permute-start(bf16[8,8320]{1,0:T(8,128)(2,1)S(1)} %get-tuple-element.13.refs_0_), channel_id=1, source_target_pairs={{0,4},{4,0},{8,12},{12,8},{16,20},{20,16},{24,28},{28,24},{1,5},{5... | collective-permute-start | bytes 399368 | tf_op jit(solution)/shard_map/ppermute | solution.py:198
  11.6 3.0 %collective-permute-start.6 = (bf16[8,8320]{1,0:T(8,128)(2,1)S(1)}, bf16[8,8320]{1,0:T(8,128)(2,1)S(1)}, u32[]{:S(2)}, u32[]{:S(2)}) collective-permute-start(bf16[8,8320]{1,0:T(8,128)(2,1)S(1)} %collective-permute-done.5.refs_6_), channel_id=1, source_target_pairs={{0,4},{4,0},{8,12},{12,8},{16,20},{20,16},{24,28},{28,24},{1,5},{5... | collective-permute-start | bytes 399368 | tf_op jit(solution)/shard_map/ppermute | solution.py:198
  14.0 1.4 %collective-permute-start.4 = (bf16[8,8320]{1,0:T(8,128)(2,1)S(1)}, bf16[8,8320]{1,0:T(8,128)(2,1)S(1)}, u32[]{:S(2)}, u32[]{:S(2)}) collective-permute-start(bf16[8,8320]{1,0:T(8,128)(2,1)S(1)} %collective-permute-done.3.refs_4_), channel_id=1, source_target_pairs={{0,4},{4,0},{8,12},{12,8},{16,20},{20,16},{24,28},{28,24},{1,5},{5... | collective-permute-start | bytes 399368 | tf_op jit(solution)/shard_map/ppermute | solution.py:198
  14.3 1.4 %collective-permute-start.2 = (bf16[8,8320]{1,0:T(8,128)(2,1)S(1)}, bf16[8,8320]{1,0:T(8,128)(2,1)S(1)}, u32[]{:S(2)}, u32[]{:S(2)}) collective-permute-start(bf16[8,8320]{1,0:T(8,128)(2,1)S(1)} %collective-permute-done.1.refs_2_), channel_id=1, source_target_pairs={{0,4},{4,0},{8,12},{12,8},{16,20},{20,16},{24,28},{28,24},{1,5},{5... | collective-permute-start | bytes 399368 | tf_op jit(solution)/shard_map/ppermute | solution.py:198
  25.7 5.6 %collective-permute-start.7 = (f32[32,128]{1,0:T(8,128)S(1)}, f32[32,128]{1,0:T(8,128)S(1)}, u32[]{:S(2)}, u32[]{:S(2)}) collective-permute-start(f32[32,128]{1,0:T(8,128)S(1)} %get-tuple-element.16), channel_id=1, source_target_pairs={{0,3},{1,2},{2,1},{3,0},{4,7},{5,6},{6,5},{7,4},{8,11},{9,10},{10,... | collective-permute-start | bytes 49160 | tf_op jit(solution)/shard_map/ppermute | solution.py:198
  29.5 4.6 %collective-permute-start.8 = (f32[32,128]{1,0:T(8,128)S(1)}, f32[32,128]{1,0:T(8,128)S(1)}, u32[]{:S(2)}, u32[]{:S(2)}) collective-permute-start(f32[32,128]{1,0:T(8,128)S(1)} %get-tuple-element.17), channel_id=1, source_target_pairs={{0,2},{1,3},{2,0},{3,1},{4,6},{5,7},{6,4},{7,5},{8,10},{9,11},{10,... | collective-permute-start | bytes 49160 | tf_op jit(solution)/shard_map/ppermute | solution.py:198
  29.5 4.6 %collective-permute-start.9 = (f32[32,128]{1,0:T(8,128)S(1)}, f32[32,128]{1,0:T(8,128)S(1)}, u32[]{:S(2)}, u32[]{:S(2)}) collective-permute-start(f32[32,128]{1,0:T(8,128)S(1)} %get-tuple-element.18), channel_id=1, source_target_pairs={{0,1},{1,0},{2,3},{3,2},{4,5},{5,4},{6,7},{7,6},{8,9},{9,8},{10,11... | collective-permute-start | bytes 49160 | tf_op jit(solution)/shard_map/ppermute | solution.py:198

commit v10 on v9

--- a/solution.py
+++ b/solution.py
@@ -92,7 +92,7 @@
     for j in range(groups):
         chosen = ranges[0]
         for g in range(1, groups):
-            chosen = jnp.where((at ^ j) == g, ranges[g], chosen)
+            chosen = jnp.where((at + j) % groups == g, ranges[g], chosen)
         ordered.append(chosen)
     wanted = jnp.concatenate(ordered, axis=1)
     known = jnp.maximum(wanted, 0)
@@ -256,7 +256,9 @@
         out_specs=[VMEM] * groups,
         compiler_params=pltpu.CompilerParams(vmem_limit_bytes=4 * 2**20 + 64 * total * slots),
     )(found, landed)
-    terms = [terms[0]] + [swap(terms[j], "layer", j) for j in reversed(range(1, groups))]
+    terms = [terms[0]] + [
+        lax.ppermute(terms[j], "layer", [(g, (g + j) % groups) for g in range(groups)]) for j in range(1, groups)
+    ]
     return pl.pallas_call(
         add_kernel,
         out_shape=jax.ShapeDtypeStruct((1, share, total), jnp.float32),

time: 35.1 us -> 34.7 us (0.989)
  waiting for transfers between devices: 11 us -> 9.45 us
  starting transfers between devices: 9.34 us -> 10.6 us
    ppermute x0 -> x3, starting transfers between devices: none -> 5.69 us  [on_device(): lax.ppermute(terms[j], 'layer', [(g, (g + j) % groups) for g in range(gro...]
    ppermute x10 -> x7, starting transfers between devices: 9.34 us -> 4.89 us  [swap(): lax.ppermute(value, axis, [(i, i ^ distance) for i in range(lax.axis_size...]
    ppermute x10 -> x7, waiting for transfers between devices: 11 us -> 7.06 us  [swap(): lax.ppermute(value, axis, [(i, i ^ distance) for i in range(lax.axis_size...]
    ppermute x0 -> x3, waiting for transfers between devices: none -> 2.38 us  [on_device(): lax.ppermute(terms[j], 'layer', [(g, (g + j) % groups) for g in range(gro...]
where the time goes in v10:
time: 34.7 us; the launch traced here: 34.6 us
  starting transfers between devices  10.6 us (31%)
  waiting for transfers between devices  9.45 us (27%)
  blocking collectives  7.86 us (23%)
  Pallas kernels  5.99 us (17%)
  between operations  0.69 us (2%)
    all_to_all x1, blocking collectives, on_device(): lax.all_to_all(asked, 'store', split_axis=0, concat_axis=0, tiled=True)  7.86 us
    ppermute x7, waiting for transfers between devices, swap(): lax.ppermute(value, axis, [(i, i ^ distance) for i in range(lax.axis_size...  7.06 us
    ppermute x3, starting transfers between devices, on_device(): lax.ppermute(terms[j], 'layer', [(g, (g + j) % groups) for g in range(gro...  5.69 us
    ppermute x7, starting transfers between devices, swap(): lax.ppermute(value, axis, [(i, i ^ distance) for i in range(lax.axis_size...  4.89 us
    pallas_call x1, Pallas kernels, on_device(): pl.pallas_call(functools.partial(condition_kernel, holders, groups, capac...  3 us
    ppermute x3, waiting for transfers between devices, on_device(): lax.ppermute(terms[j], 'layer', [(g, (g + j) % groups) for g in range(gro...  2.38 us
    pallas_call x1, Pallas kernels, on_device(): pl.pallas_call(functools.partial(score_kernel, holders, capacity), out_sh...  1.86 us
    pallas_call x1, Pallas kernels, on_device(): pl.pallas_call(add_kernel, out_shape=jax.ShapeDtypeStruct((1, share, tota...  0.76 us
  transfers between devices with their start and end apart: 10, of which 7 were waited for; matrix products, arithmetic and copies ran while one was open for 0% of the time, Pallas kernels for 0%

profile of v10, /device:TPU:0, one launch (start us, length us, event | category | flops | bytes accessed | tf_op | source)
XLA Modules:
  0.0 34.6 jit_solution(16866921371604439109)
XLA Ops:
  0.7 3.0 %shard_map.73 = (bf16[8,8320]{1,0:T(8,128)(2,1)S(1)}, bf16[256,8192]{1,0:T(8,128)(2,1)S(1)}, f32[8,256]{1,0:T(8,128)S(1)}) custom-call(s32[1]{0:T(128)S(6)} %copy.8.count_ref, bf16[8,8192]{1,0:T(8,128)(2,1)} %refs_0_.1, f32[2,64,64]{2,1,0:T(8,128)} %refs_1_.1, f32[2,64,64]{2,1,0:T(8,128)} %refs_2_.1, s32[16,128]{1,0:T(8,128)} %bitcast.1, s32[1,256]{1,0:T(1,128)} %refs_4_.1, ...), custom_call_target="tpu_custom_call" | custom-call | tf_op jit(solution)/shard_map/pallas_call | solution.py:217
  3.7 4.0 %collective-permute-start.5 = (bf16[8,8320]{1,0:T(8,128)(2,1)S(1)}, bf16[8,8320]{1,0:T(8,128)(2,1)S(1)}, u32[]{:S(2)}, u32[]{:S(2)}) collective-permute-start(bf16[8,8320]{1,0:T(8,128)(2,1)S(1)} %get-tuple-element.13.refs_0_), channel_id=1, source_target_pairs={{0,24},{4,28},{8,16},{12,20},{16,8},{20,12},{24,0},{28,4},{1,25},{... | collective-permute-start | bytes 399368 | tf_op jit(solution)/shard_map/ppermute | solution.py:198
  7.6 0.5 %collective-permute-start.3 = (bf16[8,8320]{1,0:T(8,128)(2,1)S(1)}, bf16[8,8320]{1,0:T(8,128)(2,1)S(1)}, u32[]{:S(2)}, u32[]{:S(2)}) collective-permute-start(bf16[8,8320]{1,0:T(8,128)(2,1)S(1)} %get-tuple-element.13.refs_0_), channel_id=1, source_target_pairs={{0,16},{4,20},{8,24},{12,28},{16,0},{20,4},{24,8},{28,12},{1,17},{... | collective-permute-start | bytes 399368 | tf_op jit(solution)/shard_map/ppermute | solution.py:198
  8.1 0.1 collective-permute-start.1
  8.3 0.0 collective-permute-start
  8.3 3.3 %collective-permute-done.5.refs_6_ = bf16[8,8320]{1,0:T(8,128)(2,1)S(1)} collective-permute-done((bf16[8,8320]{1,0:T(8,128)(2,1)S(1)}, bf16[8,8320]{1,0:T(8,128)(2,1)S(1)}, u32[]{:S(2)}, u32[]{:S(2)}) %collective-permute-start.5) | collective-permute-done | bytes 133152 | tf_op jit(solution)/shard_map/ppermute | solution.py:198
  11.6 0.0 collective-permute-start.6
  11.6 2.4 %collective-permute-done.3.refs_4_ = bf16[8,8320]{1,0:T(8,128)(2,1)S(1)} collective-permute-done((bf16[8,8320]{1,0:T(8,128)(2,1)S(1)}, bf16[8,8320]{1,0:T(8,128)(2,1)S(1)}, u32[]{:S(2)}, u32[]{:S(2)}) %collective-permute-start.3) | collective-permute-done | bytes 133152 | tf_op jit(solution)/shard_map/ppermute | solution.py:198
  14.0 0.0 collective-permute-start.4
  14.0 0.2 collective-permute-done.1.refs_2_
  14.3 0.3 collective-permute-start.2
  14.5 0.0 collective-permute-done.refs_1_
  14.5 0.0 collective-permute-done.6.refs_7_
  14.5 0.8 %collective-permute-done.4.refs_5_ = bf16[8,8320]{1,0:T(8,128)(2,1)S(1)} collective-permute-done((bf16[8,8320]{1,0:T(8,128)(2,1)S(1)}, bf16[8,8320]{1,0:T(8,128)(2,1)S(1)}, u32[]{:S(2)}, u32[]{:S(2)}) %collective-permute-start.4) | collective-permute-done | bytes 133152 | tf_op jit(solution)/shard_map/ppermute | solution.py:198
  15.4 0.2 collective-permute-done.2.refs_3_
  15.6 1.9 %shard_map.74 = f32[8,16,128]{2,1,0:T(8,128)S(1)} custom-call(bf16[8,8320]{1,0:T(8,128)(2,1)S(1)} %get-tuple-element.13.refs_0_, bf16[8,8320]{1,0:T(8,128)(2,1)S(1)} %collective-permute-done.refs_1_, bf16[8,8320]{1,0:T(8,128)(2,1)S(1)} %collective-permute-done.1.refs_2_, bf16[8,8320]{1,0:T(8,128)(2,1)S(1)} %collective-permute-done.2.refs_3_, ...), custom_call_target="tpu_custom_call" | custom-call | tf_op jit(solution)/shard_map/pallas_call | solution.py:241
  17.5 7.9 %all_to_all.5.landed_ref = f32[8,16,128]{2,1,0:T(8,128)S(1)} all-to-all(f32[8,16,128]{2,1,0:T(8,128)S(1)} %shard_map.74), channel_id=1, replica_groups=mesh['store'=8,'layer'=4] {'store'}, dimensions={0} | all-to-all | bytes 131072 | tf_op jit(solution)/shard_map/all_to_all | solution.py:250
  25.3 0.4 %shard_map.75 = (f32[32,128]{1,0:T(8,128)S(1)}, f32[32,128]{1,0:T(8,128)S(1)}, f32[32,128]{1,0:T(8,128)S(1)}, f32[32,128]{1,0:T(8,128)S(1)}) custom-call(f32[8,256]{1,0:T(8,128)S(1)} %get-tuple-element.12.found_ref, f32[8,16,128]{2,1,0:T(8,128)S(1)} %all_to_all.5.landed_ref), custom_call_target="tpu_custom_call" | custom-call | tf_op jit(solution)/shard_map/pallas_call | solution.py:252
  25.7 1.7 %collective-permute-start.7 = (f32[32,128]{1,0:T(8,128)S(1)}, f32[32,128]{1,0:T(8,128)S(1)}, u32[]{:S(2)}, u32[]{:S(2)}) collective-permute-start(f32[32,128]{1,0:T(8,128)S(1)} %get-tuple-element.16), channel_id=1, source_target_pairs={{0,1},{1,2},{2,3},{3,0},{4,5},{5,6},{6,7},{7,4},{8,9},{9,10},{10,1... | collective-permute-start | bytes 49160 | tf_op jit(solution)/shard_map/ppermute | solution.py:260
  27.5 2.6 %collective-permute-start.8 = (f32[32,128]{1,0:T(8,128)S(1)}, f32[32,128]{1,0:T(8,128)S(1)}, u32[]{:S(2)}, u32[]{:S(2)}) collective-permute-start(f32[32,128]{1,0:T(8,128)S(1)} %get-tuple-element.17), channel_id=1, source_target_pairs={{0,2},{1,3},{2,0},{3,1},{4,6},{5,7},{6,4},{7,5},{8,10},{9,11},{10,... | collective-permute-start | bytes 49160 | tf_op jit(solution)/shard_map/ppermute | solution.py:260
  30.1 1.4 %collective-permute-start.9 = (f32[32,128]{1,0:T(8,128)S(1)}, f32[32,128]{1,0:T(8,128)S(1)}, u32[]{:S(2)}, u32[]{:S(2)}) collective-permute-start(f32[32,128]{1,0:T(8,128)S(1)} %get-tuple-element.18), channel_id=1, source_target_pairs={{0,3},{1,0},{2,1},{3,2},{4,7},{5,4},{6,5},{7,6},{8,11},{9,8},{10,9... | collective-permute-start | bytes 49160 | tf_op jit(solution)/shard_map/ppermute | solution.py:260
  31.4 0.0 collective-permute-done.7.refs_1_
  31.4 0.7 %collective-permute-done.8.refs_2_ = f32[32,128]{1,0:T(8,128)S(1)} collective-permute-done((f32[32,128]{1,0:T(8,128)S(1)}, f32[32,128]{1,0:T(8,128)S(1)}, u32[]{:S(2)}, u32[]{:S(2)}) %collective-permute-start.8) | collective-permute-done | bytes 16416 | tf_op jit(solution)/shard_map/ppermute | solution.py:260
  32.1 1.7 %collective-permute-done.9.refs_3_ = f32[32,128]{1,0:T(8,128)S(1)} collective-permute-done((f32[32,128]{1,0:T(8,128)S(1)}, f32[32,128]{1,0:T(8,128)S(1)}, u32[]{:S(2)}, u32[]{:S(2)}) %collective-permute-start.9) | collective-permute-done | bytes 16416 | tf_op jit(solution)/shard_map/ppermute | solution.py:260
  33.8 0.8 %shard_map.76 = f32[1,64,64]{2,1,0:T(8,128)} custom-call(f32[32,128]{1,0:T(8,128)S(1)} %get-tuple-element.15.refs_0_, f32[32,128]{1,0:T(8,128)S(1)} %collective-permute-done.7.refs_1_, f32[32,128]{1,0:T(8,128)S(1)} %collective-permute-done.8.refs_2_, f32[32,128]{1,0:T(8,128)S(1)} %collective-permute-done.9.refs_3_), custom_call_target="tpu_custom_call" | custom-call | tf_op jit(solution)/shard_map/pallas_call | solution.py:262
Async XLA Ops:
  3.7 7.9 %collective-permute-start.5 = (bf16[8,8320]{1,0:T(8,128)(2,1)S(1)}, bf16[8,8320]{1,0:T(8,128)(2,1)S(1)}, u32[]{:S(2)}, u32[]{:S(2)}) collective-permute-start(bf16[8,8320]{1,0:T(8,128)(2,1)S(1)} %get-tuple-element.13.refs_0_), channel_id=1, source_target_pairs={{0,24},{4,28},{8,16},{12,20},{16,8},{20,12},{24,0},{28,4},{1,25},{... | collective-permute-start | bytes 399368 | tf_op jit(solution)/shard_map/ppermute | solution.py:198
  7.6 6.4 %collective-permute-start.3 = (bf16[8,8320]{1,0:T(8,128)(2,1)S(1)}, bf16[8,8320]{1,0:T(8,128)(2,1)S(1)}, u32[]{:S(2)}, u32[]{:S(2)}) collective-permute-start(bf16[8,8320]{1,0:T(8,128)(2,1)S(1)} %get-tuple-element.13.refs_0_), channel_id=1, source_target_pairs={{0,16},{4,20},{8,24},{12,28},{16,0},{20,4},{24,8},{28,12},{1,17},{... | collective-permute-start | bytes 399368 | tf_op jit(solution)/shard_map/ppermute | solution.py:198
  8.1 6.1 %collective-permute-start.1 = (bf16[8,8320]{1,0:T(8,128)(2,1)S(1)}, bf16[8,8320]{1,0:T(8,128)(2,1)S(1)}, u32[]{:S(2)}, u32[]{:S(2)}) collective-permute-start(bf16[8,8320]{1,0:T(8,128)(2,1)S(1)} %get-tuple-element.13.refs_0_), channel_id=1, source_target_pairs={{0,8},{4,12},{8,0},{12,4},{16,24},{20,28},{24,16},{28,20},{1,9},{5... | collective-permute-start | bytes 399368 | tf_op jit(solution)/shard_map/ppermute | solution.py:198
  8.3 6.3 %collective-permute-start = (bf16[8,8320]{1,0:T(8,128)(2,1)S(1)}, bf16[8,8320]{1,0:T(8,128)(2,1)S(1)}, u32[]{:S(2)}, u32[]{:S(2)}) collective-permute-start(bf16[8,8320]{1,0:T(8,128)(2,1)S(1)} %get-tuple-element.13.refs_0_), channel_id=1, source_target_pairs={{0,4},{4,0},{8,12},{12,8},{16,20},{20,16},{24,28},{28,24},{1,5},{5... | collective-permute-start | bytes 399368 | tf_op jit(solution)/shard_map/ppermute | solution.py:198
  11.6 3.0 %collective-permute-start.6 = (bf16[8,8320]{1,0:T(8,128)(2,1)S(1)}, bf16[8,8320]{1,0:T(8,128)(2,1)S(1)}, u32[]{:S(2)}, u32[]{:S(2)}) collective-permute-start(bf16[8,8320]{1,0:T(8,128)(2,1)S(1)} %collective-permute-done.5.refs_6_), channel_id=1, source_target_pairs={{0,4},{4,0},{8,12},{12,8},{16,20},{20,16},{24,28},{28,24},{1,5},{5... | collective-permute-start | bytes 399368 | tf_op jit(solution)/shard_map/ppermute | solution.py:198
  14.0 1.4 %collective-permute-start.4 = (bf16[8,8320]{1,0:T(8,128)(2,1)S(1)}, bf16[8,8320]{1,0:T(8,128)(2,1)S(1)}, u32[]{:S(2)}, u32[]{:S(2)}) collective-permute-start(bf16[8,8320]{1,0:T(8,128)(2,1)S(1)} %collective-permute-done.3.refs_4_), channel_id=1, source_target_pairs={{0,4},{4,0},{8,12},{12,8},{16,20},{20,16},{24,28},{28,24},{1,5},{5... | collective-permute-start | bytes 399368 | tf_op jit(solution)/shard_map/ppermute | solution.py:198
  14.3 1.4 %collective-permute-start.2 = (bf16[8,8320]{1,0:T(8,128)(2,1)S(1)}, bf16[8,8320]{1,0:T(8,128)(2,1)S(1)}, u32[]{:S(2)}, u32[]{:S(2)}) collective-permute-start(bf16[8,8320]{1,0:T(8,128)(2,1)S(1)} %collective-permute-done.1.refs_2_), channel_id=1, source_target_pairs={{0,4},{4,0},{8,12},{12,8},{16,20},{20,16},{24,28},{28,24},{1,5},{5... | collective-permute-start | bytes 399368 | tf_op jit(solution)/shard_map/ppermute | solution.py:198
  25.7 5.7 %collective-permute-start.7 = (f32[32,128]{1,0:T(8,128)S(1)}, f32[32,128]{1,0:T(8,128)S(1)}, u32[]{:S(2)}, u32[]{:S(2)}) collective-permute-start(f32[32,128]{1,0:T(8,128)S(1)} %get-tuple-element.16), channel_id=1, source_target_pairs={{0,1},{1,2},{2,3},{3,0},{4,5},{5,6},{6,7},{7,4},{8,9},{9,10},{10,1... | collective-permute-start | bytes 49160 | tf_op jit(solution)/shard_map/ppermute | solution.py:260
  27.5 4.6 %collective-permute-start.8 = (f32[32,128]{1,0:T(8,128)S(1)}, f32[32,128]{1,0:T(8,128)S(1)}, u32[]{:S(2)}, u32[]{:S(2)}) collective-permute-start(f32[32,128]{1,0:T(8,128)S(1)} %get-tuple-element.17), channel_id=1, source_target_pairs={{0,2},{1,3},{2,0},{3,1},{4,6},{5,7},{6,4},{7,5},{8,10},{9,11},{10,... | collective-permute-start | bytes 49160 | tf_op jit(solution)/shard_map/ppermute | solution.py:260
  30.1 3.7 %collective-permute-start.9 = (f32[32,128]{1,0:T(8,128)S(1)}, f32[32,128]{1,0:T(8,128)S(1)}, u32[]{:S(2)}, u32[]{:S(2)}) collective-permute-start(f32[32,128]{1,0:T(8,128)S(1)} %get-tuple-element.18), channel_id=1, source_target_pairs={{0,3},{1,0},{2,1},{3,2},{4,7},{5,4},{6,5},{7,6},{8,11},{9,8},{10,9... | collective-permute-start | bytes 49160 | tf_op jit(solution)/shard_map/ppermute | solution.py:260

commit v11 on v10

--- a/solution.py
+++ b/solution.py
@@ -7,7 +7,6 @@
 from jax.experimental.pallas import tpu as pltpu
 from jax.sharding import PartitionSpec as P
 
-HIGHEST = lax.Precision.HIGHEST
 VMEM = pl.BlockSpec(memory_space=pltpu.VMEM)
 SMEM = pl.BlockSpec(memory_space=pltpu.SMEM)
 HBM = pl.BlockSpec(memory_space=pltpu.HBM)
@@ -34,6 +33,7 @@
 
 def condition_kernel(holders, groups, capacity, count_ref, *refs):
     sources, packed_ref, pages_ref, found_ref, landing, arrived = refs[:6], refs[6], refs[7], refs[8], refs[9:14], refs[14]
+    turned_ref = refs[15]
     copies = [
         pltpu.make_async_copy(source, target, arrived.at[i])
         for i, (source, target) in enumerate(zip(sources, landing + (pages_ref,)))
@@ -50,37 +50,55 @@
     query = query_ref[...].astype(jnp.float32)
     low = iota((half, LANES), 1) < rank
     zero = jnp.zeros((rank, rank), jnp.float32)
-    source = iota((rank, rank), 0)
-    place = iota((rank, rank), 1)
-    split = (source == 2 * (place % half) + place // half).astype(jnp.float32)
+    terms = [(0, 0), (0, 1), (0, 2), (1, 0), (1, 1), (2, 0)]
+    group = 2 * LANES
+    source, place = iota((rank, 2 * group), 0), iota((rank, 2 * group), 1)
+    inside = place % group
+    column_found = (source == 2 * (inside % half) + place // group)
+    chosen_part = sum((inside >= half * start).astype(jnp.int32) for start in (3, 5, 6))
+    pickers = [exact_bf16(column_found & (chosen_part == i)) for i in range(3)]
     for layer in range(layers):
         first = layer * half
         packed = jnp.concatenate(
             [query[:, (first + t) * LANES:(first + t + 1) * LANES] for t in range(half)], axis=0
         ).astype(jnp.bfloat16)
         factor = in_factor_ref[layer]
-        doubled = jnp.concatenate(
-            [jnp.concatenate([factor, zero], axis=1), jnp.concatenate([zero, factor], axis=1)], axis=0
-        )
-        right = sum(jnp.dot(packed, part, preferred_element_type=jnp.float32) for part in parts_of(doubled)[::-1])
-        right = jnp.swapaxes(right.reshape(half, rows, LANES), 0, 1)
-        wide = jnp.concatenate([right[q] for q in range(rows)], axis=1)
-        sorted_columns = jnp.dot(out_factor_ref[layer], split, precision=HIGHEST, preferred_element_type=jnp.float32)
-        sorted_both = lax.dot_general(
-            split, sorted_columns, (((0,), (0,)), ((), ())), precision=HIGHEST, preferred_element_type=jnp.float32
+        doubled = parts_of(
+            jnp.concatenate(
+                [jnp.concatenate([factor, zero], axis=1), jnp.concatenate([zero, factor], axis=1)], axis=0
+            )
+        )
+        small = jnp.dot(
+            jnp.concatenate([packed, packed], axis=1), jnp.concatenate(doubled[1:], axis=0),
+            preferred_element_type=jnp.float32,
+        )
+        turned_ref[layer] = small + jnp.dot(packed, doubled[0], preferred_element_type=jnp.float32)
+        wide = jnp.concatenate([turned_ref[layer, pl.ds(q, half, stride=rows), :] for q in range(rows)], axis=1)
+        wide = parts_of(wide)
+        stacked = jnp.concatenate([wide[j] for _, j in terms], axis=0)
+        by_row = jnp.concatenate(
+            [out_factor_ref[layer, pl.ds(parity, half, stride=2), :] for parity in range(2)], axis=0
+        )
+        sorted_columns = sum(
+            jnp.dot(part, picker, preferred_element_type=jnp.float32) for part, picker in zip(parts_of(by_row), pickers)
         )
         quarters = jnp.concatenate(
-            [sorted_both[r * half:(r + 1) * half, c * half:(c + 1) * half] for r in range(2) for c in range(2)], axis=0
-        )
-        left = jnp.dot(quarters, wide, precision=HIGHEST, preferred_element_type=jnp.float32)
-        done = []
+            [
+                sorted_columns[r * half:(r + 1) * half, c * group:c * group + len(terms) * half]
+                for r in range(2) for c in range(2)
+            ],
+            axis=0,
+        ).astype(jnp.bfloat16)
+        left = jnp.dot(quarters, stacked, preferred_element_type=jnp.float32)
         for q in range(rows):
             part = left[:, q * LANES:(q + 1) * LANES]
             ee, eo, oe, oo = (part[i * half:(i + 1) * half] for i in range(4))
-            done.append(jnp.where(low, ee, oo) + pltpu.roll(jnp.where(low, oe, eo), rank, 1))
-        done = jnp.swapaxes(jnp.stack(done), 0, 1)
+            done = jnp.where(low, ee, oo) + pltpu.roll(jnp.where(low, oe, eo), rank, 1)
+            turned_ref[layer, pl.ds(q, half, stride=rows), :] = done
         for t in range(half):
-            packed_ref[:, (first + t) * LANES:(first + t + 1) * LANES] = done[t].astype(jnp.bfloat16)
+            packed_ref[:, (first + t) * LANES:(first + t + 1) * LANES] = (
+                turned_ref[layer, t * rows:(t + 1) * rows, :].astype(jnp.bfloat16)
+            )
 
     slots = cand_ref.shape[1]
     home_rows = home_ref.shape[0]
@@ -123,7 +141,7 @@
 
 
 def score_kernel(holders, capacity, *refs):
-    packed_refs, pages_ref, out_ref, total = refs[:holders], refs[holders], refs[holders + 1], refs[holders + 2]
+    packed_refs, pages_ref, out_ref, total, queries = refs[:holders], *refs[holders:]
     me = lax.axis_index("store")
     count, width = pages_ref.shape
     rows = packed_refs[0].shape[0]
@@ -132,10 +150,10 @@
     scores = jnp.zeros((holders * rows, count), jnp.float32)
     for i in range(CHUNKS):
         columns = slice(i * step, (i + 1) * step)
-        queries = jnp.concatenate([ref[:, columns].astype(jnp.float32) for ref in packed_refs], axis=0)
+        for k in range(holders):
+            queries[k * rows:(k + 1) * rows, columns] = packed_refs[k][:, columns]
         scores = scores + lax.dot_general(
-            queries.astype(jnp.bfloat16), pages_ref[:, columns], (((1,), (1,)), ((), ())),
-            preferred_element_type=jnp.float32,
+            queries[:, columns], pages_ref[:, columns], (((1,), (1,)), ((), ())), preferred_element_type=jnp.float32
         )
     for k in range(holders):
         start = pl.multiple_of((me ^ k) * rows, rows)
@@ -224,7 +242,7 @@
         in_specs=[SMEM] + [HBM] * len(sources),
         out_specs=[VMEM] * 3,
         scratch_shapes=[pltpu.VMEM(source.shape, source.dtype) for source in sources[:-1]]
-        + [pltpu.SemaphoreType.DMA((len(sources),))],
+        + [pltpu.SemaphoreType.DMA((len(sources),)), pltpu.VMEM((layers, rows * rank // 2, LANES), jnp.float32)],
         compiler_params=pltpu.CompilerParams(vmem_limit_bytes=10 * 2**20 + 24 * slots * slots),
     )(counts, *sources)
 
@@ -243,8 +261,8 @@
         out_shape=jax.ShapeDtypeStruct((holders, capacity // 2, 2 * total), jnp.float32),
         in_specs=[VMEM] * (holders + 1),
         out_specs=VMEM,
-        scratch_shapes=[pltpu.VMEM((total, per_holder), jnp.float32)],
-        compiler_params=pltpu.CompilerParams(vmem_limit_bytes=8 * 2**20 + bytes_in + 48 * total * slots),
+        scratch_shapes=[pltpu.VMEM((total, per_holder), jnp.float32), pltpu.VMEM((total, width), bf16)],
+        compiler_params=pltpu.CompilerParams(vmem_limit_bytes=8 * 2**20 + 2 * bytes_in + 48 * total * slots),
     )(*blocks, pltpu.with_memory_space_constraint(pages, pltpu.VMEM))
 
     landed = lax.all_to_all(asked, "store", split_axis=0, concat_axis=0, tiled=True)

time: 34.7 us -> 34.2 us (0.986)
  Pallas kernels: 5.99 us -> 5.41 us
    pallas_call x1, Pallas kernels: 3 us -> 2.43 us  [on_device(): pl.pallas_call(functools.partial(condition_kernel, holders, groups, capac...]
where the time goes in v11:
time: 34.2 us; the launch traced here: 34 us
  starting transfers between devices  10.6 us (31%)
  waiting for transfers between devices  9.45 us (28%)
  blocking collectives  7.86 us (23%)
  Pallas kernels  5.41 us (16%)
  between operations  0.69 us (2%)
    all_to_all x1, blocking collectives, on_device(): lax.all_to_all(asked, 'store', split_axis=0, concat_axis=0, tiled=True)  7.86 us
    ppermute x7, waiting for transfers between devices, swap(): lax.ppermute(value, axis, [(i, i ^ distance) for i in range(lax.axis_size...  7.06 us
    ppermute x3, starting transfers between devices, on_device(): lax.ppermute(terms[j], 'layer', [(g, (g + j) % groups) for g in range(gro...  5.69 us
    ppermute x7, starting transfers between devices, swap(): lax.ppermute(value, axis, [(i, i ^ distance) for i in range(lax.axis_size...  4.88 us
    pallas_call x1, Pallas kernels, on_device(): pl.pallas_call(functools.partial(condition_kernel, holders, groups, capac...  2.43 us
    ppermute x3, waiting for transfers between devices, on_device(): lax.ppermute(terms[j], 'layer', [(g, (g + j) % groups) for g in range(gro...  2.39 us
    pallas_call x1, Pallas kernels, on_device(): pl.pallas_call(functools.partial(score_kernel, holders, capacity), out_sh...  1.85 us
    pallas_call x1, Pallas kernels, on_device(): pl.pallas_call(add_kernel, out_shape=jax.ShapeDtypeStruct((1, share, tota...  0.76 us
  transfers between devices with their start and end apart: 10, of which 7 were waited for; matrix products, arithmetic and copies ran while one was open for 0% of the time, Pallas kernels for 0%

profile of v11, /device:TPU:0, one launch (start us, length us, event | category | flops | bytes accessed | tf_op | source)
XLA Modules:
  0.0 34.0 jit_solution(2317527864300821535)
XLA Ops:
  0.7 2.4 %shard_map.73 = (bf16[8,8320]{1,0:T(8,128)(2,1)S(1)}, bf16[256,8192]{1,0:T(8,128)(2,1)S(1)}, f32[8,256]{1,0:T(8,128)S(1)}) custom-call(s32[1]{0:T(128)S(6)} %copy.8.count_ref, bf16[8,8192]{1,0:T(8,128)(2,1)} %refs_0_.1, f32[2,64,64]{2,1,0:T(8,128)} %refs_1_.1, f32[2,64,64]{2,1,0:T(8,128)} %refs_2_.1, s32[16,128]{1,0:T(8,128)} %bitcast.1, s32[1,256]{1,0:T(1,128)} %refs_4_.1, ...), custom_call_target="tpu_custom_call" | custom-call | tf_op jit(solution)/shard_map/pallas_call | solution.py:235
  3.1 4.0 %collective-permute-start.5 = (bf16[8,8320]{1,0:T(8,128)(2,1)S(1)}, bf16[8,8320]{1,0:T(8,128)(2,1)S(1)}, u32[]{:S(2)}, u32[]{:S(2)}) collective-permute-start(bf16[8,8320]{1,0:T(8,128)(2,1)S(1)} %get-tuple-element.13.refs_0_), channel_id=1, source_target_pairs={{0,24},{4,28},{8,16},{12,20},{16,8},{20,12},{24,0},{28,4},{1,25},{... | collective-permute-start | bytes 399368 | tf_op jit(solution)/shard_map/ppermute | solution.py:216
  7.0 0.5 %collective-permute-start.3 = (bf16[8,8320]{1,0:T(8,128)(2,1)S(1)}, bf16[8,8320]{1,0:T(8,128)(2,1)S(1)}, u32[]{:S(2)}, u32[]{:S(2)}) collective-permute-start(bf16[8,8320]{1,0:T(8,128)(2,1)S(1)} %get-tuple-element.13.refs_0_), channel_id=1, source_target_pairs={{0,16},{4,20},{8,24},{12,28},{16,0},{20,4},{24,8},{28,12},{1,17},{... | collective-permute-start | bytes 399368 | tf_op jit(solution)/shard_map/ppermute | solution.py:216
  7.6 0.1 collective-permute-start.1
  7.7 0.0 collective-permute-start
  7.7 3.3 %collective-permute-done.5.refs_6_ = bf16[8,8320]{1,0:T(8,128)(2,1)S(1)} collective-permute-done((bf16[8,8320]{1,0:T(8,128)(2,1)S(1)}, bf16[8,8320]{1,0:T(8,128)(2,1)S(1)}, u32[]{:S(2)}, u32[]{:S(2)}) %collective-permute-start.5) | collective-permute-done | bytes 133152 | tf_op jit(solution)/shard_map/ppermute | solution.py:216
  11.0 0.0 collective-permute-start.6
  11.0 2.4 %collective-permute-done.3.refs_4_ = bf16[8,8320]{1,0:T(8,128)(2,1)S(1)} collective-permute-done((bf16[8,8320]{1,0:T(8,128)(2,1)S(1)}, bf16[8,8320]{1,0:T(8,128)(2,1)S(1)}, u32[]{:S(2)}, u32[]{:S(2)}) %collective-permute-start.3) | collective-permute-done | bytes 133152 | tf_op jit(solution)/shard_map/ppermute | solution.py:216
  13.4 0.0 collective-permute-start.4
  13.5 0.2 collective-permute-done.1.refs_2_
  13.7 0.3 collective-permute-start.2
  14.0 0.0 collective-permute-done.refs_1_
  14.0 0.0 collective-permute-done.6.refs_7_
  14.0 0.8 %collective-permute-done.4.refs_5_ = bf16[8,8320]{1,0:T(8,128)(2,1)S(1)} collective-permute-done((bf16[8,8320]{1,0:T(8,128)(2,1)S(1)}, bf16[8,8320]{1,0:T(8,128)(2,1)S(1)}, u32[]{:S(2)}, u32[]{:S(2)}) %collective-permute-start.4) | collective-permute-done | bytes 133152 | tf_op jit(solution)/shard_map/ppermute | solution.py:216
  14.8 0.2 collective-permute-done.2.refs_3_
  15.0 1.9 %shard_map.74 = f32[8,16,128]{2,1,0:T(8,128)S(1)} custom-call(bf16[8,8320]{1,0:T(8,128)(2,1)S(1)} %get-tuple-element.13.refs_0_, bf16[8,8320]{1,0:T(8,128)(2,1)S(1)} %collective-permute-done.refs_1_, bf16[8,8320]{1,0:T(8,128)(2,1)S(1)} %collective-permute-done.1.refs_2_, bf16[8,8320]{1,0:T(8,128)(2,1)S(1)} %collective-permute-done.2.refs_3_, ...), custom_call_target="tpu_custom_call" | custom-call | tf_op jit(solution)/shard_map/pallas_call | solution.py:259
  16.9 7.9 %all_to_all.5.landed_ref = f32[8,16,128]{2,1,0:T(8,128)S(1)} all-to-all(f32[8,16,128]{2,1,0:T(8,128)S(1)} %shard_map.74), channel_id=1, replica_groups=mesh['store'=8,'layer'=4] {'store'}, dimensions={0} | all-to-all | bytes 131072 | tf_op jit(solution)/shard_map/all_to_all | solution.py:268
  24.8 0.4 %shard_map.75 = (f32[32,128]{1,0:T(8,128)S(1)}, f32[32,128]{1,0:T(8,128)S(1)}, f32[32,128]{1,0:T(8,128)S(1)}, f32[32,128]{1,0:T(8,128)S(1)}) custom-call(f32[8,256]{1,0:T(8,128)S(1)} %get-tuple-element.12.found_ref, f32[8,16,128]{2,1,0:T(8,128)S(1)} %all_to_all.5.landed_ref), custom_call_target="tpu_custom_call" | custom-call | tf_op jit(solution)/shard_map/pallas_call | solution.py:270
  25.1 1.7 %collective-permute-start.7 = (f32[32,128]{1,0:T(8,128)S(1)}, f32[32,128]{1,0:T(8,128)S(1)}, u32[]{:S(2)}, u32[]{:S(2)}) collective-permute-start(f32[32,128]{1,0:T(8,128)S(1)} %get-tuple-element.16), channel_id=1, source_target_pairs={{0,1},{1,2},{2,3},{3,0},{4,5},{5,6},{6,7},{7,4},{8,9},{9,10},{10,1... | collective-permute-start | bytes 49160 | tf_op jit(solution)/shard_map/ppermute | solution.py:278
  26.9 2.6 %collective-permute-start.8 = (f32[32,128]{1,0:T(8,128)S(1)}, f32[32,128]{1,0:T(8,128)S(1)}, u32[]{:S(2)}, u32[]{:S(2)}) collective-permute-start(f32[32,128]{1,0:T(8,128)S(1)} %get-tuple-element.17), channel_id=1, source_target_pairs={{0,2},{1,3},{2,0},{3,1},{4,6},{5,7},{6,4},{7,5},{8,10},{9,11},{10,... | collective-permute-start | bytes 49160 | tf_op jit(solution)/shard_map/ppermute | solution.py:278
  29.5 1.3 %collective-permute-start.9 = (f32[32,128]{1,0:T(8,128)S(1)}, f32[32,128]{1,0:T(8,128)S(1)}, u32[]{:S(2)}, u32[]{:S(2)}) collective-permute-start(f32[32,128]{1,0:T(8,128)S(1)} %get-tuple-element.18), channel_id=1, source_target_pairs={{0,3},{1,0},{2,1},{3,2},{4,7},{5,4},{6,5},{7,6},{8,11},{9,8},{10,9... | collective-permute-start | bytes 49160 | tf_op jit(solution)/shard_map/ppermute | solution.py:278
  30.8 0.0 collective-permute-done.7.refs_1_
  30.8 0.7 %collective-permute-done.8.refs_2_ = f32[32,128]{1,0:T(8,128)S(1)} collective-permute-done((f32[32,128]{1,0:T(8,128)S(1)}, f32[32,128]{1,0:T(8,128)S(1)}, u32[]{:S(2)}, u32[]{:S(2)}) %collective-permute-start.8) | collective-permute-done | bytes 16416 | tf_op jit(solution)/shard_map/ppermute | solution.py:278
  31.5 1.7 %collective-permute-done.9.refs_3_ = f32[32,128]{1,0:T(8,128)S(1)} collective-permute-done((f32[32,128]{1,0:T(8,128)S(1)}, f32[32,128]{1,0:T(8,128)S(1)}, u32[]{:S(2)}, u32[]{:S(2)}) %collective-permute-start.9) | collective-permute-done | bytes 16416 | tf_op jit(solution)/shard_map/ppermute | solution.py:278
  33.2 0.8 %shard_map.76 = f32[1,64,64]{2,1,0:T(8,128)} custom-call(f32[32,128]{1,0:T(8,128)S(1)} %get-tuple-element.15.refs_0_, f32[32,128]{1,0:T(8,128)S(1)} %collective-permute-done.7.refs_1_, f32[32,128]{1,0:T(8,128)S(1)} %collective-permute-done.8.refs_2_, f32[32,128]{1,0:T(8,128)S(1)} %collective-permute-done.9.refs_3_), custom_call_target="tpu_custom_call" | custom-call | tf_op jit(solution)/shard_map/pallas_call | solution.py:280
Async XLA Ops:
  3.1 7.9 %collective-permute-start.5 = (bf16[8,8320]{1,0:T(8,128)(2,1)S(1)}, bf16[8,8320]{1,0:T(8,128)(2,1)S(1)}, u32[]{:S(2)}, u32[]{:S(2)}) collective-permute-start(bf16[8,8320]{1,0:T(8,128)(2,1)S(1)} %get-tuple-element.13.refs_0_), channel_id=1, source_target_pairs={{0,24},{4,28},{8,16},{12,20},{16,8},{20,12},{24,0},{28,4},{1,25},{... | collective-permute-start | bytes 399368 | tf_op jit(solution)/shard_map/ppermute | solution.py:216
  7.0 6.4 %collective-permute-start.3 = (bf16[8,8320]{1,0:T(8,128)(2,1)S(1)}, bf16[8,8320]{1,0:T(8,128)(2,1)S(1)}, u32[]{:S(2)}, u32[]{:S(2)}) collective-permute-start(bf16[8,8320]{1,0:T(8,128)(2,1)S(1)} %get-tuple-element.13.refs_0_), channel_id=1, source_target_pairs={{0,16},{4,20},{8,24},{12,28},{16,0},{20,4},{24,8},{28,12},{1,17},{... | collective-permute-start | bytes 399368 | tf_op jit(solution)/shard_map/ppermute | solution.py:216
  7.6 6.1 %collective-permute-start.1 = (bf16[8,8320]{1,0:T(8,128)(2,1)S(1)}, bf16[8,8320]{1,0:T(8,128)(2,1)S(1)}, u32[]{:S(2)}, u32[]{:S(2)}) collective-permute-start(bf16[8,8320]{1,0:T(8,128)(2,1)S(1)} %get-tuple-element.13.refs_0_), channel_id=1, source_target_pairs={{0,8},{4,12},{8,0},{12,4},{16,24},{20,28},{24,16},{28,20},{1,9},{5... | collective-permute-start | bytes 399368 | tf_op jit(solution)/shard_map/ppermute | solution.py:216
  7.7 6.3 %collective-permute-start = (bf16[8,8320]{1,0:T(8,128)(2,1)S(1)}, bf16[8,8320]{1,0:T(8,128)(2,1)S(1)}, u32[]{:S(2)}, u32[]{:S(2)}) collective-permute-start(bf16[8,8320]{1,0:T(8,128)(2,1)S(1)} %get-tuple-element.13.refs_0_), channel_id=1, source_target_pairs={{0,4},{4,0},{8,12},{12,8},{16,20},{20,16},{24,28},{28,24},{1,5},{5... | collective-permute-start | bytes 399368 | tf_op jit(solution)/shard_map/ppermute | solution.py:216
  11.0 3.0 %collective-permute-start.6 = (bf16[8,8320]{1,0:T(8,128)(2,1)S(1)}, bf16[8,8320]{1,0:T(8,128)(2,1)S(1)}, u32[]{:S(2)}, u32[]{:S(2)}) collective-permute-start(bf16[8,8320]{1,0:T(8,128)(2,1)S(1)} %collective-permute-done.5.refs_6_), channel_id=1, source_target_pairs={{0,4},{4,0},{8,12},{12,8},{16,20},{20,16},{24,28},{28,24},{1,5},{5... | collective-permute-start | bytes 399368 | tf_op jit(solution)/shard_map/ppermute | solution.py:216
  13.4 1.4 %collective-permute-start.4 = (bf16[8,8320]{1,0:T(8,128)(2,1)S(1)}, bf16[8,8320]{1,0:T(8,128)(2,1)S(1)}, u32[]{:S(2)}, u32[]{:S(2)}) collective-permute-start(bf16[8,8320]{1,0:T(8,128)(2,1)S(1)} %collective-permute-done.3.refs_4_), channel_id=1, source_target_pairs={{0,4},{4,0},{8,12},{12,8},{16,20},{20,16},{24,28},{28,24},{1,5},{5... | collective-permute-start | bytes 399368 | tf_op jit(solution)/shard_map/ppermute | solution.py:216
  13.7 1.4 %collective-permute-start.2 = (bf16[8,8320]{1,0:T(8,128)(2,1)S(1)}, bf16[8,8320]{1,0:T(8,128)(2,1)S(1)}, u32[]{:S(2)}, u32[]{:S(2)}) collective-permute-start(bf16[8,8320]{1,0:T(8,128)(2,1)S(1)} %collective-permute-done.1.refs_2_), channel_id=1, source_target_pairs={{0,4},{4,0},{8,12},{12,8},{16,20},{20,16},{24,28},{28,24},{1,5},{5... | collective-permute-start | bytes 399368 | tf_op jit(solution)/shard_map/ppermute | solution.py:216
  25.1 5.7 %collective-permute-start.7 = (f32[32,128]{1,0:T(8,128)S(1)}, f32[32,128]{1,0:T(8,128)S(1)}, u32[]{:S(2)}, u32[]{:S(2)}) collective-permute-start(f32[32,128]{1,0:T(8,128)S(1)} %get-tuple-element.16), channel_id=1, source_target_pairs={{0,1},{1,2},{2,3},{3,0},{4,5},{5,6},{6,7},{7,4},{8,9},{9,10},{10,1... | collective-permute-start | bytes 49160 | tf_op jit(solution)/shard_map/ppermute | solution.py:278
  26.9 4.6 %collective-permute-start.8 = (f32[32,128]{1,0:T(8,128)S(1)}, f32[32,128]{1,0:T(8,128)S(1)}, u32[]{:S(2)}, u32[]{:S(2)}) collective-permute-start(f32[32,128]{1,0:T(8,128)S(1)} %get-tuple-element.17), channel_id=1, source_target_pairs={{0,2},{1,3},{2,0},{3,1},{4,6},{5,7},{6,4},{7,5},{8,10},{9,11},{10,... | collective-permute-start | bytes 49160 | tf_op jit(solution)/shard_map/ppermute | solution.py:278
  29.5 3.7 %collective-permute-start.9 = (f32[32,128]{1,0:T(8,128)S(1)}, f32[32,128]{1,0:T(8,128)S(1)}, u32[]{:S(2)}, u32[]{:S(2)}) collective-permute-start(f32[32,128]{1,0:T(8,128)S(1)} %get-tuple-element.18), channel_id=1, source_target_pairs={{0,3},{1,0},{2,1},{3,2},{4,7},{5,4},{6,5},{7,6},{8,11},{9,8},{10,9... | collective-permute-start | bytes 49160 | tf_op jit(solution)/shard_map/ppermute | solution.py:278

commit v12 on v11

--- a/solution.py
+++ b/solution.py
@@ -31,19 +31,17 @@
     return value.astype(jnp.float32).astype(jnp.bfloat16)
 
 
-def condition_kernel(holders, groups, capacity, count_ref, *refs):
-    sources, packed_ref, pages_ref, found_ref, landing, arrived = refs[:6], refs[6], refs[7], refs[8], refs[9:14], refs[14]
-    turned_ref = refs[15]
+def condition_kernel(holders, groups, capacity, per_holder, count_ref, *refs):
+    sources, packed_ref, again_ref, found_ref, landing, arrived, turned_ref = refs[:5], *refs[5:8], refs[8:13], *refs[13:]
     copies = [
         pltpu.make_async_copy(source, target, arrived.at[i])
-        for i, (source, target) in enumerate(zip(sources, landing + (pages_ref,)))
+        for i, (source, target) in enumerate(zip(sources, landing))
     ]
     for copy in copies:
         copy.start()
-    for copy in copies[:-1]:
+    for copy in copies:
         copy.wait()
     query_ref, in_factor_ref, out_factor_ref, home_ref, cand_ref = landing
-    per_holder = pages_ref.shape[0]
     rows, width = query_ref.shape
     layers, rank, _ = in_factor_ref.shape
     half = rank // 2
@@ -136,28 +134,32 @@
     if spare:
         blocks.append(jnp.zeros((rows, spare), jnp.float32))
     packed_ref[:, width:] = jnp.concatenate(blocks, axis=1).astype(jnp.bfloat16)
+    again_ref[...] = packed_ref[...]
     found_ref[...] = jnp.concatenate([holder, rank_there, jnp.zeros((6, slots), jnp.float32)], axis=0)
-    copies[-1].wait()
+
+
+def load_kernel(block_ref, source_ref, same_block_ref, target_ref, arrived):
+    copy = pltpu.make_async_copy(source_ref, target_ref, arrived)
+    copy.start()
+    copy.wait()
 
 
 def score_kernel(holders, capacity, *refs):
-    packed_refs, pages_ref, out_ref, total, queries = refs[:holders], *refs[holders:]
+    packed_refs, pages_ref, out_ref, queries = refs[:holders], *refs[holders:]
     me = lax.axis_index("store")
     count, width = pages_ref.shape
     rows = packed_refs[0].shape[0]
+    total = holders * rows
     half = capacity // 2
     step = width // CHUNKS
-    scores = jnp.zeros((holders * rows, count), jnp.float32)
+    scores = jnp.zeros((count, total), jnp.float32)
     for i in range(CHUNKS):
         columns = slice(i * step, (i + 1) * step)
         for k in range(holders):
             queries[k * rows:(k + 1) * rows, columns] = packed_refs[k][:, columns]
         scores = scores + lax.dot_general(
-            queries[:, columns], pages_ref[:, columns], (((1,), (1,)), ((), ())), preferred_element_type=jnp.float32
-        )
-    for k in range(holders):
-        start = pl.multiple_of((me ^ k) * rows, rows)
-        total[pl.ds(start, rows), :] = scores[k * rows:(k + 1) * rows]
+            pages_ref[:, columns], queries[:, columns], (((1,), (1,)), ((), ())), preferred_element_type=jnp.float32
+        )
     asked = []
     for k in range(holders):
         notes = packed_refs[k][:, width:].astype(jnp.float32)
@@ -166,17 +168,18 @@
         for block in range(1, holders // rows):
             mine = jnp.where(me // rows == block, notes[:, block * capacity:(block + 1) * capacity], mine)
         asked.append(mine)
-    page = iota((count, holders * half), 0).astype(jnp.float32) + 1.0
-    picked = jnp.zeros((holders * half, 2 * holders * rows), jnp.float32)
-    parts = parts_of(total[...])[::-1]
-    nothing = jnp.zeros_like(parts[0])
+    page = iota((holders * half, count), 1).astype(jnp.float32) + 1.0
+    came, goes = iota((total, 2 * total), 0), iota((total, 2 * total), 1)
+    own_place = (me ^ (came // rows)) * rows + came % rows
+    picked = jnp.zeros((holders * half, 2 * total), jnp.float32)
+    parts = parts_of(scores)[::-1]
     for side in range(2):
-        chosen = exact_bf16(page == jnp.concatenate([row[:, side * half:(side + 1) * half] for row in asked], axis=1))
+        row = jnp.concatenate([row[:, side * half:(side + 1) * half] for row in asked], axis=1)
+        chosen = exact_bf16(page == jnp.broadcast_to(row, (8, holders * half)).T[:, :1])
+        placing = exact_bf16(goes == own_place + side * total)
         for part in parts:
-            wide = jnp.concatenate([nothing, part] if side else [part, nothing], axis=0)
-            picked = picked + lax.dot_general(
-                chosen, wide, (((0,), (1,)), ((), ())), preferred_element_type=jnp.float32
-            )
+            placed = jnp.dot(part, placing, preferred_element_type=jnp.float32).astype(jnp.bfloat16)
+            picked = picked + jnp.dot(chosen, placed, preferred_element_type=jnp.float32)
     for k in range(holders):
         out_ref[me ^ k] = picked[k * half:(k + 1) * half]
 
@@ -229,26 +232,37 @@
     home = page_home.reshape(-1, LANES)
     sources = [
         pltpu.with_memory_space_constraint(source, pltpu.HBM)
-        for source in (query_grads, factor_in, factor_out, home, cand_lists, page_store)
+        for source in (query_grads, factor_in, factor_out, home, cand_lists)
     ]
     notes = max(LANES, holders // rows * capacity)
-    packed, pages, found = pl.pallas_call(
-        functools.partial(condition_kernel, holders, groups, capacity),
+    packed, again, found = pl.pallas_call(
+        functools.partial(condition_kernel, holders, groups, capacity, per_holder),
         out_shape=[
             jax.ShapeDtypeStruct((rows, width + notes), bf16),
-            pltpu.VMEM(page_store.shape, bf16),
+            jax.ShapeDtypeStruct((rows, width + notes), bf16),
             jax.ShapeDtypeStruct((8, slots), jnp.float32),
         ],
         in_specs=[SMEM] + [HBM] * len(sources),
         out_specs=[VMEM] * 3,
-        scratch_shapes=[pltpu.VMEM(source.shape, source.dtype) for source in sources[:-1]]
+        scratch_shapes=[pltpu.VMEM(source.shape, source.dtype) for source in sources]
         + [pltpu.SemaphoreType.DMA((len(sources),)), pltpu.VMEM((layers, rows * rank // 2, LANES), jnp.float32)],
         compiler_params=pltpu.CompilerParams(vmem_limit_bytes=10 * 2**20 + 24 * slots * slots),
     )(counts, *sources)
 
+    again, pages = pl.pallas_call(
+        load_kernel,
+        out_shape=[jax.ShapeDtypeStruct(again.shape, bf16), pltpu.VMEM(page_store.shape, bf16)],
+        in_specs=[VMEM, HBM],
+        out_specs=[VMEM] * 2,
+        input_output_aliases={0: 0},
+        scratch_shapes=[pltpu.SemaphoreType.DMA(())],
+        compiler_params=pltpu.CompilerParams(vmem_limit_bytes=2 * 2**20),
+        cost_estimate=pl.CostEstimate(flops=0, bytes_accessed=2 * page_store.size, transcendentals=0),
+    )(again, pltpu.with_memory_space_constraint(page_store, pltpu.HBM))
+
     blocks = [None] * holders
     blocks[0] = packed
-    blocks[1] = swap(packed, "store", 1)
+    blocks[1] = swap(again, "store", 1)
     for k in range(2, holders, 2):
         blocks[k] = swap(packed, "store", k)
     for k in range(2, holders, 2):
@@ -261,7 +275,7 @@
         out_shape=jax.ShapeDtypeStruct((holders, capacity // 2, 2 * total), jnp.float32),
         in_specs=[VMEM] * (holders + 1),
         out_specs=VMEM,
-        scratch_shapes=[pltpu.VMEM((total, per_holder), jnp.float32), pltpu.VMEM((total, width), bf16)],
+        scratch_shapes=[pltpu.VMEM((total, width), bf16)],
         compiler_params=pltpu.CompilerParams(vmem_limit_bytes=8 * 2**20 + 2 * bytes_in + 48 * total * slots),
     )(*blocks, pltpu.with_memory_space_constraint(pages, pltpu.VMEM))
 

time: 34.2 us -> 34.7 us (1.015)
  Pallas kernels: 5.41 us -> 8.06 us
  waiting for transfers between devices: 9.45 us -> 7.07 us
  starting transfers between devices: 10.6 us -> 11.1 us
    ppermute x7, waiting for transfers between devices: 7.06 us -> 4.68 us  [swap(): lax.ppermute(value, axis, [(i, i ^ distance) for i in range(lax.axis_size...]
    pallas_call x0 -> x1, Pallas kernels: none -> 2.2 us  [on_device(): pl.pallas_call(load_kernel, out_shape=[jax.ShapeDtypeStruct(again.shape,...]
    pallas_call x1, Pallas kernels: 1.85 us -> 2.54 us  [on_device(): pl.pallas_call(functools.partial(score_kernel, holders, capacity), out_sh...]
    ppermute x7, starting transfers between devices: 4.88 us -> 5.5 us  [swap(): lax.ppermute(value, axis, [(i, i ^ distance) for i in range(lax.axis_size...]
  transfers between devices with their start and end apart: 10 -> 10, of which waited for: 7 -> 7; matrix products, arithmetic and copies ran while one was open for 0% -> 0% of each run, Pallas kernels for 0% -> 6%
where the time goes in v12:
time: 34.7 us; the launch traced here: 34.5 us
  starting transfers between devices  11.1 us (32%)
  Pallas kernels  8.06 us (23%)
  blocking collectives  7.61 us (22%)
  waiting for transfers between devices  7.07 us (20%)
  between operations  0.7 us (2%)
    all_to_all x1, blocking collectives, on_device(): lax.all_to_all(asked, 'store', split_axis=0, concat_axis=0, tiled=True)  7.61 us
    ppermute x3, starting transfers between devices, on_device(): lax.ppermute(terms[j], 'layer', [(g, (g + j) % groups) for g in range(gro...  5.57 us
    ppermute x7, starting transfers between devices, swap(): lax.ppermute(value, axis, [(i, i ^ distance) for i in range(lax.axis_size...  5.5 us
    ppermute x7, waiting for transfers between devices, swap(): lax.ppermute(value, axis, [(i, i ^ distance) for i in range(lax.axis_size...  4.68 us
    pallas_call x1, Pallas kernels, on_device(): pl.pallas_call(functools.partial(score_kernel, holders, capacity), out_sh...  2.54 us
    ppermute x3, waiting for transfers between devices, on_device(): lax.ppermute(terms[j], 'layer', [(g, (g + j) % groups) for g in range(gro...  2.39 us
    pallas_call x1, Pallas kernels, on_device(): pl.pallas_call(load_kernel, out_shape=[jax.ShapeDtypeStruct(again.shape,...  2.2 us
    pallas_call x1, Pallas kernels, on_device(): pl.pallas_call(functools.partial(condition_kernel, holders, groups, capac...  2.19 us
  transfers between devices with their start and end apart: 10, of which 7 were waited for; matrix products, arithmetic and copies ran while one was open for 0% of the time, Pallas kernels for 6%

profile of v12, /device:TPU:0, one launch (start us, length us, event | category | flops | bytes accessed | tf_op | source)
XLA Modules:
  0.0 34.5 jit_solution(14240039962722773961)
XLA Ops:
  0.7 2.2 %shard_map.73 = (bf16[8,8320]{1,0:T(8,128)(2,1)S(1)}, bf16[8,8320]{1,0:T(8,128)(2,1)S(1)}, f32[8,256]{1,0:T(8,128)S(1)}) custom-call(s32[1]{0:T(128)S(6)} %copy.10.count_ref, bf16[8,8192]{1,0:T(8,128)(2,1)} %refs_0_.1, f32[2,64,64]{2,1,0:T(8,128)} %refs_1_.1, f32[2,64,64]{2,1,0:T(8,128)} %refs_2_.1, s32[16,128]{1,0:T(8,128)} %bitcast.1, s32[1,256]{1,0:T(1,128)} %refs_4_.1), custom_call_target="tpu_custom_call" | custom-call | tf_op jit(solution)/shard_map/pallas_call | solution.py:238
  2.9 3.0 %collective-permute-start.1 = (bf16[8,8320]{1,0:T(8,128)(2,1)S(1)}, bf16[8,8320]{1,0:T(8,128)(2,1)S(1)}, u32[]{:S(2)}, u32[]{:S(2)}) collective-permute-start(bf16[8,8320]{1,0:T(8,128)(2,1)S(1)} %get-tuple-element.15.refs_0_), channel_id=1, source_target_pairs={{0,8},{4,12},{8,0},{12,4},{16,24},{20,28},{24,16},{28,20},{1,9},{5... | collective-permute-start | bytes 399368 | tf_op jit(solution)/shard_map/ppermute | solution.py:219
  5.9 1.5 %collective-permute-start.3 = (bf16[8,8320]{1,0:T(8,128)(2,1)S(1)}, bf16[8,8320]{1,0:T(8,128)(2,1)S(1)}, u32[]{:S(2)}, u32[]{:S(2)}) collective-permute-start(bf16[8,8320]{1,0:T(8,128)(2,1)S(1)} %get-tuple-element.15.refs_0_), channel_id=1, source_target_pairs={{0,16},{4,20},{8,24},{12,28},{16,0},{20,4},{24,8},{28,12},{1,17},{... | collective-permute-start | bytes 399368 | tf_op jit(solution)/shard_map/ppermute | solution.py:219
  7.4 0.0 collective-permute-start.5
  7.4 2.2 %shard_map.74 = (bf16[8,8320]{1,0:T(8,128)(2,1)S(1)}, bf16[256,8192]{1,0:T(8,128)(2,1)S(1)}) custom-call(bf16[8,8320]{1,0:T(8,128)(2,1)S(1)} %get-tuple-element.16.block_ref, bf16[256,8192]{1,0:T(8,128)(2,1)} %source_ref.1), custom_call_target="tpu_custom_call", output_to_operand_aliasing={{0}: (0, {})} | custom-call | bytes 4194304 | tf_op jit(solution)/shard_map/pallas_call | solution.py:252
  9.6 0.1 collective-permute-start
  9.7 0.1 collective-permute-done.1.refs_2_
  9.8 0.4 %collective-permute-start.2 = (bf16[8,8320]{1,0:T(8,128)(2,1)S(1)}, bf16[8,8320]{1,0:T(8,128)(2,1)S(1)}, u32[]{:S(2)}, u32[]{:S(2)}) collective-permute-start(bf16[8,8320]{1,0:T(8,128)(2,1)S(1)} %collective-permute-done.1.refs_2_), channel_id=1, source_target_pairs={{0,4},{4,0},{8,12},{12,8},{16,20},{20,16},{24,28},{28,24},{1,5},{5... | collective-permute-start | bytes 399368 | tf_op jit(solution)/shard_map/ppermute | solution.py:219
  10.2 3.5 %collective-permute-done.3.refs_4_ = bf16[8,8320]{1,0:T(8,128)(2,1)S(1)} collective-permute-done((bf16[8,8320]{1,0:T(8,128)(2,1)S(1)}, bf16[8,8320]{1,0:T(8,128)(2,1)S(1)}, u32[]{:S(2)}, u32[]{:S(2)}) %collective-permute-start.3) | collective-permute-done | bytes 133152 | tf_op jit(solution)/shard_map/ppermute | solution.py:219
  13.7 0.0 collective-permute-start.4
  13.7 0.0 collective-permute-done.5.refs_6_
  13.7 0.5 %collective-permute-start.6 = (bf16[8,8320]{1,0:T(8,128)(2,1)S(1)}, bf16[8,8320]{1,0:T(8,128)(2,1)S(1)}, u32[]{:S(2)}, u32[]{:S(2)}) collective-permute-start(bf16[8,8320]{1,0:T(8,128)(2,1)S(1)} %collective-permute-done.5.refs_6_), channel_id=1, source_target_pairs={{0,4},{4,0},{8,12},{12,8},{16,20},{20,16},{24,28},{28,24},{1,5},{5... | collective-permute-start | bytes 399368 | tf_op jit(solution)/shard_map/ppermute | solution.py:219
  14.2 0.0 collective-permute-done.refs_1_
  14.2 0.0 collective-permute-done.2.refs_3_
  14.2 0.8 %collective-permute-done.4.refs_5_ = bf16[8,8320]{1,0:T(8,128)(2,1)S(1)} collective-permute-done((bf16[8,8320]{1,0:T(8,128)(2,1)S(1)}, bf16[8,8320]{1,0:T(8,128)(2,1)S(1)}, u32[]{:S(2)}, u32[]{:S(2)}) %collective-permute-start.4) | collective-permute-done | bytes 133152 | tf_op jit(solution)/shard_map/ppermute | solution.py:219
  15.1 0.2 collective-permute-done.6.refs_7_
  15.3 2.5 %shard_map.75 = f32[8,16,128]{2,1,0:T(8,128)S(1)} custom-call(bf16[8,8320]{1,0:T(8,128)(2,1)S(1)} %get-tuple-element.15.refs_0_, bf16[8,8320]{1,0:T(8,128)(2,1)S(1)} %collective-permute-done.refs_1_, bf16[8,8320]{1,0:T(8,128)(2,1)S(1)} %collective-permute-done.1.refs_2_, bf16[8,8320]{1,0:T(8,128)(2,1)S(1)} %collective-permute-done.2.refs_3_, ...), custom_call_target="tpu_custom_call" | custom-call | tf_op jit(solution)/shard_map/pallas_call | solution.py:273
  17.8 7.6 %all_to_all.5.landed_ref = f32[8,16,128]{2,1,0:T(8,128)S(1)} all-to-all(f32[8,16,128]{2,1,0:T(8,128)S(1)} %shard_map.75), channel_id=1, replica_groups=mesh['store'=8,'layer'=4] {'store'}, dimensions={0} | all-to-all | bytes 131072 | tf_op jit(solution)/shard_map/all_to_all | solution.py:282
  25.4 0.4 %shard_map.76 = (f32[32,128]{1,0:T(8,128)S(1)}, f32[32,128]{1,0:T(8,128)S(1)}, f32[32,128]{1,0:T(8,128)S(1)}, f32[32,128]{1,0:T(8,128)S(1)}) custom-call(f32[8,256]{1,0:T(8,128)S(1)} %get-tuple-element.14.found_ref, f32[8,16,128]{2,1,0:T(8,128)S(1)} %all_to_all.5.landed_ref), custom_call_target="tpu_custom_call" | custom-call | tf_op jit(solution)/shard_map/pallas_call | solution.py:284
  25.8 1.6 %collective-permute-start.7 = (f32[32,128]{1,0:T(8,128)S(1)}, f32[32,128]{1,0:T(8,128)S(1)}, u32[]{:S(2)}, u32[]{:S(2)}) collective-permute-start(f32[32,128]{1,0:T(8,128)S(1)} %get-tuple-element.20), channel_id=1, source_target_pairs={{0,1},{1,2},{2,3},{3,0},{4,5},{5,6},{6,7},{7,4},{8,9},{9,10},{10,1... | collective-permute-start | bytes 49160 | tf_op jit(solution)/shard_map/ppermute | solution.py:292
  27.4 2.6 %collective-permute-start.8 = (f32[32,128]{1,0:T(8,128)S(1)}, f32[32,128]{1,0:T(8,128)S(1)}, u32[]{:S(2)}, u32[]{:S(2)}) collective-permute-start(f32[32,128]{1,0:T(8,128)S(1)} %get-tuple-element.21), channel_id=1, source_target_pairs={{0,2},{1,3},{2,0},{3,1},{4,6},{5,7},{6,4},{7,5},{8,10},{9,11},{10,... | collective-permute-start | bytes 49160 | tf_op jit(solution)/shard_map/ppermute | solution.py:292
  30.0 1.3 %collective-permute-start.9 = (f32[32,128]{1,0:T(8,128)S(1)}, f32[32,128]{1,0:T(8,128)S(1)}, u32[]{:S(2)}, u32[]{:S(2)}) collective-permute-start(f32[32,128]{1,0:T(8,128)S(1)} %get-tuple-element.22), channel_id=1, source_target_pairs={{0,3},{1,0},{2,1},{3,2},{4,7},{5,4},{6,5},{7,6},{8,11},{9,8},{10,9... | collective-permute-start | bytes 49160 | tf_op jit(solution)/shard_map/ppermute | solution.py:292
  31.4 0.1 collective-permute-done.7.refs_1_
  31.5 0.6 %collective-permute-done.8.refs_2_ = f32[32,128]{1,0:T(8,128)S(1)} collective-permute-done((f32[32,128]{1,0:T(8,128)S(1)}, f32[32,128]{1,0:T(8,128)S(1)}, u32[]{:S(2)}, u32[]{:S(2)}) %collective-permute-start.8) | collective-permute-done | bytes 16416 | tf_op jit(solution)/shard_map/ppermute | solution.py:292
  32.1 1.7 %collective-permute-done.9.refs_3_ = f32[32,128]{1,0:T(8,128)S(1)} collective-permute-done((f32[32,128]{1,0:T(8,128)S(1)}, f32[32,128]{1,0:T(8,128)S(1)}, u32[]{:S(2)}, u32[]{:S(2)}) %collective-permute-start.9) | collective-permute-done | bytes 16416 | tf_op jit(solution)/shard_map/ppermute | solution.py:292
  33.7 0.8 %shard_map.77 = f32[1,64,64]{2,1,0:T(8,128)} custom-call(f32[32,128]{1,0:T(8,128)S(1)} %get-tuple-element.19.refs_0_, f32[32,128]{1,0:T(8,128)S(1)} %collective-permute-done.7.refs_1_, f32[32,128]{1,0:T(8,128)S(1)} %collective-permute-done.8.refs_2_, f32[32,128]{1,0:T(8,128)S(1)} %collective-permute-done.9.refs_3_), custom_call_target="tpu_custom_call" | custom-call | tf_op jit(solution)/shard_map/pallas_call | solution.py:294
Async XLA Ops:
  2.9 7.0 %collective-permute-start.1 = (bf16[8,8320]{1,0:T(8,128)(2,1)S(1)}, bf16[8,8320]{1,0:T(8,128)(2,1)S(1)}, u32[]{:S(2)}, u32[]{:S(2)}) collective-permute-start(bf16[8,8320]{1,0:T(8,128)(2,1)S(1)} %get-tuple-element.15.refs_0_), channel_id=1, source_target_pairs={{0,8},{4,12},{8,0},{12,4},{16,24},{20,28},{24,16},{28,20},{1,9},{5... | collective-permute-start | bytes 399368 | tf_op jit(solution)/shard_map/ppermute | solution.py:219
  5.9 7.9 %collective-permute-start.3 = (bf16[8,8320]{1,0:T(8,128)(2,1)S(1)}, bf16[8,8320]{1,0:T(8,128)(2,1)S(1)}, u32[]{:S(2)}, u32[]{:S(2)}) collective-permute-start(bf16[8,8320]{1,0:T(8,128)(2,1)S(1)} %get-tuple-element.15.refs_0_), channel_id=1, source_target_pairs={{0,16},{4,20},{8,24},{12,28},{16,0},{20,4},{24,8},{28,12},{1,17},{... | collective-permute-start | bytes 399368 | tf_op jit(solution)/shard_map/ppermute | solution.py:219
  7.4 6.3 %collective-permute-start.5 = (bf16[8,8320]{1,0:T(8,128)(2,1)S(1)}, bf16[8,8320]{1,0:T(8,128)(2,1)S(1)}, u32[]{:S(2)}, u32[]{:S(2)}) collective-permute-start(bf16[8,8320]{1,0:T(8,128)(2,1)S(1)} %get-tuple-element.15.refs_0_), channel_id=1, source_target_pairs={{0,24},{4,28},{8,16},{12,20},{16,8},{20,12},{24,0},{28,4},{1,25},{... | collective-permute-start | bytes 399368 | tf_op jit(solution)/shard_map/ppermute | solution.py:219
  9.6 4.6 %collective-permute-start = (bf16[8,8320]{1,0:T(8,128)(2,1)S(1)}, bf16[8,8320]{1,0:T(8,128)(2,1)S(1)}, u32[]{:S(2)}, u32[]{:S(2)}) collective-permute-start(bf16[8,8320]{1,0:T(8,128)(2,1)S(1)} %get-tuple-element.17), channel_id=1, source_target_pairs={{0,4},{4,0},{8,12},{12,8},{16,20},{20,16},{24,28},{28,24},{1,5},{5... | collective-permute-start | bytes 399368 | tf_op jit(solution)/shard_map/ppermute | solution.py:219
  9.8 4.4 %collective-permute-start.2 = (bf16[8,8320]{1,0:T(8,128)(2,1)S(1)}, bf16[8,8320]{1,0:T(8,128)(2,1)S(1)}, u32[]{:S(2)}, u32[]{:S(2)}) collective-permute-start(bf16[8,8320]{1,0:T(8,128)(2,1)S(1)} %collective-permute-done.1.refs_2_), channel_id=1, source_target_pairs={{0,4},{4,0},{8,12},{12,8},{16,20},{20,16},{24,28},{28,24},{1,5},{5... | collective-permute-start | bytes 399368 | tf_op jit(solution)/shard_map/ppermute | solution.py:219
  13.7 1.4 %collective-permute-start.4 = (bf16[8,8320]{1,0:T(8,128)(2,1)S(1)}, bf16[8,8320]{1,0:T(8,128)(2,1)S(1)}, u32[]{:S(2)}, u32[]{:S(2)}) collective-permute-start(bf16[8,8320]{1,0:T(8,128)(2,1)S(1)} %collective-permute-done.3.refs_4_), channel_id=1, source_target_pairs={{0,4},{4,0},{8,12},{12,8},{16,20},{20,16},{24,28},{28,24},{1,5},{5... | collective-permute-start | bytes 399368 | tf_op jit(solution)/shard_map/ppermute | solution.py:219
  13.7 1.5 %collective-permute-start.6 = (bf16[8,8320]{1,0:T(8,128)(2,1)S(1)}, bf16[8,8320]{1,0:T(8,128)(2,1)S(1)}, u32[]{:S(2)}, u32[]{:S(2)}) collective-permute-start(bf16[8,8320]{1,0:T(8,128)(2,1)S(1)} %collective-permute-done.5.refs_6_), channel_id=1, source_target_pairs={{0,4},{4,0},{8,12},{12,8},{16,20},{20,16},{24,28},{28,24},{1,5},{5... | collective-permute-start | bytes 399368 | tf_op jit(solution)/shard_map/ppermute | solution.py:219
  25.8 5.7 %collective-permute-start.7 = (f32[32,128]{1,0:T(8,128)S(1)}, f32[32,128]{1,0:T(8,128)S(1)}, u32[]{:S(2)}, u32[]{:S(2)}) collective-permute-start(f32[32,128]{1,0:T(8,128)S(1)} %get-tuple-element.20), channel_id=1, source_target_pairs={{0,1},{1,2},{2,3},{3,0},{4,5},{5,6},{6,7},{7,4},{8,9},{9,10},{10,1... | collective-permute-start | bytes 49160 | tf_op jit(solution)/shard_map/ppermute | solution.py:292
  27.4 4.6 %collective-permute-start.8 = (f32[32,128]{1,0:T(8,128)S(1)}, f32[32,128]{1,0:T(8,128)S(1)}, u32[]{:S(2)}, u32[]{:S(2)}) collective-permute-start(f32[32,128]{1,0:T(8,128)S(1)} %get-tuple-element.21), channel_id=1, source_target_pairs={{0,2},{1,3},{2,0},{3,1},{4,6},{5,7},{6,4},{7,5},{8,10},{9,11},{10,... | collective-permute-start | bytes 49160 | tf_op jit(solution)/shard_map/ppermute | solution.py:292
  30.0 3.7 %collective-permute-start.9 = (f32[32,128]{1,0:T(8,128)S(1)}, f32[32,128]{1,0:T(8,128)S(1)}, u32[]{:S(2)}, u32[]{:S(2)}) collective-permute-start(f32[32,128]{1,0:T(8,128)S(1)} %get-tuple-element.22), channel_id=1, source_target_pairs={{0,3},{1,0},{2,1},{3,2},{4,7},{5,4},{6,5},{7,6},{8,11},{9,8},{10,9... | collective-permute-start | bytes 49160 | tf_op jit(solution)/shard_map/ppermute | solution.py:292

commit v13 on v11

--- a/solution.py
+++ b/solution.py
@@ -16,6 +16,16 @@
 
 def iota(shape, dimension):
     return lax.broadcasted_iota(jnp.int32, shape, dimension)
+
+
+def layer_plan(groups):
+    if groups == 4:
+        return [[1, 2, 0, 3], [2, 0, 1, 3], [3, 1, 2, 0], [0, 3, 2, 1], [0, 1, 3, 2]]
+    return [[(g + step) % groups for g in range(groups)] for step in range(1, groups)]
+
+
+def entry(values, index):
+    return sum(jnp.where(index == i, value, 0) for i, value in enumerate(values))
 
 
 def parts_of(value):
@@ -31,7 +41,7 @@
     return value.astype(jnp.float32).astype(jnp.bfloat16)
 
 
-def condition_kernel(holders, groups, capacity, count_ref, *refs):
+def condition_kernel(holders, capacity, count_ref, *refs):
     sources, packed_ref, pages_ref, found_ref, landing, arrived = refs[:6], refs[6], refs[7], refs[8], refs[9:14], refs[14]
     turned_ref = refs[15]
     copies = [
@@ -102,17 +112,7 @@
 
     slots = cand_ref.shape[1]
     home_rows = home_ref.shape[0]
-    share = slots // groups
-    at = lax.axis_index("layer")
     wanted = jnp.where(iota((1, slots), 1) < count_ref[0], cand_ref[...], -1)
-    ranges = [wanted[:, g * share:(g + 1) * share] for g in range(groups)]
-    ordered = []
-    for j in range(groups):
-        chosen = ranges[0]
-        for g in range(1, groups):
-            chosen = jnp.where((at + j) % groups == g, ranges[g], chosen)
-        ordered.append(chosen)
-    wanted = jnp.concatenate(ordered, axis=1)
     known = jnp.maximum(wanted, 0)
     onehot = (iota((LANES, slots), 0) == known % LANES).astype(jnp.float32).astype(jnp.bfloat16)
     home = home_ref[...]
@@ -167,25 +167,23 @@
             mine = jnp.where(me // rows == block, notes[:, block * capacity:(block + 1) * capacity], mine)
         asked.append(mine)
     page = iota((count, holders * half), 0).astype(jnp.float32) + 1.0
-    picked = jnp.zeros((holders * half, 2 * holders * rows), jnp.float32)
     parts = parts_of(total[...])[::-1]
-    nothing = jnp.zeros_like(parts[0])
+    picked = []
     for side in range(2):
-        chosen = exact_bf16(page == jnp.concatenate([row[:, side * half:(side + 1) * half] for row in asked], axis=1))
-        for part in parts:
-            wide = jnp.concatenate([nothing, part] if side else [part, nothing], axis=0)
-            picked = picked + lax.dot_general(
-                chosen, wide, (((0,), (1,)), ((), ())), preferred_element_type=jnp.float32
-            )
+        row = jnp.concatenate([row[:, side * half:(side + 1) * half] for row in asked], axis=1)
+        chosen = exact_bf16(page == row)
+        picked.append(sum(jnp.dot(part, chosen, preferred_element_type=jnp.float32) for part in parts))
+    picked = jnp.concatenate(picked, axis=0).T
     for k in range(holders):
         out_ref[me ^ k] = picked[k * half:(k + 1) * half]
 
 
-def spread_kernel(holders, found_ref, landed_ref, *out_refs):
+def spread_kernel(holders, groups, found_ref, landed_ref, *out_refs):
     half = landed_ref.shape[1]
     slots = found_ref.shape[1]
     total = landed_ref.shape[2] // 2
-    groups = len(out_refs)
+    plan = layer_plan(groups)
+    at = lax.axis_index("layer")
     share = slots // groups
     holder, rank_there = found_ref[0:1], found_ref[1:2]
     place = iota((holders * half, slots), 0).astype(jnp.float32)
@@ -198,16 +196,23 @@
         for part in parts:
             spread = lax.dot_general(part, chosen, (((0,), (0,)), ((), ())), preferred_element_type=jnp.float32)
             result = result + spread[side * total:(side + 1) * total]
+    blocks = []
     for g in range(groups):
         block = result[:, g * share:(g + 1) * share]
-        out_refs[g][...] = jnp.concatenate([block[:total // 2], block[total // 2:]], axis=1)
-
-
-def add_kernel(*refs):
+        blocks.append(jnp.concatenate([block[:total // 2], block[total // 2:]], axis=1))
+    for out_ref, targets in zip(out_refs, [list(range(groups))] + plan):
+        chosen = blocks[0]
+        for g in range(1, groups):
+            chosen = jnp.where(entry(targets, at) == g, blocks[g], chosen)
+        out_ref[...] = chosen
+
+
+def add_kernel(groups, *refs):
+    at = lax.axis_index("layer")
     out_ref = refs[-1]
     total = refs[0][...]
-    for ref in refs[1:-1]:
-        total = total + ref[...]
+    for ref, targets in zip(refs[1:], layer_plan(groups)):
+        total = total + jnp.where(entry(targets, at) == at, 0.0, ref[...])
     share = total.shape[1] // 2
     out_ref[0] = jnp.concatenate([total[:, :share], total[:, share:]], axis=0).T
 
@@ -233,7 +238,7 @@
     ]
     notes = max(LANES, holders // rows * capacity)
     packed, pages, found = pl.pallas_call(
-        functools.partial(condition_kernel, holders, groups, capacity),
+        functools.partial(condition_kernel, holders, capacity),
         out_shape=[
             jax.ShapeDtypeStruct((rows, width + notes), bf16),
             pltpu.VMEM(page_store.shape, bf16),
@@ -267,20 +272,21 @@
 
     landed = lax.all_to_all(asked, "store", split_axis=0, concat_axis=0, tiled=True)
     share = slots // groups
+    plan = layer_plan(groups)
     terms = pl.pallas_call(
-        functools.partial(spread_kernel, holders),
-        out_shape=[jax.ShapeDtypeStruct((total // 2, 2 * share), jnp.float32)] * groups,
+        functools.partial(spread_kernel, holders, groups),
+        out_shape=[jax.ShapeDtypeStruct((total // 2, 2 * share), jnp.float32)] * (1 + len(plan)),
         in_specs=[VMEM] * 2,
-        out_specs=[VMEM] * groups,
+        out_specs=[VMEM] * (1 + len(plan)),
         compiler_params=pltpu.CompilerParams(vmem_limit_bytes=4 * 2**20 + 64 * total * slots),
     )(found, landed)
     terms = [terms[0]] + [
-        lax.ppermute(terms[j], "layer", [(g, (g + j) % groups) for g in range(groups)]) for j in range(1, groups)
+        lax.ppermute(term, "layer", list(enumerate(targets))) for term, targets in zip(terms[1:], plan)
     ]
     return pl.pallas_call(
-        add_kernel,
+        functools.partial(add_kernel, groups),
         out_shape=jax.ShapeDtypeStruct((1, share, total), jnp.float32),
-        in_specs=[VMEM] * groups,
+        in_specs=[VMEM] * len(terms),
         out_specs=VMEM,
         compiler_params=pltpu.CompilerParams(vmem_limit_bytes=4 * 2**20),
     )(*terms)

time: 34.2 us -> 41.1 us (1.20)
  the two profiles are of different devices: /device:TPU:0 before, /device:TPU:24 now
where the time goes in v13:
time: 41.1 us; the launch traced here: 40.8 us
  starting transfers between devices  16.6 us (40%)
  waiting for transfers between devices  10.3 us (25%)
  blocking collectives  7.84 us (19%)
  Pallas kernels  5.32 us (13%)
  between operations  0.74 us (2%)
    ppermute x5, starting transfers between devices, on_device(): lax.ppermute(term, 'layer', list(enumerate(targets)))  12.6 us
    all_to_all x1, blocking collectives, on_device(): lax.all_to_all(asked, 'store', split_axis=0, concat_axis=0, tiled=True)  7.84 us
    ppermute x7, waiting for transfers between devices, swap(): lax.ppermute(value, axis, [(i, i ^ distance) for i in range(lax.axis_size...  6.61 us
    ppermute x7, starting transfers between devices, swap(): lax.ppermute(value, axis, [(i, i ^ distance) for i in range(lax.axis_size...  4.03 us
    ppermute x5, waiting for transfers between devices, on_device(): lax.ppermute(term, 'layer', list(enumerate(targets)))  3.68 us
    pallas_call x1, Pallas kernels, on_device(): pl.pallas_call(functools.partial(condition_kernel, holders, capacity), ou...  2.43 us
    pallas_call x1, Pallas kernels, on_device(): pl.pallas_call(functools.partial(score_kernel, holders, capacity), out_sh...  1.75 us
  transfers between devices with their start and end apart: 12, of which 6 were waited for; matrix products, arithmetic and copies ran while one was open for 0% of the time, Pallas kernels for 0%

profile of v13, /device:TPU:24, one launch (start us, length us, event | category | flops | bytes accessed | tf_op | source)
XLA Modules:
  0.0 40.8 jit_solution(12038270853809099297)
XLA Ops:
  0.7 2.4 %shard_map.73 = (bf16[8,8320]{1,0:T(8,128)(2,1)S(1)}, bf16[256,8192]{1,0:T(8,128)(2,1)S(1)}, f32[8,256]{1,0:T(8,128)S(1)}) custom-call(s32[1]{0:T(128)S(6)} %copy.8.count_ref, bf16[8,8192]{1,0:T(8,128)(2,1)} %refs_0_.1, f32[2,64,64]{2,1,0:T(8,128)} %refs_1_.1, f32[2,64,64]{2,1,0:T(8,128)} %refs_2_.1, s32[16,128]{1,0:T(8,128)} %bitcast.1, s32[1,256]{1,0:T(1,128)} %refs_4_.1, ...), custom_call_target="tpu_custom_call" | custom-call | tf_op jit(solution)/shard_map/pallas_call | solution.py:240
  3.1 2.5 %collective-permute-start.5 = (bf16[8,8320]{1,0:T(8,128)(2,1)S(1)}, bf16[8,8320]{1,0:T(8,128)(2,1)S(1)}, u32[]{:S(2)}, u32[]{:S(2)}) collective-permute-start(bf16[8,8320]{1,0:T(8,128)(2,1)S(1)} %get-tuple-element.15.refs_0_), channel_id=1, source_target_pairs={{0,24},{4,28},{8,16},{12,20},{16,8},{20,12},{24,0},{28,4},{1,25},{... | collective-permute-start | bytes 399368 | tf_op jit(solution)/shard_map/ppermute | solution.py:221
  5.6 0.5 %collective-permute-start.3 = (bf16[8,8320]{1,0:T(8,128)(2,1)S(1)}, bf16[8,8320]{1,0:T(8,128)(2,1)S(1)}, u32[]{:S(2)}, u32[]{:S(2)}) collective-permute-start(bf16[8,8320]{1,0:T(8,128)(2,1)S(1)} %get-tuple-element.15.refs_0_), channel_id=1, source_target_pairs={{0,16},{4,20},{8,24},{12,28},{16,0},{20,4},{24,8},{28,12},{1,17},{... | collective-permute-start | bytes 399368 | tf_op jit(solution)/shard_map/ppermute | solution.py:221
  6.1 0.5 %collective-permute-start.1 = (bf16[8,8320]{1,0:T(8,128)(2,1)S(1)}, bf16[8,8320]{1,0:T(8,128)(2,1)S(1)}, u32[]{:S(2)}, u32[]{:S(2)}) collective-permute-start(bf16[8,8320]{1,0:T(8,128)(2,1)S(1)} %get-tuple-element.15.refs_0_), channel_id=1, source_target_pairs={{0,8},{4,12},{8,0},{12,4},{16,24},{20,28},{24,16},{28,20},{1,9},{5... | collective-permute-start | bytes 399368 | tf_op jit(solution)/shard_map/ppermute | solution.py:221
  6.6 0.0 collective-permute-start
  6.6 3.0 %collective-permute-done.5.refs_6_ = bf16[8,8320]{1,0:T(8,128)(2,1)S(1)} collective-permute-done((bf16[8,8320]{1,0:T(8,128)(2,1)S(1)}, bf16[8,8320]{1,0:T(8,128)(2,1)S(1)}, u32[]{:S(2)}, u32[]{:S(2)}) %collective-permute-start.5) | collective-permute-done | bytes 133152 | tf_op jit(solution)/shard_map/ppermute | solution.py:221
  9.7 0.0 collective-permute-start.6
  9.7 2.5 %collective-permute-done.3.refs_4_ = bf16[8,8320]{1,0:T(8,128)(2,1)S(1)} collective-permute-done((bf16[8,8320]{1,0:T(8,128)(2,1)S(1)}, bf16[8,8320]{1,0:T(8,128)(2,1)S(1)}, u32[]{:S(2)}, u32[]{:S(2)}) %collective-permute-start.3) | collective-permute-done | bytes 133152 | tf_op jit(solution)/shard_map/ppermute | solution.py:221
  12.2 0.0 collective-permute-start.4
  12.2 0.0 collective-permute-done.1.refs_2_
  12.2 0.5 %collective-permute-start.2 = (bf16[8,8320]{1,0:T(8,128)(2,1)S(1)}, bf16[8,8320]{1,0:T(8,128)(2,1)S(1)}, u32[]{:S(2)}, u32[]{:S(2)}) collective-permute-start(bf16[8,8320]{1,0:T(8,128)(2,1)S(1)} %collective-permute-done.1.refs_2_), channel_id=1, source_target_pairs={{0,4},{4,0},{8,12},{12,8},{16,20},{20,16},{24,28},{28,24},{1,5},{5... | collective-permute-start | bytes 399368 | tf_op jit(solution)/shard_map/ppermute | solution.py:221
  12.7 0.0 collective-permute-done.refs_1_
  12.7 0.0 collective-permute-done.6.refs_7_
  12.7 0.8 %collective-permute-done.4.refs_5_ = bf16[8,8320]{1,0:T(8,128)(2,1)S(1)} collective-permute-done((bf16[8,8320]{1,0:T(8,128)(2,1)S(1)}, bf16[8,8320]{1,0:T(8,128)(2,1)S(1)}, u32[]{:S(2)}, u32[]{:S(2)}) %collective-permute-start.4) | collective-permute-done | bytes 133152 | tf_op jit(solution)/shard_map/ppermute | solution.py:221
  13.5 0.2 collective-permute-done.2.refs_3_
  13.7 1.7 %shard_map.74 = f32[8,16,128]{2,1,0:T(8,128)S(1)} custom-call(bf16[8,8320]{1,0:T(8,128)(2,1)S(1)} %get-tuple-element.15.refs_0_, bf16[8,8320]{1,0:T(8,128)(2,1)S(1)} %collective-permute-done.refs_1_, bf16[8,8320]{1,0:T(8,128)(2,1)S(1)} %collective-permute-done.1.refs_2_, bf16[8,8320]{1,0:T(8,128)(2,1)S(1)} %collective-permute-done.2.refs_3_, ...), custom_call_target="tpu_custom_call" | custom-call | tf_op jit(solution)/shard_map/pallas_call | solution.py:264
  15.5 7.8 %all_to_all.5.landed_ref = f32[8,16,128]{2,1,0:T(8,128)S(1)} all-to-all(f32[8,16,128]{2,1,0:T(8,128)S(1)} %shard_map.74), channel_id=1, replica_groups=mesh['store'=8,'layer'=4] {'store'}, dimensions={0} | all-to-all | bytes 131072 | tf_op jit(solution)/shard_map/all_to_all | solution.py:273
  23.3 0.4 shard_map.75
  23.7 0.7 %collective-permute-start.7 = (f32[32,128]{1,0:T(8,128)S(1)}, f32[32,128]{1,0:T(8,128)S(1)}, u32[]{:S(2)}, u32[]{:S(2)}) collective-permute-start(f32[32,128]{1,0:T(8,128)S(1)} %get-tuple-element.18), channel_id=1, source_target_pairs={{0,1},{1,2},{2,0},{3,3},{4,5},{5,6},{6,4},{7,7},{8,9},{9,10},{10,8... | collective-permute-start | bytes 49160 | tf_op jit(solution)/shard_map/ppermute | solution.py:284
  24.4 0.7 %collective-permute-start.8 = (f32[32,128]{1,0:T(8,128)S(1)}, f32[32,128]{1,0:T(8,128)S(1)}, u32[]{:S(2)}, u32[]{:S(2)}) collective-permute-start(f32[32,128]{1,0:T(8,128)S(1)} %get-tuple-element.19), channel_id=1, source_target_pairs={{0,2},{1,0},{2,1},{3,3},{4,6},{5,4},{6,5},{7,7},{8,10},{9,8},{10,9... | collective-permute-start | bytes 49160 | tf_op jit(solution)/shard_map/ppermute | solution.py:284
  25.0 7.4 %collective-permute-start.9 = (f32[32,128]{1,0:T(8,128)S(1)}, f32[32,128]{1,0:T(8,128)S(1)}, u32[]{:S(2)}, u32[]{:S(2)}) collective-permute-start(f32[32,128]{1,0:T(8,128)S(1)} %get-tuple-element.20), channel_id=1, source_target_pairs={{0,3},{1,1},{2,2},{3,0},{4,7},{5,5},{6,6},{7,4},{8,11},{9,9},{10,1... | collective-permute-start | bytes 49160 | tf_op jit(solution)/shard_map/ppermute | solution.py:284
  32.5 1.9 %collective-permute-start.10 = (f32[32,128]{1,0:T(8,128)S(1)}, f32[32,128]{1,0:T(8,128)S(1)}, u32[]{:S(2)}, u32[]{:S(2)}) collective-permute-start(f32[32,128]{1,0:T(8,128)S(1)} %get-tuple-element.21), channel_id=1, source_target_pairs={{0,0},{1,3},{2,2},{3,1},{4,4},{5,7},{6,6},{7,5},{8,8},{9,11},{10,1... | collective-permute-start | bytes 49160 | tf_op jit(solution)/shard_map/ppermute | solution.py:284
  34.4 1.9 %collective-permute-start.11 = (f32[32,128]{1,0:T(8,128)S(1)}, f32[32,128]{1,0:T(8,128)S(1)}, u32[]{:S(2)}, u32[]{:S(2)}) collective-permute-start(f32[32,128]{1,0:T(8,128)S(1)} %get-tuple-element.22), channel_id=1, source_target_pairs={{0,0},{1,1},{2,3},{3,2},{4,4},{5,5},{6,7},{7,6},{8,8},{9,9},{10,11... | collective-permute-start | bytes 49160 | tf_op jit(solution)/shard_map/ppermute | solution.py:284
  36.3 0.0 collective-permute-done.7.refs_1_
  36.3 0.0 collective-permute-done.8.refs_2_
  36.4 0.0 collective-permute-done.9.refs_3_
  36.4 2.6 %collective-permute-done.10.refs_4_ = f32[32,128]{1,0:T(8,128)S(1)} collective-permute-done((f32[32,128]{1,0:T(8,128)S(1)}, f32[32,128]{1,0:T(8,128)S(1)}, u32[]{:S(2)}, u32[]{:S(2)}) %collective-permute-start.10) | collective-permute-done | bytes 16416 | tf_op jit(solution)/shard_map/ppermute | solution.py:284
  39.0 1.0 %collective-permute-done.11.refs_5_ = f32[32,128]{1,0:T(8,128)S(1)} collective-permute-done((f32[32,128]{1,0:T(8,128)S(1)}, f32[32,128]{1,0:T(8,128)S(1)}, u32[]{:S(2)}, u32[]{:S(2)}) %collective-permute-start.11) | collective-permute-done | bytes 16416 | tf_op jit(solution)/shard_map/ppermute | solution.py:284
  40.0 0.8 %shard_map.76 = f32[1,64,64]{2,1,0:T(8,128)} custom-call(f32[32,128]{1,0:T(8,128)S(1)} %get-tuple-element.17.refs_0_, f32[32,128]{1,0:T(8,128)S(1)} %collective-permute-done.7.refs_1_, f32[32,128]{1,0:T(8,128)S(1)} %collective-permute-done.8.refs_2_, f32[32,128]{1,0:T(8,128)S(1)} %collective-permute-done.9.refs_3_, ...), custom_call_target="tpu_custom_call" | custom-call | tf_op jit(solution)/shard_map/pallas_call | solution.py:286
Async XLA Ops:
  3.1 6.6 %collective-permute-start.5 = (bf16[8,8320]{1,0:T(8,128)(2,1)S(1)}, bf16[8,8320]{1,0:T(8,128)(2,1)S(1)}, u32[]{:S(2)}, u32[]{:S(2)}) collective-permute-start(bf16[8,8320]{1,0:T(8,128)(2,1)S(1)} %get-tuple-element.15.refs_0_), channel_id=1, source_target_pairs={{0,24},{4,28},{8,16},{12,20},{16,8},{20,12},{24,0},{28,4},{1,25},{... | collective-permute-start | bytes 399368 | tf_op jit(solution)/shard_map/ppermute | solution.py:221
  5.6 6.6 %collective-permute-start.3 = (bf16[8,8320]{1,0:T(8,128)(2,1)S(1)}, bf16[8,8320]{1,0:T(8,128)(2,1)S(1)}, u32[]{:S(2)}, u32[]{:S(2)}) collective-permute-start(bf16[8,8320]{1,0:T(8,128)(2,1)S(1)} %get-tuple-element.15.refs_0_), channel_id=1, source_target_pairs={{0,16},{4,20},{8,24},{12,28},{16,0},{20,4},{24,8},{28,12},{1,17},{... | collective-permute-start | bytes 399368 | tf_op jit(solution)/shard_map/ppermute | solution.py:221
  6.1 6.1 %collective-permute-start.1 = (bf16[8,8320]{1,0:T(8,128)(2,1)S(1)}, bf16[8,8320]{1,0:T(8,128)(2,1)S(1)}, u32[]{:S(2)}, u32[]{:S(2)}) collective-permute-start(bf16[8,8320]{1,0:T(8,128)(2,1)S(1)} %get-tuple-element.15.refs_0_), channel_id=1, source_target_pairs={{0,8},{4,12},{8,0},{12,4},{16,24},{20,28},{24,16},{28,20},{1,9},{5... | collective-permute-start | bytes 399368 | tf_op jit(solution)/shard_map/ppermute | solution.py:221
  6.6 6.1 %collective-permute-start = (bf16[8,8320]{1,0:T(8,128)(2,1)S(1)}, bf16[8,8320]{1,0:T(8,128)(2,1)S(1)}, u32[]{:S(2)}, u32[]{:S(2)}) collective-permute-start(bf16[8,8320]{1,0:T(8,128)(2,1)S(1)} %get-tuple-element.15.refs_0_), channel_id=1, source_target_pairs={{0,4},{4,0},{8,12},{12,8},{16,20},{20,16},{24,28},{28,24},{1,5},{5... | collective-permute-start | bytes 399368 | tf_op jit(solution)/shard_map/ppermute | solution.py:221
  9.7 3.0 %collective-permute-start.6 = (bf16[8,8320]{1,0:T(8,128)(2,1)S(1)}, bf16[8,8320]{1,0:T(8,128)(2,1)S(1)}, u32[]{:S(2)}, u32[]{:S(2)}) collective-permute-start(bf16[8,8320]{1,0:T(8,128)(2,1)S(1)} %collective-permute-done.5.refs_6_), channel_id=1, source_target_pairs={{0,4},{4,0},{8,12},{12,8},{16,20},{20,16},{24,28},{28,24},{1,5},{5... | collective-permute-start | bytes 399368 | tf_op jit(solution)/shard_map/ppermute | solution.py:221
  12.2 1.4 %collective-permute-start.4 = (bf16[8,8320]{1,0:T(8,128)(2,1)S(1)}, bf16[8,8320]{1,0:T(8,128)(2,1)S(1)}, u32[]{:S(2)}, u32[]{:S(2)}) collective-permute-start(bf16[8,8320]{1,0:T(8,128)(2,1)S(1)} %collective-permute-done.3.refs_4_), channel_id=1, source_target_pairs={{0,4},{4,0},{8,12},{12,8},{16,20},{20,16},{24,28},{28,24},{1,5},{5... | collective-permute-start | bytes 399368 | tf_op jit(solution)/shard_map/ppermute | solution.py:221
  12.2 1.5 %collective-permute-start.2 = (bf16[8,8320]{1,0:T(8,128)(2,1)S(1)}, bf16[8,8320]{1,0:T(8,128)(2,1)S(1)}, u32[]{:S(2)}, u32[]{:S(2)}) collective-permute-start(bf16[8,8320]{1,0:T(8,128)(2,1)S(1)} %collective-permute-done.1.refs_2_), channel_id=1, source_target_pairs={{0,4},{4,0},{8,12},{12,8},{16,20},{20,16},{24,28},{28,24},{1,5},{5... | collective-permute-start | bytes 399368 | tf_op jit(solution)/shard_map/ppermute | solution.py:221
  23.7 12.6 %collective-permute-start.7 = (f32[32,128]{1,0:T(8,128)S(1)}, f32[32,128]{1,0:T(8,128)S(1)}, u32[]{:S(2)}, u32[]{:S(2)}) collective-permute-start(f32[32,128]{1,0:T(8,128)S(1)} %get-tuple-element.18), channel_id=1, source_target_pairs={{0,1},{1,2},{2,0},{3,3},{4,5},{5,6},{6,4},{7,7},{8,9},{9,10},{10,8... | collective-permute-start | bytes 49160 | tf_op jit(solution)/shard_map/ppermute | solution.py:284
  24.4 12.0 %collective-permute-start.8 = (f32[32,128]{1,0:T(8,128)S(1)}, f32[32,128]{1,0:T(8,128)S(1)}, u32[]{:S(2)}, u32[]{:S(2)}) collective-permute-start(f32[32,128]{1,0:T(8,128)S(1)} %get-tuple-element.19), channel_id=1, source_target_pairs={{0,2},{1,0},{2,1},{3,3},{4,6},{5,4},{6,5},{7,7},{8,10},{9,8},{10,9... | collective-permute-start | bytes 49160 | tf_op jit(solution)/shard_map/ppermute | solution.py:284
  25.0 11.3 %collective-permute-start.9 = (f32[32,128]{1,0:T(8,128)S(1)}, f32[32,128]{1,0:T(8,128)S(1)}, u32[]{:S(2)}, u32[]{:S(2)}) collective-permute-start(f32[32,128]{1,0:T(8,128)S(1)} %get-tuple-element.20), channel_id=1, source_target_pairs={{0,3},{1,1},{2,2},{3,0},{4,7},{5,5},{6,6},{7,4},{8,11},{9,9},{10,1... | collective-permute-start | bytes 49160 | tf_op jit(solution)/shard_map/ppermute | solution.py:284
  32.5 6.5 %collective-permute-start.10 = (f32[32,128]{1,0:T(8,128)S(1)}, f32[32,128]{1,0:T(8,128)S(1)}, u32[]{:S(2)}, u32[]{:S(2)}) collective-permute-start(f32[32,128]{1,0:T(8,128)S(1)} %get-tuple-element.21), channel_id=1, source_target_pairs={{0,0},{1,3},{2,2},{3,1},{4,4},{5,7},{6,6},{7,5},{8,8},{9,11},{10,1... | collective-permute-start | bytes 49160 | tf_op jit(solution)/shard_map/ppermute | solution.py:284
  34.4 5.6 %collective-permute-start.11 = (f32[32,128]{1,0:T(8,128)S(1)}, f32[32,128]{1,0:T(8,128)S(1)}, u32[]{:S(2)}, u32[]{:S(2)}) collective-permute-start(f32[32,128]{1,0:T(8,128)S(1)} %get-tuple-element.22), channel_id=1, source_target_pairs={{0,0},{1,1},{2,3},{3,2},{4,4},{5,5},{6,7},{7,6},{8,8},{9,9},{10,11... | collective-permute-start | bytes 49160 | tf_op jit(solution)/shard_map/ppermute | solution.py:284

commit v14 on v13

--- a/solution.py
+++ b/solution.py
@@ -16,16 +16,6 @@
 
 def iota(shape, dimension):
     return lax.broadcasted_iota(jnp.int32, shape, dimension)
-
-
-def layer_plan(groups):
-    if groups == 4:
-        return [[1, 2, 0, 3], [2, 0, 1, 3], [3, 1, 2, 0], [0, 3, 2, 1], [0, 1, 3, 2]]
-    return [[(g + step) % groups for g in range(groups)] for step in range(1, groups)]
-
-
-def entry(values, index):
-    return sum(jnp.where(index == i, value, 0) for i, value in enumerate(values))
 
 
 def parts_of(value):
@@ -41,9 +31,8 @@
     return value.astype(jnp.float32).astype(jnp.bfloat16)
 
 
-def condition_kernel(holders, capacity, count_ref, *refs):
-    sources, packed_ref, pages_ref, found_ref, landing, arrived = refs[:6], refs[6], refs[7], refs[8], refs[9:14], refs[14]
-    turned_ref = refs[15]
+def condition_kernel(holders, capacity, *refs):
+    sources, packed_ref, pages_ref, found_ref, landing, arrived, turned_ref = refs[:6], *refs[6:9], refs[9:14], *refs[14:]
     copies = [
         pltpu.make_async_copy(source, target, arrived.at[i])
         for i, (source, target) in enumerate(zip(sources, landing + (pages_ref,)))
@@ -112,16 +101,14 @@
 
     slots = cand_ref.shape[1]
     home_rows = home_ref.shape[0]
-    wanted = jnp.where(iota((1, slots), 1) < count_ref[0], cand_ref[...], -1)
-    known = jnp.maximum(wanted, 0)
-    onehot = (iota((LANES, slots), 0) == known % LANES).astype(jnp.float32).astype(jnp.bfloat16)
+    wanted = cand_ref[...]
+    onehot = (iota((LANES, slots), 0) == wanted % LANES).astype(jnp.float32).astype(jnp.bfloat16)
     home = home_ref[...]
     table = jnp.concatenate([home // per_holder, home % per_holder], axis=0).astype(jnp.float32).astype(jnp.bfloat16)
     found = jnp.dot(table, onehot, preferred_element_type=jnp.float32)
-    mine = iota((home_rows, slots), 0) == known // LANES
+    mine = iota((home_rows, slots), 0) == wanted // LANES
     holder = jnp.sum(jnp.where(mine, found[:home_rows], 0.0), axis=0, keepdims=True)
     within = jnp.sum(jnp.where(mine, found[home_rows:], 0.0), axis=0, keepdims=True)
-    holder = jnp.where(wanted >= 0, holder, float(holders))
     at_holder = iota((holders, slots), 0).astype(jnp.float32) == holder
     earlier = exact_bf16(iota((slots, slots), 0) < iota((slots, slots), 1))
     before = jnp.dot(exact_bf16(at_holder), earlier, preferred_element_type=jnp.float32)
@@ -178,14 +165,14 @@
         out_ref[me ^ k] = picked[k * half:(k + 1) * half]
 
 
-def spread_kernel(holders, groups, found_ref, landed_ref, *out_refs):
+def spread_kernel(holders, groups, count_ref, found_ref, landed_ref, *out_refs):
     half = landed_ref.shape[1]
     slots = found_ref.shape[1]
     total = landed_ref.shape[2] // 2
-    plan = layer_plan(groups)
     at = lax.axis_index("layer")
     share = slots // groups
-    holder, rank_there = found_ref[0:1], found_ref[1:2]
+    used = iota((1, slots), 1) < count_ref[0]
+    holder, rank_there = jnp.where(used, found_ref[0:1], float(holders)), found_ref[1:2]
     place = iota((holders * half, slots), 0).astype(jnp.float32)
     parts = parts_of(jnp.concatenate([landed_ref[h] for h in range(holders)], axis=0))[::-1]
     result = jnp.zeros((total, slots), jnp.float32)
@@ -196,25 +183,16 @@
         for part in parts:
             spread = lax.dot_general(part, chosen, (((0,), (0,)), ((), ())), preferred_element_type=jnp.float32)
             result = result + spread[side * total:(side + 1) * total]
+    result = result.T
     blocks = []
     for g in range(groups):
-        block = result[:, g * share:(g + 1) * share]
-        blocks.append(jnp.concatenate([block[:total // 2], block[total // 2:]], axis=1))
-    for out_ref, targets in zip(out_refs, [list(range(groups))] + plan):
+        block = result[g * share:(g + 1) * share]
+        blocks.append(jnp.concatenate([block[:share // 2], block[share // 2:]], axis=1))
+    for step, out_ref in enumerate(out_refs):
         chosen = blocks[0]
         for g in range(1, groups):
-            chosen = jnp.where(entry(targets, at) == g, blocks[g], chosen)
+            chosen = jnp.where((at + step) % groups == g, blocks[g], chosen)
         out_ref[...] = chosen
-
-
-def add_kernel(groups, *refs):
-    at = lax.axis_index("layer")
-    out_ref = refs[-1]
-    total = refs[0][...]
-    for ref, targets in zip(refs[1:], layer_plan(groups)):
-        total = total + jnp.where(entry(targets, at) == at, 0.0, ref[...])
-    share = total.shape[1] // 2
-    out_ref[0] = jnp.concatenate([total[:, :share], total[:, share:]], axis=0).T
 
 
 def swap(value, axis, distance):
@@ -244,12 +222,12 @@
             pltpu.VMEM(page_store.shape, bf16),
             jax.ShapeDtypeStruct((8, slots), jnp.float32),
         ],
-        in_specs=[SMEM] + [HBM] * len(sources),
+        in_specs=[HBM] * len(sources),
         out_specs=[VMEM] * 3,
         scratch_shapes=[pltpu.VMEM(source.shape, source.dtype) for source in sources[:-1]]
         + [pltpu.SemaphoreType.DMA((len(sources),)), pltpu.VMEM((layers, rows * rank // 2, LANES), jnp.float32)],
         compiler_params=pltpu.CompilerParams(vmem_limit_bytes=10 * 2**20 + 24 * slots * slots),
-    )(counts, *sources)
+    )(*sources)
 
     blocks = [None] * holders
     blocks[0] = packed
@@ -272,24 +250,17 @@
 
     landed = lax.all_to_all(asked, "store", split_axis=0, concat_axis=0, tiled=True)
     share = slots // groups
-    plan = layer_plan(groups)
     terms = pl.pallas_call(
         functools.partial(spread_kernel, holders, groups),
-        out_shape=[jax.ShapeDtypeStruct((total // 2, 2 * share), jnp.float32)] * (1 + len(plan)),
-        in_specs=[VMEM] * 2,
-        out_specs=[VMEM] * (1 + len(plan)),
+        out_shape=[jax.ShapeDtypeStruct((share // 2, 2 * total), jnp.float32)] * groups,
+        in_specs=[SMEM] + [VMEM] * 2,
+        out_specs=[VMEM] * groups,
         compiler_params=pltpu.CompilerParams(vmem_limit_bytes=4 * 2**20 + 64 * total * slots),
-    )(found, landed)
-    terms = [terms[0]] + [
-        lax.ppermute(term, "layer", list(enumerate(targets))) for term, targets in zip(terms[1:], plan)
-    ]
-    return pl.pallas_call(
-        functools.partial(add_kernel, groups),
-        out_shape=jax.ShapeDtypeStruct((1, share, total), jnp.float32),
-        in_specs=[VMEM] * len(terms),
-        out_specs=VMEM,
-        compiler_params=pltpu.CompilerParams(vmem_limit_bytes=4 * 2**20),
-    )(*terms)
+    )(counts, found, landed)
+    summed = terms[0]
+    for step in range(1, groups):
+        summed = summed + lax.ppermute(terms[step], "layer", [(g, (g + step) % groups) for g in range(groups)])
+    return jnp.concatenate([summed[:, :total], summed[:, total:]], axis=0)[None]
 
 
 def solution(mesh):

time: 41.1 us -> 34.8 us (0.85)
  the two profiles are of different devices: /device:TPU:24 before, /device:TPU:0 now
where the time goes in v14:
time: 34.8 us; the launch traced here: 34.6 us
  starting transfers between devices  14 us (40%)
  waiting for transfers between devices  14 us (40%)
  Pallas kernels  5.23 us (15%)
  between operations  0.68 us (2%)
  other arithmetic  0.63 us (2%)
    ppermute x7, waiting for transfers between devices, swap(): lax.ppermute(value, axis, [(i, i ^ distance) for i in range(lax.axis_size...  7.33 us
    ppermute x3, starting transfers between devices, on_device(): lax.ppermute(terms[step], 'layer', [(g, (g + step) % groups) for g in ran...  5.57 us
    ppermute x7, starting transfers between devices, swap(): lax.ppermute(value, axis, [(i, i ^ distance) for i in range(lax.axis_size...  5.06 us
    all_to_all x1, waiting for transfers between devices, on_device(): lax.all_to_all(asked, 'store', split_axis=0, concat_axis=0, tiled=True)  4.3 us
    all_to_all x1, starting transfers between devices, on_device(): lax.all_to_all(asked, 'store', split_axis=0, concat_axis=0, tiled=True)  3.35 us
    pallas_call x1, Pallas kernels, on_device(): pl.pallas_call(functools.partial(condition_kernel, holders, capacity), ou...  2.43 us
    ppermute x3, waiting for transfers between devices, on_device(): lax.ppermute(terms[step], 'layer', [(g, (g + step) % groups) for g in ran...  2.39 us
    pallas_call x1, Pallas kernels, on_device(): pl.pallas_call(functools.partial(score_kernel, holders, capacity), out_sh...  2.36 us
  transfers between devices with their start and end apart: 11, of which 8 were waited for; matrix products, arithmetic and copies ran while one was open for 0% of the time, Pallas kernels for 0%

profile of v14, /device:TPU:0, one launch (start us, length us, event | category | flops | bytes accessed | tf_op | source)
XLA Modules:
  0.0 34.6 jit_solution(15213505033957418446)
XLA Ops:
  0.0 2.4 %shard_map.73 = (bf16[8,8320]{1,0:T(8,128)(2,1)S(1)}, bf16[256,8192]{1,0:T(8,128)(2,1)S(1)}, f32[8,256]{1,0:T(8,128)S(1)}) custom-call(bf16[8,8192]{1,0:T(8,128)(2,1)} %refs_0_.1, f32[2,64,64]{2,1,0:T(8,128)} %refs_1_.1, f32[2,64,64]{2,1,0:T(8,128)} %refs_2_.1, s32[16,128]{1,0:T(8,128)} %bitcast.3, s32[1,256]{1,0:T(1,128)} %refs_4_.1, bf16[256,8192]{1,0:T(8,128)(2,1)} %refs_5_.1), custom_call_target="tpu_custom_call" | custom-call | tf_op jit(solution)/shard_map/pallas_call | solution.py:218
  2.4 3.0 %collective-permute-start.1 = (bf16[8,8320]{1,0:T(8,128)(2,1)S(1)}, bf16[8,8320]{1,0:T(8,128)(2,1)S(1)}, u32[]{:S(2)}, u32[]{:S(2)}) collective-permute-start(bf16[8,8320]{1,0:T(8,128)(2,1)S(1)} %get-tuple-element.13.refs_0_), channel_id=1, source_target_pairs={{0,8},{4,12},{8,0},{12,4},{16,24},{20,28},{24,16},{28,20},{1,9},{5... | collective-permute-start | bytes 399368 | tf_op jit(solution)/shard_map/ppermute | solution.py:199
  5.4 1.5 %collective-permute-start.3 = (bf16[8,8320]{1,0:T(8,128)(2,1)S(1)}, bf16[8,8320]{1,0:T(8,128)(2,1)S(1)}, u32[]{:S(2)}, u32[]{:S(2)}) collective-permute-start(bf16[8,8320]{1,0:T(8,128)(2,1)S(1)} %get-tuple-element.13.refs_0_), channel_id=1, source_target_pairs={{0,16},{4,20},{8,24},{12,28},{16,0},{20,4},{24,8},{28,12},{1,17},{... | collective-permute-start | bytes 399368 | tf_op jit(solution)/shard_map/ppermute | solution.py:199
  7.0 0.0 collective-permute-start.5
  7.0 0.0 collective-permute-start
  7.0 2.4 %collective-permute-done.1.refs_2_ = bf16[8,8320]{1,0:T(8,128)(2,1)S(1)} collective-permute-done((bf16[8,8320]{1,0:T(8,128)(2,1)S(1)}, bf16[8,8320]{1,0:T(8,128)(2,1)S(1)}, u32[]{:S(2)}, u32[]{:S(2)}) %collective-permute-start.1) | collective-permute-done | bytes 133152 | tf_op jit(solution)/shard_map/ppermute | solution.py:199
  9.4 0.0 collective-permute-start.2
  9.4 3.9 %collective-permute-done.3.refs_4_ = bf16[8,8320]{1,0:T(8,128)(2,1)S(1)} collective-permute-done((bf16[8,8320]{1,0:T(8,128)(2,1)S(1)}, bf16[8,8320]{1,0:T(8,128)(2,1)S(1)}, u32[]{:S(2)}, u32[]{:S(2)}) %collective-permute-start.3) | collective-permute-done | bytes 133152 | tf_op jit(solution)/shard_map/ppermute | solution.py:199
  13.3 0.0 collective-permute-start.4
  13.3 0.0 collective-permute-done.5.refs_6_
  13.3 0.5 %collective-permute-start.6 = (bf16[8,8320]{1,0:T(8,128)(2,1)S(1)}, bf16[8,8320]{1,0:T(8,128)(2,1)S(1)}, u32[]{:S(2)}, u32[]{:S(2)}) collective-permute-start(bf16[8,8320]{1,0:T(8,128)(2,1)S(1)} %collective-permute-done.5.refs_6_), channel_id=1, source_target_pairs={{0,4},{4,0},{8,12},{12,8},{16,20},{20,16},{24,28},{28,24},{1,5},{5... | collective-permute-start | bytes 399368 | tf_op jit(solution)/shard_map/ppermute | solution.py:199
  13.8 0.0 collective-permute-done.refs_1_
  13.8 0.0 collective-permute-done.2.refs_3_
  13.8 0.8 %collective-permute-done.4.refs_5_ = bf16[8,8320]{1,0:T(8,128)(2,1)S(1)} collective-permute-done((bf16[8,8320]{1,0:T(8,128)(2,1)S(1)}, bf16[8,8320]{1,0:T(8,128)(2,1)S(1)}, u32[]{:S(2)}, u32[]{:S(2)}) %collective-permute-start.4) | collective-permute-done | bytes 133152 | tf_op jit(solution)/shard_map/ppermute | solution.py:199
  14.6 0.2 collective-permute-done.6.refs_7_
  14.8 2.4 %shard_map.74 = f32[8,16,128]{2,1,0:T(8,128)} custom-call(bf16[8,8320]{1,0:T(8,128)(2,1)S(1)} %get-tuple-element.13.refs_0_, bf16[8,8320]{1,0:T(8,128)(2,1)S(1)} %collective-permute-done.refs_1_, bf16[8,8320]{1,0:T(8,128)(2,1)S(1)} %collective-permute-done.1.refs_2_, bf16[8,8320]{1,0:T(8,128)(2,1)S(1)} %collective-permute-done.2.refs_3_, ...), custom_call_target="tpu_custom_call" | custom-call | tf_op jit(solution)/shard_map/pallas_call | solution.py:242
  17.2 3.3 %all-to-all-start = ((f32[8,16,128]{2,1,0:T(8,128)}), f32[8,16,128]{2,1,0:T(8,128)S(1)}, u32[]{:S(2)}, u32[]{:S(2)}) async-start(f32[8,16,128]{2,1,0:T(8,128)} %shard_map.74), calls=%async_computation | async-start | bytes 131072 | tf_op jit(solution)/shard_map/all_to_all | solution.py:251
  21.2 4.3 %all-to-all-done.landed_ref = f32[8,16,128]{2,1,0:T(8,128)S(1)} async-done(((f32[8,16,128]{2,1,0:T(8,128)}), f32[8,16,128]{2,1,0:T(8,128)S(1)}, u32[]{:S(2)}, u32[]{:S(2)}) %all-to-all-start) | async-done | bytes 65568 | tf_op jit(solution)/shard_map/all_to_all | solution.py:251
  25.5 0.4 %shard_map.75 = (f32[32,128]{1,0:T(8,128)S(1)}, f32[32,128]{1,0:T(8,128)S(1)}, f32[32,128]{1,0:T(8,128)S(1)}, f32[32,128]{1,0:T(8,128)S(1)}) custom-call(s32[1]{0:T(128)S(6)} %copy.8.count_ref, f32[8,256]{1,0:T(8,128)S(1)} %get-tuple-element.12.found_ref, f32[8,16,128]{2,1,0:T(8,128)S(1)} %all-to-all-done.landed_ref), custom_call_target="tpu_custom_call" | custom-call | tf_op jit(solution)/shard_map/pallas_call | solution.py:253
  26.0 1.6 %collective-permute-start.7 = (f32[32,128]{1,0:T(8,128)S(1)}, f32[32,128]{1,0:T(8,128)S(1)}, u32[]{:S(2)}, u32[]{:S(2)}) collective-permute-start(f32[32,128]{1,0:T(8,128)S(1)} %get-tuple-element.16), channel_id=1, source_target_pairs={{0,1},{1,2},{2,3},{3,0},{4,5},{5,6},{6,7},{7,4},{8,9},{9,10},{10,1... | collective-permute-start | bytes 49160 | tf_op jit(solution)/shard_map/ppermute | solution.py:262
  27.6 2.6 %collective-permute-start.8 = (f32[32,128]{1,0:T(8,128)S(1)}, f32[32,128]{1,0:T(8,128)S(1)}, u32[]{:S(2)}, u32[]{:S(2)}) collective-permute-start(f32[32,128]{1,0:T(8,128)S(1)} %get-tuple-element.17), channel_id=1, source_target_pairs={{0,2},{1,3},{2,0},{3,1},{4,6},{5,7},{6,4},{7,5},{8,10},{9,11},{10,... | collective-permute-start | bytes 49160 | tf_op jit(solution)/shard_map/ppermute | solution.py:262
  30.2 1.3 %collective-permute-start.9 = (f32[32,128]{1,0:T(8,128)S(1)}, f32[32,128]{1,0:T(8,128)S(1)}, u32[]{:S(2)}, u32[]{:S(2)}) collective-permute-start(f32[32,128]{1,0:T(8,128)S(1)} %get-tuple-element.18), channel_id=1, source_target_pairs={{0,3},{1,0},{2,1},{3,2},{4,7},{5,4},{6,5},{7,6},{8,11},{9,8},{10,9... | collective-permute-start | bytes 49160 | tf_op jit(solution)/shard_map/ppermute | solution.py:262
  31.5 0.1 collective-permute-done.7
  31.6 0.6 %collective-permute-done.8 = f32[32,128]{1,0:T(8,128)S(1)} collective-permute-done((f32[32,128]{1,0:T(8,128)S(1)}, f32[32,128]{1,0:T(8,128)S(1)}, u32[]{:S(2)}, u32[]{:S(2)}) %collective-permute-start.8) | collective-permute-done | bytes 16416 | tf_op jit(solution)/shard_map/ppermute | solution.py:262
  32.2 1.7 %collective-permute-done.9 = f32[32,128]{1,0:T(8,128)S(1)} collective-permute-done((f32[32,128]{1,0:T(8,128)S(1)}, f32[32,128]{1,0:T(8,128)S(1)}, u32[]{:S(2)}, u32[]{:S(2)}) %collective-permute-start.9) | collective-permute-done | bytes 16416 | tf_op jit(solution)/shard_map/ppermute | solution.py:262
  33.9 0.1 fusion
  34.0 0.6 %maximum_bitcast_fusion = f32[1,64,64]{2,1,0:T(8,128)} fusion(f32[32,64]{1,0:T(8,128)S(1)} %get-tuple-element.20, f32[32,64]{1,0:T(8,128)S(1)} %get-tuple-element.19), kind=kLoop, calls=%fused_computation | loop fusion | flops 4096 | bytes 32768 | tf_op jit(solution)/shard_map/broadcast_in_dim | solution.py:263
  (1 shorter events, 0.0 us)
Async XLA Ops:
  2.4 7.0 %collective-permute-start.1 = (bf16[8,8320]{1,0:T(8,128)(2,1)S(1)}, bf16[8,8320]{1,0:T(8,128)(2,1)S(1)}, u32[]{:S(2)}, u32[]{:S(2)}) collective-permute-start(bf16[8,8320]{1,0:T(8,128)(2,1)S(1)} %get-tuple-element.13.refs_0_), channel_id=1, source_target_pairs={{0,8},{4,12},{8,0},{12,4},{16,24},{20,28},{24,16},{28,20},{1,9},{5... | collective-permute-start | bytes 399368 | tf_op jit(solution)/shard_map/ppermute | solution.py:199
  5.4 7.9 %collective-permute-start.3 = (bf16[8,8320]{1,0:T(8,128)(2,1)S(1)}, bf16[8,8320]{1,0:T(8,128)(2,1)S(1)}, u32[]{:S(2)}, u32[]{:S(2)}) collective-permute-start(bf16[8,8320]{1,0:T(8,128)(2,1)S(1)} %get-tuple-element.13.refs_0_), channel_id=1, source_target_pairs={{0,16},{4,20},{8,24},{12,28},{16,0},{20,4},{24,8},{28,12},{1,17},{... | collective-permute-start | bytes 399368 | tf_op jit(solution)/shard_map/ppermute | solution.py:199
  7.0 6.3 %collective-permute-start.5 = (bf16[8,8320]{1,0:T(8,128)(2,1)S(1)}, bf16[8,8320]{1,0:T(8,128)(2,1)S(1)}, u32[]{:S(2)}, u32[]{:S(2)}) collective-permute-start(bf16[8,8320]{1,0:T(8,128)(2,1)S(1)} %get-tuple-element.13.refs_0_), channel_id=1, source_target_pairs={{0,24},{4,28},{8,16},{12,20},{16,8},{20,12},{24,0},{28,4},{1,25},{... | collective-permute-start | bytes 399368 | tf_op jit(solution)/shard_map/ppermute | solution.py:199
  7.0 6.8 %collective-permute-start = (bf16[8,8320]{1,0:T(8,128)(2,1)S(1)}, bf16[8,8320]{1,0:T(8,128)(2,1)S(1)}, u32[]{:S(2)}, u32[]{:S(2)}) collective-permute-start(bf16[8,8320]{1,0:T(8,128)(2,1)S(1)} %get-tuple-element.13.refs_0_), channel_id=1, source_target_pairs={{0,4},{4,0},{8,12},{12,8},{16,20},{20,16},{24,28},{28,24},{1,5},{5... | collective-permute-start | bytes 399368 | tf_op jit(solution)/shard_map/ppermute | solution.py:199
  9.4 4.4 %collective-permute-start.2 = (bf16[8,8320]{1,0:T(8,128)(2,1)S(1)}, bf16[8,8320]{1,0:T(8,128)(2,1)S(1)}, u32[]{:S(2)}, u32[]{:S(2)}) collective-permute-start(bf16[8,8320]{1,0:T(8,128)(2,1)S(1)} %collective-permute-done.1.refs_2_), channel_id=1, source_target_pairs={{0,4},{4,0},{8,12},{12,8},{16,20},{20,16},{24,28},{28,24},{1,5},{5... | collective-permute-start | bytes 399368 | tf_op jit(solution)/shard_map/ppermute | solution.py:199
  13.3 1.4 %collective-permute-start.4 = (bf16[8,8320]{1,0:T(8,128)(2,1)S(1)}, bf16[8,8320]{1,0:T(8,128)(2,1)S(1)}, u32[]{:S(2)}, u32[]{:S(2)}) collective-permute-start(bf16[8,8320]{1,0:T(8,128)(2,1)S(1)} %collective-permute-done.3.refs_4_), channel_id=1, source_target_pairs={{0,4},{4,0},{8,12},{12,8},{16,20},{20,16},{24,28},{28,24},{1,5},{5... | collective-permute-start | bytes 399368 | tf_op jit(solution)/shard_map/ppermute | solution.py:199
  13.3 1.5 %collective-permute-start.6 = (bf16[8,8320]{1,0:T(8,128)(2,1)S(1)}, bf16[8,8320]{1,0:T(8,128)(2,1)S(1)}, u32[]{:S(2)}, u32[]{:S(2)}) collective-permute-start(bf16[8,8320]{1,0:T(8,128)(2,1)S(1)} %collective-permute-done.5.refs_6_), channel_id=1, source_target_pairs={{0,4},{4,0},{8,12},{12,8},{16,20},{20,16},{24,28},{28,24},{1,5},{5... | collective-permute-start | bytes 399368 | tf_op jit(solution)/shard_map/ppermute | solution.py:199
  17.2 8.3 %all-to-all-start = ((f32[8,16,128]{2,1,0:T(8,128)}), f32[8,16,128]{2,1,0:T(8,128)S(1)}, u32[]{:S(2)}, u32[]{:S(2)}) async-start(f32[8,16,128]{2,1,0:T(8,128)} %shard_map.74), calls=%async_computation | async-start | bytes 131072 | tf_op jit(solution)/shard_map/all_to_all | solution.py:251
  26.0 5.7 %collective-permute-start.7 = (f32[32,128]{1,0:T(8,128)S(1)}, f32[32,128]{1,0:T(8,128)S(1)}, u32[]{:S(2)}, u32[]{:S(2)}) collective-permute-start(f32[32,128]{1,0:T(8,128)S(1)} %get-tuple-element.16), channel_id=1, source_target_pairs={{0,1},{1,2},{2,3},{3,0},{4,5},{5,6},{6,7},{7,4},{8,9},{9,10},{10,1... | collective-permute-start | bytes 49160 | tf_op jit(solution)/shard_map/ppermute | solution.py:262
  27.6 4.6 %collective-permute-start.8 = (f32[32,128]{1,0:T(8,128)S(1)}, f32[32,128]{1,0:T(8,128)S(1)}, u32[]{:S(2)}, u32[]{:S(2)}) collective-permute-start(f32[32,128]{1,0:T(8,128)S(1)} %get-tuple-element.17), channel_id=1, source_target_pairs={{0,2},{1,3},{2,0},{3,1},{4,6},{5,7},{6,4},{7,5},{8,10},{9,11},{10,... | collective-permute-start | bytes 49160 | tf_op jit(solution)/shard_map/ppermute | solution.py:262
  30.2 3.7 %collective-permute-start.9 = (f32[32,128]{1,0:T(8,128)S(1)}, f32[32,128]{1,0:T(8,128)S(1)}, u32[]{:S(2)}, u32[]{:S(2)}) collective-permute-start(f32[32,128]{1,0:T(8,128)S(1)} %get-tuple-element.18), channel_id=1, source_target_pairs={{0,3},{1,0},{2,1},{3,2},{4,7},{5,4},{6,5},{7,6},{8,11},{9,8},{10,9... | collective-permute-start | bytes 49160 | tf_op jit(solution)/shard_map/ppermute | solution.py:262

commit v15 on v14

--- a/solution.py
+++ b/solution.py
@@ -128,7 +128,8 @@
 
 
 def score_kernel(holders, capacity, *refs):
-    packed_refs, pages_ref, out_ref, total, queries = refs[:holders], *refs[holders:]
+    count_ref, found_ref, packed_refs = *refs[:2], refs[2:2 + holders]
+    pages_ref, out_ref, used_ref, total, queries = refs[2 + holders:]
     me = lax.axis_index("store")
     count, width = pages_ref.shape
     rows = packed_refs[0].shape[0]
@@ -160,19 +161,21 @@
         row = jnp.concatenate([row[:, side * half:(side + 1) * half] for row in asked], axis=1)
         chosen = exact_bf16(page == row)
         picked.append(sum(jnp.dot(part, chosen, preferred_element_type=jnp.float32) for part in parts))
+    used_ref[...] = found_ref[...]
+    own_slots = found_ref.shape[1]
+    used_ref[0:1] = jnp.where(iota((1, own_slots), 1) < count_ref[0], found_ref[0:1], float(holders))
     picked = jnp.concatenate(picked, axis=0).T
     for k in range(holders):
         out_ref[me ^ k] = picked[k * half:(k + 1) * half]
 
 
-def spread_kernel(holders, groups, count_ref, found_ref, landed_ref, *out_refs):
+def spread_kernel(holders, groups, found_ref, landed_ref, *out_refs):
     half = landed_ref.shape[1]
     slots = found_ref.shape[1]
     total = landed_ref.shape[2] // 2
     at = lax.axis_index("layer")
     share = slots // groups
-    used = iota((1, slots), 1) < count_ref[0]
-    holder, rank_there = jnp.where(used, found_ref[0:1], float(holders)), found_ref[1:2]
+    holder, rank_there = found_ref[0:1], found_ref[1:2]
     place = iota((holders * half, slots), 0).astype(jnp.float32)
     parts = parts_of(jnp.concatenate([landed_ref[h] for h in range(holders)], axis=0))[::-1]
     result = jnp.zeros((total, slots), jnp.float32)
@@ -231,32 +234,35 @@
 
     blocks = [None] * holders
     blocks[0] = packed
+    for k in reversed(range(2, holders, 2)):
+        blocks[k] = swap(packed, "store", k)
     blocks[1] = swap(packed, "store", 1)
-    for k in range(2, holders, 2):
-        blocks[k] = swap(packed, "store", k)
-    for k in range(2, holders, 2):
+    for k in reversed(range(2, holders, 2)):
         blocks[k + 1] = swap(blocks[k], "store", 1)
 
     total = holders * rows
     bytes_in = 2 * holders * rows * (width + notes) + 2 * per_holder * width
-    asked = pl.pallas_call(
+    asked, used = pl.pallas_call(
         functools.partial(score_kernel, holders, capacity),
-        out_shape=jax.ShapeDtypeStruct((holders, capacity // 2, 2 * total), jnp.float32),
-        in_specs=[VMEM] * (holders + 1),
-        out_specs=VMEM,
+        out_shape=[
+            jax.ShapeDtypeStruct((holders, capacity // 2, 2 * total), jnp.float32),
+            jax.ShapeDtypeStruct(found.shape, jnp.float32),
+        ],
+        in_specs=[SMEM] + [VMEM] * (holders + 2),
+        out_specs=[VMEM] * 2,
         scratch_shapes=[pltpu.VMEM((total, per_holder), jnp.float32), pltpu.VMEM((total, width), bf16)],
         compiler_params=pltpu.CompilerParams(vmem_limit_bytes=8 * 2**20 + 2 * bytes_in + 48 * total * slots),
-    )(*blocks, pltpu.with_memory_space_constraint(pages, pltpu.VMEM))
+    )(counts, found, *blocks, pltpu.with_memory_space_constraint(pages, pltpu.VMEM))
 
     landed = lax.all_to_all(asked, "store", split_axis=0, concat_axis=0, tiled=True)
     share = slots // groups
     terms = pl.pallas_call(
         functools.partial(spread_kernel, holders, groups),
         out_shape=[jax.ShapeDtypeStruct((share // 2, 2 * total), jnp.float32)] * groups,
-        in_specs=[SMEM] + [VMEM] * 2,
+        in_specs=[VMEM] * 2,
         out_specs=[VMEM] * groups,
         compiler_params=pltpu.CompilerParams(vmem_limit_bytes=4 * 2**20 + 64 * total * slots),
-    )(counts, found, landed)
+    )(used, landed)
     summed = terms[0]
     for step in range(1, groups):
         summed = summed + lax.ppermute(terms[step], "layer", [(g, (g + step) % groups) for g in range(groups)])

time: 34.8 us -> 33.4 us (0.960)
  blocking collectives: 0 us -> 7.86 us
  waiting for transfers between devices: 14 us -> 8.78 us
  starting transfers between devices: 14 us -> 10.6 us
  Pallas kernels: 5.23 us -> 4.63 us
    all_to_all x0 -> x1, blocking collectives: none -> 7.86 us  [on_device(): lax.all_to_all(asked, 'store', split_axis=0, concat_axis=0, tiled=True)]
    all_to_all x1 -> x0, waiting for transfers between devices: 4.3 us -> none  [on_device(): lax.all_to_all(asked, 'store', split_axis=0, concat_axis=0, tiled=True)]
    all_to_all x1 -> x0, starting transfers between devices: 3.35 us -> none  [on_device(): lax.all_to_all(asked, 'store', split_axis=0, concat_axis=0, tiled=True)]
    ppermute x7, waiting for transfers between devices: 7.33 us -> 6.4 us  [swap(): lax.ppermute(value, axis, [(i, i ^ distance) for i in range(lax.axis_size...]
    pallas_call x1, Pallas kernels: 2.36 us -> 1.75 us  [on_device(): pl.pallas_call(functools.partial(score_kernel, holders, capacity), out_sh...]
  transfers between devices with their start and end apart: 11 -> 10, of which waited for: 8 -> 7; matrix products, arithmetic and copies ran while one was open for 0% -> 0% of each run, Pallas kernels for 0% -> 0%
where the time goes in v15:
time: 33.4 us; the launch traced here: 33.2 us
  starting transfers between devices  10.6 us (32%)
  waiting for transfers between devices  8.78 us (26%)
  blocking collectives  7.86 us (24%)
  Pallas kernels  4.63 us (14%)
  between operations  0.7 us (2%)
  other arithmetic  0.63 us (2%)
    all_to_all x1, blocking collectives, on_device(): lax.all_to_all(asked, 'store', split_axis=0, concat_axis=0, tiled=True)  7.86 us
    ppermute x7, waiting for transfers between devices, swap(): lax.ppermute(value, axis, [(i, i ^ distance) for i in range(lax.axis_size...  6.4 us
    ppermute x3, starting transfers between devices, on_device(): lax.ppermute(terms[step], 'layer', [(g, (g + step) % groups) for g in ran...  5.69 us
    ppermute x7, starting transfers between devices, swap(): lax.ppermute(value, axis, [(i, i ^ distance) for i in range(lax.axis_size...  4.88 us
    pallas_call x1, Pallas kernels, on_device(): pl.pallas_call(functools.partial(condition_kernel, holders, capacity), ou...  2.43 us
    ppermute x3, waiting for transfers between devices, on_device(): lax.ppermute(terms[step], 'layer', [(g, (g + step) % groups) for g in ran...  2.38 us
    pallas_call x1, Pallas kernels, on_device(): pl.pallas_call(functools.partial(score_kernel, holders, capacity), out_sh...  1.75 us
  transfers between devices with their start and end apart: 10, of which 7 were waited for; matrix products, arithmetic and copies ran while one was open for 0% of the time, Pallas kernels for 0%

profile of v15, /device:TPU:0, one launch (start us, length us, event | category | flops | bytes accessed | tf_op | source)
XLA Modules:
  0.0 33.2 jit_solution(1371549681252654935)
XLA Ops:
  0.0 2.4 %shard_map.73 = (bf16[8,8320]{1,0:T(8,128)(2,1)S(1)}, bf16[256,8192]{1,0:T(8,128)(2,1)S(1)}, f32[8,256]{1,0:T(8,128)S(1)}) custom-call(bf16[8,8192]{1,0:T(8,128)(2,1)} %refs_0_.2, f32[2,64,64]{2,1,0:T(8,128)} %refs_1_.1, f32[2,64,64]{2,1,0:T(8,128)} %refs_2_.1, s32[16,128]{1,0:T(8,128)} %bitcast.3, s32[1,256]{1,0:T(1,128)} %refs_4_.1, bf16[256,8192]{1,0:T(8,128)(2,1)} %refs_5_.1), custom_call_target="tpu_custom_call" | custom-call | tf_op jit(solution)/shard_map/pallas_call | solution.py:221
  2.4 4.0 %collective-permute-start.5 = (bf16[8,8320]{1,0:T(8,128)(2,1)S(1)}, bf16[8,8320]{1,0:T(8,128)(2,1)S(1)}, u32[]{:S(2)}, u32[]{:S(2)}) collective-permute-start(bf16[8,8320]{1,0:T(8,128)(2,1)S(1)} %get-tuple-element.15.refs_2_), channel_id=1, source_target_pairs={{0,24},{4,28},{8,16},{12,20},{16,8},{20,12},{24,0},{28,4},{1,25},{... | collective-permute-start | bytes 399368 | tf_op jit(solution)/shard_map/ppermute | solution.py:202
  6.4 0.5 %collective-permute-start.3 = (bf16[8,8320]{1,0:T(8,128)(2,1)S(1)}, bf16[8,8320]{1,0:T(8,128)(2,1)S(1)}, u32[]{:S(2)}, u32[]{:S(2)}) collective-permute-start(bf16[8,8320]{1,0:T(8,128)(2,1)S(1)} %get-tuple-element.15.refs_2_), channel_id=1, source_target_pairs={{0,16},{4,20},{8,24},{12,28},{16,0},{20,4},{24,8},{28,12},{1,17},{... | collective-permute-start | bytes 399368 | tf_op jit(solution)/shard_map/ppermute | solution.py:202
  6.9 0.1 collective-permute-start.1
  7.0 0.0 collective-permute-start
  7.0 3.3 %collective-permute-done.5.refs_8_ = bf16[8,8320]{1,0:T(8,128)(2,1)S(1)} collective-permute-done((bf16[8,8320]{1,0:T(8,128)(2,1)S(1)}, bf16[8,8320]{1,0:T(8,128)(2,1)S(1)}, u32[]{:S(2)}, u32[]{:S(2)}) %collective-permute-start.5) | collective-permute-done | bytes 133152 | tf_op jit(solution)/shard_map/ppermute | solution.py:202
  10.3 0.0 collective-permute-start.6
  10.3 2.4 %collective-permute-done.3.refs_6_ = bf16[8,8320]{1,0:T(8,128)(2,1)S(1)} collective-permute-done((bf16[8,8320]{1,0:T(8,128)(2,1)S(1)}, bf16[8,8320]{1,0:T(8,128)(2,1)S(1)}, u32[]{:S(2)}, u32[]{:S(2)}) %collective-permute-start.3) | collective-permute-done | bytes 133152 | tf_op jit(solution)/shard_map/ppermute | solution.py:202
  12.8 0.0 collective-permute-start.4
  12.8 0.2 collective-permute-done.1.refs_4_
  13.0 0.3 collective-permute-start.2
  14.0 0.0 collective-permute-done.refs_3_
  14.0 0.0 collective-permute-done.6.refs_9_
  14.0 0.2 collective-permute-done.4.refs_7_
  14.1 0.2 collective-permute-done.2.refs_5_
  14.4 1.8 %shard_map.74 = (f32[8,16,128]{2,1,0:T(8,128)S(1)}, f32[8,256]{1,0:T(8,128)S(1)}) custom-call(s32[1]{0:T(128)S(6)} %copy.8.refs_0_, f32[8,256]{1,0:T(8,128)S(1)} %get-tuple-element.14.refs_1_, bf16[8,8320]{1,0:T(8,128)(2,1)S(1)} %get-tuple-element.15.refs_2_, bf16[8,8320]{1,0:T(8,128)(2,1)S(1)} %collective-permute-done.refs_3_, ...), custom_call_target="tpu_custom_call" | custom-call | tf_op jit(solution)/shard_map/pallas_call | solution.py:245
  16.1 7.9 %all_to_all.5.landed_ref = f32[8,16,128]{2,1,0:T(8,128)S(1)} all-to-all(f32[8,16,128]{2,1,0:T(8,128)S(1)} %get-tuple-element.18), channel_id=1, replica_groups=mesh['store'=8,'layer'=4] {'store'}, dimensions={0} | all-to-all | bytes 131072 | tf_op jit(solution)/shard_map/all_to_all | solution.py:257
  24.0 0.5 %shard_map.75 = (f32[32,128]{1,0:T(8,128)S(1)}, f32[32,128]{1,0:T(8,128)S(1)}, f32[32,128]{1,0:T(8,128)S(1)}, f32[32,128]{1,0:T(8,128)S(1)}) custom-call(f32[8,256]{1,0:T(8,128)S(1)} %get-tuple-element.17.found_ref, f32[8,16,128]{2,1,0:T(8,128)S(1)} %all_to_all.5.landed_ref), custom_call_target="tpu_custom_call" | custom-call | tf_op jit(solution)/shard_map/pallas_call | solution.py:259
  24.5 1.7 %collective-permute-start.7 = (f32[32,128]{1,0:T(8,128)S(1)}, f32[32,128]{1,0:T(8,128)S(1)}, u32[]{:S(2)}, u32[]{:S(2)}) collective-permute-start(f32[32,128]{1,0:T(8,128)S(1)} %get-tuple-element.20), channel_id=1, source_target_pairs={{0,1},{1,2},{2,3},{3,0},{4,5},{5,6},{6,7},{7,4},{8,9},{9,10},{10,1... | collective-permute-start | bytes 49160 | tf_op jit(solution)/shard_map/ppermute | solution.py:268
  26.2 2.6 %collective-permute-start.8 = (f32[32,128]{1,0:T(8,128)S(1)}, f32[32,128]{1,0:T(8,128)S(1)}, u32[]{:S(2)}, u32[]{:S(2)}) collective-permute-start(f32[32,128]{1,0:T(8,128)S(1)} %get-tuple-element.21), channel_id=1, source_target_pairs={{0,2},{1,3},{2,0},{3,1},{4,6},{5,7},{6,4},{7,5},{8,10},{9,11},{10,... | collective-permute-start | bytes 49160 | tf_op jit(solution)/shard_map/ppermute | solution.py:268
  28.8 1.4 %collective-permute-start.9 = (f32[32,128]{1,0:T(8,128)S(1)}, f32[32,128]{1,0:T(8,128)S(1)}, u32[]{:S(2)}, u32[]{:S(2)}) collective-permute-start(f32[32,128]{1,0:T(8,128)S(1)} %get-tuple-element.22), channel_id=1, source_target_pairs={{0,3},{1,0},{2,1},{3,2},{4,7},{5,4},{6,5},{7,6},{8,11},{9,8},{10,9... | collective-permute-start | bytes 49160 | tf_op jit(solution)/shard_map/ppermute | solution.py:268
  30.1 0.0 collective-permute-done.7
  30.2 0.7 %collective-permute-done.8 = f32[32,128]{1,0:T(8,128)S(1)} collective-permute-done((f32[32,128]{1,0:T(8,128)S(1)}, f32[32,128]{1,0:T(8,128)S(1)}, u32[]{:S(2)}, u32[]{:S(2)}) %collective-permute-start.8) | collective-permute-done | bytes 16416 | tf_op jit(solution)/shard_map/ppermute | solution.py:268
  30.8 1.7 %collective-permute-done.9 = f32[32,128]{1,0:T(8,128)S(1)} collective-permute-done((f32[32,128]{1,0:T(8,128)S(1)}, f32[32,128]{1,0:T(8,128)S(1)}, u32[]{:S(2)}, u32[]{:S(2)}) %collective-permute-start.9) | collective-permute-done | bytes 16416 | tf_op jit(solution)/shard_map/ppermute | solution.py:268
  32.5 0.1 fusion
  32.6 0.6 %maximum_bitcast_fusion = f32[1,64,64]{2,1,0:T(8,128)} fusion(f32[32,64]{1,0:T(8,128)S(1)} %get-tuple-element.24, f32[32,64]{1,0:T(8,128)S(1)} %get-tuple-element.23), kind=kLoop, calls=%fused_computation | loop fusion | flops 4096 | bytes 32768 | tf_op jit(solution)/shard_map/broadcast_in_dim | solution.py:269
  (1 shorter events, 0.0 us)
Async XLA Ops:
  2.4 7.9 %collective-permute-start.5 = (bf16[8,8320]{1,0:T(8,128)(2,1)S(1)}, bf16[8,8320]{1,0:T(8,128)(2,1)S(1)}, u32[]{:S(2)}, u32[]{:S(2)}) collective-permute-start(bf16[8,8320]{1,0:T(8,128)(2,1)S(1)} %get-tuple-element.15.refs_2_), channel_id=1, source_target_pairs={{0,24},{4,28},{8,16},{12,20},{16,8},{20,12},{24,0},{28,4},{1,25},{... | collective-permute-start | bytes 399368 | tf_op jit(solution)/shard_map/ppermute | solution.py:202
  6.4 6.4 %collective-permute-start.3 = (bf16[8,8320]{1,0:T(8,128)(2,1)S(1)}, bf16[8,8320]{1,0:T(8,128)(2,1)S(1)}, u32[]{:S(2)}, u32[]{:S(2)}) collective-permute-start(bf16[8,8320]{1,0:T(8,128)(2,1)S(1)} %get-tuple-element.15.refs_2_), channel_id=1, source_target_pairs={{0,16},{4,20},{8,24},{12,28},{16,0},{20,4},{24,8},{28,12},{1,17},{... | collective-permute-start | bytes 399368 | tf_op jit(solution)/shard_map/ppermute | solution.py:202
  6.9 6.1 %collective-permute-start.1 = (bf16[8,8320]{1,0:T(8,128)(2,1)S(1)}, bf16[8,8320]{1,0:T(8,128)(2,1)S(1)}, u32[]{:S(2)}, u32[]{:S(2)}) collective-permute-start(bf16[8,8320]{1,0:T(8,128)(2,1)S(1)} %get-tuple-element.15.refs_2_), channel_id=1, source_target_pairs={{0,8},{4,12},{8,0},{12,4},{16,24},{20,28},{24,16},{28,20},{1,9},{5... | collective-permute-start | bytes 399368 | tf_op jit(solution)/shard_map/ppermute | solution.py:202
  7.0 6.9 %collective-permute-start = (bf16[8,8320]{1,0:T(8,128)(2,1)S(1)}, bf16[8,8320]{1,0:T(8,128)(2,1)S(1)}, u32[]{:S(2)}, u32[]{:S(2)}) collective-permute-start(bf16[8,8320]{1,0:T(8,128)(2,1)S(1)} %get-tuple-element.15.refs_2_), channel_id=1, source_target_pairs={{0,4},{4,0},{8,12},{12,8},{16,20},{20,16},{24,28},{28,24},{1,5},{5... | collective-permute-start | bytes 399368 | tf_op jit(solution)/shard_map/ppermute | solution.py:202
  10.3 3.6 %collective-permute-start.6 = (bf16[8,8320]{1,0:T(8,128)(2,1)S(1)}, bf16[8,8320]{1,0:T(8,128)(2,1)S(1)}, u32[]{:S(2)}, u32[]{:S(2)}) collective-permute-start(bf16[8,8320]{1,0:T(8,128)(2,1)S(1)} %collective-permute-done.5.refs_8_), channel_id=1, source_target_pairs={{0,4},{4,0},{8,12},{12,8},{16,20},{20,16},{24,28},{28,24},{1,5},{5... | collective-permute-start | bytes 399368 | tf_op jit(solution)/shard_map/ppermute | solution.py:202
  12.8 1.4 %collective-permute-start.4 = (bf16[8,8320]{1,0:T(8,128)(2,1)S(1)}, bf16[8,8320]{1,0:T(8,128)(2,1)S(1)}, u32[]{:S(2)}, u32[]{:S(2)}) collective-permute-start(bf16[8,8320]{1,0:T(8,128)(2,1)S(1)} %collective-permute-done.3.refs_6_), channel_id=1, source_target_pairs={{0,4},{4,0},{8,12},{12,8},{16,20},{20,16},{24,28},{28,24},{1,5},{5... | collective-permute-start | bytes 399368 | tf_op jit(solution)/shard_map/ppermute | solution.py:202
  13.0 1.4 %collective-permute-start.2 = (bf16[8,8320]{1,0:T(8,128)(2,1)S(1)}, bf16[8,8320]{1,0:T(8,128)(2,1)S(1)}, u32[]{:S(2)}, u32[]{:S(2)}) collective-permute-start(bf16[8,8320]{1,0:T(8,128)(2,1)S(1)} %collective-permute-done.1.refs_4_), channel_id=1, source_target_pairs={{0,4},{4,0},{8,12},{12,8},{16,20},{20,16},{24,28},{28,24},{1,5},{5... | collective-permute-start | bytes 399368 | tf_op jit(solution)/shard_map/ppermute | solution.py:202
  24.5 5.7 %collective-permute-start.7 = (f32[32,128]{1,0:T(8,128)S(1)}, f32[32,128]{1,0:T(8,128)S(1)}, u32[]{:S(2)}, u32[]{:S(2)}) collective-permute-start(f32[32,128]{1,0:T(8,128)S(1)} %get-tuple-element.20), channel_id=1, source_target_pairs={{0,1},{1,2},{2,3},{3,0},{4,5},{5,6},{6,7},{7,4},{8,9},{9,10},{10,1... | collective-permute-start | bytes 49160 | tf_op jit(solution)/shard_map/ppermute | solution.py:268
  26.2 4.6 %collective-permute-start.8 = (f32[32,128]{1,0:T(8,128)S(1)}, f32[32,128]{1,0:T(8,128)S(1)}, u32[]{:S(2)}, u32[]{:S(2)}) collective-permute-start(f32[32,128]{1,0:T(8,128)S(1)} %get-tuple-element.21), channel_id=1, source_target_pairs={{0,2},{1,3},{2,0},{3,1},{4,6},{5,7},{6,4},{7,5},{8,10},{9,11},{10,... | collective-permute-start | bytes 49160 | tf_op jit(solution)/shard_map/ppermute | solution.py:268
  28.8 3.7 %collective-permute-start.9 = (f32[32,128]{1,0:T(8,128)S(1)}, f32[32,128]{1,0:T(8,128)S(1)}, u32[]{:S(2)}, u32[]{:S(2)}) collective-permute-start(f32[32,128]{1,0:T(8,128)S(1)} %get-tuple-element.22), channel_id=1, source_target_pairs={{0,3},{1,0},{2,1},{3,2},{4,7},{5,4},{6,5},{7,6},{8,11},{9,8},{10,9... | collective-permute-start | bytes 49160 | tf_op jit(solution)/shard_map/ppermute | solution.py:268

commit v16 on v15

--- a/solution.py
+++ b/solution.py
@@ -11,7 +11,7 @@
 SMEM = pl.BlockSpec(memory_space=pltpu.SMEM)
 HBM = pl.BlockSpec(memory_space=pltpu.HBM)
 LANES = 128
-CHUNKS = 4
+CHUNKS = 2
 
 
 def iota(shape, dimension):
@@ -32,7 +32,9 @@
 
 
 def condition_kernel(holders, capacity, *refs):
-    sources, packed_ref, pages_ref, found_ref, landing, arrived, turned_ref = refs[:6], *refs[6:9], refs[9:14], *refs[14:]
+    sources, packed_refs, pages_ref, found_ref, landing, arrived, turned_ref = (
+        refs[:6], refs[6:8], *refs[8:10], refs[10:15], *refs[15:]
+    )
     copies = [
         pltpu.make_async_copy(source, target, arrived.at[i])
         for i, (source, target) in enumerate(zip(sources, landing + (pages_ref,)))
@@ -95,9 +97,8 @@
             done = jnp.where(low, ee, oo) + pltpu.roll(jnp.where(low, oe, eo), rank, 1)
             turned_ref[layer, pl.ds(q, half, stride=rows), :] = done
         for t in range(half):
-            packed_ref[:, (first + t) * LANES:(first + t + 1) * LANES] = (
-                turned_ref[layer, t * rows:(t + 1) * rows, :].astype(jnp.bfloat16)
-            )
+            packed_ref, column = packed_refs[2 * layer // layers], (first + t) * LANES % (width // 2)
+            packed_ref[:, column:column + LANES] = turned_ref[layer, t * rows:(t + 1) * rows, :].astype(jnp.bfloat16)
 
     slots = cand_ref.shape[1]
     home_rows = home_ref.shape[0]
@@ -119,30 +120,44 @@
         preferred_element_type=jnp.float32,
     )
     blocks = [asked[h:h + rows] for h in range(0, holders, rows)]
-    spare = packed_ref.shape[1] - width - capacity * len(blocks)
+    spare = packed_refs[1].shape[1] - width // 2 - capacity * len(blocks)
     if spare:
         blocks.append(jnp.zeros((rows, spare), jnp.float32))
-    packed_ref[:, width:] = jnp.concatenate(blocks, axis=1).astype(jnp.bfloat16)
+    packed_refs[1][:, width // 2:] = jnp.concatenate(blocks, axis=1).astype(jnp.bfloat16)
     found_ref[...] = jnp.concatenate([holder, rank_there, jnp.zeros((6, slots), jnp.float32)], axis=0)
     copies[-1].wait()
 
 
+def scores_of(packed_refs, pages_ref, queries, first):
+    width = queries.shape[1]
+    rows = packed_refs[0].shape[0]
+    scores = jnp.zeros((queries.shape[0], pages_ref.shape[0]), jnp.float32)
+    step = width // CHUNKS
+    for i in range(CHUNKS):
+        columns = slice(i * step, (i + 1) * step)
+        for k, ref in enumerate(packed_refs):
+            queries[k * rows:(k + 1) * rows, columns] = ref[:, columns]
+        scores = scores + lax.dot_general(
+            queries[:, columns], pages_ref[:, first + i * step:first + (i + 1) * step], (((1,), (1,)), ((), ())),
+            preferred_element_type=jnp.float32,
+        )
+    return scores
+
+
+def first_kernel(holders, *refs):
+    packed_refs, pages_ref, scores_ref, queries = refs[:holders], *refs[holders:]
+    scores_ref[...] = scores_of(packed_refs, pages_ref, queries, 0)
+
+
 def score_kernel(holders, capacity, *refs):
-    count_ref, found_ref, packed_refs = *refs[:2], refs[2:2 + holders]
-    pages_ref, out_ref, used_ref, total, queries = refs[2 + holders:]
+    count_ref, found_ref, begun_ref, packed_refs = *refs[:3], refs[3:3 + holders]
+    pages_ref, out_ref, used_ref, total, queries = refs[3 + holders:]
     me = lax.axis_index("store")
-    count, width = pages_ref.shape
+    count = pages_ref.shape[0]
+    width = queries.shape[1]
     rows = packed_refs[0].shape[0]
     half = capacity // 2
-    step = width // CHUNKS
-    scores = jnp.zeros((holders * rows, count), jnp.float32)
-    for i in range(CHUNKS):
-        columns = slice(i * step, (i + 1) * step)
-        for k in range(holders):
-            queries[k * rows:(k + 1) * rows, columns] = packed_refs[k][:, columns]
-        scores = scores + lax.dot_general(
-            queries[:, columns], pages_ref[:, columns], (((1,), (1,)), ((), ())), preferred_element_type=jnp.float32
-        )
+    scores = begun_ref[...] + scores_of(packed_refs, pages_ref, queries, width)
     for k in range(holders):
         start = pl.multiple_of((me ^ k) * rows, rows)
         total[pl.ds(start, rows), :] = scores[k * rows:(k + 1) * rows]
@@ -218,41 +233,56 @@
         for source in (query_grads, factor_in, factor_out, home, cand_lists, page_store)
     ]
     notes = max(LANES, holders // rows * capacity)
-    packed, pages, found = pl.pallas_call(
+    *packed, pages, found = pl.pallas_call(
         functools.partial(condition_kernel, holders, capacity),
         out_shape=[
-            jax.ShapeDtypeStruct((rows, width + notes), bf16),
+            jax.ShapeDtypeStruct((rows, width // 2), bf16),
+            jax.ShapeDtypeStruct((rows, width // 2 + notes), bf16),
             pltpu.VMEM(page_store.shape, bf16),
             jax.ShapeDtypeStruct((8, slots), jnp.float32),
         ],
         in_specs=[HBM] * len(sources),
-        out_specs=[VMEM] * 3,
+        out_specs=[VMEM] * 4,
         scratch_shapes=[pltpu.VMEM(source.shape, source.dtype) for source in sources[:-1]]
         + [pltpu.SemaphoreType.DMA((len(sources),)), pltpu.VMEM((layers, rows * rank // 2, LANES), jnp.float32)],
         compiler_params=pltpu.CompilerParams(vmem_limit_bytes=10 * 2**20 + 24 * slots * slots),
     )(*sources)
 
-    blocks = [None] * holders
-    blocks[0] = packed
-    for k in reversed(range(2, holders, 2)):
-        blocks[k] = swap(packed, "store", k)
-    blocks[1] = swap(packed, "store", 1)
-    for k in reversed(range(2, holders, 2)):
-        blocks[k + 1] = swap(blocks[k], "store", 1)
+    across = list(reversed(range(2, holders, 2)))
+    blocks = [[part] + [None] * (holders - 1) for part in packed]
+    for part in range(2):
+        for k in across:
+            blocks[part][k] = swap(packed[part], "store", k)
+    for part in range(2):
+        blocks[part][1] = swap(packed[part], "store", 1)
+        for k in across:
+            blocks[part][k + 1] = swap(blocks[part][k], "store", 1)
 
     total = holders * rows
     bytes_in = 2 * holders * rows * (width + notes) + 2 * per_holder * width
+    pages = pltpu.with_memory_space_constraint(pages, pltpu.VMEM)
+    begun = pl.pallas_call(
+        functools.partial(first_kernel, holders),
+        out_shape=jax.ShapeDtypeStruct((total, per_holder), jnp.float32),
+        in_specs=[VMEM] * (holders + 1),
+        out_specs=VMEM,
+        scratch_shapes=[pltpu.VMEM((total, width // 2), bf16)],
+        compiler_params=pltpu.CompilerParams(vmem_limit_bytes=8 * 2**20 + 2 * bytes_in),
+        cost_estimate=pl.CostEstimate(
+            flops=total * per_holder * width, bytes_accessed=per_holder * width, transcendentals=0
+        ),
+    )(*blocks[0], pages)
     asked, used = pl.pallas_call(
         functools.partial(score_kernel, holders, capacity),
         out_shape=[
             jax.ShapeDtypeStruct((holders, capacity // 2, 2 * total), jnp.float32),
             jax.ShapeDtypeStruct(found.shape, jnp.float32),
         ],
-        in_specs=[SMEM] + [VMEM] * (holders + 2),
+        in_specs=[SMEM] + [VMEM] * (holders + 3),
         out_specs=[VMEM] * 2,
-        scratch_shapes=[pltpu.VMEM((total, per_holder), jnp.float32), pltpu.VMEM((total, width), bf16)],
+        scratch_shapes=[pltpu.VMEM((total, per_holder), jnp.float32), pltpu.VMEM((total, width // 2), bf16)],
         compiler_params=pltpu.CompilerParams(vmem_limit_bytes=8 * 2**20 + 2 * bytes_in + 48 * total * slots),
-    )(counts, found, *blocks, pltpu.with_memory_space_constraint(pages, pltpu.VMEM))
+    )(counts, found, begun, *blocks[1], pages)
 
     landed = lax.all_to_all(asked, "store", split_axis=0, concat_axis=0, tiled=True)
     share = slots // groups

time: 33.4 us -> 35.4 us (1.060)
  starting transfers between devices: 10.6 us -> 16.7 us
  waiting for transfers between devices: 8.78 us -> 4.78 us
    ppermute x7 -> x14, starting transfers between devices: 4.88 us -> 11.1 us  [swap(): lax.ppermute(value, axis, [(i, i ^ distance) for i in range(lax.axis_size...]
    ppermute x7 -> x14, waiting for transfers between devices: 6.4 us -> 2.38 us  [swap(): lax.ppermute(value, axis, [(i, i ^ distance) for i in range(lax.axis_size...]
    pallas_call x0 -> x1, Pallas kernels: none -> 0.76 us  [on_device(): pl.pallas_call(functools.partial(first_kernel, holders), out_shape=jax.Sh...]
    pallas_call x1, Pallas kernels: 1.75 us -> 1.12 us  [on_device(): pl.pallas_call(functools.partial(score_kernel, holders, capacity), out_sh...]
  transfers between devices with their start and end apart: 10 -> 17, of which waited for: 7 -> 6; matrix products, arithmetic and copies ran while one was open for 0% -> 0% of each run, Pallas kernels for 0% -> 2%
where the time goes in v16:
time: 35.4 us; the launch traced here: 35.2 us
  starting transfers between devices  16.7 us (47%)
  blocking collectives  7.61 us (21%)
  waiting for transfers between devices  4.78 us (14%)
  Pallas kernels  4.75 us (13%)
  between operations  0.73 us (2%)
  other arithmetic  0.63 us (2%)
    ppermute x14, starting transfers between devices, swap(): lax.ppermute(value, axis, [(i, i ^ distance) for i in range(lax.axis_size...  11.1 us
    all_to_all x1, blocking collectives, on_device(): lax.all_to_all(asked, 'store', split_axis=0, concat_axis=0, tiled=True)  7.61 us
    ppermute x3, starting transfers between devices, on_device(): lax.ppermute(terms[step], 'layer', [(g, (g + step) % groups) for g in ran...  5.57 us
    pallas_call x1, Pallas kernels, on_device(): pl.pallas_call(functools.partial(condition_kernel, holders, capacity), ou...  2.43 us
    ppermute x3, waiting for transfers between devices, on_device(): lax.ppermute(terms[step], 'layer', [(g, (g + step) % groups) for g in ran...  2.39 us
    ppermute x14, waiting for transfers between devices, swap(): lax.ppermute(value, axis, [(i, i ^ distance) for i in range(lax.axis_size...  2.38 us
    pallas_call x1, Pallas kernels, on_device(): pl.pallas_call(functools.partial(score_kernel, holders, capacity), out_sh...  1.12 us
    pallas_call x1, Pallas kernels, on_device(): pl.pallas_call(functools.partial(first_kernel, holders), out_shape=jax.Sh...  0.76 us
  transfers between devices with their start and end apart: 17, of which 6 were waited for; matrix products, arithmetic and copies ran while one was open for 0% of the time, Pallas kernels for 2%

profile of v16, /device:TPU:0, one launch (start us, length us, event | category | flops | bytes accessed | tf_op | source)
XLA Modules:
  0.0 35.2 jit_solution(11387633693067797365)
XLA Ops:
  0.0 2.4 %shard_map.73 = (bf16[8,4096]{1,0:T(8,128)(2,1)S(1)}, bf16[8,4224]{1,0:T(8,128)(2,1)S(1)}, bf16[256,8192]{1,0:T(8,128)(2,1)S(1)}, f32[8,256]{1,0:T(8,128)S(1)}) custom-call(bf16[8,8192]{1,0:T(8,128)(2,1)} %refs_0_.2, f32[2,64,64]{2,1,0:T(8,128)} %refs_1_.1, f32[2,64,64]{2,1,0:T(8,128)} %refs_2_.1, s32[16,128]{1,0:T(8,128)} %bitcast.3, s32[1,256]{1,0:T(1,128)} %refs_4_.1, ...), custom_call_target="tpu_custom_call" | custom-call | tf_op jit(solution)/shard_map/pallas_call | solution.py:236
  2.4 4.0 %collective-permute-start.5 = (bf16[8,4096]{1,0:T(8,128)(2,1)S(1)}, bf16[8,4096]{1,0:T(8,128)(2,1)S(1)}, u32[]{:S(2)}, u32[]{:S(2)}) collective-permute-start(bf16[8,4096]{1,0:T(8,128)(2,1)S(1)} %get-tuple-element.16.refs_0_), channel_id=1, source_target_pairs={{0,24},{4,28},{8,16},{12,20},{16,8},{20,12},{24,0},{28,4},{1,25},{... | collective-permute-start | bytes 196616 | tf_op jit(solution)/shard_map/ppermute | solution.py:217
  6.4 0.5 %collective-permute-start.3 = (bf16[8,4096]{1,0:T(8,128)(2,1)S(1)}, bf16[8,4096]{1,0:T(8,128)(2,1)S(1)}, u32[]{:S(2)}, u32[]{:S(2)}) collective-permute-start(bf16[8,4096]{1,0:T(8,128)(2,1)S(1)} %get-tuple-element.16.refs_0_), channel_id=1, source_target_pairs={{0,16},{4,20},{8,24},{12,28},{16,0},{20,4},{24,8},{28,12},{1,17},{... | collective-permute-start | bytes 196616 | tf_op jit(solution)/shard_map/ppermute | solution.py:217
  6.9 0.1 collective-permute-start.1
  7.0 0.0 collective-permute-start
  7.0 2.8 %collective-permute-start.12 = (bf16[8,4224]{1,0:T(8,128)(2,1)S(1)}, bf16[8,4224]{1,0:T(8,128)(2,1)S(1)}, u32[]{:S(2)}, u32[]{:S(2)}) collective-permute-start(bf16[8,4224]{1,0:T(8,128)(2,1)S(1)} %get-tuple-element.18.refs_3_), channel_id=1, source_target_pairs={{0,24},{4,28},{8,16},{12,20},{16,8},{20,12},{24,0},{28,4},{1,25},{... | collective-permute-start | bytes 202760 | tf_op jit(solution)/shard_map/ppermute | solution.py:217
  9.9 0.0 collective-permute-done.5.refs_6_
  9.9 1.1 %collective-permute-start.10 = (bf16[8,4224]{1,0:T(8,128)(2,1)S(1)}, bf16[8,4224]{1,0:T(8,128)(2,1)S(1)}, u32[]{:S(2)}, u32[]{:S(2)}) collective-permute-start(bf16[8,4224]{1,0:T(8,128)(2,1)S(1)} %get-tuple-element.18.refs_3_), channel_id=1, source_target_pairs={{0,16},{4,20},{8,24},{12,28},{16,0},{20,4},{24,8},{28,12},{1,17},{... | collective-permute-start | bytes 202760 | tf_op jit(solution)/shard_map/ppermute | solution.py:217
  11.0 0.0 collective-permute-done.3.refs_4_
  11.0 1.4 %collective-permute-start.8 = (bf16[8,4224]{1,0:T(8,128)(2,1)S(1)}, bf16[8,4224]{1,0:T(8,128)(2,1)S(1)}, u32[]{:S(2)}, u32[]{:S(2)}) collective-permute-start(bf16[8,4224]{1,0:T(8,128)(2,1)S(1)} %get-tuple-element.18.refs_3_), channel_id=1, source_target_pairs={{0,8},{4,12},{8,0},{12,4},{16,24},{20,28},{24,16},{28,20},{1,9},{5... | collective-permute-start | bytes 202760 | tf_op jit(solution)/shard_map/ppermute | solution.py:217
  12.4 0.0 collective-permute-done.1.refs_2_
  12.4 0.0 collective-permute-start.6
  12.4 0.0 collective-permute-done.refs_1_
  12.4 0.5 %collective-permute-start.4 = (bf16[8,4096]{1,0:T(8,128)(2,1)S(1)}, bf16[8,4096]{1,0:T(8,128)(2,1)S(1)}, u32[]{:S(2)}, u32[]{:S(2)}) collective-permute-start(bf16[8,4096]{1,0:T(8,128)(2,1)S(1)} %collective-permute-done.3.refs_4_), channel_id=1, source_target_pairs={{0,4},{4,0},{8,12},{12,8},{16,20},{20,16},{24,28},{28,24},{1,5},{5... | collective-permute-start | bytes 196616 | tf_op jit(solution)/shard_map/ppermute | solution.py:217
  12.9 0.6 %collective-permute-done.12.refs_9_ = bf16[8,4224]{1,0:T(8,128)(2,1)S(1)} collective-permute-done((bf16[8,4224]{1,0:T(8,128)(2,1)S(1)}, bf16[8,4224]{1,0:T(8,128)(2,1)S(1)}, u32[]{:S(2)}, u32[]{:S(2)}) %collective-permute-start.12) | collective-permute-done | bytes 67616 | tf_op jit(solution)/shard_map/ppermute | solution.py:217
  13.5 0.0 collective-permute-start.2
  13.5 1.4 %collective-permute-done.10.refs_7_ = bf16[8,4224]{1,0:T(8,128)(2,1)S(1)} collective-permute-done((bf16[8,4224]{1,0:T(8,128)(2,1)S(1)}, bf16[8,4224]{1,0:T(8,128)(2,1)S(1)}, u32[]{:S(2)}, u32[]{:S(2)}) %collective-permute-start.10) | collective-permute-done | bytes 67616 | tf_op jit(solution)/shard_map/ppermute | solution.py:217
  14.8 0.0 collective-permute-start.7
  14.9 0.4 %collective-permute-done.8.refs_5_ = bf16[8,4224]{1,0:T(8,128)(2,1)S(1)} collective-permute-done((bf16[8,4224]{1,0:T(8,128)(2,1)S(1)}, bf16[8,4224]{1,0:T(8,128)(2,1)S(1)}, u32[]{:S(2)}, u32[]{:S(2)}) %collective-permute-start.8) | collective-permute-done | bytes 67616 | tf_op jit(solution)/shard_map/ppermute | solution.py:217
  15.3 0.0 collective-permute-start.13
  15.4 0.0 collective-permute-done.6.refs_7_
  15.4 0.5 %collective-permute-start.11 = (bf16[8,4224]{1,0:T(8,128)(2,1)S(1)}, bf16[8,4224]{1,0:T(8,128)(2,1)S(1)}, u32[]{:S(2)}, u32[]{:S(2)}) collective-permute-start(bf16[8,4224]{1,0:T(8,128)(2,1)S(1)} %collective-permute-done.10.refs_7_), channel_id=1, source_target_pairs={{0,4},{4,0},{8,12},{12,8},{16,20},{20,16},{24,28},{28,24},{1,5},{5... | collective-permute-start | bytes 202760 | tf_op jit(solution)/shard_map/ppermute | solution.py:217
  15.8 0.0 collective-permute-done.4.refs_5_
  15.8 0.1 collective-permute-start.9
  16.6 0.0 collective-permute-done.2.refs_3_
  16.6 0.8 %shard_map.74.refs_2_ = f32[64,256]{1,0:T(8,128)S(1)} custom-call(bf16[8,4096]{1,0:T(8,128)(2,1)S(1)} %get-tuple-element.16.refs_0_, bf16[8,4096]{1,0:T(8,128)(2,1)S(1)} %collective-permute-done.refs_1_, bf16[8,4096]{1,0:T(8,128)(2,1)S(1)} %collective-permute-done.1.refs_2_, bf16[8,4096]{1,0:T(8,128)(2,1)S(1)} %collective-permute-done.2.refs_3_, ...), custom_call_target="tpu_custom_call" | custom-call | flops 134217728 | bytes 2097152 | tf_op jit(solution)/shard_map/pallas_call | solution.py:264
  17.3 0.0 collective-permute-done.7.refs_4_
  17.3 0.0 collective-permute-done.13.refs_10_
  17.4 0.0 collective-permute-done.11.refs_8_
  17.4 0.0 collective-permute-done.9.refs_6_
  17.4 1.1 %shard_map.75 = (f32[8,16,128]{2,1,0:T(8,128)S(1)}, f32[8,256]{1,0:T(8,128)S(1)}) custom-call(s32[1]{0:T(128)S(6)} %copy.8.refs_0_, f32[8,256]{1,0:T(8,128)S(1)} %get-tuple-element.15.refs_1_, f32[64,256]{1,0:T(8,128)S(1)} %shard_map.74.refs_2_, bf16[8,4224]{1,0:T(8,128)(2,1)S(1)} %get-tuple-element.18.refs_3_, ...), custom_call_target="tpu_custom_call" | custom-call | tf_op jit(solution)/shard_map/pallas_call | solution.py:275
  18.5 7.6 %all_to_all.5.landed_ref = f32[8,16,128]{2,1,0:T(8,128)S(1)} all-to-all(f32[8,16,128]{2,1,0:T(8,128)S(1)} %get-tuple-element.20), channel_id=1, replica_groups=mesh['store'=8,'layer'=4] {'store'}, dimensions={0} | all-to-all | bytes 131072 | tf_op jit(solution)/shard_map/all_to_all | solution.py:287
  26.1 0.4 %shard_map.76 = (f32[32,128]{1,0:T(8,128)S(1)}, f32[32,128]{1,0:T(8,128)S(1)}, f32[32,128]{1,0:T(8,128)S(1)}, f32[32,128]{1,0:T(8,128)S(1)}) custom-call(f32[8,256]{1,0:T(8,128)S(1)} %get-tuple-element.19.found_ref, f32[8,16,128]{2,1,0:T(8,128)S(1)} %all_to_all.5.landed_ref), custom_call_target="tpu_custom_call" | custom-call | tf_op jit(solution)/shard_map/pallas_call | solution.py:289
  26.6 1.6 %collective-permute-start.14 = (f32[32,128]{1,0:T(8,128)S(1)}, f32[32,128]{1,0:T(8,128)S(1)}, u32[]{:S(2)}, u32[]{:S(2)}) collective-permute-start(f32[32,128]{1,0:T(8,128)S(1)} %get-tuple-element.22), channel_id=1, source_target_pairs={{0,1},{1,2},{2,3},{3,0},{4,5},{5,6},{6,7},{7,4},{8,9},{9,10},{10,1... | collective-permute-start | bytes 49160 | tf_op jit(solution)/shard_map/ppermute | solution.py:298
  28.2 2.6 %collective-permute-start.15 = (f32[32,128]{1,0:T(8,128)S(1)}, f32[32,128]{1,0:T(8,128)S(1)}, u32[]{:S(2)}, u32[]{:S(2)}) collective-permute-start(f32[32,128]{1,0:T(8,128)S(1)} %get-tuple-element.23), channel_id=1, source_target_pairs={{0,2},{1,3},{2,0},{3,1},{4,6},{5,7},{6,4},{7,5},{8,10},{9,11},{10,... | collective-permute-start | bytes 49160 | tf_op jit(solution)/shard_map/ppermute | solution.py:298
  30.8 1.3 %collective-permute-start.16 = (f32[32,128]{1,0:T(8,128)S(1)}, f32[32,128]{1,0:T(8,128)S(1)}, u32[]{:S(2)}, u32[]{:S(2)}) collective-permute-start(f32[32,128]{1,0:T(8,128)S(1)} %get-tuple-element.24), channel_id=1, source_target_pairs={{0,3},{1,0},{2,1},{3,2},{4,7},{5,4},{6,5},{7,6},{8,11},{9,8},{10,9... | collective-permute-start | bytes 49160 | tf_op jit(solution)/shard_map/ppermute | solution.py:298
  32.1 0.1 collective-permute-done.14
  32.2 0.6 %collective-permute-done.15 = f32[32,128]{1,0:T(8,128)S(1)} collective-permute-done((f32[32,128]{1,0:T(8,128)S(1)}, f32[32,128]{1,0:T(8,128)S(1)}, u32[]{:S(2)}, u32[]{:S(2)}) %collective-permute-start.15) | collective-permute-done | bytes 16416 | tf_op jit(solution)/shard_map/ppermute | solution.py:298
  32.8 1.7 %collective-permute-done.16 = f32[32,128]{1,0:T(8,128)S(1)} collective-permute-done((f32[32,128]{1,0:T(8,128)S(1)}, f32[32,128]{1,0:T(8,128)S(1)}, u32[]{:S(2)}, u32[]{:S(2)}) %collective-permute-start.16) | collective-permute-done | bytes 16416 | tf_op jit(solution)/shard_map/ppermute | solution.py:298
  34.5 0.1 fusion
  34.6 0.6 %maximum_bitcast_fusion = f32[1,64,64]{2,1,0:T(8,128)} fusion(f32[32,64]{1,0:T(8,128)S(1)} %get-tuple-element.26, f32[32,64]{1,0:T(8,128)S(1)} %get-tuple-element.25), kind=kLoop, calls=%fused_computation | loop fusion | flops 4096 | bytes 32768 | tf_op jit(solution)/shard_map/broadcast_in_dim | solution.py:299
  (1 shorter events, 0.0 us)
Async XLA Ops:
  2.4 7.5 %collective-permute-start.5 = (bf16[8,4096]{1,0:T(8,128)(2,1)S(1)}, bf16[8,4096]{1,0:T(8,128)(2,1)S(1)}, u32[]{:S(2)}, u32[]{:S(2)}) collective-permute-start(bf16[8,4096]{1,0:T(8,128)(2,1)S(1)} %get-tuple-element.16.refs_0_), channel_id=1, source_target_pairs={{0,24},{4,28},{8,16},{12,20},{16,8},{20,12},{24,0},{28,4},{1,25},{... | collective-permute-start | bytes 196616 | tf_op jit(solution)/shard_map/ppermute | solution.py:217
  6.4 4.6 %collective-permute-start.3 = (bf16[8,4096]{1,0:T(8,128)(2,1)S(1)}, bf16[8,4096]{1,0:T(8,128)(2,1)S(1)}, u32[]{:S(2)}, u32[]{:S(2)}) collective-permute-start(bf16[8,4096]{1,0:T(8,128)(2,1)S(1)} %get-tuple-element.16.refs_0_), channel_id=1, source_target_pairs={{0,16},{4,20},{8,24},{12,28},{16,0},{20,4},{24,8},{28,12},{1,17},{... | collective-permute-start | bytes 196616 | tf_op jit(solution)/shard_map/ppermute | solution.py:217
  6.9 5.5 %collective-permute-start.1 = (bf16[8,4096]{1,0:T(8,128)(2,1)S(1)}, bf16[8,4096]{1,0:T(8,128)(2,1)S(1)}, u32[]{:S(2)}, u32[]{:S(2)}) collective-permute-start(bf16[8,4096]{1,0:T(8,128)(2,1)S(1)} %get-tuple-element.16.refs_0_), channel_id=1, source_target_pairs={{0,8},{4,12},{8,0},{12,4},{16,24},{20,28},{24,16},{28,20},{1,9},{5... | collective-permute-start | bytes 196616 | tf_op jit(solution)/shard_map/ppermute | solution.py:217
  7.0 5.4 %collective-permute-start = (bf16[8,4096]{1,0:T(8,128)(2,1)S(1)}, bf16[8,4096]{1,0:T(8,128)(2,1)S(1)}, u32[]{:S(2)}, u32[]{:S(2)}) collective-permute-start(bf16[8,4096]{1,0:T(8,128)(2,1)S(1)} %get-tuple-element.16.refs_0_), channel_id=1, source_target_pairs={{0,4},{4,0},{8,12},{12,8},{16,20},{20,16},{24,28},{28,24},{1,5},{5... | collective-permute-start | bytes 196616 | tf_op jit(solution)/shard_map/ppermute | solution.py:217
  7.0 6.4 %collective-permute-start.12 = (bf16[8,4224]{1,0:T(8,128)(2,1)S(1)}, bf16[8,4224]{1,0:T(8,128)(2,1)S(1)}, u32[]{:S(2)}, u32[]{:S(2)}) collective-permute-start(bf16[8,4224]{1,0:T(8,128)(2,1)S(1)} %get-tuple-element.18.refs_3_), channel_id=1, source_target_pairs={{0,24},{4,28},{8,16},{12,20},{16,8},{20,12},{24,0},{28,4},{1,25},{... | collective-permute-start | bytes 202760 | tf_op jit(solution)/shard_map/ppermute | solution.py:217
  9.9 5.0 %collective-permute-start.10 = (bf16[8,4224]{1,0:T(8,128)(2,1)S(1)}, bf16[8,4224]{1,0:T(8,128)(2,1)S(1)}, u32[]{:S(2)}, u32[]{:S(2)}) collective-permute-start(bf16[8,4224]{1,0:T(8,128)(2,1)S(1)} %get-tuple-element.18.refs_3_), channel_id=1, source_target_pairs={{0,16},{4,20},{8,24},{12,28},{16,0},{20,4},{24,8},{28,12},{1,17},{... | collective-permute-start | bytes 202760 | tf_op jit(solution)/shard_map/ppermute | solution.py:217
  11.0 4.3 %collective-permute-start.8 = (bf16[8,4224]{1,0:T(8,128)(2,1)S(1)}, bf16[8,4224]{1,0:T(8,128)(2,1)S(1)}, u32[]{:S(2)}, u32[]{:S(2)}) collective-permute-start(bf16[8,4224]{1,0:T(8,128)(2,1)S(1)} %get-tuple-element.18.refs_3_), channel_id=1, source_target_pairs={{0,8},{4,12},{8,0},{12,4},{16,24},{20,28},{24,16},{28,20},{1,9},{5... | collective-permute-start | bytes 202760 | tf_op jit(solution)/shard_map/ppermute | solution.py:217
  12.4 3.0 %collective-permute-start.6 = (bf16[8,4096]{1,0:T(8,128)(2,1)S(1)}, bf16[8,4096]{1,0:T(8,128)(2,1)S(1)}, u32[]{:S(2)}, u32[]{:S(2)}) collective-permute-start(bf16[8,4096]{1,0:T(8,128)(2,1)S(1)} %collective-permute-done.5.refs_6_), channel_id=1, source_target_pairs={{0,4},{4,0},{8,12},{12,8},{16,20},{20,16},{24,28},{28,24},{1,5},{5... | collective-permute-start | bytes 196616 | tf_op jit(solution)/shard_map/ppermute | solution.py:217
  12.4 3.4 %collective-permute-start.4 = (bf16[8,4096]{1,0:T(8,128)(2,1)S(1)}, bf16[8,4096]{1,0:T(8,128)(2,1)S(1)}, u32[]{:S(2)}, u32[]{:S(2)}) collective-permute-start(bf16[8,4096]{1,0:T(8,128)(2,1)S(1)} %collective-permute-done.3.refs_4_), channel_id=1, source_target_pairs={{0,4},{4,0},{8,12},{12,8},{16,20},{20,16},{24,28},{28,24},{1,5},{5... | collective-permute-start | bytes 196616 | tf_op jit(solution)/shard_map/ppermute | solution.py:217
  13.5 3.1 %collective-permute-start.2 = (bf16[8,4096]{1,0:T(8,128)(2,1)S(1)}, bf16[8,4096]{1,0:T(8,128)(2,1)S(1)}, u32[]{:S(2)}, u32[]{:S(2)}) collective-permute-start(bf16[8,4096]{1,0:T(8,128)(2,1)S(1)} %collective-permute-done.1.refs_2_), channel_id=1, source_target_pairs={{0,4},{4,0},{8,12},{12,8},{16,20},{20,16},{24,28},{28,24},{1,5},{5... | collective-permute-start | bytes 196616 | tf_op jit(solution)/shard_map/ppermute | solution.py:217
  14.8 2.5 %collective-permute-start.7 = (bf16[8,4224]{1,0:T(8,128)(2,1)S(1)}, bf16[8,4224]{1,0:T(8,128)(2,1)S(1)}, u32[]{:S(2)}, u32[]{:S(2)}) collective-permute-start(bf16[8,4224]{1,0:T(8,128)(2,1)S(1)} %get-tuple-element.18.refs_3_), channel_id=1, source_target_pairs={{0,4},{4,0},{8,12},{12,8},{16,20},{20,16},{24,28},{28,24},{1,5},{5... | collective-permute-start | bytes 202760 | tf_op jit(solution)/shard_map/ppermute | solution.py:217
  15.3 2.0 %collective-permute-start.13 = (bf16[8,4224]{1,0:T(8,128)(2,1)S(1)}, bf16[8,4224]{1,0:T(8,128)(2,1)S(1)}, u32[]{:S(2)}, u32[]{:S(2)}) collective-permute-start(bf16[8,4224]{1,0:T(8,128)(2,1)S(1)} %collective-permute-done.12.refs_9_), channel_id=1, source_target_pairs={{0,4},{4,0},{8,12},{12,8},{16,20},{20,16},{24,28},{28,24},{1,5},{5... | collective-permute-start | bytes 202760 | tf_op jit(solution)/shard_map/ppermute | solution.py:217
  15.4 2.0 %collective-permute-start.11 = (bf16[8,4224]{1,0:T(8,128)(2,1)S(1)}, bf16[8,4224]{1,0:T(8,128)(2,1)S(1)}, u32[]{:S(2)}, u32[]{:S(2)}) collective-permute-start(bf16[8,4224]{1,0:T(8,128)(2,1)S(1)} %collective-permute-done.10.refs_7_), channel_id=1, source_target_pairs={{0,4},{4,0},{8,12},{12,8},{16,20},{20,16},{24,28},{28,24},{1,5},{5... | collective-permute-start | bytes 202760 | tf_op jit(solution)/shard_map/ppermute | solution.py:217
  15.8 1.5 %collective-permute-start.9 = (bf16[8,4224]{1,0:T(8,128)(2,1)S(1)}, bf16[8,4224]{1,0:T(8,128)(2,1)S(1)}, u32[]{:S(2)}, u32[]{:S(2)}) collective-permute-start(bf16[8,4224]{1,0:T(8,128)(2,1)S(1)} %collective-permute-done.8.refs_5_), channel_id=1, source_target_pairs={{0,4},{4,0},{8,12},{12,8},{16,20},{20,16},{24,28},{28,24},{1,5},{5... | collective-permute-start | bytes 202760 | tf_op jit(solution)/shard_map/ppermute | solution.py:217
  26.6 5.7 %collective-permute-start.14 = (f32[32,128]{1,0:T(8,128)S(1)}, f32[32,128]{1,0:T(8,128)S(1)}, u32[]{:S(2)}, u32[]{:S(2)}) collective-permute-start(f32[32,128]{1,0:T(8,128)S(1)} %get-tuple-element.22), channel_id=1, source_target_pairs={{0,1},{1,2},{2,3},{3,0},{4,5},{5,6},{6,7},{7,4},{8,9},{9,10},{10,1... | collective-permute-start | bytes 49160 | tf_op jit(solution)/shard_map/ppermute | solution.py:298
  28.2 4.6 %collective-permute-start.15 = (f32[32,128]{1,0:T(8,128)S(1)}, f32[32,128]{1,0:T(8,128)S(1)}, u32[]{:S(2)}, u32[]{:S(2)}) collective-permute-start(f32[32,128]{1,0:T(8,128)S(1)} %get-tuple-element.23), channel_id=1, source_target_pairs={{0,2},{1,3},{2,0},{3,1},{4,6},{5,7},{6,4},{7,5},{8,10},{9,11},{10,... | collective-permute-start | bytes 49160 | tf_op jit(solution)/shard_map/ppermute | solution.py:298
  30.8 3.7 %collective-permute-start.16 = (f32[32,128]{1,0:T(8,128)S(1)}, f32[32,128]{1,0:T(8,128)S(1)}, u32[]{:S(2)}, u32[]{:S(2)}) collective-permute-start(f32[32,128]{1,0:T(8,128)S(1)} %get-tuple-element.24), channel_id=1, source_target_pairs={{0,3},{1,0},{2,1},{3,2},{4,7},{5,4},{6,5},{7,6},{8,11},{9,8},{10,9... | collective-permute-start | bytes 49160 | tf_op jit(solution)/shard_map/ppermute | solution.py:298

commit v17 on v15

--- a/solution.py
+++ b/solution.py
@@ -16,6 +16,10 @@
 
 def iota(shape, dimension):
     return lax.broadcasted_iota(jnp.int32, shape, dimension)
+
+
+def kept_distances(holders):
+    return [0] + [k + 1 for k in range(2, holders, 2)]
 
 
 def parts_of(value):
@@ -31,18 +35,17 @@
     return value.astype(jnp.float32).astype(jnp.bfloat16)
 
 
-def condition_kernel(holders, capacity, *refs):
-    sources, packed_ref, pages_ref, found_ref, landing, arrived, turned_ref = refs[:6], *refs[6:9], refs[9:14], *refs[14:]
+def condition_kernel(holders, capacity, per_holder, *refs):
+    sources, packed_ref, again_ref, found_ref, landing, arrived, turned_ref = refs[:5], *refs[5:8], refs[8:13], *refs[13:]
     copies = [
         pltpu.make_async_copy(source, target, arrived.at[i])
-        for i, (source, target) in enumerate(zip(sources, landing + (pages_ref,)))
+        for i, (source, target) in enumerate(zip(sources, landing))
     ]
     for copy in copies:
         copy.start()
-    for copy in copies[:-1]:
+    for copy in copies:
         copy.wait()
     query_ref, in_factor_ref, out_factor_ref, home_ref, cand_ref = landing
-    per_holder = pages_ref.shape[0]
     rows, width = query_ref.shape
     layers, rank, _ = in_factor_ref.shape
     half = rank // 2
@@ -123,13 +126,19 @@
     if spare:
         blocks.append(jnp.zeros((rows, spare), jnp.float32))
     packed_ref[:, width:] = jnp.concatenate(blocks, axis=1).astype(jnp.bfloat16)
+    again_ref[...] = packed_ref[...]
     found_ref[...] = jnp.concatenate([holder, rank_there, jnp.zeros((6, slots), jnp.float32)], axis=0)
-    copies[-1].wait()
+
+
+def load_kernel(block_ref, source_ref, same_block_ref, target_ref, arrived):
+    copy = pltpu.make_async_copy(source_ref, target_ref, arrived)
+    copy.start()
+    copy.wait()
 
 
 def score_kernel(holders, capacity, *refs):
-    count_ref, found_ref, packed_refs = *refs[:2], refs[2:2 + holders]
-    pages_ref, out_ref, used_ref, total, queries = refs[2 + holders:]
+    count_ref, found_ref, packed_refs = *refs[:2], refs[2:2 + holders][::-1]
+    pages_ref, keep_ref, send_ref, used_ref, total, queries = refs[2 + holders:]
     me = lax.axis_index("store")
     count, width = pages_ref.shape
     rows = packed_refs[0].shape[0]
@@ -165,23 +174,28 @@
     own_slots = found_ref.shape[1]
     used_ref[0:1] = jnp.where(iota((1, own_slots), 1) < count_ref[0], found_ref[0:1], float(holders))
     picked = jnp.concatenate(picked, axis=0).T
-    for k in range(holders):
-        out_ref[me ^ k] = picked[k * half:(k + 1) * half]
-
-
-def spread_kernel(holders, groups, found_ref, landed_ref, *out_refs):
-    half = landed_ref.shape[1]
+    for place, k in enumerate(kept_distances(holders)):
+        keep_ref[place] = picked[k * half:(k + 1) * half]
+        send_ref[place] = picked[(k ^ 1) * half:((k ^ 1) + 1) * half]
+
+
+def spread_kernel(holders, groups, found_ref, *refs):
+    landed_refs, out_refs = refs[:holders // 2], refs[holders // 2:]
+    half = landed_refs[0].shape[1]
     slots = found_ref.shape[1]
-    total = landed_ref.shape[2] // 2
+    total = landed_refs[0].shape[2] // 2
     at = lax.axis_index("layer")
     share = slots // groups
-    holder, rank_there = found_ref[0:1], found_ref[1:2]
+    distance = found_ref[0:1].astype(jnp.int32) ^ lax.axis_index("store")
+    order = [k ^ core for k in kept_distances(holders) for core in range(2)]
+    begins = sum(jnp.where(distance == k, place * half + 1, 0) for place, k in enumerate(order)).astype(jnp.float32) - 1.0
+    rank_there = found_ref[1:2]
     place = iota((holders * half, slots), 0).astype(jnp.float32)
-    parts = parts_of(jnp.concatenate([landed_ref[h] for h in range(holders)], axis=0))[::-1]
+    parts = parts_of(jnp.concatenate([ref[core] for ref in landed_refs for core in range(2)], axis=0))[::-1]
     result = jnp.zeros((total, slots), jnp.float32)
     for side in range(2):
         on_side = (rank_there >= half) if side else (rank_there < half)
-        target = jnp.where(on_side, holder * half + rank_there - side * half, -1.0)
+        target = jnp.where(on_side & (begins >= 0.0), begins + rank_there - side * half, -1.0)
         chosen = exact_bf16(place == target)
         for part in parts:
             spread = lax.dot_general(part, chosen, (((0,), (0,)), ((), ())), preferred_element_type=jnp.float32)
@@ -215,54 +229,70 @@
     home = page_home.reshape(-1, LANES)
     sources = [
         pltpu.with_memory_space_constraint(source, pltpu.HBM)
-        for source in (query_grads, factor_in, factor_out, home, cand_lists, page_store)
+        for source in (query_grads, factor_in, factor_out, home, cand_lists)
     ]
     notes = max(LANES, holders // rows * capacity)
-    packed, pages, found = pl.pallas_call(
-        functools.partial(condition_kernel, holders, capacity),
+    packed, again, found = pl.pallas_call(
+        functools.partial(condition_kernel, holders, capacity, per_holder),
         out_shape=[
             jax.ShapeDtypeStruct((rows, width + notes), bf16),
-            pltpu.VMEM(page_store.shape, bf16),
+            jax.ShapeDtypeStruct((rows, width + notes), bf16),
             jax.ShapeDtypeStruct((8, slots), jnp.float32),
         ],
         in_specs=[HBM] * len(sources),
         out_specs=[VMEM] * 3,
-        scratch_shapes=[pltpu.VMEM(source.shape, source.dtype) for source in sources[:-1]]
+        scratch_shapes=[pltpu.VMEM(source.shape, source.dtype) for source in sources]
         + [pltpu.SemaphoreType.DMA((len(sources),)), pltpu.VMEM((layers, rows * rank // 2, LANES), jnp.float32)],
         compiler_params=pltpu.CompilerParams(vmem_limit_bytes=10 * 2**20 + 24 * slots * slots),
     )(*sources)
 
+    again, pages = pl.pallas_call(
+        load_kernel,
+        out_shape=[jax.ShapeDtypeStruct(again.shape, bf16), pltpu.VMEM(page_store.shape, bf16)],
+        in_specs=[VMEM, HBM],
+        out_specs=[VMEM] * 2,
+        input_output_aliases={0: 0},
+        scratch_shapes=[pltpu.SemaphoreType.DMA(())],
+        compiler_params=pltpu.CompilerParams(vmem_limit_bytes=2 * 2**20),
+        cost_estimate=pl.CostEstimate(flops=0, bytes_accessed=2 * page_store.size, transcendentals=0),
+    )(again, pltpu.with_memory_space_constraint(page_store, pltpu.HBM))
+
     blocks = [None] * holders
     blocks[0] = packed
-    for k in reversed(range(2, holders, 2)):
+    for k in range(2, holders, 2):
         blocks[k] = swap(packed, "store", k)
-    blocks[1] = swap(packed, "store", 1)
-    for k in reversed(range(2, holders, 2)):
+    blocks[1] = swap(again, "store", 1)
+    for k in range(2, holders, 2):
         blocks[k + 1] = swap(blocks[k], "store", 1)
 
     total = holders * rows
     bytes_in = 2 * holders * rows * (width + notes) + 2 * per_holder * width
-    asked, used = pl.pallas_call(
+    keep, send, used = pl.pallas_call(
         functools.partial(score_kernel, holders, capacity),
         out_shape=[
-            jax.ShapeDtypeStruct((holders, capacity // 2, 2 * total), jnp.float32),
+            jax.ShapeDtypeStruct((holders // 2, capacity // 2, 2 * total), jnp.float32),
+            jax.ShapeDtypeStruct((holders // 2, capacity // 2, 2 * total), jnp.float32),
             jax.ShapeDtypeStruct(found.shape, jnp.float32),
         ],
         in_specs=[SMEM] + [VMEM] * (holders + 2),
-        out_specs=[VMEM] * 2,
+        out_specs=[VMEM] * 3,
         scratch_shapes=[pltpu.VMEM((total, per_holder), jnp.float32), pltpu.VMEM((total, width), bf16)],
         compiler_params=pltpu.CompilerParams(vmem_limit_bytes=8 * 2**20 + 2 * bytes_in + 48 * total * slots),
-    )(counts, found, *blocks, pltpu.with_memory_space_constraint(pages, pltpu.VMEM))
-
-    landed = lax.all_to_all(asked, "store", split_axis=0, concat_axis=0, tiled=True)
+    )(counts, found, *blocks[::-1], pltpu.with_memory_space_constraint(pages, pltpu.VMEM))
+
+    handed = swap(send, "store", 1)
+    landed = []
+    for place, k in enumerate(kept_distances(holders)):
+        pair = jnp.stack([keep[place], handed[place]])
+        landed.append(swap(pair, "store", k) if k else pair)
     share = slots // groups
     terms = pl.pallas_call(
         functools.partial(spread_kernel, holders, groups),
         out_shape=[jax.ShapeDtypeStruct((share // 2, 2 * total), jnp.float32)] * groups,
-        in_specs=[VMEM] * 2,
+        in_specs=[VMEM] * (1 + len(landed)),
         out_specs=[VMEM] * groups,
         compiler_params=pltpu.CompilerParams(vmem_limit_bytes=4 * 2**20 + 64 * total * slots),
-    )(used, landed)
+    )(used, *landed)
     summed = terms[0]
     for step in range(1, groups):
         summed = summed + lax.ppermute(terms[step], "layer", [(g, (g + step) % groups) for g in range(groups)])

time: 33.4 us -> 32.4 us (0.970)
  blocking collectives: 7.86 us -> 0 us
  starting transfers between devices: 10.6 us -> 13.9 us
  Pallas kernels: 4.63 us -> 6.56 us
  waiting for transfers between devices: 8.78 us -> 10.3 us
    all_to_all x1 -> x0, blocking collectives: 7.86 us -> none  [on_device(): lax.all_to_all(asked, 'store', split_axis=0, concat_axis=0, tiled=True)]
    ppermute x7 -> x11, starting transfers between devices: 4.88 us -> 8.37 us  [swap(): lax.ppermute(value, axis, [(i, i ^ distance) for i in range(lax.axis_size...]
    pallas_call x1 -> x2, Pallas kernels: 2.43 us -> 4.37 us  [the longest x1 2.2 us: on_device(): pl.pallas_call(load_kernel, out_shape=[jax.ShapeDtypeStruct(again.shape,...]
    ppermute x7 -> x11, waiting for transfers between devices: 6.4 us -> 7.94 us  [swap(): lax.ppermute(value, axis, [(i, i ^ distance) for i in range(lax.axis_size...]
  transfers between devices with their start and end apart: 10 -> 14, of which waited for: 7 -> 11; matrix products, arithmetic and copies ran while one was open for 0% -> 0% of each run, Pallas kernels for 0% -> 7%
where the time goes in v17:
time: 32.4 us; the launch traced here: 32.3 us
  starting transfers between devices  13.9 us (43%)
  waiting for transfers between devices  10.3 us (32%)
  Pallas kernels  6.56 us (20%)
  between operations  0.72 us (2%)
  other arithmetic  0.64 us (2%)
    ppermute x11, starting transfers between devices, swap(): lax.ppermute(value, axis, [(i, i ^ distance) for i in range(lax.axis_size...  8.37 us
    ppermute x11, waiting for transfers between devices, swap(): lax.ppermute(value, axis, [(i, i ^ distance) for i in range(lax.axis_size...  7.94 us
    ppermute x3, starting transfers between devices, on_device(): lax.ppermute(terms[step], 'layer', [(g, (g + step) % groups) for g in ran...  5.57 us
    ppermute x3, waiting for transfers between devices, on_device(): lax.ppermute(terms[step], 'layer', [(g, (g + step) % groups) for g in ran...  2.39 us
    pallas_call x1, Pallas kernels, on_device(): pl.pallas_call(load_kernel, out_shape=[jax.ShapeDtypeStruct(again.shape,...  2.2 us
    pallas_call x1, Pallas kernels, on_device(): pl.pallas_call(functools.partial(condition_kernel, holders, capacity, per...  2.18 us
    pallas_call x1, Pallas kernels, on_device(): pl.pallas_call(functools.partial(score_kernel, holders, capacity), out_sh...  1.74 us
  transfers between devices with their start and end apart: 14, of which 11 were waited for; matrix products, arithmetic and copies ran while one was open for 0% of the time, Pallas kernels for 7%

profile of v17, /device:TPU:0, one launch (start us, length us, event | category | flops | bytes accessed | tf_op | source)
XLA Modules:
  0.0 32.3 jit_solution(4139999507006895371)
XLA Ops:
  0.0 2.2 %shard_map.73 = (bf16[8,8320]{1,0:T(8,128)(2,1)S(1)}, bf16[8,8320]{1,0:T(8,128)(2,1)S(1)}, f32[8,256]{1,0:T(8,128)S(1)}) custom-call(bf16[8,8192]{1,0:T(8,128)(2,1)} %refs_0_.2, f32[2,64,64]{2,1,0:T(8,128)} %refs_1_.1, f32[2,64,64]{2,1,0:T(8,128)} %refs_2_.1, s32[16,128]{1,0:T(8,128)} %bitcast.3, s32[1,256]{1,0:T(1,128)} %refs_4_.1), custom_call_target="tpu_custom_call" | custom-call | tf_op jit(solution)/shard_map/pallas_call | solution.py:235
  2.2 4.0 %collective-permute-start = (bf16[8,8320]{1,0:T(8,128)(2,1)S(1)}, bf16[8,8320]{1,0:T(8,128)(2,1)S(1)}, u32[]{:S(2)}, u32[]{:S(2)}) collective-permute-start(bf16[8,8320]{1,0:T(8,128)(2,1)S(1)} %get-tuple-element.18.refs_9_), channel_id=1, source_target_pairs={{0,24},{4,28},{8,16},{12,20},{16,8},{20,12},{24,0},{28,4},{1,25},{... | collective-permute-start | bytes 399368 | tf_op jit(solution)/shard_map/ppermute | solution.py:216
  6.2 0.5 %collective-permute-start.2 = (bf16[8,8320]{1,0:T(8,128)(2,1)S(1)}, bf16[8,8320]{1,0:T(8,128)(2,1)S(1)}, u32[]{:S(2)}, u32[]{:S(2)}) collective-permute-start(bf16[8,8320]{1,0:T(8,128)(2,1)S(1)} %get-tuple-element.18.refs_9_), channel_id=1, source_target_pairs={{0,16},{4,20},{8,24},{12,28},{16,0},{20,4},{24,8},{28,12},{1,17},{... | collective-permute-start | bytes 399368 | tf_op jit(solution)/shard_map/ppermute | solution.py:216
  6.7 0.1 collective-permute-start.4
  6.8 2.2 %shard_map.74 = (bf16[8,8320]{1,0:T(8,128)(2,1)S(1)}, bf16[256,8192]{1,0:T(8,128)(2,1)S(1)}) custom-call(bf16[8,8320]{1,0:T(8,128)(2,1)S(1)} %get-tuple-element.19.block_ref, bf16[256,8192]{1,0:T(8,128)(2,1)} %source_ref.1), custom_call_target="tpu_custom_call", output_to_operand_aliasing={{0}: (0, {})} | custom-call | bytes 4194304 | tf_op jit(solution)/shard_map/pallas_call | solution.py:249
  9.0 0.1 collective-permute-start.6
  9.1 1.0 %collective-permute-done.refs_3_ = bf16[8,8320]{1,0:T(8,128)(2,1)S(1)} collective-permute-done((bf16[8,8320]{1,0:T(8,128)(2,1)S(1)}, bf16[8,8320]{1,0:T(8,128)(2,1)S(1)}, u32[]{:S(2)}, u32[]{:S(2)}) %collective-permute-start) | collective-permute-done | bytes 133152 | tf_op jit(solution)/shard_map/ppermute | solution.py:216
  10.1 0.0 collective-permute-start.1
  10.1 2.4 %collective-permute-done.2.refs_5_ = bf16[8,8320]{1,0:T(8,128)(2,1)S(1)} collective-permute-done((bf16[8,8320]{1,0:T(8,128)(2,1)S(1)}, bf16[8,8320]{1,0:T(8,128)(2,1)S(1)}, u32[]{:S(2)}, u32[]{:S(2)}) %collective-permute-start.2) | collective-permute-done | bytes 133152 | tf_op jit(solution)/shard_map/ppermute | solution.py:216
  12.5 0.0 collective-permute-start.3
  12.5 0.2 collective-permute-done.4.refs_7_
  12.8 0.3 collective-permute-start.5
  13.7 0.0 collective-permute-done.6.refs_8_
  13.7 0.0 collective-permute-done.1.refs_2_
  13.7 0.2 collective-permute-done.3.refs_4_
  13.9 0.3 collective-permute-done.5.refs_6_
  14.1 1.7 %shard_map.75 = (f32[4,16,128]{2,1,0:T(8,128)S(1)}, f32[4,16,128]{2,1,0:T(8,128)S(1)}, f32[8,256]{1,0:T(8,128)S(1)}) custom-call(s32[1]{0:T(128)S(6)} %copy.10.refs_0_, f32[8,256]{1,0:T(8,128)S(1)} %get-tuple-element.17.refs_1_, bf16[8,8320]{1,0:T(8,128)(2,1)S(1)} %collective-permute-done.1.refs_2_, bf16[8,8320]{1,0:T(8,128)(2,1)S(1)} %collective-permute-done.refs_3_, ...), custom_call_target="tpu_custom_call" | custom-call | tf_op jit(solution)/shard_map/pallas_call | solution.py:270
  15.9 0.3 %collective-permute-start.7 = (f32[4,16,128]{2,1,0:T(8,128)S(1)}, f32[4,16,128]{2,1,0:T(8,128)S(1)}, u32[]{:S(2)}, u32[]{:S(2)}) collective-permute-start(f32[4,16,128]{2,1,0:T(8,128)S(1)} %get-tuple-element.24), channel_id=1, source_target_pairs={{0,4},{4,0},{8,12},{12,8},{16,20},{20,16},{24,28},{28,24},{1,5},{5... | collective-permute-start | bytes 98312 | tf_op jit(solution)/shard_map/ppermute | solution.py:216
  16.2 0.9 %collective-permute-done.7 = f32[4,16,128]{2,1,0:T(8,128)S(1)} collective-permute-done((f32[4,16,128]{2,1,0:T(8,128)S(1)}, f32[4,16,128]{2,1,0:T(8,128)S(1)}, u32[]{:S(2)}, u32[]{:S(2)}) %collective-permute-start.7) | collective-permute-done | bytes 32800 | tf_op jit(solution)/shard_map/ppermute | solution.py:216
  17.2 1.7 %collective-permute-start.10 = (f32[2,16,128]{2,1,0:T(8,128)S(1)}, f32[2,16,128]{2,1,0:T(8,128)S(1)}, u32[]{:S(2)}, u32[]{:S(2)}) collective-permute-start(f32[2,16,128]{2,1,0:T(8,128)S(1)} %pad_maximum_fusion.3), channel_id=1, source_target_pairs={{0,28},{4,24},{8,20},{12,16},{16,12},{20,8},{24,4},{28,0},{1,29},{... | collective-permute-start | bytes 49160 | tf_op jit(solution)/shard_map/ppermute | solution.py:216
  18.9 1.1 %collective-permute-start.9 = (f32[2,16,128]{2,1,0:T(8,128)S(1)}, f32[2,16,128]{2,1,0:T(8,128)S(1)}, u32[]{:S(2)}, u32[]{:S(2)}) collective-permute-start(f32[2,16,128]{2,1,0:T(8,128)S(1)} %pad_maximum_fusion.2), channel_id=1, source_target_pairs={{0,20},{4,16},{8,28},{12,24},{16,4},{20,0},{24,12},{28,8},{1,21},{... | collective-permute-start | bytes 49160 | tf_op jit(solution)/shard_map/ppermute | solution.py:216
  20.0 0.3 collective-permute-start.8
  20.3 1.0 %collective-permute-done.10.refs_3_ = f32[2,16,128]{2,1,0:T(8,128)S(1)} collective-permute-done((f32[2,16,128]{2,1,0:T(8,128)S(1)}, f32[2,16,128]{2,1,0:T(8,128)S(1)}, u32[]{:S(2)}, u32[]{:S(2)}) %collective-permute-start.10) | collective-permute-done | bytes 16416 | tf_op jit(solution)/shard_map/ppermute | solution.py:216
  21.2 0.8 %collective-permute-done.9.refs_2_ = f32[2,16,128]{2,1,0:T(8,128)S(1)} collective-permute-done((f32[2,16,128]{2,1,0:T(8,128)S(1)}, f32[2,16,128]{2,1,0:T(8,128)S(1)}, u32[]{:S(2)}, u32[]{:S(2)}) %collective-permute-start.9) | collective-permute-done | bytes 16416 | tf_op jit(solution)/shard_map/ppermute | solution.py:216
  22.0 1.1 %collective-permute-done.8.refs_1_ = f32[2,16,128]{2,1,0:T(8,128)S(1)} collective-permute-done((f32[2,16,128]{2,1,0:T(8,128)S(1)}, f32[2,16,128]{2,1,0:T(8,128)S(1)}, u32[]{:S(2)}, u32[]{:S(2)}) %collective-permute-start.8) | collective-permute-done | bytes 16416 | tf_op jit(solution)/shard_map/ppermute | solution.py:216
  23.1 0.4 %shard_map.76 = (f32[32,128]{1,0:T(8,128)S(1)}, f32[32,128]{1,0:T(8,128)S(1)}, f32[32,128]{1,0:T(8,128)S(1)}, f32[32,128]{1,0:T(8,128)S(1)}) custom-call(f32[8,256]{1,0:T(8,128)S(1)} %get-tuple-element.22.found_ref, f32[2,16,128]{2,1,0:T(8,128)S(1)} %pad_maximum_fusion.refs_0_, f32[2,16,128]{2,1,0:T(8,128)S(1)} %collective-permute-done.8.refs_1_, ...), custom_call_target="tpu_custom_call" | custom-call | tf_op jit(solution)/shard_map/pallas_call | solution.py:289
  23.6 1.6 %collective-permute-start.11 = (f32[32,128]{1,0:T(8,128)S(1)}, f32[32,128]{1,0:T(8,128)S(1)}, u32[]{:S(2)}, u32[]{:S(2)}) collective-permute-start(f32[32,128]{1,0:T(8,128)S(1)} %get-tuple-element.26), channel_id=1, source_target_pairs={{0,1},{1,2},{2,3},{3,0},{4,5},{5,6},{6,7},{7,4},{8,9},{9,10},{10,1... | collective-permute-start | bytes 49160 | tf_op jit(solution)/shard_map/ppermute | solution.py:298
  25.2 2.6 %collective-permute-start.12 = (f32[32,128]{1,0:T(8,128)S(1)}, f32[32,128]{1,0:T(8,128)S(1)}, u32[]{:S(2)}, u32[]{:S(2)}) collective-permute-start(f32[32,128]{1,0:T(8,128)S(1)} %get-tuple-element.27), channel_id=1, source_target_pairs={{0,2},{1,3},{2,0},{3,1},{4,6},{5,7},{6,4},{7,5},{8,10},{9,11},{10,... | collective-permute-start | bytes 49160 | tf_op jit(solution)/shard_map/ppermute | solution.py:298
  27.8 1.3 %collective-permute-start.13 = (f32[32,128]{1,0:T(8,128)S(1)}, f32[32,128]{1,0:T(8,128)S(1)}, u32[]{:S(2)}, u32[]{:S(2)}) collective-permute-start(f32[32,128]{1,0:T(8,128)S(1)} %get-tuple-element.28), channel_id=1, source_target_pairs={{0,3},{1,0},{2,1},{3,2},{4,7},{5,4},{6,5},{7,6},{8,11},{9,8},{10,9... | collective-permute-start | bytes 49160 | tf_op jit(solution)/shard_map/ppermute | solution.py:298
  29.2 0.0 collective-permute-done.11
  29.2 0.7 %collective-permute-done.12 = f32[32,128]{1,0:T(8,128)S(1)} collective-permute-done((f32[32,128]{1,0:T(8,128)S(1)}, f32[32,128]{1,0:T(8,128)S(1)}, u32[]{:S(2)}, u32[]{:S(2)}) %collective-permute-start.12) | collective-permute-done | bytes 16416 | tf_op jit(solution)/shard_map/ppermute | solution.py:298
  29.9 1.7 %collective-permute-done.13 = f32[32,128]{1,0:T(8,128)S(1)} collective-permute-done((f32[32,128]{1,0:T(8,128)S(1)}, f32[32,128]{1,0:T(8,128)S(1)}, u32[]{:S(2)}, u32[]{:S(2)}) %collective-permute-start.13) | collective-permute-done | bytes 16416 | tf_op jit(solution)/shard_map/ppermute | solution.py:298
  31.6 0.1 fusion.2
  31.6 0.6 %maximum_bitcast_fusion = f32[1,64,64]{2,1,0:T(8,128)} fusion(f32[32,64]{1,0:T(8,128)S(1)} %get-tuple-element.38, f32[32,64]{1,0:T(8,128)S(1)} %get-tuple-element.37), kind=kLoop, calls=%fused_computation | loop fusion | flops 4096 | bytes 32768 | tf_op jit(solution)/shard_map/broadcast_in_dim | solution.py:299
  (7 shorter events, 0.0 us)
Async XLA Ops:
  2.2 7.9 %collective-permute-start = (bf16[8,8320]{1,0:T(8,128)(2,1)S(1)}, bf16[8,8320]{1,0:T(8,128)(2,1)S(1)}, u32[]{:S(2)}, u32[]{:S(2)}) collective-permute-start(bf16[8,8320]{1,0:T(8,128)(2,1)S(1)} %get-tuple-element.18.refs_9_), channel_id=1, source_target_pairs={{0,24},{4,28},{8,16},{12,20},{16,8},{20,12},{24,0},{28,4},{1,25},{... | collective-permute-start | bytes 399368 | tf_op jit(solution)/shard_map/ppermute | solution.py:216
  6.2 6.4 %collective-permute-start.2 = (bf16[8,8320]{1,0:T(8,128)(2,1)S(1)}, bf16[8,8320]{1,0:T(8,128)(2,1)S(1)}, u32[]{:S(2)}, u32[]{:S(2)}) collective-permute-start(bf16[8,8320]{1,0:T(8,128)(2,1)S(1)} %get-tuple-element.18.refs_9_), channel_id=1, source_target_pairs={{0,16},{4,20},{8,24},{12,28},{16,0},{20,4},{24,8},{28,12},{1,17},{... | collective-permute-start | bytes 399368 | tf_op jit(solution)/shard_map/ppermute | solution.py:216
  6.7 6.1 %collective-permute-start.4 = (bf16[8,8320]{1,0:T(8,128)(2,1)S(1)}, bf16[8,8320]{1,0:T(8,128)(2,1)S(1)}, u32[]{:S(2)}, u32[]{:S(2)}) collective-permute-start(bf16[8,8320]{1,0:T(8,128)(2,1)S(1)} %get-tuple-element.18.refs_9_), channel_id=1, source_target_pairs={{0,8},{4,12},{8,0},{12,4},{16,24},{20,28},{24,16},{28,20},{1,9},{5... | collective-permute-start | bytes 399368 | tf_op jit(solution)/shard_map/ppermute | solution.py:216
  9.0 4.7 %collective-permute-start.6 = (bf16[8,8320]{1,0:T(8,128)(2,1)S(1)}, bf16[8,8320]{1,0:T(8,128)(2,1)S(1)}, u32[]{:S(2)}, u32[]{:S(2)}) collective-permute-start(bf16[8,8320]{1,0:T(8,128)(2,1)S(1)} %get-tuple-element.20), channel_id=1, source_target_pairs={{0,4},{4,0},{8,12},{12,8},{16,20},{20,16},{24,28},{28,24},{1,5},{5... | collective-permute-start | bytes 399368 | tf_op jit(solution)/shard_map/ppermute | solution.py:216
  10.1 3.6 %collective-permute-start.1 = (bf16[8,8320]{1,0:T(8,128)(2,1)S(1)}, bf16[8,8320]{1,0:T(8,128)(2,1)S(1)}, u32[]{:S(2)}, u32[]{:S(2)}) collective-permute-start(bf16[8,8320]{1,0:T(8,128)(2,1)S(1)} %collective-permute-done.refs_3_), channel_id=1, source_target_pairs={{0,4},{4,0},{8,12},{12,8},{16,20},{20,16},{24,28},{28,24},{1,5},{5... | collective-permute-start | bytes 399368 | tf_op jit(solution)/shard_map/ppermute | solution.py:216
  12.5 1.4 %collective-permute-start.3 = (bf16[8,8320]{1,0:T(8,128)(2,1)S(1)}, bf16[8,8320]{1,0:T(8,128)(2,1)S(1)}, u32[]{:S(2)}, u32[]{:S(2)}) collective-permute-start(bf16[8,8320]{1,0:T(8,128)(2,1)S(1)} %collective-permute-done.2.refs_5_), channel_id=1, source_target_pairs={{0,4},{4,0},{8,12},{12,8},{16,20},{20,16},{24,28},{28,24},{1,5},{5... | collective-permute-start | bytes 399368 | tf_op jit(solution)/shard_map/ppermute | solution.py:216
  12.8 1.4 %collective-permute-start.5 = (bf16[8,8320]{1,0:T(8,128)(2,1)S(1)}, bf16[8,8320]{1,0:T(8,128)(2,1)S(1)}, u32[]{:S(2)}, u32[]{:S(2)}) collective-permute-start(bf16[8,8320]{1,0:T(8,128)(2,1)S(1)} %collective-permute-done.4.refs_7_), channel_id=1, source_target_pairs={{0,4},{4,0},{8,12},{12,8},{16,20},{20,16},{24,28},{28,24},{1,5},{5... | collective-permute-start | bytes 399368 | tf_op jit(solution)/shard_map/ppermute | solution.py:216
  15.9 1.3 %collective-permute-start.7 = (f32[4,16,128]{2,1,0:T(8,128)S(1)}, f32[4,16,128]{2,1,0:T(8,128)S(1)}, u32[]{:S(2)}, u32[]{:S(2)}) collective-permute-start(f32[4,16,128]{2,1,0:T(8,128)S(1)} %get-tuple-element.24), channel_id=1, source_target_pairs={{0,4},{4,0},{8,12},{12,8},{16,20},{20,16},{24,28},{28,24},{1,5},{5... | collective-permute-start | bytes 98312 | tf_op jit(solution)/shard_map/ppermute | solution.py:216
  17.2 4.1 %collective-permute-start.10 = (f32[2,16,128]{2,1,0:T(8,128)S(1)}, f32[2,16,128]{2,1,0:T(8,128)S(1)}, u32[]{:S(2)}, u32[]{:S(2)}) collective-permute-start(f32[2,16,128]{2,1,0:T(8,128)S(1)} %pad_maximum_fusion.3), channel_id=1, source_target_pairs={{0,28},{4,24},{8,20},{12,16},{16,12},{20,8},{24,4},{28,0},{1,29},{... | collective-permute-start | bytes 49160 | tf_op jit(solution)/shard_map/ppermute | solution.py:216
  18.9 3.2 %collective-permute-start.9 = (f32[2,16,128]{2,1,0:T(8,128)S(1)}, f32[2,16,128]{2,1,0:T(8,128)S(1)}, u32[]{:S(2)}, u32[]{:S(2)}) collective-permute-start(f32[2,16,128]{2,1,0:T(8,128)S(1)} %pad_maximum_fusion.2), channel_id=1, source_target_pairs={{0,20},{4,16},{8,28},{12,24},{16,4},{20,0},{24,12},{28,8},{1,21},{... | collective-permute-start | bytes 49160 | tf_op jit(solution)/shard_map/ppermute | solution.py:216
  20.0 3.2 %collective-permute-start.8 = (f32[2,16,128]{2,1,0:T(8,128)S(1)}, f32[2,16,128]{2,1,0:T(8,128)S(1)}, u32[]{:S(2)}, u32[]{:S(2)}) collective-permute-start(f32[2,16,128]{2,1,0:T(8,128)S(1)} %pad_maximum_fusion.1), channel_id=1, source_target_pairs={{0,12},{4,8},{8,4},{12,0},{16,28},{20,24},{24,20},{28,16},{1,13},{... | collective-permute-start | bytes 49160 | tf_op jit(solution)/shard_map/ppermute | solution.py:216
  23.6 5.6 %collective-permute-start.11 = (f32[32,128]{1,0:T(8,128)S(1)}, f32[32,128]{1,0:T(8,128)S(1)}, u32[]{:S(2)}, u32[]{:S(2)}) collective-permute-start(f32[32,128]{1,0:T(8,128)S(1)} %get-tuple-element.26), channel_id=1, source_target_pairs={{0,1},{1,2},{2,3},{3,0},{4,5},{5,6},{6,7},{7,4},{8,9},{9,10},{10,1... | collective-permute-start | bytes 49160 | tf_op jit(solution)/shard_map/ppermute | solution.py:298
  25.2 4.6 %collective-permute-start.12 = (f32[32,128]{1,0:T(8,128)S(1)}, f32[32,128]{1,0:T(8,128)S(1)}, u32[]{:S(2)}, u32[]{:S(2)}) collective-permute-start(f32[32,128]{1,0:T(8,128)S(1)} %get-tuple-element.27), channel_id=1, source_target_pairs={{0,2},{1,3},{2,0},{3,1},{4,6},{5,7},{6,4},{7,5},{8,10},{9,11},{10,... | collective-permute-start | bytes 49160 | tf_op jit(solution)/shard_map/ppermute | solution.py:298
  27.8 3.7 %collective-permute-start.13 = (f32[32,128]{1,0:T(8,128)S(1)}, f32[32,128]{1,0:T(8,128)S(1)}, u32[]{:S(2)}, u32[]{:S(2)}) collective-permute-start(f32[32,128]{1,0:T(8,128)S(1)} %get-tuple-element.28), channel_id=1, source_target_pairs={{0,3},{1,0},{2,1},{3,2},{4,7},{5,4},{6,5},{7,6},{8,11},{9,8},{10,9... | collective-permute-start | bytes 49160 | tf_op jit(solution)/shard_map/ppermute | solution.py:298

commit v18 on v17

--- a/solution.py
+++ b/solution.py
@@ -16,6 +16,17 @@
 
 def iota(shape, dimension):
     return lax.broadcasted_iota(jnp.int32, shape, dimension)
+
+
+def gather_steps(holders):
+    if holders == 8:
+        return [(2, 4), (6, 6), (4, 2)]
+    return [(k, k) for k in range(2, holders, 2)]
+
+
+def block_owners(holders):
+    across = gather_steps(holders)
+    return [(0, 0), (1, 1)] + across + [(second ^ 1, first ^ 1) for first, second in across]
 
 
 def kept_distances(holders):
@@ -152,8 +163,10 @@
         scores = scores + lax.dot_general(
             queries[:, columns], pages_ref[:, columns], (((1,), (1,)), ((), ())), preferred_element_type=jnp.float32
         )
-    for k in range(holders):
-        start = pl.multiple_of((me ^ k) * rows, rows)
+    second_core = me % 2 == 1
+    owners = block_owners(holders)
+    for k, (first, second) in enumerate(owners):
+        start = pl.multiple_of((me ^ jnp.where(second_core, second, first)) * rows, rows)
         total[pl.ds(start, rows), :] = scores[k * rows:(k + 1) * rows]
     asked = []
     for k in range(holders):
@@ -163,6 +176,10 @@
         for block in range(1, holders // rows):
             mine = jnp.where(me // rows == block, notes[:, block * capacity:(block + 1) * capacity], mine)
         asked.append(mine)
+    places = [[pair[core] for pair in owners] for core in range(2)]
+    asked = [
+        jnp.where(second_core, asked[places[1].index(k)], asked[places[0].index(k)]) for k in range(holders)
+    ]
     page = iota((count, holders * half), 0).astype(jnp.float32) + 1.0
     parts = parts_of(total[...])[::-1]
     picked = []
@@ -257,13 +274,10 @@
         cost_estimate=pl.CostEstimate(flops=0, bytes_accessed=2 * page_store.size, transcendentals=0),
     )(again, pltpu.with_memory_space_constraint(page_store, pltpu.HBM))
 
-    blocks = [None] * holders
-    blocks[0] = packed
-    for k in range(2, holders, 2):
-        blocks[k] = swap(packed, "store", k)
-    blocks[1] = swap(again, "store", 1)
-    for k in range(2, holders, 2):
-        blocks[k + 1] = swap(blocks[k], "store", 1)
+    across = [
+        lax.ppermute(packed, "store", [(i, i ^ step[i % 2]) for i in range(holders)]) for step in gather_steps(holders)
+    ]
+    blocks = [packed, swap(again, "store", 1)] + across + [swap(block, "store", 1) for block in across]
 
     total = holders * rows
     bytes_in = 2 * holders * rows * (width + notes) + 2 * per_holder * width

time: 32.4 us -> 32.4 us (level)
  starting transfers between devices: 13.9 us -> 14.6 us
  waiting for transfers between devices: 10.3 us -> 9.61 us
    ppermute x0 -> x3, starting transfers between devices: none -> 4.57 us  [on_device(): lax.ppermute(packed, 'store', [(i, i ^ step[i % 2]) for i in range(holder...]
    ppermute x11 -> x8, starting transfers between devices: 8.37 us -> 4.45 us  [swap(): lax.ppermute(value, axis, [(i, i ^ distance) for i in range(lax.axis_size...]
    ppermute x11 -> x8, waiting for transfers between devices: 7.94 us -> 4.16 us  [swap(): lax.ppermute(value, axis, [(i, i ^ distance) for i in range(lax.axis_size...]
    ppermute x0 -> x3, waiting for transfers between devices: none -> 3.06 us  [on_device(): lax.ppermute(packed, 'store', [(i, i ^ step[i % 2]) for i in range(holder...]
  transfers between devices with their start and end apart: 14 -> 14, of which waited for: 11 -> 9; matrix products, arithmetic and copies ran while one was open for 0% -> 0% of each run, Pallas kernels for 7% -> 7%
where the time goes in v18:
time: 32.4 us; the launch traced here: 32.2 us
  starting transfers between devices  14.6 us (45%)
  waiting for transfers between devices  9.61 us (30%)
  Pallas kernels  6.57 us (20%)
  between operations  0.72 us (2%)
  other arithmetic  0.64 us (2%)
    ppermute x3, starting transfers between devices, on_device(): lax.ppermute(terms[step], 'layer', [(g, (g + step) % groups) for g in ran...  5.56 us
    ppermute x3, starting transfers between devices, on_device(): lax.ppermute(packed, 'store', [(i, i ^ step[i % 2]) for i in range(holder...  4.57 us
    ppermute x8, starting transfers between devices, swap(): lax.ppermute(value, axis, [(i, i ^ distance) for i in range(lax.axis_size...  4.45 us
    ppermute x8, waiting for transfers between devices, swap(): lax.ppermute(value, axis, [(i, i ^ distance) for i in range(lax.axis_size...  4.16 us
    ppermute x3, waiting for transfers between devices, on_device(): lax.ppermute(packed, 'store', [(i, i ^ step[i % 2]) for i in range(holder...  3.06 us
    ppermute x3, waiting for transfers between devices, on_device(): lax.ppermute(terms[step], 'layer', [(g, (g + step) % groups) for g in ran...  2.39 us
    pallas_call x1, Pallas kernels, on_device(): pl.pallas_call(load_kernel, out_shape=[jax.ShapeDtypeStruct(again.shape,...  2.2 us
    pallas_call x1, Pallas kernels, on_device(): pl.pallas_call(functools.partial(condition_kernel, holders, capacity, per...  2.18 us
  transfers between devices with their start and end apart: 14, of which 9 were waited for; matrix products, arithmetic and copies ran while one was open for 0% of the time, Pallas kernels for 7%

profile of v18, /device:TPU:0, one launch (start us, length us, event | category | flops | bytes accessed | tf_op | source)
XLA Modules:
  0.0 32.2 jit_solution(15764097027186841939)
XLA Ops:
  0.0 2.2 %shard_map.73 = (bf16[8,8320]{1,0:T(8,128)(2,1)S(1)}, bf16[8,8320]{1,0:T(8,128)(2,1)S(1)}, f32[8,256]{1,0:T(8,128)S(1)}) custom-call(bf16[8,8192]{1,0:T(8,128)(2,1)} %refs_0_.2, f32[2,64,64]{2,1,0:T(8,128)} %refs_1_.1, f32[2,64,64]{2,1,0:T(8,128)} %refs_2_.1, s32[16,128]{1,0:T(8,128)} %bitcast.3, s32[1,256]{1,0:T(1,128)} %refs_4_.1), custom_call_target="tpu_custom_call" | custom-call | tf_op jit(solution)/shard_map/pallas_call | solution.py:252
  2.2 3.0 %collective-permute-start = (bf16[8,8320]{1,0:T(8,128)(2,1)S(1)}, bf16[8,8320]{1,0:T(8,128)(2,1)S(1)}, u32[]{:S(2)}, u32[]{:S(2)}) collective-permute-start(bf16[8,8320]{1,0:T(8,128)(2,1)S(1)} %get-tuple-element.18.refs_9_), channel_id=1, source_target_pairs={{0,16},{4,12},{8,24},{12,4},{16,0},{20,28},{24,8},{28,20},{1,17},{... | collective-permute-start | bytes 399368 | tf_op jit(solution)/shard_map/ppermute | solution.py:278
  5.2 1.4 %collective-permute-start.2 = (bf16[8,8320]{1,0:T(8,128)(2,1)S(1)}, bf16[8,8320]{1,0:T(8,128)(2,1)S(1)}, u32[]{:S(2)}, u32[]{:S(2)}) collective-permute-start(bf16[8,8320]{1,0:T(8,128)(2,1)S(1)} %get-tuple-element.18.refs_9_), channel_id=1, source_target_pairs={{0,24},{4,28},{8,16},{12,20},{16,8},{20,12},{24,0},{28,4},{1,25},{... | collective-permute-start | bytes 399368 | tf_op jit(solution)/shard_map/ppermute | solution.py:278
  6.7 0.1 collective-permute-start.4
  6.8 2.2 %shard_map.74 = (bf16[8,8320]{1,0:T(8,128)(2,1)S(1)}, bf16[256,8192]{1,0:T(8,128)(2,1)S(1)}) custom-call(bf16[8,8320]{1,0:T(8,128)(2,1)S(1)} %get-tuple-element.19.block_ref, bf16[256,8192]{1,0:T(8,128)(2,1)} %source_ref.1), custom_call_target="tpu_custom_call", output_to_operand_aliasing={{0}: (0, {})} | custom-call | bytes 4194304 | tf_op jit(solution)/shard_map/pallas_call | solution.py:266
  9.0 0.1 collective-permute-start.6
  9.0 2.9 %collective-permute-done.refs_5_ = bf16[8,8320]{1,0:T(8,128)(2,1)S(1)} collective-permute-done((bf16[8,8320]{1,0:T(8,128)(2,1)S(1)}, bf16[8,8320]{1,0:T(8,128)(2,1)S(1)}, u32[]{:S(2)}, u32[]{:S(2)}) %collective-permute-start) | collective-permute-done | bytes 133152 | tf_op jit(solution)/shard_map/ppermute | solution.py:278
  11.9 0.0 collective-permute-start.1
  11.9 0.0 collective-permute-done.2.refs_6_
  11.9 0.5 %collective-permute-start.3 = (bf16[8,8320]{1,0:T(8,128)(2,1)S(1)}, bf16[8,8320]{1,0:T(8,128)(2,1)S(1)}, u32[]{:S(2)}, u32[]{:S(2)}) collective-permute-start(bf16[8,8320]{1,0:T(8,128)(2,1)S(1)} %collective-permute-done.2.refs_6_), channel_id=1, source_target_pairs={{0,4},{4,0},{8,12},{12,8},{16,20},{20,16},{24,28},{28,24},{1,5},{5... | collective-permute-start | bytes 399368 | tf_op jit(solution)/shard_map/ppermute | solution.py:233
  12.4 0.2 collective-permute-done.4.refs_7_
  12.6 0.1 collective-permute-start.5
  13.4 0.0 collective-permute-done.6.refs_8_
  13.4 0.0 collective-permute-done.1.refs_2_
  13.4 0.0 collective-permute-done.3.refs_3_
  13.4 0.5 %collective-permute-done.5.refs_4_ = bf16[8,8320]{1,0:T(8,128)(2,1)S(1)} collective-permute-done((bf16[8,8320]{1,0:T(8,128)(2,1)S(1)}, bf16[8,8320]{1,0:T(8,128)(2,1)S(1)}, u32[]{:S(2)}, u32[]{:S(2)}) %collective-permute-start.5) | collective-permute-done | bytes 133152 | tf_op jit(solution)/shard_map/ppermute | solution.py:233
  14.0 1.8 %shard_map.75 = (f32[4,16,128]{2,1,0:T(8,128)S(1)}, f32[4,16,128]{2,1,0:T(8,128)S(1)}, f32[8,256]{1,0:T(8,128)S(1)}) custom-call(s32[1]{0:T(128)S(6)} %copy.10.refs_0_, f32[8,256]{1,0:T(8,128)S(1)} %get-tuple-element.17.refs_1_, bf16[8,8320]{1,0:T(8,128)(2,1)S(1)} %collective-permute-done.1.refs_2_, bf16[8,8320]{1,0:T(8,128)(2,1)S(1)} %collective-permute-done.3.refs_3_, ...), custom_call_target="tpu_custom_call" | custom-call | tf_op jit(solution)/shard_map/pallas_call | solution.py:284
  15.7 0.2 collective-permute-start.7
  15.9 1.1 %collective-permute-done.7 = f32[4,16,128]{2,1,0:T(8,128)S(1)} collective-permute-done((f32[4,16,128]{2,1,0:T(8,128)S(1)}, f32[4,16,128]{2,1,0:T(8,128)S(1)}, u32[]{:S(2)}, u32[]{:S(2)}) %collective-permute-start.7) | collective-permute-done | bytes 32800 | tf_op jit(solution)/shard_map/ppermute | solution.py:233
  17.0 2.9 %collective-permute-start.10 = (f32[2,16,128]{2,1,0:T(8,128)S(1)}, f32[2,16,128]{2,1,0:T(8,128)S(1)}, u32[]{:S(2)}, u32[]{:S(2)}) collective-permute-start(f32[2,16,128]{2,1,0:T(8,128)S(1)} %pad_maximum_fusion.3), channel_id=1, source_target_pairs={{0,28},{4,24},{8,20},{12,16},{16,12},{20,8},{24,4},{28,0},{1,29},{... | collective-permute-start | bytes 49160 | tf_op jit(solution)/shard_map/ppermute | solution.py:233
  19.9 0.0 collective-permute-start.9
  19.9 0.7 %collective-permute-start.8 = (f32[2,16,128]{2,1,0:T(8,128)S(1)}, f32[2,16,128]{2,1,0:T(8,128)S(1)}, u32[]{:S(2)}, u32[]{:S(2)}) collective-permute-start(f32[2,16,128]{2,1,0:T(8,128)S(1)} %pad_maximum_fusion.1), channel_id=1, source_target_pairs={{0,12},{4,8},{8,4},{12,0},{16,28},{20,24},{24,20},{28,16},{1,13},{... | collective-permute-start | bytes 49160 | tf_op jit(solution)/shard_map/ppermute | solution.py:233
  20.6 0.7 %collective-permute-done.10.refs_3_ = f32[2,16,128]{2,1,0:T(8,128)S(1)} collective-permute-done((f32[2,16,128]{2,1,0:T(8,128)S(1)}, f32[2,16,128]{2,1,0:T(8,128)S(1)}, u32[]{:S(2)}, u32[]{:S(2)}) %collective-permute-start.10) | collective-permute-done | bytes 16416 | tf_op jit(solution)/shard_map/ppermute | solution.py:233
  21.3 1.7 %collective-permute-done.9.refs_2_ = f32[2,16,128]{2,1,0:T(8,128)S(1)} collective-permute-done((f32[2,16,128]{2,1,0:T(8,128)S(1)}, f32[2,16,128]{2,1,0:T(8,128)S(1)}, u32[]{:S(2)}, u32[]{:S(2)}) %collective-permute-start.9) | collective-permute-done | bytes 16416 | tf_op jit(solution)/shard_map/ppermute | solution.py:233
  23.0 0.1 collective-permute-done.8.refs_1_
  23.1 0.5 %shard_map.76 = (f32[32,128]{1,0:T(8,128)S(1)}, f32[32,128]{1,0:T(8,128)S(1)}, f32[32,128]{1,0:T(8,128)S(1)}, f32[32,128]{1,0:T(8,128)S(1)}) custom-call(f32[8,256]{1,0:T(8,128)S(1)} %get-tuple-element.22.found_ref, f32[2,16,128]{2,1,0:T(8,128)S(1)} %pad_maximum_fusion.refs_0_, f32[2,16,128]{2,1,0:T(8,128)S(1)} %collective-permute-done.8.refs_1_, ...), custom_call_target="tpu_custom_call" | custom-call | tf_op jit(solution)/shard_map/pallas_call | solution.py:303
  23.6 1.6 %collective-permute-start.11 = (f32[32,128]{1,0:T(8,128)S(1)}, f32[32,128]{1,0:T(8,128)S(1)}, u32[]{:S(2)}, u32[]{:S(2)}) collective-permute-start(f32[32,128]{1,0:T(8,128)S(1)} %get-tuple-element.26), channel_id=1, source_target_pairs={{0,1},{1,2},{2,3},{3,0},{4,5},{5,6},{6,7},{7,4},{8,9},{9,10},{10,1... | collective-permute-start | bytes 49160 | tf_op jit(solution)/shard_map/ppermute | solution.py:312
  25.2 2.6 %collective-permute-start.12 = (f32[32,128]{1,0:T(8,128)S(1)}, f32[32,128]{1,0:T(8,128)S(1)}, u32[]{:S(2)}, u32[]{:S(2)}) collective-permute-start(f32[32,128]{1,0:T(8,128)S(1)} %get-tuple-element.27), channel_id=1, source_target_pairs={{0,2},{1,3},{2,0},{3,1},{4,6},{5,7},{6,4},{7,5},{8,10},{9,11},{10,... | collective-permute-start | bytes 49160 | tf_op jit(solution)/shard_map/ppermute | solution.py:312
  27.8 1.3 %collective-permute-start.13 = (f32[32,128]{1,0:T(8,128)S(1)}, f32[32,128]{1,0:T(8,128)S(1)}, u32[]{:S(2)}, u32[]{:S(2)}) collective-permute-start(f32[32,128]{1,0:T(8,128)S(1)} %get-tuple-element.28), channel_id=1, source_target_pairs={{0,3},{1,0},{2,1},{3,2},{4,7},{5,4},{6,5},{7,6},{8,11},{9,8},{10,9... | collective-permute-start | bytes 49160 | tf_op jit(solution)/shard_map/ppermute | solution.py:312
  29.1 0.0 collective-permute-done.11
  29.1 0.7 %collective-permute-done.12 = f32[32,128]{1,0:T(8,128)S(1)} collective-permute-done((f32[32,128]{1,0:T(8,128)S(1)}, f32[32,128]{1,0:T(8,128)S(1)}, u32[]{:S(2)}, u32[]{:S(2)}) %collective-permute-start.12) | collective-permute-done | bytes 16416 | tf_op jit(solution)/shard_map/ppermute | solution.py:312
  29.8 1.7 %collective-permute-done.13 = f32[32,128]{1,0:T(8,128)S(1)} collective-permute-done((f32[32,128]{1,0:T(8,128)S(1)}, f32[32,128]{1,0:T(8,128)S(1)}, u32[]{:S(2)}, u32[]{:S(2)}) %collective-permute-start.13) | collective-permute-done | bytes 16416 | tf_op jit(solution)/shard_map/ppermute | solution.py:312
  31.5 0.1 fusion.2
  31.6 0.6 %maximum_bitcast_fusion = f32[1,64,64]{2,1,0:T(8,128)} fusion(f32[32,64]{1,0:T(8,128)S(1)} %get-tuple-element.38, f32[32,64]{1,0:T(8,128)S(1)} %get-tuple-element.37), kind=kLoop, calls=%fused_computation | loop fusion | flops 4096 | bytes 32768 | tf_op jit(solution)/shard_map/broadcast_in_dim | solution.py:313
  (7 shorter events, 0.0 us)
Async XLA Ops:
  2.2 9.7 %collective-permute-start = (bf16[8,8320]{1,0:T(8,128)(2,1)S(1)}, bf16[8,8320]{1,0:T(8,128)(2,1)S(1)}, u32[]{:S(2)}, u32[]{:S(2)}) collective-permute-start(bf16[8,8320]{1,0:T(8,128)(2,1)S(1)} %get-tuple-element.18.refs_9_), channel_id=1, source_target_pairs={{0,16},{4,12},{8,24},{12,4},{16,0},{20,28},{24,8},{28,20},{1,17},{... | collective-permute-start | bytes 399368 | tf_op jit(solution)/shard_map/ppermute | solution.py:278
  5.2 6.7 %collective-permute-start.2 = (bf16[8,8320]{1,0:T(8,128)(2,1)S(1)}, bf16[8,8320]{1,0:T(8,128)(2,1)S(1)}, u32[]{:S(2)}, u32[]{:S(2)}) collective-permute-start(bf16[8,8320]{1,0:T(8,128)(2,1)S(1)} %get-tuple-element.18.refs_9_), channel_id=1, source_target_pairs={{0,24},{4,28},{8,16},{12,20},{16,8},{20,12},{24,0},{28,4},{1,25},{... | collective-permute-start | bytes 399368 | tf_op jit(solution)/shard_map/ppermute | solution.py:278
  6.7 6.0 %collective-permute-start.4 = (bf16[8,8320]{1,0:T(8,128)(2,1)S(1)}, bf16[8,8320]{1,0:T(8,128)(2,1)S(1)}, u32[]{:S(2)}, u32[]{:S(2)}) collective-permute-start(bf16[8,8320]{1,0:T(8,128)(2,1)S(1)} %get-tuple-element.18.refs_9_), channel_id=1, source_target_pairs={{0,8},{4,20},{8,0},{12,28},{16,24},{20,4},{24,16},{28,12},{1,9},{5... | collective-permute-start | bytes 399368 | tf_op jit(solution)/shard_map/ppermute | solution.py:278
  9.0 4.4 %collective-permute-start.6 = (bf16[8,8320]{1,0:T(8,128)(2,1)S(1)}, bf16[8,8320]{1,0:T(8,128)(2,1)S(1)}, u32[]{:S(2)}, u32[]{:S(2)}) collective-permute-start(bf16[8,8320]{1,0:T(8,128)(2,1)S(1)} %get-tuple-element.20), channel_id=1, source_target_pairs={{0,4},{4,0},{8,12},{12,8},{16,20},{20,16},{24,28},{28,24},{1,5},{5... | collective-permute-start | bytes 399368 | tf_op jit(solution)/shard_map/ppermute | solution.py:233
  11.9 1.5 %collective-permute-start.1 = (bf16[8,8320]{1,0:T(8,128)(2,1)S(1)}, bf16[8,8320]{1,0:T(8,128)(2,1)S(1)}, u32[]{:S(2)}, u32[]{:S(2)}) collective-permute-start(bf16[8,8320]{1,0:T(8,128)(2,1)S(1)} %collective-permute-done.refs_5_), channel_id=1, source_target_pairs={{0,4},{4,0},{8,12},{12,8},{16,20},{20,16},{24,28},{28,24},{1,5},{5... | collective-permute-start | bytes 399368 | tf_op jit(solution)/shard_map/ppermute | solution.py:233
  11.9 1.5 %collective-permute-start.3 = (bf16[8,8320]{1,0:T(8,128)(2,1)S(1)}, bf16[8,8320]{1,0:T(8,128)(2,1)S(1)}, u32[]{:S(2)}, u32[]{:S(2)}) collective-permute-start(bf16[8,8320]{1,0:T(8,128)(2,1)S(1)} %collective-permute-done.2.refs_6_), channel_id=1, source_target_pairs={{0,4},{4,0},{8,12},{12,8},{16,20},{20,16},{24,28},{28,24},{1,5},{5... | collective-permute-start | bytes 399368 | tf_op jit(solution)/shard_map/ppermute | solution.py:233
  12.6 1.4 %collective-permute-start.5 = (bf16[8,8320]{1,0:T(8,128)(2,1)S(1)}, bf16[8,8320]{1,0:T(8,128)(2,1)S(1)}, u32[]{:S(2)}, u32[]{:S(2)}) collective-permute-start(bf16[8,8320]{1,0:T(8,128)(2,1)S(1)} %collective-permute-done.4.refs_7_), channel_id=1, source_target_pairs={{0,4},{4,0},{8,12},{12,8},{16,20},{20,16},{24,28},{28,24},{1,5},{5... | collective-permute-start | bytes 399368 | tf_op jit(solution)/shard_map/ppermute | solution.py:233
  15.7 1.3 %collective-permute-start.7 = (f32[4,16,128]{2,1,0:T(8,128)S(1)}, f32[4,16,128]{2,1,0:T(8,128)S(1)}, u32[]{:S(2)}, u32[]{:S(2)}) collective-permute-start(f32[4,16,128]{2,1,0:T(8,128)S(1)} %get-tuple-element.24), channel_id=1, source_target_pairs={{0,4},{4,0},{8,12},{12,8},{16,20},{20,16},{24,28},{28,24},{1,5},{5... | collective-permute-start | bytes 98312 | tf_op jit(solution)/shard_map/ppermute | solution.py:233
  17.0 4.3 %collective-permute-start.10 = (f32[2,16,128]{2,1,0:T(8,128)S(1)}, f32[2,16,128]{2,1,0:T(8,128)S(1)}, u32[]{:S(2)}, u32[]{:S(2)}) collective-permute-start(f32[2,16,128]{2,1,0:T(8,128)S(1)} %pad_maximum_fusion.3), channel_id=1, source_target_pairs={{0,28},{4,24},{8,20},{12,16},{16,12},{20,8},{24,4},{28,0},{1,29},{... | collective-permute-start | bytes 49160 | tf_op jit(solution)/shard_map/ppermute | solution.py:233
  19.9 3.2 %collective-permute-start.9 = (f32[2,16,128]{2,1,0:T(8,128)S(1)}, f32[2,16,128]{2,1,0:T(8,128)S(1)}, u32[]{:S(2)}, u32[]{:S(2)}) collective-permute-start(f32[2,16,128]{2,1,0:T(8,128)S(1)} %pad_maximum_fusion.2), channel_id=1, source_target_pairs={{0,20},{4,16},{8,28},{12,24},{16,4},{20,0},{24,12},{28,8},{1,21},{... | collective-permute-start | bytes 49160 | tf_op jit(solution)/shard_map/ppermute | solution.py:233
  19.9 3.2 %collective-permute-start.8 = (f32[2,16,128]{2,1,0:T(8,128)S(1)}, f32[2,16,128]{2,1,0:T(8,128)S(1)}, u32[]{:S(2)}, u32[]{:S(2)}) collective-permute-start(f32[2,16,128]{2,1,0:T(8,128)S(1)} %pad_maximum_fusion.1), channel_id=1, source_target_pairs={{0,12},{4,8},{8,4},{12,0},{16,28},{20,24},{24,20},{28,16},{1,13},{... | collective-permute-start | bytes 49160 | tf_op jit(solution)/shard_map/ppermute | solution.py:233
  23.6 5.6 %collective-permute-start.11 = (f32[32,128]{1,0:T(8,128)S(1)}, f32[32,128]{1,0:T(8,128)S(1)}, u32[]{:S(2)}, u32[]{:S(2)}) collective-permute-start(f32[32,128]{1,0:T(8,128)S(1)} %get-tuple-element.26), channel_id=1, source_target_pairs={{0,1},{1,2},{2,3},{3,0},{4,5},{5,6},{6,7},{7,4},{8,9},{9,10},{10,1... | collective-permute-start | bytes 49160 | tf_op jit(solution)/shard_map/ppermute | solution.py:312
  25.2 4.6 %collective-permute-start.12 = (f32[32,128]{1,0:T(8,128)S(1)}, f32[32,128]{1,0:T(8,128)S(1)}, u32[]{:S(2)}, u32[]{:S(2)}) collective-permute-start(f32[32,128]{1,0:T(8,128)S(1)} %get-tuple-element.27), channel_id=1, source_target_pairs={{0,2},{1,3},{2,0},{3,1},{4,6},{5,7},{6,4},{7,5},{8,10},{9,11},{10,... | collective-permute-start | bytes 49160 | tf_op jit(solution)/shard_map/ppermute | solution.py:312
  27.8 3.7 %collective-permute-start.13 = (f32[32,128]{1,0:T(8,128)S(1)}, f32[32,128]{1,0:T(8,128)S(1)}, u32[]{:S(2)}, u32[]{:S(2)}) collective-permute-start(f32[32,128]{1,0:T(8,128)S(1)} %get-tuple-element.28), channel_id=1, source_target_pairs={{0,3},{1,0},{2,1},{3,2},{4,7},{5,4},{6,5},{7,6},{8,11},{9,8},{10,9... | collective-permute-start | bytes 49160 | tf_op jit(solution)/shard_map/ppermute | solution.py:312

commit v19 on v17

--- a/solution.py
+++ b/solution.py
@@ -12,6 +12,7 @@
 HBM = pl.BlockSpec(memory_space=pltpu.HBM)
 LANES = 128
 CHUNKS = 4
+LOADS = 8
 
 
 def iota(shape, dimension):
@@ -130,17 +131,26 @@
     found_ref[...] = jnp.concatenate([holder, rank_there, jnp.zeros((6, slots), jnp.float32)], axis=0)
 
 
-def load_kernel(block_ref, source_ref, same_block_ref, target_ref, arrived):
-    copy = pltpu.make_async_copy(source_ref, target_ref, arrived)
-    copy.start()
-    copy.wait()
+def load_kernel(block_ref, source_ref, same_block_ref, target_ref, landing, arrived):
+    step = landing.shape[1] // LOADS
+    copies = [
+        pltpu.make_async_copy(
+            source_ref.at[:, pl.ds(i * step, step)], landing.at[:, pl.ds(i * step, step)], arrived.at[i]
+        )
+        for i in range(LOADS)
+    ]
+    for copy in copies:
+        copy.start()
+    for i, copy in enumerate(copies):
+        copy.wait()
+        target_ref[i * step:(i + 1) * step, :] = landing[:, i * step:(i + 1) * step].T
 
 
 def score_kernel(holders, capacity, *refs):
     count_ref, found_ref, packed_refs = *refs[:2], refs[2:2 + holders][::-1]
     pages_ref, keep_ref, send_ref, used_ref, total, queries = refs[2 + holders:]
     me = lax.axis_index("store")
-    count, width = pages_ref.shape
+    width, count = pages_ref.shape
     rows = packed_refs[0].shape[0]
     half = capacity // 2
     step = width // CHUNKS
@@ -149,9 +159,7 @@
         columns = slice(i * step, (i + 1) * step)
         for k in range(holders):
             queries[k * rows:(k + 1) * rows, columns] = packed_refs[k][:, columns]
-        scores = scores + lax.dot_general(
-            queries[:, columns], pages_ref[:, columns], (((1,), (1,)), ((), ())), preferred_element_type=jnp.float32
-        )
+        scores = scores + jnp.dot(queries[:, columns], pages_ref[columns], preferred_element_type=jnp.float32)
     for k in range(holders):
         start = pl.multiple_of((me ^ k) * rows, rows)
         total[pl.ds(start, rows), :] = scores[k * rows:(k + 1) * rows]
@@ -248,12 +256,12 @@
 
     again, pages = pl.pallas_call(
         load_kernel,
-        out_shape=[jax.ShapeDtypeStruct(again.shape, bf16), pltpu.VMEM(page_store.shape, bf16)],
+        out_shape=[jax.ShapeDtypeStruct(again.shape, bf16), pltpu.VMEM((width, per_holder), bf16)],
         in_specs=[VMEM, HBM],
         out_specs=[VMEM] * 2,
         input_output_aliases={0: 0},
-        scratch_shapes=[pltpu.SemaphoreType.DMA(())],
-        compiler_params=pltpu.CompilerParams(vmem_limit_bytes=2 * 2**20),
+        scratch_shapes=[pltpu.VMEM(page_store.shape, bf16), pltpu.SemaphoreType.DMA((LOADS,))],
+        compiler_params=pltpu.CompilerParams(vmem_limit_bytes=4 * 2**20 + 4 * per_holder * width),
         cost_estimate=pl.CostEstimate(flops=0, bytes_accessed=2 * page_store.size, transcendentals=0),
     )(again, pltpu.with_memory_space_constraint(page_store, pltpu.HBM))
 

time: 32.4 us -> 31.9 us (0.985)
  waiting for transfers between devices: 10.3 us -> 9.89 us
    pallas_call x1, Pallas kernels: 1.74 us -> 1.2 us  [on_device(): pl.pallas_call(functools.partial(score_kernel, holders, capacity), out_sh...]
    pallas_call x1, Pallas kernels: 2.2 us -> 2.65 us  [on_device(): pl.pallas_call(load_kernel, out_shape=[jax.ShapeDtypeStruct(again.shape,...]
    ppermute x11, waiting for transfers between devices: 7.94 us -> 7.5 us  [swap(): lax.ppermute(value, axis, [(i, i ^ distance) for i in range(lax.axis_size...]
  transfers between devices with their start and end apart: 14 -> 14, of which waited for: 11 -> 11; matrix products, arithmetic and copies ran while one was open for 0% -> 0% of each run, Pallas kernels for 7% -> 8%
where the time goes in v19:
time: 31.9 us; the launch traced here: 31.7 us
  starting transfers between devices  13.9 us (44%)
  waiting for transfers between devices  9.89 us (31%)
  Pallas kernels  6.48 us (20%)
  between operations  0.72 us (2%)
  other arithmetic  0.64 us (2%)
    ppermute x11, starting transfers between devices, swap(): lax.ppermute(value, axis, [(i, i ^ distance) for i in range(lax.axis_size...  8.36 us
    ppermute x11, waiting for transfers between devices, swap(): lax.ppermute(value, axis, [(i, i ^ distance) for i in range(lax.axis_size...  7.5 us
    ppermute x3, starting transfers between devices, on_device(): lax.ppermute(terms[step], 'layer', [(g, (g + step) % groups) for g in ran...  5.57 us
    pallas_call x1, Pallas kernels, on_device(): pl.pallas_call(load_kernel, out_shape=[jax.ShapeDtypeStruct(again.shape,...  2.65 us
    ppermute x3, waiting for transfers between devices, on_device(): lax.ppermute(terms[step], 'layer', [(g, (g + step) % groups) for g in ran...  2.39 us
    pallas_call x1, Pallas kernels, on_device(): pl.pallas_call(functools.partial(condition_kernel, holders, capacity, per...  2.18 us
    pallas_call x1, Pallas kernels, on_device(): pl.pallas_call(functools.partial(score_kernel, holders, capacity), out_sh...  1.2 us
  transfers between devices with their start and end apart: 14, of which 11 were waited for; matrix products, arithmetic and copies ran while one was open for 0% of the time, Pallas kernels for 8%

profile of v19, /device:TPU:0, one launch (start us, length us, event | category | flops | bytes accessed | tf_op | source)
XLA Modules:
  0.0 31.7 jit_solution(3907657840555078233)
XLA Ops:
  0.0 2.2 %shard_map.73 = (bf16[8,8320]{1,0:T(8,128)(2,1)S(1)}, bf16[8,8320]{1,0:T(8,128)(2,1)S(1)}, f32[8,256]{1,0:T(8,128)S(1)}) custom-call(bf16[8,8192]{1,0:T(8,128)(2,1)} %refs_0_.2, f32[2,64,64]{2,1,0:T(8,128)} %refs_1_.1, f32[2,64,64]{2,1,0:T(8,128)} %refs_2_.1, s32[16,128]{1,0:T(8,128)} %bitcast.3, s32[1,256]{1,0:T(1,128)} %refs_4_.1), custom_call_target="tpu_custom_call" | custom-call | tf_op jit(solution)/shard_map/pallas_call | solution.py:243
  2.2 4.0 %collective-permute-start = (bf16[8,8320]{1,0:T(8,128)(2,1)S(1)}, bf16[8,8320]{1,0:T(8,128)(2,1)S(1)}, u32[]{:S(2)}, u32[]{:S(2)}) collective-permute-start(bf16[8,8320]{1,0:T(8,128)(2,1)S(1)} %get-tuple-element.18.refs_9_), channel_id=1, source_target_pairs={{0,24},{4,28},{8,16},{12,20},{16,8},{20,12},{24,0},{28,4},{1,25},{... | collective-permute-start | bytes 399368 | tf_op jit(solution)/shard_map/ppermute | solution.py:224
  6.2 0.5 %collective-permute-start.2 = (bf16[8,8320]{1,0:T(8,128)(2,1)S(1)}, bf16[8,8320]{1,0:T(8,128)(2,1)S(1)}, u32[]{:S(2)}, u32[]{:S(2)}) collective-permute-start(bf16[8,8320]{1,0:T(8,128)(2,1)S(1)} %get-tuple-element.18.refs_9_), channel_id=1, source_target_pairs={{0,16},{4,20},{8,24},{12,28},{16,0},{20,4},{24,8},{28,12},{1,17},{... | collective-permute-start | bytes 399368 | tf_op jit(solution)/shard_map/ppermute | solution.py:224
  6.7 0.1 collective-permute-start.4
  6.8 2.6 %shard_map.74 = (bf16[8,8320]{1,0:T(8,128)(2,1)S(1)}, bf16[8192,256]{1,0:T(8,128)(2,1)S(1)}) custom-call(bf16[8,8320]{1,0:T(8,128)(2,1)S(1)} %get-tuple-element.19.block_ref, bf16[256,8192]{1,0:T(8,128)(2,1)} %source_ref.1), custom_call_target="tpu_custom_call", output_to_operand_aliasing={{0}: (0, {})} | custom-call | bytes 4194304 | tf_op jit(solution)/shard_map/pallas_call | solution.py:257
  9.4 0.1 collective-permute-start.6
  9.5 0.6 %collective-permute-done.refs_3_ = bf16[8,8320]{1,0:T(8,128)(2,1)S(1)} collective-permute-done((bf16[8,8320]{1,0:T(8,128)(2,1)S(1)}, bf16[8,8320]{1,0:T(8,128)(2,1)S(1)}, u32[]{:S(2)}, u32[]{:S(2)}) %collective-permute-start) | collective-permute-done | bytes 133152 | tf_op jit(solution)/shard_map/ppermute | solution.py:224
  10.1 0.0 collective-permute-start.1
  10.1 2.4 %collective-permute-done.2.refs_5_ = bf16[8,8320]{1,0:T(8,128)(2,1)S(1)} collective-permute-done((bf16[8,8320]{1,0:T(8,128)(2,1)S(1)}, bf16[8,8320]{1,0:T(8,128)(2,1)S(1)}, u32[]{:S(2)}, u32[]{:S(2)}) %collective-permute-start.2) | collective-permute-done | bytes 133152 | tf_op jit(solution)/shard_map/ppermute | solution.py:224
  12.5 0.0 collective-permute-start.3
  12.5 0.2 collective-permute-done.4.refs_7_
  12.8 0.3 collective-permute-start.5
  13.7 0.0 collective-permute-done.6.refs_8_
  13.7 0.0 collective-permute-done.1.refs_2_
  13.7 0.2 collective-permute-done.3.refs_4_
  13.9 0.3 collective-permute-done.5.refs_6_
  14.1 1.2 %shard_map.75 = (f32[4,16,128]{2,1,0:T(8,128)S(1)}, f32[4,16,128]{2,1,0:T(8,128)S(1)}, f32[8,256]{1,0:T(8,128)S(1)}) custom-call(s32[1]{0:T(128)S(6)} %copy.10.refs_0_, f32[8,256]{1,0:T(8,128)S(1)} %get-tuple-element.17.refs_1_, bf16[8,8320]{1,0:T(8,128)(2,1)S(1)} %collective-permute-done.1.refs_2_, bf16[8,8320]{1,0:T(8,128)(2,1)S(1)} %collective-permute-done.refs_3_, ...), custom_call_target="tpu_custom_call" | custom-call | tf_op jit(solution)/shard_map/pallas_call | solution.py:278
  15.3 0.3 %collective-permute-start.7 = (f32[4,16,128]{2,1,0:T(8,128)S(1)}, f32[4,16,128]{2,1,0:T(8,128)S(1)}, u32[]{:S(2)}, u32[]{:S(2)}) collective-permute-start(f32[4,16,128]{2,1,0:T(8,128)S(1)} %get-tuple-element.24), channel_id=1, source_target_pairs={{0,4},{4,0},{8,12},{12,8},{16,20},{20,16},{24,28},{28,24},{1,5},{5... | collective-permute-start | bytes 98312 | tf_op jit(solution)/shard_map/ppermute | solution.py:224
  15.7 0.9 %collective-permute-done.7 = f32[4,16,128]{2,1,0:T(8,128)S(1)} collective-permute-done((f32[4,16,128]{2,1,0:T(8,128)S(1)}, f32[4,16,128]{2,1,0:T(8,128)S(1)}, u32[]{:S(2)}, u32[]{:S(2)}) %collective-permute-start.7) | collective-permute-done | bytes 32800 | tf_op jit(solution)/shard_map/ppermute | solution.py:224
  16.6 1.7 %collective-permute-start.10 = (f32[2,16,128]{2,1,0:T(8,128)S(1)}, f32[2,16,128]{2,1,0:T(8,128)S(1)}, u32[]{:S(2)}, u32[]{:S(2)}) collective-permute-start(f32[2,16,128]{2,1,0:T(8,128)S(1)} %pad_maximum_fusion.3), channel_id=1, source_target_pairs={{0,28},{4,24},{8,20},{12,16},{16,12},{20,8},{24,4},{28,0},{1,29},{... | collective-permute-start | bytes 49160 | tf_op jit(solution)/shard_map/ppermute | solution.py:224
  18.3 1.1 %collective-permute-start.9 = (f32[2,16,128]{2,1,0:T(8,128)S(1)}, f32[2,16,128]{2,1,0:T(8,128)S(1)}, u32[]{:S(2)}, u32[]{:S(2)}) collective-permute-start(f32[2,16,128]{2,1,0:T(8,128)S(1)} %pad_maximum_fusion.2), channel_id=1, source_target_pairs={{0,20},{4,16},{8,28},{12,24},{16,4},{20,0},{24,12},{28,8},{1,21},{... | collective-permute-start | bytes 49160 | tf_op jit(solution)/shard_map/ppermute | solution.py:224
  19.4 0.3 collective-permute-start.8
  19.7 1.0 %collective-permute-done.10.refs_3_ = f32[2,16,128]{2,1,0:T(8,128)S(1)} collective-permute-done((f32[2,16,128]{2,1,0:T(8,128)S(1)}, f32[2,16,128]{2,1,0:T(8,128)S(1)}, u32[]{:S(2)}, u32[]{:S(2)}) %collective-permute-start.10) | collective-permute-done | bytes 16416 | tf_op jit(solution)/shard_map/ppermute | solution.py:224
  20.7 0.8 %collective-permute-done.9.refs_2_ = f32[2,16,128]{2,1,0:T(8,128)S(1)} collective-permute-done((f32[2,16,128]{2,1,0:T(8,128)S(1)}, f32[2,16,128]{2,1,0:T(8,128)S(1)}, u32[]{:S(2)}, u32[]{:S(2)}) %collective-permute-start.9) | collective-permute-done | bytes 16416 | tf_op jit(solution)/shard_map/ppermute | solution.py:224
  21.5 1.1 %collective-permute-done.8.refs_1_ = f32[2,16,128]{2,1,0:T(8,128)S(1)} collective-permute-done((f32[2,16,128]{2,1,0:T(8,128)S(1)}, f32[2,16,128]{2,1,0:T(8,128)S(1)}, u32[]{:S(2)}, u32[]{:S(2)}) %collective-permute-start.8) | collective-permute-done | bytes 16416 | tf_op jit(solution)/shard_map/ppermute | solution.py:224
  22.6 0.4 %shard_map.76 = (f32[32,128]{1,0:T(8,128)S(1)}, f32[32,128]{1,0:T(8,128)S(1)}, f32[32,128]{1,0:T(8,128)S(1)}, f32[32,128]{1,0:T(8,128)S(1)}) custom-call(f32[8,256]{1,0:T(8,128)S(1)} %get-tuple-element.22.found_ref, f32[2,16,128]{2,1,0:T(8,128)S(1)} %pad_maximum_fusion.refs_0_, f32[2,16,128]{2,1,0:T(8,128)S(1)} %collective-permute-done.8.refs_1_, ...), custom_call_target="tpu_custom_call" | custom-call | tf_op jit(solution)/shard_map/pallas_call | solution.py:297
  23.1 1.6 %collective-permute-start.11 = (f32[32,128]{1,0:T(8,128)S(1)}, f32[32,128]{1,0:T(8,128)S(1)}, u32[]{:S(2)}, u32[]{:S(2)}) collective-permute-start(f32[32,128]{1,0:T(8,128)S(1)} %get-tuple-element.26), channel_id=1, source_target_pairs={{0,1},{1,2},{2,3},{3,0},{4,5},{5,6},{6,7},{7,4},{8,9},{9,10},{10,1... | collective-permute-start | bytes 49160 | tf_op jit(solution)/shard_map/ppermute | solution.py:306
  24.7 2.6 %collective-permute-start.12 = (f32[32,128]{1,0:T(8,128)S(1)}, f32[32,128]{1,0:T(8,128)S(1)}, u32[]{:S(2)}, u32[]{:S(2)}) collective-permute-start(f32[32,128]{1,0:T(8,128)S(1)} %get-tuple-element.27), channel_id=1, source_target_pairs={{0,2},{1,3},{2,0},{3,1},{4,6},{5,7},{6,4},{7,5},{8,10},{9,11},{10,... | collective-permute-start | bytes 49160 | tf_op jit(solution)/shard_map/ppermute | solution.py:306
  27.3 1.3 %collective-permute-start.13 = (f32[32,128]{1,0:T(8,128)S(1)}, f32[32,128]{1,0:T(8,128)S(1)}, u32[]{:S(2)}, u32[]{:S(2)}) collective-permute-start(f32[32,128]{1,0:T(8,128)S(1)} %get-tuple-element.28), channel_id=1, source_target_pairs={{0,3},{1,0},{2,1},{3,2},{4,7},{5,4},{6,5},{7,6},{8,11},{9,8},{10,9... | collective-permute-start | bytes 49160 | tf_op jit(solution)/shard_map/ppermute | solution.py:306
  28.6 0.0 collective-permute-done.11
  28.7 0.7 %collective-permute-done.12 = f32[32,128]{1,0:T(8,128)S(1)} collective-permute-done((f32[32,128]{1,0:T(8,128)S(1)}, f32[32,128]{1,0:T(8,128)S(1)}, u32[]{:S(2)}, u32[]{:S(2)}) %collective-permute-start.12) | collective-permute-done | bytes 16416 | tf_op jit(solution)/shard_map/ppermute | solution.py:306
  29.3 1.7 %collective-permute-done.13 = f32[32,128]{1,0:T(8,128)S(1)} collective-permute-done((f32[32,128]{1,0:T(8,128)S(1)}, f32[32,128]{1,0:T(8,128)S(1)}, u32[]{:S(2)}, u32[]{:S(2)}) %collective-permute-start.13) | collective-permute-done | bytes 16416 | tf_op jit(solution)/shard_map/ppermute | solution.py:306
  31.0 0.1 fusion.2
  31.1 0.6 %maximum_bitcast_fusion = f32[1,64,64]{2,1,0:T(8,128)} fusion(f32[32,64]{1,0:T(8,128)S(1)} %get-tuple-element.38, f32[32,64]{1,0:T(8,128)S(1)} %get-tuple-element.37), kind=kLoop, calls=%fused_computation | loop fusion | flops 4096 | bytes 32768 | tf_op jit(solution)/shard_map/broadcast_in_dim | solution.py:307
  (7 shorter events, 0.0 us)
Async XLA Ops:
  2.2 7.9 %collective-permute-start = (bf16[8,8320]{1,0:T(8,128)(2,1)S(1)}, bf16[8,8320]{1,0:T(8,128)(2,1)S(1)}, u32[]{:S(2)}, u32[]{:S(2)}) collective-permute-start(bf16[8,8320]{1,0:T(8,128)(2,1)S(1)} %get-tuple-element.18.refs_9_), channel_id=1, source_target_pairs={{0,24},{4,28},{8,16},{12,20},{16,8},{20,12},{24,0},{28,4},{1,25},{... | collective-permute-start | bytes 399368 | tf_op jit(solution)/shard_map/ppermute | solution.py:224
  6.2 6.4 %collective-permute-start.2 = (bf16[8,8320]{1,0:T(8,128)(2,1)S(1)}, bf16[8,8320]{1,0:T(8,128)(2,1)S(1)}, u32[]{:S(2)}, u32[]{:S(2)}) collective-permute-start(bf16[8,8320]{1,0:T(8,128)(2,1)S(1)} %get-tuple-element.18.refs_9_), channel_id=1, source_target_pairs={{0,16},{4,20},{8,24},{12,28},{16,0},{20,4},{24,8},{28,12},{1,17},{... | collective-permute-start | bytes 399368 | tf_op jit(solution)/shard_map/ppermute | solution.py:224
  6.7 6.1 %collective-permute-start.4 = (bf16[8,8320]{1,0:T(8,128)(2,1)S(1)}, bf16[8,8320]{1,0:T(8,128)(2,1)S(1)}, u32[]{:S(2)}, u32[]{:S(2)}) collective-permute-start(bf16[8,8320]{1,0:T(8,128)(2,1)S(1)} %get-tuple-element.18.refs_9_), channel_id=1, source_target_pairs={{0,8},{4,12},{8,0},{12,4},{16,24},{20,28},{24,16},{28,20},{1,9},{5... | collective-permute-start | bytes 399368 | tf_op jit(solution)/shard_map/ppermute | solution.py:224
  9.4 4.3 %collective-permute-start.6 = (bf16[8,8320]{1,0:T(8,128)(2,1)S(1)}, bf16[8,8320]{1,0:T(8,128)(2,1)S(1)}, u32[]{:S(2)}, u32[]{:S(2)}) collective-permute-start(bf16[8,8320]{1,0:T(8,128)(2,1)S(1)} %get-tuple-element.20), channel_id=1, source_target_pairs={{0,4},{4,0},{8,12},{12,8},{16,20},{20,16},{24,28},{28,24},{1,5},{5... | collective-permute-start | bytes 399368 | tf_op jit(solution)/shard_map/ppermute | solution.py:224
  10.1 3.6 %collective-permute-start.1 = (bf16[8,8320]{1,0:T(8,128)(2,1)S(1)}, bf16[8,8320]{1,0:T(8,128)(2,1)S(1)}, u32[]{:S(2)}, u32[]{:S(2)}) collective-permute-start(bf16[8,8320]{1,0:T(8,128)(2,1)S(1)} %collective-permute-done.refs_3_), channel_id=1, source_target_pairs={{0,4},{4,0},{8,12},{12,8},{16,20},{20,16},{24,28},{28,24},{1,5},{5... | collective-permute-start | bytes 399368 | tf_op jit(solution)/shard_map/ppermute | solution.py:224
  12.5 1.4 %collective-permute-start.3 = (bf16[8,8320]{1,0:T(8,128)(2,1)S(1)}, bf16[8,8320]{1,0:T(8,128)(2,1)S(1)}, u32[]{:S(2)}, u32[]{:S(2)}) collective-permute-start(bf16[8,8320]{1,0:T(8,128)(2,1)S(1)} %collective-permute-done.2.refs_5_), channel_id=1, source_target_pairs={{0,4},{4,0},{8,12},{12,8},{16,20},{20,16},{24,28},{28,24},{1,5},{5... | collective-permute-start | bytes 399368 | tf_op jit(solution)/shard_map/ppermute | solution.py:224
  12.8 1.4 %collective-permute-start.5 = (bf16[8,8320]{1,0:T(8,128)(2,1)S(1)}, bf16[8,8320]{1,0:T(8,128)(2,1)S(1)}, u32[]{:S(2)}, u32[]{:S(2)}) collective-permute-start(bf16[8,8320]{1,0:T(8,128)(2,1)S(1)} %collective-permute-done.4.refs_7_), channel_id=1, source_target_pairs={{0,4},{4,0},{8,12},{12,8},{16,20},{20,16},{24,28},{28,24},{1,5},{5... | collective-permute-start | bytes 399368 | tf_op jit(solution)/shard_map/ppermute | solution.py:224
  15.3 1.3 %collective-permute-start.7 = (f32[4,16,128]{2,1,0:T(8,128)S(1)}, f32[4,16,128]{2,1,0:T(8,128)S(1)}, u32[]{:S(2)}, u32[]{:S(2)}) collective-permute-start(f32[4,16,128]{2,1,0:T(8,128)S(1)} %get-tuple-element.24), channel_id=1, source_target_pairs={{0,4},{4,0},{8,12},{12,8},{16,20},{20,16},{24,28},{28,24},{1,5},{5... | collective-permute-start | bytes 98312 | tf_op jit(solution)/shard_map/ppermute | solution.py:224
  16.6 4.1 %collective-permute-start.10 = (f32[2,16,128]{2,1,0:T(8,128)S(1)}, f32[2,16,128]{2,1,0:T(8,128)S(1)}, u32[]{:S(2)}, u32[]{:S(2)}) collective-permute-start(f32[2,16,128]{2,1,0:T(8,128)S(1)} %pad_maximum_fusion.3), channel_id=1, source_target_pairs={{0,28},{4,24},{8,20},{12,16},{16,12},{20,8},{24,4},{28,0},{1,29},{... | collective-permute-start | bytes 49160 | tf_op jit(solution)/shard_map/ppermute | solution.py:224
  18.3 3.2 %collective-permute-start.9 = (f32[2,16,128]{2,1,0:T(8,128)S(1)}, f32[2,16,128]{2,1,0:T(8,128)S(1)}, u32[]{:S(2)}, u32[]{:S(2)}) collective-permute-start(f32[2,16,128]{2,1,0:T(8,128)S(1)} %pad_maximum_fusion.2), channel_id=1, source_target_pairs={{0,20},{4,16},{8,28},{12,24},{16,4},{20,0},{24,12},{28,8},{1,21},{... | collective-permute-start | bytes 49160 | tf_op jit(solution)/shard_map/ppermute | solution.py:224
  19.4 3.2 %collective-permute-start.8 = (f32[2,16,128]{2,1,0:T(8,128)S(1)}, f32[2,16,128]{2,1,0:T(8,128)S(1)}, u32[]{:S(2)}, u32[]{:S(2)}) collective-permute-start(f32[2,16,128]{2,1,0:T(8,128)S(1)} %pad_maximum_fusion.1), channel_id=1, source_target_pairs={{0,12},{4,8},{8,4},{12,0},{16,28},{20,24},{24,20},{28,16},{1,13},{... | collective-permute-start | bytes 49160 | tf_op jit(solution)/shard_map/ppermute | solution.py:224
  23.1 5.6 %collective-permute-start.11 = (f32[32,128]{1,0:T(8,128)S(1)}, f32[32,128]{1,0:T(8,128)S(1)}, u32[]{:S(2)}, u32[]{:S(2)}) collective-permute-start(f32[32,128]{1,0:T(8,128)S(1)} %get-tuple-element.26), channel_id=1, source_target_pairs={{0,1},{1,2},{2,3},{3,0},{4,5},{5,6},{6,7},{7,4},{8,9},{9,10},{10,1... | collective-permute-start | bytes 49160 | tf_op jit(solution)/shard_map/ppermute | solution.py:306
  24.7 4.6 %collective-permute-start.12 = (f32[32,128]{1,0:T(8,128)S(1)}, f32[32,128]{1,0:T(8,128)S(1)}, u32[]{:S(2)}, u32[]{:S(2)}) collective-permute-start(f32[32,128]{1,0:T(8,128)S(1)} %get-tuple-element.27), channel_id=1, source_target_pairs={{0,2},{1,3},{2,0},{3,1},{4,6},{5,7},{6,4},{7,5},{8,10},{9,11},{10,... | collective-permute-start | bytes 49160 | tf_op jit(solution)/shard_map/ppermute | solution.py:306
  27.3 3.7 %collective-permute-start.13 = (f32[32,128]{1,0:T(8,128)S(1)}, f32[32,128]{1,0:T(8,128)S(1)}, u32[]{:S(2)}, u32[]{:S(2)}) collective-permute-start(f32[32,128]{1,0:T(8,128)S(1)} %get-tuple-element.28), channel_id=1, source_target_pairs={{0,3},{1,0},{2,1},{3,2},{4,7},{5,4},{6,5},{7,6},{8,11},{9,8},{10,9... | collective-permute-start | bytes 49160 | tf_op jit(solution)/shard_map/ppermute | solution.py:306

commit v20 on v19

--- a/solution.py
+++ b/solution.py
@@ -30,6 +30,12 @@
         value = value - part.astype(jnp.float32)
         parts.append(part)
     return parts
+
+
+def exact_product(value, chosen):
+    rows = value.shape[0]
+    product = jnp.dot(jnp.concatenate(parts_of(value), axis=0), chosen, preferred_element_type=jnp.float32)
+    return product[2 * rows:] + product[rows:2 * rows] + product[:rows]
 
 
 def exact_bf16(value):
@@ -99,9 +105,9 @@
             done = jnp.where(low, ee, oo) + pltpu.roll(jnp.where(low, oe, eo), rank, 1)
             turned_ref[layer, pl.ds(q, half, stride=rows), :] = done
         for t in range(half):
-            packed_ref[:, (first + t) * LANES:(first + t + 1) * LANES] = (
-                turned_ref[layer, t * rows:(t + 1) * rows, :].astype(jnp.bfloat16)
-            )
+            tile = turned_ref[layer, t * rows:(t + 1) * rows, :].astype(jnp.bfloat16)
+            for target_ref in (packed_ref, again_ref):
+                target_ref[:, (first + t) * LANES:(first + t + 1) * LANES] = tile
 
     slots = cand_ref.shape[1]
     home_rows = home_ref.shape[0]
@@ -126,8 +132,8 @@
     spare = packed_ref.shape[1] - width - capacity * len(blocks)
     if spare:
         blocks.append(jnp.zeros((rows, spare), jnp.float32))
-    packed_ref[:, width:] = jnp.concatenate(blocks, axis=1).astype(jnp.bfloat16)
-    again_ref[...] = packed_ref[...]
+    for target_ref in (packed_ref, again_ref):
+        target_ref[:, width:] = jnp.concatenate(blocks, axis=1).astype(jnp.bfloat16)
     found_ref[...] = jnp.concatenate([holder, rank_there, jnp.zeros((6, slots), jnp.float32)], axis=0)
 
 
@@ -171,17 +177,15 @@
         for block in range(1, holders // rows):
             mine = jnp.where(me // rows == block, notes[:, block * capacity:(block + 1) * capacity], mine)
         asked.append(mine)
-    page = iota((count, holders * half), 0).astype(jnp.float32) + 1.0
-    parts = parts_of(total[...])[::-1]
-    picked = []
-    for side in range(2):
-        row = jnp.concatenate([row[:, side * half:(side + 1) * half] for row in asked], axis=1)
-        chosen = exact_bf16(page == row)
-        picked.append(sum(jnp.dot(part, chosen, preferred_element_type=jnp.float32) for part in parts))
+    wanted = jnp.concatenate(
+        [row[:, side * half:(side + 1) * half] for side in range(2) for row in asked], axis=1
+    )
+    chosen = exact_bf16(iota((count, 2 * holders * half), 0).astype(jnp.float32) + 1.0 == wanted)
+    picked = exact_product(total[...], chosen)
     used_ref[...] = found_ref[...]
     own_slots = found_ref.shape[1]
     used_ref[0:1] = jnp.where(iota((1, own_slots), 1) < count_ref[0], found_ref[0:1], float(holders))
-    picked = jnp.concatenate(picked, axis=0).T
+    picked = jnp.concatenate([picked[:, :holders * half], picked[:, holders * half:]], axis=0).T
     for place, k in enumerate(kept_distances(holders)):
         keep_ref[place] = picked[k * half:(k + 1) * half]
         send_ref[place] = picked[(k ^ 1) * half:((k ^ 1) + 1) * half]
@@ -198,16 +202,12 @@
     order = [k ^ core for k in kept_distances(holders) for core in range(2)]
     begins = sum(jnp.where(distance == k, place * half + 1, 0) for place, k in enumerate(order)).astype(jnp.float32) - 1.0
     rank_there = found_ref[1:2]
-    place = iota((holders * half, slots), 0).astype(jnp.float32)
-    parts = parts_of(jnp.concatenate([ref[core] for ref in landed_refs for core in range(2)], axis=0))[::-1]
-    result = jnp.zeros((total, slots), jnp.float32)
-    for side in range(2):
-        on_side = (rank_there >= half) if side else (rank_there < half)
-        target = jnp.where(on_side & (begins >= 0.0), begins + rank_there - side * half, -1.0)
-        chosen = exact_bf16(place == target)
-        for part in parts:
-            spread = lax.dot_general(part, chosen, (((0,), (0,)), ((), ())), preferred_element_type=jnp.float32)
-            result = result + spread[side * total:(side + 1) * total]
+    place = iota((2 * holders * half, slots), 0).astype(jnp.float32)
+    upper = rank_there >= half
+    target = begins + rank_there + jnp.where(upper, float(holders * half - half), 0.0)
+    chosen = exact_bf16(place == jnp.where(begins >= 0.0, target, -1.0))
+    landed = jnp.concatenate([ref[core] for ref in landed_refs for core in range(2)], axis=0).T
+    result = exact_product(jnp.concatenate([landed[:total], landed[total:]], axis=1), chosen)
     result = result.T
     blocks = []
     for g in range(groups):

time: 31.9 us -> 31.8 us (level)
  no operation moved by 1% of the time
where the time goes in v20:
time: 31.8 us; the launch traced here: 31.6 us
  starting transfers between devices  13.9 us (44%)
  waiting for transfers between devices  9.89 us (31%)
  Pallas kernels  6.39 us (20%)
  between operations  0.72 us (2%)
  other arithmetic  0.64 us (2%)
    ppermute x11, starting transfers between devices, swap(): lax.ppermute(value, axis, [(i, i ^ distance) for i in range(lax.axis_size...  8.35 us
    ppermute x11, waiting for transfers between devices, swap(): lax.ppermute(value, axis, [(i, i ^ distance) for i in range(lax.axis_size...  7.5 us
    ppermute x3, starting transfers between devices, on_device(): lax.ppermute(terms[step], 'layer', [(g, (g + step) % groups) for g in ran...  5.57 us
    pallas_call x1, Pallas kernels, on_device(): pl.pallas_call(load_kernel, out_shape=[jax.ShapeDtypeStruct(again.shape,...  2.65 us
    ppermute x3, waiting for transfers between devices, on_device(): lax.ppermute(terms[step], 'layer', [(g, (g + step) % groups) for g in ran...  2.39 us
    pallas_call x1, Pallas kernels, on_device(): pl.pallas_call(functools.partial(condition_kernel, holders, capacity, per...  2.17 us
    pallas_call x1, Pallas kernels, on_device(): pl.pallas_call(functools.partial(score_kernel, holders, capacity), out_sh...  1.14 us
  transfers between devices with their start and end apart: 14, of which 11 were waited for; matrix products, arithmetic and copies ran while one was open for 0% of the time, Pallas kernels for 8%

profile of v20, /device:TPU:0, one launch (start us, length us, event | category | flops | bytes accessed | tf_op | source)
XLA Modules:
  0.0 31.6 jit_solution(17110831697308528004)
XLA Ops:
  0.0 2.2 %shard_map.73 = (bf16[8,8320]{1,0:T(8,128)(2,1)S(1)}, bf16[8,8320]{1,0:T(8,128)(2,1)S(1)}, f32[8,256]{1,0:T(8,128)S(1)}) custom-call(bf16[8,8192]{1,0:T(8,128)(2,1)} %refs_0_.2, f32[2,64,64]{2,1,0:T(8,128)} %refs_1_.1, f32[2,64,64]{2,1,0:T(8,128)} %refs_2_.1, s32[16,128]{1,0:T(8,128)} %bitcast.3, s32[1,256]{1,0:T(1,128)} %refs_4_.1), custom_call_target="tpu_custom_call" | custom-call | tf_op jit(solution)/shard_map/pallas_call | solution.py:243
  2.2 4.0 %collective-permute-start = (bf16[8,8320]{1,0:T(8,128)(2,1)S(1)}, bf16[8,8320]{1,0:T(8,128)(2,1)S(1)}, u32[]{:S(2)}, u32[]{:S(2)}) collective-permute-start(bf16[8,8320]{1,0:T(8,128)(2,1)S(1)} %get-tuple-element.18.refs_9_), channel_id=1, source_target_pairs={{0,24},{4,28},{8,16},{12,20},{16,8},{20,12},{24,0},{28,4},{1,25},{... | collective-permute-start | bytes 399368 | tf_op jit(solution)/shard_map/ppermute | solution.py:224
  6.1 0.5 %collective-permute-start.2 = (bf16[8,8320]{1,0:T(8,128)(2,1)S(1)}, bf16[8,8320]{1,0:T(8,128)(2,1)S(1)}, u32[]{:S(2)}, u32[]{:S(2)}) collective-permute-start(bf16[8,8320]{1,0:T(8,128)(2,1)S(1)} %get-tuple-element.18.refs_9_), channel_id=1, source_target_pairs={{0,16},{4,20},{8,24},{12,28},{16,0},{20,4},{24,8},{28,12},{1,17},{... | collective-permute-start | bytes 399368 | tf_op jit(solution)/shard_map/ppermute | solution.py:224
  6.7 0.1 collective-permute-start.4
  6.8 2.6 %shard_map.74 = (bf16[8,8320]{1,0:T(8,128)(2,1)S(1)}, bf16[8192,256]{1,0:T(8,128)(2,1)S(1)}) custom-call(bf16[8,8320]{1,0:T(8,128)(2,1)S(1)} %get-tuple-element.19.block_ref, bf16[256,8192]{1,0:T(8,128)(2,1)} %source_ref.1), custom_call_target="tpu_custom_call", output_to_operand_aliasing={{0}: (0, {})} | custom-call | bytes 4194304 | tf_op jit(solution)/shard_map/pallas_call | solution.py:257
  9.4 0.1 collective-permute-start.6
  9.5 0.6 %collective-permute-done.refs_3_ = bf16[8,8320]{1,0:T(8,128)(2,1)S(1)} collective-permute-done((bf16[8,8320]{1,0:T(8,128)(2,1)S(1)}, bf16[8,8320]{1,0:T(8,128)(2,1)S(1)}, u32[]{:S(2)}, u32[]{:S(2)}) %collective-permute-start) | collective-permute-done | bytes 133152 | tf_op jit(solution)/shard_map/ppermute | solution.py:224
  10.1 0.0 collective-permute-start.1
  10.1 2.4 %collective-permute-done.2.refs_5_ = bf16[8,8320]{1,0:T(8,128)(2,1)S(1)} collective-permute-done((bf16[8,8320]{1,0:T(8,128)(2,1)S(1)}, bf16[8,8320]{1,0:T(8,128)(2,1)S(1)}, u32[]{:S(2)}, u32[]{:S(2)}) %collective-permute-start.2) | collective-permute-done | bytes 133152 | tf_op jit(solution)/shard_map/ppermute | solution.py:224
  12.5 0.0 collective-permute-start.3
  12.5 0.2 collective-permute-done.4.refs_7_
  12.8 0.3 collective-permute-start.5
  13.7 0.0 collective-permute-done.6.refs_8_
  13.7 0.0 collective-permute-done.1.refs_2_
  13.7 0.2 collective-permute-done.3.refs_4_
  13.9 0.3 collective-permute-done.5.refs_6_
  14.1 1.1 %shard_map.75 = (f32[4,16,128]{2,1,0:T(8,128)S(1)}, f32[4,16,128]{2,1,0:T(8,128)S(1)}, f32[8,256]{1,0:T(8,128)S(1)}) custom-call(s32[1]{0:T(128)S(6)} %copy.10.refs_0_, f32[8,256]{1,0:T(8,128)S(1)} %get-tuple-element.17.refs_1_, bf16[8,8320]{1,0:T(8,128)(2,1)S(1)} %collective-permute-done.1.refs_2_, bf16[8,8320]{1,0:T(8,128)(2,1)S(1)} %collective-permute-done.refs_3_, ...), custom_call_target="tpu_custom_call" | custom-call | tf_op jit(solution)/shard_map/pallas_call | solution.py:278
  15.3 0.3 %collective-permute-start.7 = (f32[4,16,128]{2,1,0:T(8,128)S(1)}, f32[4,16,128]{2,1,0:T(8,128)S(1)}, u32[]{:S(2)}, u32[]{:S(2)}) collective-permute-start(f32[4,16,128]{2,1,0:T(8,128)S(1)} %get-tuple-element.24), channel_id=1, source_target_pairs={{0,4},{4,0},{8,12},{12,8},{16,20},{20,16},{24,28},{28,24},{1,5},{5... | collective-permute-start | bytes 98312 | tf_op jit(solution)/shard_map/ppermute | solution.py:224
  15.6 0.9 %collective-permute-done.7 = f32[4,16,128]{2,1,0:T(8,128)S(1)} collective-permute-done((f32[4,16,128]{2,1,0:T(8,128)S(1)}, f32[4,16,128]{2,1,0:T(8,128)S(1)}, u32[]{:S(2)}, u32[]{:S(2)}) %collective-permute-start.7) | collective-permute-done | bytes 32800 | tf_op jit(solution)/shard_map/ppermute | solution.py:224
  16.6 1.7 %collective-permute-start.10 = (f32[2,16,128]{2,1,0:T(8,128)S(1)}, f32[2,16,128]{2,1,0:T(8,128)S(1)}, u32[]{:S(2)}, u32[]{:S(2)}) collective-permute-start(f32[2,16,128]{2,1,0:T(8,128)S(1)} %pad_maximum_fusion.3), channel_id=1, source_target_pairs={{0,28},{4,24},{8,20},{12,16},{16,12},{20,8},{24,4},{28,0},{1,29},{... | collective-permute-start | bytes 49160 | tf_op jit(solution)/shard_map/ppermute | solution.py:224
  18.2 1.1 %collective-permute-start.9 = (f32[2,16,128]{2,1,0:T(8,128)S(1)}, f32[2,16,128]{2,1,0:T(8,128)S(1)}, u32[]{:S(2)}, u32[]{:S(2)}) collective-permute-start(f32[2,16,128]{2,1,0:T(8,128)S(1)} %pad_maximum_fusion.2), channel_id=1, source_target_pairs={{0,20},{4,16},{8,28},{12,24},{16,4},{20,0},{24,12},{28,8},{1,21},{... | collective-permute-start | bytes 49160 | tf_op jit(solution)/shard_map/ppermute | solution.py:224
  19.4 0.3 collective-permute-start.8
  19.6 1.0 %collective-permute-done.10.refs_3_ = f32[2,16,128]{2,1,0:T(8,128)S(1)} collective-permute-done((f32[2,16,128]{2,1,0:T(8,128)S(1)}, f32[2,16,128]{2,1,0:T(8,128)S(1)}, u32[]{:S(2)}, u32[]{:S(2)}) %collective-permute-start.10) | collective-permute-done | bytes 16416 | tf_op jit(solution)/shard_map/ppermute | solution.py:224
  20.6 0.8 %collective-permute-done.9.refs_2_ = f32[2,16,128]{2,1,0:T(8,128)S(1)} collective-permute-done((f32[2,16,128]{2,1,0:T(8,128)S(1)}, f32[2,16,128]{2,1,0:T(8,128)S(1)}, u32[]{:S(2)}, u32[]{:S(2)}) %collective-permute-start.9) | collective-permute-done | bytes 16416 | tf_op jit(solution)/shard_map/ppermute | solution.py:224
  21.4 1.1 %collective-permute-done.8.refs_1_ = f32[2,16,128]{2,1,0:T(8,128)S(1)} collective-permute-done((f32[2,16,128]{2,1,0:T(8,128)S(1)}, f32[2,16,128]{2,1,0:T(8,128)S(1)}, u32[]{:S(2)}, u32[]{:S(2)}) %collective-permute-start.8) | collective-permute-done | bytes 16416 | tf_op jit(solution)/shard_map/ppermute | solution.py:224
  22.5 0.4 %shard_map.76 = (f32[32,128]{1,0:T(8,128)S(1)}, f32[32,128]{1,0:T(8,128)S(1)}, f32[32,128]{1,0:T(8,128)S(1)}, f32[32,128]{1,0:T(8,128)S(1)}) custom-call(f32[8,256]{1,0:T(8,128)S(1)} %get-tuple-element.22.found_ref, f32[2,16,128]{2,1,0:T(8,128)S(1)} %pad_maximum_fusion.refs_0_, f32[2,16,128]{2,1,0:T(8,128)S(1)} %collective-permute-done.8.refs_1_, ...), custom_call_target="tpu_custom_call" | custom-call | tf_op jit(solution)/shard_map/pallas_call | solution.py:297
  23.0 1.6 %collective-permute-start.11 = (f32[32,128]{1,0:T(8,128)S(1)}, f32[32,128]{1,0:T(8,128)S(1)}, u32[]{:S(2)}, u32[]{:S(2)}) collective-permute-start(f32[32,128]{1,0:T(8,128)S(1)} %get-tuple-element.26), channel_id=1, source_target_pairs={{0,1},{1,2},{2,3},{3,0},{4,5},{5,6},{6,7},{7,4},{8,9},{9,10},{10,1... | collective-permute-start | bytes 49160 | tf_op jit(solution)/shard_map/ppermute | solution.py:306
  24.6 2.6 %collective-permute-start.12 = (f32[32,128]{1,0:T(8,128)S(1)}, f32[32,128]{1,0:T(8,128)S(1)}, u32[]{:S(2)}, u32[]{:S(2)}) collective-permute-start(f32[32,128]{1,0:T(8,128)S(1)} %get-tuple-element.27), channel_id=1, source_target_pairs={{0,2},{1,3},{2,0},{3,1},{4,6},{5,7},{6,4},{7,5},{8,10},{9,11},{10,... | collective-permute-start | bytes 49160 | tf_op jit(solution)/shard_map/ppermute | solution.py:306
  27.2 1.3 %collective-permute-start.13 = (f32[32,128]{1,0:T(8,128)S(1)}, f32[32,128]{1,0:T(8,128)S(1)}, u32[]{:S(2)}, u32[]{:S(2)}) collective-permute-start(f32[32,128]{1,0:T(8,128)S(1)} %get-tuple-element.28), channel_id=1, source_target_pairs={{0,3},{1,0},{2,1},{3,2},{4,7},{5,4},{6,5},{7,6},{8,11},{9,8},{10,9... | collective-permute-start | bytes 49160 | tf_op jit(solution)/shard_map/ppermute | solution.py:306
  28.6 0.0 collective-permute-done.11
  28.6 0.7 %collective-permute-done.12 = f32[32,128]{1,0:T(8,128)S(1)} collective-permute-done((f32[32,128]{1,0:T(8,128)S(1)}, f32[32,128]{1,0:T(8,128)S(1)}, u32[]{:S(2)}, u32[]{:S(2)}) %collective-permute-start.12) | collective-permute-done | bytes 16416 | tf_op jit(solution)/shard_map/ppermute | solution.py:306
  29.3 1.7 %collective-permute-done.13 = f32[32,128]{1,0:T(8,128)S(1)} collective-permute-done((f32[32,128]{1,0:T(8,128)S(1)}, f32[32,128]{1,0:T(8,128)S(1)}, u32[]{:S(2)}, u32[]{:S(2)}) %collective-permute-start.13) | collective-permute-done | bytes 16416 | tf_op jit(solution)/shard_map/ppermute | solution.py:306
  30.9 0.1 fusion.2
  31.0 0.6 %maximum_bitcast_fusion = f32[1,64,64]{2,1,0:T(8,128)} fusion(f32[32,64]{1,0:T(8,128)S(1)} %get-tuple-element.38, f32[32,64]{1,0:T(8,128)S(1)} %get-tuple-element.37), kind=kLoop, calls=%fused_computation | loop fusion | flops 4096 | bytes 32768 | tf_op jit(solution)/shard_map/broadcast_in_dim | solution.py:307
  (7 shorter events, 0.0 us)
Async XLA Ops:
  2.2 7.9 %collective-permute-start = (bf16[8,8320]{1,0:T(8,128)(2,1)S(1)}, bf16[8,8320]{1,0:T(8,128)(2,1)S(1)}, u32[]{:S(2)}, u32[]{:S(2)}) collective-permute-start(bf16[8,8320]{1,0:T(8,128)(2,1)S(1)} %get-tuple-element.18.refs_9_), channel_id=1, source_target_pairs={{0,24},{4,28},{8,16},{12,20},{16,8},{20,12},{24,0},{28,4},{1,25},{... | collective-permute-start | bytes 399368 | tf_op jit(solution)/shard_map/ppermute | solution.py:224
  6.1 6.4 %collective-permute-start.2 = (bf16[8,8320]{1,0:T(8,128)(2,1)S(1)}, bf16[8,8320]{1,0:T(8,128)(2,1)S(1)}, u32[]{:S(2)}, u32[]{:S(2)}) collective-permute-start(bf16[8,8320]{1,0:T(8,128)(2,1)S(1)} %get-tuple-element.18.refs_9_), channel_id=1, source_target_pairs={{0,16},{4,20},{8,24},{12,28},{16,0},{20,4},{24,8},{28,12},{1,17},{... | collective-permute-start | bytes 399368 | tf_op jit(solution)/shard_map/ppermute | solution.py:224
  6.7 6.1 %collective-permute-start.4 = (bf16[8,8320]{1,0:T(8,128)(2,1)S(1)}, bf16[8,8320]{1,0:T(8,128)(2,1)S(1)}, u32[]{:S(2)}, u32[]{:S(2)}) collective-permute-start(bf16[8,8320]{1,0:T(8,128)(2,1)S(1)} %get-tuple-element.18.refs_9_), channel_id=1, source_target_pairs={{0,8},{4,12},{8,0},{12,4},{16,24},{20,28},{24,16},{28,20},{1,9},{5... | collective-permute-start | bytes 399368 | tf_op jit(solution)/shard_map/ppermute | solution.py:224
  9.4 4.3 %collective-permute-start.6 = (bf16[8,8320]{1,0:T(8,128)(2,1)S(1)}, bf16[8,8320]{1,0:T(8,128)(2,1)S(1)}, u32[]{:S(2)}, u32[]{:S(2)}) collective-permute-start(bf16[8,8320]{1,0:T(8,128)(2,1)S(1)} %get-tuple-element.20), channel_id=1, source_target_pairs={{0,4},{4,0},{8,12},{12,8},{16,20},{20,16},{24,28},{28,24},{1,5},{5... | collective-permute-start | bytes 399368 | tf_op jit(solution)/shard_map/ppermute | solution.py:224
  10.1 3.6 %collective-permute-start.1 = (bf16[8,8320]{1,0:T(8,128)(2,1)S(1)}, bf16[8,8320]{1,0:T(8,128)(2,1)S(1)}, u32[]{:S(2)}, u32[]{:S(2)}) collective-permute-start(bf16[8,8320]{1,0:T(8,128)(2,1)S(1)} %collective-permute-done.refs_3_), channel_id=1, source_target_pairs={{0,4},{4,0},{8,12},{12,8},{16,20},{20,16},{24,28},{28,24},{1,5},{5... | collective-permute-start | bytes 399368 | tf_op jit(solution)/shard_map/ppermute | solution.py:224
  12.5 1.4 %collective-permute-start.3 = (bf16[8,8320]{1,0:T(8,128)(2,1)S(1)}, bf16[8,8320]{1,0:T(8,128)(2,1)S(1)}, u32[]{:S(2)}, u32[]{:S(2)}) collective-permute-start(bf16[8,8320]{1,0:T(8,128)(2,1)S(1)} %collective-permute-done.2.refs_5_), channel_id=1, source_target_pairs={{0,4},{4,0},{8,12},{12,8},{16,20},{20,16},{24,28},{28,24},{1,5},{5... | collective-permute-start | bytes 399368 | tf_op jit(solution)/shard_map/ppermute | solution.py:224
  12.8 1.4 %collective-permute-start.5 = (bf16[8,8320]{1,0:T(8,128)(2,1)S(1)}, bf16[8,8320]{1,0:T(8,128)(2,1)S(1)}, u32[]{:S(2)}, u32[]{:S(2)}) collective-permute-start(bf16[8,8320]{1,0:T(8,128)(2,1)S(1)} %collective-permute-done.4.refs_7_), channel_id=1, source_target_pairs={{0,4},{4,0},{8,12},{12,8},{16,20},{20,16},{24,28},{28,24},{1,5},{5... | collective-permute-start | bytes 399368 | tf_op jit(solution)/shard_map/ppermute | solution.py:224
  15.3 1.3 %collective-permute-start.7 = (f32[4,16,128]{2,1,0:T(8,128)S(1)}, f32[4,16,128]{2,1,0:T(8,128)S(1)}, u32[]{:S(2)}, u32[]{:S(2)}) collective-permute-start(f32[4,16,128]{2,1,0:T(8,128)S(1)} %get-tuple-element.24), channel_id=1, source_target_pairs={{0,4},{4,0},{8,12},{12,8},{16,20},{20,16},{24,28},{28,24},{1,5},{5... | collective-permute-start | bytes 98312 | tf_op jit(solution)/shard_map/ppermute | solution.py:224
  16.6 4.1 %collective-permute-start.10 = (f32[2,16,128]{2,1,0:T(8,128)S(1)}, f32[2,16,128]{2,1,0:T(8,128)S(1)}, u32[]{:S(2)}, u32[]{:S(2)}) collective-permute-start(f32[2,16,128]{2,1,0:T(8,128)S(1)} %pad_maximum_fusion.3), channel_id=1, source_target_pairs={{0,28},{4,24},{8,20},{12,16},{16,12},{20,8},{24,4},{28,0},{1,29},{... | collective-permute-start | bytes 49160 | tf_op jit(solution)/shard_map/ppermute | solution.py:224
  18.2 3.2 %collective-permute-start.9 = (f32[2,16,128]{2,1,0:T(8,128)S(1)}, f32[2,16,128]{2,1,0:T(8,128)S(1)}, u32[]{:S(2)}, u32[]{:S(2)}) collective-permute-start(f32[2,16,128]{2,1,0:T(8,128)S(1)} %pad_maximum_fusion.2), channel_id=1, source_target_pairs={{0,20},{4,16},{8,28},{12,24},{16,4},{20,0},{24,12},{28,8},{1,21},{... | collective-permute-start | bytes 49160 | tf_op jit(solution)/shard_map/ppermute | solution.py:224
  19.4 3.2 %collective-permute-start.8 = (f32[2,16,128]{2,1,0:T(8,128)S(1)}, f32[2,16,128]{2,1,0:T(8,128)S(1)}, u32[]{:S(2)}, u32[]{:S(2)}) collective-permute-start(f32[2,16,128]{2,1,0:T(8,128)S(1)} %pad_maximum_fusion.1), channel_id=1, source_target_pairs={{0,12},{4,8},{8,4},{12,0},{16,28},{20,24},{24,20},{28,16},{1,13},{... | collective-permute-start | bytes 49160 | tf_op jit(solution)/shard_map/ppermute | solution.py:224
  23.0 5.6 %collective-permute-start.11 = (f32[32,128]{1,0:T(8,128)S(1)}, f32[32,128]{1,0:T(8,128)S(1)}, u32[]{:S(2)}, u32[]{:S(2)}) collective-permute-start(f32[32,128]{1,0:T(8,128)S(1)} %get-tuple-element.26), channel_id=1, source_target_pairs={{0,1},{1,2},{2,3},{3,0},{4,5},{5,6},{6,7},{7,4},{8,9},{9,10},{10,1... | collective-permute-start | bytes 49160 | tf_op jit(solution)/shard_map/ppermute | solution.py:306
  24.6 4.6 %collective-permute-start.12 = (f32[32,128]{1,0:T(8,128)S(1)}, f32[32,128]{1,0:T(8,128)S(1)}, u32[]{:S(2)}, u32[]{:S(2)}) collective-permute-start(f32[32,128]{1,0:T(8,128)S(1)} %get-tuple-element.27), channel_id=1, source_target_pairs={{0,2},{1,3},{2,0},{3,1},{4,6},{5,7},{6,4},{7,5},{8,10},{9,11},{10,... | collective-permute-start | bytes 49160 | tf_op jit(solution)/shard_map/ppermute | solution.py:306
  27.2 3.7 %collective-permute-start.13 = (f32[32,128]{1,0:T(8,128)S(1)}, f32[32,128]{1,0:T(8,128)S(1)}, u32[]{:S(2)}, u32[]{:S(2)}) collective-permute-start(f32[32,128]{1,0:T(8,128)S(1)} %get-tuple-element.28), channel_id=1, source_target_pairs={{0,3},{1,0},{2,1},{3,2},{4,7},{5,4},{6,5},{7,6},{8,11},{9,8},{10,9... | collective-permute-start | bytes 49160 | tf_op jit(solution)/shard_map/ppermute | solution.py:306

commit v21 on v20

--- a/solution.py
+++ b/solution.py
@@ -137,7 +137,7 @@
     found_ref[...] = jnp.concatenate([holder, rank_there, jnp.zeros((6, slots), jnp.float32)], axis=0)
 
 
-def load_kernel(block_ref, source_ref, same_block_ref, target_ref, landing, arrived):
+def load_kernel(holders, count_ref, found_ref, block_ref, source_ref, same_block_ref, target_ref, used_ref, landing, arrived):
     step = landing.shape[1] // LOADS
     copies = [
         pltpu.make_async_copy(
@@ -147,14 +147,23 @@
     ]
     for copy in copies:
         copy.start()
+    used_ref[...] = found_ref[...]
+    slots = found_ref.shape[1]
+    used_ref[0:1] = jnp.where(iota((1, slots), 1) < count_ref[0], found_ref[0:1], float(holders))
     for i, copy in enumerate(copies):
         copy.wait()
         target_ref[i * step:(i + 1) * step, :] = landing[:, i * step:(i + 1) * step].T
 
 
+def pick(scores, wanted):
+    chosen = exact_bf16(iota((scores.shape[1], wanted.shape[1]), 0).astype(jnp.float32) + 1.0 == wanted)
+    picked = exact_product(scores, chosen)
+    cut = wanted.shape[1] // 2
+    return jnp.concatenate([picked[:, :cut], picked[:, cut:]], axis=0).T
+
+
 def score_kernel(holders, capacity, *refs):
-    count_ref, found_ref, packed_refs = *refs[:2], refs[2:2 + holders][::-1]
-    pages_ref, keep_ref, send_ref, used_ref, total, queries = refs[2 + holders:]
+    packed_refs, pages_ref, send_ref, scores_ref, rest_ref, queries = refs[:holders][::-1], *refs[holders:]
     me = lax.axis_index("store")
     width, count = pages_ref.shape
     rows = packed_refs[0].shape[0]
@@ -168,7 +177,7 @@
         scores = scores + jnp.dot(queries[:, columns], pages_ref[columns], preferred_element_type=jnp.float32)
     for k in range(holders):
         start = pl.multiple_of((me ^ k) * rows, rows)
-        total[pl.ds(start, rows), :] = scores[k * rows:(k + 1) * rows]
+        scores_ref[pl.ds(start, rows), :] = scores[k * rows:(k + 1) * rows]
     asked = []
     for k in range(holders):
         notes = packed_refs[k][:, width:].astype(jnp.float32)
@@ -177,18 +186,22 @@
         for block in range(1, holders // rows):
             mine = jnp.where(me // rows == block, notes[:, block * capacity:(block + 1) * capacity], mine)
         asked.append(mine)
-    wanted = jnp.concatenate(
-        [row[:, side * half:(side + 1) * half] for side in range(2) for row in asked], axis=1
-    )
-    chosen = exact_bf16(iota((count, 2 * holders * half), 0).astype(jnp.float32) + 1.0 == wanted)
-    picked = exact_product(total[...], chosen)
-    used_ref[...] = found_ref[...]
-    own_slots = found_ref.shape[1]
-    used_ref[0:1] = jnp.where(iota((1, own_slots), 1) < count_ref[0], found_ref[0:1], float(holders))
-    picked = jnp.concatenate([picked[:, :holders * half], picked[:, holders * half:]], axis=0).T
-    for place, k in enumerate(kept_distances(holders)):
-        keep_ref[place] = picked[k * half:(k + 1) * half]
-        send_ref[place] = picked[(k ^ 1) * half:((k ^ 1) + 1) * half]
+    kept = kept_distances(holders)
+    wanted = [
+        jnp.concatenate([asked[k][:, side * half:(side + 1) * half] for side in range(2) for k in distances], axis=1)
+        for distances in ([k ^ 1 for k in kept], kept)
+    ]
+    rest_ref[...] = wanted[1]
+    picked = pick(scores_ref[...], wanted[0])
+    for place in range(len(kept)):
+        send_ref[place] = picked[place * half:(place + 1) * half]
+
+
+def rest_kernel(scores_ref, rest_ref, keep_ref):
+    picked = pick(scores_ref[...], rest_ref[...])
+    half = keep_ref.shape[1]
+    for place in range(keep_ref.shape[0]):
+        keep_ref[place] = picked[place * half:(place + 1) * half]
 
 
 def spread_kernel(holders, groups, found_ref, *refs):
@@ -254,16 +267,20 @@
         compiler_params=pltpu.CompilerParams(vmem_limit_bytes=10 * 2**20 + 24 * slots * slots),
     )(*sources)
 
-    again, pages = pl.pallas_call(
-        load_kernel,
-        out_shape=[jax.ShapeDtypeStruct(again.shape, bf16), pltpu.VMEM((width, per_holder), bf16)],
-        in_specs=[VMEM, HBM],
-        out_specs=[VMEM] * 2,
-        input_output_aliases={0: 0},
+    again, pages, used = pl.pallas_call(
+        functools.partial(load_kernel, holders),
+        out_shape=[
+            jax.ShapeDtypeStruct(again.shape, bf16),
+            pltpu.VMEM((width, per_holder), bf16),
+            jax.ShapeDtypeStruct(found.shape, jnp.float32),
+        ],
+        in_specs=[SMEM, VMEM, VMEM, HBM],
+        out_specs=[VMEM] * 3,
+        input_output_aliases={2: 0},
         scratch_shapes=[pltpu.VMEM(page_store.shape, bf16), pltpu.SemaphoreType.DMA((LOADS,))],
         compiler_params=pltpu.CompilerParams(vmem_limit_bytes=4 * 2**20 + 4 * per_holder * width),
         cost_estimate=pl.CostEstimate(flops=0, bytes_accessed=2 * page_store.size, transcendentals=0),
-    )(again, pltpu.with_memory_space_constraint(page_store, pltpu.HBM))
+    )(counts, found, again, pltpu.with_memory_space_constraint(page_store, pltpu.HBM))
 
     blocks = [None] * holders
     blocks[0] = packed
@@ -275,20 +292,28 @@
 
     total = holders * rows
     bytes_in = 2 * holders * rows * (width + notes) + 2 * per_holder * width
-    keep, send, used = pl.pallas_call(
+    picked_shape = jax.ShapeDtypeStruct((holders // 2, capacity // 2, 2 * total), jnp.float32)
+    send, scores, rest = pl.pallas_call(
         functools.partial(score_kernel, holders, capacity),
         out_shape=[
-            jax.ShapeDtypeStruct((holders // 2, capacity // 2, 2 * total), jnp.float32),
-            jax.ShapeDtypeStruct((holders // 2, capacity // 2, 2 * total), jnp.float32),
-            jax.ShapeDtypeStruct(found.shape, jnp.float32),
+            picked_shape,
+            jax.ShapeDtypeStruct((total, per_holder), jnp.float32),
+            jax.ShapeDtypeStruct((1, slots // 2), jnp.float32),
         ],
-        in_specs=[SMEM] + [VMEM] * (holders + 2),
+        in_specs=[VMEM] * (holders + 1),
         out_specs=[VMEM] * 3,
-        scratch_shapes=[pltpu.VMEM((total, per_holder), jnp.float32), pltpu.VMEM((total, width), bf16)],
+        scratch_shapes=[pltpu.VMEM((total, width), bf16)],
         compiler_params=pltpu.CompilerParams(vmem_limit_bytes=8 * 2**20 + 2 * bytes_in + 48 * total * slots),
-    )(counts, found, *blocks[::-1], pltpu.with_memory_space_constraint(pages, pltpu.VMEM))
+    )(*blocks[::-1], pltpu.with_memory_space_constraint(pages, pltpu.VMEM))
 
     handed = swap(send, "store", 1)
+    keep = pl.pallas_call(
+        rest_kernel,
+        out_shape=picked_shape,
+        in_specs=[VMEM] * 2,
+        out_specs=VMEM,
+        compiler_params=pltpu.CompilerParams(vmem_limit_bytes=4 * 2**20 + 24 * total * slots),
+    )(scores, rest)
     landed = []
     for place, k in enumerate(kept_distances(holders)):
         pair = jnp.stack([keep[place], handed[place]])

time: 31.8 us -> 31.8 us (level)
  waiting for transfers between devices: 9.89 us -> 9.1 us
  starting transfers between devices: 13.9 us -> 14.4 us
  Pallas kernels: 6.39 us -> 6.71 us
    ppermute x11, waiting for transfers between devices: 7.5 us -> 6.71 us  [swap(): lax.ppermute(value, axis, [(i, i ^ distance) for i in range(lax.axis_size...]
    ppermute x11, starting transfers between devices: 8.35 us -> 8.82 us  [swap(): lax.ppermute(value, axis, [(i, i ^ distance) for i in range(lax.axis_size...]
    pallas_call x1 -> x2, Pallas kernels: 2.65 us -> 2.92 us  [the longest x1 2.65 us: on_device(): pl.pallas_call(functools.partial(load_kernel, holders), out_shape=[jax.Sh...]
  transfers between devices with their start and end apart: 14 -> 14, of which waited for: 11 -> 10; matrix products, arithmetic and copies ran while one was open for 0% -> 0% of each run, Pallas kernels for 8% -> 9%
where the time goes in v21:
time: 31.8 us; the launch traced here: 31.7 us
  starting transfers between devices  14.4 us (45%)
  waiting for transfers between devices  9.1 us (29%)
  Pallas kernels  6.71 us (21%)
  between operations  0.72 us (2%)
  other arithmetic  0.64 us (2%)
    ppermute x11, starting transfers between devices, swap(): lax.ppermute(value, axis, [(i, i ^ distance) for i in range(lax.axis_size...  8.82 us
    ppermute x11, waiting for transfers between devices, swap(): lax.ppermute(value, axis, [(i, i ^ distance) for i in range(lax.axis_size...  6.71 us
    ppermute x3, starting transfers between devices, on_device(): lax.ppermute(terms[step], 'layer', [(g, (g + step) % groups) for g in ran...  5.57 us
    pallas_call x1, Pallas kernels, on_device(): pl.pallas_call(functools.partial(load_kernel, holders), out_shape=[jax.Sh...  2.65 us
    ppermute x3, waiting for transfers between devices, on_device(): lax.ppermute(terms[step], 'layer', [(g, (g + step) % groups) for g in ran...  2.39 us
    pallas_call x1, Pallas kernels, on_device(): pl.pallas_call(functools.partial(condition_kernel, holders, capacity, per...  2.17 us
    pallas_call x1, Pallas kernels, on_device(): pl.pallas_call(functools.partial(score_kernel, holders, capacity), out_sh...  1.19 us
  transfers between devices with their start and end apart: 14, of which 10 were waited for; matrix products, arithmetic and copies ran while one was open for 0% of the time, Pallas kernels for 9%

profile of v21, /device:TPU:0, one launch (start us, length us, event | category | flops | bytes accessed | tf_op | source)
XLA Modules:
  0.0 31.7 jit_solution(11359861881587102901)
XLA Ops:
  0.0 2.2 %shard_map.73 = (bf16[8,8320]{1,0:T(8,128)(2,1)S(1)}, bf16[8,8320]{1,0:T(8,128)(2,1)S(1)}, f32[8,256]{1,0:T(8,128)S(1)}) custom-call(bf16[8,8192]{1,0:T(8,128)(2,1)} %refs_0_.1, f32[2,64,64]{2,1,0:T(8,128)} %refs_1_.1, f32[2,64,64]{2,1,0:T(8,128)} %refs_2_.1, s32[16,128]{1,0:T(8,128)} %bitcast.3, s32[1,256]{1,0:T(1,128)} %refs_4_.1), custom_call_target="tpu_custom_call" | custom-call | tf_op jit(solution)/shard_map/pallas_call | solution.py:256
  2.2 4.0 %collective-permute-start = (bf16[8,8320]{1,0:T(8,128)(2,1)S(1)}, bf16[8,8320]{1,0:T(8,128)(2,1)S(1)}, u32[]{:S(2)}, u32[]{:S(2)}) collective-permute-start(bf16[8,8320]{1,0:T(8,128)(2,1)S(1)} %get-tuple-element.21.refs_7_), channel_id=1, source_target_pairs={{0,24},{4,28},{8,16},{12,20},{16,8},{20,12},{24,0},{28,4},{1,25},{... | collective-permute-start | bytes 399368 | tf_op jit(solution)/shard_map/ppermute | solution.py:237
  6.1 0.5 %collective-permute-start.2 = (bf16[8,8320]{1,0:T(8,128)(2,1)S(1)}, bf16[8,8320]{1,0:T(8,128)(2,1)S(1)}, u32[]{:S(2)}, u32[]{:S(2)}) collective-permute-start(bf16[8,8320]{1,0:T(8,128)(2,1)S(1)} %get-tuple-element.21.refs_7_), channel_id=1, source_target_pairs={{0,16},{4,20},{8,24},{12,28},{16,0},{20,4},{24,8},{28,12},{1,17},{... | collective-permute-start | bytes 399368 | tf_op jit(solution)/shard_map/ppermute | solution.py:237
  6.7 0.1 collective-permute-start.4
  7.4 2.7 %shard_map.74 = (bf16[8,8320]{1,0:T(8,128)(2,1)S(1)}, bf16[8192,256]{1,0:T(8,128)(2,1)S(1)}, f32[8,256]{1,0:T(8,128)S(1)}) custom-call(s32[1]{0:T(128)S(6)} %copy.10.count_ref, f32[8,256]{1,0:T(8,128)S(1)} %get-tuple-element.18.found_ref, bf16[8,8320]{1,0:T(8,128)(2,1)S(1)} %get-tuple-element.19.block_ref, ...), custom_call_target="tpu_custom_call", output_to_operand_aliasing={{0}: (2, {})} | custom-call | bytes 4194304 | tf_op jit(solution)/shard_map/pallas_call | solution.py:270
  10.1 0.1 collective-permute-start.6
  10.2 0.0 collective-permute-done.refs_1_
  10.2 0.5 %collective-permute-start.1 = (bf16[8,8320]{1,0:T(8,128)(2,1)S(1)}, bf16[8,8320]{1,0:T(8,128)(2,1)S(1)}, u32[]{:S(2)}, u32[]{:S(2)}) collective-permute-start(bf16[8,8320]{1,0:T(8,128)(2,1)S(1)} %collective-permute-done.refs_1_), channel_id=1, source_target_pairs={{0,4},{4,0},{8,12},{12,8},{16,20},{20,16},{24,28},{28,24},{1,5},{5... | collective-permute-start | bytes 399368 | tf_op jit(solution)/shard_map/ppermute | solution.py:237
  10.7 1.8 %collective-permute-done.2.refs_3_ = bf16[8,8320]{1,0:T(8,128)(2,1)S(1)} collective-permute-done((bf16[8,8320]{1,0:T(8,128)(2,1)S(1)}, bf16[8,8320]{1,0:T(8,128)(2,1)S(1)}, u32[]{:S(2)}, u32[]{:S(2)}) %collective-permute-start.2) | collective-permute-done | bytes 133152 | tf_op jit(solution)/shard_map/ppermute | solution.py:237
  12.5 0.0 collective-permute-start.3
  12.5 0.2 collective-permute-done.4.refs_5_
  12.8 0.3 collective-permute-start.5
  13.0 0.0 collective-permute-done.6.refs_6_
  13.0 0.0 collective-permute-done.1.refs_0_
  13.0 0.8 %collective-permute-done.3.refs_2_ = bf16[8,8320]{1,0:T(8,128)(2,1)S(1)} collective-permute-done((bf16[8,8320]{1,0:T(8,128)(2,1)S(1)}, bf16[8,8320]{1,0:T(8,128)(2,1)S(1)}, u32[]{:S(2)}, u32[]{:S(2)}) %collective-permute-start.3) | collective-permute-done | bytes 133152 | tf_op jit(solution)/shard_map/ppermute | solution.py:237
  13.9 0.3 collective-permute-done.5.refs_4_
  14.1 1.2 %shard_map.75 = (f32[4,16,128]{2,1,0:T(8,128)S(1)}, f32[64,256]{1,0:T(8,128)S(1)}, f32[1,128]{1,0:T(1,128)S(1)}) custom-call(bf16[8,8320]{1,0:T(8,128)(2,1)S(1)} %collective-permute-done.1.refs_0_, bf16[8,8320]{1,0:T(8,128)(2,1)S(1)} %collective-permute-done.refs_1_, bf16[8,8320]{1,0:T(8,128)(2,1)S(1)} %collective-permute-done.3.refs_2_, ...), custom_call_target="tpu_custom_call" | custom-call | tf_op jit(solution)/shard_map/pallas_call | solution.py:296
  15.3 0.3 collective-permute-start.7
  15.6 0.3 shard_map.76
  15.9 0.6 %collective-permute-done.7 = f32[4,16,128]{2,1,0:T(8,128)S(1)} collective-permute-done((f32[4,16,128]{2,1,0:T(8,128)S(1)}, f32[4,16,128]{2,1,0:T(8,128)S(1)}, u32[]{:S(2)}, u32[]{:S(2)}) %collective-permute-start.7) | collective-permute-done | bytes 32800 | tf_op jit(solution)/shard_map/ppermute | solution.py:237
  16.6 1.7 %collective-permute-start.10 = (f32[2,16,128]{2,1,0:T(8,128)S(1)}, f32[2,16,128]{2,1,0:T(8,128)S(1)}, u32[]{:S(2)}, u32[]{:S(2)}) collective-permute-start(f32[2,16,128]{2,1,0:T(8,128)S(1)} %pad_maximum_fusion.3), channel_id=1, source_target_pairs={{0,28},{4,24},{8,20},{12,16},{16,12},{20,8},{24,4},{28,0},{1,29},{... | collective-permute-start | bytes 49160 | tf_op jit(solution)/shard_map/ppermute | solution.py:237
  18.3 1.1 %collective-permute-start.9 = (f32[2,16,128]{2,1,0:T(8,128)S(1)}, f32[2,16,128]{2,1,0:T(8,128)S(1)}, u32[]{:S(2)}, u32[]{:S(2)}) collective-permute-start(f32[2,16,128]{2,1,0:T(8,128)S(1)} %pad_maximum_fusion.2), channel_id=1, source_target_pairs={{0,20},{4,16},{8,28},{12,24},{16,4},{20,0},{24,12},{28,8},{1,21},{... | collective-permute-start | bytes 49160 | tf_op jit(solution)/shard_map/ppermute | solution.py:237
  19.4 0.3 collective-permute-start.8
  19.7 1.0 %collective-permute-done.10.refs_3_ = f32[2,16,128]{2,1,0:T(8,128)S(1)} collective-permute-done((f32[2,16,128]{2,1,0:T(8,128)S(1)}, f32[2,16,128]{2,1,0:T(8,128)S(1)}, u32[]{:S(2)}, u32[]{:S(2)}) %collective-permute-start.10) | collective-permute-done | bytes 16416 | tf_op jit(solution)/shard_map/ppermute | solution.py:237
  20.6 0.8 %collective-permute-done.9.refs_2_ = f32[2,16,128]{2,1,0:T(8,128)S(1)} collective-permute-done((f32[2,16,128]{2,1,0:T(8,128)S(1)}, f32[2,16,128]{2,1,0:T(8,128)S(1)}, u32[]{:S(2)}, u32[]{:S(2)}) %collective-permute-start.9) | collective-permute-done | bytes 16416 | tf_op jit(solution)/shard_map/ppermute | solution.py:237
  21.4 1.1 %collective-permute-done.8.refs_1_ = f32[2,16,128]{2,1,0:T(8,128)S(1)} collective-permute-done((f32[2,16,128]{2,1,0:T(8,128)S(1)}, f32[2,16,128]{2,1,0:T(8,128)S(1)}, u32[]{:S(2)}, u32[]{:S(2)}) %collective-permute-start.8) | collective-permute-done | bytes 16416 | tf_op jit(solution)/shard_map/ppermute | solution.py:237
  22.6 0.4 %shard_map.77 = (f32[32,128]{1,0:T(8,128)S(1)}, f32[32,128]{1,0:T(8,128)S(1)}, f32[32,128]{1,0:T(8,128)S(1)}, f32[32,128]{1,0:T(8,128)S(1)}) custom-call(f32[8,256]{1,0:T(8,128)S(1)} %get-tuple-element.20.found_ref, f32[2,16,128]{2,1,0:T(8,128)S(1)} %pad_maximum_fusion.refs_0_, f32[2,16,128]{2,1,0:T(8,128)S(1)} %collective-permute-done.8.refs_1_, ...), custom_call_target="tpu_custom_call" | custom-call | tf_op jit(solution)/shard_map/pallas_call | solution.py:322
  23.0 1.6 %collective-permute-start.11 = (f32[32,128]{1,0:T(8,128)S(1)}, f32[32,128]{1,0:T(8,128)S(1)}, u32[]{:S(2)}, u32[]{:S(2)}) collective-permute-start(f32[32,128]{1,0:T(8,128)S(1)} %get-tuple-element.28), channel_id=1, source_target_pairs={{0,1},{1,2},{2,3},{3,0},{4,5},{5,6},{6,7},{7,4},{8,9},{9,10},{10,1... | collective-permute-start | bytes 49160 | tf_op jit(solution)/shard_map/ppermute | solution.py:331
  24.6 2.6 %collective-permute-start.12 = (f32[32,128]{1,0:T(8,128)S(1)}, f32[32,128]{1,0:T(8,128)S(1)}, u32[]{:S(2)}, u32[]{:S(2)}) collective-permute-start(f32[32,128]{1,0:T(8,128)S(1)} %get-tuple-element.29), channel_id=1, source_target_pairs={{0,2},{1,3},{2,0},{3,1},{4,6},{5,7},{6,4},{7,5},{8,10},{9,11},{10,... | collective-permute-start | bytes 49160 | tf_op jit(solution)/shard_map/ppermute | solution.py:331
  27.2 1.3 %collective-permute-start.13 = (f32[32,128]{1,0:T(8,128)S(1)}, f32[32,128]{1,0:T(8,128)S(1)}, u32[]{:S(2)}, u32[]{:S(2)}) collective-permute-start(f32[32,128]{1,0:T(8,128)S(1)} %get-tuple-element.30), channel_id=1, source_target_pairs={{0,3},{1,0},{2,1},{3,2},{4,7},{5,4},{6,5},{7,6},{8,11},{9,8},{10,9... | collective-permute-start | bytes 49160 | tf_op jit(solution)/shard_map/ppermute | solution.py:331
  28.6 0.0 collective-permute-done.11
  28.6 0.7 %collective-permute-done.12 = f32[32,128]{1,0:T(8,128)S(1)} collective-permute-done((f32[32,128]{1,0:T(8,128)S(1)}, f32[32,128]{1,0:T(8,128)S(1)}, u32[]{:S(2)}, u32[]{:S(2)}) %collective-permute-start.12) | collective-permute-done | bytes 16416 | tf_op jit(solution)/shard_map/ppermute | solution.py:331
  29.3 1.7 %collective-permute-done.13 = f32[32,128]{1,0:T(8,128)S(1)} collective-permute-done((f32[32,128]{1,0:T(8,128)S(1)}, f32[32,128]{1,0:T(8,128)S(1)}, u32[]{:S(2)}, u32[]{:S(2)}) %collective-permute-start.13) | collective-permute-done | bytes 16416 | tf_op jit(solution)/shard_map/ppermute | solution.py:331
  31.0 0.1 fusion.2
  31.0 0.6 %maximum_bitcast_fusion = f32[1,64,64]{2,1,0:T(8,128)} fusion(f32[32,64]{1,0:T(8,128)S(1)} %get-tuple-element.40, f32[32,64]{1,0:T(8,128)S(1)} %get-tuple-element.39), kind=kLoop, calls=%fused_computation | loop fusion | flops 4096 | bytes 32768 | tf_op jit(solution)/shard_map/broadcast_in_dim | solution.py:332
  (7 shorter events, 0.1 us)
Async XLA Ops:
  2.2 8.0 %collective-permute-start = (bf16[8,8320]{1,0:T(8,128)(2,1)S(1)}, bf16[8,8320]{1,0:T(8,128)(2,1)S(1)}, u32[]{:S(2)}, u32[]{:S(2)}) collective-permute-start(bf16[8,8320]{1,0:T(8,128)(2,1)S(1)} %get-tuple-element.21.refs_7_), channel_id=1, source_target_pairs={{0,24},{4,28},{8,16},{12,20},{16,8},{20,12},{24,0},{28,4},{1,25},{... | collective-permute-start | bytes 399368 | tf_op jit(solution)/shard_map/ppermute | solution.py:237
  6.1 6.4 %collective-permute-start.2 = (bf16[8,8320]{1,0:T(8,128)(2,1)S(1)}, bf16[8,8320]{1,0:T(8,128)(2,1)S(1)}, u32[]{:S(2)}, u32[]{:S(2)}) collective-permute-start(bf16[8,8320]{1,0:T(8,128)(2,1)S(1)} %get-tuple-element.21.refs_7_), channel_id=1, source_target_pairs={{0,16},{4,20},{8,24},{12,28},{16,0},{20,4},{24,8},{28,12},{1,17},{... | collective-permute-start | bytes 399368 | tf_op jit(solution)/shard_map/ppermute | solution.py:237
  6.7 6.1 %collective-permute-start.4 = (bf16[8,8320]{1,0:T(8,128)(2,1)S(1)}, bf16[8,8320]{1,0:T(8,128)(2,1)S(1)}, u32[]{:S(2)}, u32[]{:S(2)}) collective-permute-start(bf16[8,8320]{1,0:T(8,128)(2,1)S(1)} %get-tuple-element.21.refs_7_), channel_id=1, source_target_pairs={{0,8},{4,12},{8,0},{12,4},{16,24},{20,28},{24,16},{28,20},{1,9},{5... | collective-permute-start | bytes 399368 | tf_op jit(solution)/shard_map/ppermute | solution.py:237
  10.1 2.9 %collective-permute-start.6 = (bf16[8,8320]{1,0:T(8,128)(2,1)S(1)}, bf16[8,8320]{1,0:T(8,128)(2,1)S(1)}, u32[]{:S(2)}, u32[]{:S(2)}) collective-permute-start(bf16[8,8320]{1,0:T(8,128)(2,1)S(1)} %get-tuple-element.22), channel_id=1, source_target_pairs={{0,4},{4,0},{8,12},{12,8},{16,20},{20,16},{24,28},{28,24},{1,5},{5... | collective-permute-start | bytes 399368 | tf_op jit(solution)/shard_map/ppermute | solution.py:237
  10.2 2.9 %collective-permute-start.1 = (bf16[8,8320]{1,0:T(8,128)(2,1)S(1)}, bf16[8,8320]{1,0:T(8,128)(2,1)S(1)}, u32[]{:S(2)}, u32[]{:S(2)}) collective-permute-start(bf16[8,8320]{1,0:T(8,128)(2,1)S(1)} %collective-permute-done.refs_1_), channel_id=1, source_target_pairs={{0,4},{4,0},{8,12},{12,8},{16,20},{20,16},{24,28},{28,24},{1,5},{5... | collective-permute-start | bytes 399368 | tf_op jit(solution)/shard_map/ppermute | solution.py:237
  12.5 1.4 %collective-permute-start.3 = (bf16[8,8320]{1,0:T(8,128)(2,1)S(1)}, bf16[8,8320]{1,0:T(8,128)(2,1)S(1)}, u32[]{:S(2)}, u32[]{:S(2)}) collective-permute-start(bf16[8,8320]{1,0:T(8,128)(2,1)S(1)} %collective-permute-done.2.refs_3_), channel_id=1, source_target_pairs={{0,4},{4,0},{8,12},{12,8},{16,20},{20,16},{24,28},{28,24},{1,5},{5... | collective-permute-start | bytes 399368 | tf_op jit(solution)/shard_map/ppermute | solution.py:237
  12.8 1.4 %collective-permute-start.5 = (bf16[8,8320]{1,0:T(8,128)(2,1)S(1)}, bf16[8,8320]{1,0:T(8,128)(2,1)S(1)}, u32[]{:S(2)}, u32[]{:S(2)}) collective-permute-start(bf16[8,8320]{1,0:T(8,128)(2,1)S(1)} %collective-permute-done.4.refs_5_), channel_id=1, source_target_pairs={{0,4},{4,0},{8,12},{12,8},{16,20},{20,16},{24,28},{28,24},{1,5},{5... | collective-permute-start | bytes 399368 | tf_op jit(solution)/shard_map/ppermute | solution.py:237
  15.3 1.3 %collective-permute-start.7 = (f32[4,16,128]{2,1,0:T(8,128)S(1)}, f32[4,16,128]{2,1,0:T(8,128)S(1)}, u32[]{:S(2)}, u32[]{:S(2)}) collective-permute-start(f32[4,16,128]{2,1,0:T(8,128)S(1)} %get-tuple-element.26), channel_id=1, source_target_pairs={{0,4},{4,0},{8,12},{12,8},{16,20},{20,16},{24,28},{28,24},{1,5},{5... | collective-permute-start | bytes 98312 | tf_op jit(solution)/shard_map/ppermute | solution.py:237
  16.6 4.1 %collective-permute-start.10 = (f32[2,16,128]{2,1,0:T(8,128)S(1)}, f32[2,16,128]{2,1,0:T(8,128)S(1)}, u32[]{:S(2)}, u32[]{:S(2)}) collective-permute-start(f32[2,16,128]{2,1,0:T(8,128)S(1)} %pad_maximum_fusion.3), channel_id=1, source_target_pairs={{0,28},{4,24},{8,20},{12,16},{16,12},{20,8},{24,4},{28,0},{1,29},{... | collective-permute-start | bytes 49160 | tf_op jit(solution)/shard_map/ppermute | solution.py:237
  18.3 3.2 %collective-permute-start.9 = (f32[2,16,128]{2,1,0:T(8,128)S(1)}, f32[2,16,128]{2,1,0:T(8,128)S(1)}, u32[]{:S(2)}, u32[]{:S(2)}) collective-permute-start(f32[2,16,128]{2,1,0:T(8,128)S(1)} %pad_maximum_fusion.2), channel_id=1, source_target_pairs={{0,20},{4,16},{8,28},{12,24},{16,4},{20,0},{24,12},{28,8},{1,21},{... | collective-permute-start | bytes 49160 | tf_op jit(solution)/shard_map/ppermute | solution.py:237
  19.4 3.2 %collective-permute-start.8 = (f32[2,16,128]{2,1,0:T(8,128)S(1)}, f32[2,16,128]{2,1,0:T(8,128)S(1)}, u32[]{:S(2)}, u32[]{:S(2)}) collective-permute-start(f32[2,16,128]{2,1,0:T(8,128)S(1)} %pad_maximum_fusion.1), channel_id=1, source_target_pairs={{0,12},{4,8},{8,4},{12,0},{16,28},{20,24},{24,20},{28,16},{1,13},{... | collective-permute-start | bytes 49160 | tf_op jit(solution)/shard_map/ppermute | solution.py:237
  23.0 5.6 %collective-permute-start.11 = (f32[32,128]{1,0:T(8,128)S(1)}, f32[32,128]{1,0:T(8,128)S(1)}, u32[]{:S(2)}, u32[]{:S(2)}) collective-permute-start(f32[32,128]{1,0:T(8,128)S(1)} %get-tuple-element.28), channel_id=1, source_target_pairs={{0,1},{1,2},{2,3},{3,0},{4,5},{5,6},{6,7},{7,4},{8,9},{9,10},{10,1... | collective-permute-start | bytes 49160 | tf_op jit(solution)/shard_map/ppermute | solution.py:331
  24.6 4.6 %collective-permute-start.12 = (f32[32,128]{1,0:T(8,128)S(1)}, f32[32,128]{1,0:T(8,128)S(1)}, u32[]{:S(2)}, u32[]{:S(2)}) collective-permute-start(f32[32,128]{1,0:T(8,128)S(1)} %get-tuple-element.29), channel_id=1, source_target_pairs={{0,2},{1,3},{2,0},{3,1},{4,6},{5,7},{6,4},{7,5},{8,10},{9,11},{10,... | collective-permute-start | bytes 49160 | tf_op jit(solution)/shard_map/ppermute | solution.py:331
  27.2 3.7 %collective-permute-start.13 = (f32[32,128]{1,0:T(8,128)S(1)}, f32[32,128]{1,0:T(8,128)S(1)}, u32[]{:S(2)}, u32[]{:S(2)}) collective-permute-start(f32[32,128]{1,0:T(8,128)S(1)} %get-tuple-element.30), channel_id=1, source_target_pairs={{0,3},{1,0},{2,1},{3,2},{4,7},{5,4},{6,5},{7,6},{8,11},{9,8},{10,9... | collective-permute-start | bytes 49160 | tf_op jit(solution)/shard_map/ppermute | solution.py:331

commit v22 on v21

--- a/solution.py
+++ b/solution.py
@@ -11,7 +11,7 @@
 SMEM = pl.BlockSpec(memory_space=pltpu.SMEM)
 HBM = pl.BlockSpec(memory_space=pltpu.HBM)
 LANES = 128
-CHUNKS = 4
+CHUNKS = 8
 LOADS = 8
 
 
@@ -50,13 +50,10 @@
     ]
     for copy in copies:
         copy.start()
-    for copy in copies:
-        copy.wait()
     query_ref, in_factor_ref, out_factor_ref, home_ref, cand_ref = landing
     rows, width = query_ref.shape
     layers, rank, _ = in_factor_ref.shape
     half = rank // 2
-    query = query_ref[...].astype(jnp.float32)
     low = iota((half, LANES), 1) < rank
     zero = jnp.zeros((rank, rank), jnp.float32)
     terms = [(0, 0), (0, 1), (0, 2), (1, 0), (1, 1), (2, 0)]
@@ -66,48 +63,33 @@
     column_found = (source == 2 * (inside % half) + place // group)
     chosen_part = sum((inside >= half * start).astype(jnp.int32) for start in (3, 5, 6))
     pickers = [exact_bf16(column_found & (chosen_part == i)) for i in range(3)]
+    for copy in copies[1:]:
+        copy.wait()
+    doubled, quarters = [], []
     for layer in range(layers):
-        first = layer * half
-        packed = jnp.concatenate(
-            [query[:, (first + t) * LANES:(first + t + 1) * LANES] for t in range(half)], axis=0
-        ).astype(jnp.bfloat16)
         factor = in_factor_ref[layer]
-        doubled = parts_of(
-            jnp.concatenate(
-                [jnp.concatenate([factor, zero], axis=1), jnp.concatenate([zero, factor], axis=1)], axis=0
+        doubled.append(
+            parts_of(
+                jnp.concatenate(
+                    [jnp.concatenate([factor, zero], axis=1), jnp.concatenate([zero, factor], axis=1)], axis=0
+                )
             )
         )
-        small = jnp.dot(
-            jnp.concatenate([packed, packed], axis=1), jnp.concatenate(doubled[1:], axis=0),
-            preferred_element_type=jnp.float32,
-        )
-        turned_ref[layer] = small + jnp.dot(packed, doubled[0], preferred_element_type=jnp.float32)
-        wide = jnp.concatenate([turned_ref[layer, pl.ds(q, half, stride=rows), :] for q in range(rows)], axis=1)
-        wide = parts_of(wide)
-        stacked = jnp.concatenate([wide[j] for _, j in terms], axis=0)
         by_row = jnp.concatenate(
             [out_factor_ref[layer, pl.ds(parity, half, stride=2), :] for parity in range(2)], axis=0
         )
         sorted_columns = sum(
             jnp.dot(part, picker, preferred_element_type=jnp.float32) for part, picker in zip(parts_of(by_row), pickers)
         )
-        quarters = jnp.concatenate(
-            [
-                sorted_columns[r * half:(r + 1) * half, c * group:c * group + len(terms) * half]
-                for r in range(2) for c in range(2)
-            ],
-            axis=0,
-        ).astype(jnp.bfloat16)
-        left = jnp.dot(quarters, stacked, preferred_element_type=jnp.float32)
-        for q in range(rows):
-            part = left[:, q * LANES:(q + 1) * LANES]
-            ee, eo, oe, oo = (part[i * half:(i + 1) * half] for i in range(4))
-            done = jnp.where(low, ee, oo) + pltpu.roll(jnp.where(low, oe, eo), rank, 1)
-            turned_ref[layer, pl.ds(q, half, stride=rows), :] = done
-        for t in range(half):
-            tile = turned_ref[layer, t * rows:(t + 1) * rows, :].astype(jnp.bfloat16)
-            for target_ref in (packed_ref, again_ref):
-                target_ref[:, (first + t) * LANES:(first + t + 1) * LANES] = tile
+        quarters.append(
+            jnp.concatenate(
+                [
+                    sorted_columns[r * half:(r + 1) * half, c * group:c * group + len(terms) * half]
+                    for r in range(2) for c in range(2)
+                ],
+                axis=0,
+            ).astype(jnp.bfloat16)
+        )
 
     slots = cand_ref.shape[1]
     home_rows = home_ref.shape[0]
@@ -135,6 +117,32 @@
     for target_ref in (packed_ref, again_ref):
         target_ref[:, width:] = jnp.concatenate(blocks, axis=1).astype(jnp.bfloat16)
     found_ref[...] = jnp.concatenate([holder, rank_there, jnp.zeros((6, slots), jnp.float32)], axis=0)
+
+    copies[0].wait()
+    query = query_ref[...].astype(jnp.float32)
+    for layer in range(layers):
+        first = layer * half
+        packed = jnp.concatenate(
+            [query[:, (first + t) * LANES:(first + t + 1) * LANES] for t in range(half)], axis=0
+        ).astype(jnp.bfloat16)
+        small = jnp.dot(
+            jnp.concatenate([packed, packed], axis=1), jnp.concatenate(doubled[layer][1:], axis=0),
+            preferred_element_type=jnp.float32,
+        )
+        turned_ref[layer] = small + jnp.dot(packed, doubled[layer][0], preferred_element_type=jnp.float32)
+        wide = jnp.concatenate([turned_ref[layer, pl.ds(q, half, stride=rows), :] for q in range(rows)], axis=1)
+        wide = parts_of(wide)
+        stacked = jnp.concatenate([wide[j] for _, j in terms], axis=0)
+        left = jnp.dot(quarters[layer], stacked, preferred_element_type=jnp.float32)
+        for q in range(rows):
+            part = left[:, q * LANES:(q + 1) * LANES]
+            ee, eo, oe, oo = (part[i * half:(i + 1) * half] for i in range(4))
+            done = jnp.where(low, ee, oo) + pltpu.roll(jnp.where(low, oe, eo), rank, 1)
+            turned_ref[layer, pl.ds(q, half, stride=rows), :] = done
+        for t in range(half):
+            tile = turned_ref[layer, t * rows:(t + 1) * rows, :].astype(jnp.bfloat16)
+            for target_ref in (packed_ref, again_ref):
+                target_ref[:, (first + t) * LANES:(first + t + 1) * LANES] = tile
 
 
 def load_kernel(holders, count_ref, found_ref, block_ref, source_ref, same_block_ref, target_ref, used_ref, landing, arrived):

time: 31.8 us -> 32 us (level)
  no operation moved by 1% of the time
where the time goes in v22:
time: 32 us; the launch traced here: 31.9 us
  starting transfers between devices  14.4 us (45%)
  waiting for transfers between devices  9.1 us (28%)
  Pallas kernels  6.9 us (22%)
  between operations  0.72 us (2%)
  other arithmetic  0.64 us (2%)
    ppermute x11, starting transfers between devices, swap(): lax.ppermute(value, axis, [(i, i ^ distance) for i in range(lax.axis_size...  8.84 us
    ppermute x11, waiting for transfers between devices, swap(): lax.ppermute(value, axis, [(i, i ^ distance) for i in range(lax.axis_size...  6.71 us
    ppermute x3, starting transfers between devices, on_device(): lax.ppermute(terms[step], 'layer', [(g, (g + step) % groups) for g in ran...  5.56 us
    pallas_call x1, Pallas kernels, on_device(): pl.pallas_call(functools.partial(load_kernel, holders), out_shape=[jax.Sh...  2.65 us
    ppermute x3, waiting for transfers between devices, on_device(): lax.ppermute(terms[step], 'layer', [(g, (g + step) % groups) for g in ran...  2.39 us
    pallas_call x1, Pallas kernels, on_device(): pl.pallas_call(functools.partial(condition_kernel, holders, capacity, per...  2.37 us
    pallas_call x1, Pallas kernels, on_device(): pl.pallas_call(functools.partial(score_kernel, holders, capacity), out_sh...  1.18 us
  transfers between devices with their start and end apart: 14, of which 10 were waited for; matrix products, arithmetic and copies ran while one was open for 0% of the time, Pallas kernels for 9%

profile of v22, /device:TPU:0, one launch (start us, length us, event | category | flops | bytes accessed | tf_op | source)
XLA Modules:
  0.0 31.9 jit_solution(1570232879625979403)
XLA Ops:
  0.0 2.4 %shard_map.73 = (bf16[8,8320]{1,0:T(8,128)(2,1)S(1)}, bf16[8,8320]{1,0:T(8,128)(2,1)S(1)}, f32[8,256]{1,0:T(8,128)S(1)}) custom-call(bf16[8,8192]{1,0:T(8,128)(2,1)} %refs_0_.1, f32[2,64,64]{2,1,0:T(8,128)} %refs_1_.1, f32[2,64,64]{2,1,0:T(8,128)} %refs_2_.1, s32[16,128]{1,0:T(8,128)} %bitcast.3, s32[1,256]{1,0:T(1,128)} %refs_4_.1), custom_call_target="tpu_custom_call" | custom-call | tf_op jit(solution)/shard_map/pallas_call | solution.py:264
  2.4 4.0 %collective-permute-start = (bf16[8,8320]{1,0:T(8,128)(2,1)S(1)}, bf16[8,8320]{1,0:T(8,128)(2,1)S(1)}, u32[]{:S(2)}, u32[]{:S(2)}) collective-permute-start(bf16[8,8320]{1,0:T(8,128)(2,1)S(1)} %get-tuple-element.21.refs_7_), channel_id=1, source_target_pairs={{0,24},{4,28},{8,16},{12,20},{16,8},{20,12},{24,0},{28,4},{1,25},{... | collective-permute-start | bytes 399368 | tf_op jit(solution)/shard_map/ppermute | solution.py:245
  6.3 0.5 %collective-permute-start.2 = (bf16[8,8320]{1,0:T(8,128)(2,1)S(1)}, bf16[8,8320]{1,0:T(8,128)(2,1)S(1)}, u32[]{:S(2)}, u32[]{:S(2)}) collective-permute-start(bf16[8,8320]{1,0:T(8,128)(2,1)S(1)} %get-tuple-element.21.refs_7_), channel_id=1, source_target_pairs={{0,16},{4,20},{8,24},{12,28},{16,0},{20,4},{24,8},{28,12},{1,17},{... | collective-permute-start | bytes 399368 | tf_op jit(solution)/shard_map/ppermute | solution.py:245
  6.8 0.1 collective-permute-start.4
  7.6 2.7 %shard_map.74 = (bf16[8,8320]{1,0:T(8,128)(2,1)S(1)}, bf16[8192,256]{1,0:T(8,128)(2,1)S(1)}, f32[8,256]{1,0:T(8,128)S(1)}) custom-call(s32[1]{0:T(128)S(6)} %copy.10.count_ref, f32[8,256]{1,0:T(8,128)S(1)} %get-tuple-element.18.found_ref, bf16[8,8320]{1,0:T(8,128)(2,1)S(1)} %get-tuple-element.19.block_ref, ...), custom_call_target="tpu_custom_call", output_to_operand_aliasing={{0}: (2, {})} | custom-call | bytes 4194304 | tf_op jit(solution)/shard_map/pallas_call | solution.py:278
  10.3 0.1 collective-permute-start.6
  10.4 0.0 collective-permute-done.refs_1_
  10.4 0.5 %collective-permute-start.1 = (bf16[8,8320]{1,0:T(8,128)(2,1)S(1)}, bf16[8,8320]{1,0:T(8,128)(2,1)S(1)}, u32[]{:S(2)}, u32[]{:S(2)}) collective-permute-start(bf16[8,8320]{1,0:T(8,128)(2,1)S(1)} %collective-permute-done.refs_1_), channel_id=1, source_target_pairs={{0,4},{4,0},{8,12},{12,8},{16,20},{20,16},{24,28},{28,24},{1,5},{5... | collective-permute-start | bytes 399368 | tf_op jit(solution)/shard_map/ppermute | solution.py:245
  10.9 1.9 %collective-permute-done.2.refs_3_ = bf16[8,8320]{1,0:T(8,128)(2,1)S(1)} collective-permute-done((bf16[8,8320]{1,0:T(8,128)(2,1)S(1)}, bf16[8,8320]{1,0:T(8,128)(2,1)S(1)}, u32[]{:S(2)}, u32[]{:S(2)}) %collective-permute-start.2) | collective-permute-done | bytes 133152 | tf_op jit(solution)/shard_map/ppermute | solution.py:245
  12.7 0.0 collective-permute-start.3
  12.7 0.2 collective-permute-done.4.refs_5_
  13.0 0.3 collective-permute-start.5
  13.2 0.0 collective-permute-done.6.refs_6_
  13.2 0.0 collective-permute-done.1.refs_0_
  13.2 0.8 %collective-permute-done.3.refs_2_ = bf16[8,8320]{1,0:T(8,128)(2,1)S(1)} collective-permute-done((bf16[8,8320]{1,0:T(8,128)(2,1)S(1)}, bf16[8,8320]{1,0:T(8,128)(2,1)S(1)}, u32[]{:S(2)}, u32[]{:S(2)}) %collective-permute-start.3) | collective-permute-done | bytes 133152 | tf_op jit(solution)/shard_map/ppermute | solution.py:245
  14.1 0.2 collective-permute-done.5.refs_4_
  14.3 1.2 %shard_map.75 = (f32[4,16,128]{2,1,0:T(8,128)S(1)}, f32[64,256]{1,0:T(8,128)S(1)}, f32[1,128]{1,0:T(1,128)S(1)}) custom-call(bf16[8,8320]{1,0:T(8,128)(2,1)S(1)} %collective-permute-done.1.refs_0_, bf16[8,8320]{1,0:T(8,128)(2,1)S(1)} %collective-permute-done.refs_1_, bf16[8,8320]{1,0:T(8,128)(2,1)S(1)} %collective-permute-done.3.refs_2_, ...), custom_call_target="tpu_custom_call" | custom-call | tf_op jit(solution)/shard_map/pallas_call | solution.py:304
  15.5 0.3 collective-permute-start.7
  15.8 0.3 shard_map.76
  16.1 0.6 %collective-permute-done.7 = f32[4,16,128]{2,1,0:T(8,128)S(1)} collective-permute-done((f32[4,16,128]{2,1,0:T(8,128)S(1)}, f32[4,16,128]{2,1,0:T(8,128)S(1)}, u32[]{:S(2)}, u32[]{:S(2)}) %collective-permute-start.7) | collective-permute-done | bytes 32800 | tf_op jit(solution)/shard_map/ppermute | solution.py:245
  16.8 1.7 %collective-permute-start.10 = (f32[2,16,128]{2,1,0:T(8,128)S(1)}, f32[2,16,128]{2,1,0:T(8,128)S(1)}, u32[]{:S(2)}, u32[]{:S(2)}) collective-permute-start(f32[2,16,128]{2,1,0:T(8,128)S(1)} %pad_maximum_fusion.3), channel_id=1, source_target_pairs={{0,28},{4,24},{8,20},{12,16},{16,12},{20,8},{24,4},{28,0},{1,29},{... | collective-permute-start | bytes 49160 | tf_op jit(solution)/shard_map/ppermute | solution.py:245
  18.5 1.1 %collective-permute-start.9 = (f32[2,16,128]{2,1,0:T(8,128)S(1)}, f32[2,16,128]{2,1,0:T(8,128)S(1)}, u32[]{:S(2)}, u32[]{:S(2)}) collective-permute-start(f32[2,16,128]{2,1,0:T(8,128)S(1)} %pad_maximum_fusion.2), channel_id=1, source_target_pairs={{0,20},{4,16},{8,28},{12,24},{16,4},{20,0},{24,12},{28,8},{1,21},{... | collective-permute-start | bytes 49160 | tf_op jit(solution)/shard_map/ppermute | solution.py:245
  19.6 0.3 collective-permute-start.8
  19.9 1.0 %collective-permute-done.10.refs_3_ = f32[2,16,128]{2,1,0:T(8,128)S(1)} collective-permute-done((f32[2,16,128]{2,1,0:T(8,128)S(1)}, f32[2,16,128]{2,1,0:T(8,128)S(1)}, u32[]{:S(2)}, u32[]{:S(2)}) %collective-permute-start.10) | collective-permute-done | bytes 16416 | tf_op jit(solution)/shard_map/ppermute | solution.py:245
  20.8 0.8 %collective-permute-done.9.refs_2_ = f32[2,16,128]{2,1,0:T(8,128)S(1)} collective-permute-done((f32[2,16,128]{2,1,0:T(8,128)S(1)}, f32[2,16,128]{2,1,0:T(8,128)S(1)}, u32[]{:S(2)}, u32[]{:S(2)}) %collective-permute-start.9) | collective-permute-done | bytes 16416 | tf_op jit(solution)/shard_map/ppermute | solution.py:245
  21.6 1.1 %collective-permute-done.8.refs_1_ = f32[2,16,128]{2,1,0:T(8,128)S(1)} collective-permute-done((f32[2,16,128]{2,1,0:T(8,128)S(1)}, f32[2,16,128]{2,1,0:T(8,128)S(1)}, u32[]{:S(2)}, u32[]{:S(2)}) %collective-permute-start.8) | collective-permute-done | bytes 16416 | tf_op jit(solution)/shard_map/ppermute | solution.py:245
  22.8 0.4 %shard_map.77 = (f32[32,128]{1,0:T(8,128)S(1)}, f32[32,128]{1,0:T(8,128)S(1)}, f32[32,128]{1,0:T(8,128)S(1)}, f32[32,128]{1,0:T(8,128)S(1)}) custom-call(f32[8,256]{1,0:T(8,128)S(1)} %get-tuple-element.20.found_ref, f32[2,16,128]{2,1,0:T(8,128)S(1)} %pad_maximum_fusion.refs_0_, f32[2,16,128]{2,1,0:T(8,128)S(1)} %collective-permute-done.8.refs_1_, ...), custom_call_target="tpu_custom_call" | custom-call | tf_op jit(solution)/shard_map/pallas_call | solution.py:330
  23.2 1.6 %collective-permute-start.11 = (f32[32,128]{1,0:T(8,128)S(1)}, f32[32,128]{1,0:T(8,128)S(1)}, u32[]{:S(2)}, u32[]{:S(2)}) collective-permute-start(f32[32,128]{1,0:T(8,128)S(1)} %get-tuple-element.28), channel_id=1, source_target_pairs={{0,1},{1,2},{2,3},{3,0},{4,5},{5,6},{6,7},{7,4},{8,9},{9,10},{10,1... | collective-permute-start | bytes 49160 | tf_op jit(solution)/shard_map/ppermute | solution.py:339
  24.8 2.6 %collective-permute-start.12 = (f32[32,128]{1,0:T(8,128)S(1)}, f32[32,128]{1,0:T(8,128)S(1)}, u32[]{:S(2)}, u32[]{:S(2)}) collective-permute-start(f32[32,128]{1,0:T(8,128)S(1)} %get-tuple-element.29), channel_id=1, source_target_pairs={{0,2},{1,3},{2,0},{3,1},{4,6},{5,7},{6,4},{7,5},{8,10},{9,11},{10,... | collective-permute-start | bytes 49160 | tf_op jit(solution)/shard_map/ppermute | solution.py:339
  27.4 1.3 %collective-permute-start.13 = (f32[32,128]{1,0:T(8,128)S(1)}, f32[32,128]{1,0:T(8,128)S(1)}, u32[]{:S(2)}, u32[]{:S(2)}) collective-permute-start(f32[32,128]{1,0:T(8,128)S(1)} %get-tuple-element.30), channel_id=1, source_target_pairs={{0,3},{1,0},{2,1},{3,2},{4,7},{5,4},{6,5},{7,6},{8,11},{9,8},{10,9... | collective-permute-start | bytes 49160 | tf_op jit(solution)/shard_map/ppermute | solution.py:339
  28.8 0.0 collective-permute-done.11
  28.8 0.7 %collective-permute-done.12 = f32[32,128]{1,0:T(8,128)S(1)} collective-permute-done((f32[32,128]{1,0:T(8,128)S(1)}, f32[32,128]{1,0:T(8,128)S(1)}, u32[]{:S(2)}, u32[]{:S(2)}) %collective-permute-start.12) | collective-permute-done | bytes 16416 | tf_op jit(solution)/shard_map/ppermute | solution.py:339
  29.5 1.7 %collective-permute-done.13 = f32[32,128]{1,0:T(8,128)S(1)} collective-permute-done((f32[32,128]{1,0:T(8,128)S(1)}, f32[32,128]{1,0:T(8,128)S(1)}, u32[]{:S(2)}, u32[]{:S(2)}) %collective-permute-start.13) | collective-permute-done | bytes 16416 | tf_op jit(solution)/shard_map/ppermute | solution.py:339
  31.2 0.1 fusion.2
  31.2 0.6 %maximum_bitcast_fusion = f32[1,64,64]{2,1,0:T(8,128)} fusion(f32[32,64]{1,0:T(8,128)S(1)} %get-tuple-element.40, f32[32,64]{1,0:T(8,128)S(1)} %get-tuple-element.39), kind=kLoop, calls=%fused_computation | loop fusion | flops 4096 | bytes 32768 | tf_op jit(solution)/shard_map/broadcast_in_dim | solution.py:340
  (7 shorter events, 0.1 us)
Async XLA Ops:
  2.4 8.0 %collective-permute-start = (bf16[8,8320]{1,0:T(8,128)(2,1)S(1)}, bf16[8,8320]{1,0:T(8,128)(2,1)S(1)}, u32[]{:S(2)}, u32[]{:S(2)}) collective-permute-start(bf16[8,8320]{1,0:T(8,128)(2,1)S(1)} %get-tuple-element.21.refs_7_), channel_id=1, source_target_pairs={{0,24},{4,28},{8,16},{12,20},{16,8},{20,12},{24,0},{28,4},{1,25},{... | collective-permute-start | bytes 399368 | tf_op jit(solution)/shard_map/ppermute | solution.py:245
  6.3 6.4 %collective-permute-start.2 = (bf16[8,8320]{1,0:T(8,128)(2,1)S(1)}, bf16[8,8320]{1,0:T(8,128)(2,1)S(1)}, u32[]{:S(2)}, u32[]{:S(2)}) collective-permute-start(bf16[8,8320]{1,0:T(8,128)(2,1)S(1)} %get-tuple-element.21.refs_7_), channel_id=1, source_target_pairs={{0,16},{4,20},{8,24},{12,28},{16,0},{20,4},{24,8},{28,12},{1,17},{... | collective-permute-start | bytes 399368 | tf_op jit(solution)/shard_map/ppermute | solution.py:245
  6.8 6.1 %collective-permute-start.4 = (bf16[8,8320]{1,0:T(8,128)(2,1)S(1)}, bf16[8,8320]{1,0:T(8,128)(2,1)S(1)}, u32[]{:S(2)}, u32[]{:S(2)}) collective-permute-start(bf16[8,8320]{1,0:T(8,128)(2,1)S(1)} %get-tuple-element.21.refs_7_), channel_id=1, source_target_pairs={{0,8},{4,12},{8,0},{12,4},{16,24},{20,28},{24,16},{28,20},{1,9},{5... | collective-permute-start | bytes 399368 | tf_op jit(solution)/shard_map/ppermute | solution.py:245
  10.3 2.9 %collective-permute-start.6 = (bf16[8,8320]{1,0:T(8,128)(2,1)S(1)}, bf16[8,8320]{1,0:T(8,128)(2,1)S(1)}, u32[]{:S(2)}, u32[]{:S(2)}) collective-permute-start(bf16[8,8320]{1,0:T(8,128)(2,1)S(1)} %get-tuple-element.22), channel_id=1, source_target_pairs={{0,4},{4,0},{8,12},{12,8},{16,20},{20,16},{24,28},{28,24},{1,5},{5... | collective-permute-start | bytes 399368 | tf_op jit(solution)/shard_map/ppermute | solution.py:245
  10.4 2.9 %collective-permute-start.1 = (bf16[8,8320]{1,0:T(8,128)(2,1)S(1)}, bf16[8,8320]{1,0:T(8,128)(2,1)S(1)}, u32[]{:S(2)}, u32[]{:S(2)}) collective-permute-start(bf16[8,8320]{1,0:T(8,128)(2,1)S(1)} %collective-permute-done.refs_1_), channel_id=1, source_target_pairs={{0,4},{4,0},{8,12},{12,8},{16,20},{20,16},{24,28},{28,24},{1,5},{5... | collective-permute-start | bytes 399368 | tf_op jit(solution)/shard_map/ppermute | solution.py:245
  12.7 1.4 %collective-permute-start.3 = (bf16[8,8320]{1,0:T(8,128)(2,1)S(1)}, bf16[8,8320]{1,0:T(8,128)(2,1)S(1)}, u32[]{:S(2)}, u32[]{:S(2)}) collective-permute-start(bf16[8,8320]{1,0:T(8,128)(2,1)S(1)} %collective-permute-done.2.refs_3_), channel_id=1, source_target_pairs={{0,4},{4,0},{8,12},{12,8},{16,20},{20,16},{24,28},{28,24},{1,5},{5... | collective-permute-start | bytes 399368 | tf_op jit(solution)/shard_map/ppermute | solution.py:245
  13.0 1.4 %collective-permute-start.5 = (bf16[8,8320]{1,0:T(8,128)(2,1)S(1)}, bf16[8,8320]{1,0:T(8,128)(2,1)S(1)}, u32[]{:S(2)}, u32[]{:S(2)}) collective-permute-start(bf16[8,8320]{1,0:T(8,128)(2,1)S(1)} %collective-permute-done.4.refs_5_), channel_id=1, source_target_pairs={{0,4},{4,0},{8,12},{12,8},{16,20},{20,16},{24,28},{28,24},{1,5},{5... | collective-permute-start | bytes 399368 | tf_op jit(solution)/shard_map/ppermute | solution.py:245
  15.5 1.3 %collective-permute-start.7 = (f32[4,16,128]{2,1,0:T(8,128)S(1)}, f32[4,16,128]{2,1,0:T(8,128)S(1)}, u32[]{:S(2)}, u32[]{:S(2)}) collective-permute-start(f32[4,16,128]{2,1,0:T(8,128)S(1)} %get-tuple-element.26), channel_id=1, source_target_pairs={{0,4},{4,0},{8,12},{12,8},{16,20},{20,16},{24,28},{28,24},{1,5},{5... | collective-permute-start | bytes 98312 | tf_op jit(solution)/shard_map/ppermute | solution.py:245
  16.8 4.1 %collective-permute-start.10 = (f32[2,16,128]{2,1,0:T(8,128)S(1)}, f32[2,16,128]{2,1,0:T(8,128)S(1)}, u32[]{:S(2)}, u32[]{:S(2)}) collective-permute-start(f32[2,16,128]{2,1,0:T(8,128)S(1)} %pad_maximum_fusion.3), channel_id=1, source_target_pairs={{0,28},{4,24},{8,20},{12,16},{16,12},{20,8},{24,4},{28,0},{1,29},{... | collective-permute-start | bytes 49160 | tf_op jit(solution)/shard_map/ppermute | solution.py:245
  18.5 3.2 %collective-permute-start.9 = (f32[2,16,128]{2,1,0:T(8,128)S(1)}, f32[2,16,128]{2,1,0:T(8,128)S(1)}, u32[]{:S(2)}, u32[]{:S(2)}) collective-permute-start(f32[2,16,128]{2,1,0:T(8,128)S(1)} %pad_maximum_fusion.2), channel_id=1, source_target_pairs={{0,20},{4,16},{8,28},{12,24},{16,4},{20,0},{24,12},{28,8},{1,21},{... | collective-permute-start | bytes 49160 | tf_op jit(solution)/shard_map/ppermute | solution.py:245
  19.6 3.2 %collective-permute-start.8 = (f32[2,16,128]{2,1,0:T(8,128)S(1)}, f32[2,16,128]{2,1,0:T(8,128)S(1)}, u32[]{:S(2)}, u32[]{:S(2)}) collective-permute-start(f32[2,16,128]{2,1,0:T(8,128)S(1)} %pad_maximum_fusion.1), channel_id=1, source_target_pairs={{0,12},{4,8},{8,4},{12,0},{16,28},{20,24},{24,20},{28,16},{1,13},{... | collective-permute-start | bytes 49160 | tf_op jit(solution)/shard_map/ppermute | solution.py:245
  23.2 5.6 %collective-permute-start.11 = (f32[32,128]{1,0:T(8,128)S(1)}, f32[32,128]{1,0:T(8,128)S(1)}, u32[]{:S(2)}, u32[]{:S(2)}) collective-permute-start(f32[32,128]{1,0:T(8,128)S(1)} %get-tuple-element.28), channel_id=1, source_target_pairs={{0,1},{1,2},{2,3},{3,0},{4,5},{5,6},{6,7},{7,4},{8,9},{9,10},{10,1... | collective-permute-start | bytes 49160 | tf_op jit(solution)/shard_map/ppermute | solution.py:339
  24.8 4.6 %collective-permute-start.12 = (f32[32,128]{1,0:T(8,128)S(1)}, f32[32,128]{1,0:T(8,128)S(1)}, u32[]{:S(2)}, u32[]{:S(2)}) collective-permute-start(f32[32,128]{1,0:T(8,128)S(1)} %get-tuple-element.29), channel_id=1, source_target_pairs={{0,2},{1,3},{2,0},{3,1},{4,6},{5,7},{6,4},{7,5},{8,10},{9,11},{10,... | collective-permute-start | bytes 49160 | tf_op jit(solution)/shard_map/ppermute | solution.py:339
  27.4 3.7 %collective-permute-start.13 = (f32[32,128]{1,0:T(8,128)S(1)}, f32[32,128]{1,0:T(8,128)S(1)}, u32[]{:S(2)}, u32[]{:S(2)}) collective-permute-start(f32[32,128]{1,0:T(8,128)S(1)} %get-tuple-element.30), channel_id=1, source_target_pairs={{0,3},{1,0},{2,1},{3,2},{4,7},{5,4},{6,5},{7,6},{8,11},{9,8},{10,9... | collective-permute-start | bytes 49160 | tf_op jit(solution)/shard_map/ppermute | solution.py:339

commit v23 on v21

--- a/solution.py
+++ b/solution.py
@@ -17,10 +17,6 @@
 
 def iota(shape, dimension):
     return lax.broadcasted_iota(jnp.int32, shape, dimension)
-
-
-def kept_distances(holders):
-    return [0] + [k + 1 for k in range(2, holders, 2)]
 
 
 def parts_of(value):
@@ -186,14 +182,23 @@
         for block in range(1, holders // rows):
             mine = jnp.where(me // rows == block, notes[:, block * capacity:(block + 1) * capacity], mine)
         asked.append(mine)
-    kept = kept_distances(holders)
+    chips = holders // 2
+    chip = me // 2
+    kept, handed = [asked[0]], [asked[1]]
+    for step in range(1, chips):
+        apart = chip ^ ((chip + step) % chips)
+        for rows_of, core in ((kept, 1), (handed, 0)):
+            chosen = asked[2 + core]
+            for distance in range(2, chips):
+                chosen = jnp.where(apart == distance, asked[2 * distance + core], chosen)
+            rows_of.append(chosen)
     wanted = [
-        jnp.concatenate([asked[k][:, side * half:(side + 1) * half] for side in range(2) for k in distances], axis=1)
-        for distances in ([k ^ 1 for k in kept], kept)
+        jnp.concatenate([row[:, side * half:(side + 1) * half] for side in range(2) for row in rows_of], axis=1)
+        for rows_of in (handed, kept)
     ]
     rest_ref[...] = wanted[1]
     picked = pick(scores_ref[...], wanted[0])
-    for place in range(len(kept)):
+    for place in range(chips):
         send_ref[place] = picked[place * half:(place + 1) * half]
 
 
@@ -205,15 +210,19 @@
 
 
 def spread_kernel(holders, groups, found_ref, *refs):
-    landed_refs, out_refs = refs[:holders // 2], refs[holders // 2:]
+    landed_refs, out_refs = refs[:holders // 2][::-1], refs[holders // 2:]
     half = landed_refs[0].shape[1]
     slots = found_ref.shape[1]
     total = landed_refs[0].shape[2] // 2
     at = lax.axis_index("layer")
     share = slots // groups
-    distance = found_ref[0:1].astype(jnp.int32) ^ lax.axis_index("store")
-    order = [k ^ core for k in kept_distances(holders) for core in range(2)]
-    begins = sum(jnp.where(distance == k, place * half + 1, 0) for place, k in enumerate(order)).astype(jnp.float32) - 1.0
+    me = lax.axis_index("store")
+    chips = holders // 2
+    holder = found_ref[0:1].astype(jnp.int32)
+    step = (me // 2 - holder // 2 + 2 * chips) % chips
+    same_core = (holder % 2 == me % 2).astype(jnp.int32)
+    place = 2 * step + jnp.where(step == 0, 1 - same_core, same_core)
+    begins = jnp.where(holder < holders, place * half, -1).astype(jnp.float32)
     rank_there = found_ref[1:2]
     place = iota((2 * holders * half, slots), 0).astype(jnp.float32)
     upper = rank_there >= half
@@ -314,10 +323,12 @@
         out_specs=VMEM,
         compiler_params=pltpu.CompilerParams(vmem_limit_bytes=4 * 2**20 + 24 * total * slots),
     )(scores, rest)
+    chips = holders // 2
     landed = []
-    for place, k in enumerate(kept_distances(holders)):
-        pair = jnp.stack([keep[place], handed[place]])
-        landed.append(swap(pair, "store", k) if k else pair)
+    for step in range(chips):
+        pair = jnp.stack([keep[step], handed[step]])
+        to = [(i, (i // 2 + step) % chips * 2 + 1 - i % 2) for i in range(holders)]
+        landed.append(lax.ppermute(pair, "store", to) if step else pair)
     share = slots // groups
     terms = pl.pallas_call(
         functools.partial(spread_kernel, holders, groups),
@@ -325,7 +336,7 @@
         in_specs=[VMEM] * (1 + len(landed)),
         out_specs=[VMEM] * groups,
         compiler_params=pltpu.CompilerParams(vmem_limit_bytes=4 * 2**20 + 64 * total * slots),
-    )(used, *landed)
+    )(used, *landed[::-1])
     summed = terms[0]
     for step in range(1, groups):
         summed = summed + lax.ppermute(terms[step], "layer", [(g, (g + step) % groups) for g in range(groups)])

time: 31.8 us -> 31.5 us (level)
  waiting for transfers between devices: 9.1 us -> 7.65 us
  starting transfers between devices: 14.4 us -> 15.5 us
    ppermute x0 -> x3, starting transfers between devices: none -> 4.22 us  [on_device(): landed.append(lax.ppermute(pair, 'store', to) if step else pair)]
    ppermute x11 -> x8, starting transfers between devices: 8.82 us -> 5.75 us  [swap(): lax.ppermute(value, axis, [(i, i ^ distance) for i in range(lax.axis_size...]
    ppermute x11 -> x8, waiting for transfers between devices: 6.71 us -> 3.82 us  [swap(): lax.ppermute(value, axis, [(i, i ^ distance) for i in range(lax.axis_size...]
    ppermute x0 -> x3, waiting for transfers between devices: none -> 1.44 us  [on_device(): landed.append(lax.ppermute(pair, 'store', to) if step else pair)]
  transfers between devices with their start and end apart: 14 -> 14, of which waited for: 10 -> 9; matrix products, arithmetic and copies ran while one was open for 0% -> 0% of each run, Pallas kernels for 9% -> 9%
where the time goes in v23:
time: 31.5 us; the launch traced here: 31.4 us
  starting transfers between devices  15.5 us (49%)
  waiting for transfers between devices  7.65 us (24%)
  Pallas kernels  6.71 us (21%)
  between operations  0.72 us (2%)
  other arithmetic  0.64 us (2%)
    ppermute x8, starting transfers between devices, swap(): lax.ppermute(value, axis, [(i, i ^ distance) for i in range(lax.axis_size...  5.75 us
    ppermute x3, starting transfers between devices, on_device(): lax.ppermute(terms[step], 'layer', [(g, (g + step) % groups) for g in ran...  5.58 us
    ppermute x3, starting transfers between devices, on_device(): landed.append(lax.ppermute(pair, 'store', to) if step else pair)  4.22 us
    ppermute x8, waiting for transfers between devices, swap(): lax.ppermute(value, axis, [(i, i ^ distance) for i in range(lax.axis_size...  3.82 us
    pallas_call x1, Pallas kernels, on_device(): pl.pallas_call(functools.partial(load_kernel, holders), out_shape=[jax.Sh...  2.65 us
    ppermute x3, waiting for transfers between devices, on_device(): lax.ppermute(terms[step], 'layer', [(g, (g + step) % groups) for g in ran...  2.39 us
    pallas_call x1, Pallas kernels, on_device(): pl.pallas_call(functools.partial(condition_kernel, holders, capacity, per...  2.17 us
    ppermute x3, waiting for transfers between devices, on_device(): landed.append(lax.ppermute(pair, 'store', to) if step else pair)  1.44 us
  transfers between devices with their start and end apart: 14, of which 9 were waited for; matrix products, arithmetic and copies ran while one was open for 0% of the time, Pallas kernels for 9%

profile of v23, /device:TPU:0, one launch (start us, length us, event | category | flops | bytes accessed | tf_op | source)
XLA Modules:
  0.0 31.4 jit_solution(1313872868899278063)
XLA Ops:
  0.0 2.2 %shard_map.73 = (bf16[8,8320]{1,0:T(8,128)(2,1)S(1)}, bf16[8,8320]{1,0:T(8,128)(2,1)S(1)}, f32[8,256]{1,0:T(8,128)S(1)}) custom-call(bf16[8,8192]{1,0:T(8,128)(2,1)} %refs_0_.1, f32[2,64,64]{2,1,0:T(8,128)} %refs_1_.1, f32[2,64,64]{2,1,0:T(8,128)} %refs_2_.1, s32[16,128]{1,0:T(8,128)} %bitcast.3, s32[1,256]{1,0:T(1,128)} %refs_4_.1), custom_call_target="tpu_custom_call" | custom-call | tf_op jit(solution)/shard_map/pallas_call | solution.py:265
  2.2 4.0 %collective-permute-start = (bf16[8,8320]{1,0:T(8,128)(2,1)S(1)}, bf16[8,8320]{1,0:T(8,128)(2,1)S(1)}, u32[]{:S(2)}, u32[]{:S(2)}) collective-permute-start(bf16[8,8320]{1,0:T(8,128)(2,1)S(1)} %get-tuple-element.21.refs_7_), channel_id=1, source_target_pairs={{0,24},{4,28},{8,16},{12,20},{16,8},{20,12},{24,0},{28,4},{1,25},{... | collective-permute-start | bytes 399368 | tf_op jit(solution)/shard_map/ppermute | solution.py:246
  6.1 0.5 %collective-permute-start.2 = (bf16[8,8320]{1,0:T(8,128)(2,1)S(1)}, bf16[8,8320]{1,0:T(8,128)(2,1)S(1)}, u32[]{:S(2)}, u32[]{:S(2)}) collective-permute-start(bf16[8,8320]{1,0:T(8,128)(2,1)S(1)} %get-tuple-element.21.refs_7_), channel_id=1, source_target_pairs={{0,16},{4,20},{8,24},{12,28},{16,0},{20,4},{24,8},{28,12},{1,17},{... | collective-permute-start | bytes 399368 | tf_op jit(solution)/shard_map/ppermute | solution.py:246
  6.7 0.1 collective-permute-start.4
  7.4 2.7 %shard_map.74 = (bf16[8,8320]{1,0:T(8,128)(2,1)S(1)}, bf16[8192,256]{1,0:T(8,128)(2,1)S(1)}, f32[8,256]{1,0:T(8,128)S(1)}) custom-call(s32[1]{0:T(128)S(6)} %copy.10.count_ref, f32[8,256]{1,0:T(8,128)S(1)} %get-tuple-element.18.found_ref, bf16[8,8320]{1,0:T(8,128)(2,1)S(1)} %get-tuple-element.19.block_ref, ...), custom_call_target="tpu_custom_call", output_to_operand_aliasing={{0}: (2, {})} | custom-call | bytes 4194304 | tf_op jit(solution)/shard_map/pallas_call | solution.py:279
  10.1 0.1 collective-permute-start.6
  10.2 0.0 collective-permute-done.refs_1_
  10.2 0.5 %collective-permute-start.1 = (bf16[8,8320]{1,0:T(8,128)(2,1)S(1)}, bf16[8,8320]{1,0:T(8,128)(2,1)S(1)}, u32[]{:S(2)}, u32[]{:S(2)}) collective-permute-start(bf16[8,8320]{1,0:T(8,128)(2,1)S(1)} %collective-permute-done.refs_1_), channel_id=1, source_target_pairs={{0,4},{4,0},{8,12},{12,8},{16,20},{20,16},{24,28},{28,24},{1,5},{5... | collective-permute-start | bytes 399368 | tf_op jit(solution)/shard_map/ppermute | solution.py:246
  10.7 1.8 %collective-permute-done.2.refs_3_ = bf16[8,8320]{1,0:T(8,128)(2,1)S(1)} collective-permute-done((bf16[8,8320]{1,0:T(8,128)(2,1)S(1)}, bf16[8,8320]{1,0:T(8,128)(2,1)S(1)}, u32[]{:S(2)}, u32[]{:S(2)}) %collective-permute-start.2) | collective-permute-done | bytes 133152 | tf_op jit(solution)/shard_map/ppermute | solution.py:246
  12.5 0.0 collective-permute-start.3
  12.5 0.2 collective-permute-done.4.refs_5_
  12.8 0.3 collective-permute-start.5
  13.0 0.0 collective-permute-done.6.refs_6_
  13.0 0.0 collective-permute-done.1.refs_0_
  13.0 0.8 %collective-permute-done.3.refs_2_ = bf16[8,8320]{1,0:T(8,128)(2,1)S(1)} collective-permute-done((bf16[8,8320]{1,0:T(8,128)(2,1)S(1)}, bf16[8,8320]{1,0:T(8,128)(2,1)S(1)}, u32[]{:S(2)}, u32[]{:S(2)}) %collective-permute-start.3) | collective-permute-done | bytes 133152 | tf_op jit(solution)/shard_map/ppermute | solution.py:246
  13.9 0.3 collective-permute-done.5.refs_4_
  14.1 1.2 %shard_map.75 = (f32[4,16,128]{2,1,0:T(8,128)S(1)}, f32[64,256]{1,0:T(8,128)S(1)}, f32[1,128]{1,0:T(1,128)S(1)}) custom-call(bf16[8,8320]{1,0:T(8,128)(2,1)S(1)} %collective-permute-done.1.refs_0_, bf16[8,8320]{1,0:T(8,128)(2,1)S(1)} %collective-permute-done.refs_1_, bf16[8,8320]{1,0:T(8,128)(2,1)S(1)} %collective-permute-done.3.refs_2_, ...), custom_call_target="tpu_custom_call" | custom-call | tf_op jit(solution)/shard_map/pallas_call | solution.py:305
  15.3 0.3 collective-permute-start.7
  15.6 0.3 shard_map.76
  15.9 0.6 %collective-permute-done.7 = f32[4,16,128]{2,1,0:T(8,128)S(1)} collective-permute-done((f32[4,16,128]{2,1,0:T(8,128)S(1)}, f32[4,16,128]{2,1,0:T(8,128)S(1)}, u32[]{:S(2)}, u32[]{:S(2)}) %collective-permute-start.7) | collective-permute-done | bytes 32800 | tf_op jit(solution)/shard_map/ppermute | solution.py:246
  16.6 1.6 %collective-permute-start.10 = (f32[2,16,128]{2,1,0:T(8,128)S(1)}, f32[2,16,128]{2,1,0:T(8,128)S(1)}, u32[]{:S(2)}, u32[]{:S(2)}) collective-permute-start(f32[2,16,128]{2,1,0:T(8,128)S(1)} %pad_maximum_fusion.2), channel_id=1, source_target_pairs={{0,12},{4,8},{8,20},{12,16},{16,28},{20,24},{24,4},{28,0},{1,13},{... | collective-permute-start | bytes 49160 | tf_op jit(solution)/shard_map/ppermute | solution.py:331
  18.1 0.5 %collective-permute-start.9 = (f32[2,16,128]{2,1,0:T(8,128)S(1)}, f32[2,16,128]{2,1,0:T(8,128)S(1)}, u32[]{:S(2)}, u32[]{:S(2)}) collective-permute-start(f32[2,16,128]{2,1,0:T(8,128)S(1)} %pad_maximum_fusion.1), channel_id=1, source_target_pairs={{0,20},{4,16},{8,28},{12,24},{16,4},{20,0},{24,12},{28,8},{1,21},{... | collective-permute-start | bytes 49160 | tf_op jit(solution)/shard_map/ppermute | solution.py:331
  18.6 2.2 %collective-permute-start.8 = (f32[2,16,128]{2,1,0:T(8,128)S(1)}, f32[2,16,128]{2,1,0:T(8,128)S(1)}, u32[]{:S(2)}, u32[]{:S(2)}) collective-permute-start(f32[2,16,128]{2,1,0:T(8,128)S(1)} %pad_maximum_fusion), channel_id=1, source_target_pairs={{0,28},{4,24},{8,4},{12,0},{16,12},{20,8},{24,20},{28,16},{1,29},{... | collective-permute-start | bytes 49160 | tf_op jit(solution)/shard_map/ppermute | solution.py:331
  20.8 0.0 collective-permute-done.10.refs_2_
  20.8 0.5 %collective-permute-done.9.refs_1_ = f32[2,16,128]{2,1,0:T(8,128)S(1)} collective-permute-done((f32[2,16,128]{2,1,0:T(8,128)S(1)}, f32[2,16,128]{2,1,0:T(8,128)S(1)}, u32[]{:S(2)}, u32[]{:S(2)}) %collective-permute-start.9) | collective-permute-done | bytes 16416 | tf_op jit(solution)/shard_map/ppermute | solution.py:331
  21.3 0.9 %collective-permute-done.8.refs_0_ = f32[2,16,128]{2,1,0:T(8,128)S(1)} collective-permute-done((f32[2,16,128]{2,1,0:T(8,128)S(1)}, f32[2,16,128]{2,1,0:T(8,128)S(1)}, u32[]{:S(2)}, u32[]{:S(2)}) %collective-permute-start.8) | collective-permute-done | bytes 16416 | tf_op jit(solution)/shard_map/ppermute | solution.py:331
  22.3 0.4 %shard_map.77 = (f32[32,128]{1,0:T(8,128)S(1)}, f32[32,128]{1,0:T(8,128)S(1)}, f32[32,128]{1,0:T(8,128)S(1)}, f32[32,128]{1,0:T(8,128)S(1)}) custom-call(f32[8,256]{1,0:T(8,128)S(1)} %get-tuple-element.20.found_ref, f32[2,16,128]{2,1,0:T(8,128)S(1)} %collective-permute-done.8.refs_0_, f32[2,16,128]{2,1,0:T(8,128)S(1)} %collective-permute-done.9.refs_1_, ...), custom_call_target="tpu_custom_call" | custom-call | tf_op jit(solution)/shard_map/pallas_call | solution.py:333
  22.7 1.6 %collective-permute-start.11 = (f32[32,128]{1,0:T(8,128)S(1)}, f32[32,128]{1,0:T(8,128)S(1)}, u32[]{:S(2)}, u32[]{:S(2)}) collective-permute-start(f32[32,128]{1,0:T(8,128)S(1)} %get-tuple-element.28), channel_id=1, source_target_pairs={{0,1},{1,2},{2,3},{3,0},{4,5},{5,6},{6,7},{7,4},{8,9},{9,10},{10,1... | collective-permute-start | bytes 49160 | tf_op jit(solution)/shard_map/ppermute | solution.py:342
  24.3 2.6 %collective-permute-start.12 = (f32[32,128]{1,0:T(8,128)S(1)}, f32[32,128]{1,0:T(8,128)S(1)}, u32[]{:S(2)}, u32[]{:S(2)}) collective-permute-start(f32[32,128]{1,0:T(8,128)S(1)} %get-tuple-element.29), channel_id=1, source_target_pairs={{0,2},{1,3},{2,0},{3,1},{4,6},{5,7},{6,4},{7,5},{8,10},{9,11},{10,... | collective-permute-start | bytes 49160 | tf_op jit(solution)/shard_map/ppermute | solution.py:342
  26.9 1.3 %collective-permute-start.13 = (f32[32,128]{1,0:T(8,128)S(1)}, f32[32,128]{1,0:T(8,128)S(1)}, u32[]{:S(2)}, u32[]{:S(2)}) collective-permute-start(f32[32,128]{1,0:T(8,128)S(1)} %get-tuple-element.30), channel_id=1, source_target_pairs={{0,3},{1,0},{2,1},{3,2},{4,7},{5,4},{6,5},{7,6},{8,11},{9,8},{10,9... | collective-permute-start | bytes 49160 | tf_op jit(solution)/shard_map/ppermute | solution.py:342
  28.3 0.0 collective-permute-done.11
  28.3 0.9 %collective-permute-done.12 = f32[32,128]{1,0:T(8,128)S(1)} collective-permute-done((f32[32,128]{1,0:T(8,128)S(1)}, f32[32,128]{1,0:T(8,128)S(1)}, u32[]{:S(2)}, u32[]{:S(2)}) %collective-permute-start.12) | collective-permute-done | bytes 16416 | tf_op jit(solution)/shard_map/ppermute | solution.py:342
  29.2 1.5 %collective-permute-done.13 = f32[32,128]{1,0:T(8,128)S(1)} collective-permute-done((f32[32,128]{1,0:T(8,128)S(1)}, f32[32,128]{1,0:T(8,128)S(1)}, u32[]{:S(2)}, u32[]{:S(2)}) %collective-permute-start.13) | collective-permute-done | bytes 16416 | tf_op jit(solution)/shard_map/ppermute | solution.py:342
  30.7 0.1 fusion.2
  30.7 0.6 %maximum_bitcast_fusion = f32[1,64,64]{2,1,0:T(8,128)} fusion(f32[32,64]{1,0:T(8,128)S(1)} %get-tuple-element.40, f32[32,64]{1,0:T(8,128)S(1)} %get-tuple-element.39), kind=kLoop, calls=%fused_computation | loop fusion | flops 4096 | bytes 32768 | tf_op jit(solution)/shard_map/broadcast_in_dim | solution.py:343
  (7 shorter events, 0.1 us)
Async XLA Ops:
  2.2 8.0 %collective-permute-start = (bf16[8,8320]{1,0:T(8,128)(2,1)S(1)}, bf16[8,8320]{1,0:T(8,128)(2,1)S(1)}, u32[]{:S(2)}, u32[]{:S(2)}) collective-permute-start(bf16[8,8320]{1,0:T(8,128)(2,1)S(1)} %get-tuple-element.21.refs_7_), channel_id=1, source_target_pairs={{0,24},{4,28},{8,16},{12,20},{16,8},{20,12},{24,0},{28,4},{1,25},{... | collective-permute-start | bytes 399368 | tf_op jit(solution)/shard_map/ppermute | solution.py:246
  6.1 6.4 %collective-permute-start.2 = (bf16[8,8320]{1,0:T(8,128)(2,1)S(1)}, bf16[8,8320]{1,0:T(8,128)(2,1)S(1)}, u32[]{:S(2)}, u32[]{:S(2)}) collective-permute-start(bf16[8,8320]{1,0:T(8,128)(2,1)S(1)} %get-tuple-element.21.refs_7_), channel_id=1, source_target_pairs={{0,16},{4,20},{8,24},{12,28},{16,0},{20,4},{24,8},{28,12},{1,17},{... | collective-permute-start | bytes 399368 | tf_op jit(solution)/shard_map/ppermute | solution.py:246
  6.7 6.1 %collective-permute-start.4 = (bf16[8,8320]{1,0:T(8,128)(2,1)S(1)}, bf16[8,8320]{1,0:T(8,128)(2,1)S(1)}, u32[]{:S(2)}, u32[]{:S(2)}) collective-permute-start(bf16[8,8320]{1,0:T(8,128)(2,1)S(1)} %get-tuple-element.21.refs_7_), channel_id=1, source_target_pairs={{0,8},{4,12},{8,0},{12,4},{16,24},{20,28},{24,16},{28,20},{1,9},{5... | collective-permute-start | bytes 399368 | tf_op jit(solution)/shard_map/ppermute | solution.py:246
  10.1 2.9 %collective-permute-start.6 = (bf16[8,8320]{1,0:T(8,128)(2,1)S(1)}, bf16[8,8320]{1,0:T(8,128)(2,1)S(1)}, u32[]{:S(2)}, u32[]{:S(2)}) collective-permute-start(bf16[8,8320]{1,0:T(8,128)(2,1)S(1)} %get-tuple-element.22), channel_id=1, source_target_pairs={{0,4},{4,0},{8,12},{12,8},{16,20},{20,16},{24,28},{28,24},{1,5},{5... | collective-permute-start | bytes 399368 | tf_op jit(solution)/shard_map/ppermute | solution.py:246
  10.2 2.9 %collective-permute-start.1 = (bf16[8,8320]{1,0:T(8,128)(2,1)S(1)}, bf16[8,8320]{1,0:T(8,128)(2,1)S(1)}, u32[]{:S(2)}, u32[]{:S(2)}) collective-permute-start(bf16[8,8320]{1,0:T(8,128)(2,1)S(1)} %collective-permute-done.refs_1_), channel_id=1, source_target_pairs={{0,4},{4,0},{8,12},{12,8},{16,20},{20,16},{24,28},{28,24},{1,5},{5... | collective-permute-start | bytes 399368 | tf_op jit(solution)/shard_map/ppermute | solution.py:246
  12.5 1.4 %collective-permute-start.3 = (bf16[8,8320]{1,0:T(8,128)(2,1)S(1)}, bf16[8,8320]{1,0:T(8,128)(2,1)S(1)}, u32[]{:S(2)}, u32[]{:S(2)}) collective-permute-start(bf16[8,8320]{1,0:T(8,128)(2,1)S(1)} %collective-permute-done.2.refs_3_), channel_id=1, source_target_pairs={{0,4},{4,0},{8,12},{12,8},{16,20},{20,16},{24,28},{28,24},{1,5},{5... | collective-permute-start | bytes 399368 | tf_op jit(solution)/shard_map/ppermute | solution.py:246
  12.8 1.4 %collective-permute-start.5 = (bf16[8,8320]{1,0:T(8,128)(2,1)S(1)}, bf16[8,8320]{1,0:T(8,128)(2,1)S(1)}, u32[]{:S(2)}, u32[]{:S(2)}) collective-permute-start(bf16[8,8320]{1,0:T(8,128)(2,1)S(1)} %collective-permute-done.4.refs_5_), channel_id=1, source_target_pairs={{0,4},{4,0},{8,12},{12,8},{16,20},{20,16},{24,28},{28,24},{1,5},{5... | collective-permute-start | bytes 399368 | tf_op jit(solution)/shard_map/ppermute | solution.py:246
  15.3 1.3 %collective-permute-start.7 = (f32[4,16,128]{2,1,0:T(8,128)S(1)}, f32[4,16,128]{2,1,0:T(8,128)S(1)}, u32[]{:S(2)}, u32[]{:S(2)}) collective-permute-start(f32[4,16,128]{2,1,0:T(8,128)S(1)} %get-tuple-element.26), channel_id=1, source_target_pairs={{0,4},{4,0},{8,12},{12,8},{16,20},{20,16},{24,28},{28,24},{1,5},{5... | collective-permute-start | bytes 98312 | tf_op jit(solution)/shard_map/ppermute | solution.py:246
  16.6 4.2 %collective-permute-start.10 = (f32[2,16,128]{2,1,0:T(8,128)S(1)}, f32[2,16,128]{2,1,0:T(8,128)S(1)}, u32[]{:S(2)}, u32[]{:S(2)}) collective-permute-start(f32[2,16,128]{2,1,0:T(8,128)S(1)} %pad_maximum_fusion.2), channel_id=1, source_target_pairs={{0,12},{4,8},{8,20},{12,16},{16,28},{20,24},{24,4},{28,0},{1,13},{... | collective-permute-start | bytes 49160 | tf_op jit(solution)/shard_map/ppermute | solution.py:331
  18.1 3.2 %collective-permute-start.9 = (f32[2,16,128]{2,1,0:T(8,128)S(1)}, f32[2,16,128]{2,1,0:T(8,128)S(1)}, u32[]{:S(2)}, u32[]{:S(2)}) collective-permute-start(f32[2,16,128]{2,1,0:T(8,128)S(1)} %pad_maximum_fusion.1), channel_id=1, source_target_pairs={{0,20},{4,16},{8,28},{12,24},{16,4},{20,0},{24,12},{28,8},{1,21},{... | collective-permute-start | bytes 49160 | tf_op jit(solution)/shard_map/ppermute | solution.py:331
  18.6 3.6 %collective-permute-start.8 = (f32[2,16,128]{2,1,0:T(8,128)S(1)}, f32[2,16,128]{2,1,0:T(8,128)S(1)}, u32[]{:S(2)}, u32[]{:S(2)}) collective-permute-start(f32[2,16,128]{2,1,0:T(8,128)S(1)} %pad_maximum_fusion), channel_id=1, source_target_pairs={{0,28},{4,24},{8,4},{12,0},{16,12},{20,8},{24,20},{28,16},{1,29},{... | collective-permute-start | bytes 49160 | tf_op jit(solution)/shard_map/ppermute | solution.py:331
  22.7 5.6 %collective-permute-start.11 = (f32[32,128]{1,0:T(8,128)S(1)}, f32[32,128]{1,0:T(8,128)S(1)}, u32[]{:S(2)}, u32[]{:S(2)}) collective-permute-start(f32[32,128]{1,0:T(8,128)S(1)} %get-tuple-element.28), channel_id=1, source_target_pairs={{0,1},{1,2},{2,3},{3,0},{4,5},{5,6},{6,7},{7,4},{8,9},{9,10},{10,1... | collective-permute-start | bytes 49160 | tf_op jit(solution)/shard_map/ppermute | solution.py:342
  24.3 4.9 %collective-permute-start.12 = (f32[32,128]{1,0:T(8,128)S(1)}, f32[32,128]{1,0:T(8,128)S(1)}, u32[]{:S(2)}, u32[]{:S(2)}) collective-permute-start(f32[32,128]{1,0:T(8,128)S(1)} %get-tuple-element.29), channel_id=1, source_target_pairs={{0,2},{1,3},{2,0},{3,1},{4,6},{5,7},{6,4},{7,5},{8,10},{9,11},{10,... | collective-permute-start | bytes 49160 | tf_op jit(solution)/shard_map/ppermute | solution.py:342
  26.9 3.7 %collective-permute-start.13 = (f32[32,128]{1,0:T(8,128)S(1)}, f32[32,128]{1,0:T(8,128)S(1)}, u32[]{:S(2)}, u32[]{:S(2)}) collective-permute-start(f32[32,128]{1,0:T(8,128)S(1)} %get-tuple-element.30), channel_id=1, source_target_pairs={{0,3},{1,0},{2,1},{3,2},{4,7},{5,4},{6,5},{7,6},{8,11},{9,8},{10,9... | collective-permute-start | bytes 49160 | tf_op jit(solution)/shard_map/ppermute | solution.py:342

commit v24 on v23

--- a/solution.py
+++ b/solution.py
@@ -17,6 +17,10 @@
 
 def iota(shape, dimension):
     return lax.broadcasted_iota(jnp.int32, shape, dimension)
+
+
+def ring_place(chip, chips):
+    return chip % 2 * 2 + chip // 2 if chips == 4 else chip
 
 
 def parts_of(value):
@@ -186,7 +190,7 @@
     chip = me // 2
     kept, handed = [asked[0]], [asked[1]]
     for step in range(1, chips):
-        apart = chip ^ ((chip + step) % chips)
+        apart = chip ^ ring_place((ring_place(chip, chips) + step) % chips, chips)
         for rows_of, core in ((kept, 1), (handed, 0)):
             chosen = asked[2 + core]
             for distance in range(2, chips):
@@ -219,7 +223,7 @@
     me = lax.axis_index("store")
     chips = holders // 2
     holder = found_ref[0:1].astype(jnp.int32)
-    step = (me // 2 - holder // 2 + 2 * chips) % chips
+    step = (ring_place(me // 2, chips) - ring_place(holder // 2, chips) + 2 * chips) % chips
     same_core = (holder % 2 == me % 2).astype(jnp.int32)
     place = 2 * step + jnp.where(step == 0, 1 - same_core, same_core)
     begins = jnp.where(holder < holders, place * half, -1).astype(jnp.float32)
@@ -327,7 +331,9 @@
     landed = []
     for step in range(chips):
         pair = jnp.stack([keep[step], handed[step]])
-        to = [(i, (i // 2 + step) % chips * 2 + 1 - i % 2) for i in range(holders)]
+        to = [
+            (i, ring_place((ring_place(i // 2, chips) + step) % chips, chips) * 2 + 1 - i % 2) for i in range(holders)
+        ]
         landed.append(lax.ppermute(pair, "store", to) if step else pair)
     share = slots // groups
     terms = pl.pallas_call(

time: 31.5 us -> 31.5 us (level)
  no operation moved by 1% of the time
where the time goes in v24:
time: 31.5 us; the launch traced here: 31.3 us
  starting transfers between devices  15.5 us (49%)
  waiting for transfers between devices  7.65 us (24%)
  Pallas kernels  6.71 us (21%)
  between operations  0.72 us (2%)
  other arithmetic  0.64 us (2%)
    ppermute x8, starting transfers between devices, swap(): lax.ppermute(value, axis, [(i, i ^ distance) for i in range(lax.axis_size...  5.75 us
    ppermute x3, starting transfers between devices, on_device(): lax.ppermute(terms[step], 'layer', [(g, (g + step) % groups) for g in ran...  5.57 us
    ppermute x3, starting transfers between devices, on_device(): landed.append(lax.ppermute(pair, 'store', to) if step else pair)  4.2 us
    ppermute x8, waiting for transfers between devices, swap(): lax.ppermute(value, axis, [(i, i ^ distance) for i in range(lax.axis_size...  3.82 us
    pallas_call x1, Pallas kernels, on_device(): pl.pallas_call(functools.partial(load_kernel, holders), out_shape=[jax.Sh...  2.65 us
    ppermute x3, waiting for transfers between devices, on_device(): lax.ppermute(terms[step], 'layer', [(g, (g + step) % groups) for g in ran...  2.39 us
    pallas_call x1, Pallas kernels, on_device(): pl.pallas_call(functools.partial(condition_kernel, holders, capacity, per...  2.17 us
    ppermute x3, waiting for transfers between devices, on_device(): landed.append(lax.ppermute(pair, 'store', to) if step else pair)  1.44 us
  transfers between devices with their start and end apart: 14, of which 9 were waited for; matrix products, arithmetic and copies ran while one was open for 0% of the time, Pallas kernels for 9%

profile of v24, /device:TPU:0, one launch (start us, length us, event | category | flops | bytes accessed | tf_op | source)
XLA Modules:
  0.0 31.3 jit_solution(954078722182127816)
XLA Ops:
  0.0 2.2 %shard_map.73 = (bf16[8,8320]{1,0:T(8,128)(2,1)S(1)}, bf16[8,8320]{1,0:T(8,128)(2,1)S(1)}, f32[8,256]{1,0:T(8,128)S(1)}) custom-call(bf16[8,8192]{1,0:T(8,128)(2,1)} %refs_0_.1, f32[2,64,64]{2,1,0:T(8,128)} %refs_1_.1, f32[2,64,64]{2,1,0:T(8,128)} %refs_2_.1, s32[16,128]{1,0:T(8,128)} %bitcast.3, s32[1,256]{1,0:T(1,128)} %refs_4_.1), custom_call_target="tpu_custom_call" | custom-call | tf_op jit(solution)/shard_map/pallas_call | solution.py:269
  2.2 4.0 %collective-permute-start = (bf16[8,8320]{1,0:T(8,128)(2,1)S(1)}, bf16[8,8320]{1,0:T(8,128)(2,1)S(1)}, u32[]{:S(2)}, u32[]{:S(2)}) collective-permute-start(bf16[8,8320]{1,0:T(8,128)(2,1)S(1)} %get-tuple-element.21.refs_7_), channel_id=1, source_target_pairs={{0,24},{4,28},{8,16},{12,20},{16,8},{20,12},{24,0},{28,4},{1,25},{... | collective-permute-start | bytes 399368 | tf_op jit(solution)/shard_map/ppermute | solution.py:250
  6.1 0.5 %collective-permute-start.2 = (bf16[8,8320]{1,0:T(8,128)(2,1)S(1)}, bf16[8,8320]{1,0:T(8,128)(2,1)S(1)}, u32[]{:S(2)}, u32[]{:S(2)}) collective-permute-start(bf16[8,8320]{1,0:T(8,128)(2,1)S(1)} %get-tuple-element.21.refs_7_), channel_id=1, source_target_pairs={{0,16},{4,20},{8,24},{12,28},{16,0},{20,4},{24,8},{28,12},{1,17},{... | collective-permute-start | bytes 399368 | tf_op jit(solution)/shard_map/ppermute | solution.py:250
  6.7 0.1 collective-permute-start.4
  7.4 2.7 %shard_map.74 = (bf16[8,8320]{1,0:T(8,128)(2,1)S(1)}, bf16[8192,256]{1,0:T(8,128)(2,1)S(1)}, f32[8,256]{1,0:T(8,128)S(1)}) custom-call(s32[1]{0:T(128)S(6)} %copy.10.count_ref, f32[8,256]{1,0:T(8,128)S(1)} %get-tuple-element.18.found_ref, bf16[8,8320]{1,0:T(8,128)(2,1)S(1)} %get-tuple-element.19.block_ref, ...), custom_call_target="tpu_custom_call", output_to_operand_aliasing={{0}: (2, {})} | custom-call | bytes 4194304 | tf_op jit(solution)/shard_map/pallas_call | solution.py:283
  10.1 0.1 collective-permute-start.6
  10.2 0.0 collective-permute-done.refs_1_
  10.2 0.5 %collective-permute-start.1 = (bf16[8,8320]{1,0:T(8,128)(2,1)S(1)}, bf16[8,8320]{1,0:T(8,128)(2,1)S(1)}, u32[]{:S(2)}, u32[]{:S(2)}) collective-permute-start(bf16[8,8320]{1,0:T(8,128)(2,1)S(1)} %collective-permute-done.refs_1_), channel_id=1, source_target_pairs={{0,4},{4,0},{8,12},{12,8},{16,20},{20,16},{24,28},{28,24},{1,5},{5... | collective-permute-start | bytes 399368 | tf_op jit(solution)/shard_map/ppermute | solution.py:250
  10.7 1.8 %collective-permute-done.2.refs_3_ = bf16[8,8320]{1,0:T(8,128)(2,1)S(1)} collective-permute-done((bf16[8,8320]{1,0:T(8,128)(2,1)S(1)}, bf16[8,8320]{1,0:T(8,128)(2,1)S(1)}, u32[]{:S(2)}, u32[]{:S(2)}) %collective-permute-start.2) | collective-permute-done | bytes 133152 | tf_op jit(solution)/shard_map/ppermute | solution.py:250
  12.5 0.0 collective-permute-start.3
  12.5 0.2 collective-permute-done.4.refs_5_
  12.8 0.3 collective-permute-start.5
  13.0 0.0 collective-permute-done.6.refs_6_
  13.0 0.0 collective-permute-done.1.refs_0_
  13.0 0.8 %collective-permute-done.3.refs_2_ = bf16[8,8320]{1,0:T(8,128)(2,1)S(1)} collective-permute-done((bf16[8,8320]{1,0:T(8,128)(2,1)S(1)}, bf16[8,8320]{1,0:T(8,128)(2,1)S(1)}, u32[]{:S(2)}, u32[]{:S(2)}) %collective-permute-start.3) | collective-permute-done | bytes 133152 | tf_op jit(solution)/shard_map/ppermute | solution.py:250
  13.9 0.3 collective-permute-done.5.refs_4_
  14.1 1.2 %shard_map.75 = (f32[4,16,128]{2,1,0:T(8,128)S(1)}, f32[64,256]{1,0:T(8,128)S(1)}, f32[1,128]{1,0:T(1,128)S(1)}) custom-call(bf16[8,8320]{1,0:T(8,128)(2,1)S(1)} %collective-permute-done.1.refs_0_, bf16[8,8320]{1,0:T(8,128)(2,1)S(1)} %collective-permute-done.refs_1_, bf16[8,8320]{1,0:T(8,128)(2,1)S(1)} %collective-permute-done.3.refs_2_, ...), custom_call_target="tpu_custom_call" | custom-call | tf_op jit(solution)/shard_map/pallas_call | solution.py:309
  15.3 0.3 collective-permute-start.7
  15.6 0.3 shard_map.76
  15.9 0.6 %collective-permute-done.7 = f32[4,16,128]{2,1,0:T(8,128)S(1)} collective-permute-done((f32[4,16,128]{2,1,0:T(8,128)S(1)}, f32[4,16,128]{2,1,0:T(8,128)S(1)}, u32[]{:S(2)}, u32[]{:S(2)}) %collective-permute-start.7) | collective-permute-done | bytes 32800 | tf_op jit(solution)/shard_map/ppermute | solution.py:250
  16.6 1.6 %collective-permute-start.10 = (f32[2,16,128]{2,1,0:T(8,128)S(1)}, f32[2,16,128]{2,1,0:T(8,128)S(1)}, u32[]{:S(2)}, u32[]{:S(2)}) collective-permute-start(f32[2,16,128]{2,1,0:T(8,128)S(1)} %pad_maximum_fusion.2), channel_id=1, source_target_pairs={{0,20},{4,16},{8,28},{12,24},{16,12},{20,8},{24,4},{28,0},{1,21},{... | collective-permute-start | bytes 49160 | tf_op jit(solution)/shard_map/ppermute | solution.py:337
  18.2 0.5 %collective-permute-start.9 = (f32[2,16,128]{2,1,0:T(8,128)S(1)}, f32[2,16,128]{2,1,0:T(8,128)S(1)}, u32[]{:S(2)}, u32[]{:S(2)}) collective-permute-start(f32[2,16,128]{2,1,0:T(8,128)S(1)} %pad_maximum_fusion.1), channel_id=1, source_target_pairs={{0,12},{4,8},{8,4},{12,0},{16,28},{20,24},{24,20},{28,16},{1,13},{... | collective-permute-start | bytes 49160 | tf_op jit(solution)/shard_map/ppermute | solution.py:337
  18.6 2.2 %collective-permute-start.8 = (f32[2,16,128]{2,1,0:T(8,128)S(1)}, f32[2,16,128]{2,1,0:T(8,128)S(1)}, u32[]{:S(2)}, u32[]{:S(2)}) collective-permute-start(f32[2,16,128]{2,1,0:T(8,128)S(1)} %pad_maximum_fusion), channel_id=1, source_target_pairs={{0,28},{4,24},{8,20},{12,16},{16,4},{20,0},{24,12},{28,8},{1,29},{... | collective-permute-start | bytes 49160 | tf_op jit(solution)/shard_map/ppermute | solution.py:337
  20.8 0.0 collective-permute-done.10.refs_2_
  20.8 0.5 %collective-permute-done.9.refs_1_ = f32[2,16,128]{2,1,0:T(8,128)S(1)} collective-permute-done((f32[2,16,128]{2,1,0:T(8,128)S(1)}, f32[2,16,128]{2,1,0:T(8,128)S(1)}, u32[]{:S(2)}, u32[]{:S(2)}) %collective-permute-start.9) | collective-permute-done | bytes 16416 | tf_op jit(solution)/shard_map/ppermute | solution.py:337
  21.3 0.9 %collective-permute-done.8.refs_0_ = f32[2,16,128]{2,1,0:T(8,128)S(1)} collective-permute-done((f32[2,16,128]{2,1,0:T(8,128)S(1)}, f32[2,16,128]{2,1,0:T(8,128)S(1)}, u32[]{:S(2)}, u32[]{:S(2)}) %collective-permute-start.8) | collective-permute-done | bytes 16416 | tf_op jit(solution)/shard_map/ppermute | solution.py:337
  22.2 0.4 %shard_map.77 = (f32[32,128]{1,0:T(8,128)S(1)}, f32[32,128]{1,0:T(8,128)S(1)}, f32[32,128]{1,0:T(8,128)S(1)}, f32[32,128]{1,0:T(8,128)S(1)}) custom-call(f32[8,256]{1,0:T(8,128)S(1)} %get-tuple-element.20.found_ref, f32[2,16,128]{2,1,0:T(8,128)S(1)} %collective-permute-done.8.refs_0_, f32[2,16,128]{2,1,0:T(8,128)S(1)} %collective-permute-done.9.refs_1_, ...), custom_call_target="tpu_custom_call" | custom-call | tf_op jit(solution)/shard_map/pallas_call | solution.py:339
  22.7 1.6 %collective-permute-start.11 = (f32[32,128]{1,0:T(8,128)S(1)}, f32[32,128]{1,0:T(8,128)S(1)}, u32[]{:S(2)}, u32[]{:S(2)}) collective-permute-start(f32[32,128]{1,0:T(8,128)S(1)} %get-tuple-element.28), channel_id=1, source_target_pairs={{0,1},{1,2},{2,3},{3,0},{4,5},{5,6},{6,7},{7,4},{8,9},{9,10},{10,1... | collective-permute-start | bytes 49160 | tf_op jit(solution)/shard_map/ppermute | solution.py:348
  24.3 2.6 %collective-permute-start.12 = (f32[32,128]{1,0:T(8,128)S(1)}, f32[32,128]{1,0:T(8,128)S(1)}, u32[]{:S(2)}, u32[]{:S(2)}) collective-permute-start(f32[32,128]{1,0:T(8,128)S(1)} %get-tuple-element.29), channel_id=1, source_target_pairs={{0,2},{1,3},{2,0},{3,1},{4,6},{5,7},{6,4},{7,5},{8,10},{9,11},{10,... | collective-permute-start | bytes 49160 | tf_op jit(solution)/shard_map/ppermute | solution.py:348
  26.9 1.3 %collective-permute-start.13 = (f32[32,128]{1,0:T(8,128)S(1)}, f32[32,128]{1,0:T(8,128)S(1)}, u32[]{:S(2)}, u32[]{:S(2)}) collective-permute-start(f32[32,128]{1,0:T(8,128)S(1)} %get-tuple-element.30), channel_id=1, source_target_pairs={{0,3},{1,0},{2,1},{3,2},{4,7},{5,4},{6,5},{7,6},{8,11},{9,8},{10,9... | collective-permute-start | bytes 49160 | tf_op jit(solution)/shard_map/ppermute | solution.py:348
  28.2 0.0 collective-permute-done.11
  28.3 0.9 %collective-permute-done.12 = f32[32,128]{1,0:T(8,128)S(1)} collective-permute-done((f32[32,128]{1,0:T(8,128)S(1)}, f32[32,128]{1,0:T(8,128)S(1)}, u32[]{:S(2)}, u32[]{:S(2)}) %collective-permute-start.12) | collective-permute-done | bytes 16416 | tf_op jit(solution)/shard_map/ppermute | solution.py:348
  29.2 1.4 %collective-permute-done.13 = f32[32,128]{1,0:T(8,128)S(1)} collective-permute-done((f32[32,128]{1,0:T(8,128)S(1)}, f32[32,128]{1,0:T(8,128)S(1)}, u32[]{:S(2)}, u32[]{:S(2)}) %collective-permute-start.13) | collective-permute-done | bytes 16416 | tf_op jit(solution)/shard_map/ppermute | solution.py:348
  30.6 0.1 fusion.2
  30.7 0.6 %maximum_bitcast_fusion = f32[1,64,64]{2,1,0:T(8,128)} fusion(f32[32,64]{1,0:T(8,128)S(1)} %get-tuple-element.40, f32[32,64]{1,0:T(8,128)S(1)} %get-tuple-element.39), kind=kLoop, calls=%fused_computation | loop fusion | flops 4096 | bytes 32768 | tf_op jit(solution)/shard_map/broadcast_in_dim | solution.py:349
  (7 shorter events, 0.1 us)
Async XLA Ops:
  2.2 8.0 %collective-permute-start = (bf16[8,8320]{1,0:T(8,128)(2,1)S(1)}, bf16[8,8320]{1,0:T(8,128)(2,1)S(1)}, u32[]{:S(2)}, u32[]{:S(2)}) collective-permute-start(bf16[8,8320]{1,0:T(8,128)(2,1)S(1)} %get-tuple-element.21.refs_7_), channel_id=1, source_target_pairs={{0,24},{4,28},{8,16},{12,20},{16,8},{20,12},{24,0},{28,4},{1,25},{... | collective-permute-start | bytes 399368 | tf_op jit(solution)/shard_map/ppermute | solution.py:250
  6.1 6.4 %collective-permute-start.2 = (bf16[8,8320]{1,0:T(8,128)(2,1)S(1)}, bf16[8,8320]{1,0:T(8,128)(2,1)S(1)}, u32[]{:S(2)}, u32[]{:S(2)}) collective-permute-start(bf16[8,8320]{1,0:T(8,128)(2,1)S(1)} %get-tuple-element.21.refs_7_), channel_id=1, source_target_pairs={{0,16},{4,20},{8,24},{12,28},{16,0},{20,4},{24,8},{28,12},{1,17},{... | collective-permute-start | bytes 399368 | tf_op jit(solution)/shard_map/ppermute | solution.py:250
  6.7 6.1 %collective-permute-start.4 = (bf16[8,8320]{1,0:T(8,128)(2,1)S(1)}, bf16[8,8320]{1,0:T(8,128)(2,1)S(1)}, u32[]{:S(2)}, u32[]{:S(2)}) collective-permute-start(bf16[8,8320]{1,0:T(8,128)(2,1)S(1)} %get-tuple-element.21.refs_7_), channel_id=1, source_target_pairs={{0,8},{4,12},{8,0},{12,4},{16,24},{20,28},{24,16},{28,20},{1,9},{5... | collective-permute-start | bytes 399368 | tf_op jit(solution)/shard_map/ppermute | solution.py:250
  10.1 2.9 %collective-permute-start.6 = (bf16[8,8320]{1,0:T(8,128)(2,1)S(1)}, bf16[8,8320]{1,0:T(8,128)(2,1)S(1)}, u32[]{:S(2)}, u32[]{:S(2)}) collective-permute-start(bf16[8,8320]{1,0:T(8,128)(2,1)S(1)} %get-tuple-element.22), channel_id=1, source_target_pairs={{0,4},{4,0},{8,12},{12,8},{16,20},{20,16},{24,28},{28,24},{1,5},{5... | collective-permute-start | bytes 399368 | tf_op jit(solution)/shard_map/ppermute | solution.py:250
  10.2 2.9 %collective-permute-start.1 = (bf16[8,8320]{1,0:T(8,128)(2,1)S(1)}, bf16[8,8320]{1,0:T(8,128)(2,1)S(1)}, u32[]{:S(2)}, u32[]{:S(2)}) collective-permute-start(bf16[8,8320]{1,0:T(8,128)(2,1)S(1)} %collective-permute-done.refs_1_), channel_id=1, source_target_pairs={{0,4},{4,0},{8,12},{12,8},{16,20},{20,16},{24,28},{28,24},{1,5},{5... | collective-permute-start | bytes 399368 | tf_op jit(solution)/shard_map/ppermute | solution.py:250
  12.5 1.4 %collective-permute-start.3 = (bf16[8,8320]{1,0:T(8,128)(2,1)S(1)}, bf16[8,8320]{1,0:T(8,128)(2,1)S(1)}, u32[]{:S(2)}, u32[]{:S(2)}) collective-permute-start(bf16[8,8320]{1,0:T(8,128)(2,1)S(1)} %collective-permute-done.2.refs_3_), channel_id=1, source_target_pairs={{0,4},{4,0},{8,12},{12,8},{16,20},{20,16},{24,28},{28,24},{1,5},{5... | collective-permute-start | bytes 399368 | tf_op jit(solution)/shard_map/ppermute | solution.py:250
  12.8 1.4 %collective-permute-start.5 = (bf16[8,8320]{1,0:T(8,128)(2,1)S(1)}, bf16[8,8320]{1,0:T(8,128)(2,1)S(1)}, u32[]{:S(2)}, u32[]{:S(2)}) collective-permute-start(bf16[8,8320]{1,0:T(8,128)(2,1)S(1)} %collective-permute-done.4.refs_5_), channel_id=1, source_target_pairs={{0,4},{4,0},{8,12},{12,8},{16,20},{20,16},{24,28},{28,24},{1,5},{5... | collective-permute-start | bytes 399368 | tf_op jit(solution)/shard_map/ppermute | solution.py:250
  15.3 1.3 %collective-permute-start.7 = (f32[4,16,128]{2,1,0:T(8,128)S(1)}, f32[4,16,128]{2,1,0:T(8,128)S(1)}, u32[]{:S(2)}, u32[]{:S(2)}) collective-permute-start(f32[4,16,128]{2,1,0:T(8,128)S(1)} %get-tuple-element.26), channel_id=1, source_target_pairs={{0,4},{4,0},{8,12},{12,8},{16,20},{20,16},{24,28},{28,24},{1,5},{5... | collective-permute-start | bytes 98312 | tf_op jit(solution)/shard_map/ppermute | solution.py:250
  16.6 4.2 %collective-permute-start.10 = (f32[2,16,128]{2,1,0:T(8,128)S(1)}, f32[2,16,128]{2,1,0:T(8,128)S(1)}, u32[]{:S(2)}, u32[]{:S(2)}) collective-permute-start(f32[2,16,128]{2,1,0:T(8,128)S(1)} %pad_maximum_fusion.2), channel_id=1, source_target_pairs={{0,20},{4,16},{8,28},{12,24},{16,12},{20,8},{24,4},{28,0},{1,21},{... | collective-permute-start | bytes 49160 | tf_op jit(solution)/shard_map/ppermute | solution.py:337
  18.2 3.2 %collective-permute-start.9 = (f32[2,16,128]{2,1,0:T(8,128)S(1)}, f32[2,16,128]{2,1,0:T(8,128)S(1)}, u32[]{:S(2)}, u32[]{:S(2)}) collective-permute-start(f32[2,16,128]{2,1,0:T(8,128)S(1)} %pad_maximum_fusion.1), channel_id=1, source_target_pairs={{0,12},{4,8},{8,4},{12,0},{16,28},{20,24},{24,20},{28,16},{1,13},{... | collective-permute-start | bytes 49160 | tf_op jit(solution)/shard_map/ppermute | solution.py:337
  18.6 3.6 %collective-permute-start.8 = (f32[2,16,128]{2,1,0:T(8,128)S(1)}, f32[2,16,128]{2,1,0:T(8,128)S(1)}, u32[]{:S(2)}, u32[]{:S(2)}) collective-permute-start(f32[2,16,128]{2,1,0:T(8,128)S(1)} %pad_maximum_fusion), channel_id=1, source_target_pairs={{0,28},{4,24},{8,20},{12,16},{16,4},{20,0},{24,12},{28,8},{1,29},{... | collective-permute-start | bytes 49160 | tf_op jit(solution)/shard_map/ppermute | solution.py:337
  22.7 5.6 %collective-permute-start.11 = (f32[32,128]{1,0:T(8,128)S(1)}, f32[32,128]{1,0:T(8,128)S(1)}, u32[]{:S(2)}, u32[]{:S(2)}) collective-permute-start(f32[32,128]{1,0:T(8,128)S(1)} %get-tuple-element.28), channel_id=1, source_target_pairs={{0,1},{1,2},{2,3},{3,0},{4,5},{5,6},{6,7},{7,4},{8,9},{9,10},{10,1... | collective-permute-start | bytes 49160 | tf_op jit(solution)/shard_map/ppermute | solution.py:348
  24.3 4.9 %collective-permute-start.12 = (f32[32,128]{1,0:T(8,128)S(1)}, f32[32,128]{1,0:T(8,128)S(1)}, u32[]{:S(2)}, u32[]{:S(2)}) collective-permute-start(f32[32,128]{1,0:T(8,128)S(1)} %get-tuple-element.29), channel_id=1, source_target_pairs={{0,2},{1,3},{2,0},{3,1},{4,6},{5,7},{6,4},{7,5},{8,10},{9,11},{10,... | collective-permute-start | bytes 49160 | tf_op jit(solution)/shard_map/ppermute | solution.py:348
  26.9 3.7 %collective-permute-start.13 = (f32[32,128]{1,0:T(8,128)S(1)}, f32[32,128]{1,0:T(8,128)S(1)}, u32[]{:S(2)}, u32[]{:S(2)}) collective-permute-start(f32[32,128]{1,0:T(8,128)S(1)} %get-tuple-element.30), channel_id=1, source_target_pairs={{0,3},{1,0},{2,1},{3,2},{4,7},{5,4},{6,5},{7,6},{8,11},{9,8},{10,9... | collective-permute-start | bytes 49160 | tf_op jit(solution)/shard_map/ppermute | solution.py:348

commit v25 on v23

--- a/solution.py
+++ b/solution.py
@@ -38,17 +38,7 @@
     return value.astype(jnp.float32).astype(jnp.bfloat16)
 
 
-def condition_kernel(holders, capacity, per_holder, *refs):
-    sources, packed_ref, again_ref, found_ref, landing, arrived, turned_ref = refs[:5], *refs[5:8], refs[8:13], *refs[13:]
-    copies = [
-        pltpu.make_async_copy(source, target, arrived.at[i])
-        for i, (source, target) in enumerate(zip(sources, landing))
-    ]
-    for copy in copies:
-        copy.start()
-    for copy in copies:
-        copy.wait()
-    query_ref, in_factor_ref, out_factor_ref, home_ref, cand_ref = landing
+def condition(query_ref, in_factor_ref, out_factor_ref, turned_ref, target_refs):
     rows, width = query_ref.shape
     layers, rank, _ = in_factor_ref.shape
     half = rank // 2
@@ -102,9 +92,25 @@
             turned_ref[layer, pl.ds(q, half, stride=rows), :] = done
         for t in range(half):
             tile = turned_ref[layer, t * rows:(t + 1) * rows, :].astype(jnp.bfloat16)
-            for target_ref in (packed_ref, again_ref):
+            for target_ref in target_refs:
                 target_ref[:, (first + t) * LANES:(first + t + 1) * LANES] = tile
 
+
+def condition_kernel(holders, capacity, per_holder, *refs):
+    sources, packed_ref, again_ref, notes_ref, found_ref = refs[:6], *refs[6:10]
+    in_factor_ref, out_factor_ref, pages_ref, query_ref, home_ref, cand_ref, arrived, turned_ref = refs[10:]
+    copies = [
+        pltpu.make_async_copy(source, target, arrived.at[i])
+        for i, (source, target) in enumerate(
+            zip(sources, (query_ref, in_factor_ref, out_factor_ref, home_ref, cand_ref, pages_ref))
+        )
+    ]
+    for copy in copies:
+        copy.start()
+    for copy in copies[:-1]:
+        copy.wait()
+    rows, width = query_ref.shape
+    condition(query_ref, in_factor_ref, out_factor_ref, turned_ref, (packed_ref, again_ref))
     slots = cand_ref.shape[1]
     home_rows = home_ref.shape[0]
     wanted = cand_ref[...]
@@ -128,27 +134,26 @@
     spare = packed_ref.shape[1] - width - capacity * len(blocks)
     if spare:
         blocks.append(jnp.zeros((rows, spare), jnp.float32))
+    notes = jnp.concatenate(blocks, axis=1).astype(jnp.bfloat16)
+    notes_ref[...] = notes
     for target_ref in (packed_ref, again_ref):
-        target_ref[:, width:] = jnp.concatenate(blocks, axis=1).astype(jnp.bfloat16)
+        target_ref[:, width:] = notes
     found_ref[...] = jnp.concatenate([holder, rank_there, jnp.zeros((6, slots), jnp.float32)], axis=0)
-
-
-def load_kernel(holders, count_ref, found_ref, block_ref, source_ref, same_block_ref, target_ref, used_ref, landing, arrived):
-    step = landing.shape[1] // LOADS
-    copies = [
-        pltpu.make_async_copy(
-            source_ref.at[:, pl.ds(i * step, step)], landing.at[:, pl.ds(i * step, step)], arrived.at[i]
-        )
-        for i in range(LOADS)
-    ]
-    for copy in copies:
-        copy.start()
+    copies[-1].wait()
+
+
+def late_kernel(query_ref, notes_ref, in_factor_ref, out_factor_ref, packed_ref, turned_ref):
+    condition(query_ref, in_factor_ref, out_factor_ref, turned_ref, (packed_ref,))
+    packed_ref[:, query_ref.shape[1]:] = notes_ref[...]
+
+
+def load_kernel(holders, count_ref, found_ref, block_ref, source_ref, same_block_ref, target_ref, used_ref):
     used_ref[...] = found_ref[...]
     slots = found_ref.shape[1]
     used_ref[0:1] = jnp.where(iota((1, slots), 1) < count_ref[0], found_ref[0:1], float(holders))
-    for i, copy in enumerate(copies):
-        copy.wait()
-        target_ref[i * step:(i + 1) * step, :] = landing[:, i * step:(i + 1) * step].T
+    step = source_ref.shape[1] // LOADS
+    for i in range(LOADS):
+        target_ref[i * step:(i + 1) * step, :] = source_ref[:, i * step:(i + 1) * step].T
 
 
 def pick(scores, wanted):
@@ -259,21 +264,28 @@
     home = page_home.reshape(-1, LANES)
     sources = [
         pltpu.with_memory_space_constraint(source, pltpu.HBM)
-        for source in (query_grads, factor_in, factor_out, home, cand_lists)
+        for source in (query_grads, factor_in, factor_out, home, cand_lists, page_store)
     ]
     notes = max(LANES, holders // rows * capacity)
-    packed, again, found = pl.pallas_call(
+    far = holders - 2
+    raw = swap(query_grads, "store", far)
+    turned = pltpu.VMEM((layers, rows * rank // 2, LANES), jnp.float32)
+    packed, again, own_notes, found, in_factor, out_factor, pages = pl.pallas_call(
         functools.partial(condition_kernel, holders, capacity, per_holder),
         out_shape=[
             jax.ShapeDtypeStruct((rows, width + notes), bf16),
             jax.ShapeDtypeStruct((rows, width + notes), bf16),
+            jax.ShapeDtypeStruct((rows, notes), bf16),
             jax.ShapeDtypeStruct((8, slots), jnp.float32),
+            jax.ShapeDtypeStruct(factor_in.shape, jnp.float32),
+            jax.ShapeDtypeStruct(factor_out.shape, jnp.float32),
+            pltpu.VMEM(page_store.shape, bf16),
         ],
         in_specs=[HBM] * len(sources),
-        out_specs=[VMEM] * 3,
-        scratch_shapes=[pltpu.VMEM(source.shape, source.dtype) for source in sources]
-        + [pltpu.SemaphoreType.DMA((len(sources),)), pltpu.VMEM((layers, rows * rank // 2, LANES), jnp.float32)],
-        compiler_params=pltpu.CompilerParams(vmem_limit_bytes=10 * 2**20 + 24 * slots * slots),
+        out_specs=[VMEM] * 7,
+        scratch_shapes=[pltpu.VMEM(sources[i].shape, sources[i].dtype) for i in (0, 3, 4)]
+        + [pltpu.SemaphoreType.DMA((len(sources),)), turned],
+        compiler_params=pltpu.CompilerParams(vmem_limit_bytes=14 * 2**20 + 24 * slots * slots),
     )(*sources)
 
     again, pages, used = pl.pallas_call(
@@ -283,18 +295,26 @@
             pltpu.VMEM((width, per_holder), bf16),
             jax.ShapeDtypeStruct(found.shape, jnp.float32),
         ],
-        in_specs=[SMEM, VMEM, VMEM, HBM],
+        in_specs=[SMEM, VMEM, VMEM, VMEM],
         out_specs=[VMEM] * 3,
         input_output_aliases={2: 0},
-        scratch_shapes=[pltpu.VMEM(page_store.shape, bf16), pltpu.SemaphoreType.DMA((LOADS,))],
         compiler_params=pltpu.CompilerParams(vmem_limit_bytes=4 * 2**20 + 4 * per_holder * width),
         cost_estimate=pl.CostEstimate(flops=0, bytes_accessed=2 * page_store.size, transcendentals=0),
-    )(counts, found, again, pltpu.with_memory_space_constraint(page_store, pltpu.HBM))
+    )(counts, found, again, pltpu.with_memory_space_constraint(pages, pltpu.VMEM))
 
     blocks = [None] * holders
     blocks[0] = packed
-    for k in range(2, holders, 2):
+    for k in range(2, holders - 2, 2):
         blocks[k] = swap(packed, "store", k)
+    blocks[far] = pl.pallas_call(
+        late_kernel,
+        out_shape=jax.ShapeDtypeStruct(packed.shape, bf16),
+        in_specs=[VMEM] * 4,
+        out_specs=VMEM,
+        scratch_shapes=[turned],
+        compiler_params=pltpu.CompilerParams(vmem_limit_bytes=8 * 2**20),
+        cost_estimate=pl.CostEstimate(flops=10**8, bytes_accessed=8 * packed.size, transcendentals=0),
+    )(raw, swap(own_notes, "store", far), in_factor, out_factor)
     blocks[1] = swap(again, "store", 1)
     for k in range(2, holders, 2):
         blocks[k + 1] = swap(blocks[k], "store", 1)

time: 31.5 us -> 32.5 us (1.032)
  starting transfers between devices: 15.5 us -> 17 us
    ppermute x8 -> x9, starting transfers between devices: 5.75 us -> 8.4 us  [swap(): lax.ppermute(value, axis, [(i, i ^ distance) for i in range(lax.axis_size...]
    pallas_call x1, Pallas kernels: 2.65 us -> 1.14 us  [on_device(): pl.pallas_call(functools.partial(load_kernel, holders), out_shape=[jax.Sh...]
    ppermute x3, starting transfers between devices: 4.22 us -> 3.01 us  [on_device(): landed.append(lax.ppermute(pair, 'store', to) if step else pair)]
    pallas_call x0 -> x1, Pallas kernels: none -> 1 us  [on_device(): pl.pallas_call(late_kernel, out_shape=jax.ShapeDtypeStruct(packed.shape,...]
    ppermute x8 -> x9, waiting for transfers between devices: 3.82 us -> 3.1 us  [swap(): lax.ppermute(value, axis, [(i, i ^ distance) for i in range(lax.axis_size...]
    ppermute x3, waiting for transfers between devices: 1.44 us -> 1.93 us  [on_device(): landed.append(lax.ppermute(pair, 'store', to) if step else pair)]
  transfers between devices with their start and end apart: 14 -> 15, of which waited for: 9 -> 9; matrix products, arithmetic and copies ran while one was open for 0% -> 0% of each run, Pallas kernels for 9% -> 15%
where the time goes in v25:
time: 32.5 us; the launch traced here: 32.3 us
  starting transfers between devices  17 us (52%)
  waiting for transfers between devices  7.42 us (23%)
  Pallas kernels  6.44 us (20%)
  between operations  0.73 us (2%)
  other arithmetic  0.64 us (2%)
    ppermute x9, starting transfers between devices, swap(): lax.ppermute(value, axis, [(i, i ^ distance) for i in range(lax.axis_size...  8.4 us
    ppermute x3, starting transfers between devices, on_device(): lax.ppermute(terms[step], 'layer', [(g, (g + step) % groups) for g in ran...  5.57 us
    ppermute x9, waiting for transfers between devices, swap(): lax.ppermute(value, axis, [(i, i ^ distance) for i in range(lax.axis_size...  3.1 us
    ppermute x3, starting transfers between devices, on_device(): landed.append(lax.ppermute(pair, 'store', to) if step else pair)  3.01 us
    pallas_call x1, Pallas kernels, on_device(): pl.pallas_call(functools.partial(condition_kernel, holders, capacity, per...  2.42 us
    ppermute x3, waiting for transfers between devices, on_device(): lax.ppermute(terms[step], 'layer', [(g, (g + step) % groups) for g in ran...  2.39 us
    ppermute x3, waiting for transfers between devices, on_device(): landed.append(lax.ppermute(pair, 'store', to) if step else pair)  1.93 us
    pallas_call x1, Pallas kernels, on_device(): pl.pallas_call(functools.partial(score_kernel, holders, capacity), out_sh...  1.18 us
  transfers between devices with their start and end apart: 15, of which 9 were waited for; matrix products, arithmetic and copies ran while one was open for 0% of the time, Pallas kernels for 15%

profile of v25, /device:TPU:0, one launch (start us, length us, event | category | flops | bytes accessed | tf_op | source)
XLA Modules:
  0.0 32.3 jit_solution(8820240324577322674)
XLA Ops:
  0.0 3.9 %collective-permute-start = (bf16[8,8192]{1,0:T(8,128)(2,1)}, bf16[8,8192]{1,0:T(8,128)(2,1)S(1)}, u32[]{:S(2)}, u32[]{:S(2)}) collective-permute-start(bf16[8,8192]{1,0:T(8,128)(2,1)} %refs_0_.1), channel_id=1, source_target_pairs={{0,24},{4,28},{8,16},{12,20},{16,8},{20,12},{24,0},{28,4},{1,25},{... | collective-permute-start | bytes 393224 | tf_op jit(solution)/shard_map/ppermute | solution.py:251
  3.9 2.4 %shard_map.73 = (bf16[8,8320]{1,0:T(8,128)(2,1)S(1)}, bf16[8,8320]{1,0:T(8,128)(2,1)S(1)}, bf16[8,128]{1,0:T(8,128)(2,1)S(1)}, f32[8,256]{1,0:T(8,128)S(1)}, f32...) custom-call(bf16[8,8192]{1,0:T(8,128)(2,1)} %refs_0_.1, f32[2,64,64]{2,1,0:T(8,128)} %refs_1_.1, ...), custom_call_target="tpu_custom_call" | custom-call | tf_op jit(solution)/shard_map/pallas_call | solution.py:273
  6.3 0.6 %collective-permute-start.3 = (bf16[8,8320]{1,0:T(8,128)(2,1)S(1)}, bf16[8,8320]{1,0:T(8,128)(2,1)S(1)}, u32[]{:S(2)}, u32[]{:S(2)}) collective-permute-start(bf16[8,8320]{1,0:T(8,128)(2,1)S(1)} %get-tuple-element.29.refs_7_), channel_id=1, source_target_pairs={{0,16},{4,20},{8,24},{12,28},{16,0},{20,4},{24,8},{28,12},{1,17},{... | collective-permute-start | bytes 399368 | tf_op jit(solution)/shard_map/ppermute | solution.py:251
  6.9 0.1 collective-permute-start.5
  7.0 2.9 %collective-permute-start.1 = (bf16[8,128]{1,0:T(8,128)(2,1)S(1)}, bf16[8,128]{1,0:T(8,128)(2,1)S(1)}, u32[]{:S(2)}, u32[]{:S(2)}) collective-permute-start(bf16[8,128]{1,0:T(8,128)(2,1)S(1)} %get-tuple-element.26), channel_id=1, source_target_pairs={{0,24},{4,28},{8,16},{12,20},{16,8},{20,12},{24,0},{28,4},{1,25},{... | collective-permute-start | bytes 6152 | tf_op jit(solution)/shard_map/ppermute | solution.py:251
  10.5 1.1 %shard_map.74 = (bf16[8,8320]{1,0:T(8,128)(2,1)S(1)}, bf16[8192,256]{1,0:T(8,128)(2,1)S(1)}, f32[8,256]{1,0:T(8,128)S(1)}) custom-call(s32[1]{0:T(128)S(6)} %copy.10.count_ref, f32[8,256]{1,0:T(8,128)S(1)} %get-tuple-element.22.found_ref, bf16[8,8320]{1,0:T(8,128)(2,1)S(1)} %get-tuple-element.23.block_ref, ...), custom_call_target="tpu_custom_call", output_to_operand_aliasing={{0}: (2, {})} | custom-call | bytes 4194304 | tf_op jit(solution)/shard_map/pallas_call | solution.py:291
  11.7 0.1 collective-permute-start.7
  11.8 1.1 %collective-permute-done.1.notes_ref = bf16[8,128]{1,0:T(8,128)(2,1)S(1)} collective-permute-done((bf16[8,128]{1,0:T(8,128)(2,1)S(1)}, bf16[8,128]{1,0:T(8,128)(2,1)S(1)}, u32[]{:S(2)}, u32[]{:S(2)}) %collective-permute-start.1) | collective-permute-done | bytes 2080 | tf_op jit(solution)/shard_map/ppermute | solution.py:251
  12.9 0.0 collective-permute-done.query_ref
  12.9 1.0 %shard_map.75.refs_1_ = bf16[8,8320]{1,0:T(8,128)(2,1)S(1)} custom-call(bf16[8,8192]{1,0:T(8,128)(2,1)S(1)} %collective-permute-done.query_ref, bf16[8,128]{1,0:T(8,128)(2,1)S(1)} %collective-permute-done.1.notes_ref, f32[2,64,64]{2,1,0:T(8,128)S(1)} %get-tuple-element.27.in_factor_ref, f32[2,64,64]{2,1,0:T(8,128)S(1)} %get-tuple-element.28.out_factor_ref), custom_call_target="tpu_custom_call" | custom-call | flops 100000000 | bytes 532480 | tf_op jit(solution)/shard_map/pallas_call | solution.py:309
  13.9 0.1 collective-permute-start.2
  14.0 0.0 collective-permute-done.3.refs_3_
  14.0 0.5 %collective-permute-start.4 = (bf16[8,8320]{1,0:T(8,128)(2,1)S(1)}, bf16[8,8320]{1,0:T(8,128)(2,1)S(1)}, u32[]{:S(2)}, u32[]{:S(2)}) collective-permute-start(bf16[8,8320]{1,0:T(8,128)(2,1)S(1)} %collective-permute-done.3.refs_3_), channel_id=1, source_target_pairs={{0,4},{4,0},{8,12},{12,8},{16,20},{20,16},{24,28},{28,24},{1,5},{5... | collective-permute-start | bytes 399368 | tf_op jit(solution)/shard_map/ppermute | solution.py:251
  14.5 0.0 collective-permute-done.5.refs_5_
  14.5 0.1 collective-permute-start.6
  14.5 0.0 collective-permute-done.7.refs_6_
  14.5 0.7 %collective-permute-done.2.refs_0_ = bf16[8,8320]{1,0:T(8,128)(2,1)S(1)} collective-permute-done((bf16[8,8320]{1,0:T(8,128)(2,1)S(1)}, bf16[8,8320]{1,0:T(8,128)(2,1)S(1)}, u32[]{:S(2)}, u32[]{:S(2)}) %collective-permute-start.2) | collective-permute-done | bytes 133152 | tf_op jit(solution)/shard_map/ppermute | solution.py:251
  15.3 0.2 collective-permute-done.4.refs_2_
  15.5 0.3 %collective-permute-done.6.refs_4_ = bf16[8,8320]{1,0:T(8,128)(2,1)S(1)} collective-permute-done((bf16[8,8320]{1,0:T(8,128)(2,1)S(1)}, bf16[8,8320]{1,0:T(8,128)(2,1)S(1)}, u32[]{:S(2)}, u32[]{:S(2)}) %collective-permute-start.6) | collective-permute-done | bytes 133152 | tf_op jit(solution)/shard_map/ppermute | solution.py:251
  15.8 1.2 %shard_map.76 = (f32[4,16,128]{2,1,0:T(8,128)S(1)}, f32[64,256]{1,0:T(8,128)S(1)}, f32[1,128]{1,0:T(1,128)S(1)}) custom-call(bf16[8,8320]{1,0:T(8,128)(2,1)S(1)} %collective-permute-done.2.refs_0_, bf16[8,8320]{1,0:T(8,128)(2,1)S(1)} %shard_map.75.refs_1_, bf16[8,8320]{1,0:T(8,128)(2,1)S(1)} %collective-permute-done.4.refs_2_, ...), custom_call_target="tpu_custom_call" | custom-call | tf_op jit(solution)/shard_map/pallas_call | solution.py:325
  17.0 0.2 collective-permute-start.8
  17.2 0.3 shard_map.77
  17.5 0.7 %collective-permute-done.8 = f32[4,16,128]{2,1,0:T(8,128)S(1)} collective-permute-done((f32[4,16,128]{2,1,0:T(8,128)S(1)}, f32[4,16,128]{2,1,0:T(8,128)S(1)}, u32[]{:S(2)}, u32[]{:S(2)}) %collective-permute-start.8) | collective-permute-done | bytes 32800 | tf_op jit(solution)/shard_map/ppermute | solution.py:251
  18.3 0.3 %collective-permute-start.11 = (f32[2,16,128]{2,1,0:T(8,128)S(1)}, f32[2,16,128]{2,1,0:T(8,128)S(1)}, u32[]{:S(2)}, u32[]{:S(2)}) collective-permute-start(f32[2,16,128]{2,1,0:T(8,128)S(1)} %pad_maximum_fusion.2), channel_id=1, source_target_pairs={{0,12},{4,8},{8,20},{12,16},{16,28},{20,24},{24,4},{28,0},{1,13},{... | collective-permute-start | bytes 49160 | tf_op jit(solution)/shard_map/ppermute | solution.py:351
  18.6 1.5 %collective-permute-start.10 = (f32[2,16,128]{2,1,0:T(8,128)S(1)}, f32[2,16,128]{2,1,0:T(8,128)S(1)}, u32[]{:S(2)}, u32[]{:S(2)}) collective-permute-start(f32[2,16,128]{2,1,0:T(8,128)S(1)} %pad_maximum_fusion.1), channel_id=1, source_target_pairs={{0,20},{4,16},{8,28},{12,24},{16,4},{20,0},{24,12},{28,8},{1,21},{... | collective-permute-start | bytes 49160 | tf_op jit(solution)/shard_map/ppermute | solution.py:351
  20.0 1.2 %collective-permute-start.9 = (f32[2,16,128]{2,1,0:T(8,128)S(1)}, f32[2,16,128]{2,1,0:T(8,128)S(1)}, u32[]{:S(2)}, u32[]{:S(2)}) collective-permute-start(f32[2,16,128]{2,1,0:T(8,128)S(1)} %pad_maximum_fusion), channel_id=1, source_target_pairs={{0,28},{4,24},{8,4},{12,0},{16,12},{20,8},{24,20},{28,16},{1,29},{... | collective-permute-start | bytes 49160 | tf_op jit(solution)/shard_map/ppermute | solution.py:351
  21.3 1.2 %collective-permute-done.11.refs_2_ = f32[2,16,128]{2,1,0:T(8,128)S(1)} collective-permute-done((f32[2,16,128]{2,1,0:T(8,128)S(1)}, f32[2,16,128]{2,1,0:T(8,128)S(1)}, u32[]{:S(2)}, u32[]{:S(2)}) %collective-permute-start.11) | collective-permute-done | bytes 16416 | tf_op jit(solution)/shard_map/ppermute | solution.py:351
  22.4 0.0 collective-permute-done.10.refs_1_
  22.4 0.8 %collective-permute-done.9.refs_0_ = f32[2,16,128]{2,1,0:T(8,128)S(1)} collective-permute-done((f32[2,16,128]{2,1,0:T(8,128)S(1)}, f32[2,16,128]{2,1,0:T(8,128)S(1)}, u32[]{:S(2)}, u32[]{:S(2)}) %collective-permute-start.9) | collective-permute-done | bytes 16416 | tf_op jit(solution)/shard_map/ppermute | solution.py:351
  23.2 0.4 %shard_map.78 = (f32[32,128]{1,0:T(8,128)S(1)}, f32[32,128]{1,0:T(8,128)S(1)}, f32[32,128]{1,0:T(8,128)S(1)}, f32[32,128]{1,0:T(8,128)S(1)}) custom-call(f32[8,256]{1,0:T(8,128)S(1)} %get-tuple-element.25.found_ref, f32[2,16,128]{2,1,0:T(8,128)S(1)} %collective-permute-done.9.refs_0_, f32[2,16,128]{2,1,0:T(8,128)S(1)} %collective-permute-done.10.refs_1_, ...), custom_call_target="tpu_custom_call" | custom-call | tf_op jit(solution)/shard_map/pallas_call | solution.py:353
  23.6 1.6 %collective-permute-start.12 = (f32[32,128]{1,0:T(8,128)S(1)}, f32[32,128]{1,0:T(8,128)S(1)}, u32[]{:S(2)}, u32[]{:S(2)}) collective-permute-start(f32[32,128]{1,0:T(8,128)S(1)} %get-tuple-element.36), channel_id=1, source_target_pairs={{0,1},{1,2},{2,3},{3,0},{4,5},{5,6},{6,7},{7,4},{8,9},{9,10},{10,1... | collective-permute-start | bytes 49160 | tf_op jit(solution)/shard_map/ppermute | solution.py:362
  25.3 2.6 %collective-permute-start.13 = (f32[32,128]{1,0:T(8,128)S(1)}, f32[32,128]{1,0:T(8,128)S(1)}, u32[]{:S(2)}, u32[]{:S(2)}) collective-permute-start(f32[32,128]{1,0:T(8,128)S(1)} %get-tuple-element.37), channel_id=1, source_target_pairs={{0,2},{1,3},{2,0},{3,1},{4,6},{5,7},{6,4},{7,5},{8,10},{9,11},{10,... | collective-permute-start | bytes 49160 | tf_op jit(solution)/shard_map/ppermute | solution.py:362
  27.9 1.3 %collective-permute-start.14 = (f32[32,128]{1,0:T(8,128)S(1)}, f32[32,128]{1,0:T(8,128)S(1)}, u32[]{:S(2)}, u32[]{:S(2)}) collective-permute-start(f32[32,128]{1,0:T(8,128)S(1)} %get-tuple-element.38), channel_id=1, source_target_pairs={{0,3},{1,0},{2,1},{3,2},{4,7},{5,4},{6,5},{7,6},{8,11},{9,8},{10,9... | collective-permute-start | bytes 49160 | tf_op jit(solution)/shard_map/ppermute | solution.py:362
  29.2 0.0 collective-permute-done.12
  29.2 1.0 %collective-permute-done.13 = f32[32,128]{1,0:T(8,128)S(1)} collective-permute-done((f32[32,128]{1,0:T(8,128)S(1)}, f32[32,128]{1,0:T(8,128)S(1)}, u32[]{:S(2)}, u32[]{:S(2)}) %collective-permute-start.13) | collective-permute-done | bytes 16416 | tf_op jit(solution)/shard_map/ppermute | solution.py:362
  30.2 1.4 %collective-permute-done.14 = f32[32,128]{1,0:T(8,128)S(1)} collective-permute-done((f32[32,128]{1,0:T(8,128)S(1)}, f32[32,128]{1,0:T(8,128)S(1)}, u32[]{:S(2)}, u32[]{:S(2)}) %collective-permute-start.14) | collective-permute-done | bytes 16416 | tf_op jit(solution)/shard_map/ppermute | solution.py:362
  31.6 0.1 fusion.2
  31.7 0.6 %maximum_bitcast_fusion = f32[1,64,64]{2,1,0:T(8,128)} fusion(f32[32,64]{1,0:T(8,128)S(1)} %get-tuple-element.48, f32[32,64]{1,0:T(8,128)S(1)} %get-tuple-element.47), kind=kLoop, calls=%fused_computation | loop fusion | flops 4096 | bytes 32768 | tf_op jit(solution)/shard_map/broadcast_in_dim | solution.py:363
  (7 shorter events, 0.1 us)
Async XLA Ops:
  0.0 12.9 %collective-permute-start = (bf16[8,8192]{1,0:T(8,128)(2,1)}, bf16[8,8192]{1,0:T(8,128)(2,1)S(1)}, u32[]{:S(2)}, u32[]{:S(2)}) collective-permute-start(bf16[8,8192]{1,0:T(8,128)(2,1)} %refs_0_.1), channel_id=1, source_target_pairs={{0,24},{4,28},{8,16},{12,20},{16,8},{20,12},{24,0},{28,4},{1,25},{... | collective-permute-start | bytes 393224 | tf_op jit(solution)/shard_map/ppermute | solution.py:251
  6.3 7.6 %collective-permute-start.3 = (bf16[8,8320]{1,0:T(8,128)(2,1)S(1)}, bf16[8,8320]{1,0:T(8,128)(2,1)S(1)}, u32[]{:S(2)}, u32[]{:S(2)}) collective-permute-start(bf16[8,8320]{1,0:T(8,128)(2,1)S(1)} %get-tuple-element.29.refs_7_), channel_id=1, source_target_pairs={{0,16},{4,20},{8,24},{12,28},{16,0},{20,4},{24,8},{28,12},{1,17},{... | collective-permute-start | bytes 399368 | tf_op jit(solution)/shard_map/ppermute | solution.py:251
  6.9 7.6 %collective-permute-start.5 = (bf16[8,8320]{1,0:T(8,128)(2,1)S(1)}, bf16[8,8320]{1,0:T(8,128)(2,1)S(1)}, u32[]{:S(2)}, u32[]{:S(2)}) collective-permute-start(bf16[8,8320]{1,0:T(8,128)(2,1)S(1)} %get-tuple-element.29.refs_7_), channel_id=1, source_target_pairs={{0,8},{4,12},{8,0},{12,4},{16,24},{20,28},{24,16},{28,20},{1,9},{5... | collective-permute-start | bytes 399368 | tf_op jit(solution)/shard_map/ppermute | solution.py:251
  7.0 5.9 %collective-permute-start.1 = (bf16[8,128]{1,0:T(8,128)(2,1)S(1)}, bf16[8,128]{1,0:T(8,128)(2,1)S(1)}, u32[]{:S(2)}, u32[]{:S(2)}) collective-permute-start(bf16[8,128]{1,0:T(8,128)(2,1)S(1)} %get-tuple-element.26), channel_id=1, source_target_pairs={{0,24},{4,28},{8,16},{12,20},{16,8},{20,12},{24,0},{28,4},{1,25},{... | collective-permute-start | bytes 6152 | tf_op jit(solution)/shard_map/ppermute | solution.py:251
  11.7 2.9 %collective-permute-start.7 = (bf16[8,8320]{1,0:T(8,128)(2,1)S(1)}, bf16[8,8320]{1,0:T(8,128)(2,1)S(1)}, u32[]{:S(2)}, u32[]{:S(2)}) collective-permute-start(bf16[8,8320]{1,0:T(8,128)(2,1)S(1)} %get-tuple-element.30), channel_id=1, source_target_pairs={{0,4},{4,0},{8,12},{12,8},{16,20},{20,16},{24,28},{28,24},{1,5},{5... | collective-permute-start | bytes 399368 | tf_op jit(solution)/shard_map/ppermute | solution.py:251
  13.9 1.4 %collective-permute-start.2 = (bf16[8,8320]{1,0:T(8,128)(2,1)S(1)}, bf16[8,8320]{1,0:T(8,128)(2,1)S(1)}, u32[]{:S(2)}, u32[]{:S(2)}) collective-permute-start(bf16[8,8320]{1,0:T(8,128)(2,1)S(1)} %shard_map.75.refs_1_), channel_id=1, source_target_pairs={{0,4},{4,0},{8,12},{12,8},{16,20},{20,16},{24,28},{28,24},{1,5},{5... | collective-permute-start | bytes 399368 | tf_op jit(solution)/shard_map/ppermute | solution.py:251
  14.0 1.5 %collective-permute-start.4 = (bf16[8,8320]{1,0:T(8,128)(2,1)S(1)}, bf16[8,8320]{1,0:T(8,128)(2,1)S(1)}, u32[]{:S(2)}, u32[]{:S(2)}) collective-permute-start(bf16[8,8320]{1,0:T(8,128)(2,1)S(1)} %collective-permute-done.3.refs_3_), channel_id=1, source_target_pairs={{0,4},{4,0},{8,12},{12,8},{16,20},{20,16},{24,28},{28,24},{1,5},{5... | collective-permute-start | bytes 399368 | tf_op jit(solution)/shard_map/ppermute | solution.py:251
  14.5 1.4 %collective-permute-start.6 = (bf16[8,8320]{1,0:T(8,128)(2,1)S(1)}, bf16[8,8320]{1,0:T(8,128)(2,1)S(1)}, u32[]{:S(2)}, u32[]{:S(2)}) collective-permute-start(bf16[8,8320]{1,0:T(8,128)(2,1)S(1)} %collective-permute-done.5.refs_5_), channel_id=1, source_target_pairs={{0,4},{4,0},{8,12},{12,8},{16,20},{20,16},{24,28},{28,24},{1,5},{5... | collective-permute-start | bytes 399368 | tf_op jit(solution)/shard_map/ppermute | solution.py:251
  17.0 1.3 %collective-permute-start.8 = (f32[4,16,128]{2,1,0:T(8,128)S(1)}, f32[4,16,128]{2,1,0:T(8,128)S(1)}, u32[]{:S(2)}, u32[]{:S(2)}) collective-permute-start(f32[4,16,128]{2,1,0:T(8,128)S(1)} %get-tuple-element.34), channel_id=1, source_target_pairs={{0,4},{4,0},{8,12},{12,8},{16,20},{20,16},{24,28},{28,24},{1,5},{5... | collective-permute-start | bytes 98312 | tf_op jit(solution)/shard_map/ppermute | solution.py:251
  18.3 4.2 %collective-permute-start.11 = (f32[2,16,128]{2,1,0:T(8,128)S(1)}, f32[2,16,128]{2,1,0:T(8,128)S(1)}, u32[]{:S(2)}, u32[]{:S(2)}) collective-permute-start(f32[2,16,128]{2,1,0:T(8,128)S(1)} %pad_maximum_fusion.2), channel_id=1, source_target_pairs={{0,12},{4,8},{8,20},{12,16},{16,28},{20,24},{24,4},{28,0},{1,13},{... | collective-permute-start | bytes 49160 | tf_op jit(solution)/shard_map/ppermute | solution.py:351
  18.6 3.8 %collective-permute-start.10 = (f32[2,16,128]{2,1,0:T(8,128)S(1)}, f32[2,16,128]{2,1,0:T(8,128)S(1)}, u32[]{:S(2)}, u32[]{:S(2)}) collective-permute-start(f32[2,16,128]{2,1,0:T(8,128)S(1)} %pad_maximum_fusion.1), channel_id=1, source_target_pairs={{0,20},{4,16},{8,28},{12,24},{16,4},{20,0},{24,12},{28,8},{1,21},{... | collective-permute-start | bytes 49160 | tf_op jit(solution)/shard_map/ppermute | solution.py:351
  20.0 3.2 %collective-permute-start.9 = (f32[2,16,128]{2,1,0:T(8,128)S(1)}, f32[2,16,128]{2,1,0:T(8,128)S(1)}, u32[]{:S(2)}, u32[]{:S(2)}) collective-permute-start(f32[2,16,128]{2,1,0:T(8,128)S(1)} %pad_maximum_fusion), channel_id=1, source_target_pairs={{0,28},{4,24},{8,4},{12,0},{16,12},{20,8},{24,20},{28,16},{1,29},{... | collective-permute-start | bytes 49160 | tf_op jit(solution)/shard_map/ppermute | solution.py:351
  23.6 5.6 %collective-permute-start.12 = (f32[32,128]{1,0:T(8,128)S(1)}, f32[32,128]{1,0:T(8,128)S(1)}, u32[]{:S(2)}, u32[]{:S(2)}) collective-permute-start(f32[32,128]{1,0:T(8,128)S(1)} %get-tuple-element.36), channel_id=1, source_target_pairs={{0,1},{1,2},{2,3},{3,0},{4,5},{5,6},{6,7},{7,4},{8,9},{9,10},{10,1... | collective-permute-start | bytes 49160 | tf_op jit(solution)/shard_map/ppermute | solution.py:362
  25.3 4.9 %collective-permute-start.13 = (f32[32,128]{1,0:T(8,128)S(1)}, f32[32,128]{1,0:T(8,128)S(1)}, u32[]{:S(2)}, u32[]{:S(2)}) collective-permute-start(f32[32,128]{1,0:T(8,128)S(1)} %get-tuple-element.37), channel_id=1, source_target_pairs={{0,2},{1,3},{2,0},{3,1},{4,6},{5,7},{6,4},{7,5},{8,10},{9,11},{10,... | collective-permute-start | bytes 49160 | tf_op jit(solution)/shard_map/ppermute | solution.py:362
  27.9 3.7 %collective-permute-start.14 = (f32[32,128]{1,0:T(8,128)S(1)}, f32[32,128]{1,0:T(8,128)S(1)}, u32[]{:S(2)}, u32[]{:S(2)}) collective-permute-start(f32[32,128]{1,0:T(8,128)S(1)} %get-tuple-element.38), channel_id=1, source_target_pairs={{0,3},{1,0},{2,1},{3,2},{4,7},{5,4},{6,5},{7,6},{8,11},{9,8},{10,9... | collective-permute-start | bytes 49160 | tf_op jit(solution)/shard_map/ppermute | solution.py:362

commit v26 on v25

--- a/solution.py
+++ b/solution.py
@@ -12,6 +12,7 @@
 HBM = pl.BlockSpec(memory_space=pltpu.HBM)
 LANES = 128
 CHUNKS = 4
+LATE_FLOPS = 5 * 10**9
 LOADS = 8
 
 
@@ -96,21 +97,7 @@
                 target_ref[:, (first + t) * LANES:(first + t + 1) * LANES] = tile
 
 
-def condition_kernel(holders, capacity, per_holder, *refs):
-    sources, packed_ref, again_ref, notes_ref, found_ref = refs[:6], *refs[6:10]
-    in_factor_ref, out_factor_ref, pages_ref, query_ref, home_ref, cand_ref, arrived, turned_ref = refs[10:]
-    copies = [
-        pltpu.make_async_copy(source, target, arrived.at[i])
-        for i, (source, target) in enumerate(
-            zip(sources, (query_ref, in_factor_ref, out_factor_ref, home_ref, cand_ref, pages_ref))
-        )
-    ]
-    for copy in copies:
-        copy.start()
-    for copy in copies[:-1]:
-        copy.wait()
-    rows, width = query_ref.shape
-    condition(query_ref, in_factor_ref, out_factor_ref, turned_ref, (packed_ref, again_ref))
+def look_up(holders, capacity, per_holder, rows, cand_ref, home_ref):
     slots = cand_ref.shape[1]
     home_rows = home_ref.shape[0]
     wanted = cand_ref[...]
@@ -131,20 +118,42 @@
         preferred_element_type=jnp.float32,
     )
     blocks = [asked[h:h + rows] for h in range(0, holders, rows)]
-    spare = packed_ref.shape[1] - width - capacity * len(blocks)
+    spare = max(LANES, capacity * len(blocks)) - capacity * len(blocks)
     if spare:
         blocks.append(jnp.zeros((rows, spare), jnp.float32))
     notes = jnp.concatenate(blocks, axis=1).astype(jnp.bfloat16)
-    notes_ref[...] = notes
+    return notes, holder, rank_there
+
+
+def condition_kernel(holders, capacity, per_holder, *refs):
+    sources, packed_ref, again_ref, found_ref = refs[:6], *refs[6:9]
+    in_factor_ref, out_factor_ref, home_ref, pages_ref, query_ref, cand_ref, arrived, turned_ref = refs[9:]
+    copies = [
+        pltpu.make_async_copy(source, target, arrived.at[i])
+        for i, (source, target) in enumerate(
+            zip(sources, (query_ref, in_factor_ref, out_factor_ref, home_ref, cand_ref, pages_ref))
+        )
+    ]
+    for copy in copies:
+        copy.start()
+    for copy in copies[:-1]:
+        copy.wait()
+    rows, width = query_ref.shape
+    condition(query_ref, in_factor_ref, out_factor_ref, turned_ref, (packed_ref, again_ref))
+    notes, holder, rank_there = look_up(holders, capacity, per_holder, rows, cand_ref, home_ref)
+    slots = cand_ref.shape[1]
     for target_ref in (packed_ref, again_ref):
         target_ref[:, width:] = notes
     found_ref[...] = jnp.concatenate([holder, rank_there, jnp.zeros((6, slots), jnp.float32)], axis=0)
     copies[-1].wait()
 
 
-def late_kernel(query_ref, notes_ref, in_factor_ref, out_factor_ref, packed_ref, turned_ref):
+def late_kernel(
+    holders, capacity, per_holder, query_ref, cand_ref, in_factor_ref, out_factor_ref, home_ref, packed_ref, turned_ref
+):
+    rows, width = query_ref.shape
     condition(query_ref, in_factor_ref, out_factor_ref, turned_ref, (packed_ref,))
-    packed_ref[:, query_ref.shape[1]:] = notes_ref[...]
+    packed_ref[:, width:] = look_up(holders, capacity, per_holder, rows, cand_ref, home_ref)[0]
 
 
 def load_kernel(holders, count_ref, found_ref, block_ref, source_ref, same_block_ref, target_ref, used_ref):
@@ -269,21 +278,22 @@
     notes = max(LANES, holders // rows * capacity)
     far = holders - 2
     raw = swap(query_grads, "store", far)
+    far_list = swap(cand_lists, "store", far)
     turned = pltpu.VMEM((layers, rows * rank // 2, LANES), jnp.float32)
-    packed, again, own_notes, found, in_factor, out_factor, pages = pl.pallas_call(
+    packed, again, found, in_factor, out_factor, home_here, pages = pl.pallas_call(
         functools.partial(condition_kernel, holders, capacity, per_holder),
         out_shape=[
             jax.ShapeDtypeStruct((rows, width + notes), bf16),
             jax.ShapeDtypeStruct((rows, width + notes), bf16),
-            jax.ShapeDtypeStruct((rows, notes), bf16),
             jax.ShapeDtypeStruct((8, slots), jnp.float32),
             jax.ShapeDtypeStruct(factor_in.shape, jnp.float32),
             jax.ShapeDtypeStruct(factor_out.shape, jnp.float32),
+            jax.ShapeDtypeStruct(home.shape, jnp.int32),
             pltpu.VMEM(page_store.shape, bf16),
         ],
         in_specs=[HBM] * len(sources),
         out_specs=[VMEM] * 7,
-        scratch_shapes=[pltpu.VMEM(sources[i].shape, sources[i].dtype) for i in (0, 3, 4)]
+        scratch_shapes=[pltpu.VMEM(sources[i].shape, sources[i].dtype) for i in (0, 4)]
         + [pltpu.SemaphoreType.DMA((len(sources),)), turned],
         compiler_params=pltpu.CompilerParams(vmem_limit_bytes=14 * 2**20 + 24 * slots * slots),
     )(*sources)
@@ -307,14 +317,14 @@
     for k in range(2, holders - 2, 2):
         blocks[k] = swap(packed, "store", k)
     blocks[far] = pl.pallas_call(
-        late_kernel,
+        functools.partial(late_kernel, holders, capacity, per_holder),
         out_shape=jax.ShapeDtypeStruct(packed.shape, bf16),
-        in_specs=[VMEM] * 4,
+        in_specs=[VMEM] * 5,
         out_specs=VMEM,
         scratch_shapes=[turned],
-        compiler_params=pltpu.CompilerParams(vmem_limit_bytes=8 * 2**20),
-        cost_estimate=pl.CostEstimate(flops=10**8, bytes_accessed=8 * packed.size, transcendentals=0),
-    )(raw, swap(own_notes, "store", far), in_factor, out_factor)
+        compiler_params=pltpu.CompilerParams(vmem_limit_bytes=10 * 2**20 + 24 * slots * slots),
+        cost_estimate=pl.CostEstimate(flops=LATE_FLOPS, bytes_accessed=8 * packed.size, transcendentals=0),
+    )(raw, far_list, in_factor, out_factor, home_here)
     blocks[1] = swap(again, "store", 1)
     for k in range(2, holders, 2):
         blocks[k + 1] = swap(blocks[k], "store", 1)

time: 32.5 us -> 31.3 us (0.963)
  waiting for transfers between devices: 7.42 us -> 5.54 us
  starting transfers between devices: 17 us -> 17.5 us
    ppermute x9, waiting for transfers between devices: 3.1 us -> 1.61 us  [swap(): lax.ppermute(value, axis, [(i, i ^ distance) for i in range(lax.axis_size...]
    ppermute x9, starting transfers between devices: 8.4 us -> 8.9 us  [swap(): lax.ppermute(value, axis, [(i, i ^ distance) for i in range(lax.axis_size...]
    ppermute x3, waiting for transfers between devices: 1.93 us -> 1.53 us  [on_device(): landed.append(lax.ppermute(pair, 'store', to) if step else pair)]
  transfers between devices with their start and end apart: 15 -> 15, of which waited for: 9 -> 9; matrix products, arithmetic and copies ran while one was open for 0% -> 0% of each run, Pallas kernels for 15% -> 16%
where the time goes in v26:
time: 31.3 us; the launch traced here: 31.2 us
  starting transfers between devices  17.5 us (56%)
  Pallas kernels  6.62 us (21%)
  waiting for transfers between devices  5.54 us (18%)
  between operations  0.72 us (2%)
  other arithmetic  0.64 us (2%)
    ppermute x9, starting transfers between devices, swap(): lax.ppermute(value, axis, [(i, i ^ distance) for i in range(lax.axis_size...  8.9 us
    ppermute x3, starting transfers between devices, on_device(): lax.ppermute(terms[step], 'layer', [(g, (g + step) % groups) for g in ran...  5.57 us
    ppermute x3, starting transfers between devices, on_device(): landed.append(lax.ppermute(pair, 'store', to) if step else pair)  3.07 us
    pallas_call x1, Pallas kernels, on_device(): pl.pallas_call(functools.partial(condition_kernel, holders, capacity, per...  2.43 us
    ppermute x3, waiting for transfers between devices, on_device(): lax.ppermute(terms[step], 'layer', [(g, (g + step) % groups) for g in ran...  2.39 us
    ppermute x9, waiting for transfers between devices, swap(): lax.ppermute(value, axis, [(i, i ^ distance) for i in range(lax.axis_size...  1.61 us
    ppermute x3, waiting for transfers between devices, on_device(): landed.append(lax.ppermute(pair, 'store', to) if step else pair)  1.53 us
    pallas_call x1, Pallas kernels, on_device(): pl.pallas_call(functools.partial(late_kernel, holders, capacity, per_hold...  1.19 us
  transfers between devices with their start and end apart: 15, of which 9 were waited for; matrix products, arithmetic and copies ran while one was open for 0% of the time, Pallas kernels for 16%

profile of v26, /device:TPU:0, one launch (start us, length us, event | category | flops | bytes accessed | tf_op | source)
XLA Modules:
  0.0 31.2 jit_solution(12044670698925485611)
XLA Ops:
  0.0 3.9 %collective-permute-start = (bf16[8,8192]{1,0:T(8,128)(2,1)}, bf16[8,8192]{1,0:T(8,128)(2,1)S(1)}, u32[]{:S(2)}, u32[]{:S(2)}) collective-permute-start(bf16[8,8192]{1,0:T(8,128)(2,1)} %refs_0_.1), channel_id=1, source_target_pairs={{0,24},{4,28},{8,16},{12,20},{16,8},{20,12},{24,0},{28,4},{1,25},{... | collective-permute-start | bytes 393224 | tf_op jit(solution)/shard_map/ppermute | solution.py:260
  3.9 0.0 collective-permute-start.1
  3.9 2.4 %shard_map.73 = (bf16[8,8320]{1,0:T(8,128)(2,1)S(1)}, bf16[8,8320]{1,0:T(8,128)(2,1)S(1)}, f32[8,256]{1,0:T(8,128)S(1)}, f32[2,64,64]{2,1,0:T(8,128)S(1)}, f32[2...) custom-call(bf16[8,8192]{1,0:T(8,128)(2,1)} %refs_0_.1, f32[2,64,64]{2,1,0:T(8,128)} %refs_1_.1, ...), custom_call_target="tpu_custom_call" | custom-call | tf_op jit(solution)/shard_map/pallas_call | solution.py:283
  6.4 2.0 %collective-permute-start.3 = (bf16[8,8320]{1,0:T(8,128)(2,1)S(1)}, bf16[8,8320]{1,0:T(8,128)(2,1)S(1)}, u32[]{:S(2)}, u32[]{:S(2)}) collective-permute-start(bf16[8,8320]{1,0:T(8,128)(2,1)S(1)} %get-tuple-element.29.refs_7_), channel_id=1, source_target_pairs={{0,16},{4,20},{8,24},{12,28},{16,0},{20,4},{24,8},{28,12},{1,17},{... | collective-permute-start | bytes 399368 | tf_op jit(solution)/shard_map/ppermute | solution.py:260
  8.4 1.5 %collective-permute-start.5 = (bf16[8,8320]{1,0:T(8,128)(2,1)S(1)}, bf16[8,8320]{1,0:T(8,128)(2,1)S(1)}, u32[]{:S(2)}, u32[]{:S(2)}) collective-permute-start(bf16[8,8320]{1,0:T(8,128)(2,1)S(1)} %get-tuple-element.29.refs_7_), channel_id=1, source_target_pairs={{0,8},{4,12},{8,0},{12,4},{16,24},{20,28},{24,16},{28,20},{1,9},{5... | collective-permute-start | bytes 399368 | tf_op jit(solution)/shard_map/ppermute | solution.py:260
  10.5 1.1 %shard_map.74 = (bf16[8,8320]{1,0:T(8,128)(2,1)S(1)}, bf16[8192,256]{1,0:T(8,128)(2,1)S(1)}, f32[8,256]{1,0:T(8,128)S(1)}) custom-call(s32[1]{0:T(128)S(6)} %copy.10.count_ref, f32[8,256]{1,0:T(8,128)S(1)} %get-tuple-element.22.found_ref, bf16[8,8320]{1,0:T(8,128)(2,1)S(1)} %get-tuple-element.23.block_ref, ...), custom_call_target="tpu_custom_call", output_to_operand_aliasing={{0}: (2, {})} | custom-call | bytes 4194304 | tf_op jit(solution)/shard_map/pallas_call | solution.py:301
  11.7 0.1 collective-permute-start.7
  11.8 0.0 collective-permute-done.1.cand_ref
  11.8 0.0 collective-permute-done.query_ref
  11.8 1.2 %shard_map.75.refs_1_ = bf16[8,8320]{1,0:T(8,128)(2,1)S(1)} custom-call(bf16[8,8192]{1,0:T(8,128)(2,1)S(1)} %collective-permute-done.query_ref, s32[1,256]{1,0:T(1,128)S(1)} %collective-permute-done.1.cand_ref, f32[2,64,64]{2,1,0:T(8,128)S(1)} %get-tuple-element.26.in_factor_ref, f32[2,64,64]{2,1,0:T(8,128)S(1)} %get-tuple-element.27.out_factor_ref, ...), custom_call_target="tpu_custom_call" | custom-call | flops 5000000000 | bytes 532480 | tf_op jit(solution)/shard_map/pallas_call | solution.py:319
  13.0 0.5 %collective-permute-start.2 = (bf16[8,8320]{1,0:T(8,128)(2,1)S(1)}, bf16[8,8320]{1,0:T(8,128)(2,1)S(1)}, u32[]{:S(2)}, u32[]{:S(2)}) collective-permute-start(bf16[8,8320]{1,0:T(8,128)(2,1)S(1)} %shard_map.75.refs_1_), channel_id=1, source_target_pairs={{0,4},{4,0},{8,12},{12,8},{16,20},{20,16},{24,28},{28,24},{1,5},{5... | collective-permute-start | bytes 399368 | tf_op jit(solution)/shard_map/ppermute | solution.py:260
  13.5 0.0 collective-permute-done.3.refs_3_
  13.5 0.1 collective-permute-start.4
  13.5 0.0 collective-permute-done.5.refs_5_
  13.5 0.5 %collective-permute-start.6 = (bf16[8,8320]{1,0:T(8,128)(2,1)S(1)}, bf16[8,8320]{1,0:T(8,128)(2,1)S(1)}, u32[]{:S(2)}, u32[]{:S(2)}) collective-permute-start(bf16[8,8320]{1,0:T(8,128)(2,1)S(1)} %collective-permute-done.5.refs_5_), channel_id=1, source_target_pairs={{0,4},{4,0},{8,12},{12,8},{16,20},{20,16},{24,28},{28,24},{1,5},{5... | collective-permute-start | bytes 399368 | tf_op jit(solution)/shard_map/ppermute | solution.py:260
  14.0 0.0 collective-permute-done.7.refs_6_
  14.0 0.5 %collective-permute-done.2.refs_0_ = bf16[8,8320]{1,0:T(8,128)(2,1)S(1)} collective-permute-done((bf16[8,8320]{1,0:T(8,128)(2,1)S(1)}, bf16[8,8320]{1,0:T(8,128)(2,1)S(1)}, u32[]{:S(2)}, u32[]{:S(2)}) %collective-permute-start.2) | collective-permute-done | bytes 133152 | tf_op jit(solution)/shard_map/ppermute | solution.py:260
  14.4 0.4 %collective-permute-done.4.refs_2_ = bf16[8,8320]{1,0:T(8,128)(2,1)S(1)} collective-permute-done((bf16[8,8320]{1,0:T(8,128)(2,1)S(1)}, bf16[8,8320]{1,0:T(8,128)(2,1)S(1)}, u32[]{:S(2)}, u32[]{:S(2)}) %collective-permute-start.4) | collective-permute-done | bytes 133152 | tf_op jit(solution)/shard_map/ppermute | solution.py:260
  14.8 0.2 collective-permute-done.6.refs_4_
  15.0 1.2 %shard_map.76 = (f32[4,16,128]{2,1,0:T(8,128)S(1)}, f32[64,256]{1,0:T(8,128)S(1)}, f32[1,128]{1,0:T(1,128)S(1)}) custom-call(bf16[8,8320]{1,0:T(8,128)(2,1)S(1)} %collective-permute-done.2.refs_0_, bf16[8,8320]{1,0:T(8,128)(2,1)S(1)} %shard_map.75.refs_1_, bf16[8,8320]{1,0:T(8,128)(2,1)S(1)} %collective-permute-done.4.refs_2_, ...), custom_call_target="tpu_custom_call" | custom-call | tf_op jit(solution)/shard_map/pallas_call | solution.py:335
  16.2 0.4 %collective-permute-start.8 = (f32[4,16,128]{2,1,0:T(8,128)S(1)}, f32[4,16,128]{2,1,0:T(8,128)S(1)}, u32[]{:S(2)}, u32[]{:S(2)}) collective-permute-start(f32[4,16,128]{2,1,0:T(8,128)S(1)} %get-tuple-element.34), channel_id=1, source_target_pairs={{0,4},{4,0},{8,12},{12,8},{16,20},{20,16},{24,28},{28,24},{1,5},{5... | collective-permute-start | bytes 98312 | tf_op jit(solution)/shard_map/ppermute | solution.py:260
  16.5 0.3 shard_map.77
  16.9 0.6 %collective-permute-done.8 = f32[4,16,128]{2,1,0:T(8,128)S(1)} collective-permute-done((f32[4,16,128]{2,1,0:T(8,128)S(1)}, f32[4,16,128]{2,1,0:T(8,128)S(1)}, u32[]{:S(2)}, u32[]{:S(2)}) %collective-permute-start.8) | collective-permute-done | bytes 32800 | tf_op jit(solution)/shard_map/ppermute | solution.py:260
  17.4 1.0 %collective-permute-start.11 = (f32[2,16,128]{2,1,0:T(8,128)S(1)}, f32[2,16,128]{2,1,0:T(8,128)S(1)}, u32[]{:S(2)}, u32[]{:S(2)}) collective-permute-start(f32[2,16,128]{2,1,0:T(8,128)S(1)} %pad_maximum_fusion.2), channel_id=1, source_target_pairs={{0,12},{4,8},{8,20},{12,16},{16,28},{20,24},{24,4},{28,0},{1,13},{... | collective-permute-start | bytes 49160 | tf_op jit(solution)/shard_map/ppermute | solution.py:361
  18.4 0.5 %collective-permute-start.10 = (f32[2,16,128]{2,1,0:T(8,128)S(1)}, f32[2,16,128]{2,1,0:T(8,128)S(1)}, u32[]{:S(2)}, u32[]{:S(2)}) collective-permute-start(f32[2,16,128]{2,1,0:T(8,128)S(1)} %pad_maximum_fusion.1), channel_id=1, source_target_pairs={{0,20},{4,16},{8,28},{12,24},{16,4},{20,0},{24,12},{28,8},{1,21},{... | collective-permute-start | bytes 49160 | tf_op jit(solution)/shard_map/ppermute | solution.py:361
  18.9 1.6 %collective-permute-start.9 = (f32[2,16,128]{2,1,0:T(8,128)S(1)}, f32[2,16,128]{2,1,0:T(8,128)S(1)}, u32[]{:S(2)}, u32[]{:S(2)}) collective-permute-start(f32[2,16,128]{2,1,0:T(8,128)S(1)} %pad_maximum_fusion), channel_id=1, source_target_pairs={{0,28},{4,24},{8,4},{12,0},{16,12},{20,8},{24,20},{28,16},{1,29},{... | collective-permute-start | bytes 49160 | tf_op jit(solution)/shard_map/ppermute | solution.py:361
  20.5 1.0 %collective-permute-done.11.refs_2_ = f32[2,16,128]{2,1,0:T(8,128)S(1)} collective-permute-done((f32[2,16,128]{2,1,0:T(8,128)S(1)}, f32[2,16,128]{2,1,0:T(8,128)S(1)}, u32[]{:S(2)}, u32[]{:S(2)}) %collective-permute-start.11) | collective-permute-done | bytes 16416 | tf_op jit(solution)/shard_map/ppermute | solution.py:361
  21.5 0.2 collective-permute-done.10.refs_1_
  21.7 0.4 %collective-permute-done.9.refs_0_ = f32[2,16,128]{2,1,0:T(8,128)S(1)} collective-permute-done((f32[2,16,128]{2,1,0:T(8,128)S(1)}, f32[2,16,128]{2,1,0:T(8,128)S(1)}, u32[]{:S(2)}, u32[]{:S(2)}) %collective-permute-start.9) | collective-permute-done | bytes 16416 | tf_op jit(solution)/shard_map/ppermute | solution.py:361
  22.1 0.4 %shard_map.78 = (f32[32,128]{1,0:T(8,128)S(1)}, f32[32,128]{1,0:T(8,128)S(1)}, f32[32,128]{1,0:T(8,128)S(1)}, f32[32,128]{1,0:T(8,128)S(1)}) custom-call(f32[8,256]{1,0:T(8,128)S(1)} %get-tuple-element.25.found_ref, f32[2,16,128]{2,1,0:T(8,128)S(1)} %collective-permute-done.9.refs_0_, f32[2,16,128]{2,1,0:T(8,128)S(1)} %collective-permute-done.10.refs_1_, ...), custom_call_target="tpu_custom_call" | custom-call | tf_op jit(solution)/shard_map/pallas_call | solution.py:363
  22.5 1.6 %collective-permute-start.12 = (f32[32,128]{1,0:T(8,128)S(1)}, f32[32,128]{1,0:T(8,128)S(1)}, u32[]{:S(2)}, u32[]{:S(2)}) collective-permute-start(f32[32,128]{1,0:T(8,128)S(1)} %get-tuple-element.36), channel_id=1, source_target_pairs={{0,1},{1,2},{2,3},{3,0},{4,5},{5,6},{6,7},{7,4},{8,9},{9,10},{10,1... | collective-permute-start | bytes 49160 | tf_op jit(solution)/shard_map/ppermute | solution.py:372
  24.1 2.6 %collective-permute-start.13 = (f32[32,128]{1,0:T(8,128)S(1)}, f32[32,128]{1,0:T(8,128)S(1)}, u32[]{:S(2)}, u32[]{:S(2)}) collective-permute-start(f32[32,128]{1,0:T(8,128)S(1)} %get-tuple-element.37), channel_id=1, source_target_pairs={{0,2},{1,3},{2,0},{3,1},{4,6},{5,7},{6,4},{7,5},{8,10},{9,11},{10,... | collective-permute-start | bytes 49160 | tf_op jit(solution)/shard_map/ppermute | solution.py:372
  26.7 1.3 %collective-permute-start.14 = (f32[32,128]{1,0:T(8,128)S(1)}, f32[32,128]{1,0:T(8,128)S(1)}, u32[]{:S(2)}, u32[]{:S(2)}) collective-permute-start(f32[32,128]{1,0:T(8,128)S(1)} %get-tuple-element.38), channel_id=1, source_target_pairs={{0,3},{1,0},{2,1},{3,2},{4,7},{5,4},{6,5},{7,6},{8,11},{9,8},{10,9... | collective-permute-start | bytes 49160 | tf_op jit(solution)/shard_map/ppermute | solution.py:372
  28.1 0.0 collective-permute-done.12
  28.1 0.9 %collective-permute-done.13 = f32[32,128]{1,0:T(8,128)S(1)} collective-permute-done((f32[32,128]{1,0:T(8,128)S(1)}, f32[32,128]{1,0:T(8,128)S(1)}, u32[]{:S(2)}, u32[]{:S(2)}) %collective-permute-start.13) | collective-permute-done | bytes 16416 | tf_op jit(solution)/shard_map/ppermute | solution.py:372
  29.0 1.4 %collective-permute-done.14 = f32[32,128]{1,0:T(8,128)S(1)} collective-permute-done((f32[32,128]{1,0:T(8,128)S(1)}, f32[32,128]{1,0:T(8,128)S(1)}, u32[]{:S(2)}, u32[]{:S(2)}) %collective-permute-start.14) | collective-permute-done | bytes 16416 | tf_op jit(solution)/shard_map/ppermute | solution.py:372
  30.5 0.1 fusion.2
  30.5 0.6 %maximum_bitcast_fusion = f32[1,64,64]{2,1,0:T(8,128)} fusion(f32[32,64]{1,0:T(8,128)S(1)} %get-tuple-element.48, f32[32,64]{1,0:T(8,128)S(1)} %get-tuple-element.47), kind=kLoop, calls=%fused_computation | loop fusion | flops 4096 | bytes 32768 | tf_op jit(solution)/shard_map/broadcast_in_dim | solution.py:373
  (7 shorter events, 0.1 us)
Async XLA Ops:
  0.0 11.8 %collective-permute-start = (bf16[8,8192]{1,0:T(8,128)(2,1)}, bf16[8,8192]{1,0:T(8,128)(2,1)S(1)}, u32[]{:S(2)}, u32[]{:S(2)}) collective-permute-start(bf16[8,8192]{1,0:T(8,128)(2,1)} %refs_0_.1), channel_id=1, source_target_pairs={{0,24},{4,28},{8,16},{12,20},{16,8},{20,12},{24,0},{28,4},{1,25},{... | collective-permute-start | bytes 393224 | tf_op jit(solution)/shard_map/ppermute | solution.py:260
  3.9 7.9 %collective-permute-start.1 = (s32[1,256]{1,0:T(1,128)}, s32[1,256]{1,0:T(1,128)S(1)}, u32[]{:S(2)}, u32[]{:S(2)}) collective-permute-start(s32[1,256]{1,0:T(1,128)} %refs_4_.1), channel_id=1, source_target_pairs={{0,24},{4,28},{8,16},{12,20},{16,8},{20,12},{24,0},{28,4},{1,25},{... | collective-permute-start | bytes 3080 | tf_op jit(solution)/shard_map/ppermute | solution.py:260
  6.4 7.1 %collective-permute-start.3 = (bf16[8,8320]{1,0:T(8,128)(2,1)S(1)}, bf16[8,8320]{1,0:T(8,128)(2,1)S(1)}, u32[]{:S(2)}, u32[]{:S(2)}) collective-permute-start(bf16[8,8320]{1,0:T(8,128)(2,1)S(1)} %get-tuple-element.29.refs_7_), channel_id=1, source_target_pairs={{0,16},{4,20},{8,24},{12,28},{16,0},{20,4},{24,8},{28,12},{1,17},{... | collective-permute-start | bytes 399368 | tf_op jit(solution)/shard_map/ppermute | solution.py:260
  8.4 5.1 %collective-permute-start.5 = (bf16[8,8320]{1,0:T(8,128)(2,1)S(1)}, bf16[8,8320]{1,0:T(8,128)(2,1)S(1)}, u32[]{:S(2)}, u32[]{:S(2)}) collective-permute-start(bf16[8,8320]{1,0:T(8,128)(2,1)S(1)} %get-tuple-element.29.refs_7_), channel_id=1, source_target_pairs={{0,8},{4,12},{8,0},{12,4},{16,24},{20,28},{24,16},{28,20},{1,9},{5... | collective-permute-start | bytes 399368 | tf_op jit(solution)/shard_map/ppermute | solution.py:260
  11.7 2.3 %collective-permute-start.7 = (bf16[8,8320]{1,0:T(8,128)(2,1)S(1)}, bf16[8,8320]{1,0:T(8,128)(2,1)S(1)}, u32[]{:S(2)}, u32[]{:S(2)}) collective-permute-start(bf16[8,8320]{1,0:T(8,128)(2,1)S(1)} %get-tuple-element.30), channel_id=1, source_target_pairs={{0,4},{4,0},{8,12},{12,8},{16,20},{20,16},{24,28},{28,24},{1,5},{5... | collective-permute-start | bytes 399368 | tf_op jit(solution)/shard_map/ppermute | solution.py:260
  13.0 1.5 %collective-permute-start.2 = (bf16[8,8320]{1,0:T(8,128)(2,1)S(1)}, bf16[8,8320]{1,0:T(8,128)(2,1)S(1)}, u32[]{:S(2)}, u32[]{:S(2)}) collective-permute-start(bf16[8,8320]{1,0:T(8,128)(2,1)S(1)} %shard_map.75.refs_1_), channel_id=1, source_target_pairs={{0,4},{4,0},{8,12},{12,8},{16,20},{20,16},{24,28},{28,24},{1,5},{5... | collective-permute-start | bytes 399368 | tf_op jit(solution)/shard_map/ppermute | solution.py:260
  13.5 1.4 %collective-permute-start.4 = (bf16[8,8320]{1,0:T(8,128)(2,1)S(1)}, bf16[8,8320]{1,0:T(8,128)(2,1)S(1)}, u32[]{:S(2)}, u32[]{:S(2)}) collective-permute-start(bf16[8,8320]{1,0:T(8,128)(2,1)S(1)} %collective-permute-done.3.refs_3_), channel_id=1, source_target_pairs={{0,4},{4,0},{8,12},{12,8},{16,20},{20,16},{24,28},{28,24},{1,5},{5... | collective-permute-start | bytes 399368 | tf_op jit(solution)/shard_map/ppermute | solution.py:260
  13.5 1.5 %collective-permute-start.6 = (bf16[8,8320]{1,0:T(8,128)(2,1)S(1)}, bf16[8,8320]{1,0:T(8,128)(2,1)S(1)}, u32[]{:S(2)}, u32[]{:S(2)}) collective-permute-start(bf16[8,8320]{1,0:T(8,128)(2,1)S(1)} %collective-permute-done.5.refs_5_), channel_id=1, source_target_pairs={{0,4},{4,0},{8,12},{12,8},{16,20},{20,16},{24,28},{28,24},{1,5},{5... | collective-permute-start | bytes 399368 | tf_op jit(solution)/shard_map/ppermute | solution.py:260
  16.2 1.3 %collective-permute-start.8 = (f32[4,16,128]{2,1,0:T(8,128)S(1)}, f32[4,16,128]{2,1,0:T(8,128)S(1)}, u32[]{:S(2)}, u32[]{:S(2)}) collective-permute-start(f32[4,16,128]{2,1,0:T(8,128)S(1)} %get-tuple-element.34), channel_id=1, source_target_pairs={{0,4},{4,0},{8,12},{12,8},{16,20},{20,16},{24,28},{28,24},{1,5},{5... | collective-permute-start | bytes 98312 | tf_op jit(solution)/shard_map/ppermute | solution.py:260
  17.4 4.1 %collective-permute-start.11 = (f32[2,16,128]{2,1,0:T(8,128)S(1)}, f32[2,16,128]{2,1,0:T(8,128)S(1)}, u32[]{:S(2)}, u32[]{:S(2)}) collective-permute-start(f32[2,16,128]{2,1,0:T(8,128)S(1)} %pad_maximum_fusion.2), channel_id=1, source_target_pairs={{0,12},{4,8},{8,20},{12,16},{16,28},{20,24},{24,4},{28,0},{1,13},{... | collective-permute-start | bytes 49160 | tf_op jit(solution)/shard_map/ppermute | solution.py:361
  18.4 3.2 %collective-permute-start.10 = (f32[2,16,128]{2,1,0:T(8,128)S(1)}, f32[2,16,128]{2,1,0:T(8,128)S(1)}, u32[]{:S(2)}, u32[]{:S(2)}) collective-permute-start(f32[2,16,128]{2,1,0:T(8,128)S(1)} %pad_maximum_fusion.1), channel_id=1, source_target_pairs={{0,20},{4,16},{8,28},{12,24},{16,4},{20,0},{24,12},{28,8},{1,21},{... | collective-permute-start | bytes 49160 | tf_op jit(solution)/shard_map/ppermute | solution.py:361
  18.9 3.2 %collective-permute-start.9 = (f32[2,16,128]{2,1,0:T(8,128)S(1)}, f32[2,16,128]{2,1,0:T(8,128)S(1)}, u32[]{:S(2)}, u32[]{:S(2)}) collective-permute-start(f32[2,16,128]{2,1,0:T(8,128)S(1)} %pad_maximum_fusion), channel_id=1, source_target_pairs={{0,28},{4,24},{8,4},{12,0},{16,12},{20,8},{24,20},{28,16},{1,29},{... | collective-permute-start | bytes 49160 | tf_op jit(solution)/shard_map/ppermute | solution.py:361
  22.5 5.6 %collective-permute-start.12 = (f32[32,128]{1,0:T(8,128)S(1)}, f32[32,128]{1,0:T(8,128)S(1)}, u32[]{:S(2)}, u32[]{:S(2)}) collective-permute-start(f32[32,128]{1,0:T(8,128)S(1)} %get-tuple-element.36), channel_id=1, source_target_pairs={{0,1},{1,2},{2,3},{3,0},{4,5},{5,6},{6,7},{7,4},{8,9},{9,10},{10,1... | collective-permute-start | bytes 49160 | tf_op jit(solution)/shard_map/ppermute | solution.py:372
  24.1 4.9 %collective-permute-start.13 = (f32[32,128]{1,0:T(8,128)S(1)}, f32[32,128]{1,0:T(8,128)S(1)}, u32[]{:S(2)}, u32[]{:S(2)}) collective-permute-start(f32[32,128]{1,0:T(8,128)S(1)} %get-tuple-element.37), channel_id=1, source_target_pairs={{0,2},{1,3},{2,0},{3,1},{4,6},{5,7},{6,4},{7,5},{8,10},{9,11},{10,... | collective-permute-start | bytes 49160 | tf_op jit(solution)/shard_map/ppermute | solution.py:372
  26.7 3.7 %collective-permute-start.14 = (f32[32,128]{1,0:T(8,128)S(1)}, f32[32,128]{1,0:T(8,128)S(1)}, u32[]{:S(2)}, u32[]{:S(2)}) collective-permute-start(f32[32,128]{1,0:T(8,128)S(1)} %get-tuple-element.38), channel_id=1, source_target_pairs={{0,3},{1,0},{2,1},{3,2},{4,7},{5,4},{6,5},{7,6},{8,11},{9,8},{10,9... | collective-permute-start | bytes 49160 | tf_op jit(solution)/shard_map/ppermute | solution.py:372

commit v27 on v26

--- a/solution.py
+++ b/solution.py
@@ -156,10 +156,7 @@
     packed_ref[:, width:] = look_up(holders, capacity, per_holder, rows, cand_ref, home_ref)[0]
 
 
-def load_kernel(holders, count_ref, found_ref, block_ref, source_ref, same_block_ref, target_ref, used_ref):
-    used_ref[...] = found_ref[...]
-    slots = found_ref.shape[1]
-    used_ref[0:1] = jnp.where(iota((1, slots), 1) < count_ref[0], found_ref[0:1], float(holders))
+def load_kernel(block_ref, source_ref, same_block_ref, target_ref):
     step = source_ref.shape[1] // LOADS
     for i in range(LOADS):
         target_ref[i * step:(i + 1) * step, :] = source_ref[:, i * step:(i + 1) * step].T
@@ -223,7 +220,7 @@
         keep_ref[place] = picked[place * half:(place + 1) * half]
 
 
-def spread_kernel(holders, groups, found_ref, *refs):
+def spread_kernel(holders, groups, count_ref, found_ref, *refs):
     landed_refs, out_refs = refs[:holders // 2][::-1], refs[holders // 2:]
     half = landed_refs[0].shape[1]
     slots = found_ref.shape[1]
@@ -236,7 +233,8 @@
     step = (me // 2 - holder // 2 + 2 * chips) % chips
     same_core = (holder % 2 == me % 2).astype(jnp.int32)
     place = 2 * step + jnp.where(step == 0, 1 - same_core, same_core)
-    begins = jnp.where(holder < holders, place * half, -1).astype(jnp.float32)
+    used = iota((1, slots), 1) < count_ref[0]
+    begins = jnp.where(used, place * half, -1).astype(jnp.float32)
     rank_there = found_ref[1:2]
     place = iota((2 * holders * half, slots), 0).astype(jnp.float32)
     upper = rank_there >= half
@@ -298,19 +296,15 @@
         compiler_params=pltpu.CompilerParams(vmem_limit_bytes=14 * 2**20 + 24 * slots * slots),
     )(*sources)
 
-    again, pages, used = pl.pallas_call(
-        functools.partial(load_kernel, holders),
-        out_shape=[
-            jax.ShapeDtypeStruct(again.shape, bf16),
-            pltpu.VMEM((width, per_holder), bf16),
-            jax.ShapeDtypeStruct(found.shape, jnp.float32),
-        ],
-        in_specs=[SMEM, VMEM, VMEM, VMEM],
-        out_specs=[VMEM] * 3,
-        input_output_aliases={2: 0},
+    again, pages = pl.pallas_call(
+        load_kernel,
+        out_shape=[jax.ShapeDtypeStruct(again.shape, bf16), pltpu.VMEM((width, per_holder), bf16)],
+        in_specs=[VMEM] * 2,
+        out_specs=[VMEM] * 2,
+        input_output_aliases={0: 0},
         compiler_params=pltpu.CompilerParams(vmem_limit_bytes=4 * 2**20 + 4 * per_holder * width),
         cost_estimate=pl.CostEstimate(flops=0, bytes_accessed=2 * page_store.size, transcendentals=0),
-    )(counts, found, again, pltpu.with_memory_space_constraint(pages, pltpu.VMEM))
+    )(again, pltpu.with_memory_space_constraint(pages, pltpu.VMEM))
 
     blocks = [None] * holders
     blocks[0] = packed
@@ -363,10 +357,10 @@
     terms = pl.pallas_call(
         functools.partial(spread_kernel, holders, groups),
         out_shape=[jax.ShapeDtypeStruct((share // 2, 2 * total), jnp.float32)] * groups,
-        in_specs=[VMEM] * (1 + len(landed)),
+        in_specs=[SMEM] + [VMEM] * (1 + len(landed)),
         out_specs=[VMEM] * groups,
         compiler_params=pltpu.CompilerParams(vmem_limit_bytes=4 * 2**20 + 64 * total * slots),
-    )(used, *landed[::-1])
+    )(counts, found, *landed[::-1])
     summed = terms[0]
     for step in range(1, groups):
         summed = summed + lax.ppermute(terms[step], "layer", [(g, (g + step) % groups) for g in range(groups)])

time: 31.3 us -> 31.3 us (level)
  waiting for transfers between devices: 5.54 us -> 6.47 us
  starting transfers between devices: 17.5 us -> 16.6 us
    ppermute x9, starting transfers between devices: 8.9 us -> 8.26 us  [swap(): lax.ppermute(value, axis, [(i, i ^ distance) for i in range(lax.axis_size...]
    ppermute x3, waiting for transfers between devices: 1.53 us -> 2.11 us  [on_device(): landed.append(lax.ppermute(pair, 'store', to) if step else pair)]
    ppermute x9, waiting for transfers between devices: 1.61 us -> 1.96 us  [swap(): lax.ppermute(value, axis, [(i, i ^ distance) for i in range(lax.axis_size...]
where the time goes in v27:
time: 31.3 us; the launch traced here: 31.2 us
  starting transfers between devices  16.6 us (53%)
  Pallas kernels  6.63 us (21%)
  waiting for transfers between devices  6.47 us (21%)
  between operations  0.74 us (2%)
  other arithmetic  0.64 us (2%)
    ppermute x9, starting transfers between devices, swap(): lax.ppermute(value, axis, [(i, i ^ distance) for i in range(lax.axis_size...  8.26 us
    ppermute x3, starting transfers between devices, on_device(): lax.ppermute(terms[step], 'layer', [(g, (g + step) % groups) for g in ran...  5.56 us
    ppermute x3, starting transfers between devices, on_device(): landed.append(lax.ppermute(pair, 'store', to) if step else pair)  2.77 us
    pallas_call x1, Pallas kernels, on_device(): pl.pallas_call(functools.partial(condition_kernel, holders, capacity, per...  2.43 us
    ppermute x3, waiting for transfers between devices, on_device(): lax.ppermute(terms[step], 'layer', [(g, (g + step) % groups) for g in ran...  2.39 us
    ppermute x3, waiting for transfers between devices, on_device(): landed.append(lax.ppermute(pair, 'store', to) if step else pair)  2.11 us
    ppermute x9, waiting for transfers between devices, swap(): lax.ppermute(value, axis, [(i, i ^ distance) for i in range(lax.axis_size...  1.96 us
    pallas_call x1, Pallas kernels, on_device(): pl.pallas_call(functools.partial(late_kernel, holders, capacity, per_hold...  1.19 us
  transfers between devices with their start and end apart: 15, of which 9 were waited for; matrix products, arithmetic and copies ran while one was open for 0% of the time, Pallas kernels for 16%

profile of v27, /device:TPU:0, one launch (start us, length us, event | category | flops | bytes accessed | tf_op | source)
XLA Modules:
  0.0 31.2 jit_solution(12731311817601770059)
XLA Ops:
  0.0 3.9 %collective-permute-start = (bf16[8,8192]{1,0:T(8,128)(2,1)}, bf16[8,8192]{1,0:T(8,128)(2,1)S(1)}, u32[]{:S(2)}, u32[]{:S(2)}) collective-permute-start(bf16[8,8192]{1,0:T(8,128)(2,1)} %refs_0_.1), channel_id=1, source_target_pairs={{0,24},{4,28},{8,16},{12,20},{16,8},{20,12},{24,0},{28,4},{1,25},{... | collective-permute-start | bytes 393224 | tf_op jit(solution)/shard_map/ppermute | solution.py:258
  3.9 0.0 collective-permute-start.1
  3.9 2.4 %shard_map.73 = (bf16[8,8320]{1,0:T(8,128)(2,1)S(1)}, bf16[8,8320]{1,0:T(8,128)(2,1)S(1)}, f32[8,256]{1,0:T(8,128)S(1)}, f32[2,64,64]{2,1,0:T(8,128)S(1)}, f32[2...) custom-call(bf16[8,8192]{1,0:T(8,128)(2,1)} %refs_0_.1, f32[2,64,64]{2,1,0:T(8,128)} %refs_1_.1, ...), custom_call_target="tpu_custom_call" | custom-call | tf_op jit(solution)/shard_map/pallas_call | solution.py:281
  6.4 2.0 %collective-permute-start.3 = (bf16[8,8320]{1,0:T(8,128)(2,1)S(1)}, bf16[8,8320]{1,0:T(8,128)(2,1)S(1)}, u32[]{:S(2)}, u32[]{:S(2)}) collective-permute-start(bf16[8,8320]{1,0:T(8,128)(2,1)S(1)} %get-tuple-element.25.refs_7_), channel_id=1, source_target_pairs={{0,16},{4,20},{8,24},{12,28},{16,0},{20,4},{24,8},{28,12},{1,17},{... | collective-permute-start | bytes 399368 | tf_op jit(solution)/shard_map/ppermute | solution.py:258
  8.4 1.5 %collective-permute-start.5 = (bf16[8,8320]{1,0:T(8,128)(2,1)S(1)}, bf16[8,8320]{1,0:T(8,128)(2,1)S(1)}, u32[]{:S(2)}, u32[]{:S(2)}) collective-permute-start(bf16[8,8320]{1,0:T(8,128)(2,1)S(1)} %get-tuple-element.25.refs_7_), channel_id=1, source_target_pairs={{0,8},{4,12},{8,0},{12,4},{16,24},{20,28},{24,16},{28,20},{1,9},{5... | collective-permute-start | bytes 399368 | tf_op jit(solution)/shard_map/ppermute | solution.py:258
  9.9 1.1 %shard_map.75 = (bf16[8,8320]{1,0:T(8,128)(2,1)S(1)}, bf16[8192,256]{1,0:T(8,128)(2,1)S(1)}) custom-call(bf16[8,8320]{1,0:T(8,128)(2,1)S(1)} %get-tuple-element.26.block_ref, bf16[256,8192]{1,0:T(8,128)(2,1)S(1)} %get-tuple-element.27.source_ref), custom_call_target="tpu_custom_call", output_to_operand_aliasing={{0}: (0, {})} | custom-call | bytes 4194304 | tf_op jit(solution)/shard_map/pallas_call | solution.py:299
  11.0 0.1 collective-permute-start.7
  11.1 0.0 collective-permute-done.1.cand_ref
  11.1 0.0 collective-permute-done.query_ref
  11.1 1.2 %shard_map.74.refs_1_ = bf16[8,8320]{1,0:T(8,128)(2,1)S(1)} custom-call(bf16[8,8192]{1,0:T(8,128)(2,1)S(1)} %collective-permute-done.query_ref, s32[1,256]{1,0:T(1,128)S(1)} %collective-permute-done.1.cand_ref, f32[2,64,64]{2,1,0:T(8,128)S(1)} %get-tuple-element.22.in_factor_ref, f32[2,64,64]{2,1,0:T(8,128)S(1)} %get-tuple-element.23.out_factor_ref, ...), custom_call_target="tpu_custom_call" | custom-call | flops 5000000000 | bytes 532480 | tf_op jit(solution)/shard_map/pallas_call | solution.py:313
  12.3 0.5 %collective-permute-start.2 = (bf16[8,8320]{1,0:T(8,128)(2,1)S(1)}, bf16[8,8320]{1,0:T(8,128)(2,1)S(1)}, u32[]{:S(2)}, u32[]{:S(2)}) collective-permute-start(bf16[8,8320]{1,0:T(8,128)(2,1)S(1)} %shard_map.74.refs_1_), channel_id=1, source_target_pairs={{0,4},{4,0},{8,12},{12,8},{16,20},{20,16},{24,28},{28,24},{1,5},{5... | collective-permute-start | bytes 399368 | tf_op jit(solution)/shard_map/ppermute | solution.py:258
  12.8 0.0 collective-permute-done.3.refs_3_
  12.8 0.1 collective-permute-start.4
  12.9 0.5 %collective-permute-done.5.refs_5_ = bf16[8,8320]{1,0:T(8,128)(2,1)S(1)} collective-permute-done((bf16[8,8320]{1,0:T(8,128)(2,1)S(1)}, bf16[8,8320]{1,0:T(8,128)(2,1)S(1)}, u32[]{:S(2)}, u32[]{:S(2)}) %collective-permute-start.5) | collective-permute-done | bytes 133152 | tf_op jit(solution)/shard_map/ppermute | solution.py:258
  13.4 0.0 collective-permute-start.6
  14.0 0.0 collective-permute-done.7.refs_6_
  14.1 0.0 collective-permute-done.2.refs_0_
  14.1 0.1 collective-permute-done.4.refs_2_
  14.2 0.6 %collective-permute-done.6.refs_4_ = bf16[8,8320]{1,0:T(8,128)(2,1)S(1)} collective-permute-done((bf16[8,8320]{1,0:T(8,128)(2,1)S(1)}, bf16[8,8320]{1,0:T(8,128)(2,1)S(1)}, u32[]{:S(2)}, u32[]{:S(2)}) %collective-permute-start.6) | collective-permute-done | bytes 133152 | tf_op jit(solution)/shard_map/ppermute | solution.py:258
  14.7 1.2 %shard_map.76 = (f32[4,16,128]{2,1,0:T(8,128)S(1)}, f32[64,256]{1,0:T(8,128)S(1)}, f32[1,128]{1,0:T(1,128)S(1)}) custom-call(bf16[8,8320]{1,0:T(8,128)(2,1)S(1)} %collective-permute-done.2.refs_0_, bf16[8,8320]{1,0:T(8,128)(2,1)S(1)} %shard_map.74.refs_1_, bf16[8,8320]{1,0:T(8,128)(2,1)S(1)} %collective-permute-done.4.refs_2_, ...), custom_call_target="tpu_custom_call" | custom-call | tf_op jit(solution)/shard_map/pallas_call | solution.py:329
  15.9 0.2 collective-permute-start.8
  16.1 0.3 shard_map.77
  16.4 0.8 %collective-permute-done.8 = f32[4,16,128]{2,1,0:T(8,128)S(1)} collective-permute-done((f32[4,16,128]{2,1,0:T(8,128)S(1)}, f32[4,16,128]{2,1,0:T(8,128)S(1)}, u32[]{:S(2)}, u32[]{:S(2)}) %collective-permute-start.8) | collective-permute-done | bytes 32800 | tf_op jit(solution)/shard_map/ppermute | solution.py:258
  17.2 1.3 %collective-permute-start.11 = (f32[2,16,128]{2,1,0:T(8,128)S(1)}, f32[2,16,128]{2,1,0:T(8,128)S(1)}, u32[]{:S(2)}, u32[]{:S(2)}) collective-permute-start(f32[2,16,128]{2,1,0:T(8,128)S(1)} %pad_maximum_fusion.2), channel_id=1, source_target_pairs={{0,12},{4,8},{8,20},{12,16},{16,28},{20,24},{24,4},{28,0},{1,13},{... | collective-permute-start | bytes 49160 | tf_op jit(solution)/shard_map/ppermute | solution.py:355
  18.4 0.5 %collective-permute-start.10 = (f32[2,16,128]{2,1,0:T(8,128)S(1)}, f32[2,16,128]{2,1,0:T(8,128)S(1)}, u32[]{:S(2)}, u32[]{:S(2)}) collective-permute-start(f32[2,16,128]{2,1,0:T(8,128)S(1)} %pad_maximum_fusion.1), channel_id=1, source_target_pairs={{0,20},{4,16},{8,28},{12,24},{16,4},{20,0},{24,12},{28,8},{1,21},{... | collective-permute-start | bytes 49160 | tf_op jit(solution)/shard_map/ppermute | solution.py:355
  18.9 1.0 %collective-permute-start.9 = (f32[2,16,128]{2,1,0:T(8,128)S(1)}, f32[2,16,128]{2,1,0:T(8,128)S(1)}, u32[]{:S(2)}, u32[]{:S(2)}) collective-permute-start(f32[2,16,128]{2,1,0:T(8,128)S(1)} %pad_maximum_fusion), channel_id=1, source_target_pairs={{0,28},{4,24},{8,4},{12,0},{16,12},{20,8},{24,20},{28,16},{1,29},{... | collective-permute-start | bytes 49160 | tf_op jit(solution)/shard_map/ppermute | solution.py:355
  20.0 1.3 %collective-permute-done.11.refs_2_ = f32[2,16,128]{2,1,0:T(8,128)S(1)} collective-permute-done((f32[2,16,128]{2,1,0:T(8,128)S(1)}, f32[2,16,128]{2,1,0:T(8,128)S(1)}, u32[]{:S(2)}, u32[]{:S(2)}) %collective-permute-start.11) | collective-permute-done | bytes 16416 | tf_op jit(solution)/shard_map/ppermute | solution.py:355
  21.2 0.5 %collective-permute-done.10.refs_1_ = f32[2,16,128]{2,1,0:T(8,128)S(1)} collective-permute-done((f32[2,16,128]{2,1,0:T(8,128)S(1)}, f32[2,16,128]{2,1,0:T(8,128)S(1)}, u32[]{:S(2)}, u32[]{:S(2)}) %collective-permute-start.10) | collective-permute-done | bytes 16416 | tf_op jit(solution)/shard_map/ppermute | solution.py:355
  21.8 0.3 collective-permute-done.9.refs_0_
  22.1 0.4 %shard_map.78 = (f32[32,128]{1,0:T(8,128)S(1)}, f32[32,128]{1,0:T(8,128)S(1)}, f32[32,128]{1,0:T(8,128)S(1)}, f32[32,128]{1,0:T(8,128)S(1)}) custom-call(s32[1]{0:T(128)S(6)} %copy.10.count_ref, f32[8,256]{1,0:T(8,128)S(1)} %get-tuple-element.21.found_ref, f32[2,16,128]{2,1,0:T(8,128)S(1)} %collective-permute-done.9.refs_0_, ...), custom_call_target="tpu_custom_call" | custom-call | tf_op jit(solution)/shard_map/pallas_call | solution.py:357
  22.5 1.6 %collective-permute-start.12 = (f32[32,128]{1,0:T(8,128)S(1)}, f32[32,128]{1,0:T(8,128)S(1)}, u32[]{:S(2)}, u32[]{:S(2)}) collective-permute-start(f32[32,128]{1,0:T(8,128)S(1)} %get-tuple-element.34), channel_id=1, source_target_pairs={{0,1},{1,2},{2,3},{3,0},{4,5},{5,6},{6,7},{7,4},{8,9},{9,10},{10,1... | collective-permute-start | bytes 49160 | tf_op jit(solution)/shard_map/ppermute | solution.py:366
  24.1 2.6 %collective-permute-start.13 = (f32[32,128]{1,0:T(8,128)S(1)}, f32[32,128]{1,0:T(8,128)S(1)}, u32[]{:S(2)}, u32[]{:S(2)}) collective-permute-start(f32[32,128]{1,0:T(8,128)S(1)} %get-tuple-element.35), channel_id=1, source_target_pairs={{0,2},{1,3},{2,0},{3,1},{4,6},{5,7},{6,4},{7,5},{8,10},{9,11},{10,... | collective-permute-start | bytes 49160 | tf_op jit(solution)/shard_map/ppermute | solution.py:366
  26.7 1.3 %collective-permute-start.14 = (f32[32,128]{1,0:T(8,128)S(1)}, f32[32,128]{1,0:T(8,128)S(1)}, u32[]{:S(2)}, u32[]{:S(2)}) collective-permute-start(f32[32,128]{1,0:T(8,128)S(1)} %get-tuple-element.36), channel_id=1, source_target_pairs={{0,3},{1,0},{2,1},{3,2},{4,7},{5,4},{6,5},{7,6},{8,11},{9,8},{10,9... | collective-permute-start | bytes 49160 | tf_op jit(solution)/shard_map/ppermute | solution.py:366
  28.1 0.0 collective-permute-done.12
  28.1 0.9 %collective-permute-done.13 = f32[32,128]{1,0:T(8,128)S(1)} collective-permute-done((f32[32,128]{1,0:T(8,128)S(1)}, f32[32,128]{1,0:T(8,128)S(1)}, u32[]{:S(2)}, u32[]{:S(2)}) %collective-permute-start.13) | collective-permute-done | bytes 16416 | tf_op jit(solution)/shard_map/ppermute | solution.py:366
  29.0 1.4 %collective-permute-done.14 = f32[32,128]{1,0:T(8,128)S(1)} collective-permute-done((f32[32,128]{1,0:T(8,128)S(1)}, f32[32,128]{1,0:T(8,128)S(1)}, u32[]{:S(2)}, u32[]{:S(2)}) %collective-permute-start.14) | collective-permute-done | bytes 16416 | tf_op jit(solution)/shard_map/ppermute | solution.py:366
  30.5 0.1 fusion.2
  30.6 0.6 %maximum_bitcast_fusion = f32[1,64,64]{2,1,0:T(8,128)} fusion(f32[32,64]{1,0:T(8,128)S(1)} %get-tuple-element.46, f32[32,64]{1,0:T(8,128)S(1)} %get-tuple-element.45), kind=kLoop, calls=%fused_computation | loop fusion | flops 4096 | bytes 32768 | tf_op jit(solution)/shard_map/broadcast_in_dim | solution.py:367
  (7 shorter events, 0.1 us)
Async XLA Ops:
  0.0 11.1 %collective-permute-start = (bf16[8,8192]{1,0:T(8,128)(2,1)}, bf16[8,8192]{1,0:T(8,128)(2,1)S(1)}, u32[]{:S(2)}, u32[]{:S(2)}) collective-permute-start(bf16[8,8192]{1,0:T(8,128)(2,1)} %refs_0_.1), channel_id=1, source_target_pairs={{0,24},{4,28},{8,16},{12,20},{16,8},{20,12},{24,0},{28,4},{1,25},{... | collective-permute-start | bytes 393224 | tf_op jit(solution)/shard_map/ppermute | solution.py:258
  3.9 7.2 %collective-permute-start.1 = (s32[1,256]{1,0:T(1,128)}, s32[1,256]{1,0:T(1,128)S(1)}, u32[]{:S(2)}, u32[]{:S(2)}) collective-permute-start(s32[1,256]{1,0:T(1,128)} %refs_4_.1), channel_id=1, source_target_pairs={{0,24},{4,28},{8,16},{12,20},{16,8},{20,12},{24,0},{28,4},{1,25},{... | collective-permute-start | bytes 3080 | tf_op jit(solution)/shard_map/ppermute | solution.py:258
  6.4 6.4 %collective-permute-start.3 = (bf16[8,8320]{1,0:T(8,128)(2,1)S(1)}, bf16[8,8320]{1,0:T(8,128)(2,1)S(1)}, u32[]{:S(2)}, u32[]{:S(2)}) collective-permute-start(bf16[8,8320]{1,0:T(8,128)(2,1)S(1)} %get-tuple-element.25.refs_7_), channel_id=1, source_target_pairs={{0,16},{4,20},{8,24},{12,28},{16,0},{20,4},{24,8},{28,12},{1,17},{... | collective-permute-start | bytes 399368 | tf_op jit(solution)/shard_map/ppermute | solution.py:258
  8.4 5.0 %collective-permute-start.5 = (bf16[8,8320]{1,0:T(8,128)(2,1)S(1)}, bf16[8,8320]{1,0:T(8,128)(2,1)S(1)}, u32[]{:S(2)}, u32[]{:S(2)}) collective-permute-start(bf16[8,8320]{1,0:T(8,128)(2,1)S(1)} %get-tuple-element.25.refs_7_), channel_id=1, source_target_pairs={{0,8},{4,12},{8,0},{12,4},{16,24},{20,28},{24,16},{28,20},{1,9},{5... | collective-permute-start | bytes 399368 | tf_op jit(solution)/shard_map/ppermute | solution.py:258
  11.0 3.0 %collective-permute-start.7 = (bf16[8,8320]{1,0:T(8,128)(2,1)S(1)}, bf16[8,8320]{1,0:T(8,128)(2,1)S(1)}, u32[]{:S(2)}, u32[]{:S(2)}) collective-permute-start(bf16[8,8320]{1,0:T(8,128)(2,1)S(1)} %get-tuple-element.28), channel_id=1, source_target_pairs={{0,4},{4,0},{8,12},{12,8},{16,20},{20,16},{24,28},{28,24},{1,5},{5... | collective-permute-start | bytes 399368 | tf_op jit(solution)/shard_map/ppermute | solution.py:258
  12.3 1.7 %collective-permute-start.2 = (bf16[8,8320]{1,0:T(8,128)(2,1)S(1)}, bf16[8,8320]{1,0:T(8,128)(2,1)S(1)}, u32[]{:S(2)}, u32[]{:S(2)}) collective-permute-start(bf16[8,8320]{1,0:T(8,128)(2,1)S(1)} %shard_map.74.refs_1_), channel_id=1, source_target_pairs={{0,4},{4,0},{8,12},{12,8},{16,20},{20,16},{24,28},{28,24},{1,5},{5... | collective-permute-start | bytes 399368 | tf_op jit(solution)/shard_map/ppermute | solution.py:258
  12.8 1.4 %collective-permute-start.4 = (bf16[8,8320]{1,0:T(8,128)(2,1)S(1)}, bf16[8,8320]{1,0:T(8,128)(2,1)S(1)}, u32[]{:S(2)}, u32[]{:S(2)}) collective-permute-start(bf16[8,8320]{1,0:T(8,128)(2,1)S(1)} %collective-permute-done.3.refs_3_), channel_id=1, source_target_pairs={{0,4},{4,0},{8,12},{12,8},{16,20},{20,16},{24,28},{28,24},{1,5},{5... | collective-permute-start | bytes 399368 | tf_op jit(solution)/shard_map/ppermute | solution.py:258
  13.4 1.4 %collective-permute-start.6 = (bf16[8,8320]{1,0:T(8,128)(2,1)S(1)}, bf16[8,8320]{1,0:T(8,128)(2,1)S(1)}, u32[]{:S(2)}, u32[]{:S(2)}) collective-permute-start(bf16[8,8320]{1,0:T(8,128)(2,1)S(1)} %collective-permute-done.5.refs_5_), channel_id=1, source_target_pairs={{0,4},{4,0},{8,12},{12,8},{16,20},{20,16},{24,28},{28,24},{1,5},{5... | collective-permute-start | bytes 399368 | tf_op jit(solution)/shard_map/ppermute | solution.py:258
  15.9 1.3 %collective-permute-start.8 = (f32[4,16,128]{2,1,0:T(8,128)S(1)}, f32[4,16,128]{2,1,0:T(8,128)S(1)}, u32[]{:S(2)}, u32[]{:S(2)}) collective-permute-start(f32[4,16,128]{2,1,0:T(8,128)S(1)} %get-tuple-element.32), channel_id=1, source_target_pairs={{0,4},{4,0},{8,12},{12,8},{16,20},{20,16},{24,28},{28,24},{1,5},{5... | collective-permute-start | bytes 98312 | tf_op jit(solution)/shard_map/ppermute | solution.py:258
  17.2 4.1 %collective-permute-start.11 = (f32[2,16,128]{2,1,0:T(8,128)S(1)}, f32[2,16,128]{2,1,0:T(8,128)S(1)}, u32[]{:S(2)}, u32[]{:S(2)}) collective-permute-start(f32[2,16,128]{2,1,0:T(8,128)S(1)} %pad_maximum_fusion.2), channel_id=1, source_target_pairs={{0,12},{4,8},{8,20},{12,16},{16,28},{20,24},{24,4},{28,0},{1,13},{... | collective-permute-start | bytes 49160 | tf_op jit(solution)/shard_map/ppermute | solution.py:355
  18.4 3.3 %collective-permute-start.10 = (f32[2,16,128]{2,1,0:T(8,128)S(1)}, f32[2,16,128]{2,1,0:T(8,128)S(1)}, u32[]{:S(2)}, u32[]{:S(2)}) collective-permute-start(f32[2,16,128]{2,1,0:T(8,128)S(1)} %pad_maximum_fusion.1), channel_id=1, source_target_pairs={{0,20},{4,16},{8,28},{12,24},{16,4},{20,0},{24,12},{28,8},{1,21},{... | collective-permute-start | bytes 49160 | tf_op jit(solution)/shard_map/ppermute | solution.py:355
  18.9 3.2 %collective-permute-start.9 = (f32[2,16,128]{2,1,0:T(8,128)S(1)}, f32[2,16,128]{2,1,0:T(8,128)S(1)}, u32[]{:S(2)}, u32[]{:S(2)}) collective-permute-start(f32[2,16,128]{2,1,0:T(8,128)S(1)} %pad_maximum_fusion), channel_id=1, source_target_pairs={{0,28},{4,24},{8,4},{12,0},{16,12},{20,8},{24,20},{28,16},{1,29},{... | collective-permute-start | bytes 49160 | tf_op jit(solution)/shard_map/ppermute | solution.py:355
  22.5 5.6 %collective-permute-start.12 = (f32[32,128]{1,0:T(8,128)S(1)}, f32[32,128]{1,0:T(8,128)S(1)}, u32[]{:S(2)}, u32[]{:S(2)}) collective-permute-start(f32[32,128]{1,0:T(8,128)S(1)} %get-tuple-element.34), channel_id=1, source_target_pairs={{0,1},{1,2},{2,3},{3,0},{4,5},{5,6},{6,7},{7,4},{8,9},{9,10},{10,1... | collective-permute-start | bytes 49160 | tf_op jit(solution)/shard_map/ppermute | solution.py:366
  24.1 4.9 %collective-permute-start.13 = (f32[32,128]{1,0:T(8,128)S(1)}, f32[32,128]{1,0:T(8,128)S(1)}, u32[]{:S(2)}, u32[]{:S(2)}) collective-permute-start(f32[32,128]{1,0:T(8,128)S(1)} %get-tuple-element.35), channel_id=1, source_target_pairs={{0,2},{1,3},{2,0},{3,1},{4,6},{5,7},{6,4},{7,5},{8,10},{9,11},{10,... | collective-permute-start | bytes 49160 | tf_op jit(solution)/shard_map/ppermute | solution.py:366
  26.7 3.7 %collective-permute-start.14 = (f32[32,128]{1,0:T(8,128)S(1)}, f32[32,128]{1,0:T(8,128)S(1)}, u32[]{:S(2)}, u32[]{:S(2)}) collective-permute-start(f32[32,128]{1,0:T(8,128)S(1)} %get-tuple-element.36), channel_id=1, source_target_pairs={{0,3},{1,0},{2,1},{3,2},{4,7},{5,4},{6,5},{7,6},{8,11},{9,8},{10,9... | collective-permute-start | bytes 49160 | tf_op jit(solution)/shard_map/ppermute | solution.py:366

commit v28 on v27

--- a/solution.py
+++ b/solution.py
@@ -18,6 +18,12 @@
 
 def iota(shape, dimension):
     return lax.broadcasted_iota(jnp.int32, shape, dimension)
+
+
+def block_owners(holders):
+    if holders == 8:
+        return [(0, 0), (1, 1), (2, 4), (5, 3), (4, 2), (3, 5), (6, 6), (7, 7)]
+    return [(k, k) for k in range(holders)]
 
 
 def parts_of(value):
@@ -182,8 +188,10 @@
         for k in range(holders):
             queries[k * rows:(k + 1) * rows, columns] = packed_refs[k][:, columns]
         scores = scores + jnp.dot(queries[:, columns], pages_ref[columns], preferred_element_type=jnp.float32)
-    for k in range(holders):
-        start = pl.multiple_of((me ^ k) * rows, rows)
+    second_core = me % 2 == 1
+    owners = block_owners(holders)
+    for k, (first, second) in enumerate(owners):
+        start = pl.multiple_of((me ^ jnp.where(second_core, second, first)) * rows, rows)
         scores_ref[pl.ds(start, rows), :] = scores[k * rows:(k + 1) * rows]
     asked = []
     for k in range(holders):
@@ -193,6 +201,10 @@
         for block in range(1, holders // rows):
             mine = jnp.where(me // rows == block, notes[:, block * capacity:(block + 1) * capacity], mine)
         asked.append(mine)
+    places = [[pair[core] for pair in owners] for core in range(2)]
+    asked = [
+        jnp.where(second_core, asked[places[1].index(k)], asked[places[0].index(k)]) for k in range(holders)
+    ]
     chips = holders // 2
     chip = me // 2
     kept, handed = [asked[0]], [asked[1]]
@@ -309,7 +321,8 @@
     blocks = [None] * holders
     blocks[0] = packed
     for k in range(2, holders - 2, 2):
-        blocks[k] = swap(packed, "store", k)
+        pair = block_owners(holders)[k]
+        blocks[k] = lax.ppermute(packed, "store", [(i, i ^ pair[i % 2]) for i in range(holders)])
     blocks[far] = pl.pallas_call(
         functools.partial(late_kernel, holders, capacity, per_holder),
         out_shape=jax.ShapeDtypeStruct(packed.shape, bf16),

time: 31.3 us -> 31.6 us (level)
  starting transfers between devices: 16.6 us -> 17.5 us
  waiting for transfers between devices: 6.47 us -> 5.79 us
    ppermute x9 -> x7, starting transfers between devices: 8.26 us -> 4.74 us  [swap(): lax.ppermute(value, axis, [(i, i ^ distance) for i in range(lax.axis_size...]
    ppermute x0 -> x2, starting transfers between devices: none -> 3.52 us  [on_device(): lax.ppermute(packed, 'store', [(i, i ^ pair[i % 2]) for i in range(holder...]
    ppermute x3, starting transfers between devices: 2.77 us -> 3.71 us  [on_device(): landed.append(lax.ppermute(pair, 'store', to) if step else pair)]
    ppermute x3, waiting for transfers between devices: 2.11 us -> 1.44 us  [on_device(): landed.append(lax.ppermute(pair, 'store', to) if step else pair)]
    ppermute x0 -> x2, waiting for transfers between devices: none -> 0.53 us  [on_device(): lax.ppermute(packed, 'store', [(i, i ^ pair[i % 2]) for i in range(holder...]
    ppermute x9 -> x7, waiting for transfers between devices: 1.96 us -> 1.44 us  [swap(): lax.ppermute(value, axis, [(i, i ^ distance) for i in range(lax.axis_size...]
where the time goes in v28:
time: 31.6 us; the launch traced here: 31.4 us
  starting transfers between devices  17.5 us (55%)
  Pallas kernels  6.64 us (21%)
  waiting for transfers between devices  5.79 us (18%)
  between operations  0.74 us (2%)
  other arithmetic  0.64 us (2%)
    ppermute x3, starting transfers between devices, on_device(): lax.ppermute(terms[step], 'layer', [(g, (g + step) % groups) for g in ran...  5.56 us
    ppermute x7, starting transfers between devices, swap(): lax.ppermute(value, axis, [(i, i ^ distance) for i in range(lax.axis_size...  4.74 us
    ppermute x3, starting transfers between devices, on_device(): landed.append(lax.ppermute(pair, 'store', to) if step else pair)  3.71 us
    ppermute x2, starting transfers between devices, on_device(): lax.ppermute(packed, 'store', [(i, i ^ pair[i % 2]) for i in range(holder...  3.52 us
    pallas_call x1, Pallas kernels, on_device(): pl.pallas_call(functools.partial(condition_kernel, holders, capacity, per...  2.43 us
    ppermute x3, waiting for transfers between devices, on_device(): lax.ppermute(terms[step], 'layer', [(g, (g + step) % groups) for g in ran...  2.39 us
    ppermute x3, waiting for transfers between devices, on_device(): landed.append(lax.ppermute(pair, 'store', to) if step else pair)  1.44 us
    ppermute x7, waiting for transfers between devices, swap(): lax.ppermute(value, axis, [(i, i ^ distance) for i in range(lax.axis_size...  1.44 us
  transfers between devices with their start and end apart: 15, of which 9 were waited for; matrix products, arithmetic and copies ran while one was open for 0% of the time, Pallas kernels for 16%

profile of v28, /device:TPU:0, one launch (start us, length us, event | category | flops | bytes accessed | tf_op | source)
XLA Modules:
  0.0 31.4 jit_solution(16138454904106294914)
XLA Ops:
  0.0 3.9 %collective-permute-start = (bf16[8,8192]{1,0:T(8,128)(2,1)}, bf16[8,8192]{1,0:T(8,128)(2,1)S(1)}, u32[]{:S(2)}, u32[]{:S(2)}) collective-permute-start(bf16[8,8192]{1,0:T(8,128)(2,1)} %refs_0_.1), channel_id=1, source_target_pairs={{0,24},{4,28},{8,16},{12,20},{16,8},{20,12},{24,0},{28,4},{1,25},{... | collective-permute-start | bytes 393224 | tf_op jit(solution)/shard_map/ppermute | solution.py:270
  3.9 0.0 collective-permute-start.1
  3.9 2.4 %shard_map.73 = (bf16[8,8320]{1,0:T(8,128)(2,1)S(1)}, bf16[8,8320]{1,0:T(8,128)(2,1)S(1)}, f32[8,256]{1,0:T(8,128)S(1)}, f32[2,64,64]{2,1,0:T(8,128)S(1)}, f32[2...) custom-call(bf16[8,8192]{1,0:T(8,128)(2,1)} %refs_0_.1, f32[2,64,64]{2,1,0:T(8,128)} %refs_1_.1, ...), custom_call_target="tpu_custom_call" | custom-call | tf_op jit(solution)/shard_map/pallas_call | solution.py:293
  6.4 2.0 %collective-permute-start.3 = (bf16[8,8320]{1,0:T(8,128)(2,1)S(1)}, bf16[8,8320]{1,0:T(8,128)(2,1)S(1)}, u32[]{:S(2)}, u32[]{:S(2)}) collective-permute-start(bf16[8,8320]{1,0:T(8,128)(2,1)S(1)} %get-tuple-element.25.refs_7_), channel_id=1, source_target_pairs={{0,16},{4,12},{8,24},{12,4},{16,0},{20,28},{24,8},{28,20},{1,17},{... | collective-permute-start | bytes 399368 | tf_op jit(solution)/shard_map/ppermute | solution.py:325
  8.4 1.5 %collective-permute-start.5 = (bf16[8,8320]{1,0:T(8,128)(2,1)S(1)}, bf16[8,8320]{1,0:T(8,128)(2,1)S(1)}, u32[]{:S(2)}, u32[]{:S(2)}) collective-permute-start(bf16[8,8320]{1,0:T(8,128)(2,1)S(1)} %get-tuple-element.25.refs_7_), channel_id=1, source_target_pairs={{0,8},{4,20},{8,0},{12,28},{16,24},{20,4},{24,16},{28,12},{1,9},{5... | collective-permute-start | bytes 399368 | tf_op jit(solution)/shard_map/ppermute | solution.py:325
  9.9 1.1 %shard_map.75 = (bf16[8,8320]{1,0:T(8,128)(2,1)S(1)}, bf16[8192,256]{1,0:T(8,128)(2,1)S(1)}) custom-call(bf16[8,8320]{1,0:T(8,128)(2,1)S(1)} %get-tuple-element.26.block_ref, bf16[256,8192]{1,0:T(8,128)(2,1)S(1)} %get-tuple-element.27.source_ref), custom_call_target="tpu_custom_call", output_to_operand_aliasing={{0}: (0, {})} | custom-call | bytes 4194304 | tf_op jit(solution)/shard_map/pallas_call | solution.py:311
  11.0 0.1 collective-permute-start.7
  11.1 0.0 collective-permute-done.1.cand_ref
  11.1 0.0 collective-permute-done.query_ref
  11.1 1.2 %shard_map.74.refs_1_ = bf16[8,8320]{1,0:T(8,128)(2,1)S(1)} custom-call(bf16[8,8192]{1,0:T(8,128)(2,1)S(1)} %collective-permute-done.query_ref, s32[1,256]{1,0:T(1,128)S(1)} %collective-permute-done.1.cand_ref, f32[2,64,64]{2,1,0:T(8,128)S(1)} %get-tuple-element.22.in_factor_ref, f32[2,64,64]{2,1,0:T(8,128)S(1)} %get-tuple-element.23.out_factor_ref, ...), custom_call_target="tpu_custom_call" | custom-call | flops 5000000000 | bytes 532480 | tf_op jit(solution)/shard_map/pallas_call | solution.py:326
  12.3 0.5 %collective-permute-start.2 = (bf16[8,8320]{1,0:T(8,128)(2,1)S(1)}, bf16[8,8320]{1,0:T(8,128)(2,1)S(1)}, u32[]{:S(2)}, u32[]{:S(2)}) collective-permute-start(bf16[8,8320]{1,0:T(8,128)(2,1)S(1)} %shard_map.74.refs_1_), channel_id=1, source_target_pairs={{0,4},{4,0},{8,12},{12,8},{16,20},{20,16},{24,28},{28,24},{1,5},{5... | collective-permute-start | bytes 399368 | tf_op jit(solution)/shard_map/ppermute | solution.py:270
  12.8 0.0 collective-permute-done.3.refs_3_
  12.8 0.1 collective-permute-start.4
  12.9 0.5 %collective-permute-done.5.refs_5_ = bf16[8,8320]{1,0:T(8,128)(2,1)S(1)} collective-permute-done((bf16[8,8320]{1,0:T(8,128)(2,1)S(1)}, bf16[8,8320]{1,0:T(8,128)(2,1)S(1)}, u32[]{:S(2)}, u32[]{:S(2)}) %collective-permute-start.5) | collective-permute-done | bytes 133152 | tf_op jit(solution)/shard_map/ppermute | solution.py:325
  13.4 0.0 collective-permute-start.6
  14.0 0.0 collective-permute-done.7.refs_6_
  14.1 0.0 collective-permute-done.2.refs_0_
  14.1 0.1 collective-permute-done.4.refs_2_
  14.2 0.6 %collective-permute-done.6.refs_4_ = bf16[8,8320]{1,0:T(8,128)(2,1)S(1)} collective-permute-done((bf16[8,8320]{1,0:T(8,128)(2,1)S(1)}, bf16[8,8320]{1,0:T(8,128)(2,1)S(1)}, u32[]{:S(2)}, u32[]{:S(2)}) %collective-permute-start.6) | collective-permute-done | bytes 133152 | tf_op jit(solution)/shard_map/ppermute | solution.py:270
  14.7 1.2 %shard_map.76 = (f32[4,16,128]{2,1,0:T(8,128)S(1)}, f32[64,256]{1,0:T(8,128)S(1)}, f32[1,128]{1,0:T(1,128)S(1)}) custom-call(bf16[8,8320]{1,0:T(8,128)(2,1)S(1)} %collective-permute-done.2.refs_0_, bf16[8,8320]{1,0:T(8,128)(2,1)S(1)} %shard_map.74.refs_1_, bf16[8,8320]{1,0:T(8,128)(2,1)S(1)} %collective-permute-done.4.refs_2_, ...), custom_call_target="tpu_custom_call" | custom-call | tf_op jit(solution)/shard_map/pallas_call | solution.py:342
  15.9 0.2 collective-permute-start.8
  16.1 0.3 shard_map.77
  16.4 0.8 %collective-permute-done.8 = f32[4,16,128]{2,1,0:T(8,128)S(1)} collective-permute-done((f32[4,16,128]{2,1,0:T(8,128)S(1)}, f32[4,16,128]{2,1,0:T(8,128)S(1)}, u32[]{:S(2)}, u32[]{:S(2)}) %collective-permute-start.8) | collective-permute-done | bytes 32800 | tf_op jit(solution)/shard_map/ppermute | solution.py:270
  17.2 1.3 %collective-permute-start.11 = (f32[2,16,128]{2,1,0:T(8,128)S(1)}, f32[2,16,128]{2,1,0:T(8,128)S(1)}, u32[]{:S(2)}, u32[]{:S(2)}) collective-permute-start(f32[2,16,128]{2,1,0:T(8,128)S(1)} %pad_maximum_fusion.2), channel_id=1, source_target_pairs={{0,12},{4,8},{8,20},{12,16},{16,28},{20,24},{24,4},{28,0},{1,13},{... | collective-permute-start | bytes 49160 | tf_op jit(solution)/shard_map/ppermute | solution.py:368
  18.4 0.5 %collective-permute-start.10 = (f32[2,16,128]{2,1,0:T(8,128)S(1)}, f32[2,16,128]{2,1,0:T(8,128)S(1)}, u32[]{:S(2)}, u32[]{:S(2)}) collective-permute-start(f32[2,16,128]{2,1,0:T(8,128)S(1)} %pad_maximum_fusion.1), channel_id=1, source_target_pairs={{0,20},{4,16},{8,28},{12,24},{16,4},{20,0},{24,12},{28,8},{1,21},{... | collective-permute-start | bytes 49160 | tf_op jit(solution)/shard_map/ppermute | solution.py:368
  18.9 2.0 %collective-permute-start.9 = (f32[2,16,128]{2,1,0:T(8,128)S(1)}, f32[2,16,128]{2,1,0:T(8,128)S(1)}, u32[]{:S(2)}, u32[]{:S(2)}) collective-permute-start(f32[2,16,128]{2,1,0:T(8,128)S(1)} %pad_maximum_fusion), channel_id=1, source_target_pairs={{0,28},{4,24},{8,4},{12,0},{16,12},{20,8},{24,20},{28,16},{1,29},{... | collective-permute-start | bytes 49160 | tf_op jit(solution)/shard_map/ppermute | solution.py:368
  20.9 0.3 %collective-permute-done.11.refs_2_ = f32[2,16,128]{2,1,0:T(8,128)S(1)} collective-permute-done((f32[2,16,128]{2,1,0:T(8,128)S(1)}, f32[2,16,128]{2,1,0:T(8,128)S(1)}, u32[]{:S(2)}, u32[]{:S(2)}) %collective-permute-start.11) | collective-permute-done | bytes 16416 | tf_op jit(solution)/shard_map/ppermute | solution.py:368
  21.2 0.5 %collective-permute-done.10.refs_1_ = f32[2,16,128]{2,1,0:T(8,128)S(1)} collective-permute-done((f32[2,16,128]{2,1,0:T(8,128)S(1)}, f32[2,16,128]{2,1,0:T(8,128)S(1)}, u32[]{:S(2)}, u32[]{:S(2)}) %collective-permute-start.10) | collective-permute-done | bytes 16416 | tf_op jit(solution)/shard_map/ppermute | solution.py:368
  21.8 0.6 %collective-permute-done.9.refs_0_ = f32[2,16,128]{2,1,0:T(8,128)S(1)} collective-permute-done((f32[2,16,128]{2,1,0:T(8,128)S(1)}, f32[2,16,128]{2,1,0:T(8,128)S(1)}, u32[]{:S(2)}, u32[]{:S(2)}) %collective-permute-start.9) | collective-permute-done | bytes 16416 | tf_op jit(solution)/shard_map/ppermute | solution.py:368
  22.3 0.4 %shard_map.78 = (f32[32,128]{1,0:T(8,128)S(1)}, f32[32,128]{1,0:T(8,128)S(1)}, f32[32,128]{1,0:T(8,128)S(1)}, f32[32,128]{1,0:T(8,128)S(1)}) custom-call(s32[1]{0:T(128)S(6)} %copy.10.count_ref, f32[8,256]{1,0:T(8,128)S(1)} %get-tuple-element.21.found_ref, f32[2,16,128]{2,1,0:T(8,128)S(1)} %collective-permute-done.9.refs_0_, ...), custom_call_target="tpu_custom_call" | custom-call | tf_op jit(solution)/shard_map/pallas_call | solution.py:370
  22.8 1.6 %collective-permute-start.12 = (f32[32,128]{1,0:T(8,128)S(1)}, f32[32,128]{1,0:T(8,128)S(1)}, u32[]{:S(2)}, u32[]{:S(2)}) collective-permute-start(f32[32,128]{1,0:T(8,128)S(1)} %get-tuple-element.34), channel_id=1, source_target_pairs={{0,1},{1,2},{2,3},{3,0},{4,5},{5,6},{6,7},{7,4},{8,9},{9,10},{10,1... | collective-permute-start | bytes 49160 | tf_op jit(solution)/shard_map/ppermute | solution.py:379
  24.4 2.6 %collective-permute-start.13 = (f32[32,128]{1,0:T(8,128)S(1)}, f32[32,128]{1,0:T(8,128)S(1)}, u32[]{:S(2)}, u32[]{:S(2)}) collective-permute-start(f32[32,128]{1,0:T(8,128)S(1)} %get-tuple-element.35), channel_id=1, source_target_pairs={{0,2},{1,3},{2,0},{3,1},{4,6},{5,7},{6,4},{7,5},{8,10},{9,11},{10,... | collective-permute-start | bytes 49160 | tf_op jit(solution)/shard_map/ppermute | solution.py:379
  27.0 1.3 %collective-permute-start.14 = (f32[32,128]{1,0:T(8,128)S(1)}, f32[32,128]{1,0:T(8,128)S(1)}, u32[]{:S(2)}, u32[]{:S(2)}) collective-permute-start(f32[32,128]{1,0:T(8,128)S(1)} %get-tuple-element.36), channel_id=1, source_target_pairs={{0,3},{1,0},{2,1},{3,2},{4,7},{5,4},{6,5},{7,6},{8,11},{9,8},{10,9... | collective-permute-start | bytes 49160 | tf_op jit(solution)/shard_map/ppermute | solution.py:379
  28.4 0.0 collective-permute-done.12
  28.4 0.7 %collective-permute-done.13 = f32[32,128]{1,0:T(8,128)S(1)} collective-permute-done((f32[32,128]{1,0:T(8,128)S(1)}, f32[32,128]{1,0:T(8,128)S(1)}, u32[]{:S(2)}, u32[]{:S(2)}) %collective-permute-start.13) | collective-permute-done | bytes 16416 | tf_op jit(solution)/shard_map/ppermute | solution.py:379
  29.1 1.7 %collective-permute-done.14 = f32[32,128]{1,0:T(8,128)S(1)} collective-permute-done((f32[32,128]{1,0:T(8,128)S(1)}, f32[32,128]{1,0:T(8,128)S(1)}, u32[]{:S(2)}, u32[]{:S(2)}) %collective-permute-start.14) | collective-permute-done | bytes 16416 | tf_op jit(solution)/shard_map/ppermute | solution.py:379
  30.7 0.1 fusion.2
  30.8 0.6 %maximum_bitcast_fusion = f32[1,64,64]{2,1,0:T(8,128)} fusion(f32[32,64]{1,0:T(8,128)S(1)} %get-tuple-element.46, f32[32,64]{1,0:T(8,128)S(1)} %get-tuple-element.45), kind=kLoop, calls=%fused_computation | loop fusion | flops 4096 | bytes 32768 | tf_op jit(solution)/shard_map/broadcast_in_dim | solution.py:380
  (7 shorter events, 0.1 us)
Async XLA Ops:
  0.0 11.1 %collective-permute-start = (bf16[8,8192]{1,0:T(8,128)(2,1)}, bf16[8,8192]{1,0:T(8,128)(2,1)S(1)}, u32[]{:S(2)}, u32[]{:S(2)}) collective-permute-start(bf16[8,8192]{1,0:T(8,128)(2,1)} %refs_0_.1), channel_id=1, source_target_pairs={{0,24},{4,28},{8,16},{12,20},{16,8},{20,12},{24,0},{28,4},{1,25},{... | collective-permute-start | bytes 393224 | tf_op jit(solution)/shard_map/ppermute | solution.py:270
  3.9 7.2 %collective-permute-start.1 = (s32[1,256]{1,0:T(1,128)}, s32[1,256]{1,0:T(1,128)S(1)}, u32[]{:S(2)}, u32[]{:S(2)}) collective-permute-start(s32[1,256]{1,0:T(1,128)} %refs_4_.1), channel_id=1, source_target_pairs={{0,24},{4,28},{8,16},{12,20},{16,8},{20,12},{24,0},{28,4},{1,25},{... | collective-permute-start | bytes 3080 | tf_op jit(solution)/shard_map/ppermute | solution.py:270
  6.4 6.4 %collective-permute-start.3 = (bf16[8,8320]{1,0:T(8,128)(2,1)S(1)}, bf16[8,8320]{1,0:T(8,128)(2,1)S(1)}, u32[]{:S(2)}, u32[]{:S(2)}) collective-permute-start(bf16[8,8320]{1,0:T(8,128)(2,1)S(1)} %get-tuple-element.25.refs_7_), channel_id=1, source_target_pairs={{0,16},{4,12},{8,24},{12,4},{16,0},{20,28},{24,8},{28,20},{1,17},{... | collective-permute-start | bytes 399368 | tf_op jit(solution)/shard_map/ppermute | solution.py:325
  8.4 5.0 %collective-permute-start.5 = (bf16[8,8320]{1,0:T(8,128)(2,1)S(1)}, bf16[8,8320]{1,0:T(8,128)(2,1)S(1)}, u32[]{:S(2)}, u32[]{:S(2)}) collective-permute-start(bf16[8,8320]{1,0:T(8,128)(2,1)S(1)} %get-tuple-element.25.refs_7_), channel_id=1, source_target_pairs={{0,8},{4,20},{8,0},{12,28},{16,24},{20,4},{24,16},{28,12},{1,9},{5... | collective-permute-start | bytes 399368 | tf_op jit(solution)/shard_map/ppermute | solution.py:325
  11.0 3.0 %collective-permute-start.7 = (bf16[8,8320]{1,0:T(8,128)(2,1)S(1)}, bf16[8,8320]{1,0:T(8,128)(2,1)S(1)}, u32[]{:S(2)}, u32[]{:S(2)}) collective-permute-start(bf16[8,8320]{1,0:T(8,128)(2,1)S(1)} %get-tuple-element.28), channel_id=1, source_target_pairs={{0,4},{4,0},{8,12},{12,8},{16,20},{20,16},{24,28},{28,24},{1,5},{5... | collective-permute-start | bytes 399368 | tf_op jit(solution)/shard_map/ppermute | solution.py:270
  12.3 1.7 %collective-permute-start.2 = (bf16[8,8320]{1,0:T(8,128)(2,1)S(1)}, bf16[8,8320]{1,0:T(8,128)(2,1)S(1)}, u32[]{:S(2)}, u32[]{:S(2)}) collective-permute-start(bf16[8,8320]{1,0:T(8,128)(2,1)S(1)} %shard_map.74.refs_1_), channel_id=1, source_target_pairs={{0,4},{4,0},{8,12},{12,8},{16,20},{20,16},{24,28},{28,24},{1,5},{5... | collective-permute-start | bytes 399368 | tf_op jit(solution)/shard_map/ppermute | solution.py:270
  12.8 1.4 %collective-permute-start.4 = (bf16[8,8320]{1,0:T(8,128)(2,1)S(1)}, bf16[8,8320]{1,0:T(8,128)(2,1)S(1)}, u32[]{:S(2)}, u32[]{:S(2)}) collective-permute-start(bf16[8,8320]{1,0:T(8,128)(2,1)S(1)} %collective-permute-done.3.refs_3_), channel_id=1, source_target_pairs={{0,4},{4,0},{8,12},{12,8},{16,20},{20,16},{24,28},{28,24},{1,5},{5... | collective-permute-start | bytes 399368 | tf_op jit(solution)/shard_map/ppermute | solution.py:270
  13.4 1.4 %collective-permute-start.6 = (bf16[8,8320]{1,0:T(8,128)(2,1)S(1)}, bf16[8,8320]{1,0:T(8,128)(2,1)S(1)}, u32[]{:S(2)}, u32[]{:S(2)}) collective-permute-start(bf16[8,8320]{1,0:T(8,128)(2,1)S(1)} %collective-permute-done.5.refs_5_), channel_id=1, source_target_pairs={{0,4},{4,0},{8,12},{12,8},{16,20},{20,16},{24,28},{28,24},{1,5},{5... | collective-permute-start | bytes 399368 | tf_op jit(solution)/shard_map/ppermute | solution.py:270
  15.9 1.3 %collective-permute-start.8 = (f32[4,16,128]{2,1,0:T(8,128)S(1)}, f32[4,16,128]{2,1,0:T(8,128)S(1)}, u32[]{:S(2)}, u32[]{:S(2)}) collective-permute-start(f32[4,16,128]{2,1,0:T(8,128)S(1)} %get-tuple-element.32), channel_id=1, source_target_pairs={{0,4},{4,0},{8,12},{12,8},{16,20},{20,16},{24,28},{28,24},{1,5},{5... | collective-permute-start | bytes 98312 | tf_op jit(solution)/shard_map/ppermute | solution.py:270
  17.2 4.1 %collective-permute-start.11 = (f32[2,16,128]{2,1,0:T(8,128)S(1)}, f32[2,16,128]{2,1,0:T(8,128)S(1)}, u32[]{:S(2)}, u32[]{:S(2)}) collective-permute-start(f32[2,16,128]{2,1,0:T(8,128)S(1)} %pad_maximum_fusion.2), channel_id=1, source_target_pairs={{0,12},{4,8},{8,20},{12,16},{16,28},{20,24},{24,4},{28,0},{1,13},{... | collective-permute-start | bytes 49160 | tf_op jit(solution)/shard_map/ppermute | solution.py:368
  18.4 3.3 %collective-permute-start.10 = (f32[2,16,128]{2,1,0:T(8,128)S(1)}, f32[2,16,128]{2,1,0:T(8,128)S(1)}, u32[]{:S(2)}, u32[]{:S(2)}) collective-permute-start(f32[2,16,128]{2,1,0:T(8,128)S(1)} %pad_maximum_fusion.1), channel_id=1, source_target_pairs={{0,20},{4,16},{8,28},{12,24},{16,4},{20,0},{24,12},{28,8},{1,21},{... | collective-permute-start | bytes 49160 | tf_op jit(solution)/shard_map/ppermute | solution.py:368
  18.9 3.4 %collective-permute-start.9 = (f32[2,16,128]{2,1,0:T(8,128)S(1)}, f32[2,16,128]{2,1,0:T(8,128)S(1)}, u32[]{:S(2)}, u32[]{:S(2)}) collective-permute-start(f32[2,16,128]{2,1,0:T(8,128)S(1)} %pad_maximum_fusion), channel_id=1, source_target_pairs={{0,28},{4,24},{8,4},{12,0},{16,12},{20,8},{24,20},{28,16},{1,29},{... | collective-permute-start | bytes 49160 | tf_op jit(solution)/shard_map/ppermute | solution.py:368
  22.8 5.6 %collective-permute-start.12 = (f32[32,128]{1,0:T(8,128)S(1)}, f32[32,128]{1,0:T(8,128)S(1)}, u32[]{:S(2)}, u32[]{:S(2)}) collective-permute-start(f32[32,128]{1,0:T(8,128)S(1)} %get-tuple-element.34), channel_id=1, source_target_pairs={{0,1},{1,2},{2,3},{3,0},{4,5},{5,6},{6,7},{7,4},{8,9},{9,10},{10,1... | collective-permute-start | bytes 49160 | tf_op jit(solution)/shard_map/ppermute | solution.py:379
  24.4 4.7 %collective-permute-start.13 = (f32[32,128]{1,0:T(8,128)S(1)}, f32[32,128]{1,0:T(8,128)S(1)}, u32[]{:S(2)}, u32[]{:S(2)}) collective-permute-start(f32[32,128]{1,0:T(8,128)S(1)} %get-tuple-element.35), channel_id=1, source_target_pairs={{0,2},{1,3},{2,0},{3,1},{4,6},{5,7},{6,4},{7,5},{8,10},{9,11},{10,... | collective-permute-start | bytes 49160 | tf_op jit(solution)/shard_map/ppermute | solution.py:379
  27.0 3.7 %collective-permute-start.14 = (f32[32,128]{1,0:T(8,128)S(1)}, f32[32,128]{1,0:T(8,128)S(1)}, u32[]{:S(2)}, u32[]{:S(2)}) collective-permute-start(f32[32,128]{1,0:T(8,128)S(1)} %get-tuple-element.36), channel_id=1, source_target_pairs={{0,3},{1,0},{2,1},{3,2},{4,7},{5,4},{6,5},{7,6},{8,11},{9,8},{10,9... | collective-permute-start | bytes 49160 | tf_op jit(solution)/shard_map/ppermute | solution.py:379

commit v29 on v26

--- a/solution.py
+++ b/solution.py
@@ -148,12 +148,12 @@
     copies[-1].wait()
 
 
-def late_kernel(
-    holders, capacity, per_holder, query_ref, cand_ref, in_factor_ref, out_factor_ref, home_ref, packed_ref, turned_ref
-):
-    rows, width = query_ref.shape
-    condition(query_ref, in_factor_ref, out_factor_ref, turned_ref, (packed_ref,))
-    packed_ref[:, width:] = look_up(holders, capacity, per_holder, rows, cand_ref, home_ref)[0]
+def late_kernel(query_ref, in_factor_ref, out_factor_ref, target_ref, turned_ref):
+    condition(query_ref, in_factor_ref, out_factor_ref, turned_ref, (target_ref,))
+
+
+def list_kernel(holders, capacity, per_holder, rows, cand_ref, home_ref, notes_ref):
+    notes_ref[...] = look_up(holders, capacity, per_holder, rows, cand_ref, home_ref)[0]
 
 
 def load_kernel(holders, count_ref, found_ref, block_ref, source_ref, same_block_ref, target_ref, used_ref):
@@ -173,7 +173,8 @@
 
 
 def score_kernel(holders, capacity, *refs):
-    packed_refs, pages_ref, send_ref, scores_ref, rest_ref, queries = refs[:holders][::-1], *refs[holders:]
+    packed_refs, far_refs = refs[:holders][::-1], refs[holders:holders + 2]
+    pages_ref, send_ref, scores_ref, rest_ref, queries = refs[holders + 2:]
     me = lax.axis_index("store")
     width, count = pages_ref.shape
     rows = packed_refs[0].shape[0]
@@ -190,7 +191,8 @@
         scores_ref[pl.ds(start, rows), :] = scores[k * rows:(k + 1) * rows]
     asked = []
     for k in range(holders):
-        notes = packed_refs[k][:, width:].astype(jnp.float32)
+        notes = packed_refs[k][:, width:] if k < holders - 2 else far_refs[k - holders + 2][...]
+        notes = notes.astype(jnp.float32)
         notes = jnp.sum(jnp.where(iota(notes.shape, 0) == me % rows, notes, 0.0), axis=0, keepdims=True)
         mine = notes[:, :capacity]
         for block in range(1, holders // rows):
@@ -317,14 +319,23 @@
     for k in range(2, holders - 2, 2):
         blocks[k] = swap(packed, "store", k)
     blocks[far] = pl.pallas_call(
-        functools.partial(late_kernel, holders, capacity, per_holder),
-        out_shape=jax.ShapeDtypeStruct(packed.shape, bf16),
-        in_specs=[VMEM] * 5,
+        late_kernel,
+        out_shape=jax.ShapeDtypeStruct((rows, width), bf16),
+        in_specs=[VMEM] * 3,
         out_specs=VMEM,
         scratch_shapes=[turned],
         compiler_params=pltpu.CompilerParams(vmem_limit_bytes=10 * 2**20 + 24 * slots * slots),
         cost_estimate=pl.CostEstimate(flops=LATE_FLOPS, bytes_accessed=8 * packed.size, transcendentals=0),
-    )(raw, far_list, in_factor, out_factor, home_here)
+    )(raw, in_factor, out_factor)
+    far_notes = pl.pallas_call(
+        functools.partial(list_kernel, holders, capacity, per_holder, rows),
+        out_shape=jax.ShapeDtypeStruct((rows, notes), bf16),
+        in_specs=[VMEM] * 2,
+        out_specs=VMEM,
+        compiler_params=pltpu.CompilerParams(vmem_limit_bytes=4 * 2**20 + 24 * slots * slots),
+        cost_estimate=pl.CostEstimate(flops=LATE_FLOPS, bytes_accessed=4 * home.size, transcendentals=0),
+    )(far_list, home_here)
+    far_notes = [far_notes, swap(far_notes, "store", 1)]
     blocks[1] = swap(again, "store", 1)
     for k in range(2, holders, 2):
         blocks[k + 1] = swap(blocks[k], "store", 1)
@@ -339,11 +350,11 @@
             jax.ShapeDtypeStruct((total, per_holder), jnp.float32),
             jax.ShapeDtypeStruct((1, slots // 2), jnp.float32),
         ],
-        in_specs=[VMEM] * (holders + 1),
+        in_specs=[VMEM] * (holders + 3),
         out_specs=[VMEM] * 3,
         scratch_shapes=[pltpu.VMEM((total, width), bf16)],
         compiler_params=pltpu.CompilerParams(vmem_limit_bytes=8 * 2**20 + 2 * bytes_in + 48 * total * slots),
-    )(*blocks[::-1], pltpu.with_memory_space_constraint(pages, pltpu.VMEM))
+    )(*blocks[::-1], *far_notes, pltpu.with_memory_space_constraint(pages, pltpu.VMEM))
 
     handed = swap(send, "store", 1)
     keep = pl.pallas_call(

time: 31.3 us -> 31.5 us (level)
    ppermute x9 -> x10, waiting for transfers between devices: 1.61 us -> 1.82 us  [swap(): lax.ppermute(value, axis, [(i, i ^ distance) for i in range(lax.axis_size...]
    pallas_call x1 -> x2, Pallas kernels: 1.19 us -> 1.38 us  [the longest x1 1 us: on_device(): pl.pallas_call(late_kernel, out_shape=jax.ShapeDtypeStruct((rows, width),...]
    ppermute x9 -> x10, starting transfers between devices: 8.9 us -> 8.9 us  [swap(): lax.ppermute(value, axis, [(i, i ^ distance) for i in range(lax.axis_size...]
  transfers between devices with their start and end apart: 15 -> 16, of which waited for: 9 -> 6; matrix products, arithmetic and copies ran while one was open for 0% -> 0% of each run, Pallas kernels for 16% -> 17%
where the time goes in v29:
time: 31.5 us; the launch traced here: 31.4 us
  starting transfers between devices  17.4 us (55%)
  Pallas kernels  6.82 us (22%)
  waiting for transfers between devices  5.68 us (18%)
  between operations  0.73 us (2%)
  other arithmetic  0.64 us (2%)
    ppermute x10, starting transfers between devices, swap(): lax.ppermute(value, axis, [(i, i ^ distance) for i in range(lax.axis_size...  8.9 us
    ppermute x3, starting transfers between devices, on_device(): lax.ppermute(terms[step], 'layer', [(g, (g + step) % groups) for g in ran...  5.57 us
    ppermute x3, starting transfers between devices, on_device(): landed.append(lax.ppermute(pair, 'store', to) if step else pair)  2.94 us
    pallas_call x1, Pallas kernels, on_device(): pl.pallas_call(functools.partial(condition_kernel, holders, capacity, per...  2.42 us
    ppermute x3, waiting for transfers between devices, on_device(): lax.ppermute(terms[step], 'layer', [(g, (g + step) % groups) for g in ran...  2.39 us
    ppermute x10, waiting for transfers between devices, swap(): lax.ppermute(value, axis, [(i, i ^ distance) for i in range(lax.axis_size...  1.82 us
    ppermute x3, waiting for transfers between devices, on_device(): landed.append(lax.ppermute(pair, 'store', to) if step else pair)  1.47 us
    pallas_call x1, Pallas kernels, on_device(): pl.pallas_call(functools.partial(score_kernel, holders, capacity), out_sh...  1.18 us
  transfers between devices with their start and end apart: 16, of which 6 were waited for; matrix products, arithmetic and copies ran while one was open for 0% of the time, Pallas kernels for 17%

profile of v29, /device:TPU:0, one launch (start us, length us, event | category | flops | bytes accessed | tf_op | source)
XLA Modules:
  0.0 31.4 jit_solution(8847466584230924248)
XLA Ops:
  0.0 0.0 copy-start
  0.0 3.9 %collective-permute-start = (bf16[8,8192]{1,0:T(8,128)(2,1)}, bf16[8,8192]{1,0:T(8,128)(2,1)S(1)}, u32[]{:S(2)}, u32[]{:S(2)}) collective-permute-start(bf16[8,8192]{1,0:T(8,128)(2,1)} %refs_0_.1), channel_id=1, source_target_pairs={{0,24},{4,28},{8,16},{12,20},{16,8},{20,12},{24,0},{28,4},{1,25},{... | collective-permute-start | bytes 393224 | tf_op jit(solution)/shard_map/ppermute | solution.py:262
  3.9 2.4 %shard_map.73 = (bf16[8,8320]{1,0:T(8,128)(2,1)S(1)}, bf16[8,8320]{1,0:T(8,128)(2,1)S(1)}, f32[8,256]{1,0:T(8,128)S(1)}, f32[2,64,64]{2,1,0:T(8,128)S(1)}, f32[2...) custom-call(bf16[8,8192]{1,0:T(8,128)(2,1)} %refs_0_.1, f32[2,64,64]{2,1,0:T(8,128)} %refs_1_.1, ...), custom_call_target="tpu_custom_call" | custom-call | tf_op jit(solution)/shard_map/pallas_call | solution.py:285
  6.3 0.6 %collective-permute-start.2 = (bf16[8,8320]{1,0:T(8,128)(2,1)S(1)}, bf16[8,8320]{1,0:T(8,128)(2,1)S(1)}, u32[]{:S(2)}, u32[]{:S(2)}) collective-permute-start(bf16[8,8320]{1,0:T(8,128)(2,1)S(1)} %get-tuple-element.28.refs_7_), channel_id=1, source_target_pairs={{0,16},{4,20},{8,24},{12,28},{16,0},{20,4},{24,8},{28,12},{1,17},{... | collective-permute-start | bytes 399368 | tf_op jit(solution)/shard_map/ppermute | solution.py:262
  6.9 0.1 collective-permute-start.4
  7.0 0.0 copy-done
  7.0 2.9 %collective-permute-start.7 = (s32[1,256]{1,0:T(1,128)S(1)}, s32[1,256]{1,0:T(1,128)S(1)}, u32[]{:S(2)}, u32[]{:S(2)}) collective-permute-start(s32[1,256]{1,0:T(1,128)S(1)} %copy-done), channel_id=1, source_target_pairs={{0,24},{4,28},{8,16},{12,20},{16,8},{20,12},{24,0},{28,4},{1,25},{... | collective-permute-start | bytes 3080 | tf_op jit(solution)/shard_map/ppermute | solution.py:262
  10.5 1.1 %shard_map.74 = (bf16[8,8320]{1,0:T(8,128)(2,1)S(1)}, bf16[8192,256]{1,0:T(8,128)(2,1)S(1)}, f32[8,256]{1,0:T(8,128)S(1)}) custom-call(s32[1]{0:T(128)S(6)} %copy.10.count_ref, f32[8,256]{1,0:T(8,128)S(1)} %get-tuple-element.22.found_ref, bf16[8,8320]{1,0:T(8,128)(2,1)S(1)} %get-tuple-element.23.block_ref, ...), custom_call_target="tpu_custom_call", output_to_operand_aliasing={{0}: (2, {})} | custom-call | bytes 4194304 | tf_op jit(solution)/shard_map/pallas_call | solution.py:303
  11.7 0.1 collective-permute-start.6
  11.8 0.0 collective-permute-done.query_ref
  11.8 1.0 %shard_map.75.refs_1_ = bf16[8,8192]{1,0:T(8,128)(2,1)S(1)} custom-call(bf16[8,8192]{1,0:T(8,128)(2,1)S(1)} %collective-permute-done.query_ref, f32[2,64,64]{2,1,0:T(8,128)S(1)} %get-tuple-element.26.in_factor_ref, f32[2,64,64]{2,1,0:T(8,128)S(1)} %get-tuple-element.27.out_factor_ref), custom_call_target="tpu_custom_call" | custom-call | flops 5000000000 | bytes 532480 | tf_op jit(solution)/shard_map/pallas_call | solution.py:321
  12.8 0.6 %collective-permute-start.1 = (bf16[8,8192]{1,0:T(8,128)(2,1)S(1)}, bf16[8,8192]{1,0:T(8,128)(2,1)S(1)}, u32[]{:S(2)}, u32[]{:S(2)}) collective-permute-start(bf16[8,8192]{1,0:T(8,128)(2,1)S(1)} %shard_map.75.refs_1_), channel_id=1, source_target_pairs={{0,4},{4,0},{8,12},{12,8},{16,20},{20,16},{24,28},{28,24},{1,5},{5... | collective-permute-start | bytes 393224 | tf_op jit(solution)/shard_map/ppermute | solution.py:262
  13.3 0.0 collective-permute-done.2.refs_3_
  13.3 0.1 collective-permute-start.3
  13.4 0.0 collective-permute-done.4.refs_5_
  13.4 0.4 %collective-permute-start.5 = (bf16[8,8320]{1,0:T(8,128)(2,1)S(1)}, bf16[8,8320]{1,0:T(8,128)(2,1)S(1)}, u32[]{:S(2)}, u32[]{:S(2)}) collective-permute-start(bf16[8,8320]{1,0:T(8,128)(2,1)S(1)} %collective-permute-done.4.refs_5_), channel_id=1, source_target_pairs={{0,4},{4,0},{8,12},{12,8},{16,20},{20,16},{24,28},{28,24},{1,5},{5... | collective-permute-start | bytes 399368 | tf_op jit(solution)/shard_map/ppermute | solution.py:262
  13.8 0.0 collective-permute-done.7.cand_ref
  13.8 0.4 %shard_map.76.refs_8_ = bf16[8,128]{1,0:T(8,128)(2,1)S(1)} custom-call(s32[1,256]{1,0:T(1,128)S(1)} %collective-permute-done.7.cand_ref, s32[16,128]{1,0:T(8,128)S(1)} %get-tuple-element.30.home_ref), custom_call_target="tpu_custom_call" | custom-call | flops 5000000000 | bytes 8192 | tf_op jit(solution)/shard_map/pallas_call | solution.py:330
  14.2 0.1 collective-permute-start.8
  14.3 1.1 %collective-permute-done.8.refs_9_ = bf16[8,128]{1,0:T(8,128)(2,1)S(1)} collective-permute-done((bf16[8,128]{1,0:T(8,128)(2,1)S(1)}, bf16[8,128]{1,0:T(8,128)(2,1)S(1)}, u32[]{:S(2)}, u32[]{:S(2)}) %collective-permute-start.8) | collective-permute-done | bytes 2080 | tf_op jit(solution)/shard_map/ppermute | solution.py:262
  15.4 0.0 collective-permute-done.6.refs_6_
  15.4 0.0 collective-permute-done.1.refs_0_
  15.4 0.0 collective-permute-done.3.refs_2_
  15.4 0.0 collective-permute-done.5.refs_4_
  15.4 1.2 %shard_map.77 = (f32[4,16,128]{2,1,0:T(8,128)S(1)}, f32[64,256]{1,0:T(8,128)S(1)}, f32[1,128]{1,0:T(1,128)S(1)}) custom-call(bf16[8,8192]{1,0:T(8,128)(2,1)S(1)} %collective-permute-done.1.refs_0_, bf16[8,8192]{1,0:T(8,128)(2,1)S(1)} %shard_map.75.refs_1_, bf16[8,8320]{1,0:T(8,128)(2,1)S(1)} %collective-permute-done.3.refs_2_, ...), custom_call_target="tpu_custom_call" | custom-call | tf_op jit(solution)/shard_map/pallas_call | solution.py:346
  16.6 0.2 collective-permute-start.9
  16.8 0.3 shard_map.78
  17.1 0.7 %collective-permute-done.9 = f32[4,16,128]{2,1,0:T(8,128)S(1)} collective-permute-done((f32[4,16,128]{2,1,0:T(8,128)S(1)}, f32[4,16,128]{2,1,0:T(8,128)S(1)}, u32[]{:S(2)}, u32[]{:S(2)}) %collective-permute-start.9) | collective-permute-done | bytes 32800 | tf_op jit(solution)/shard_map/ppermute | solution.py:262
  17.9 0.3 %collective-permute-start.12 = (f32[2,16,128]{2,1,0:T(8,128)S(1)}, f32[2,16,128]{2,1,0:T(8,128)S(1)}, u32[]{:S(2)}, u32[]{:S(2)}) collective-permute-start(f32[2,16,128]{2,1,0:T(8,128)S(1)} %pad_maximum_fusion.2), channel_id=1, source_target_pairs={{0,12},{4,8},{8,20},{12,16},{16,28},{20,24},{24,4},{28,0},{1,13},{... | collective-permute-start | bytes 49160 | tf_op jit(solution)/shard_map/ppermute | solution.py:372
  18.2 0.5 %collective-permute-start.11 = (f32[2,16,128]{2,1,0:T(8,128)S(1)}, f32[2,16,128]{2,1,0:T(8,128)S(1)}, u32[]{:S(2)}, u32[]{:S(2)}) collective-permute-start(f32[2,16,128]{2,1,0:T(8,128)S(1)} %pad_maximum_fusion.1), channel_id=1, source_target_pairs={{0,20},{4,16},{8,28},{12,24},{16,4},{20,0},{24,12},{28,8},{1,21},{... | collective-permute-start | bytes 49160 | tf_op jit(solution)/shard_map/ppermute | solution.py:372
  18.7 2.1 %collective-permute-start.10 = (f32[2,16,128]{2,1,0:T(8,128)S(1)}, f32[2,16,128]{2,1,0:T(8,128)S(1)}, u32[]{:S(2)}, u32[]{:S(2)}) collective-permute-start(f32[2,16,128]{2,1,0:T(8,128)S(1)} %pad_maximum_fusion), channel_id=1, source_target_pairs={{0,28},{4,24},{8,4},{12,0},{16,12},{20,8},{24,20},{28,16},{1,29},{... | collective-permute-start | bytes 49160 | tf_op jit(solution)/shard_map/ppermute | solution.py:372
  20.8 1.2 %collective-permute-done.12.refs_2_ = f32[2,16,128]{2,1,0:T(8,128)S(1)} collective-permute-done((f32[2,16,128]{2,1,0:T(8,128)S(1)}, f32[2,16,128]{2,1,0:T(8,128)S(1)}, u32[]{:S(2)}, u32[]{:S(2)}) %collective-permute-start.12) | collective-permute-done | bytes 16416 | tf_op jit(solution)/shard_map/ppermute | solution.py:372
  22.0 0.0 collective-permute-done.11.refs_1_
  22.0 0.2 collective-permute-done.10.refs_0_
  22.3 0.4 %shard_map.79 = (f32[32,128]{1,0:T(8,128)S(1)}, f32[32,128]{1,0:T(8,128)S(1)}, f32[32,128]{1,0:T(8,128)S(1)}, f32[32,128]{1,0:T(8,128)S(1)}) custom-call(f32[8,256]{1,0:T(8,128)S(1)} %get-tuple-element.25.found_ref, f32[2,16,128]{2,1,0:T(8,128)S(1)} %collective-permute-done.10.refs_0_, f32[2,16,128]{2,1,0:T(8,128)S(1)} %collective-permute-done.11.refs_1_, ...), custom_call_target="tpu_custom_call" | custom-call | tf_op jit(solution)/shard_map/pallas_call | solution.py:374
  22.7 1.6 %collective-permute-start.13 = (f32[32,128]{1,0:T(8,128)S(1)}, f32[32,128]{1,0:T(8,128)S(1)}, u32[]{:S(2)}, u32[]{:S(2)}) collective-permute-start(f32[32,128]{1,0:T(8,128)S(1)} %get-tuple-element.36), channel_id=1, source_target_pairs={{0,1},{1,2},{2,3},{3,0},{4,5},{5,6},{6,7},{7,4},{8,9},{9,10},{10,1... | collective-permute-start | bytes 49160 | tf_op jit(solution)/shard_map/ppermute | solution.py:383
  24.4 2.6 %collective-permute-start.14 = (f32[32,128]{1,0:T(8,128)S(1)}, f32[32,128]{1,0:T(8,128)S(1)}, u32[]{:S(2)}, u32[]{:S(2)}) collective-permute-start(f32[32,128]{1,0:T(8,128)S(1)} %get-tuple-element.37), channel_id=1, source_target_pairs={{0,2},{1,3},{2,0},{3,1},{4,6},{5,7},{6,4},{7,5},{8,10},{9,11},{10,... | collective-permute-start | bytes 49160 | tf_op jit(solution)/shard_map/ppermute | solution.py:383
  27.0 1.4 %collective-permute-start.15 = (f32[32,128]{1,0:T(8,128)S(1)}, f32[32,128]{1,0:T(8,128)S(1)}, u32[]{:S(2)}, u32[]{:S(2)}) collective-permute-start(f32[32,128]{1,0:T(8,128)S(1)} %get-tuple-element.38), channel_id=1, source_target_pairs={{0,3},{1,0},{2,1},{3,2},{4,7},{5,4},{6,5},{7,6},{8,11},{9,8},{10,9... | collective-permute-start | bytes 49160 | tf_op jit(solution)/shard_map/ppermute | solution.py:383
  28.3 0.0 collective-permute-done.13
  28.3 0.7 %collective-permute-done.14 = f32[32,128]{1,0:T(8,128)S(1)} collective-permute-done((f32[32,128]{1,0:T(8,128)S(1)}, f32[32,128]{1,0:T(8,128)S(1)}, u32[]{:S(2)}, u32[]{:S(2)}) %collective-permute-start.14) | collective-permute-done | bytes 16416 | tf_op jit(solution)/shard_map/ppermute | solution.py:383
  29.0 1.7 %collective-permute-done.15 = f32[32,128]{1,0:T(8,128)S(1)} collective-permute-done((f32[32,128]{1,0:T(8,128)S(1)}, f32[32,128]{1,0:T(8,128)S(1)}, u32[]{:S(2)}, u32[]{:S(2)}) %collective-permute-start.15) | collective-permute-done | bytes 16416 | tf_op jit(solution)/shard_map/ppermute | solution.py:383
  30.7 0.1 fusion.2
  30.8 0.6 %maximum_bitcast_fusion = f32[1,64,64]{2,1,0:T(8,128)} fusion(f32[32,64]{1,0:T(8,128)S(1)} %get-tuple-element.48, f32[32,64]{1,0:T(8,128)S(1)} %get-tuple-element.47), kind=kLoop, calls=%fused_computation | loop fusion | flops 4096 | bytes 32768 | tf_op jit(solution)/shard_map/broadcast_in_dim | solution.py:384
  (7 shorter events, 0.1 us)
Async XLA Ops:
  0.0 7.0 %copy-start = (s32[1,256]{1,0:T(1,128)S(1)}, s32[1,256]{1,0:T(1,128)}, u32[]{:S(2)}) copy-start(s32[1,256]{1,0:T(1,128)} %refs_4_.1) | copy-start | bytes 3076
  0.0 11.8 %collective-permute-start = (bf16[8,8192]{1,0:T(8,128)(2,1)}, bf16[8,8192]{1,0:T(8,128)(2,1)S(1)}, u32[]{:S(2)}, u32[]{:S(2)}) collective-permute-start(bf16[8,8192]{1,0:T(8,128)(2,1)} %refs_0_.1), channel_id=1, source_target_pairs={{0,24},{4,28},{8,16},{12,20},{16,8},{20,12},{24,0},{28,4},{1,25},{... | collective-permute-start | bytes 393224 | tf_op jit(solution)/shard_map/ppermute | solution.py:262
  6.3 7.0 %collective-permute-start.2 = (bf16[8,8320]{1,0:T(8,128)(2,1)S(1)}, bf16[8,8320]{1,0:T(8,128)(2,1)S(1)}, u32[]{:S(2)}, u32[]{:S(2)}) collective-permute-start(bf16[8,8320]{1,0:T(8,128)(2,1)S(1)} %get-tuple-element.28.refs_7_), channel_id=1, source_target_pairs={{0,16},{4,20},{8,24},{12,28},{16,0},{20,4},{24,8},{28,12},{1,17},{... | collective-permute-start | bytes 399368 | tf_op jit(solution)/shard_map/ppermute | solution.py:262
  6.9 6.5 %collective-permute-start.4 = (bf16[8,8320]{1,0:T(8,128)(2,1)S(1)}, bf16[8,8320]{1,0:T(8,128)(2,1)S(1)}, u32[]{:S(2)}, u32[]{:S(2)}) collective-permute-start(bf16[8,8320]{1,0:T(8,128)(2,1)S(1)} %get-tuple-element.28.refs_7_), channel_id=1, source_target_pairs={{0,8},{4,12},{8,0},{12,4},{16,24},{20,28},{24,16},{28,20},{1,9},{5... | collective-permute-start | bytes 399368 | tf_op jit(solution)/shard_map/ppermute | solution.py:262
  7.0 6.8 %collective-permute-start.7 = (s32[1,256]{1,0:T(1,128)S(1)}, s32[1,256]{1,0:T(1,128)S(1)}, u32[]{:S(2)}, u32[]{:S(2)}) collective-permute-start(s32[1,256]{1,0:T(1,128)S(1)} %copy-done), channel_id=1, source_target_pairs={{0,24},{4,28},{8,16},{12,20},{16,8},{20,12},{24,0},{28,4},{1,25},{... | collective-permute-start | bytes 3080 | tf_op jit(solution)/shard_map/ppermute | solution.py:262
  11.7 3.7 %collective-permute-start.6 = (bf16[8,8320]{1,0:T(8,128)(2,1)S(1)}, bf16[8,8320]{1,0:T(8,128)(2,1)S(1)}, u32[]{:S(2)}, u32[]{:S(2)}) collective-permute-start(bf16[8,8320]{1,0:T(8,128)(2,1)S(1)} %get-tuple-element.29), channel_id=1, source_target_pairs={{0,4},{4,0},{8,12},{12,8},{16,20},{20,16},{24,28},{28,24},{1,5},{5... | collective-permute-start | bytes 399368 | tf_op jit(solution)/shard_map/ppermute | solution.py:262
  12.8 2.6 %collective-permute-start.1 = (bf16[8,8192]{1,0:T(8,128)(2,1)S(1)}, bf16[8,8192]{1,0:T(8,128)(2,1)S(1)}, u32[]{:S(2)}, u32[]{:S(2)}) collective-permute-start(bf16[8,8192]{1,0:T(8,128)(2,1)S(1)} %shard_map.75.refs_1_), channel_id=1, source_target_pairs={{0,4},{4,0},{8,12},{12,8},{16,20},{20,16},{24,28},{28,24},{1,5},{5... | collective-permute-start | bytes 393224 | tf_op jit(solution)/shard_map/ppermute | solution.py:262
  13.3 2.1 %collective-permute-start.3 = (bf16[8,8320]{1,0:T(8,128)(2,1)S(1)}, bf16[8,8320]{1,0:T(8,128)(2,1)S(1)}, u32[]{:S(2)}, u32[]{:S(2)}) collective-permute-start(bf16[8,8320]{1,0:T(8,128)(2,1)S(1)} %collective-permute-done.2.refs_3_), channel_id=1, source_target_pairs={{0,4},{4,0},{8,12},{12,8},{16,20},{20,16},{24,28},{28,24},{1,5},{5... | collective-permute-start | bytes 399368 | tf_op jit(solution)/shard_map/ppermute | solution.py:262
  13.4 2.0 %collective-permute-start.5 = (bf16[8,8320]{1,0:T(8,128)(2,1)S(1)}, bf16[8,8320]{1,0:T(8,128)(2,1)S(1)}, u32[]{:S(2)}, u32[]{:S(2)}) collective-permute-start(bf16[8,8320]{1,0:T(8,128)(2,1)S(1)} %collective-permute-done.4.refs_5_), channel_id=1, source_target_pairs={{0,4},{4,0},{8,12},{12,8},{16,20},{20,16},{24,28},{28,24},{1,5},{5... | collective-permute-start | bytes 399368 | tf_op jit(solution)/shard_map/ppermute | solution.py:262
  14.2 1.2 %collective-permute-start.8 = (bf16[8,128]{1,0:T(8,128)(2,1)S(1)}, bf16[8,128]{1,0:T(8,128)(2,1)S(1)}, u32[]{:S(2)}, u32[]{:S(2)}) collective-permute-start(bf16[8,128]{1,0:T(8,128)(2,1)S(1)} %shard_map.76.refs_8_), channel_id=1, source_target_pairs={{0,4},{4,0},{8,12},{12,8},{16,20},{20,16},{24,28},{28,24},{1,5},{5... | collective-permute-start | bytes 6152 | tf_op jit(solution)/shard_map/ppermute | solution.py:262
  16.6 1.3 %collective-permute-start.9 = (f32[4,16,128]{2,1,0:T(8,128)S(1)}, f32[4,16,128]{2,1,0:T(8,128)S(1)}, u32[]{:S(2)}, u32[]{:S(2)}) collective-permute-start(f32[4,16,128]{2,1,0:T(8,128)S(1)} %get-tuple-element.34), channel_id=1, source_target_pairs={{0,4},{4,0},{8,12},{12,8},{16,20},{20,16},{24,28},{28,24},{1,5},{5... | collective-permute-start | bytes 98312 | tf_op jit(solution)/shard_map/ppermute | solution.py:262
  17.9 4.2 %collective-permute-start.12 = (f32[2,16,128]{2,1,0:T(8,128)S(1)}, f32[2,16,128]{2,1,0:T(8,128)S(1)}, u32[]{:S(2)}, u32[]{:S(2)}) collective-permute-start(f32[2,16,128]{2,1,0:T(8,128)S(1)} %pad_maximum_fusion.2), channel_id=1, source_target_pairs={{0,12},{4,8},{8,20},{12,16},{16,28},{20,24},{24,4},{28,0},{1,13},{... | collective-permute-start | bytes 49160 | tf_op jit(solution)/shard_map/ppermute | solution.py:372
  18.2 3.9 %collective-permute-start.11 = (f32[2,16,128]{2,1,0:T(8,128)S(1)}, f32[2,16,128]{2,1,0:T(8,128)S(1)}, u32[]{:S(2)}, u32[]{:S(2)}) collective-permute-start(f32[2,16,128]{2,1,0:T(8,128)S(1)} %pad_maximum_fusion.1), channel_id=1, source_target_pairs={{0,20},{4,16},{8,28},{12,24},{16,4},{20,0},{24,12},{28,8},{1,21},{... | collective-permute-start | bytes 49160 | tf_op jit(solution)/shard_map/ppermute | solution.py:372
  18.7 3.6 %collective-permute-start.10 = (f32[2,16,128]{2,1,0:T(8,128)S(1)}, f32[2,16,128]{2,1,0:T(8,128)S(1)}, u32[]{:S(2)}, u32[]{:S(2)}) collective-permute-start(f32[2,16,128]{2,1,0:T(8,128)S(1)} %pad_maximum_fusion), channel_id=1, source_target_pairs={{0,28},{4,24},{8,4},{12,0},{16,12},{20,8},{24,20},{28,16},{1,29},{... | collective-permute-start | bytes 49160 | tf_op jit(solution)/shard_map/ppermute | solution.py:372
  22.7 5.6 %collective-permute-start.13 = (f32[32,128]{1,0:T(8,128)S(1)}, f32[32,128]{1,0:T(8,128)S(1)}, u32[]{:S(2)}, u32[]{:S(2)}) collective-permute-start(f32[32,128]{1,0:T(8,128)S(1)} %get-tuple-element.36), channel_id=1, source_target_pairs={{0,1},{1,2},{2,3},{3,0},{4,5},{5,6},{6,7},{7,4},{8,9},{9,10},{10,1... | collective-permute-start | bytes 49160 | tf_op jit(solution)/shard_map/ppermute | solution.py:383
  24.4 4.6 %collective-permute-start.14 = (f32[32,128]{1,0:T(8,128)S(1)}, f32[32,128]{1,0:T(8,128)S(1)}, u32[]{:S(2)}, u32[]{:S(2)}) collective-permute-start(f32[32,128]{1,0:T(8,128)S(1)} %get-tuple-element.37), channel_id=1, source_target_pairs={{0,2},{1,3},{2,0},{3,1},{4,6},{5,7},{6,4},{7,5},{8,10},{9,11},{10,... | collective-permute-start | bytes 49160 | tf_op jit(solution)/shard_map/ppermute | solution.py:383
  27.0 3.7 %collective-permute-start.15 = (f32[32,128]{1,0:T(8,128)S(1)}, f32[32,128]{1,0:T(8,128)S(1)}, u32[]{:S(2)}, u32[]{:S(2)}) collective-permute-start(f32[32,128]{1,0:T(8,128)S(1)} %get-tuple-element.38), channel_id=1, source_target_pairs={{0,3},{1,0},{2,1},{3,2},{4,7},{5,4},{6,5},{7,6},{8,11},{9,8},{10,9... | collective-permute-start | bytes 49160 | tf_op jit(solution)/shard_map/ppermute | solution.py:383

commit v30 on v29

--- a/solution.py
+++ b/solution.py
@@ -156,10 +156,7 @@
     notes_ref[...] = look_up(holders, capacity, per_holder, rows, cand_ref, home_ref)[0]
 
 
-def load_kernel(holders, count_ref, found_ref, block_ref, source_ref, same_block_ref, target_ref, used_ref):
-    used_ref[...] = found_ref[...]
-    slots = found_ref.shape[1]
-    used_ref[0:1] = jnp.where(iota((1, slots), 1) < count_ref[0], found_ref[0:1], float(holders))
+def load_kernel(block_ref, source_ref, same_block_ref, target_ref):
     step = source_ref.shape[1] // LOADS
     for i in range(LOADS):
         target_ref[i * step:(i + 1) * step, :] = source_ref[:, i * step:(i + 1) * step].T
@@ -225,7 +222,7 @@
         keep_ref[place] = picked[place * half:(place + 1) * half]
 
 
-def spread_kernel(holders, groups, found_ref, *refs):
+def spread_kernel(holders, groups, count_ref, found_ref, *refs):
     landed_refs, out_refs = refs[:holders // 2][::-1], refs[holders // 2:]
     half = landed_refs[0].shape[1]
     slots = found_ref.shape[1]
@@ -238,7 +235,8 @@
     step = (me // 2 - holder // 2 + 2 * chips) % chips
     same_core = (holder % 2 == me % 2).astype(jnp.int32)
     place = 2 * step + jnp.where(step == 0, 1 - same_core, same_core)
-    begins = jnp.where(holder < holders, place * half, -1).astype(jnp.float32)
+    used = iota((1, slots), 1) < count_ref[0]
+    begins = jnp.where(used, place * half, -1).astype(jnp.float32)
     rank_there = found_ref[1:2]
     place = iota((2 * holders * half, slots), 0).astype(jnp.float32)
     upper = rank_there >= half
@@ -300,19 +298,15 @@
         compiler_params=pltpu.CompilerParams(vmem_limit_bytes=14 * 2**20 + 24 * slots * slots),
     )(*sources)
 
-    again, pages, used = pl.pallas_call(
-        functools.partial(load_kernel, holders),
-        out_shape=[
-            jax.ShapeDtypeStruct(again.shape, bf16),
-            pltpu.VMEM((width, per_holder), bf16),
-            jax.ShapeDtypeStruct(found.shape, jnp.float32),
-        ],
-        in_specs=[SMEM, VMEM, VMEM, VMEM],
-        out_specs=[VMEM] * 3,
-        input_output_aliases={2: 0},
+    again, pages = pl.pallas_call(
+        load_kernel,
+        out_shape=[jax.ShapeDtypeStruct(again.shape, bf16), pltpu.VMEM((width, per_holder), bf16)],
+        in_specs=[VMEM] * 2,
+        out_specs=[VMEM] * 2,
+        input_output_aliases={0: 0},
         compiler_params=pltpu.CompilerParams(vmem_limit_bytes=4 * 2**20 + 4 * per_holder * width),
         cost_estimate=pl.CostEstimate(flops=0, bytes_accessed=2 * page_store.size, transcendentals=0),
-    )(counts, found, again, pltpu.with_memory_space_constraint(pages, pltpu.VMEM))
+    )(again, pltpu.with_memory_space_constraint(pages, pltpu.VMEM))
 
     blocks = [None] * holders
     blocks[0] = packed
@@ -374,10 +368,10 @@
     terms = pl.pallas_call(
         functools.partial(spread_kernel, holders, groups),
         out_shape=[jax.ShapeDtypeStruct((share // 2, 2 * total), jnp.float32)] * groups,
-        in_specs=[VMEM] * (1 + len(landed)),
+        in_specs=[SMEM] + [VMEM] * (1 + len(landed)),
         out_specs=[VMEM] * groups,
         compiler_params=pltpu.CompilerParams(vmem_limit_bytes=4 * 2**20 + 64 * total * slots),
-    )(used, *landed[::-1])
+    )(counts, found, *landed[::-1])
     summed = terms[0]
     for step in range(1, groups):
         summed = summed + lax.ppermute(terms[step], "layer", [(g, (g + step) % groups) for g in range(groups)])

time: 31.5 us -> 31.1 us (0.987)
  waiting for transfers between devices: 5.68 us -> 5.18 us
    ppermute x10, waiting for transfers between devices: 1.82 us -> 1.17 us  [swap(): lax.ppermute(value, axis, [(i, i ^ distance) for i in range(lax.axis_size...]
where the time goes in v30:
time: 31.1 us; the launch traced here: 30.9 us
  starting transfers between devices  17.4 us (56%)
  Pallas kernels  6.82 us (22%)
  waiting for transfers between devices  5.18 us (17%)
  between operations  0.73 us (2%)
  other arithmetic  0.64 us (2%)
    ppermute x10, starting transfers between devices, swap(): lax.ppermute(value, axis, [(i, i ^ distance) for i in range(lax.axis_size...  8.91 us
    ppermute x3, starting transfers between devices, on_device(): lax.ppermute(terms[step], 'layer', [(g, (g + step) % groups) for g in ran...  5.57 us
    ppermute x3, starting transfers between devices, on_device(): landed.append(lax.ppermute(pair, 'store', to) if step else pair)  2.98 us
    pallas_call x1, Pallas kernels, on_device(): pl.pallas_call(functools.partial(condition_kernel, holders, capacity, per...  2.42 us
    ppermute x3, waiting for transfers between devices, on_device(): lax.ppermute(terms[step], 'layer', [(g, (g + step) % groups) for g in ran...  2.39 us
    ppermute x3, waiting for transfers between devices, on_device(): landed.append(lax.ppermute(pair, 'store', to) if step else pair)  1.63 us
    pallas_call x1, Pallas kernels, on_device(): pl.pallas_call(functools.partial(score_kernel, holders, capacity), out_sh...  1.18 us
    ppermute x10, waiting for transfers between devices, swap(): lax.ppermute(value, axis, [(i, i ^ distance) for i in range(lax.axis_size...  1.17 us
  transfers between devices with their start and end apart: 16, of which 6 were waited for; matrix products, arithmetic and copies ran while one was open for 0% of the time, Pallas kernels for 17%

profile of v30, /device:TPU:0, one launch (start us, length us, event | category | flops | bytes accessed | tf_op | source)
XLA Modules:
  0.0 30.9 jit_solution(5488279913056797227)
XLA Ops:
  0.0 0.0 copy-start
  0.0 3.9 %collective-permute-start = (bf16[8,8192]{1,0:T(8,128)(2,1)}, bf16[8,8192]{1,0:T(8,128)(2,1)S(1)}, u32[]{:S(2)}, u32[]{:S(2)}) collective-permute-start(bf16[8,8192]{1,0:T(8,128)(2,1)} %refs_0_.1), channel_id=1, source_target_pairs={{0,24},{4,28},{8,16},{12,20},{16,8},{20,12},{24,0},{28,4},{1,25},{... | collective-permute-start | bytes 393224 | tf_op jit(solution)/shard_map/ppermute | solution.py:260
  3.9 2.4 %shard_map.73 = (bf16[8,8320]{1,0:T(8,128)(2,1)S(1)}, bf16[8,8320]{1,0:T(8,128)(2,1)S(1)}, f32[8,256]{1,0:T(8,128)S(1)}, f32[2,64,64]{2,1,0:T(8,128)S(1)}, f32[2...) custom-call(bf16[8,8192]{1,0:T(8,128)(2,1)} %refs_0_.1, f32[2,64,64]{2,1,0:T(8,128)} %refs_1_.1, ...), custom_call_target="tpu_custom_call" | custom-call | tf_op jit(solution)/shard_map/pallas_call | solution.py:283
  6.3 0.6 %collective-permute-start.2 = (bf16[8,8320]{1,0:T(8,128)(2,1)S(1)}, bf16[8,8320]{1,0:T(8,128)(2,1)S(1)}, u32[]{:S(2)}, u32[]{:S(2)}) collective-permute-start(bf16[8,8320]{1,0:T(8,128)(2,1)S(1)} %get-tuple-element.24.refs_7_), channel_id=1, source_target_pairs={{0,16},{4,20},{8,24},{12,28},{16,0},{20,4},{24,8},{28,12},{1,17},{... | collective-permute-start | bytes 399368 | tf_op jit(solution)/shard_map/ppermute | solution.py:260
  6.9 0.1 collective-permute-start.4
  7.0 0.0 copy-done
  7.0 2.9 %collective-permute-start.7 = (s32[1,256]{1,0:T(1,128)S(1)}, s32[1,256]{1,0:T(1,128)S(1)}, u32[]{:S(2)}, u32[]{:S(2)}) collective-permute-start(s32[1,256]{1,0:T(1,128)S(1)} %copy-done), channel_id=1, source_target_pairs={{0,24},{4,28},{8,16},{12,20},{16,8},{20,12},{24,0},{28,4},{1,25},{... | collective-permute-start | bytes 3080 | tf_op jit(solution)/shard_map/ppermute | solution.py:260
  9.9 1.1 %shard_map.75 = (bf16[8,8320]{1,0:T(8,128)(2,1)S(1)}, bf16[8192,256]{1,0:T(8,128)(2,1)S(1)}) custom-call(bf16[8,8320]{1,0:T(8,128)(2,1)S(1)} %get-tuple-element.25.block_ref, bf16[256,8192]{1,0:T(8,128)(2,1)S(1)} %get-tuple-element.26.source_ref), custom_call_target="tpu_custom_call", output_to_operand_aliasing={{0}: (0, {})} | custom-call | bytes 4194304 | tf_op jit(solution)/shard_map/pallas_call | solution.py:301
  11.0 0.1 collective-permute-start.6
  11.1 0.0 collective-permute-done.query_ref
  11.1 1.0 %shard_map.74.refs_1_ = bf16[8,8192]{1,0:T(8,128)(2,1)S(1)} custom-call(bf16[8,8192]{1,0:T(8,128)(2,1)S(1)} %collective-permute-done.query_ref, f32[2,64,64]{2,1,0:T(8,128)S(1)} %get-tuple-element.22.in_factor_ref, f32[2,64,64]{2,1,0:T(8,128)S(1)} %get-tuple-element.23.out_factor_ref), custom_call_target="tpu_custom_call" | custom-call | flops 5000000000 | bytes 532480 | tf_op jit(solution)/shard_map/pallas_call | solution.py:315
  12.1 0.6 %collective-permute-start.1 = (bf16[8,8192]{1,0:T(8,128)(2,1)S(1)}, bf16[8,8192]{1,0:T(8,128)(2,1)S(1)}, u32[]{:S(2)}, u32[]{:S(2)}) collective-permute-start(bf16[8,8192]{1,0:T(8,128)(2,1)S(1)} %shard_map.74.refs_1_), channel_id=1, source_target_pairs={{0,4},{4,0},{8,12},{12,8},{16,20},{20,16},{24,28},{28,24},{1,5},{5... | collective-permute-start | bytes 393224 | tf_op jit(solution)/shard_map/ppermute | solution.py:260
  12.7 0.0 collective-permute-done.2.refs_3_
  12.7 0.1 collective-permute-start.3
  12.8 0.0 collective-permute-done.4.refs_5_
  12.8 0.4 %collective-permute-start.5 = (bf16[8,8320]{1,0:T(8,128)(2,1)S(1)}, bf16[8,8320]{1,0:T(8,128)(2,1)S(1)}, u32[]{:S(2)}, u32[]{:S(2)}) collective-permute-start(bf16[8,8320]{1,0:T(8,128)(2,1)S(1)} %collective-permute-done.4.refs_5_), channel_id=1, source_target_pairs={{0,4},{4,0},{8,12},{12,8},{16,20},{20,16},{24,28},{28,24},{1,5},{5... | collective-permute-start | bytes 399368 | tf_op jit(solution)/shard_map/ppermute | solution.py:260
  13.2 0.0 collective-permute-done.7.cand_ref
  13.2 0.4 %shard_map.76.refs_8_ = bf16[8,128]{1,0:T(8,128)(2,1)S(1)} custom-call(s32[1,256]{1,0:T(1,128)S(1)} %collective-permute-done.7.cand_ref, s32[16,128]{1,0:T(8,128)S(1)} %get-tuple-element.28.home_ref), custom_call_target="tpu_custom_call" | custom-call | flops 5000000000 | bytes 8192 | tf_op jit(solution)/shard_map/pallas_call | solution.py:324
  13.6 0.1 collective-permute-start.8
  14.3 0.4 %collective-permute-done.8.refs_9_ = bf16[8,128]{1,0:T(8,128)(2,1)S(1)} collective-permute-done((bf16[8,128]{1,0:T(8,128)(2,1)S(1)}, bf16[8,128]{1,0:T(8,128)(2,1)S(1)}, u32[]{:S(2)}, u32[]{:S(2)}) %collective-permute-start.8) | collective-permute-done | bytes 2080 | tf_op jit(solution)/shard_map/ppermute | solution.py:260
  14.8 0.0 collective-permute-done.6.refs_6_
  14.8 0.0 collective-permute-done.1.refs_0_
  14.8 0.0 collective-permute-done.3.refs_2_
  14.8 0.0 collective-permute-done.5.refs_4_
  14.8 1.2 %shard_map.77 = (f32[4,16,128]{2,1,0:T(8,128)S(1)}, f32[64,256]{1,0:T(8,128)S(1)}, f32[1,128]{1,0:T(1,128)S(1)}) custom-call(bf16[8,8192]{1,0:T(8,128)(2,1)S(1)} %collective-permute-done.1.refs_0_, bf16[8,8192]{1,0:T(8,128)(2,1)S(1)} %shard_map.74.refs_1_, bf16[8,8320]{1,0:T(8,128)(2,1)S(1)} %collective-permute-done.3.refs_2_, ...), custom_call_target="tpu_custom_call" | custom-call | tf_op jit(solution)/shard_map/pallas_call | solution.py:340
  16.0 0.2 collective-permute-start.9
  16.2 0.3 shard_map.78
  16.5 0.7 %collective-permute-done.9 = f32[4,16,128]{2,1,0:T(8,128)S(1)} collective-permute-done((f32[4,16,128]{2,1,0:T(8,128)S(1)}, f32[4,16,128]{2,1,0:T(8,128)S(1)}, u32[]{:S(2)}, u32[]{:S(2)}) %collective-permute-start.9) | collective-permute-done | bytes 32800 | tf_op jit(solution)/shard_map/ppermute | solution.py:260
  17.2 0.3 %collective-permute-start.12 = (f32[2,16,128]{2,1,0:T(8,128)S(1)}, f32[2,16,128]{2,1,0:T(8,128)S(1)}, u32[]{:S(2)}, u32[]{:S(2)}) collective-permute-start(f32[2,16,128]{2,1,0:T(8,128)S(1)} %pad_maximum_fusion.2), channel_id=1, source_target_pairs={{0,12},{4,8},{8,20},{12,16},{16,28},{20,24},{24,4},{28,0},{1,13},{... | collective-permute-start | bytes 49160 | tf_op jit(solution)/shard_map/ppermute | solution.py:366
  17.5 1.1 %collective-permute-start.11 = (f32[2,16,128]{2,1,0:T(8,128)S(1)}, f32[2,16,128]{2,1,0:T(8,128)S(1)}, u32[]{:S(2)}, u32[]{:S(2)}) collective-permute-start(f32[2,16,128]{2,1,0:T(8,128)S(1)} %pad_maximum_fusion.1), channel_id=1, source_target_pairs={{0,20},{4,16},{8,28},{12,24},{16,4},{20,0},{24,12},{28,8},{1,21},{... | collective-permute-start | bytes 49160 | tf_op jit(solution)/shard_map/ppermute | solution.py:366
  18.7 1.5 %collective-permute-start.10 = (f32[2,16,128]{2,1,0:T(8,128)S(1)}, f32[2,16,128]{2,1,0:T(8,128)S(1)}, u32[]{:S(2)}, u32[]{:S(2)}) collective-permute-start(f32[2,16,128]{2,1,0:T(8,128)S(1)} %pad_maximum_fusion), channel_id=1, source_target_pairs={{0,28},{4,24},{8,4},{12,0},{16,12},{20,8},{24,20},{28,16},{1,29},{... | collective-permute-start | bytes 49160 | tf_op jit(solution)/shard_map/ppermute | solution.py:366
  20.2 1.2 %collective-permute-done.12.refs_2_ = f32[2,16,128]{2,1,0:T(8,128)S(1)} collective-permute-done((f32[2,16,128]{2,1,0:T(8,128)S(1)}, f32[2,16,128]{2,1,0:T(8,128)S(1)}, u32[]{:S(2)}, u32[]{:S(2)}) %collective-permute-start.12) | collective-permute-done | bytes 16416 | tf_op jit(solution)/shard_map/ppermute | solution.py:366
  21.4 0.0 collective-permute-done.11.refs_1_
  21.4 0.4 %collective-permute-done.10.refs_0_ = f32[2,16,128]{2,1,0:T(8,128)S(1)} collective-permute-done((f32[2,16,128]{2,1,0:T(8,128)S(1)}, f32[2,16,128]{2,1,0:T(8,128)S(1)}, u32[]{:S(2)}, u32[]{:S(2)}) %collective-permute-start.10) | collective-permute-done | bytes 16416 | tf_op jit(solution)/shard_map/ppermute | solution.py:366
  21.8 0.4 %shard_map.79 = (f32[32,128]{1,0:T(8,128)S(1)}, f32[32,128]{1,0:T(8,128)S(1)}, f32[32,128]{1,0:T(8,128)S(1)}, f32[32,128]{1,0:T(8,128)S(1)}) custom-call(s32[1]{0:T(128)S(6)} %copy.10.count_ref, f32[8,256]{1,0:T(8,128)S(1)} %get-tuple-element.21.found_ref, f32[2,16,128]{2,1,0:T(8,128)S(1)} %collective-permute-done.10.refs_0_, ...), custom_call_target="tpu_custom_call" | custom-call | tf_op jit(solution)/shard_map/pallas_call | solution.py:368
  22.3 1.6 %collective-permute-start.13 = (f32[32,128]{1,0:T(8,128)S(1)}, f32[32,128]{1,0:T(8,128)S(1)}, u32[]{:S(2)}, u32[]{:S(2)}) collective-permute-start(f32[32,128]{1,0:T(8,128)S(1)} %get-tuple-element.34), channel_id=1, source_target_pairs={{0,1},{1,2},{2,3},{3,0},{4,5},{5,6},{6,7},{7,4},{8,9},{9,10},{10,1... | collective-permute-start | bytes 49160 | tf_op jit(solution)/shard_map/ppermute | solution.py:377
  23.9 2.6 %collective-permute-start.14 = (f32[32,128]{1,0:T(8,128)S(1)}, f32[32,128]{1,0:T(8,128)S(1)}, u32[]{:S(2)}, u32[]{:S(2)}) collective-permute-start(f32[32,128]{1,0:T(8,128)S(1)} %get-tuple-element.35), channel_id=1, source_target_pairs={{0,2},{1,3},{2,0},{3,1},{4,6},{5,7},{6,4},{7,5},{8,10},{9,11},{10,... | collective-permute-start | bytes 49160 | tf_op jit(solution)/shard_map/ppermute | solution.py:377
  26.5 1.3 %collective-permute-start.15 = (f32[32,128]{1,0:T(8,128)S(1)}, f32[32,128]{1,0:T(8,128)S(1)}, u32[]{:S(2)}, u32[]{:S(2)}) collective-permute-start(f32[32,128]{1,0:T(8,128)S(1)} %get-tuple-element.36), channel_id=1, source_target_pairs={{0,3},{1,0},{2,1},{3,2},{4,7},{5,4},{6,5},{7,6},{8,11},{9,8},{10,9... | collective-permute-start | bytes 49160 | tf_op jit(solution)/shard_map/ppermute | solution.py:377
  27.8 0.0 collective-permute-done.13
  27.9 0.9 %collective-permute-done.14 = f32[32,128]{1,0:T(8,128)S(1)} collective-permute-done((f32[32,128]{1,0:T(8,128)S(1)}, f32[32,128]{1,0:T(8,128)S(1)}, u32[]{:S(2)}, u32[]{:S(2)}) %collective-permute-start.14) | collective-permute-done | bytes 16416 | tf_op jit(solution)/shard_map/ppermute | solution.py:377
  28.8 1.4 %collective-permute-done.15 = f32[32,128]{1,0:T(8,128)S(1)} collective-permute-done((f32[32,128]{1,0:T(8,128)S(1)}, f32[32,128]{1,0:T(8,128)S(1)}, u32[]{:S(2)}, u32[]{:S(2)}) %collective-permute-start.15) | collective-permute-done | bytes 16416 | tf_op jit(solution)/shard_map/ppermute | solution.py:377
  30.2 0.1 fusion.2
  30.3 0.6 %maximum_bitcast_fusion = f32[1,64,64]{2,1,0:T(8,128)} fusion(f32[32,64]{1,0:T(8,128)S(1)} %get-tuple-element.46, f32[32,64]{1,0:T(8,128)S(1)} %get-tuple-element.45), kind=kLoop, calls=%fused_computation | loop fusion | flops 4096 | bytes 32768 | tf_op jit(solution)/shard_map/broadcast_in_dim | solution.py:378
  (7 shorter events, 0.1 us)
Async XLA Ops:
  0.0 7.0 %copy-start = (s32[1,256]{1,0:T(1,128)S(1)}, s32[1,256]{1,0:T(1,128)}, u32[]{:S(2)}) copy-start(s32[1,256]{1,0:T(1,128)} %refs_4_.1) | copy-start | bytes 3076
  0.0 11.1 %collective-permute-start = (bf16[8,8192]{1,0:T(8,128)(2,1)}, bf16[8,8192]{1,0:T(8,128)(2,1)S(1)}, u32[]{:S(2)}, u32[]{:S(2)}) collective-permute-start(bf16[8,8192]{1,0:T(8,128)(2,1)} %refs_0_.1), channel_id=1, source_target_pairs={{0,24},{4,28},{8,16},{12,20},{16,8},{20,12},{24,0},{28,4},{1,25},{... | collective-permute-start | bytes 393224 | tf_op jit(solution)/shard_map/ppermute | solution.py:260
  6.3 6.4 %collective-permute-start.2 = (bf16[8,8320]{1,0:T(8,128)(2,1)S(1)}, bf16[8,8320]{1,0:T(8,128)(2,1)S(1)}, u32[]{:S(2)}, u32[]{:S(2)}) collective-permute-start(bf16[8,8320]{1,0:T(8,128)(2,1)S(1)} %get-tuple-element.24.refs_7_), channel_id=1, source_target_pairs={{0,16},{4,20},{8,24},{12,28},{16,0},{20,4},{24,8},{28,12},{1,17},{... | collective-permute-start | bytes 399368 | tf_op jit(solution)/shard_map/ppermute | solution.py:260
  6.9 5.9 %collective-permute-start.4 = (bf16[8,8320]{1,0:T(8,128)(2,1)S(1)}, bf16[8,8320]{1,0:T(8,128)(2,1)S(1)}, u32[]{:S(2)}, u32[]{:S(2)}) collective-permute-start(bf16[8,8320]{1,0:T(8,128)(2,1)S(1)} %get-tuple-element.24.refs_7_), channel_id=1, source_target_pairs={{0,8},{4,12},{8,0},{12,4},{16,24},{20,28},{24,16},{28,20},{1,9},{5... | collective-permute-start | bytes 399368 | tf_op jit(solution)/shard_map/ppermute | solution.py:260
  7.0 6.2 %collective-permute-start.7 = (s32[1,256]{1,0:T(1,128)S(1)}, s32[1,256]{1,0:T(1,128)S(1)}, u32[]{:S(2)}, u32[]{:S(2)}) collective-permute-start(s32[1,256]{1,0:T(1,128)S(1)} %copy-done), channel_id=1, source_target_pairs={{0,24},{4,28},{8,16},{12,20},{16,8},{20,12},{24,0},{28,4},{1,25},{... | collective-permute-start | bytes 3080 | tf_op jit(solution)/shard_map/ppermute | solution.py:260
  11.0 3.7 %collective-permute-start.6 = (bf16[8,8320]{1,0:T(8,128)(2,1)S(1)}, bf16[8,8320]{1,0:T(8,128)(2,1)S(1)}, u32[]{:S(2)}, u32[]{:S(2)}) collective-permute-start(bf16[8,8320]{1,0:T(8,128)(2,1)S(1)} %get-tuple-element.27), channel_id=1, source_target_pairs={{0,4},{4,0},{8,12},{12,8},{16,20},{20,16},{24,28},{28,24},{1,5},{5... | collective-permute-start | bytes 399368 | tf_op jit(solution)/shard_map/ppermute | solution.py:260
  12.1 2.6 %collective-permute-start.1 = (bf16[8,8192]{1,0:T(8,128)(2,1)S(1)}, bf16[8,8192]{1,0:T(8,128)(2,1)S(1)}, u32[]{:S(2)}, u32[]{:S(2)}) collective-permute-start(bf16[8,8192]{1,0:T(8,128)(2,1)S(1)} %shard_map.74.refs_1_), channel_id=1, source_target_pairs={{0,4},{4,0},{8,12},{12,8},{16,20},{20,16},{24,28},{28,24},{1,5},{5... | collective-permute-start | bytes 393224 | tf_op jit(solution)/shard_map/ppermute | solution.py:260
  12.7 2.1 %collective-permute-start.3 = (bf16[8,8320]{1,0:T(8,128)(2,1)S(1)}, bf16[8,8320]{1,0:T(8,128)(2,1)S(1)}, u32[]{:S(2)}, u32[]{:S(2)}) collective-permute-start(bf16[8,8320]{1,0:T(8,128)(2,1)S(1)} %collective-permute-done.2.refs_3_), channel_id=1, source_target_pairs={{0,4},{4,0},{8,12},{12,8},{16,20},{20,16},{24,28},{28,24},{1,5},{5... | collective-permute-start | bytes 399368 | tf_op jit(solution)/shard_map/ppermute | solution.py:260
  12.8 2.0 %collective-permute-start.5 = (bf16[8,8320]{1,0:T(8,128)(2,1)S(1)}, bf16[8,8320]{1,0:T(8,128)(2,1)S(1)}, u32[]{:S(2)}, u32[]{:S(2)}) collective-permute-start(bf16[8,8320]{1,0:T(8,128)(2,1)S(1)} %collective-permute-done.4.refs_5_), channel_id=1, source_target_pairs={{0,4},{4,0},{8,12},{12,8},{16,20},{20,16},{24,28},{28,24},{1,5},{5... | collective-permute-start | bytes 399368 | tf_op jit(solution)/shard_map/ppermute | solution.py:260
  13.6 1.2 %collective-permute-start.8 = (bf16[8,128]{1,0:T(8,128)(2,1)S(1)}, bf16[8,128]{1,0:T(8,128)(2,1)S(1)}, u32[]{:S(2)}, u32[]{:S(2)}) collective-permute-start(bf16[8,128]{1,0:T(8,128)(2,1)S(1)} %shard_map.76.refs_8_), channel_id=1, source_target_pairs={{0,4},{4,0},{8,12},{12,8},{16,20},{20,16},{24,28},{28,24},{1,5},{5... | collective-permute-start | bytes 6152 | tf_op jit(solution)/shard_map/ppermute | solution.py:260
  16.0 1.3 %collective-permute-start.9 = (f32[4,16,128]{2,1,0:T(8,128)S(1)}, f32[4,16,128]{2,1,0:T(8,128)S(1)}, u32[]{:S(2)}, u32[]{:S(2)}) collective-permute-start(f32[4,16,128]{2,1,0:T(8,128)S(1)} %get-tuple-element.32), channel_id=1, source_target_pairs={{0,4},{4,0},{8,12},{12,8},{16,20},{20,16},{24,28},{28,24},{1,5},{5... | collective-permute-start | bytes 98312 | tf_op jit(solution)/shard_map/ppermute | solution.py:260
  17.2 4.2 %collective-permute-start.12 = (f32[2,16,128]{2,1,0:T(8,128)S(1)}, f32[2,16,128]{2,1,0:T(8,128)S(1)}, u32[]{:S(2)}, u32[]{:S(2)}) collective-permute-start(f32[2,16,128]{2,1,0:T(8,128)S(1)} %pad_maximum_fusion.2), channel_id=1, source_target_pairs={{0,12},{4,8},{8,20},{12,16},{16,28},{20,24},{24,4},{28,0},{1,13},{... | collective-permute-start | bytes 49160 | tf_op jit(solution)/shard_map/ppermute | solution.py:366
  17.5 3.9 %collective-permute-start.11 = (f32[2,16,128]{2,1,0:T(8,128)S(1)}, f32[2,16,128]{2,1,0:T(8,128)S(1)}, u32[]{:S(2)}, u32[]{:S(2)}) collective-permute-start(f32[2,16,128]{2,1,0:T(8,128)S(1)} %pad_maximum_fusion.1), channel_id=1, source_target_pairs={{0,20},{4,16},{8,28},{12,24},{16,4},{20,0},{24,12},{28,8},{1,21},{... | collective-permute-start | bytes 49160 | tf_op jit(solution)/shard_map/ppermute | solution.py:366
  18.7 3.2 %collective-permute-start.10 = (f32[2,16,128]{2,1,0:T(8,128)S(1)}, f32[2,16,128]{2,1,0:T(8,128)S(1)}, u32[]{:S(2)}, u32[]{:S(2)}) collective-permute-start(f32[2,16,128]{2,1,0:T(8,128)S(1)} %pad_maximum_fusion), channel_id=1, source_target_pairs={{0,28},{4,24},{8,4},{12,0},{16,12},{20,8},{24,20},{28,16},{1,29},{... | collective-permute-start | bytes 49160 | tf_op jit(solution)/shard_map/ppermute | solution.py:366
  22.3 5.6 %collective-permute-start.13 = (f32[32,128]{1,0:T(8,128)S(1)}, f32[32,128]{1,0:T(8,128)S(1)}, u32[]{:S(2)}, u32[]{:S(2)}) collective-permute-start(f32[32,128]{1,0:T(8,128)S(1)} %get-tuple-element.34), channel_id=1, source_target_pairs={{0,1},{1,2},{2,3},{3,0},{4,5},{5,6},{6,7},{7,4},{8,9},{9,10},{10,1... | collective-permute-start | bytes 49160 | tf_op jit(solution)/shard_map/ppermute | solution.py:377
  23.9 4.9 %collective-permute-start.14 = (f32[32,128]{1,0:T(8,128)S(1)}, f32[32,128]{1,0:T(8,128)S(1)}, u32[]{:S(2)}, u32[]{:S(2)}) collective-permute-start(f32[32,128]{1,0:T(8,128)S(1)} %get-tuple-element.35), channel_id=1, source_target_pairs={{0,2},{1,3},{2,0},{3,1},{4,6},{5,7},{6,4},{7,5},{8,10},{9,11},{10,... | collective-permute-start | bytes 49160 | tf_op jit(solution)/shard_map/ppermute | solution.py:377
  26.5 3.7 %collective-permute-start.15 = (f32[32,128]{1,0:T(8,128)S(1)}, f32[32,128]{1,0:T(8,128)S(1)}, u32[]{:S(2)}, u32[]{:S(2)}) collective-permute-start(f32[32,128]{1,0:T(8,128)S(1)} %get-tuple-element.36), channel_id=1, source_target_pairs={{0,3},{1,0},{2,1},{3,2},{4,7},{5,4},{6,5},{7,6},{8,11},{9,8},{10,9... | collective-permute-start | bytes 49160 | tf_op jit(solution)/shard_map/ppermute | solution.py:377
